TPU v7x, 32 devices: a whole 2x2x4 slice. The times are simulated.
32 devices in a mesh: user: 4 (over z), cand: 8 (over y, x, core).
Axes of the slice: x: 2, y: 2, z: 4, core: 2. Of those that a mesh axis runs over, the one named last changes fastest.
Arguments:
- cand_x: bfloat16 [16384, 1024], P(('user', 'cand')), may hold values from -6 to 6
- cand_user: int32 [16384, 1], P(('user', 'cand')), may hold values from 0 to 7; in each aligned block of 512 rows (0 to 511, 512 to 1023, ...) at most 128 rows name the same one
- visible: int32 [16384], P(('user', 'cand')), may hold values from 1 to 8
- hist_len: int32 [8], P('cand'), may hold values from 1 to 1024
- kv_cache: bfloat16 [8, 1024, 2048], P('cand', 'user'), may hold values from -6 to 6
- w_in: bfloat16 [1024, 2048], replicated, may hold values from -0.1875 to 0.1875
- w_out: bfloat16 [1024, 1024], replicated, may hold values from -0.1875 to 0.1875
- ln_gain: float32 [1024], replicated, may hold values from 0.1 to 1.9
Outputs:
- scored: bfloat16 [16384, 1024], P(('user', 'cand'))
Inputs may be any that keep to these rules, and one draw needn't show every extreme that they name: `cand_user`: among the 512 candidates of one device no user is named more than 128 times, a bound that some block reaches.
All inputs are finite; a program needn't handle non-finite values.
Results may differ from a plain program's by a relative error of at most 0.0055.
Values may be sent and summed in bfloat16 or wider, within the bound.
No kernel may reach another device: no remote copies, remote signals or barrier semaphores. Data moves between devices by JAX's collectives and lax.ppermute only.
A program may use at most 128 MiB of HBM per device.

v0:
```python
import math

import jax
import jax.numpy as jnp
from jax import lax
from jax.sharding import PartitionSpec as P

HEADS = 8
BLK = 128


norm_eps = 1e-06


def attend_rows(queries, limits, piece):
    total_rows, width = queries.shape
    head_size = width // HEADS
    block_rows = min(512, total_rows)
    keys_count = piece.shape[0]
    keys = piece[:, :width].reshape(keys_count, HEADS, head_size)
    values = piece[:, width:].reshape(keys_count, HEADS, head_size)
    positions = jnp.arange(keys_count, dtype=jnp.int32).astype(jnp.float32)
    scale = 1.0 / math.sqrt(head_size)

    def one_block(packed):
        query_block, limit_block = packed
        scores = jnp.einsum(
            "bhd,nhd->hbn",
            query_block.reshape(block_rows, HEADS, head_size),
            keys,
            preferred_element_type=jnp.float32,
        )
        visible_mask = (positions[None, :] < limit_block[:, None]).astype(jnp.float32)
        weights = (jax.nn.silu(scores * scale) * visible_mask[None]).astype(jnp.bfloat16)
        mixed = jnp.einsum("hbn,nhd->bhd", weights, values, preferred_element_type=jnp.float32)
        return mixed.reshape(block_rows, width)

    blocks = lax.map(
        one_block, (queries.reshape(-1, block_rows, width), limits.reshape(-1, block_rows))
    )
    return blocks.reshape(total_rows, width)


def per_device(cand_x, cand_user, visible, hist_len, kv_cache, w_in, w_out, ln_gain):
    rows, width = cand_x.shape
    columns = lax.axis_size("cand")
    capacity = 2 * rows // columns
    slots = columns * capacity
    hidden = jax.nn.silu(jnp.dot(cand_x, w_in, preferred_element_type=jnp.float32))
    queries = hidden[:, :width].astype(jnp.bfloat16)
    gate = hidden[:, width:].astype(jnp.bfloat16)
    owner = cand_user[:, 0]
    onehot = (owner[:, None] == jnp.arange(columns, dtype=jnp.int32)[None, :]).astype(jnp.int32)
    earlier = jnp.cumsum(onehot, axis=0) - onehot
    slot_of = owner * capacity + jnp.sum(earlier * onehot, axis=1)
    send_rows = jnp.zeros((slots, width), jnp.bfloat16).at[slot_of].set(queries)
    send_vis = jnp.zeros((slots,), jnp.bfloat16).at[slot_of].set(visible.astype(jnp.bfloat16))
    got_rows, got_vis = (
        lax.all_to_all(
            send_rows.reshape(columns, capacity, width),
            "cand",
            split_axis=0,
            concat_axis=0,
            tiled=True,
        ),
        lax.all_to_all(
            send_vis.reshape(columns, capacity), "cand", split_axis=0, concat_axis=0, tiled=True
        ),
    )
    got_rows = got_rows.reshape(slots, width)
    got_vis = got_vis.reshape(slots)
    user_length = hist_len[0].astype(jnp.float32)
    limits = jnp.minimum(user_length, BLK * got_vis.astype(jnp.float32))
    partial_value = attend_rows(
        got_rows, limits, lax.all_gather(kv_cache, "user", axis=1, tiled=True)[0]
    )
    mean_row = jnp.mean(partial_value, axis=1, keepdims=True)
    centered = partial_value - mean_row
    variance = jnp.mean(centered * centered, axis=1, keepdims=True)
    normed = (centered * lax.rsqrt(variance + norm_eps) * ln_gain).astype(jnp.bfloat16)
    returned = lax.all_to_all(
        normed.reshape(columns, capacity, width), "cand", split_axis=0, concat_axis=0, tiled=True
    ).reshape(slots, width)
    home_rows = returned[slot_of]
    mixed_rows = (home_rows.astype(jnp.float32) * gate.astype(jnp.float32)).astype(jnp.bfloat16)
    projected = jnp.dot(mixed_rows, w_out, preferred_element_type=jnp.float32)
    return (cand_x.astype(jnp.float32) + projected).astype(jnp.bfloat16)


def solution(mesh):
    in_specs = (
        P(("user", "cand"), None),
        P(("user", "cand"), None),
        P(("user", "cand")),
        P("cand"),
        P("cand", "user", None),
        P(),
        P(),
        P(),
    )
    out_specs = P(("user", "cand"), None)
    return jax.shard_map(
        per_device, mesh=mesh, in_specs=in_specs, out_specs=out_specs, check_vma=False
    )
```

profile of v0, /device:TPU:0, one launch (start us, length us, event | category | flops | bytes accessed | tf_op | source)
XLA Modules:
  0.0 202.5 jit_solution(1138304037995756651)
XLA Ops:
  6.5 0.0 copy-start
  6.5 0.0 copy-start.1
  6.5 0.0 copy-start.5
  6.5 0.0 copy-start.6
  6.5 0.0 all-gather.2.cloned.1.call-start
  6.6 2.4 %copy.25 = bf16[1,256,2048]{1,2,0:T(8,128)(2,1)} copy(bf16[1,256,2048]{2,1,0:T(8,128)(2,1)} %param.14) | data formatting | bytes 2097152 | tf_op args[4]
  9.0 0.0 all-gather.2.cloned.1.call-update
  9.0 0.0 copy-done.1
  9.0 1.1 reduce-window.6
  10.2 0.2 slice_reduce_fusion
  10.4 0.0 copy-done.5
  10.5 0.1 fusion.10
  10.6 0.0 copy-start.2
  10.6 3.8 %scatter_custom_fusion.1 = bf16[1024]{0:T(1024)(128)(2,1)S(1)} fusion(s32[512]{0:T(512)S(1)} %bitcast.56, bf16[512]{0:T(512)(128)(2,1)S(1)} %convert_element_type.61, bf16[]{:T(256)} %constant.21.clone.1), kind=kCustom, calls=%fused_computation.34 | custom fusion | bytes 2050 | tf_op jit(solution)/shard_map/scatter | solution.py:57
  14.3 0.6 copy.26
  14.9 5.2 %all-to-all-start.1 = ((bf16[8,1,128]{2,1,0:T(2,128)(2,1)}), bf16[8,1,128]{2,1,0:T(2,128)(2,1)S(1)}, u32[]{:S(2)}, u32[]{:S(2)}) async-start(bf16[8,1,128]{2,1,0:T(2,128)(2,1)} %copy.26), calls=%async_computation.1 | async-start | bytes 8192 | tf_op jit(solution)/shard_map/all_to_all | solution.py:66
  20.1 0.0 copy-done.6
  20.1 6.5 %multiply_convert_fusion.2 = bf16[512,2048]{1,0:T(8,128)(2,1)} fusion(bf16[512,1024]{1,0:T(8,128)(2,1)S(1)} %copy-done.6, bf16[1024,2048]{1,0:T(8,128)(2,1)} %param.15), kind=kOutput, calls=%fused_computation.15 | convolution fusion | flops 2152726528 | bytes 7340032 | tf_op jit(solution)/shard_map/dot_general | solution.py:49
  26.6 0.0 copy-done.2
  26.6 4.8 %scatter_custom_fusion = bf16[1024,1024]{1,0:T(8,128)(2,1)} fusion(s32[512]{0:T(512)S(1)} %bitcast.57, bf16[512,2048]{1,0:T(8,128)(2,1)} %multiply_convert_fusion.2, bf16[]{:T(256)} %constant.21.clone.1), kind=kCustom, calls=%fused_computation.19 | custom fusion | bytes 3146240 | tf_op jit(solution)/shard_map/scatter | solution.py:56
  31.4 0.0 all-to-all-done.1
  31.4 4.5 %all-to-all-start = ((bf16[8,128,1024]{2,1,0:T(8,128)(2,1)}), bf16[8,128,1024]{2,1,0:T(8,128)(2,1)}, u32[]{:S(2)}, u32[]{:S(2)}) async-start(bf16[8,128,1024]{2,1,0:T(8,128)(2,1)} %bitcast.49), calls=%async_computation | async-start | bytes 4194304 | tf_op jit(solution)/shard_map/all_to_all | solution.py:59
  36.7 55.8 %all-gather.2.cloned.1.call-done = bf16[1,1024,2048]{1,2,0:T(8,128)(2,1)} async-done(((bf16[1,256,2048]{1,2,0:T(8,128)(2,1)}), bf16[1,1024,2048]{1,2,0:T(8,128)(2,1)}) %all-gather.2.cloned.1.call-update) | async-done | bytes 4194320 | tf_op jit(solution)/shard_map/all_gather | solution.py:75
  92.4 4.8 %fusion.14 = (bf16[1024,1024]{0,1:T(8,128)(2,1)}, bf16[1024,1024]{0,1:T(8,128)(2,1)}) fusion(bf16[1024,2048]{0,1:T(8,128)(2,1)} %bitcast.51), kind=kLoop, calls=%fused_computation.36 | loop fusion | bytes 8388608 | tf_op jit(solution)/shard_map/slice | solution.py:21
  97.2 3.9 %copy.28 = bf16[1024,8,128]{2,0,1:T(8,128)(2,1)} copy(bf16[1024,8,128]{0,2,1:T(8,128)(2,1)} %bitcast.50) | data formatting | bytes 4194304
  101.1 0.0 all-to-all-done
  101.1 40.3 %while.11 = (s32[]{:T(128)}, f32[2,512,1024]{1,2,0:T(8,128)}, bf16[2,512,1024]{2,1,0:T(8,128)(2,1)}, bf16[1024,8,128]{2,0,1:T(8,128)(2,1)}, f32[2,512]{1,0:T(2,1...) while((s32[]{:T(128)}, f32[2,512,1024]{1,2,0:T(8,128)}, bf16[2,512,1024]{2,1,0:T(8,128)(2,1)}, ...), condition=%wide.region_6.7_spmd.clone, body=%wide.region_5.6_spmd.clone.sunk | while | flops 2177893376 | bytes 19937876 | solution.py:38
  101.2 1.5 compare_convert_fusion.2
  102.7 1.3 constant_dynamic-slice_fusion.4
  104.0 1.3 copy.33
  105.3 12.9 %fusion.28 = f32[8,512,128]{1,2,0:T(8,128)} fusion(bf16[1024,8,128]{0,2,1:T(8,128)(2,1)} %get-tuple-element.151, bf16[512,8,128]{0,2,1:T(8,128)(2,1)} %bitcast.47, bf16[1024,8,128]{2,0,1:T(8,128)(2,1)} %get-tuple-element.149, f32[512,1024]{1,0:T(8,128)} %compare_convert_fusion.2), kind=kOutput, calls=%fused_computation.7.clone.1 | convolution fusion | flops 2176843776 | bytes 9437184 | tf_op jit(solution)/shard_map/while/body/eval_jaxpr/hbn,nhd->bhd/dot_general | solution.py:35
  118.2 3.1 %bitcast_dynamic-update-slice_fusion.2 = f32[2,512,1024]{1,2,0:T(8,128)} fusion(f32[2,512,1024]{1,2,0:T(8,128)} %get-tuple-element.140, s32[]{:T(128)} %get-tuple-element.139, f32[1,512,1024]{1,2,0:T(8,128)} %bitcast.46), kind=kLoop, calls=%fused_computation.5.clone.1 | loop fusion | bytes 4194816 | tf_op jit(solution)/shard_map/while/body/jit(dynamic_update_index_in_dim)/dynamic_update_slice | solution.py:38
  121.3 1.5 compare_convert_fusion.2
  122.8 1.3 constant_dynamic-slice_fusion.4
  124.1 1.3 copy.33
  125.5 12.9 %fusion.28 = f32[8,512,128]{1,2,0:T(8,128)} fusion(bf16[1024,8,128]{0,2,1:T(8,128)(2,1)} %get-tuple-element.151, bf16[512,8,128]{0,2,1:T(8,128)(2,1)} %bitcast.47, bf16[1024,8,128]{2,0,1:T(8,128)(2,1)} %get-tuple-element.149, f32[512,1024]{1,0:T(8,128)} %compare_convert_fusion.2), kind=kOutput, calls=%fused_computation.7.clone.1 | convolution fusion | flops 2176843776 | bytes 9437184 | tf_op jit(solution)/shard_map/while/body/eval_jaxpr/hbn,nhd->bhd/dot_general | solution.py:35
  138.3 3.1 %bitcast_dynamic-update-slice_fusion.2 = f32[2,512,1024]{1,2,0:T(8,128)} fusion(f32[2,512,1024]{1,2,0:T(8,128)} %get-tuple-element.140, s32[]{:T(128)} %get-tuple-element.139, f32[1,512,1024]{1,2,0:T(8,128)} %bitcast.46), kind=kLoop, calls=%fused_computation.5.clone.1 | loop fusion | bytes 4194816 | tf_op jit(solution)/shard_map/while/body/jit(dynamic_update_index_in_dim)/dynamic_update_slice | solution.py:38
  141.4 2.5 %reduce_sum.31 = f32[2,512]{1,0:T(2,128)S(1)} reduce(f32[2,512,1024]{1,2,0:T(8,128)} %get-tuple-element.42, f32[]{:T(128)} %constant.17.clone.1), dimensions={2}, to_apply=%region_7.8 | reduce | flops 1047552 | bytes 4198404 | tf_op jit(solution)/shard_map/reduce_sum | solution.py:77
  143.9 2.7 %multiply_reduce_fusion = f32[2,512]{1,0:T(2,128)S(1)} fusion(f32[2,512,1024]{1,2,0:T(8,128)} %get-tuple-element.42, f32[2,512]{1,0:T(2,128)S(1)} %broadcast_multiply_fusion), kind=kLoop, calls=%fused_computation.14 | loop fusion | flops 3144704 | bytes 4202496 | tf_op jit(solution)/shard_map/reduce_sum | solution.py:79
  146.6 0.0 copy-start.4
  146.6 5.4 %copy.29 = f32[2,512,1024]{2,1,0:T(8,128)} copy(f32[2,512,1024]{1,2,0:T(8,128)} %get-tuple-element.42) | data formatting | bytes 8388608 | tf_op jit(solution)/shard_map/while | solution.py:38
  152.0 0.0 copy-done.4
  152.1 4.1 %multiply_convert_fusion.1 = bf16[8,128,1024]{2,1,0:T(8,128)(2,1)} fusion(f32[8,128,1024]{2,1,0:T(8,128)} %bitcast.48, f32[1024]{0:T(1024)S(1)} %copy-done.4, f32[8,128]{1,0:T(8,128)S(1)} %rsqrt.12, f32[8,128]{1,0:T(8,128)S(1)} %div.18), kind=kLoop, calls=%fused_computation.13 | loop fusion | flops 4194304 | bytes 6303744 | tf_op jit(solution)/shard_map/convert_element_type | solution.py:80
  156.2 0.0 copy-start.3
  156.2 4.7 %all-to-all-start.2 = ((bf16[8,128,1024]{2,1,0:T(8,128)(2,1)}), bf16[8,128,1024]{2,1,0:T(8,128)(2,1)}, u32[]{:S(2)}, u32[]{:S(2)}) async-start(bf16[8,128,1024]{2,1,0:T(8,128)(2,1)} %multiply_convert_fusion.1), calls=%async_computation.2 | async-start | bytes 4194304 | tf_op jit(solution)/shard_map/all_to_all | solution.py:81
  160.9 0.0 copy-done.3
  160.9 26.4 %all-to-all-done.2 = bf16[8,128,1024]{2,1,0:T(8,128)(2,1)} async-done(((bf16[8,128,1024]{2,1,0:T(8,128)(2,1)}), bf16[8,128,1024]{2,1,0:T(8,128)(2,1)}, u32[]{:S(2)}, u32[]{:S(2)}) %all-to-all-start.2) | async-done | bytes 2097184 | tf_op jit(solution)/shard_map/all_to_all | solution.py:81
  187.3 4.6 %gather_fusion = bf16[512,1024]{1,0:T(8,128)(2,1)S(1)} fusion(bf16[1024,1024]{1,0:T(8,128)(2,1)} %bitcast.14, s32[1024]{0:T(1024)S(1)} %pad_clamp_fusion), kind=kCustom, calls=%fused_computation | custom fusion | bytes 2099200 | tf_op jit(solution)/shard_map/gather | solution.py:84
  191.9 0.0 copy-done
  191.9 3.8 %add_convert_fusion = bf16[512,1024]{1,0:T(8,128)(2,1)} fusion(bf16[512,1024]{1,0:T(8,128)(2,1)} %param.10, bf16[1024,1024]{1,0:T(8,128)(2,1)S(1)} %copy-done, bf16[512,1024]{1,0:T(8,128)(2,1)S(1)} %gather_fusion, bf16[512,2048]{1,0:T(8,128)(2,1)} %multiply_convert_fusion.2), kind=kOutput, calls=%fused_computation.16 | convolution fusion | flops 1077411840 | bytes 6291456 | tf_op jit(solution)/shard_map/dot_general | solution.py:86
  (17 shorter events, 0.1 us)
Async XLA Ops:
  6.5 185.4 %copy-start = (bf16[1024,1024]{1,0:T(8,128)(2,1)S(1)}, bf16[1024,1024]{1,0:T(8,128)(2,1)}, u32[]{:S(2)}) copy-start(bf16[1024,1024]{1,0:T(8,128)(2,1)} %param.16) | copy-start | bytes 6291460
  6.5 2.5 %copy-start.1 = (s32[512,1]{0,1:T(1,128)S(1)}, s32[512,1]{0,1:T(1,128)}, u32[]{:S(2)}) copy-start(s32[512,1]{0,1:T(1,128)} %param.11) | copy-start | bytes 6148
  6.5 3.9 %copy-start.5 = (s32[512]{0:T(512)S(1)}, s32[512]{0:T(512)}, u32[]{:S(2)}) copy-start(s32[512]{0:T(512)} %param.12) | copy-start | bytes 6148
  6.5 13.6 %copy-start.6 = (bf16[512,1024]{1,0:T(8,128)(2,1)S(1)}, bf16[512,1024]{1,0:T(8,128)(2,1)}, u32[]{:S(2)}) copy-start(bf16[512,1024]{1,0:T(8,128)(2,1)} %param.10) | copy-start | bytes 3145732
  6.5 85.9 %all-gather.2.cloned.1.call-start = ((), (), s32[]{:S(2)}) async-start(), calls=%async_computation.3 | async-start | bytes 5242880 | tf_op jit(solution)/shard_map/all_gather | solution.py:75
  10.6 16.0 %copy-start.2 = (s32[512,1]{0,1:T(1,128)}, s32[512,1]{0,1:T(1,128)S(1)}, u32[]{:S(2)}) copy-start(s32[512,1]{0,1:T(1,128)S(1)} %compare_select_fusion) | copy-start | bytes 6148
  14.9 16.5 %all-to-all-start.1 = ((bf16[8,1,128]{2,1,0:T(2,128)(2,1)}), bf16[8,1,128]{2,1,0:T(2,128)(2,1)S(1)}, u32[]{:S(2)}, u32[]{:S(2)}) async-start(bf16[8,1,128]{2,1,0:T(2,128)(2,1)} %copy.26), calls=%async_computation.1 | async-start | bytes 8192 | tf_op jit(solution)/shard_map/all_to_all | solution.py:66
  31.4 69.7 %all-to-all-start = ((bf16[8,128,1024]{2,1,0:T(8,128)(2,1)}), bf16[8,128,1024]{2,1,0:T(8,128)(2,1)}, u32[]{:S(2)}, u32[]{:S(2)}) async-start(bf16[8,128,1024]{2,1,0:T(8,128)(2,1)} %bitcast.49), calls=%async_computation | async-start | bytes 4194304 | tf_op jit(solution)/shard_map/all_to_all | solution.py:59
  146.6 5.5 %copy-start.4 = (f32[1024]{0:T(1024)S(1)}, f32[1024]{0:T(1024)}, u32[]{:S(2)}) copy-start(f32[1024]{0:T(1024)} %param.17) | copy-start | bytes 12292
  156.2 4.7 %copy-start.3 = (s32[512,1]{0,1:T(1,128)S(1)}, s32[512,1]{0,1:T(1,128)}, u32[]{:S(2)}) copy-start(s32[512,1]{0,1:T(1,128)} %copy-done.2) | copy-start | bytes 6148
  156.2 31.1 %all-to-all-start.2 = ((bf16[8,128,1024]{2,1,0:T(8,128)(2,1)}), bf16[8,128,1024]{2,1,0:T(8,128)(2,1)}, u32[]{:S(2)}, u32[]{:S(2)}) async-start(bf16[8,128,1024]{2,1,0:T(8,128)(2,1)} %multiply_convert_fusion.1), calls=%async_computation.2 | async-start | bytes 4194304 | tf_op jit(solution)/shard_map/all_to_all | solution.py:81
Sparse Core Ops, SparseCore 0:
  9.1 83.2 all-gather.1
where the time goes:
time: 203 us
  waiting for transfers between devices  82.2 us (40%)
  local copies, waits for them, and re-layouts  42 us (21%)
  matrix products  36 us (18%)
  starting transfers between devices  14.5 us (7%)
  between operations  14.2 us (7%)
  other arithmetic  13.7 us (7%)
    all_gather x1, waiting for transfers between devices, per_device(): lax.all_gather(kv_cache, 'user', axis=1, tiled=True)[0]  55.8 us
    all_to_all x1, waiting for transfers between devices, per_device(): lax.all_to_all(normed.reshape(columns, capacity, width), 'cand', split_ax...  26.4 us
    dot_general x2, matrix products, one_block(): jnp.einsum('hbn,nhd->bhd', weights, values, preferred_element_type=jnp.fl...  25.7 us
    dot_general x1, matrix products, per_device(): jnp.dot(cand_x, w_in, preferred_element_type=jnp.float32)  6.47 us
    unnamed x16, local copies, waits for them, and re-layouts  6.36 us
    dynamic_update_slice x2, local copies, waits for them, and re-layouts, attend_rows(): lax.map(one_block, (queries.reshape(-1, block_rows, width), limits.reshap...  6.19 us
    while x1, local copies, waits for them, and re-layouts, attend_rows(): lax.map(one_block, (queries.reshape(-1, block_rows, width), limits.reshap...  5.42 us
    dynamic_slice x6, local copies, waits for them, and re-layouts, attend_rows(): lax.map(one_block, (queries.reshape(-1, block_rows, width), limits.reshap...  5.25 us
  transfers between devices with their start and end apart: 4, of which 2 were waited for; matrix products, arithmetic and copies ran while one was open for 13% of the time, Pallas kernels for 0%

commit v1 on v0

v1 whole, which is shorter than its diff:
```python
import functools
import math

import jax
import jax.numpy as jnp
from jax import lax
from jax.experimental import pallas as pl
from jax.experimental.pallas import tpu as pltpu
from jax.sharding import PartitionSpec as P

HEADS = 8
BLK = 128
GROUPS = (2, 2, 2, 2)
norm_eps = 1e-06
F32 = jnp.float32
BF16 = jnp.bfloat16
VMEM_BYTES = 40 * 1024 * 1024


def params():
    return pltpu.CompilerParams(vmem_limit_bytes=VMEM_BYTES)


def cost(flops, nbytes, transcendentals=0):
    return pl.CostEstimate(
        flops=int(flops), bytes_accessed=int(nbytes), transcendentals=int(transcendentals)
    )


def silu(v):
    half = 0.5 * v
    return half * jnp.tanh(half) + half


def earlier_mask(rows):
    first = lax.broadcasted_iota(jnp.int32, (rows, rows), 0)
    second = lax.broadcasted_iota(jnp.int32, (rows, rows), 1)
    return (first < second).astype(BF16)


def slot_row(owner_row, columns, capacity):
    rows = owner_row.shape[1]
    users = lax.broadcasted_iota(jnp.int32, (columns, rows), 0)
    mine = users == owner_row
    before = jnp.dot(mine.astype(BF16), earlier_mask(rows), preferred_element_type=F32)
    rank = jnp.sum(jnp.where(mine, before, 0.0), axis=0, keepdims=True)
    return owner_row.astype(F32) * capacity + rank


def query_kernel(columns, capacity, owner_ref, x_ref, w_ref, send_ref, place):
    rows = x_ref.shape[0]
    slots = send_ref.shape[0]

    @pl.when(pl.program_id(0) == 0)
    def _():
        slot = slot_row(owner_ref[...], columns, capacity).astype(jnp.int32)
        index = lax.broadcasted_iota(jnp.int32, (slots, rows), 0)
        place[...] = (index == slot).astype(BF16)

    queries = silu(jnp.dot(x_ref[...], w_ref[...], preferred_element_type=F32)).astype(BF16)
    send_ref[...] = jnp.dot(place[...], queries, preferred_element_type=F32).astype(BF16)


def project_queries(owner_row, cand_x, w_in, columns, capacity):
    rows, width = cand_x.shape
    slots = columns * capacity
    tile = min(256, width)
    return pl.pallas_call(
        functools.partial(query_kernel, columns, capacity),
        grid=(width // tile,),
        in_specs=[
            pl.BlockSpec((1, rows), lambda i: (0, 0)),
            pl.BlockSpec((rows, width), lambda i: (0, 0)),
            pl.BlockSpec((width, tile), lambda i: (0, i)),
        ],
        out_specs=pl.BlockSpec((slots, tile), lambda i: (0, i)),
        out_shape=jax.ShapeDtypeStruct((slots, width), BF16),
        scratch_shapes=[pltpu.VMEM((slots, rows), BF16)],
        compiler_params=params(),
        cost_estimate=cost(
            2 * rows * width * width + 2 * slots * rows * width,
            2 * (rows * width + width * width + slots * width),
            rows * width,
        ),
        name="project_queries",
    )(owner_row, cand_x, w_in)


def gate_kernel(columns, capacity, owner_ref, x_ref, w_ref, gate_ref, slot_ref):
    @pl.when(pl.program_id(0) == 0)
    def _():
        slot = slot_row(owner_ref[...], columns, capacity)
        slot_ref[...] = jnp.broadcast_to(slot, (BLK, slot.shape[1])).T.astype(jnp.int32)

    hidden = jnp.dot(x_ref[...], w_ref[...], preferred_element_type=F32)
    gate_ref[...] = silu(hidden).astype(BF16)


def project_gate(owner_row, cand_x, w_in, columns, capacity):
    rows, width = cand_x.shape
    tile = min(256, width)
    first = width // tile
    return pl.pallas_call(
        functools.partial(gate_kernel, columns, capacity),
        grid=(first,),
        in_specs=[
            pl.BlockSpec((1, rows), lambda i: (0, 0)),
            pl.BlockSpec((rows, width), lambda i: (0, 0)),
            pl.BlockSpec((width, tile), lambda i: (0, first + i)),
        ],
        out_specs=[
            pl.BlockSpec((rows, tile), lambda i: (0, i)),
            pl.BlockSpec((rows, BLK), lambda i: (0, 0)),
        ],
        out_shape=[
            jax.ShapeDtypeStruct((rows, width), BF16),
            jax.ShapeDtypeStruct((rows, BLK), jnp.int32),
        ],
        compiler_params=params(),
        cost_estimate=cost(
            2 * rows * width * width, 2 * (2 * rows * width + width * width), rows * width
        ),
        name="project_gate",
    )(owner_row, cand_x, w_in)


def limits_kernel(capacity, scalars_ref, owner_ref, visible_ref, limit_ref):
    user, length = scalars_ref[0], scalars_ref[1]
    sources, rows = owner_ref.shape
    mine = owner_ref[...] == user
    rank = jnp.dot(mine.astype(BF16), earlier_mask(rows), preferred_element_type=F32)
    slot = jnp.where(mine, rank, -1.0).astype(jnp.int32)
    index = lax.broadcasted_iota(jnp.int32, (capacity, rows), 0)
    seen = visible_ref[...].astype(F32).astype(BF16)
    for source in range(sources):
        pick = (index == slot[source : source + 1, :]).astype(BF16)
        spread = jnp.broadcast_to(seen[source : source + 1, :], (BLK, rows))
        blocks = lax.dot_general(pick, spread, (((1,), (1,)), ((), ())), preferred_element_type=F32)
        limit_ref[source * capacity : (source + 1) * capacity, :] = jnp.minimum(
            blocks.astype(jnp.int32) * BLK, length
        )


def slot_limits(user, length, owners, seen, capacity):
    sources, rows = owners.shape
    slots = sources * capacity
    scalars = jnp.stack([user, length]).astype(jnp.int32)
    return pl.pallas_call(
        functools.partial(limits_kernel, capacity),
        in_specs=[
            pl.BlockSpec(memory_space=pltpu.SMEM),
            pl.BlockSpec(memory_space=pltpu.VMEM),
            pl.BlockSpec(memory_space=pltpu.VMEM),
        ],
        out_specs=pl.BlockSpec(memory_space=pltpu.VMEM),
        out_shape=jax.ShapeDtypeStruct((slots, BLK), jnp.int32),
        compiler_params=params(),
        cost_estimate=cost(2 * slots * rows * BLK, 4 * (slots * BLK + 2 * sources * rows)),
        name="slot_limits",
    )(scalars, owners, seen)


def attend_kernel(heads, size, shard_ref, query_ref, limit_ref, *refs):
    pieces, out_ref = refs[:-1], refs[-1]
    half_scale = 0.5 / math.sqrt(size)
    rows = query_ref.shape[0]
    keys = pieces[0].shape[0]
    wide = heads * size
    lane = lax.broadcasted_iota(jnp.int32, (1, BLK), 1)
    totals = [None] * heads
    for number, piece in enumerate(pieces):
        left = limit_ref[...] - shard_ref[number] * keys
        open_ = jnp.concatenate(
            [lane + start < left for start in range(0, keys, BLK)], axis=1
        )
        for head in range(heads):
            lo, hi = head * size, (head + 1) * size
            scores = lax.dot_general(
                query_ref[:, lo:hi],
                piece[:, lo:hi],
                (((1,), (1,)), ((), ())),
                preferred_element_type=F32,
            )
            half = scores * half_scale
            weights = jnp.where(open_, half * jnp.tanh(half) + half, 0.0).astype(BF16)
            part = jnp.dot(weights, piece[:, wide + lo : wide + hi], preferred_element_type=F32)
            totals[head] = part if totals[head] is None else totals[head] + part
    for head in range(heads):
        out_ref[:, head * size : (head + 1) * size] = totals[head].astype(BF16)


def attend(shards, queries, limits, pieces, first, heads, size):
    slots = queries.shape[0]
    keys = pieces[0].shape[0]
    tile = min(256, slots)
    wide = heads * size
    count = len(pieces)
    return pl.pallas_call(
        functools.partial(attend_kernel, heads, size),
        grid=(slots // tile,),
        in_specs=[
            pl.BlockSpec(memory_space=pltpu.SMEM),
            pl.BlockSpec((tile, wide), lambda i: (i, first // heads)),
            pl.BlockSpec((tile, BLK), lambda i: (i, 0)),
        ]
        + [pl.BlockSpec((keys, 2 * wide), lambda i: (0, 0))] * count,
        out_specs=pl.BlockSpec((tile, wide), lambda i: (i, 0)),
        out_shape=jax.ShapeDtypeStruct((slots, wide), BF16),
        compiler_params=params(),
        cost_estimate=cost(
            4 * slots * keys * count * wide,
            2 * (2 * slots * wide + count * keys * 2 * wide),
            slots * keys * count * heads,
        ),
        name="attend",
    )(shards, queries, limits, *pieces)


def finish_kernel(slot_ref, x_ref, gate_ref, gain_ref, w_ref, *refs):
    returned, out_ref = refs[:-1], refs[-1]
    rows, width = x_ref.shape
    slots = returned[0].shape[0]
    lane = lax.broadcasted_iota(jnp.int32, (1, BLK), 1)
    slot = slot_ref[...]
    place = jnp.concatenate(
        [(lane + start == slot).astype(BF16) for start in range(0, slots, BLK)], axis=1
    )
    attn = jnp.concatenate(
        [jnp.dot(place, part[...], preferred_element_type=F32) for part in returned], axis=1
    )
    centered = attn - jnp.mean(attn, axis=1, keepdims=True)
    variance = jnp.mean(centered * centered, axis=1, keepdims=True)
    normed = (centered * lax.rsqrt(variance + norm_eps) * gain_ref[...]).astype(BF16)
    mixed = (normed.astype(F32) * gate_ref[...].astype(F32)).astype(BF16)
    projected = jnp.dot(mixed, w_ref[...], preferred_element_type=F32)
    out_ref[...] = (x_ref[...].astype(F32) + projected).astype(BF16)


def finish(slot, cand_x, gate, ln_gain, w_out, returned):
    rows, width = cand_x.shape
    slots = returned[0].shape[0]
    tile = min(256, rows)
    return pl.pallas_call(
        finish_kernel,
        grid=(rows // tile,),
        in_specs=[
            pl.BlockSpec((tile, BLK), lambda i: (i, 0)),
            pl.BlockSpec((tile, width), lambda i: (i, 0)),
            pl.BlockSpec((tile, width), lambda i: (i, 0)),
            pl.BlockSpec((1, width), lambda i: (0, 0)),
            pl.BlockSpec((width, width), lambda i: (0, 0)),
        ]
        + [pl.BlockSpec((slots, part.shape[1]), lambda i: (0, 0)) for part in returned],
        out_specs=pl.BlockSpec((tile, width), lambda i: (i, 0)),
        out_shape=jax.ShapeDtypeStruct((rows, width), BF16),
        compiler_params=params(),
        cost_estimate=cost(
            2 * rows * width * (width + slots), 2 * (3 * rows * width + width * width + slots * width)
        ),
        name="finish",
    )(slot, cand_x, gate, ln_gain.reshape(1, width), w_out, *returned)


def swap(array, bit, count):
    return lax.ppermute(array, "user", [(i, i ^ bit) for i in range(count)])


def gather_segments(own, count):
    held = {0: own}
    bit = count // 2
    while bit:
        for key in sorted(held):
            held[key | bit] = swap(held[key], bit, count)
        bit //= 2
    return [held[key] for key in range(count)]


def per_device(cand_x, cand_user, visible, hist_len, kv_cache, w_in, w_out, ln_gain):
    rows, width = cand_x.shape
    columns = lax.axis_size("cand")
    count = lax.axis_size("user")
    size = width // HEADS
    capacity = 2 * rows // columns
    slots = columns * capacity
    kv = kv_cache[0]
    owner_row = cand_user.reshape(1, rows)

    heads_of = []
    first = 0
    for heads in GROUPS:
        heads_of.append((first, heads))
        first += heads

    pieces = []
    for number, (first, heads) in enumerate(heads_of):
        lo, hi = first * size, (first + heads) * size
        own = jnp.concatenate([kv[:, lo:hi], kv[:, width + lo : width + hi]], axis=1)
        if number >= 2:
            own, _ = lax.optimization_barrier((own, pieces[number - 2][count // 2]))
        pieces.append(gather_segments(own, count))

    packed = owner_row * 64 + visible.reshape(1, rows)
    packed = lax.all_gather(packed, "cand", axis=0, tiled=True)
    owners, seen = packed // 64, packed % 64

    send = project_queries(owner_row, cand_x, w_in, columns, capacity)
    got = lax.all_to_all(
        send.reshape(columns, capacity, width), "cand", split_axis=0, concat_axis=0, tiled=True
    ).reshape(slots, width)
    gate, slot = project_gate(owner_row, cand_x, w_in, columns, capacity)
    limits = slot_limits(lax.axis_index("cand"), hist_len[0], owners, seen, capacity)
    shards = lax.axis_index("user").astype(jnp.int32) ^ jnp.arange(count, dtype=jnp.int32)

    returned = []
    for (first, heads), segments in zip(heads_of, pieces):
        wide = heads * size
        attn = attend(shards, got, limits, segments, first, heads, size)
        back = lax.all_to_all(
            attn.reshape(columns, capacity, wide), "cand", split_axis=0, concat_axis=0, tiled=True
        )
        returned.append(back.reshape(slots, wide))
    return finish(slot, cand_x, gate, ln_gain, w_out, returned)


def solution(mesh):
    in_specs = (
        P(("user", "cand"), None),
        P(("user", "cand"), None),
        P(("user", "cand")),
        P("cand"),
        P("cand", "user", None),
        P(),
        P(),
        P(),
    )
    out_specs = P(("user", "cand"), None)
    return jax.shard_map(
        per_device, mesh=mesh, in_specs=in_specs, out_specs=out_specs, check_vma=False
    )
```

time: 203 us -> 181 us (0.89)
  Pallas kernels: 0 us -> 40.7 us
  matrix products: 36 us -> 0 us
  local copies, waits for them, and re-layouts: 42 us -> 14.6 us
  starting transfers between devices: 14.5 us -> 35 us
  between operations: 14.2 us -> 0.82 us
  other arithmetic: 13.7 us -> 0.87 us
  blocking collectives: 0 us -> 11.2 us
  waiting for transfers between devices: 82.2 us -> 76.5 us
    ppermute x0 -> x12, waiting for transfers between devices: none -> 73.7 us  [swap(): return lax.ppermute(array, 'user', [(i, i ^ bit) for i in range(count)])]
    all_gather x1 -> x0, waiting for transfers between devices: 55.8 us -> none  [per_device(): lax.all_gather(kv_cache, 'user', axis=1, tiled=True)[0]]
    pallas_call x0 -> x8, Pallas kernels: none -> 40.7 us  [the longest x4 25.3 us: attend(): pl.pallas_call(functools.partial(attend_kernel, heads, size), grid=(slots...]
    dot_general x4 -> x0, matrix products: 36 us -> none  [the longest x2 25.7 us: one_block(): jnp.einsum('hbn,nhd->bhd', weights, values, preferred_element_type=jnp.fl...]
    all_to_all x3 -> x5, waiting for transfers between devices: 26.4 us -> 2.81 us  [the longest x4 2.81 us: per_device(): lax.all_to_all(attn.reshape(columns, capacity, wide), 'cand', split_axis=...]
    ppermute x0 -> x12, starting transfers between devices: none -> 13.4 us  [swap(): return lax.ppermute(array, 'user', [(i, i ^ bit) for i in range(count)])]
    all_gather x0 -> x1, blocking collectives: none -> 11.2 us  [per_device(): packed = lax.all_gather(packed, 'cand', axis=0, tiled=True)]
    scatter x2 -> x0, local copies, waits for them, and re-layouts: 8.57 us -> none  [the longest x1 4.8 us: per_device(): send_rows = jnp.zeros((slots, width), jnp.bfloat16).at[slot_of].set(queries)]
  transfers between devices with their start and end apart: 4 -> 17, of which waited for: 2 -> 12; matrix products, arithmetic and copies ran while one was open for 13% -> 1% of each run, Pallas kernels for 0% -> 16%
where the time goes in v1:
time: 181 us; the launch traced here: 180 us
  waiting for transfers between devices  76.5 us (42%)
  Pallas kernels  40.7 us (22%)
  starting transfers between devices  35 us (19%)
  local copies, waits for them, and re-layouts  14.6 us (8%)
  blocking collectives  11.2 us (6%)
    ppermute x12, waiting for transfers between devices, swap(): return lax.ppermute(array, 'user', [(i, i ^ bit) for i in range(count)])  73.7 us
    pallas_call x4, Pallas kernels, attend(): pl.pallas_call(functools.partial(attend_kernel, heads, size), grid=(slots...  25.3 us
    all_to_all x4, starting transfers between devices, per_device(): lax.all_to_all(attn.reshape(columns, capacity, wide), 'cand', split_axis=...  16.3 us
    unnamed x32, local copies, waits for them, and re-layouts  14.5 us
    ppermute x12, starting transfers between devices, swap(): return lax.ppermute(array, 'user', [(i, i ^ bit) for i in range(count)])  13.4 us
    all_gather x1, blocking collectives, per_device(): packed = lax.all_gather(packed, 'cand', axis=0, tiled=True)  11.2 us
    pallas_call x1, Pallas kernels, project_queries(): pl.pallas_call(functools.partial(query_kernel, columns, capacity), grid=(...  6.29 us
    pallas_call x1, Pallas kernels, finish(): pl.pallas_call(finish_kernel, grid=(rows // tile,), in_specs=[pl.BlockSpe...  5.39 us
  transfers between devices with their start and end apart: 17, of which 12 were waited for; matrix products, arithmetic and copies ran while one was open for 1% of the time, Pallas kernels for 16%

profile of v1, /device:TPU:0, one launch (start us, length us, event | category | flops | bytes accessed | tf_op | source)
XLA Modules:
  0.0 179.6 jit_solution(4195418232189749870)
XLA Ops:
  0.0 2.2 %copy-done = bf16[1024,2048]{1,0:T(8,128)(2,1)S(1)} copy-done((bf16[1024,2048]{1,0:T(8,128)(2,1)S(1)}, bf16[1024,2048]{1,0:T(8,128)(2,1)}, u32[]{:S(2)}) %copy-start) | copy-done | bytes 4194328
  2.2 1.2 copy-done.3
  3.4 0.7 copy-done.8
  4.1 6.3 %project_queries.1 = bf16[1024,1024]{1,0:T(8,128)(2,1)S(1)} custom-call(s32[1,512]{1,0:T(1,128)S(1)} %bitcast.48, bf16[512,1024]{1,0:T(8,128)(2,1)S(1)} %copy-done.3, bf16[1024,2048]{1,0:T(8,128)(2,1)S(1)} %copy-done), custom_call_target="tpu_custom_call" | custom-call | flops 2147483648 | bytes 5242880 | tf_op jit(solution)/shard_map/project_queries/pallas_call | solution.py:68
  10.4 0.0 copy-start.2
  10.4 1.3 copy-done.2
  11.7 5.3 %all-to-all-start = ((bf16[8,128,1024]{2,1,0:T(8,128)(2,1)}), bf16[8,128,1024]{2,1,0:T(8,128)(2,1)S(1)}, u32[]{:S(2)}, u32[]{:S(2)}) async-start(bf16[8,128,1024]{2,1,0:T(8,128)(2,1)} %bitcast.46), calls=%async_computation | async-start | bytes 4194304 | tf_op jit(solution)/shard_map/all_to_all | solution.py:307
  17.1 0.0 copy-done.14
  17.1 0.0 copy-start.9
  17.1 0.0 copy-start.15
  17.1 0.1 fusion.3
  17.2 2.7 %collective-permute-start.4 = (bf16[256,512]{1,0:T(8,128)(2,1)S(1)}, bf16[256,512]{1,0:T(8,128)(2,1)}, u32[]{:S(2)}, u32[]{:S(2)}) collective-permute-start(bf16[256,512]{1,0:T(8,128)(2,1)S(1)} %pad_maximum_fusion.1.refs_0_), channel_id=1, source_target_pairs={{0,16},{8,24},{16,0},{24,8},{1,17},{9,25},{17,1},{25,9},{2,18},{10... | collective-permute-start | bytes 786440 | tf_op jit(solution)/shard_map/ppermute | solution.py:265
  19.8 0.7 pad_maximum_fusion.2
  20.6 12.0 %collective-permute-done.4.refs_2_ = bf16[256,512]{1,0:T(8,128)(2,1)} collective-permute-done((bf16[256,512]{1,0:T(8,128)(2,1)S(1)}, bf16[256,512]{1,0:T(8,128)(2,1)}, u32[]{:S(2)}, u32[]{:S(2)}) %collective-permute-start.4) | collective-permute-done | bytes 262176 | tf_op jit(solution)/shard_map/ppermute | solution.py:265
  32.6 0.0 collective-permute-start.10
  32.6 3.0 %collective-permute-start.1 = (bf16[256,512]{1,0:T(8,128)(2,1)S(1)}, bf16[256,512]{1,0:T(8,128)(2,1)}, u32[]{:S(2)}, u32[]{:S(2)}) collective-permute-start(bf16[256,512]{1,0:T(8,128)(2,1)S(1)} %pad_maximum_fusion.refs_0_), channel_id=1, source_target_pairs={{0,16},{8,24},{16,0},{24,8},{1,17},{9,25},{17,1},{25,9},{2,18},{10... | collective-permute-start | bytes 786440 | tf_op jit(solution)/shard_map/ppermute | solution.py:265
  35.6 0.0 copy-done.9
  35.6 11.2 %all-gather.1 = s32[8,1,512]{2,1,0:T(1,128)S(1)} all-gather(s32[1,1,512]{2,1,0:T(1,128)S(1)} %bitcast.52), channel_id=2, replica_groups=mesh['user'=4,'cand'=8] {'cand'}, dimensions={0}, use_global_device_ids=true | all-gather | bytes 18432 | tf_op jit(solution)/shard_map/all_gather | solution.py:303
  46.8 1.6 collective-permute-start.9
  48.4 6.0 %collective-permute-done.10.refs_2_ = bf16[256,512]{1,0:T(8,128)(2,1)} collective-permute-done((bf16[256,512]{1,0:T(8,128)(2,1)}, bf16[256,512]{1,0:T(8,128)(2,1)}, u32[]{:S(2)}, u32[]{:S(2)}) %collective-permute-start.10) | collective-permute-done | bytes 262176 | tf_op jit(solution)/shard_map/ppermute | solution.py:265
  54.3 0.0 collective-permute-start.11
  55.0 0.1 pad_add_fusion.scalars_ref
  55.1 1.1 slot_limits.1.limit_ref
  56.2 2.5 %collective-permute-done.1.refs_2_ = bf16[256,512]{1,0:T(8,128)(2,1)} collective-permute-done((bf16[256,512]{1,0:T(8,128)(2,1)S(1)}, bf16[256,512]{1,0:T(8,128)(2,1)}, u32[]{:S(2)}, u32[]{:S(2)}) %collective-permute-start.1) | collective-permute-done | bytes 262176 | tf_op jit(solution)/shard_map/ppermute | solution.py:265
  58.7 0.0 collective-permute-start.7
  58.7 7.9 %collective-permute-done.9.refs_1_ = bf16[256,512]{1,0:T(8,128)(2,1)} collective-permute-done((bf16[256,512]{1,0:T(8,128)(2,1)}, bf16[256,512]{1,0:T(8,128)(2,1)}, u32[]{:S(2)}, u32[]{:S(2)}) %collective-permute-start.9) | collective-permute-done | bytes 262176 | tf_op jit(solution)/shard_map/ppermute | solution.py:265
  66.5 8.9 %collective-permute-done.11.refs_3_ = bf16[256,512]{1,0:T(8,128)(2,1)} collective-permute-done((bf16[256,512]{1,0:T(8,128)(2,1)}, bf16[256,512]{1,0:T(8,128)(2,1)}, u32[]{:S(2)}, u32[]{:S(2)}) %collective-permute-start.11) | collective-permute-done | bytes 262176 | tf_op jit(solution)/shard_map/ppermute | solution.py:265
  75.4 0.0 all-to-all-done
  75.4 6.5 %attend.7 = bf16[1024,256]{1,0:T(8,128)(2,1)} custom-call(s32[4]{0:T(128)S(1)} %iota_xor_fusion.shard_ref, bf16[1024,1024]{1,0:T(8,128)(2,1)S(1)} %bitcast.42, s32[1024,128]{1,0:T(8,128)S(1)} %slot_limits.1.limit_ref, bf16[256,512]{1,0:T(8,128)(2,1)} %get-tuple-element.12.refs_0_, bf16[256,512]{1,0:T(8,128)(2,1)} %collective-permute-done.9.refs_1_, ...), custom_call_target="tpu_custom_call" | custom-call | flops 1073741824 | bytes 2097152 | tf_op jit(solution)/shard_map/attend/pallas_call | solution.py:198
  82.0 4.2 %all-to-all-start.4 = ((bf16[8,128,256]{2,1,0:T(8,128)(2,1)}), bf16[8,128,256]{2,1,0:T(8,128)(2,1)}, u32[]{:S(2)}, u32[]{:S(2)}) async-start(bf16[8,128,256]{2,1,0:T(8,128)(2,1)} %bitcast.14), calls=%async_computation.4 | async-start | bytes 1048576 | tf_op jit(solution)/shard_map/all_to_all | solution.py:318
  86.1 0.1 collective-permute-start.6
  86.2 0.0 collective-permute-done.7.refs_2_
  86.2 2.0 %collective-permute-start.8 = (bf16[256,512]{1,0:T(8,128)(2,1)}, bf16[256,512]{1,0:T(8,128)(2,1)S(1)}, u32[]{:S(2)}, u32[]{:S(2)}) collective-permute-start(bf16[256,512]{1,0:T(8,128)(2,1)} %collective-permute-done.7.refs_2_), channel_id=1, source_target_pairs={{0,8},{8,0},{16,24},{24,16},{1,9},{9,1},{17,25},{25,17},{2,10},{10... | collective-permute-start | bytes 786440 | tf_op jit(solution)/shard_map/ppermute | solution.py:265
  88.2 7.1 %collective-permute-done.6.refs_1_ = bf16[256,512]{1,0:T(8,128)(2,1)S(1)} collective-permute-done((bf16[256,512]{1,0:T(8,128)(2,1)S(1)}, bf16[256,512]{1,0:T(8,128)(2,1)S(1)}, u32[]{:S(2)}, u32[]{:S(2)}) %collective-permute-start.6) | collective-permute-done | bytes 262176 | tf_op jit(solution)/shard_map/ppermute | solution.py:265
  95.3 5.0 %collective-permute-done.8.refs_3_ = bf16[256,512]{1,0:T(8,128)(2,1)S(1)} collective-permute-done((bf16[256,512]{1,0:T(8,128)(2,1)}, bf16[256,512]{1,0:T(8,128)(2,1)S(1)}, u32[]{:S(2)}, u32[]{:S(2)}) %collective-permute-start.8) | collective-permute-done | bytes 262176 | tf_op jit(solution)/shard_map/ppermute | solution.py:265
  100.3 6.3 %attend.6 = bf16[1024,256]{1,0:T(8,128)(2,1)} custom-call(s32[4]{0:T(128)S(1)} %iota_xor_fusion.shard_ref, bf16[1024,1024]{1,0:T(8,128)(2,1)S(1)} %bitcast.43, s32[1024,128]{1,0:T(8,128)S(1)} %slot_limits.1.limit_ref, bf16[256,512]{1,0:T(8,128)(2,1)S(1)} %get-tuple-element.11.refs_0_, bf16[256,512]{1,0:T(8,128)(2,1)S(1)} %collective-permute-done.6.refs_1_, ...), custom_call_target="tpu_custom_call" | custom-call | flops 1073741824 | bytes 2097152 | tf_op jit(solution)/shard_map/attend/pallas_call | solution.py:198
  106.6 0.0 all-to-all-done.4
  106.6 4.1 %all-to-all-start.3 = ((bf16[8,128,256]{2,1,0:T(8,128)(2,1)}), bf16[8,128,256]{2,1,0:T(8,128)(2,1)}, u32[]{:S(2)}, u32[]{:S(2)}) async-start(bf16[8,128,256]{2,1,0:T(8,128)(2,1)} %bitcast.12), calls=%async_computation.3 | async-start | bytes 1048576 | tf_op jit(solution)/shard_map/all_to_all | solution.py:318
  110.7 0.4 collective-permute-start.3
  111.1 1.7 collective-permute-start.5
  112.8 7.1 %collective-permute-done.3.refs_1_ = bf16[256,512]{1,0:T(8,128)(2,1)S(1)} collective-permute-done((bf16[256,512]{1,0:T(8,128)(2,1)S(1)}, bf16[256,512]{1,0:T(8,128)(2,1)S(1)}, u32[]{:S(2)}, u32[]{:S(2)}) %collective-permute-start.3) | collective-permute-done | bytes 262176 | tf_op jit(solution)/shard_map/ppermute | solution.py:265
  119.9 5.0 %collective-permute-done.5.refs_3_ = bf16[256,512]{1,0:T(8,128)(2,1)S(1)} collective-permute-done((bf16[256,512]{1,0:T(8,128)(2,1)}, bf16[256,512]{1,0:T(8,128)(2,1)S(1)}, u32[]{:S(2)}, u32[]{:S(2)}) %collective-permute-start.5) | collective-permute-done | bytes 262176 | tf_op jit(solution)/shard_map/ppermute | solution.py:265
  125.0 6.3 %attend.5 = bf16[1024,256]{1,0:T(8,128)(2,1)} custom-call(s32[4]{0:T(128)S(1)} %iota_xor_fusion.shard_ref, bf16[1024,1024]{1,0:T(8,128)(2,1)S(1)} %bitcast.44, s32[1024,128]{1,0:T(8,128)S(1)} %slot_limits.1.limit_ref, bf16[256,512]{1,0:T(8,128)(2,1)S(1)} %pad_maximum_fusion.1.refs_0_, bf16[256,512]{1,0:T(8,128)(2,1)S(1)} %collective-permute-done.3.refs_1_, ...), custom_call_target="tpu_custom_call" | custom-call | flops 1073741824 | bytes 2097152 | tf_op jit(solution)/shard_map/attend/pallas_call | solution.py:198
  131.2 0.0 all-to-all-done.3
  131.2 3.8 %all-to-all-start.2 = ((bf16[8,128,256]{2,1,0:T(8,128)(2,1)}), bf16[8,128,256]{2,1,0:T(8,128)(2,1)S(1)}, u32[]{:S(2)}, u32[]{:S(2)}) async-start(bf16[8,128,256]{2,1,0:T(8,128)(2,1)} %bitcast.10), calls=%async_computation.2 | async-start | bytes 1048576 | tf_op jit(solution)/shard_map/all_to_all | solution.py:318
  135.1 0.3 collective-permute-start
  135.4 1.7 collective-permute-start.2
  137.1 7.1 %collective-permute-done.refs_1_ = bf16[256,512]{1,0:T(8,128)(2,1)S(1)} collective-permute-done((bf16[256,512]{1,0:T(8,128)(2,1)S(1)}, bf16[256,512]{1,0:T(8,128)(2,1)S(1)}, u32[]{:S(2)}, u32[]{:S(2)}) %collective-permute-start) | collective-permute-done | bytes 262176 | tf_op jit(solution)/shard_map/ppermute | solution.py:265
  144.2 5.2 %collective-permute-done.2.refs_3_ = bf16[256,512]{1,0:T(8,128)(2,1)S(1)} collective-permute-done((bf16[256,512]{1,0:T(8,128)(2,1)}, bf16[256,512]{1,0:T(8,128)(2,1)S(1)}, u32[]{:S(2)}, u32[]{:S(2)}) %collective-permute-start.2) | collective-permute-done | bytes 262176 | tf_op jit(solution)/shard_map/ppermute | solution.py:265
  149.4 6.3 %attend.4 = bf16[1024,256]{1,0:T(8,128)(2,1)} custom-call(s32[4]{0:T(128)S(1)} %iota_xor_fusion.shard_ref, bf16[1024,1024]{1,0:T(8,128)(2,1)S(1)} %bitcast.45, s32[1024,128]{1,0:T(8,128)S(1)} %slot_limits.1.limit_ref, bf16[256,512]{1,0:T(8,128)(2,1)S(1)} %pad_maximum_fusion.refs_0_, bf16[256,512]{1,0:T(8,128)(2,1)S(1)} %collective-permute-done.refs_1_, ...), custom_call_target="tpu_custom_call" | custom-call | flops 1073741824 | bytes 2097152 | tf_op jit(solution)/shard_map/attend/pallas_call | solution.py:198
  155.7 0.0 all-to-all-done.2
  155.7 0.8 copy-done.6
  156.5 4.1 %all-to-all-start.1 = ((bf16[8,128,256]{2,1,0:T(8,128)(2,1)}), bf16[8,128,256]{2,1,0:T(8,128)(2,1)}, u32[]{:S(2)}, u32[]{:S(2)}) async-start(bf16[8,128,256]{2,1,0:T(8,128)(2,1)} %bitcast.8), calls=%async_computation.1 | async-start | bytes 1048576 | tf_op jit(solution)/shard_map/all_to_all | solution.py:318
  160.6 0.0 copy-start.1
  160.6 2.2 %copy-done.1 = bf16[1024,2048]{1,0:T(8,128)(2,1)S(1)} copy-done((bf16[1024,2048]{1,0:T(8,128)(2,1)S(1)}, bf16[1024,2048]{1,0:T(8,128)(2,1)}, u32[]{:S(2)}) %copy-start.1) | copy-done | bytes 4194328
  162.8 1.2 copy-done.4
  164.0 2.5 %project_gate.1 = (bf16[512,1024]{1,0:T(8,128)(2,1)S(1)}, s32[512,128]{1,0:T(8,128)S(1)}) custom-call(s32[1,512]{1,0:T(1,128)S(1)} %bitcast.49, bf16[512,1024]{1,0:T(8,128)(2,1)S(1)} %copy-done.4, bf16[1024,2048]{1,0:T(8,128)(2,1)S(1)} %copy-done.1), custom_call_target="tpu_custom_call" | custom-call | flops 1073741824 | bytes 4194304 | tf_op jit(solution)/shard_map/project_gate/pallas_call | solution.py:103
  166.6 0.0 copy-start.11
  166.6 1.0 copy-done.11
  167.6 2.8 %all-to-all-done.1 = bf16[8,128,256]{2,1,0:T(8,128)(2,1)} async-done(((bf16[8,128,256]{2,1,0:T(8,128)(2,1)}), bf16[8,128,256]{2,1,0:T(8,128)(2,1)}, u32[]{:S(2)}, u32[]{:S(2)}) %all-to-all-start.1) | async-done | bytes 524320 | tf_op jit(solution)/shard_map/all_to_all | solution.py:318
  170.4 1.0 copy-done.7
  171.4 1.6 copy-done.10
  173.0 1.2 copy-done.12
  174.2 5.4 %finish.1 = bf16[512,1024]{1,0:T(8,128)(2,1)} custom-call(s32[512,128]{1,0:T(8,128)S(1)} %get-tuple-element.9.slot_ref, bf16[512,1024]{1,0:T(8,128)(2,1)S(1)} %copy-done.5, bf16[512,1024]{1,0:T(8,128)(2,1)S(1)} %copy-done.12, f32[1,1024]{1,0:T(1,128)S(1)} %bitcast.50, bf16[1024,1024]{1,0:T(8,128)(2,1)S(1)} %copy-done.10, bf16[1024,256]{1,0:T(8,128)(2,1)} %bitcast.9.refs_0_, ...), custom_call_target="tpu_custom_call" | custom-call | flops 2147483648 | bytes 7340032 | tf_op jit(solution)/shard_map/finish/pallas_call | solution.py:243
  (20 shorter events, 0.1 us)
Async XLA Ops:
  0.0 2.2 %copy-start = (bf16[1024,2048]{1,0:T(8,128)(2,1)S(1)}, bf16[1024,2048]{1,0:T(8,128)(2,1)}, u32[]{:S(2)}) copy-start(bf16[1024,2048]{1,0:T(8,128)(2,1)} %w_ref.4) | copy-start | bytes 12582916
  2.2 1.2 copy-start.3
  3.4 0.7 copy-start.8
  10.4 1.4 copy-start.2
  11.7 5.3 %copy-start.14 = (bf16[1,256,2048]{2,1,0:T(8,128)(2,1)S(1)}, bf16[1,256,2048]{2,1,0:T(8,128)(2,1)}, u32[]{:S(2)}) copy-start(bf16[1,256,2048]{2,1,0:T(8,128)(2,1)} %param.12) | copy-start | bytes 3145732
  11.7 63.7 %all-to-all-start = ((bf16[8,128,1024]{2,1,0:T(8,128)(2,1)}), bf16[8,128,1024]{2,1,0:T(8,128)(2,1)S(1)}, u32[]{:S(2)}, u32[]{:S(2)}) async-start(bf16[8,128,1024]{2,1,0:T(8,128)(2,1)} %bitcast.46), calls=%async_computation | async-start | bytes 4194304 | tf_op jit(solution)/shard_map/all_to_all | solution.py:307
  17.1 18.5 %copy-start.9 = (s32[512,1]{0,1:T(1,128)S(1)}, s32[512,1]{0,1:T(1,128)}, u32[]{:S(2)}) copy-start(s32[512,1]{0,1:T(1,128)} %param.9) | copy-start | bytes 6148
  17.1 18.5 %copy-start.15 = (s32[512]{0:T(512)S(1)}, s32[512]{0:T(512)}, u32[]{:S(2)}) copy-start(s32[512]{0:T(512)} %param.10) | copy-start | bytes 6148
  17.2 15.4 %collective-permute-start.4 = (bf16[256,512]{1,0:T(8,128)(2,1)S(1)}, bf16[256,512]{1,0:T(8,128)(2,1)}, u32[]{:S(2)}, u32[]{:S(2)}) collective-permute-start(bf16[256,512]{1,0:T(8,128)(2,1)S(1)} %pad_maximum_fusion.1.refs_0_), channel_id=1, source_target_pairs={{0,16},{8,24},{16,0},{24,8},{1,17},{9,25},{17,1},{25,9},{2,18},{10... | collective-permute-start | bytes 786440 | tf_op jit(solution)/shard_map/ppermute | solution.py:265
  32.6 21.7 %collective-permute-start.10 = (bf16[256,512]{1,0:T(8,128)(2,1)}, bf16[256,512]{1,0:T(8,128)(2,1)}, u32[]{:S(2)}, u32[]{:S(2)}) collective-permute-start(bf16[256,512]{1,0:T(8,128)(2,1)} %get-tuple-element.12.refs_0_), channel_id=1, source_target_pairs={{0,16},{8,24},{16,0},{24,8},{1,17},{9,25},{17,1},{25,9},{2,18},{10... | collective-permute-start | bytes 786440 | tf_op jit(solution)/shard_map/ppermute | solution.py:265
  32.6 26.1 %collective-permute-start.1 = (bf16[256,512]{1,0:T(8,128)(2,1)S(1)}, bf16[256,512]{1,0:T(8,128)(2,1)}, u32[]{:S(2)}, u32[]{:S(2)}) collective-permute-start(bf16[256,512]{1,0:T(8,128)(2,1)S(1)} %pad_maximum_fusion.refs_0_), channel_id=1, source_target_pairs={{0,16},{8,24},{16,0},{24,8},{1,17},{9,25},{17,1},{25,9},{2,18},{10... | collective-permute-start | bytes 786440 | tf_op jit(solution)/shard_map/ppermute | solution.py:265
  46.8 19.8 %collective-permute-start.9 = (bf16[256,512]{1,0:T(8,128)(2,1)}, bf16[256,512]{1,0:T(8,128)(2,1)}, u32[]{:S(2)}, u32[]{:S(2)}) collective-permute-start(bf16[256,512]{1,0:T(8,128)(2,1)} %get-tuple-element.12.refs_0_), channel_id=1, source_target_pairs={{0,8},{8,0},{16,24},{24,16},{1,9},{9,1},{17,25},{25,17},{2,10},{10... | collective-permute-start | bytes 786440 | tf_op jit(solution)/shard_map/ppermute | solution.py:265
  54.3 21.1 %collective-permute-start.11 = (bf16[256,512]{1,0:T(8,128)(2,1)}, bf16[256,512]{1,0:T(8,128)(2,1)}, u32[]{:S(2)}, u32[]{:S(2)}) collective-permute-start(bf16[256,512]{1,0:T(8,128)(2,1)} %collective-permute-done.10.refs_2_), channel_id=1, source_target_pairs={{0,8},{8,0},{16,24},{24,16},{1,9},{9,1},{17,25},{25,17},{2,10},{10... | collective-permute-start | bytes 786440 | tf_op jit(solution)/shard_map/ppermute | solution.py:265
  58.7 27.5 %collective-permute-start.7 = (bf16[256,512]{1,0:T(8,128)(2,1)S(1)}, bf16[256,512]{1,0:T(8,128)(2,1)}, u32[]{:S(2)}, u32[]{:S(2)}) collective-permute-start(bf16[256,512]{1,0:T(8,128)(2,1)S(1)} %get-tuple-element.11.refs_0_), channel_id=1, source_target_pairs={{0,16},{8,24},{16,0},{24,8},{1,17},{9,25},{17,1},{25,9},{2,18},{10... | collective-permute-start | bytes 786440 | tf_op jit(solution)/shard_map/ppermute | solution.py:265
  82.0 24.6 %all-to-all-start.4 = ((bf16[8,128,256]{2,1,0:T(8,128)(2,1)}), bf16[8,128,256]{2,1,0:T(8,128)(2,1)}, u32[]{:S(2)}, u32[]{:S(2)}) async-start(bf16[8,128,256]{2,1,0:T(8,128)(2,1)} %bitcast.14), calls=%async_computation.4 | async-start | bytes 1048576 | tf_op jit(solution)/shard_map/all_to_all | solution.py:318
  86.1 9.2 %collective-permute-start.6 = (bf16[256,512]{1,0:T(8,128)(2,1)S(1)}, bf16[256,512]{1,0:T(8,128)(2,1)S(1)}, u32[]{:S(2)}, u32[]{:S(2)}) collective-permute-start(bf16[256,512]{1,0:T(8,128)(2,1)S(1)} %get-tuple-element.11.refs_0_), channel_id=1, source_target_pairs={{0,8},{8,0},{16,24},{24,16},{1,9},{9,1},{17,25},{25,17},{2,10},{10... | collective-permute-start | bytes 786440 | tf_op jit(solution)/shard_map/ppermute | solution.py:265
  86.2 14.1 %collective-permute-start.8 = (bf16[256,512]{1,0:T(8,128)(2,1)}, bf16[256,512]{1,0:T(8,128)(2,1)S(1)}, u32[]{:S(2)}, u32[]{:S(2)}) collective-permute-start(bf16[256,512]{1,0:T(8,128)(2,1)} %collective-permute-done.7.refs_2_), channel_id=1, source_target_pairs={{0,8},{8,0},{16,24},{24,16},{1,9},{9,1},{17,25},{25,17},{2,10},{10... | collective-permute-start | bytes 786440 | tf_op jit(solution)/shard_map/ppermute | solution.py:265
  106.6 24.6 %all-to-all-start.3 = ((bf16[8,128,256]{2,1,0:T(8,128)(2,1)}), bf16[8,128,256]{2,1,0:T(8,128)(2,1)}, u32[]{:S(2)}, u32[]{:S(2)}) async-start(bf16[8,128,256]{2,1,0:T(8,128)(2,1)} %bitcast.12), calls=%async_computation.3 | async-start | bytes 1048576 | tf_op jit(solution)/shard_map/all_to_all | solution.py:318
  110.7 9.2 %collective-permute-start.3 = (bf16[256,512]{1,0:T(8,128)(2,1)S(1)}, bf16[256,512]{1,0:T(8,128)(2,1)S(1)}, u32[]{:S(2)}, u32[]{:S(2)}) collective-permute-start(bf16[256,512]{1,0:T(8,128)(2,1)S(1)} %pad_maximum_fusion.1.refs_0_), channel_id=1, source_target_pairs={{0,8},{8,0},{16,24},{24,16},{1,9},{9,1},{17,25},{25,17},{2,10},{10... | collective-permute-start | bytes 786440 | tf_op jit(solution)/shard_map/ppermute | solution.py:265
  111.1 13.9 %collective-permute-start.5 = (bf16[256,512]{1,0:T(8,128)(2,1)}, bf16[256,512]{1,0:T(8,128)(2,1)S(1)}, u32[]{:S(2)}, u32[]{:S(2)}) collective-permute-start(bf16[256,512]{1,0:T(8,128)(2,1)} %collective-permute-done.4.refs_2_), channel_id=1, source_target_pairs={{0,8},{8,0},{16,24},{24,16},{1,9},{9,1},{17,25},{25,17},{2,10},{10... | collective-permute-start | bytes 786440 | tf_op jit(solution)/shard_map/ppermute | solution.py:265
  131.2 24.4 %all-to-all-start.2 = ((bf16[8,128,256]{2,1,0:T(8,128)(2,1)}), bf16[8,128,256]{2,1,0:T(8,128)(2,1)S(1)}, u32[]{:S(2)}, u32[]{:S(2)}) async-start(bf16[8,128,256]{2,1,0:T(8,128)(2,1)} %bitcast.10), calls=%async_computation.2 | async-start | bytes 1048576 | tf_op jit(solution)/shard_map/all_to_all | solution.py:318
  135.1 9.1 %collective-permute-start = (bf16[256,512]{1,0:T(8,128)(2,1)S(1)}, bf16[256,512]{1,0:T(8,128)(2,1)S(1)}, u32[]{:S(2)}, u32[]{:S(2)}) collective-permute-start(bf16[256,512]{1,0:T(8,128)(2,1)S(1)} %pad_maximum_fusion.refs_0_), channel_id=1, source_target_pairs={{0,8},{8,0},{16,24},{24,16},{1,9},{9,1},{17,25},{25,17},{2,10},{10... | collective-permute-start | bytes 786440 | tf_op jit(solution)/shard_map/ppermute | solution.py:265
  135.4 14.0 %collective-permute-start.2 = (bf16[256,512]{1,0:T(8,128)(2,1)}, bf16[256,512]{1,0:T(8,128)(2,1)S(1)}, u32[]{:S(2)}, u32[]{:S(2)}) collective-permute-start(bf16[256,512]{1,0:T(8,128)(2,1)} %collective-permute-done.1.refs_2_), channel_id=1, source_target_pairs={{0,8},{8,0},{16,24},{24,16},{1,9},{9,1},{17,25},{25,17},{2,10},{10... | collective-permute-start | bytes 786440 | tf_op jit(solution)/shard_map/ppermute | solution.py:265
  155.7 0.8 copy-start.6
  156.5 13.9 %all-to-all-start.1 = ((bf16[8,128,256]{2,1,0:T(8,128)(2,1)}), bf16[8,128,256]{2,1,0:T(8,128)(2,1)}, u32[]{:S(2)}, u32[]{:S(2)}) async-start(bf16[8,128,256]{2,1,0:T(8,128)(2,1)} %bitcast.8), calls=%async_computation.1 | async-start | bytes 1048576 | tf_op jit(solution)/shard_map/all_to_all | solution.py:318
  160.6 2.2 %copy-start.1 = (bf16[1024,2048]{1,0:T(8,128)(2,1)S(1)}, bf16[1024,2048]{1,0:T(8,128)(2,1)}, u32[]{:S(2)}) copy-start(bf16[1024,2048]{1,0:T(8,128)(2,1)} %w_ref.4) | copy-start | bytes 12582916
  162.8 1.2 copy-start.4
  164.0 6.3 %copy-start.5 = (bf16[512,1024]{1,0:T(8,128)(2,1)S(1)}, bf16[512,1024]{1,0:T(8,128)(2,1)}, u32[]{:S(2)}) copy-start(bf16[512,1024]{1,0:T(8,128)(2,1)} %x_ref.5) | copy-start | bytes 3145732
  164.0 6.3 %copy-start.13 = (f32[1024]{0:T(1024)S(1)}, f32[1024]{0:T(1024)}, u32[]{:S(2)}) copy-start(f32[1024]{0:T(1024)} %param.15) | copy-start | bytes 12292
  166.6 1.0 copy-start.11
  170.4 1.0 copy-start.7
  171.4 1.6 copy-start.10
  173.0 1.2 copy-start.12

commit v2 on v1

v2 whole, which is shorter than its diff:
```python
import functools
import math

import jax
import jax.numpy as jnp
from jax import lax
from jax.experimental import pallas as pl
from jax.experimental.pallas import tpu as pltpu
from jax.sharding import PartitionSpec as P

HEADS = 8
BLK = 128
GROUPS = (2, 2, 2, 2)
norm_eps = 1e-06
F32 = jnp.float32
BF16 = jnp.bfloat16
MIB = 1024 * 1024
GATE_COST = 12.0


def params(mib):
    return pltpu.CompilerParams(vmem_limit_bytes=mib * MIB)


def cost(flops, nbytes, transcendentals=0):
    return pl.CostEstimate(
        flops=int(flops), bytes_accessed=int(nbytes), transcendentals=int(transcendentals)
    )


def silu(v):
    half = 0.5 * v
    return half * jnp.tanh(half) + half


def earlier_mask(rows):
    first = lax.broadcasted_iota(jnp.int32, (rows, rows), 0)
    second = lax.broadcasted_iota(jnp.int32, (rows, rows), 1)
    return (first < second).astype(BF16)


def slot_row(owner_row, columns, capacity):
    rows = owner_row.shape[1]
    users = lax.broadcasted_iota(jnp.int32, (columns, rows), 0)
    mine = users == owner_row
    before = jnp.dot(mine.astype(BF16), earlier_mask(rows), preferred_element_type=F32)
    rank = jnp.sum(jnp.where(mine, before, 0.0), axis=0, keepdims=True)
    return owner_row.astype(F32) * capacity + rank


def query_kernel(columns, capacity, last, owner_ref, visible_ref, x_ref, w_ref, send_ref, place):
    rows = x_ref.shape[0]
    slots, tile = send_ref.shape

    @pl.when(pl.program_id(0) == 0)
    def _():
        slot = slot_row(owner_ref[...], columns, capacity).astype(jnp.int32)
        index = lax.broadcasted_iota(jnp.int32, (slots, rows), 0)
        place[...] = (index == slot).astype(BF16)

    @pl.when(pl.program_id(0) < last)
    def _():
        queries = silu(jnp.dot(x_ref[...], w_ref[...], preferred_element_type=F32)).astype(BF16)
        send_ref[...] = jnp.dot(place[...], queries, preferred_element_type=F32).astype(BF16)

    @pl.when(pl.program_id(0) == last)
    def _():
        seen = jnp.broadcast_to(visible_ref[...].astype(F32), (tile, rows)).astype(BF16)
        spread = lax.dot_general(
            place[...], seen, (((1,), (1,)), ((), ())), preferred_element_type=F32
        )
        send_ref[...] = spread.astype(BF16)


def project_queries(owner_row, visible_row, cand_x, w_in, columns, capacity):
    rows, width = cand_x.shape
    slots = columns * capacity
    tile = BLK
    last = width // tile
    return pl.pallas_call(
        functools.partial(query_kernel, columns, capacity, last),
        grid=(last + 1,),
        in_specs=[
            pl.BlockSpec((1, rows), lambda i: (0, 0)),
            pl.BlockSpec((1, rows), lambda i: (0, 0)),
            pl.BlockSpec((rows, width), lambda i: (0, 0)),
            pl.BlockSpec((width, tile), lambda i: (0, i)),
        ],
        out_specs=pl.BlockSpec((slots, tile), lambda i: (0, i)),
        out_shape=jax.ShapeDtypeStruct((slots, width + tile), BF16),
        scratch_shapes=[pltpu.VMEM((slots, rows), BF16)],
        compiler_params=params(60),
        cost_estimate=cost(
            2 * rows * width * width + 2 * slots * rows * width,
            2 * (rows * width + width * width + slots * width),
            rows * width,
        ),
        name="project_queries",
    )(owner_row, visible_row, cand_x, w_in)


def gate_kernel(columns, capacity, _first, _second, owner_ref, x_ref, w_ref, gate_ref, slot_ref):

    @pl.when(pl.program_id(0) == 0)
    def _():
        slot = slot_row(owner_ref[...], columns, capacity)
        slot_ref[...] = jnp.broadcast_to(slot, (BLK, slot.shape[1])).T.astype(jnp.int32)

    hidden = jnp.dot(x_ref[...], w_ref[...], preferred_element_type=F32)
    gate_ref[...] = silu(hidden).astype(BF16)


def project_gate(after, owner_row, cand_x, w_in, columns, capacity):
    rows, width = cand_x.shape
    tile = min(256, width)
    first = width // tile
    return pl.pallas_call(
        functools.partial(gate_kernel, columns, capacity),
        grid=(first,),
        in_specs=[
            pl.BlockSpec(memory_space=pl.ANY),
            pl.BlockSpec(memory_space=pl.ANY),
            pl.BlockSpec((1, rows), lambda i: (0, 0)),
            pl.BlockSpec((rows, width), lambda i: (0, 0)),
            pl.BlockSpec((width, tile), lambda i: (0, first + i)),
        ],
        out_specs=[
            pl.BlockSpec((rows, tile), lambda i: (0, i)),
            pl.BlockSpec((rows, BLK), lambda i: (0, 0)),
        ],
        out_shape=[
            jax.ShapeDtypeStruct((rows, width), BF16),
            jax.ShapeDtypeStruct((rows, BLK), jnp.int32),
        ],
        compiler_params=params(60),
        cost_estimate=cost(GATE_COST * 1e9, 2 * (2 * rows * width + width * width), rows * width),
        name="project_gate",
    )(*after, owner_row, cand_x, w_in)


def attend_kernel(heads, size, whole, behind, place_ref, *refs):
    seen_ref, refs = refs[behind], refs[behind + 1 :]
    out_ref = refs[-1]
    queries, refs = refs[:heads], refs[heads:-1]
    full, cut = refs[: 2 * whole * heads], refs[2 * whole * heads :]
    half_scale = 0.5 / math.sqrt(size)
    wide = heads * size
    seen = seen_ref[...].astype(F32)
    length = place_ref[0]
    totals = [None] * heads
    for number in range(whole + len(cut)):
        shard = place_ref[1 + number]
        if number < whole:
            parts = full[2 * number * heads : 2 * (number + 1) * heads]
            keys_of = [part[...] for part in parts[:heads]]
            values_of = [part[...] for part in parts[heads:]]
        else:
            part = cut[number - whole]
            keys_of = [part[:, h * size : (h + 1) * size] for h in range(heads)]
            values_of = [part[:, wide + h * size : wide + (h + 1) * size] for h in range(heads)]
        keys = keys_of[0].shape[0]
        row = lax.broadcasted_iota(jnp.int32, (keys, size), 0) + shard * keys
        blocks = keys // BLK
        scales = [
            jnp.where((shard * blocks + block).astype(F32) < seen, half_scale, 0.0)
            for block in range(blocks)
        ]
        for head in range(heads):
            values = jnp.where(row < length, values_of[head].astype(F32), 0.0).astype(BF16)
            scores = lax.dot_general(
                queries[head][...],
                keys_of[head],
                (((1,), (1,)), ((), ())),
                preferred_element_type=F32,
            )
            weights = []
            for block in range(blocks):
                half = scores[:, block * BLK : (block + 1) * BLK] * scales[block]
                weights.append((half * jnp.tanh(half) + half).astype(BF16))
            part = jnp.dot(
                jnp.concatenate(weights, axis=1), values, preferred_element_type=F32
            )
            totals[head] = part if totals[head] is None else totals[head] + part
    for head in range(heads):
        out_ref[:, head * size : (head + 1) * size] = totals[head].astype(BF16)


def attend(place, after, rows, full, cut, first, heads, size):
    slots, width = rows.shape[0], HEADS * size
    keys = full[0].shape[0]
    tile = min(512, slots)
    wide = heads * size
    count = len(full) + len(cut)

    def column(block, index):
        return pl.BlockSpec(block, lambda i: (0, index))

    in_specs = [
        pl.BlockSpec(memory_space=pltpu.SMEM),
        *[pl.BlockSpec(memory_space=pl.ANY) for _ in after],
        pl.BlockSpec((tile, BLK), lambda i: (i, width // BLK)),
    ]
    args = [place, *after, rows]
    for head in range(first, first + heads):
        in_specs.append(pl.BlockSpec((tile, size), lambda i, head=head: (i, head)))
        args.append(rows)
    for piece in full:
        for head in range(first, first + heads):
            in_specs.append(column((keys, size), head))
            args.append(piece)
        for head in range(first, first + heads):
            in_specs.append(column((keys, size), HEADS + head))
            args.append(piece)
    for piece in cut:
        in_specs.append(column((keys, 2 * wide), 0))
        args.append(piece)
    return pl.pallas_call(
        functools.partial(attend_kernel, heads, size, len(full), len(after)),
        grid=(slots // tile,),
        in_specs=in_specs,
        out_specs=pl.BlockSpec((tile, wide), lambda i: (i, 0)),
        out_shape=jax.ShapeDtypeStruct((slots, wide), BF16),
        compiler_params=params(60),
        cost_estimate=cost(
            4 * slots * keys * count * wide,
            2 * (2 * slots * wide + count * keys * 2 * wide),
            slots * keys * count * heads,
        ),
        name="attend",
    )(*args)


def finish_kernel(slot_ref, gain_ref, x_hbm, gate_hbm, w_hbm, *refs):
    returned = refs[:-7]
    out_hbm, x_ref, gate_ref, w_ref, out_ref, in_sems, out_sems = refs[-7:]
    loads = [
        pltpu.make_async_copy(source, target, in_sems.at[number])
        for number, (source, target) in enumerate(
            [(gate_hbm, gate_ref), (w_hbm, w_ref), (x_hbm, x_ref)]
        )
    ]
    for load in loads:
        load.start()
    rows, width = x_ref.shape
    slots = returned[0].shape[0]
    tile = rows // 2
    lane = lax.broadcasted_iota(jnp.int32, (1, BLK), 1)
    stores = []
    for half in range(2):
        span = slice(half * tile, (half + 1) * tile)
        slot = slot_ref[span, :]
        place = jnp.concatenate(
            [(lane + start == slot).astype(BF16) for start in range(0, slots, BLK)], axis=1
        )
        attn = jnp.concatenate(
            [jnp.dot(place, part[...], preferred_element_type=F32) for part in returned], axis=1
        )
        centered = attn - jnp.mean(attn, axis=1, keepdims=True)
        variance = jnp.mean(centered * centered, axis=1, keepdims=True)
        normed = (centered * lax.rsqrt(variance + norm_eps) * gain_ref[...]).astype(BF16)
        if half == 0:
            for load in loads:
                load.wait()
        mixed = (normed.astype(F32) * gate_ref[span, :].astype(F32)).astype(BF16)
        projected = jnp.dot(mixed, w_ref[...], preferred_element_type=F32)
        out_ref[span, :] = (x_ref[span, :].astype(F32) + projected).astype(BF16)
        store = pltpu.make_async_copy(out_ref.at[span, :], out_hbm.at[span, :], out_sems.at[half])
        store.start()
        stores.append(store)
    for store in stores:
        store.wait()


def finish(slot, cand_x, gate, ln_gain, w_out, returned):
    rows, width = cand_x.shape
    slots = returned[0].shape[0]
    vmem = pl.BlockSpec(memory_space=pltpu.VMEM)
    hbm = pl.BlockSpec(memory_space=pltpu.HBM)
    return pl.pallas_call(
        finish_kernel,
        in_specs=[vmem, vmem, hbm, hbm, hbm] + [vmem] * len(returned),
        out_specs=hbm,
        out_shape=jax.ShapeDtypeStruct((rows, width), BF16),
        scratch_shapes=[
            pltpu.VMEM((rows, width), BF16),
            pltpu.VMEM((rows, width), BF16),
            pltpu.VMEM((width, width), BF16),
            pltpu.VMEM((rows, width), BF16),
            pltpu.SemaphoreType.DMA((3,)),
            pltpu.SemaphoreType.DMA((2,)),
        ],
        compiler_params=params(60),
        cost_estimate=cost(
            2 * rows * width * (width + slots), 2 * (3 * rows * width + width * width + slots * width)
        ),
        name="finish",
    )(slot, ln_gain.reshape(1, width), cand_x, gate, w_out, *returned)


def swap(array, bit, count):
    return lax.ppermute(array, "user", [(i, i ^ bit) for i in range(count)])


def per_device(cand_x, cand_user, visible, hist_len, kv_cache, w_in, w_out, ln_gain):
    rows, width = cand_x.shape
    columns = lax.axis_size("cand")
    count = lax.axis_size("user")
    size = width // HEADS
    capacity = 2 * rows // columns
    slots = columns * capacity
    own = kv_cache[0]
    owner_row = cand_user.reshape(1, rows)
    visible_row = visible.reshape(1, rows)

    held = {0: own}
    bit = count // 2
    while bit > 1:
        for key in sorted(held):
            held[key | bit] = swap(held[key], bit, count)
        bit //= 2
    evens = sorted(held)
    full = [held[key] for key in evens] + [swap(own, 1, count)]
    order = evens + [1] + [key | 1 for key in evens[1:]]

    send = project_queries(owner_row, visible_row, cand_x, w_in, columns, capacity)
    got = lax.all_to_all(
        send.reshape(columns, capacity, -1), "cand", split_axis=0, concat_axis=0, tiled=True
    ).reshape(slots, -1)
    gate, slot = project_gate((full[1], full[-1]), owner_row, cand_x, w_in, columns, capacity)
    position = lax.axis_index("user").astype(jnp.int32)
    place = jnp.concatenate([hist_len, position ^ jnp.array(order, jnp.int32)])

    def forward(first, heads, behind):
        lo, hi = first * size, (first + heads) * size
        parts = [
            jnp.concatenate([held[key][:, lo:hi], held[key][:, width + lo : width + hi]], axis=1)
            for key in evens[1:]
        ]
        if behind is not None:
            parts, _ = lax.optimization_barrier((parts, behind))
        return [swap(part, 1, count) for part in parts]

    spans = [(sum(GROUPS[:number]), heads) for number, heads in enumerate(GROUPS)]
    cuts = []
    for number, (first, heads) in enumerate(spans):
        cuts.append(forward(first, heads, cuts[number - 2] if number >= 2 else None))
    returned = []
    after = [slot]
    for number, (first, heads) in enumerate(spans):
        attn = attend(place, after, got, full, cuts[number], first, heads, size)
        after = [attn] + returned[-1:]
        if number + 1 < len(spans):
            attn, _ = lax.optimization_barrier((attn, cuts[number + 1]))
        back = lax.all_to_all(
            attn.reshape(columns, capacity, heads * size),
            "cand",
            split_axis=0,
            concat_axis=0,
            tiled=True,
        )
        returned.append(back.reshape(slots, heads * size))
    return finish(slot, cand_x, gate, ln_gain, w_out, returned)


def solution(mesh):
    in_specs = (
        P(("user", "cand"), None),
        P(("user", "cand"), None),
        P(("user", "cand")),
        P("cand"),
        P("cand", "user", None),
        P(),
        P(),
        P(),
    )
    out_specs = P(("user", "cand"), None)
    return jax.shard_map(
        per_device, mesh=mesh, in_specs=in_specs, out_specs=out_specs, check_vma=False
    )
```

time: 181 us -> 128 us (0.71)
  waiting for transfers between devices: 76.5 us -> 39.2 us
  local copies, waits for them, and re-layouts: 14.6 us -> 2.36 us
  starting transfers between devices: 35 us -> 23.7 us
  Pallas kernels: 40.7 us -> 46.3 us
  blocking collectives: 11.2 us -> 13.9 us
    ppermute x12 -> x6, waiting for transfers between devices: 73.7 us -> 32.8 us  [swap(): return lax.ppermute(array, 'user', [(i, i ^ bit) for i in range(count)])]
    all_to_all x0 -> x1, blocking collectives: none -> 13.9 us  [per_device(): lax.all_to_all(attn.reshape(columns, capacity, heads * size), 'cand', spl...]
    unnamed x32 -> x22, local copies, waits for them, and re-layouts: 14.5 us -> 1.48 us
    all_gather x1 -> x0, blocking collectives: 11.2 us -> none  [per_device(): packed = lax.all_gather(packed, 'cand', axis=0, tiled=True)]
    all_to_all x5 -> x4, starting transfers between devices: 21.6 us -> 14.6 us  [the longest x3 10.8 us: per_device(): lax.all_to_all(attn.reshape(columns, capacity, heads * size), 'cand', spl...]
    ppermute x12 -> x6, starting transfers between devices: 13.4 us -> 9.02 us  [swap(): return lax.ppermute(array, 'user', [(i, i ^ bit) for i in range(count)])]
    all_to_all x5 -> x4, waiting for transfers between devices: 2.81 us -> 6.44 us  [the longest x3 6.44 us: per_device(): lax.all_to_all(attn.reshape(columns, capacity, heads * size), 'cand', spl...]
    pallas_call x7 -> x6, Pallas kernels: 38.1 us -> 41.1 us  [the longest x4 20.6 us: attend(): pl.pallas_call(functools.partial(attend_kernel, heads, size, len(full), l...]
  transfers between devices with their start and end apart: 17 -> 10, of which waited for: 12 -> 7; matrix products, arithmetic and copies ran while one was open for 1% -> 2% of each run, Pallas kernels for 16% -> 31%
where the time goes in v2:
time: 128 us; the launch traced here: 127 us
  Pallas kernels  46.3 us (36%)
  waiting for transfers between devices  39.2 us (31%)
  starting transfers between devices  23.7 us (19%)
  blocking collectives  13.9 us (11%)
  local copies, waits for them, and re-layouts  2.36 us (2%)
  other arithmetic  1.34 us (1%)
    ppermute x6, waiting for transfers between devices, swap(): return lax.ppermute(array, 'user', [(i, i ^ bit) for i in range(count)])  32.8 us
    pallas_call x4, Pallas kernels, attend(): pl.pallas_call(functools.partial(attend_kernel, heads, size, len(full), l...  20.6 us
    all_to_all x1, blocking collectives, per_device(): lax.all_to_all(attn.reshape(columns, capacity, heads * size), 'cand', spl...  13.9 us
    pallas_call x1, Pallas kernels, project_queries(): pl.pallas_call(functools.partial(query_kernel, columns, capacity, last),...  13.7 us
    all_to_all x3, starting transfers between devices, per_device(): lax.all_to_all(attn.reshape(columns, capacity, heads * size), 'cand', spl...  10.8 us
    ppermute x6, starting transfers between devices, swap(): return lax.ppermute(array, 'user', [(i, i ^ bit) for i in range(count)])  9.02 us
    pallas_call x1, Pallas kernels, finish(): pl.pallas_call(finish_kernel, in_specs=[vmem, vmem, hbm, hbm, hbm] + [vme...  6.8 us
    all_to_all x3, waiting for transfers between devices, per_device(): lax.all_to_all(attn.reshape(columns, capacity, heads * size), 'cand', spl...  6.44 us
  transfers between devices with their start and end apart: 10, of which 7 were waited for; matrix products, arithmetic and copies ran while one was open for 2% of the time, Pallas kernels for 31%

profile of v2, /device:TPU:0, one launch (start us, length us, event | category | flops | bytes accessed | tf_op | source)
XLA Modules:
  0.0 127.5 jit_solution(12536715311565074111)
XLA Ops:
  0.0 4.0 %collective-permute-start = (bf16[256,2048]{1,0:T(8,128)(2,1)}, bf16[256,2048]{1,0:T(8,128)(2,1)S(1)}, u32[]{:S(2)}, u32[]{:S(2)}) collective-permute-start(bf16[256,2048]{1,0:T(8,128)(2,1)} %bitcast.26), channel_id=1, source_target_pairs={{0,16},{8,24},{16,0},{24,8},{1,17},{9,25},{17,1},{25,9},{2,18},{10... | collective-permute-start | bytes 3145736 | tf_op jit(solution)/shard_map/ppermute | solution.py:301
  4.0 1.6 %collective-permute-start.1 = (bf16[256,2048]{1,0:T(8,128)(2,1)}, bf16[256,2048]{1,0:T(8,128)(2,1)}, u32[]{:S(2)}, u32[]{:S(2)}) collective-permute-start(bf16[256,2048]{1,0:T(8,128)(2,1)} %bitcast.27), channel_id=1, source_target_pairs={{0,8},{8,0},{16,24},{24,16},{1,9},{9,1},{17,25},{25,17},{2,10},{10... | collective-permute-start | bytes 3145736 | tf_op jit(solution)/shard_map/ppermute | solution.py:301
  5.6 13.7 %project_queries.1 = bf16[1024,1152]{1,0:T(8,128)(2,1)} custom-call(s32[1,512]{1,0:T(1,128)} %bitcast.57, s32[1,512]{1,0:T(1,128)} %bitcast.56, bf16[512,1024]{1,0:T(8,128)(2,1)} %x_hbm.1, bf16[1024,2048]{1,0:T(8,128)(2,1)} %w_ref.3), custom_call_target="tpu_custom_call" | custom-call | flops 2147483648 | bytes 5242880 | tf_op jit(solution)/shard_map/project_queries/pallas_call | solution.py:80
  19.3 0.0 copy-start.10
  19.3 3.9 %all-to-all-start = ((bf16[8,128,1152]{2,1,0:T(8,128)(2,1)}), bf16[8,128,1152]{2,1,0:T(8,128)(2,1)S(1)}, u32[]{:S(2)}, u32[]{:S(2)}) async-start(bf16[8,128,1152]{2,1,0:T(8,128)(2,1)} %bitcast.47), calls=%async_computation | async-start | bytes 4718592 | tf_op jit(solution)/shard_map/all_to_all | solution.py:326
  23.8 0.0 copy-done.10
  23.8 0.6 pad_add_fusion.place_ref
  24.4 25.6 %collective-permute-done._first.refs_8_.refs_9_.refs_10_.refs_11_.refs_12_ = bf16[256,2048]{1,0:T(8,128)(2,1)S(1)} collective-permute-done((bf16[256,2048]{1,0:T(8,128)(2,1)}, bf16[256,2048]{1,0:T(8,128)(2,1)S(1)}, u32[]{:S(2)}, u32[]{:S(2)}) %collective-permute-start) | collective-permute-done | bytes 1048608 | tf_op jit(solution)/shard_map/ppermute | solution.py:301
  50.0 0.0 copy-start.1
  50.0 0.9 fusion
  50.9 0.8 collective-permute-start.2
  51.7 0.7 pad_maximum_fusion.1
  52.4 1.3 %collective-permute-start.3 = (bf16[256,512]{1,0:T(8,128)(2,1)}, bf16[256,512]{1,0:T(8,128)(2,1)}, u32[]{:S(2)}, u32[]{:S(2)}) collective-permute-start(bf16[256,512]{1,0:T(8,128)(2,1)} %pad_maximum_fusion.1), channel_id=1, source_target_pairs={{0,8},{8,0},{16,24},{24,16},{1,9},{9,1},{17,25},{25,17},{2,10},{10... | collective-permute-start | bytes 786440 | tf_op jit(solution)/shard_map/ppermute | solution.py:301
  53.7 0.0 collective-permute-done.1._second.refs_12_.refs_13_.refs_14_.refs_15_.refs_16_
  53.7 0.0 copy-done.1
  53.7 5.2 %project_gate.1 = (bf16[512,1024]{1,0:T(8,128)(2,1)}, s32[512,128]{1,0:T(8,128)}) custom-call(bf16[256,2048]{1,0:T(8,128)(2,1)} %copy-done.1, bf16[256,2048]{1,0:T(8,128)(2,1)} %collective-permute-done.1._second.refs_12_.refs_13_.refs_14_.refs_15_.refs_16_, s32[1,512]{1,0:T(1,128)} %bitcast.58, bf16[512,1024]{1,0:T(8,128)(2,1)} %x_hbm.1, ...), custom_call_target="tpu_custom_call" | custom-call | flops 12000000000 | bytes 4194304 | tf_op jit(solution)/shard_map/project_gate/pallas_call | solution.py:117
  58.9 1.4 %collective-permute-done.2.refs_16_ = bf16[256,512]{1,0:T(8,128)(2,1)} collective-permute-done((bf16[256,512]{1,0:T(8,128)(2,1)S(1)}, bf16[256,512]{1,0:T(8,128)(2,1)}, u32[]{:S(2)}, u32[]{:S(2)}) %collective-permute-start.2) | collective-permute-done | bytes 262176 | tf_op jit(solution)/shard_map/ppermute | solution.py:301
  60.3 0.0 all-to-all-done
  60.3 0.0 copy-start
  60.3 1.4 %copy-done = bf16[8,128,1152]{2,1,0:T(8,128)(2,1)} copy-done((bf16[8,128,1152]{2,1,0:T(8,128)(2,1)}, bf16[8,128,1152]{2,1,0:T(8,128)(2,1)S(1)}, u32[]{:S(2)}) %copy-start) | copy-done | bytes 2359320
  61.7 0.0 copy-start.5
  61.8 0.0 copy-start.6
  61.8 0.0 copy-start.7
  61.8 5.2 %attend.4.refs_0_ = bf16[1024,256]{1,0:T(8,128)(2,1)} custom-call(s32[5]{0:T(128)} %pad_add_fusion.place_ref, s32[512,128]{1,0:T(8,128)} %get-tuple-element.12.refs_0_.slot_ref, bf16[1024,1152]{1,0:T(8,128)(2,1)} %bitcast.14, bf16[1024,1152]{1,0:T(8,128)(2,1)} %bitcast.15, bf16[1024,1152]{1,0:T(8,128)(2,1)} %bitcast.16, bf16[256,2048]{1,0:T(8,128)(2,1)} %bitcast.28, ...), custom_call_target="tpu_custom_call" | custom-call | flops 1073741824 | bytes 2097152 | tf_op jit(solution)/shard_map/attend/pallas_call | solution.py:217
  66.9 0.0 collective-permute-done.3.refs_16_
  66.9 3.8 %all-to-all-start.1 = ((bf16[8,128,256]{2,1,0:T(8,128)(2,1)}), bf16[8,128,256]{2,1,0:T(8,128)(2,1)S(1)}, u32[]{:S(2)}, u32[]{:S(2)}) async-start(bf16[8,128,256]{2,1,0:T(8,128)(2,1)} %bitcast.44), calls=%async_computation.1 | async-start | bytes 1048576 | tf_op jit(solution)/shard_map/all_to_all | solution.py:354
  70.7 0.0 copy-done.5
  70.7 0.0 copy-done.6
  70.7 0.0 copy-done.7
  70.8 0.7 collective-permute-start.4
  71.5 5.1 %attend.5.refs_0_ = bf16[1024,256]{1,0:T(8,128)(2,1)} custom-call(s32[5]{0:T(128)} %pad_add_fusion.place_ref, bf16[1024,256]{1,0:T(8,128)(2,1)} %attend.4.refs_0_, bf16[1024,1152]{1,0:T(8,128)(2,1)} %bitcast.17, bf16[1024,1152]{1,0:T(8,128)(2,1)} %bitcast.18, bf16[1024,1152]{1,0:T(8,128)(2,1)} %bitcast.19, bf16[256,2048]{1,0:T(8,128)(2,1)} %bitcast.32, ...), custom_call_target="tpu_custom_call" | custom-call | flops 1073741824 | bytes 2097152 | tf_op jit(solution)/shard_map/attend/pallas_call | solution.py:217
  76.6 3.0 %collective-permute-done.4.refs_17_ = bf16[256,512]{1,0:T(8,128)(2,1)S(1)} collective-permute-done((bf16[256,512]{1,0:T(8,128)(2,1)S(1)}, bf16[256,512]{1,0:T(8,128)(2,1)S(1)}, u32[]{:S(2)}, u32[]{:S(2)}) %collective-permute-start.4) | collective-permute-done | bytes 262176 | tf_op jit(solution)/shard_map/ppermute | solution.py:301
  79.6 0.0 copy-start.8
  79.6 0.9 all-to-all-done.1
  80.5 0.0 copy-start.2
  80.5 3.5 %all-to-all-start.2 = ((bf16[8,128,256]{2,1,0:T(8,128)(2,1)}), bf16[8,128,256]{2,1,0:T(8,128)(2,1)S(1)}, u32[]{:S(2)}, u32[]{:S(2)}) async-start(bf16[8,128,256]{2,1,0:T(8,128)(2,1)} %bitcast.45), calls=%async_computation.2 | async-start | bytes 1048576 | tf_op jit(solution)/shard_map/all_to_all | solution.py:354
  84.0 0.7 collective-permute-start.5
  84.6 0.0 copy-done.8
  84.6 0.0 copy-done.2
  84.6 5.1 %attend.6.refs_0_ = bf16[1024,256]{1,0:T(8,128)(2,1)} custom-call(s32[5]{0:T(128)} %pad_add_fusion.place_ref, bf16[1024,256]{1,0:T(8,128)(2,1)} %attend.5.refs_0_, bf16[1024,256]{1,0:T(8,128)(2,1)} %bitcast.48, bf16[1024,1152]{1,0:T(8,128)(2,1)} %bitcast.20, bf16[1024,1152]{1,0:T(8,128)(2,1)} %bitcast.21, bf16[1024,1152]{1,0:T(8,128)(2,1)} %bitcast.22, ...), custom_call_target="tpu_custom_call" | custom-call | flops 1073741824 | bytes 2097152 | tf_op jit(solution)/shard_map/attend/pallas_call | solution.py:217
  89.8 2.8 %collective-permute-done.5.refs_17_ = bf16[256,512]{1,0:T(8,128)(2,1)S(1)} collective-permute-done((bf16[256,512]{1,0:T(8,128)(2,1)S(1)}, bf16[256,512]{1,0:T(8,128)(2,1)S(1)}, u32[]{:S(2)}, u32[]{:S(2)}) %collective-permute-start.5) | collective-permute-done | bytes 262176 | tf_op jit(solution)/shard_map/ppermute | solution.py:301
  92.6 0.0 copy-start.9
  92.6 1.1 all-to-all-done.2
  93.7 0.0 copy-start.3
  93.7 3.5 %all-to-all-start.3 = ((bf16[8,128,256]{2,1,0:T(8,128)(2,1)}), bf16[8,128,256]{2,1,0:T(8,128)(2,1)S(1)}, u32[]{:S(2)}, u32[]{:S(2)}) async-start(bf16[8,128,256]{2,1,0:T(8,128)(2,1)} %bitcast.46), calls=%async_computation.3 | async-start | bytes 1048576 | tf_op jit(solution)/shard_map/all_to_all | solution.py:354
  97.2 0.0 copy-done.9
  97.2 0.0 copy-done.3
  97.2 5.2 %attend.7 = bf16[1024,256]{1,0:T(8,128)(2,1)} custom-call(s32[5]{0:T(128)} %pad_add_fusion.place_ref, bf16[1024,256]{1,0:T(8,128)(2,1)} %attend.6.refs_0_, bf16[1024,256]{1,0:T(8,128)(2,1)} %bitcast.50, bf16[1024,1152]{1,0:T(8,128)(2,1)} %bitcast.23, bf16[1024,1152]{1,0:T(8,128)(2,1)} %bitcast.24, bf16[1024,1152]{1,0:T(8,128)(2,1)} %bitcast.25, ...), custom_call_target="tpu_custom_call" | custom-call | flops 1073741824 | bytes 2097152 | tf_op jit(solution)/shard_map/attend/pallas_call | solution.py:217
  102.3 4.5 %all-to-all-done.3 = bf16[8,128,256]{2,1,0:T(8,128)(2,1)S(1)} async-done(((bf16[8,128,256]{2,1,0:T(8,128)(2,1)}), bf16[8,128,256]{2,1,0:T(8,128)(2,1)S(1)}, u32[]{:S(2)}, u32[]{:S(2)}) %all-to-all-start.3) | async-done | bytes 524320 | tf_op jit(solution)/shard_map/all_to_all | solution.py:354
  106.8 0.0 copy-start.4
  106.8 13.9 %all_to_all.25 = bf16[8,128,256]{2,1,0:T(8,128)(2,1)} all-to-all(bf16[8,128,256]{2,1,0:T(8,128)(2,1)} %bitcast.52), channel_id=1, replica_groups=mesh['user'=4,'cand'=8] {'cand'}, dimensions={0} | all-to-all | bytes 1048576 | tf_op jit(solution)/shard_map/all_to_all | solution.py:354
  120.7 0.0 copy-done.4
  120.7 6.8 %finish.1 = bf16[512,1024]{1,0:T(8,128)(2,1)} custom-call(s32[512,128]{1,0:T(8,128)} %get-tuple-element.12.refs_0_.slot_ref, f32[1,1024]{1,0:T(1,128)} %bitcast.55, bf16[512,1024]{1,0:T(8,128)(2,1)} %x_hbm.1, bf16[512,1024]{1,0:T(8,128)(2,1)} %get-tuple-element.13.gate_hbm, bf16[1024,1024]{1,0:T(8,128)(2,1)} %w_hbm.1, bf16[1024,256]{1,0:T(8,128)(2,1)} %bitcast.49, ...), custom_call_target="tpu_custom_call" | custom-call | flops 2147483648 | bytes 7340032 | tf_op jit(solution)/shard_map/finish/pallas_call | solution.py:279
  (3 shorter events, 0.1 us)
Async XLA Ops:
  0.0 50.0 %collective-permute-start = (bf16[256,2048]{1,0:T(8,128)(2,1)}, bf16[256,2048]{1,0:T(8,128)(2,1)S(1)}, u32[]{:S(2)}, u32[]{:S(2)}) collective-permute-start(bf16[256,2048]{1,0:T(8,128)(2,1)} %bitcast.26), channel_id=1, source_target_pairs={{0,16},{8,24},{16,0},{24,8},{1,17},{9,25},{17,1},{25,9},{2,18},{10... | collective-permute-start | bytes 3145736 | tf_op jit(solution)/shard_map/ppermute | solution.py:301
  4.0 49.7 %collective-permute-start.1 = (bf16[256,2048]{1,0:T(8,128)(2,1)}, bf16[256,2048]{1,0:T(8,128)(2,1)}, u32[]{:S(2)}, u32[]{:S(2)}) collective-permute-start(bf16[256,2048]{1,0:T(8,128)(2,1)} %bitcast.27), channel_id=1, source_target_pairs={{0,8},{8,0},{16,24},{24,16},{1,9},{9,1},{17,25},{25,17},{2,10},{10... | collective-permute-start | bytes 3145736 | tf_op jit(solution)/shard_map/ppermute | solution.py:301
  19.3 4.5 %copy-start.10 = (s32[4]{0:T(128)S(1)}, s32[4]{0:T(128)}, u32[]{:S(2)}) copy-start(s32[4]{0:T(128)} %constant.7.clone) | copy-start | bytes 52
  19.3 41.0 %all-to-all-start = ((bf16[8,128,1152]{2,1,0:T(8,128)(2,1)}), bf16[8,128,1152]{2,1,0:T(8,128)(2,1)S(1)}, u32[]{:S(2)}, u32[]{:S(2)}) async-start(bf16[8,128,1152]{2,1,0:T(8,128)(2,1)} %bitcast.47), calls=%async_computation | async-start | bytes 4718592 | tf_op jit(solution)/shard_map/all_to_all | solution.py:326
  50.0 3.7 %copy-start.1 = (bf16[256,2048]{1,0:T(8,128)(2,1)}, bf16[256,2048]{1,0:T(8,128)(2,1)S(1)}, u32[]{:S(2)}) copy-start(bf16[256,2048]{1,0:T(8,128)(2,1)S(1)} %collective-permute-done._first.refs_8_.refs_9_.refs_10_.refs_11_.refs_12_) | copy-start | bytes 3145732
  50.9 9.4 %collective-permute-start.2 = (bf16[256,512]{1,0:T(8,128)(2,1)S(1)}, bf16[256,512]{1,0:T(8,128)(2,1)}, u32[]{:S(2)}, u32[]{:S(2)}) collective-permute-start(bf16[256,512]{1,0:T(8,128)(2,1)S(1)} %pad_maximum_fusion), channel_id=1, source_target_pairs={{0,8},{8,0},{16,24},{24,16},{1,9},{9,1},{17,25},{25,17},{2,10},{10... | collective-permute-start | bytes 786440 | tf_op jit(solution)/shard_map/ppermute | solution.py:301
  52.4 14.5 %collective-permute-start.3 = (bf16[256,512]{1,0:T(8,128)(2,1)}, bf16[256,512]{1,0:T(8,128)(2,1)}, u32[]{:S(2)}, u32[]{:S(2)}) collective-permute-start(bf16[256,512]{1,0:T(8,128)(2,1)} %pad_maximum_fusion.1), channel_id=1, source_target_pairs={{0,8},{8,0},{16,24},{24,16},{1,9},{9,1},{17,25},{25,17},{2,10},{10... | collective-permute-start | bytes 786440 | tf_op jit(solution)/shard_map/ppermute | solution.py:301
  60.3 1.4 %copy-start = (bf16[8,128,1152]{2,1,0:T(8,128)(2,1)}, bf16[8,128,1152]{2,1,0:T(8,128)(2,1)S(1)}, u32[]{:S(2)}) copy-start(bf16[8,128,1152]{2,1,0:T(8,128)(2,1)S(1)} %all-to-all-done) | copy-start | bytes 7077892
  61.7 9.0 %copy-start.5 = (bf16[256,256]{1,0:T(8,128)(2,1)S(1)}, bf16[256,256]{1,0:T(8,128)(2,1)}, u32[]{:S(2)}) copy-start(bf16[256,256]{1,0:T(8,128)(2,1)} %get-tuple-element.20) | copy-start | bytes 393220
  61.8 9.0 %copy-start.6 = (bf16[256,256]{1,0:T(8,128)(2,1)S(1)}, bf16[256,256]{1,0:T(8,128)(2,1)}, u32[]{:S(2)}) copy-start(bf16[256,256]{1,0:T(8,128)(2,1)} %get-tuple-element.21) | copy-start | bytes 393220
  61.8 9.0 %copy-start.7 = (bf16[256,256]{1,0:T(8,128)(2,1)S(1)}, bf16[256,256]{1,0:T(8,128)(2,1)}, u32[]{:S(2)}) copy-start(bf16[256,256]{1,0:T(8,128)(2,1)} %get-tuple-element.22) | copy-start | bytes 393220
  66.9 13.5 %all-to-all-start.1 = ((bf16[8,128,256]{2,1,0:T(8,128)(2,1)}), bf16[8,128,256]{2,1,0:T(8,128)(2,1)S(1)}, u32[]{:S(2)}, u32[]{:S(2)}) async-start(bf16[8,128,256]{2,1,0:T(8,128)(2,1)} %bitcast.44), calls=%async_computation.1 | async-start | bytes 1048576 | tf_op jit(solution)/shard_map/all_to_all | solution.py:354
  70.8 8.8 %collective-permute-start.4 = (bf16[256,512]{1,0:T(8,128)(2,1)S(1)}, bf16[256,512]{1,0:T(8,128)(2,1)S(1)}, u32[]{:S(2)}, u32[]{:S(2)}) collective-permute-start(bf16[256,512]{1,0:T(8,128)(2,1)S(1)} %get-tuple-element.15), channel_id=1, source_target_pairs={{0,8},{8,0},{16,24},{24,16},{1,9},{9,1},{17,25},{25,17},{2,10},{10... | collective-permute-start | bytes 786440 | tf_op jit(solution)/shard_map/ppermute | solution.py:301
  79.6 5.1 %copy-start.8 = (bf16[256,512]{1,0:T(8,128)(2,1)}, bf16[256,512]{1,0:T(8,128)(2,1)S(1)}, u32[]{:S(2)}) copy-start(bf16[256,512]{1,0:T(8,128)(2,1)S(1)} %collective-permute-done.4.refs_17_) | copy-start | bytes 786436
  80.5 4.2 %copy-start.2 = (bf16[8,128,256]{2,1,0:T(8,128)(2,1)}, bf16[8,128,256]{2,1,0:T(8,128)(2,1)S(1)}, u32[]{:S(2)}) copy-start(bf16[8,128,256]{2,1,0:T(8,128)(2,1)S(1)} %all-to-all-done.1) | copy-start | bytes 1572868
  80.5 13.2 %all-to-all-start.2 = ((bf16[8,128,256]{2,1,0:T(8,128)(2,1)}), bf16[8,128,256]{2,1,0:T(8,128)(2,1)S(1)}, u32[]{:S(2)}, u32[]{:S(2)}) async-start(bf16[8,128,256]{2,1,0:T(8,128)(2,1)} %bitcast.45), calls=%async_computation.2 | async-start | bytes 1048576 | tf_op jit(solution)/shard_map/all_to_all | solution.py:354
  84.0 8.6 %collective-permute-start.5 = (bf16[256,512]{1,0:T(8,128)(2,1)S(1)}, bf16[256,512]{1,0:T(8,128)(2,1)S(1)}, u32[]{:S(2)}, u32[]{:S(2)}) collective-permute-start(bf16[256,512]{1,0:T(8,128)(2,1)S(1)} %get-tuple-element.17), channel_id=1, source_target_pairs={{0,8},{8,0},{16,24},{24,16},{1,9},{9,1},{17,25},{25,17},{2,10},{10... | collective-permute-start | bytes 786440 | tf_op jit(solution)/shard_map/ppermute | solution.py:301
  92.6 4.6 %copy-start.9 = (bf16[256,512]{1,0:T(8,128)(2,1)}, bf16[256,512]{1,0:T(8,128)(2,1)S(1)}, u32[]{:S(2)}) copy-start(bf16[256,512]{1,0:T(8,128)(2,1)S(1)} %collective-permute-done.5.refs_17_) | copy-start | bytes 786436
  93.7 3.5 %copy-start.3 = (bf16[8,128,256]{2,1,0:T(8,128)(2,1)}, bf16[8,128,256]{2,1,0:T(8,128)(2,1)S(1)}, u32[]{:S(2)}) copy-start(bf16[8,128,256]{2,1,0:T(8,128)(2,1)S(1)} %all-to-all-done.2) | copy-start | bytes 1572868
  93.7 13.2 %all-to-all-start.3 = ((bf16[8,128,256]{2,1,0:T(8,128)(2,1)}), bf16[8,128,256]{2,1,0:T(8,128)(2,1)S(1)}, u32[]{:S(2)}, u32[]{:S(2)}) async-start(bf16[8,128,256]{2,1,0:T(8,128)(2,1)} %bitcast.46), calls=%async_computation.3 | async-start | bytes 1048576 | tf_op jit(solution)/shard_map/all_to_all | solution.py:354
  106.8 13.9 %copy-start.4 = (bf16[8,128,256]{2,1,0:T(8,128)(2,1)}, bf16[8,128,256]{2,1,0:T(8,128)(2,1)S(1)}, u32[]{:S(2)}) copy-start(bf16[8,128,256]{2,1,0:T(8,128)(2,1)S(1)} %all-to-all-done.3) | copy-start | bytes 1572868

commit v3 on v2

v3 whole, which is shorter than its diff:
```python
import functools
import math

import jax
import jax.numpy as jnp
from jax import lax
from jax.experimental import pallas as pl
from jax.experimental.pallas import tpu as pltpu
from jax.sharding import PartitionSpec as P

HEADS = 8
BLK = 128
GROUPS = (3, 3, 2)
norm_eps = 1e-06
F32 = jnp.float32
BF16 = jnp.bfloat16
MIB = 1024 * 1024
BASE_COST = 4.0


def params(mib):
    return pltpu.CompilerParams(vmem_limit_bytes=mib * MIB)


def cost(flops, nbytes, transcendentals=0):
    return pl.CostEstimate(
        flops=int(flops), bytes_accessed=int(nbytes), transcendentals=int(transcendentals)
    )


def silu(v):
    half = 0.5 * v
    return half * jnp.tanh(half) + half


def earlier_mask(rows):
    first = lax.broadcasted_iota(jnp.int32, (rows, rows), 0)
    second = lax.broadcasted_iota(jnp.int32, (rows, rows), 1)
    return (first < second).astype(BF16)


def slot_row(owner_row, columns, capacity):
    rows = owner_row.shape[1]
    users = lax.broadcasted_iota(jnp.int32, (columns, rows), 0)
    mine = users == owner_row
    before = jnp.dot(mine.astype(BF16), earlier_mask(rows), preferred_element_type=F32)
    rank = jnp.sum(jnp.where(mine, before, 0.0), axis=0, keepdims=True)
    return owner_row.astype(F32) * capacity + rank


def query_kernel(columns, capacity, owner_ref, visible_ref, x_ref, w_ref, *refs):
    sends, place = refs[:-1], refs[-1]
    rows = x_ref.shape[0]
    tile = w_ref.shape[1]
    slots = columns * capacity

    @pl.when(pl.program_id(0) == 0)
    def _():
        slot = slot_row(owner_ref[...], columns, capacity).astype(jnp.int32)
        index = lax.broadcasted_iota(jnp.int32, (slots, rows), 0)
        place[...] = (index == slot).astype(BF16)

    def send(block):
        spread = jnp.dot(place[...], block, preferred_element_type=F32).astype(BF16)
        for number, ref in enumerate(sends):
            ref[...] = spread[number * capacity : (number + 1) * capacity, :]

    queries = silu(jnp.dot(x_ref[...], w_ref[...], preferred_element_type=F32)).astype(BF16)
    final = pl.program_id(0) == pl.num_programs(0) - 1

    @pl.when(jnp.logical_not(final))
    def _():
        send(queries)

    @pl.when(final)
    def _():
        seen = jnp.broadcast_to(visible_ref[...].astype(F32), (BLK, rows)).T.astype(BF16)
        send(jnp.concatenate([queries[:, : tile - BLK], seen], axis=1))


def project_queries(owner_row, visible_row, cand_x, w_in, columns, capacity):
    rows, width = cand_x.shape
    slots = columns * capacity
    steps = 3
    tile = (width + BLK) // steps
    return pl.pallas_call(
        functools.partial(query_kernel, columns, capacity),
        grid=(steps,),
        in_specs=[
            pl.BlockSpec((1, rows), lambda i: (0, 0)),
            pl.BlockSpec((1, rows), lambda i: (0, 0)),
            pl.BlockSpec((rows, width), lambda i: (0, 0)),
            pl.BlockSpec((width, tile), lambda i: (0, i)),
        ],
        out_specs=[pl.BlockSpec((capacity, tile), lambda i: (0, i))] * columns,
        out_shape=[jax.ShapeDtypeStruct((capacity, width + BLK), BF16)] * columns,
        scratch_shapes=[pltpu.VMEM((slots, rows), BF16)],
        compiler_params=params(60),
        cost_estimate=cost(
            2 * rows * width * width + 2 * slots * rows * width,
            2 * (rows * width + width * width + slots * width),
            rows * width,
        ),
        name="project_queries",
    )(owner_row, visible_row, cand_x, w_in)


def gate_kernel(columns, capacity, owner_ref, x_ref, w_ref, gate_ref, slot_ref):

    @pl.when(pl.program_id(0) == 0)
    def _():
        slot = slot_row(owner_ref[...], columns, capacity)
        slot_ref[...] = jnp.broadcast_to(slot, (BLK, slot.shape[1])).T.astype(jnp.int32)

    hidden = jnp.dot(x_ref[...], w_ref[...], preferred_element_type=F32)
    gate_ref[...] = silu(hidden).astype(BF16)


def project_gate(owner_row, cand_x, w_in, columns, capacity):
    rows, width = cand_x.shape
    tile = min(256, width)
    first = width // tile
    return pl.pallas_call(
        functools.partial(gate_kernel, columns, capacity),
        grid=(first,),
        in_specs=[
            pl.BlockSpec((1, rows), lambda i: (0, 0)),
            pl.BlockSpec((rows, width), lambda i: (0, 0)),
            pl.BlockSpec((width, tile), lambda i: (0, first + i)),
        ],
        out_specs=[
            pl.BlockSpec((rows, tile), lambda i: (0, i)),
            pl.BlockSpec((rows, BLK), lambda i: (0, 0)),
        ],
        out_shape=[
            jax.ShapeDtypeStruct((rows, width), BF16),
            jax.ShapeDtypeStruct((rows, BLK), jnp.int32),
        ],
        compiler_params=params(60),
        cost_estimate=cost(
            2 * rows * width * width, 2 * (2 * rows * width + width * width), rows * width
        ),
        name="project_gate",
    )(owner_row, cand_x, w_in)


def attend_kernel(size, behind, segments, has_base, outs, place_ref, *refs):
    refs = refs[behind:]
    seen_ref, query_ref, refs = refs[0], refs[1], refs[2:]
    parts, refs = refs[: 2 * segments], refs[2 * segments :]
    base_ref = refs[0] if has_base else None
    out_refs, scales = refs[-1 - outs : -1], refs[-1]
    slots = query_ref.shape[0]
    keys = parts[0].shape[0]
    blocks = keys // BLK

    @pl.when(pl.program_id(0) == 0)
    def _():
        seen = seen_ref[...].astype(F32)
        for number in range(segments):
            for block in range(blocks):
                first = (place_ref[1 + number] * blocks + block).astype(F32)
                scales[number * blocks + block] = jnp.where(
                    first < seen, 0.5 / math.sqrt(size), 0.0
                )

    row = lax.broadcasted_iota(jnp.int32, (keys, size), 0)
    values = []
    for number in range(segments):
        shown = row + place_ref[1 + number] * keys < place_ref[0]
        value = parts[2 * number + 1][...].astype(F32)
        values.append(jnp.where(shown, value, 0.0).astype(BF16))
    values = jnp.concatenate(values, axis=0)
    tile = min(256, slots)
    results = []
    for start in range(0, slots, tile):
        span = slice(start, start + tile)
        weights = []
        for number in range(segments):
            scores = lax.dot_general(
                query_ref[span, :],
                parts[2 * number][...],
                (((1,), (1,)), ((), ())),
                preferred_element_type=F32,
            )
            for block in range(blocks):
                half = scores[:, block * BLK : (block + 1) * BLK]
                half = half * scales[number * blocks + block, span, :]
                weights.append((half * jnp.tanh(half) + half).astype(BF16))
        total = jnp.dot(
            jnp.concatenate(weights, axis=1), values, preferred_element_type=F32
        )
        if has_base:
            total = total + base_ref[span, :]
        results.append(total)
    capacity = slots // outs
    for number, ref in enumerate(out_refs):
        start = number * capacity
        piece = results[start // tile][start % tile : start % tile + capacity, :]
        if outs == 1:
            piece = jnp.concatenate(results, axis=0)
        ref[...] = piece.astype(ref.dtype)


def attend(place, after, rows, segments, base, first, heads, size, outs, dtype, share=1.0):
    slots, width = rows.shape[0], HEADS * size
    keys = segments[0][0].shape[0]
    capacity = slots // outs
    count = len(segments)

    def column(height, index):
        return pl.BlockSpec((height, size), lambda i: (0, index + i))

    in_specs = [
        pl.BlockSpec(memory_space=pltpu.SMEM),
        *[pl.BlockSpec(memory_space=pl.ANY) for _ in after],
        pl.BlockSpec((slots, BLK), lambda i: (0, width // BLK)),
        column(slots, first),
    ]
    args = [place, *after, rows, rows]
    for piece, key, value in segments:
        in_specs += [column(keys, key), column(keys, value)]
        args += [piece, piece]
    if base is not None:
        in_specs.append(column(slots, first))
        args.append(base)
    return pl.pallas_call(
        functools.partial(attend_kernel, size, len(after), count, base is not None, outs),
        grid=(heads,),
        in_specs=in_specs,
        out_specs=[column(capacity, 0)] * outs,
        out_shape=[jax.ShapeDtypeStruct((capacity, heads * size), dtype)] * outs,
        scratch_shapes=[pltpu.VMEM((count * (keys // BLK), slots, BLK), F32)],
        compiler_params=params(60),
        cost_estimate=cost(
            share * 4 * slots * keys * count * heads * size,
            2 * (2 * slots + count * keys * 2) * heads * size,
            slots * keys * count * heads,
        ),
        name="attend",
    )(*args)


def placement(slot, slots):
    lane = lax.broadcasted_iota(jnp.int32, (1, BLK), 1)
    return jnp.concatenate(
        [(lane + start == slot).astype(BF16) for start in range(0, slots, BLK)], axis=1
    )


def collect_kernel(groups, slot_ref, *refs):
    parts, out_ref = refs[:-1], refs[-1]
    each = len(parts) // groups
    place = placement(slot_ref[...], each * parts[0].shape[0])
    first = 0
    for group in range(groups):
        rows = jnp.concatenate(
            [part[...] for part in parts[group * each : (group + 1) * each]], axis=0
        )
        last = first + rows.shape[1]
        out_ref[:, first:last] = jnp.dot(place, rows, preferred_element_type=F32).astype(BF16)
        first = last


def collect(slot, groups):
    rows = slot.shape[0]
    parts = [part for group in groups for part in group]
    width = sum(group[0].shape[1] for group in groups)
    slots = len(groups[0]) * groups[0][0].shape[0]
    vmem = pl.BlockSpec(memory_space=pltpu.VMEM)
    return pl.pallas_call(
        functools.partial(collect_kernel, len(groups)),
        in_specs=[vmem] * (1 + len(parts)),
        out_specs=vmem,
        out_shape=jax.ShapeDtypeStruct((rows, width), BF16),
        compiler_params=params(60),
        cost_estimate=cost(2 * rows * slots * width, 2 * (rows + slots) * width),
        name="collect",
    )(slot, *parts)


def finish_kernel(pieces, gain_ref, slot_hbm, early_hbm, gate_hbm, x_hbm, w_hbm, *refs):
    parts, refs = refs[:pieces], refs[pieces:]
    out_hbm, slot_ref, early_ref, gate_ref, x_ref, w_ref, rows_ref, out_ref = refs[:8]
    sems, out_sems = refs[8:]
    capacity = parts[0].shape[0]
    moves = [(slot_hbm, slot_ref)]
    for number, part in enumerate(parts):
        moves.append((part, rows_ref.at[number * capacity : (number + 1) * capacity, :]))
    needed = len(moves)
    for source, target in ((early_hbm, early_ref), (gate_hbm, gate_ref), (w_hbm, w_ref), (x_hbm, x_ref)):
        step = source.shape[0] // 4
        for quarter in range(4):
            span = slice(quarter * step, (quarter + 1) * step)
            moves.append((source.at[span, :], target.at[span, :]))
    loads = [
        pltpu.make_async_copy(source, target, sems.at[number])
        for number, (source, target) in enumerate(moves)
    ]
    for load in loads:
        load.start()
    for load in loads[:needed]:
        load.wait()
    rows = x_ref.shape[0]
    slots = rows_ref.shape[0]
    late = jnp.dot(placement(slot_ref[...], slots), rows_ref[...], preferred_element_type=F32)
    for load in loads[needed:]:
        load.wait()
    tile = rows // 2
    stores = []
    for half in range(2):
        span = slice(half * tile, (half + 1) * tile)
        attn = jnp.concatenate([early_ref[span, :].astype(F32), late[span, :]], axis=1)
        centered = attn - jnp.mean(attn, axis=1, keepdims=True)
        variance = jnp.mean(centered * centered, axis=1, keepdims=True)
        normed = (centered * lax.rsqrt(variance + norm_eps) * gain_ref[...]).astype(BF16)
        mixed = (normed.astype(F32) * gate_ref[span, :].astype(F32)).astype(BF16)
        projected = jnp.dot(mixed, w_ref[...], preferred_element_type=F32)
        out_ref[span, :] = (x_ref[span, :].astype(F32) + projected).astype(BF16)
        store = pltpu.make_async_copy(out_ref.at[span, :], out_hbm.at[span, :], out_sems.at[half])
        store.start()
        stores.append(store)
    for store in stores:
        store.wait()


def finish(slot, early, gate, cand_x, ln_gain, w_out, parts):
    rows, width = cand_x.shape
    capacity, wide = parts[0].shape
    slots = len(parts) * capacity
    vmem = pl.BlockSpec(memory_space=pltpu.VMEM)
    anywhere = pl.BlockSpec(memory_space=pl.ANY)
    return pl.pallas_call(
        functools.partial(finish_kernel, len(parts)),
        in_specs=[vmem] + [anywhere] * (5 + len(parts)),
        out_specs=anywhere,
        out_shape=jax.ShapeDtypeStruct((rows, width), BF16),
        scratch_shapes=[
            pltpu.VMEM(slot.shape, jnp.int32),
            pltpu.VMEM(early.shape, BF16),
            pltpu.VMEM((rows, width), BF16),
            pltpu.VMEM((rows, width), BF16),
            pltpu.VMEM((width, width), BF16),
            pltpu.VMEM((slots, wide), BF16),
            pltpu.VMEM((rows, width), BF16),
            pltpu.SemaphoreType.DMA((len(parts) + 17,)),
            pltpu.SemaphoreType.DMA((2,)),
        ],
        compiler_params=params(60),
        cost_estimate=cost(
            2 * rows * width * (width + slots), 2 * (3 * rows * width + width * width + slots * width)
        ),
        name="finish",
    )(ln_gain.reshape(1, width), slot, early, gate, cand_x, w_out, *parts)


def swap(array, axis, bits, count):
    return lax.ppermute(array, axis, [(i, i ^ bits) for i in range(count)])


def exchange(blocks):
    count = len(blocks)
    return [block if d == 0 else swap(block, "cand", d, count) for d, block in enumerate(blocks)]


def per_device(cand_x, cand_user, visible, hist_len, kv_cache, w_in, w_out, ln_gain):
    rows, width = cand_x.shape
    columns = lax.axis_size("cand")
    count = lax.axis_size("user")
    size = width // HEADS
    capacity = 2 * rows // columns
    own = kv_cache[0]
    owner_row = cand_user.reshape(1, rows) ^ lax.axis_index("cand").astype(jnp.int32)
    visible_row = visible.reshape(1, rows)

    held = {0: own}
    bit = count // 2
    while bit > 1:
        for key in sorted(held):
            held[key | bit] = swap(held[key], "user", bit, count)
        bit //= 2
    evens = sorted(held)
    near = swap(own, "user", 1, count)

    send = project_queries(owner_row, visible_row, cand_x, w_in, columns, capacity)
    got = jnp.concatenate(exchange(send), axis=0)
    gate, slot = project_gate(owner_row, cand_x, w_in, columns, capacity)
    position = lax.axis_index("user").astype(jnp.int32)
    order = evens[1:] + [key | 1 for key in evens[1:]]
    place_first = jnp.concatenate([hist_len, position ^ jnp.array([0, 1], jnp.int32)])
    place = jnp.concatenate([hist_len, position ^ jnp.array(order, jnp.int32)])
    base = attend(
        place_first,
        [slot, held[evens[-1]]],
        got,
        [(own, 0, HEADS), (near, 0, HEADS)],
        None,
        0,
        HEADS,
        size,
        1,
        F32,
        BASE_COST,
    )[0]

    def forward(first, heads, behind):
        lo, hi = first * size, (first + heads) * size
        parts = [
            jnp.concatenate([held[key][:, lo:hi], held[key][:, width + lo : width + hi]], axis=1)
            for key in evens[1:]
        ]
        if behind is not None:
            parts, _ = lax.optimization_barrier((parts, behind))
        return [swap(part, "user", 1, count) for part in parts]

    spans = [(sum(GROUPS[:number]), heads) for number, heads in enumerate(GROUPS)]
    cuts = [forward(*spans[0], None)]
    returned = []
    after = []
    done = base
    for number, (first, heads) in enumerate(spans):
        if number + 1 < len(spans):
            cuts.append(forward(*spans[number + 1], (cuts[number], done)))
        segments = [(held[key], first, HEADS + first) for key in evens[1:]]
        segments += [(cut, 0, heads) for cut in cuts[number]]
        attn = attend(place, after, got, segments, base, first, heads, size, columns, BF16)
        done = attn[0]
        after = [attn[0]] + [group[-1] for group in returned[-1:]]
        returned.append(exchange(attn))
    early = collect(slot, returned[:-1])
    return finish(slot, early, gate, cand_x, ln_gain, w_out, returned[-1])


def solution(mesh):
    in_specs = (
        P(("user", "cand"), None),
        P(("user", "cand"), None),
        P(("user", "cand")),
        P("cand"),
        P("cand", "user", None),
        P(),
        P(),
        P(),
    )
    out_specs = P(("user", "cand"), None)
    return jax.shard_map(
        per_device, mesh=mesh, in_specs=in_specs, out_specs=out_specs, check_vma=False
    )
```

time: 128 us -> 123 us (0.961)
  blocking collectives: 13.9 us -> 0 us
  waiting for transfers between devices: 39.2 us -> 26.6 us
  starting transfers between devices: 23.7 us -> 34.6 us
  Pallas kernels: 46.3 us -> 50 us
  other arithmetic: 1.34 us -> 4.47 us
  local copies, waits for them, and re-layouts: 2.36 us -> 5.41 us
    ppermute x6 -> x33, starting transfers between devices: 9.02 us -> 34.6 us  [swap(): return lax.ppermute(array, axis, [(i, i ^ bits) for i in range(count)])]
    all_to_all x4 -> x0, starting transfers between devices: 14.6 us -> none  [the longest x3 10.8 us: per_device(): lax.all_to_all(attn.reshape(columns, capacity, heads * size), 'cand', spl...]
    all_to_all x1 -> x0, blocking collectives: 13.9 us -> none  [per_device(): lax.all_to_all(attn.reshape(columns, capacity, heads * size), 'cand', spl...]
    all_to_all x4 -> x0, waiting for transfers between devices: 6.44 us -> none  [the longest x3 6.44 us: per_device(): lax.all_to_all(attn.reshape(columns, capacity, heads * size), 'cand', spl...]
    ppermute x6 -> x33, waiting for transfers between devices: 32.8 us -> 26.6 us  [swap(): return lax.ppermute(array, axis, [(i, i ^ bits) for i in range(count)])]
    pallas_call x6 -> x7, Pallas kernels: 41.1 us -> 44.8 us  [the longest x4 27.3 us: attend(): pl.pallas_call(functools.partial(attend_kernel, size, len(after), count,...]
    unnamed x22 -> x61, local copies, waits for them, and re-layouts: 1.48 us -> 3.49 us
  transfers between devices with their start and end apart: 10 -> 33, of which waited for: 7 -> 6; matrix products, arithmetic and copies ran while one was open for 2% -> 7% of each run, Pallas kernels for 31% -> 36%
where the time goes in v3:
time: 123 us; the launch traced here: 122 us
  Pallas kernels  50 us (41%)
  starting transfers between devices  34.6 us (28%)
  waiting for transfers between devices  26.6 us (22%)
  local copies, waits for them, and re-layouts  5.41 us (4%)
  other arithmetic  4.47 us (4%)
  between operations  1.26 us (1%)
    ppermute x33, starting transfers between devices, swap(): return lax.ppermute(array, axis, [(i, i ^ bits) for i in range(count)])  34.6 us
    pallas_call x4, Pallas kernels, attend(): pl.pallas_call(functools.partial(attend_kernel, size, len(after), count,...  27.3 us
    ppermute x33, waiting for transfers between devices, swap(): return lax.ppermute(array, axis, [(i, i ^ bits) for i in range(count)])  26.6 us
    pallas_call x1, Pallas kernels, project_queries(): pl.pallas_call(functools.partial(query_kernel, columns, capacity), grid=(...  7.52 us
    pallas_call x1, Pallas kernels, finish(): pl.pallas_call(functools.partial(finish_kernel, len(parts)), in_specs=[vm...  6.39 us
    pallas_call x1, Pallas kernels, project_gate(): pl.pallas_call(functools.partial(gate_kernel, columns, capacity), grid=(f...  5.2 us
    pallas_call x1, Pallas kernels, collect(): pl.pallas_call(functools.partial(collect_kernel, len(groups)), in_specs=[...  3.68 us
    unnamed x61, local copies, waits for them, and re-layouts  3.49 us
  transfers between devices with their start and end apart: 33, of which 6 were waited for; matrix products, arithmetic and copies ran while one was open for 7% of the time, Pallas kernels for 36%

profile of v3, /device:TPU:0, one launch (start us, length us, event | category | flops | bytes accessed | tf_op | source)
XLA Modules:
  0.0 122.4 jit_solution(16114315982384357581)
XLA Ops:
  0.0 3.0 %collective-permute-start.9 = (bf16[256,2048]{1,0:T(8,128)(2,1)}, bf16[256,2048]{1,0:T(8,128)(2,1)}, u32[]{:S(2)}, u32[]{:S(2)}) collective-permute-start(bf16[256,2048]{1,0:T(8,128)(2,1)} %bitcast.5), channel_id=1, source_target_pairs={{0,8},{8,0},{16,24},{24,16},{1,9},{9,1},{17,25},{25,17},{2,10},{10... | collective-permute-start | bytes 3145736 | tf_op jit(solution)/shard_map/ppermute | solution.py:358
  3.0 2.6 %collective-permute-start.7 = (bf16[256,2048]{1,0:T(8,128)(2,1)}, bf16[256,2048]{1,0:T(8,128)(2,1)S(1)}, u32[]{:S(2)}, u32[]{:S(2)}) collective-permute-start(bf16[256,2048]{1,0:T(8,128)(2,1)} %bitcast.6), channel_id=1, source_target_pairs={{0,16},{8,24},{16,0},{24,8},{1,17},{9,25},{17,1},{25,9},{2,18},{10... | collective-permute-start | bytes 3145736 | tf_op jit(solution)/shard_map/ppermute | solution.py:358
  5.6 1.3 %xor_bitcast_fusion.owner_ref = s32[1,512]{1,0:T(1,128)} fusion(s32[512,1]{0,1:T(1,128)} %param.11, s32[]{:T(128)S(6)} %axis_index.22), kind=kLoop, calls=%fused_computation.11 | loop fusion | flops 512 | bytes 4100 | tf_op jit(solution)/shard_map/xor | solution.py:373
  6.9 7.5 %project_queries.1 = (bf16[128,1152]{1,0:T(8,128)(2,1)}, bf16[128,1152]{1,0:T(8,128)(2,1)}, bf16[128,1152]{1,0:T(8,128)(2,1)}, bf16[128,1152]{1,0:T(8,128)(2,1)}...) custom-call(s32[1,512]{1,0:T(1,128)} %xor_bitcast_fusion.owner_ref, ...), custom_call_target="tpu_custom_call" | custom-call | flops 2147483648 | bytes 5242880 | tf_op jit(solution)/shard_map/project_queries/pallas_call | solution.py:86
  14.4 0.1 collective-permute-start
  14.5 1.6 %collective-permute-start.1 = (bf16[128,1152]{1,0:T(8,128)(2,1)}, bf16[128,1152]{1,0:T(8,128)(2,1)S(1)}, u32[]{:S(2)}, u32[]{:S(2)}) collective-permute-start(bf16[128,1152]{1,0:T(8,128)(2,1)} %get-tuple-element.44), channel_id=1, source_target_pairs={{0,2},{1,3},{2,0},{3,1},{4,6},{5,7},{6,4},{7,5},{8,10},{9,11},{10,... | collective-permute-start | bytes 884744 | tf_op jit(solution)/shard_map/ppermute | solution.py:358
  16.0 0.3 collective-permute-start.2
  17.0 0.6 pad_add_fusion.place_ref
  17.6 0.7 pad_add_fusion.1.place_ref
  18.3 1.0 constant_dynamic-update-slice_fusion.7
  19.2 5.2 %project_gate.1 = (bf16[512,1024]{1,0:T(8,128)(2,1)}, s32[512,128]{1,0:T(8,128)}) custom-call(s32[1,512]{1,0:T(1,128)} %xor_bitcast_fusion.owner_ref, bf16[512,1024]{1,0:T(8,128)(2,1)} %x_hbm.1, bf16[1024,2048]{1,0:T(8,128)(2,1)} %w_ref.3), custom_call_target="tpu_custom_call" | custom-call | flops 1073741824 | bytes 4194304 | tf_op jit(solution)/shard_map/project_gate/pallas_call | solution.py:123
  24.4 1.5 %collective-permute-start.3 = (bf16[128,1152]{1,0:T(8,128)(2,1)}, bf16[128,1152]{1,0:T(8,128)(2,1)S(1)}, u32[]{:S(2)}, u32[]{:S(2)}) collective-permute-start(bf16[128,1152]{1,0:T(8,128)(2,1)} %get-tuple-element.46), channel_id=1, source_target_pairs={{0,4},{1,5},{2,6},{3,7},{4,0},{5,1},{6,2},{7,3},{8,12},{9,13},{10,... | collective-permute-start | bytes 884744 | tf_op jit(solution)/shard_map/ppermute | solution.py:358
  26.0 1.0 constant_dynamic-update-slice_fusion.6
  27.0 0.0 collective-permute-done.1
  27.0 0.2 collective-permute-start.4
  27.2 2.7 %collective-permute-done.2 = bf16[128,1152]{1,0:T(8,128)(2,1)S(1)} collective-permute-done((bf16[128,1152]{1,0:T(8,128)(2,1)}, bf16[128,1152]{1,0:T(8,128)(2,1)S(1)}, u32[]{:S(2)}, u32[]{:S(2)}) %collective-permute-start.2) | collective-permute-done | bytes 294944 | tf_op jit(solution)/shard_map/ppermute | solution.py:358
  30.0 2.4 %collective-permute-start.5 = (bf16[128,1152]{1,0:T(8,128)(2,1)}, bf16[128,1152]{1,0:T(8,128)(2,1)S(1)}, u32[]{:S(2)}, u32[]{:S(2)}) collective-permute-start(bf16[128,1152]{1,0:T(8,128)(2,1)} %get-tuple-element.48), channel_id=1, source_target_pairs={{0,6},{1,7},{2,4},{3,5},{4,2},{5,3},{6,0},{7,1},{8,14},{9,15},{10,... | collective-permute-start | bytes 884744 | tf_op jit(solution)/shard_map/ppermute | solution.py:358
  32.4 8.4 %collective-permute-done.3 = bf16[128,1152]{1,0:T(8,128)(2,1)S(1)} collective-permute-done((bf16[128,1152]{1,0:T(8,128)(2,1)}, bf16[128,1152]{1,0:T(8,128)(2,1)S(1)}, u32[]{:S(2)}, u32[]{:S(2)}) %collective-permute-start.3) | collective-permute-done | bytes 294944 | tf_op jit(solution)/shard_map/ppermute | solution.py:358
  40.8 11.5 %collective-permute-done.4 = bf16[128,1152]{1,0:T(8,128)(2,1)S(1)} collective-permute-done((bf16[128,1152]{1,0:T(8,128)(2,1)}, bf16[128,1152]{1,0:T(8,128)(2,1)S(1)}, u32[]{:S(2)}, u32[]{:S(2)}) %collective-permute-start.4) | collective-permute-done | bytes 294944 | tf_op jit(solution)/shard_map/ppermute | solution.py:358
  52.4 0.0 collective-permute-done.6
  52.4 0.0 collective-permute-done.7.refs_1_.refs_2_.refs_3_.refs_4_.refs_5_
  52.5 0.0 copy-start.1
  52.5 0.9 fusion.1
  53.4 1.0 pad_maximum_fusion
  54.4 0.5 collective-permute-start.8
  54.8 0.0 collective-permute-done.9.refs_6_.refs_7_
  54.9 11.4 %attend.4.refs_6_.refs_7_.refs_8_ = f32[1024,1024]{1,0:T(8,128)} custom-call(s32[3]{0:T(128)} %pad_add_fusion.1.place_ref, s32[512,128]{1,0:T(8,128)} %get-tuple-element.41.refs_0_.slot_ref.slot_hbm, bf16[256,2048]{1,0:T(8,128)(2,1)} %copy-done.1, bf16[1024,1152]{1,0:T(8,128)(2,1)} %copy-done, bf16[1024,1152]{1,0:T(8,128)(2,1)} %copy-done, ...), custom_call_target="tpu_custom_call" | custom-call | flops 8589934592 | bytes 6291456 | tf_op jit(solution)/shard_map/attend/pallas_call | solution.py:227
  66.3 1.0 pad_maximum_fusion.1
  67.3 0.0 collective-permute-done.8.refs_4_.refs_5_
  67.3 1.6 %collective-permute-start.17 = (bf16[256,768]{1,0:T(8,128)(2,1)S(1)}, bf16[256,768]{1,0:T(8,128)(2,1)S(1)}, u32[]{:S(2)}, u32[]{:S(2)}) collective-permute-start(bf16[256,768]{1,0:T(8,128)(2,1)S(1)} %pad_maximum_fusion.1), channel_id=1, source_target_pairs={{0,8},{8,0},{16,24},{24,16},{1,9},{9,1},{17,25},{25,17},{2,10},{10... | collective-permute-start | bytes 1179656 | tf_op jit(solution)/shard_map/ppermute | solution.py:358
  68.9 1.0 fusion
  69.9 5.7 %attend.5 = (bf16[128,384]{1,0:T(8,128)(2,1)}, bf16[128,384]{1,0:T(8,128)(2,1)}, bf16[128,384]{1,0:T(8,128)(2,1)}, bf16[128,384]{1,0:T(8,128)(2,1)}, bf16[128,38...) custom-call(s32[3]{0:T(128)} %pad_add_fusion.place_ref, ...), custom_call_target="tpu_custom_call" | custom-call | flops 805306368 | bytes 2359296 | tf_op jit(solution)/shard_map/attend/pallas_call | solution.py:227
  75.6 0.1 collective-permute-start.10
  75.7 1.6 %collective-permute-start.11 = (bf16[128,384]{1,0:T(8,128)(2,1)}, bf16[128,384]{1,0:T(8,128)(2,1)S(1)}, u32[]{:S(2)}, u32[]{:S(2)}) collective-permute-start(bf16[128,384]{1,0:T(8,128)(2,1)} %get-tuple-element.52), channel_id=1, source_target_pairs={{0,2},{1,3},{2,0},{3,1},{4,6},{5,7},{6,4},{7,5},{8,10},{9,11},{10,... | collective-permute-start | bytes 294920 | tf_op jit(solution)/shard_map/ppermute | solution.py:358
  77.2 0.3 collective-permute-start.12
  77.6 0.9 collective-permute-done.17.refs_5_.refs_6_
  78.4 1.6 %collective-permute-start.25 = (bf16[256,512]{1,0:T(8,128)(2,1)S(1)}, bf16[256,512]{1,0:T(8,128)(2,1)S(1)}, u32[]{:S(2)}, u32[]{:S(2)}) collective-permute-start(bf16[256,512]{1,0:T(8,128)(2,1)S(1)} %pad_maximum_fusion.2), channel_id=1, source_target_pairs={{0,8},{8,0},{16,24},{24,16},{1,9},{9,1},{17,25},{25,17},{2,10},{10... | collective-permute-start | bytes 786440 | tf_op jit(solution)/shard_map/ppermute | solution.py:358
  80.0 1.5 %collective-permute-start.13 = (bf16[128,384]{1,0:T(8,128)(2,1)}, bf16[128,384]{1,0:T(8,128)(2,1)S(1)}, u32[]{:S(2)}, u32[]{:S(2)}) collective-permute-start(bf16[128,384]{1,0:T(8,128)(2,1)} %get-tuple-element.54), channel_id=1, source_target_pairs={{0,4},{1,5},{2,6},{3,7},{4,0},{5,1},{6,2},{7,3},{8,12},{9,13},{10,... | collective-permute-start | bytes 294920 | tf_op jit(solution)/shard_map/ppermute | solution.py:358
  81.6 0.0 collective-permute-done.11.refs_2_
  81.6 2.4 %collective-permute-start.15 = (bf16[128,384]{1,0:T(8,128)(2,1)}, bf16[128,384]{1,0:T(8,128)(2,1)S(1)}, u32[]{:S(2)}, u32[]{:S(2)}) collective-permute-start(bf16[128,384]{1,0:T(8,128)(2,1)} %get-tuple-element.56), channel_id=1, source_target_pairs={{0,6},{1,7},{2,4},{3,5},{4,2},{5,3},{6,0},{7,1},{8,14},{9,15},{10,... | collective-permute-start | bytes 294920 | tf_op jit(solution)/shard_map/ppermute | solution.py:358
  84.0 1.4 %collective-permute-start.16 = (bf16[128,384]{1,0:T(8,128)(2,1)}, bf16[128,384]{1,0:T(8,128)(2,1)S(1)}, u32[]{:S(2)}, u32[]{:S(2)}) collective-permute-start(bf16[128,384]{1,0:T(8,128)(2,1)} %get-tuple-element.57), channel_id=1, source_target_pairs={{0,7},{1,6},{2,5},{3,4},{4,3},{5,2},{6,1},{7,0},{8,15},{9,14},{10,... | collective-permute-start | bytes 294920 | tf_op jit(solution)/shard_map/ppermute | solution.py:358
  85.3 5.7 %attend.6 = (bf16[128,384]{1,0:T(8,128)(2,1)}, bf16[128,384]{1,0:T(8,128)(2,1)}, bf16[128,384]{1,0:T(8,128)(2,1)}, bf16[128,384]{1,0:T(8,128)(2,1)}, bf16[128,38...) custom-call(s32[3]{0:T(128)} %pad_add_fusion.place_ref, ...), custom_call_target="tpu_custom_call" | custom-call | flops 805306368 | bytes 2359296 | tf_op jit(solution)/shard_map/attend/pallas_call | solution.py:227
  91.1 0.0 collective-permute-done.13.refs_4_
  91.1 0.1 collective-permute-start.18
  91.2 1.4 %collective-permute-start.19 = (bf16[128,384]{1,0:T(8,128)(2,1)}, bf16[128,384]{1,0:T(8,128)(2,1)S(1)}, u32[]{:S(2)}, u32[]{:S(2)}) collective-permute-start(bf16[128,384]{1,0:T(8,128)(2,1)} %get-tuple-element.61), channel_id=1, source_target_pairs={{0,2},{1,3},{2,0},{3,1},{4,6},{5,7},{6,4},{7,5},{8,10},{9,11},{10,... | collective-permute-start | bytes 294920 | tf_op jit(solution)/shard_map/ppermute | solution.py:358
  92.6 0.4 collective-permute-start.20
  93.0 0.8 collective-permute-start.21
  93.8 0.9 collective-permute-start.22
  94.7 2.3 %collective-permute-done.19.refs_10_ = bf16[128,384]{1,0:T(8,128)(2,1)S(1)} collective-permute-done((bf16[128,384]{1,0:T(8,128)(2,1)}, bf16[128,384]{1,0:T(8,128)(2,1)S(1)}, u32[]{:S(2)}, u32[]{:S(2)}) %collective-permute-start.19) | collective-permute-done | bytes 98336 | tf_op jit(solution)/shard_map/ppermute | solution.py:358
  97.1 1.6 %collective-permute-start.23 = (bf16[128,384]{1,0:T(8,128)(2,1)}, bf16[128,384]{1,0:T(8,128)(2,1)S(1)}, u32[]{:S(2)}, u32[]{:S(2)}) collective-permute-start(bf16[128,384]{1,0:T(8,128)(2,1)} %get-tuple-element.65), channel_id=1, source_target_pairs={{0,6},{1,7},{2,4},{3,5},{4,2},{5,3},{6,0},{7,1},{8,14},{9,15},{10,... | collective-permute-start | bytes 294920 | tf_op jit(solution)/shard_map/ppermute | solution.py:358
  98.6 0.7 copy-done.4
  99.3 4.5 %attend.7 = (bf16[128,256]{1,0:T(8,128)(2,1)}, bf16[128,256]{1,0:T(8,128)(2,1)}, bf16[128,256]{1,0:T(8,128)(2,1)}, bf16[128,256]{1,0:T(8,128)(2,1)}, bf16[128,25...) custom-call(s32[3]{0:T(128)} %pad_add_fusion.place_ref, ...), custom_call_target="tpu_custom_call" | custom-call | flops 536870912 | bytes 1572864 | tf_op jit(solution)/shard_map/attend/pallas_call | solution.py:227
  103.8 0.0 copy-start.14
  103.8 0.8 collective-permute-start.26
  104.7 1.4 %collective-permute-start.27 = (bf16[128,256]{1,0:T(8,128)(2,1)}, bf16[128,256]{1,0:T(8,128)(2,1)S(1)}, u32[]{:S(2)}, u32[]{:S(2)}) collective-permute-start(bf16[128,256]{1,0:T(8,128)(2,1)} %get-tuple-element.71), channel_id=1, source_target_pairs={{0,2},{1,3},{2,0},{3,1},{4,6},{5,7},{6,4},{7,5},{8,10},{9,11},{10,... | collective-permute-start | bytes 196616 | tf_op jit(solution)/shard_map/ppermute | solution.py:358
  106.1 0.1 collective-permute-start.28
  106.1 0.9 collective-permute-start.29
  107.0 1.1 collective-permute-start.30
  108.2 1.6 %collective-permute-start.31 = (bf16[128,256]{1,0:T(8,128)(2,1)}, bf16[128,256]{1,0:T(8,128)(2,1)S(1)}, u32[]{:S(2)}, u32[]{:S(2)}) collective-permute-start(bf16[128,256]{1,0:T(8,128)(2,1)} %get-tuple-element.75), channel_id=1, source_target_pairs={{0,6},{1,7},{2,4},{3,5},{4,2},{5,3},{6,0},{7,1},{8,14},{9,15},{10,... | collective-permute-start | bytes 196616 | tf_op jit(solution)/shard_map/ppermute | solution.py:358
  109.8 0.8 collective-permute-start.32
  110.7 3.7 %collect.1.early_hbm = bf16[512,768]{1,0:T(8,128)(2,1)} custom-call(s32[512,128]{1,0:T(8,128)} %get-tuple-element.41.refs_0_.slot_ref.slot_hbm, bf16[128,384]{1,0:T(8,128)(2,1)} %get-tuple-element.50.refs_0_, bf16[128,384]{1,0:T(8,128)(2,1)} %copy-done.6, bf16[128,384]{1,0:T(8,128)(2,1)} %copy-done.7, bf16[128,384]{1,0:T(8,128)(2,1)} %copy-done.8, ...), custom_call_target="tpu_custom_call" | custom-call | flops 805306368 | bytes 2359296 | tf_op jit(solution)/shard_map/collect/pallas_call | solution.py:271
  114.4 0.8 collective-permute-done.32.refs_7_
  115.3 0.6 copy-done.25
  115.9 6.4 %finish.1 = bf16[512,1024]{1,0:T(8,128)(2,1)} custom-call(f32[1,1024]{1,0:T(1,128)} %bitcast.9, s32[512,128]{1,0:T(8,128)} %get-tuple-element.41.refs_0_.slot_ref.slot_hbm, bf16[512,768]{1,0:T(8,128)(2,1)} %collect.1.early_hbm, bf16[512,1024]{1,0:T(8,128)(2,1)} %get-tuple-element.67.gate_hbm, bf16[512,1024]{1,0:T(8,128)(2,1)} %x_hbm.1, ...), custom_call_target="tpu_custom_call" | custom-call | flops 2147483648 | bytes 7340032 | tf_op jit(solution)/shard_map/finish/pallas_call | solution.py:333
  (82 shorter events, 0.4 us)
Async XLA Ops:
  0.0 54.8 %collective-permute-start.9 = (bf16[256,2048]{1,0:T(8,128)(2,1)}, bf16[256,2048]{1,0:T(8,128)(2,1)}, u32[]{:S(2)}, u32[]{:S(2)}) collective-permute-start(bf16[256,2048]{1,0:T(8,128)(2,1)} %bitcast.5), channel_id=1, source_target_pairs={{0,8},{8,0},{16,24},{24,16},{1,9},{9,1},{17,25},{25,17},{2,10},{10... | collective-permute-start | bytes 3145736 | tf_op jit(solution)/shard_map/ppermute | solution.py:358
  3.0 49.4 %collective-permute-start.7 = (bf16[256,2048]{1,0:T(8,128)(2,1)}, bf16[256,2048]{1,0:T(8,128)(2,1)S(1)}, u32[]{:S(2)}, u32[]{:S(2)}) collective-permute-start(bf16[256,2048]{1,0:T(8,128)(2,1)} %bitcast.6), channel_id=1, source_target_pairs={{0,16},{8,24},{16,0},{24,8},{1,17},{9,25},{17,1},{25,9},{2,18},{10... | collective-permute-start | bytes 3145736 | tf_op jit(solution)/shard_map/ppermute | solution.py:358
  6.9 10.1 %copy-start.26 = (s32[2]{0:T(128)S(1)}, s32[2]{0:T(128)}, u32[]{:S(2)}) copy-start(s32[2]{0:T(128)} %constant.12.clone) | copy-start | bytes 28
  14.4 10.1 %collective-permute-start = (bf16[128,1152]{1,0:T(8,128)(2,1)}, bf16[128,1152]{1,0:T(8,128)(2,1)}, u32[]{:S(2)}, u32[]{:S(2)}) collective-permute-start(bf16[128,1152]{1,0:T(8,128)(2,1)} %get-tuple-element.43), channel_id=1, source_target_pairs={{0,1},{1,0},{2,3},{3,2},{4,5},{5,4},{6,7},{7,6},{8,9},{9,8},{10,11... | collective-permute-start | bytes 884744 | tf_op jit(solution)/shard_map/ppermute | solution.py:358
  14.5 12.5 %collective-permute-start.1 = (bf16[128,1152]{1,0:T(8,128)(2,1)}, bf16[128,1152]{1,0:T(8,128)(2,1)S(1)}, u32[]{:S(2)}, u32[]{:S(2)}) collective-permute-start(bf16[128,1152]{1,0:T(8,128)(2,1)} %get-tuple-element.44), channel_id=1, source_target_pairs={{0,2},{1,3},{2,0},{3,1},{4,6},{5,7},{6,4},{7,5},{8,10},{9,11},{10,... | collective-permute-start | bytes 884744 | tf_op jit(solution)/shard_map/ppermute | solution.py:358
  16.0 13.9 %collective-permute-start.2 = (bf16[128,1152]{1,0:T(8,128)(2,1)}, bf16[128,1152]{1,0:T(8,128)(2,1)S(1)}, u32[]{:S(2)}, u32[]{:S(2)}) collective-permute-start(bf16[128,1152]{1,0:T(8,128)(2,1)} %get-tuple-element.45), channel_id=1, source_target_pairs={{0,3},{1,2},{2,1},{3,0},{4,7},{5,6},{6,5},{7,4},{8,11},{9,10},{10,... | collective-permute-start | bytes 884744 | tf_op jit(solution)/shard_map/ppermute | solution.py:358
  24.4 16.4 %collective-permute-start.3 = (bf16[128,1152]{1,0:T(8,128)(2,1)}, bf16[128,1152]{1,0:T(8,128)(2,1)S(1)}, u32[]{:S(2)}, u32[]{:S(2)}) collective-permute-start(bf16[128,1152]{1,0:T(8,128)(2,1)} %get-tuple-element.46), channel_id=1, source_target_pairs={{0,4},{1,5},{2,6},{3,7},{4,0},{5,1},{6,2},{7,3},{8,12},{9,13},{10,... | collective-permute-start | bytes 884744 | tf_op jit(solution)/shard_map/ppermute | solution.py:358
  27.0 25.3 %collective-permute-start.4 = (bf16[128,1152]{1,0:T(8,128)(2,1)}, bf16[128,1152]{1,0:T(8,128)(2,1)S(1)}, u32[]{:S(2)}, u32[]{:S(2)}) collective-permute-start(bf16[128,1152]{1,0:T(8,128)(2,1)} %get-tuple-element.47), channel_id=1, source_target_pairs={{0,5},{1,4},{2,7},{3,6},{4,1},{5,0},{6,3},{7,2},{8,13},{9,12},{10,... | collective-permute-start | bytes 884744 | tf_op jit(solution)/shard_map/ppermute | solution.py:358
  30.0 22.4 %collective-permute-start.5 = (bf16[128,1152]{1,0:T(8,128)(2,1)}, bf16[128,1152]{1,0:T(8,128)(2,1)S(1)}, u32[]{:S(2)}, u32[]{:S(2)}) collective-permute-start(bf16[128,1152]{1,0:T(8,128)(2,1)} %get-tuple-element.48), channel_id=1, source_target_pairs={{0,6},{1,7},{2,4},{3,5},{4,2},{5,3},{6,0},{7,1},{8,14},{9,15},{10,... | collective-permute-start | bytes 884744 | tf_op jit(solution)/shard_map/ppermute | solution.py:358
  40.8 11.6 %collective-permute-start.6 = (bf16[128,1152]{1,0:T(8,128)(2,1)}, bf16[128,1152]{1,0:T(8,128)(2,1)S(1)}, u32[]{:S(2)}, u32[]{:S(2)}) collective-permute-start(bf16[128,1152]{1,0:T(8,128)(2,1)} %get-tuple-element.49), channel_id=1, source_target_pairs={{0,7},{1,6},{2,5},{3,4},{4,3},{5,2},{6,1},{7,0},{8,15},{9,14},{10,... | collective-permute-start | bytes 884744 | tf_op jit(solution)/shard_map/ppermute | solution.py:358
  52.4 2.4 %copy-start = (bf16[1024,1152]{1,0:T(8,128)(2,1)}, bf16[1024,1152]{1,0:T(8,128)(2,1)S(1)}, u32[]{:S(2)}) copy-start(bf16[1024,1152]{1,0:T(8,128)(2,1)S(1)} %constant_dynamic-update-slice_fusion.refs_2_.refs_3_.refs_0_.refs_1_) | copy-start | bytes 7077892
  52.5 2.4 %copy-start.1 = (bf16[256,2048]{1,0:T(8,128)(2,1)}, bf16[256,2048]{1,0:T(8,128)(2,1)S(1)}, u32[]{:S(2)}) copy-start(bf16[256,2048]{1,0:T(8,128)(2,1)S(1)} %collective-permute-done.7.refs_1_.refs_2_.refs_3_.refs_4_.refs_5_) | copy-start | bytes 3145732
  54.4 12.9 %collective-permute-start.8 = (bf16[256,768]{1,0:T(8,128)(2,1)}, bf16[256,768]{1,0:T(8,128)(2,1)S(1)}, u32[]{:S(2)}, u32[]{:S(2)}) collective-permute-start(bf16[256,768]{1,0:T(8,128)(2,1)} %pad_maximum_fusion), channel_id=1, source_target_pairs={{0,8},{8,0},{16,24},{24,16},{1,9},{9,1},{17,25},{25,17},{2,10},{10... | collective-permute-start | bytes 1179656 | tf_op jit(solution)/shard_map/ppermute | solution.py:358
  67.3 2.6 %copy-start.3 = (bf16[256,768]{1,0:T(8,128)(2,1)}, bf16[256,768]{1,0:T(8,128)(2,1)S(1)}, u32[]{:S(2)}) copy-start(bf16[256,768]{1,0:T(8,128)(2,1)S(1)} %collective-permute-done.8.refs_4_.refs_5_) | copy-start | bytes 1179652
  67.3 11.2 %collective-permute-start.17 = (bf16[256,768]{1,0:T(8,128)(2,1)S(1)}, bf16[256,768]{1,0:T(8,128)(2,1)S(1)}, u32[]{:S(2)}, u32[]{:S(2)}) collective-permute-start(bf16[256,768]{1,0:T(8,128)(2,1)S(1)} %pad_maximum_fusion.1), channel_id=1, source_target_pairs={{0,8},{8,0},{16,24},{24,16},{1,9},{9,1},{17,25},{25,17},{2,10},{10... | collective-permute-start | bytes 1179656 | tf_op jit(solution)/shard_map/ppermute | solution.py:358
  75.6 5.9 %collective-permute-start.10 = (bf16[128,384]{1,0:T(8,128)(2,1)}, bf16[128,384]{1,0:T(8,128)(2,1)S(1)}, u32[]{:S(2)}, u32[]{:S(2)}) collective-permute-start(bf16[128,384]{1,0:T(8,128)(2,1)} %get-tuple-element.51), channel_id=1, source_target_pairs={{0,1},{1,0},{2,3},{3,2},{4,5},{5,4},{6,7},{7,6},{8,9},{9,8},{10,11... | collective-permute-start | bytes 294920 | tf_op jit(solution)/shard_map/ppermute | solution.py:358
  75.7 5.9 %collective-permute-start.11 = (bf16[128,384]{1,0:T(8,128)(2,1)}, bf16[128,384]{1,0:T(8,128)(2,1)S(1)}, u32[]{:S(2)}, u32[]{:S(2)}) collective-permute-start(bf16[128,384]{1,0:T(8,128)(2,1)} %get-tuple-element.52), channel_id=1, source_target_pairs={{0,2},{1,3},{2,0},{3,1},{4,6},{5,7},{6,4},{7,5},{8,10},{9,11},{10,... | collective-permute-start | bytes 294920 | tf_op jit(solution)/shard_map/ppermute | solution.py:358
  77.2 6.7 %collective-permute-start.12 = (bf16[128,384]{1,0:T(8,128)(2,1)}, bf16[128,384]{1,0:T(8,128)(2,1)S(1)}, u32[]{:S(2)}, u32[]{:S(2)}) collective-permute-start(bf16[128,384]{1,0:T(8,128)(2,1)} %get-tuple-element.53), channel_id=1, source_target_pairs={{0,3},{1,2},{2,1},{3,0},{4,7},{5,6},{6,5},{7,4},{8,11},{9,10},{10,... | collective-permute-start | bytes 294920 | tf_op jit(solution)/shard_map/ppermute | solution.py:358
  78.4 6.9 %copy-start.2 = (bf16[256,768]{1,0:T(8,128)(2,1)}, bf16[256,768]{1,0:T(8,128)(2,1)S(1)}, u32[]{:S(2)}) copy-start(bf16[256,768]{1,0:T(8,128)(2,1)S(1)} %collective-permute-done.17.refs_5_.refs_6_) | copy-start | bytes 1179652
  78.4 20.2 %collective-permute-start.25 = (bf16[256,512]{1,0:T(8,128)(2,1)S(1)}, bf16[256,512]{1,0:T(8,128)(2,1)S(1)}, u32[]{:S(2)}, u32[]{:S(2)}) collective-permute-start(bf16[256,512]{1,0:T(8,128)(2,1)S(1)} %pad_maximum_fusion.2), channel_id=1, source_target_pairs={{0,8},{8,0},{16,24},{24,16},{1,9},{9,1},{17,25},{25,17},{2,10},{10... | collective-permute-start | bytes 786440 | tf_op jit(solution)/shard_map/ppermute | solution.py:358
  80.0 11.0 %collective-permute-start.13 = (bf16[128,384]{1,0:T(8,128)(2,1)}, bf16[128,384]{1,0:T(8,128)(2,1)S(1)}, u32[]{:S(2)}, u32[]{:S(2)}) collective-permute-start(bf16[128,384]{1,0:T(8,128)(2,1)} %get-tuple-element.54), channel_id=1, source_target_pairs={{0,4},{1,5},{2,6},{3,7},{4,0},{5,1},{6,2},{7,3},{8,12},{9,13},{10,... | collective-permute-start | bytes 294920 | tf_op jit(solution)/shard_map/ppermute | solution.py:358
  81.5 9.5 %copy-start.6 = (bf16[128,384]{1,0:T(8,128)(2,1)}, bf16[128,384]{1,0:T(8,128)(2,1)S(1)}, u32[]{:S(2)}) copy-start(bf16[128,384]{1,0:T(8,128)(2,1)S(1)} %collective-permute-done.10.refs_1_) | copy-start | bytes 294916
  81.6 9.6 %collective-permute-start.14 = (bf16[128,384]{1,0:T(8,128)(2,1)}, bf16[128,384]{1,0:T(8,128)(2,1)S(1)}, u32[]{:S(2)}, u32[]{:S(2)}) collective-permute-start(bf16[128,384]{1,0:T(8,128)(2,1)} %get-tuple-element.55), channel_id=1, source_target_pairs={{0,5},{1,4},{2,7},{3,6},{4,1},{5,0},{6,3},{7,2},{8,13},{9,12},{10,... | collective-permute-start | bytes 294920 | tf_op jit(solution)/shard_map/ppermute | solution.py:358
  81.6 9.5 %copy-start.7 = (bf16[128,384]{1,0:T(8,128)(2,1)}, bf16[128,384]{1,0:T(8,128)(2,1)S(1)}, u32[]{:S(2)}) copy-start(bf16[128,384]{1,0:T(8,128)(2,1)S(1)} %collective-permute-done.11.refs_2_) | copy-start | bytes 294916
  81.6 11.0 %collective-permute-start.15 = (bf16[128,384]{1,0:T(8,128)(2,1)}, bf16[128,384]{1,0:T(8,128)(2,1)S(1)}, u32[]{:S(2)}, u32[]{:S(2)}) collective-permute-start(bf16[128,384]{1,0:T(8,128)(2,1)} %get-tuple-element.56), channel_id=1, source_target_pairs={{0,6},{1,7},{2,4},{3,5},{4,2},{5,3},{6,0},{7,1},{8,14},{9,15},{10,... | collective-permute-start | bytes 294920 | tf_op jit(solution)/shard_map/ppermute | solution.py:358
  84.0 7.1 %copy-start.8 = (bf16[128,384]{1,0:T(8,128)(2,1)}, bf16[128,384]{1,0:T(8,128)(2,1)S(1)}, u32[]{:S(2)}) copy-start(bf16[128,384]{1,0:T(8,128)(2,1)S(1)} %collective-permute-done.12.refs_3_) | copy-start | bytes 294916
  84.0 9.1 %collective-permute-start.16 = (bf16[128,384]{1,0:T(8,128)(2,1)}, bf16[128,384]{1,0:T(8,128)(2,1)S(1)}, u32[]{:S(2)}, u32[]{:S(2)}) collective-permute-start(bf16[128,384]{1,0:T(8,128)(2,1)} %get-tuple-element.57), channel_id=1, source_target_pairs={{0,7},{1,6},{2,5},{3,4},{4,3},{5,2},{6,1},{7,0},{8,15},{9,14},{10,... | collective-permute-start | bytes 294920 | tf_op jit(solution)/shard_map/ppermute | solution.py:358
  91.1 19.5 %copy-start.9 = (bf16[128,384]{1,0:T(8,128)(2,1)}, bf16[128,384]{1,0:T(8,128)(2,1)S(1)}, u32[]{:S(2)}) copy-start(bf16[128,384]{1,0:T(8,128)(2,1)S(1)} %collective-permute-done.13.refs_4_) | copy-start | bytes 294916
  91.1 2.7 %collective-permute-start.18 = (bf16[128,384]{1,0:T(8,128)(2,1)}, bf16[128,384]{1,0:T(8,128)(2,1)S(1)}, u32[]{:S(2)}, u32[]{:S(2)}) collective-permute-start(bf16[128,384]{1,0:T(8,128)(2,1)} %get-tuple-element.60), channel_id=1, source_target_pairs={{0,1},{1,0},{2,3},{3,2},{4,5},{5,4},{6,7},{7,6},{8,9},{9,8},{10,11... | collective-permute-start | bytes 294920 | tf_op jit(solution)/shard_map/ppermute | solution.py:358
  91.2 19.4 %copy-start.10 = (bf16[128,384]{1,0:T(8,128)(2,1)}, bf16[128,384]{1,0:T(8,128)(2,1)S(1)}, u32[]{:S(2)}) copy-start(bf16[128,384]{1,0:T(8,128)(2,1)S(1)} %collective-permute-done.14.refs_5_) | copy-start | bytes 294916
  91.2 5.9 %collective-permute-start.19 = (bf16[128,384]{1,0:T(8,128)(2,1)}, bf16[128,384]{1,0:T(8,128)(2,1)S(1)}, u32[]{:S(2)}, u32[]{:S(2)}) collective-permute-start(bf16[128,384]{1,0:T(8,128)(2,1)} %get-tuple-element.61), channel_id=1, source_target_pairs={{0,2},{1,3},{2,0},{3,1},{4,6},{5,7},{6,4},{7,5},{8,10},{9,11},{10,... | collective-permute-start | bytes 294920 | tf_op jit(solution)/shard_map/ppermute | solution.py:358
  92.6 18.0 %copy-start.11 = (bf16[128,384]{1,0:T(8,128)(2,1)}, bf16[128,384]{1,0:T(8,128)(2,1)S(1)}, u32[]{:S(2)}) copy-start(bf16[128,384]{1,0:T(8,128)(2,1)S(1)} %collective-permute-done.15.refs_6_) | copy-start | bytes 294916
  92.6 11.2 %collective-permute-start.20 = (bf16[128,384]{1,0:T(8,128)(2,1)}, bf16[128,384]{1,0:T(8,128)(2,1)S(1)}, u32[]{:S(2)}, u32[]{:S(2)}) collective-permute-start(bf16[128,384]{1,0:T(8,128)(2,1)} %get-tuple-element.62), channel_id=1, source_target_pairs={{0,3},{1,2},{2,1},{3,0},{4,7},{5,6},{6,5},{7,4},{8,11},{9,10},{10,... | collective-permute-start | bytes 294920 | tf_op jit(solution)/shard_map/ppermute | solution.py:358
  93.0 5.6 %copy-start.5 = (bf16[128,384]{1,0:T(8,128)(2,1)}, bf16[128,384]{1,0:T(8,128)(2,1)S(1)}, u32[]{:S(2)}) copy-start(bf16[128,384]{1,0:T(8,128)(2,1)S(1)} %collective-permute-done.16.refs_7_.refs_1_) | copy-start | bytes 294916
  93.0 11.6 %collective-permute-start.21 = (bf16[128,384]{1,0:T(8,128)(2,1)}, bf16[128,384]{1,0:T(8,128)(2,1)S(1)}, u32[]{:S(2)}, u32[]{:S(2)}) collective-permute-start(bf16[128,384]{1,0:T(8,128)(2,1)} %get-tuple-element.63), channel_id=1, source_target_pairs={{0,4},{1,5},{2,6},{3,7},{4,0},{5,1},{6,2},{7,3},{8,12},{9,13},{10,... | collective-permute-start | bytes 294920 | tf_op jit(solution)/shard_map/ppermute | solution.py:358
  93.8 16.8 %copy-start.12 = (bf16[128,384]{1,0:T(8,128)(2,1)}, bf16[128,384]{1,0:T(8,128)(2,1)S(1)}, u32[]{:S(2)}) copy-start(bf16[128,384]{1,0:T(8,128)(2,1)S(1)} %collective-permute-done.18.refs_9_) | copy-start | bytes 294916
  93.8 12.2 %collective-permute-start.22 = (bf16[128,384]{1,0:T(8,128)(2,1)}, bf16[128,384]{1,0:T(8,128)(2,1)S(1)}, u32[]{:S(2)}, u32[]{:S(2)}) collective-permute-start(bf16[128,384]{1,0:T(8,128)(2,1)} %get-tuple-element.64), channel_id=1, source_target_pairs={{0,5},{1,4},{2,7},{3,6},{4,1},{5,0},{6,3},{7,2},{8,13},{9,12},{10,... | collective-permute-start | bytes 294920 | tf_op jit(solution)/shard_map/ppermute | solution.py:358
  97.1 13.5 %copy-start.13 = (bf16[128,384]{1,0:T(8,128)(2,1)}, bf16[128,384]{1,0:T(8,128)(2,1)S(1)}, u32[]{:S(2)}) copy-start(bf16[128,384]{1,0:T(8,128)(2,1)S(1)} %collective-permute-done.19.refs_10_) | copy-start | bytes 294916
  97.1 9.1 %collective-permute-start.23 = (bf16[128,384]{1,0:T(8,128)(2,1)}, bf16[128,384]{1,0:T(8,128)(2,1)S(1)}, u32[]{:S(2)}, u32[]{:S(2)}) collective-permute-start(bf16[128,384]{1,0:T(8,128)(2,1)} %get-tuple-element.65), channel_id=1, source_target_pairs={{0,6},{1,7},{2,4},{3,5},{4,2},{5,3},{6,0},{7,1},{8,14},{9,15},{10,... | collective-permute-start | bytes 294920 | tf_op jit(solution)/shard_map/ppermute | solution.py:358
  98.6 0.7 copy-start.4
  98.6 8.4 %collective-permute-start.24 = (bf16[128,384]{1,0:T(8,128)(2,1)}, bf16[128,384]{1,0:T(8,128)(2,1)S(1)}, u32[]{:S(2)}, u32[]{:S(2)}) collective-permute-start(bf16[128,384]{1,0:T(8,128)(2,1)} %get-tuple-element.66), channel_id=1, source_target_pairs={{0,7},{1,6},{2,5},{3,4},{4,3},{5,2},{6,1},{7,0},{8,15},{9,14},{10,... | collective-permute-start | bytes 294920 | tf_op jit(solution)/shard_map/ppermute | solution.py:358
  103.8 6.8 %copy-start.14 = (bf16[128,384]{1,0:T(8,128)(2,1)}, bf16[128,384]{1,0:T(8,128)(2,1)S(1)}, u32[]{:S(2)}) copy-start(bf16[128,384]{1,0:T(8,128)(2,1)S(1)} %collective-permute-done.20.refs_11_) | copy-start | bytes 294916
  103.8 4.4 %collective-permute-start.26 = (bf16[128,256]{1,0:T(8,128)(2,1)}, bf16[128,256]{1,0:T(8,128)(2,1)S(1)}, u32[]{:S(2)}, u32[]{:S(2)}) collective-permute-start(bf16[128,256]{1,0:T(8,128)(2,1)} %get-tuple-element.70), channel_id=1, source_target_pairs={{0,1},{1,0},{2,3},{3,2},{4,5},{5,4},{6,7},{7,6},{8,9},{9,8},{10,11... | collective-permute-start | bytes 196616 | tf_op jit(solution)/shard_map/ppermute | solution.py:358
  104.7 6.0 %copy-start.15 = (bf16[128,384]{1,0:T(8,128)(2,1)}, bf16[128,384]{1,0:T(8,128)(2,1)S(1)}, u32[]{:S(2)}) copy-start(bf16[128,384]{1,0:T(8,128)(2,1)S(1)} %collective-permute-done.21.refs_12_) | copy-start | bytes 294916
  104.7 5.1 %collective-permute-start.27 = (bf16[128,256]{1,0:T(8,128)(2,1)}, bf16[128,256]{1,0:T(8,128)(2,1)S(1)}, u32[]{:S(2)}, u32[]{:S(2)}) collective-permute-start(bf16[128,256]{1,0:T(8,128)(2,1)} %get-tuple-element.71), channel_id=1, source_target_pairs={{0,2},{1,3},{2,0},{3,1},{4,6},{5,7},{6,4},{7,5},{8,10},{9,11},{10,... | collective-permute-start | bytes 196616 | tf_op jit(solution)/shard_map/ppermute | solution.py:358
  106.1 4.6 %copy-start.16 = (bf16[128,384]{1,0:T(8,128)(2,1)}, bf16[128,384]{1,0:T(8,128)(2,1)S(1)}, u32[]{:S(2)}) copy-start(bf16[128,384]{1,0:T(8,128)(2,1)S(1)} %collective-permute-done.22.refs_13_) | copy-start | bytes 294916
  106.1 8.3 %collective-permute-start.28 = (bf16[128,256]{1,0:T(8,128)(2,1)}, bf16[128,256]{1,0:T(8,128)(2,1)S(1)}, u32[]{:S(2)}, u32[]{:S(2)}) collective-permute-start(bf16[128,256]{1,0:T(8,128)(2,1)} %get-tuple-element.72), channel_id=1, source_target_pairs={{0,3},{1,2},{2,1},{3,0},{4,7},{5,6},{6,5},{7,4},{8,11},{9,10},{10,... | collective-permute-start | bytes 196616 | tf_op jit(solution)/shard_map/ppermute | solution.py:358
  106.1 4.5 %copy-start.17 = (bf16[128,384]{1,0:T(8,128)(2,1)}, bf16[128,384]{1,0:T(8,128)(2,1)S(1)}, u32[]{:S(2)}) copy-start(bf16[128,384]{1,0:T(8,128)(2,1)S(1)} %collective-permute-done.23.refs_14_) | copy-start | bytes 294916
  106.1 8.2 %collective-permute-start.29 = (bf16[128,256]{1,0:T(8,128)(2,1)}, bf16[128,256]{1,0:T(8,128)(2,1)S(1)}, u32[]{:S(2)}, u32[]{:S(2)}) collective-permute-start(bf16[128,256]{1,0:T(8,128)(2,1)} %get-tuple-element.73), channel_id=1, source_target_pairs={{0,4},{1,5},{2,6},{3,7},{4,0},{5,1},{6,2},{7,3},{8,12},{9,13},{10,... | collective-permute-start | bytes 196616 | tf_op jit(solution)/shard_map/ppermute | solution.py:358
  107.0 3.6 %copy-start.18 = (bf16[128,384]{1,0:T(8,128)(2,1)}, bf16[128,384]{1,0:T(8,128)(2,1)S(1)}, u32[]{:S(2)}) copy-start(bf16[128,384]{1,0:T(8,128)(2,1)S(1)} %collective-permute-done.24.refs_15_) | copy-start | bytes 294916
  107.0 7.3 %collective-permute-start.30 = (bf16[128,256]{1,0:T(8,128)(2,1)}, bf16[128,256]{1,0:T(8,128)(2,1)S(1)}, u32[]{:S(2)}, u32[]{:S(2)}) collective-permute-start(bf16[128,256]{1,0:T(8,128)(2,1)} %get-tuple-element.74), channel_id=1, source_target_pairs={{0,5},{1,4},{2,7},{3,6},{4,1},{5,0},{6,3},{7,2},{8,13},{9,12},{10,... | collective-permute-start | bytes 196616 | tf_op jit(solution)/shard_map/ppermute | solution.py:358
  108.2 7.1 %copy-start.19 = (bf16[128,256]{1,0:T(8,128)(2,1)}, bf16[128,256]{1,0:T(8,128)(2,1)S(1)}, u32[]{:S(2)}) copy-start(bf16[128,256]{1,0:T(8,128)(2,1)S(1)} %collective-permute-done.26.refs_1_) | copy-start | bytes 196612
  108.2 6.2 %collective-permute-start.31 = (bf16[128,256]{1,0:T(8,128)(2,1)}, bf16[128,256]{1,0:T(8,128)(2,1)S(1)}, u32[]{:S(2)}, u32[]{:S(2)}) collective-permute-start(bf16[128,256]{1,0:T(8,128)(2,1)} %get-tuple-element.75), channel_id=1, source_target_pairs={{0,6},{1,7},{2,4},{3,5},{4,2},{5,3},{6,0},{7,1},{8,14},{9,15},{10,... | collective-permute-start | bytes 196616 | tf_op jit(solution)/shard_map/ppermute | solution.py:358
  109.8 5.5 %copy-start.20 = (bf16[128,256]{1,0:T(8,128)(2,1)}, bf16[128,256]{1,0:T(8,128)(2,1)S(1)}, u32[]{:S(2)}) copy-start(bf16[128,256]{1,0:T(8,128)(2,1)S(1)} %collective-permute-done.27.refs_2_) | copy-start | bytes 196612
  109.8 5.5 %collective-permute-start.32 = (bf16[128,256]{1,0:T(8,128)(2,1)}, bf16[128,256]{1,0:T(8,128)(2,1)S(1)}, u32[]{:S(2)}, u32[]{:S(2)}) collective-permute-start(bf16[128,256]{1,0:T(8,128)(2,1)} %get-tuple-element.76), channel_id=1, source_target_pairs={{0,7},{1,6},{2,5},{3,4},{4,3},{5,2},{6,1},{7,0},{8,15},{9,14},{10,... | collective-permute-start | bytes 196616 | tf_op jit(solution)/shard_map/ppermute | solution.py:358
  114.3 0.9 copy-start.21
  114.4 0.9 copy-start.22
  114.4 0.9 copy-start.23
  114.4 0.9 copy-start.24
  115.2 0.6 copy-start.25

commit v4 on v3

--- a/solution.py
+++ b/solution.py
@@ -15,7 +15,7 @@
 F32 = jnp.float32
 BF16 = jnp.bfloat16
 MIB = 1024 * 1024
-BASE_COST = 4.0
+WAIT_COST = 20.0
 
 
 def params(mib):
@@ -48,8 +48,7 @@
     return owner_row.astype(F32) * capacity + rank
 
 
-def query_kernel(columns, capacity, owner_ref, visible_ref, x_ref, w_ref, *refs):
-    sends, place = refs[:-1], refs[-1]
+def query_kernel(columns, capacity, owner_ref, visible_ref, x_ref, w_ref, send_ref, place):
     rows = x_ref.shape[0]
     tile = w_ref.shape[1]
     slots = columns * capacity
@@ -61,9 +60,7 @@
         place[...] = (index == slot).astype(BF16)
 
     def send(block):
-        spread = jnp.dot(place[...], block, preferred_element_type=F32).astype(BF16)
-        for number, ref in enumerate(sends):
-            ref[...] = spread[number * capacity : (number + 1) * capacity, :]
+        send_ref[...] = jnp.dot(place[...], block, preferred_element_type=F32).astype(BF16)
 
     queries = silu(jnp.dot(x_ref[...], w_ref[...], preferred_element_type=F32)).astype(BF16)
     final = pl.program_id(0) == pl.num_programs(0) - 1
@@ -92,8 +89,8 @@
             pl.BlockSpec((rows, width), lambda i: (0, 0)),
             pl.BlockSpec((width, tile), lambda i: (0, i)),
         ],
-        out_specs=[pl.BlockSpec((capacity, tile), lambda i: (0, i))] * columns,
-        out_shape=[jax.ShapeDtypeStruct((capacity, width + BLK), BF16)] * columns,
+        out_specs=pl.BlockSpec((slots, tile), lambda i: (0, i)),
+        out_shape=jax.ShapeDtypeStruct((slots, width + BLK), BF16),
         scratch_shapes=[pltpu.VMEM((slots, rows), BF16)],
         compiler_params=params(60),
         cost_estimate=cost(
@@ -105,43 +102,49 @@
     )(owner_row, visible_row, cand_x, w_in)
 
 
-def gate_kernel(columns, capacity, owner_ref, x_ref, w_ref, gate_ref, slot_ref):
-
-    @pl.when(pl.program_id(0) == 0)
-    def _():
-        slot = slot_row(owner_ref[...], columns, capacity)
-        slot_ref[...] = jnp.broadcast_to(slot, (BLK, slot.shape[1])).T.astype(jnp.int32)
-
+def gate_kernel(x_ref, w_ref, gate_ref):
     hidden = jnp.dot(x_ref[...], w_ref[...], preferred_element_type=F32)
     gate_ref[...] = silu(hidden).astype(BF16)
 
 
-def project_gate(owner_row, cand_x, w_in, columns, capacity):
+def project_gate(cand_x, w_in):
     rows, width = cand_x.shape
     tile = min(256, width)
     first = width // tile
     return pl.pallas_call(
-        functools.partial(gate_kernel, columns, capacity),
+        gate_kernel,
         grid=(first,),
         in_specs=[
-            pl.BlockSpec((1, rows), lambda i: (0, 0)),
             pl.BlockSpec((rows, width), lambda i: (0, 0)),
             pl.BlockSpec((width, tile), lambda i: (0, first + i)),
         ],
-        out_specs=[
-            pl.BlockSpec((rows, tile), lambda i: (0, i)),
-            pl.BlockSpec((rows, BLK), lambda i: (0, 0)),
-        ],
-        out_shape=[
-            jax.ShapeDtypeStruct((rows, width), BF16),
-            jax.ShapeDtypeStruct((rows, BLK), jnp.int32),
-        ],
+        out_specs=pl.BlockSpec((rows, tile), lambda i: (0, i)),
+        out_shape=jax.ShapeDtypeStruct((rows, width), BF16),
         compiler_params=params(60),
         cost_estimate=cost(
             2 * rows * width * width, 2 * (2 * rows * width + width * width), rows * width
         ),
         name="project_gate",
-    )(owner_row, cand_x, w_in)
+    )(cand_x, w_in)
+
+
+def slots_kernel(columns, capacity, owner_ref, *refs):
+    slot = slot_row(owner_ref[...], columns, capacity)
+    refs[-1][...] = jnp.broadcast_to(slot, (BLK, slot.shape[1])).T.astype(jnp.int32)
+
+
+def slot_column(owner_row, columns, capacity, after):
+    rows = owner_row.shape[1]
+    vmem = pl.BlockSpec(memory_space=pltpu.VMEM)
+    return pl.pallas_call(
+        functools.partial(slots_kernel, columns, capacity),
+        in_specs=[vmem] + [pl.BlockSpec(memory_space=pl.ANY)] * len(after),
+        out_specs=vmem,
+        out_shape=jax.ShapeDtypeStruct((rows, BLK), jnp.int32),
+        compiler_params=params(60),
+        cost_estimate=cost(WAIT_COST * 1e9, 4 * rows * BLK),
+        name="slot_column",
+    )(owner_row, *after)
 
 
 def attend_kernel(size, behind, segments, has_base, outs, place_ref, *refs):
@@ -149,7 +152,8 @@
     seen_ref, query_ref, refs = refs[0], refs[1], refs[2:]
     parts, refs = refs[: 2 * segments], refs[2 * segments :]
     base_ref = refs[0] if has_base else None
-    out_refs, scales = refs[-1 - outs : -1], refs[-1]
+    out_refs, shown = refs[-2 - outs : -2], refs[-2]
+    result = out_refs[0] if outs == 1 else refs[-1]
     slots = query_ref.shape[0]
     keys = parts[0].shape[0]
     blocks = keys // BLK
@@ -159,20 +163,17 @@
         seen = seen_ref[...].astype(F32)
         for number in range(segments):
             for block in range(blocks):
-                first = (place_ref[1 + number] * blocks + block).astype(F32)
-                scales[number * blocks + block] = jnp.where(
-                    first < seen, 0.5 / math.sqrt(size), 0.0
-                )
+                first = (place_ref[2 + number] * blocks + block).astype(F32)
+                shown[number * blocks + block] = (first < seen).astype(F32).astype(BF16)
 
     row = lax.broadcasted_iota(jnp.int32, (keys, size), 0)
     values = []
     for number in range(segments):
-        shown = row + place_ref[1 + number] * keys < place_ref[0]
+        inside = row + place_ref[2 + number] * keys < place_ref[0]
         value = parts[2 * number + 1][...].astype(F32)
-        values.append(jnp.where(shown, value, 0.0).astype(BF16))
+        values.append(jnp.where(inside, value, 0.0).astype(BF16))
     values = jnp.concatenate(values, axis=0)
-    tile = min(256, slots)
-    results = []
+    tile = min(512, slots)
     for start in range(0, slots, tile):
         span = slice(start, start + tile)
         weights = []
@@ -184,25 +185,23 @@
                 preferred_element_type=F32,
             )
             for block in range(blocks):
-                half = scores[:, block * BLK : (block + 1) * BLK]
-                half = half * scales[number * blocks + block, span, :]
-                weights.append((half * jnp.tanh(half) + half).astype(BF16))
+                half = scores[:, block * BLK : (block + 1) * BLK] * (0.5 / math.sqrt(size))
+                half = half.astype(BF16) * shown[number * blocks + block, span, :]
+                weights.append(half * jnp.tanh(half) + half)
         total = jnp.dot(
             jnp.concatenate(weights, axis=1), values, preferred_element_type=F32
         )
         if has_base:
             total = total + base_ref[span, :]
-        results.append(total)
-    capacity = slots // outs
-    for number, ref in enumerate(out_refs):
-        start = number * capacity
-        piece = results[start // tile][start % tile : start % tile + capacity, :]
-        if outs == 1:
-            piece = jnp.concatenate(results, axis=0)
-        ref[...] = piece.astype(ref.dtype)
-
-
-def attend(place, after, rows, segments, base, first, heads, size, outs, dtype, share=1.0):
+        result[span, :] = total.astype(result.dtype)
+    if outs > 1:
+        capacity = slots // outs
+        for number, ref in enumerate(out_refs):
+            start = pl.multiple_of((place_ref[1] ^ number) * capacity, capacity)
+            ref[...] = result[pl.ds(start, capacity), :]
+
+
+def attend(place, after, rows, segments, base, first, heads, size, outs, dtype):
     slots, width = rows.shape[0], HEADS * size
     keys = segments[0][0].shape[0]
     capacity = slots // outs
@@ -230,10 +229,13 @@
         in_specs=in_specs,
         out_specs=[column(capacity, 0)] * outs,
         out_shape=[jax.ShapeDtypeStruct((capacity, heads * size), dtype)] * outs,
-        scratch_shapes=[pltpu.VMEM((count * (keys // BLK), slots, BLK), F32)],
+        scratch_shapes=[
+            pltpu.VMEM((count * (keys // BLK), slots, BLK), BF16),
+            pltpu.VMEM((slots, size), BF16),
+        ],
         compiler_params=params(60),
         cost_estimate=cost(
-            share * 4 * slots * keys * count * heads * size,
+            4 * slots * keys * count * heads * size,
             2 * (2 * slots + count * keys * 2) * heads * size,
             slots * keys * count * heads,
         ),
@@ -370,28 +372,40 @@
     size = width // HEADS
     capacity = 2 * rows // columns
     own = kv_cache[0]
-    owner_row = cand_user.reshape(1, rows) ^ lax.axis_index("cand").astype(jnp.int32)
+    me = lax.axis_index("cand").astype(jnp.int32)
+    owner_row = cand_user.reshape(1, rows)
     visible_row = visible.reshape(1, rows)
 
-    held = {0: own}
-    bit = count // 2
-    while bit > 1:
-        for key in sorted(held):
-            held[key | bit] = swap(held[key], "user", bit, count)
-        bit //= 2
-    evens = sorted(held)
+    spans = [(sum(GROUPS[:number]), heads) for number, heads in enumerate(GROUPS)]
+    far = []
+    for first, heads in spans:
+        lo, hi = first * size, (first + heads) * size
+        held = {0: jnp.concatenate([own[:, lo:hi], own[:, width + lo : width + hi]], axis=1)}
+        bit = count // 2
+        while bit > 1:
+            for key in sorted(held):
+                held[key | bit] = swap(held[key], "user", bit, count)
+            bit //= 2
+        far.append(held)
+    evens = sorted(far[0])
     near = swap(own, "user", 1, count)
 
     send = project_queries(owner_row, visible_row, cand_x, w_in, columns, capacity)
-    got = jnp.concatenate(exchange(send), axis=0)
-    gate, slot = project_gate(owner_row, cand_x, w_in, columns, capacity)
+    got = lax.all_to_all(
+        send.reshape(columns, capacity, -1), "cand", split_axis=0, concat_axis=0, tiled=True
+    ).reshape(columns * capacity, -1)
+    gate = project_gate(cand_x, w_in)
+    arrived = [near] + [held[evens[-1]] for held in far]
+    slot = slot_column(owner_row ^ me, columns, capacity, [gate] + arrived)
     position = lax.axis_index("user").astype(jnp.int32)
-    order = evens[1:] + [key | 1 for key in evens[1:]]
-    place_first = jnp.concatenate([hist_len, position ^ jnp.array([0, 1], jnp.int32)])
-    place = jnp.concatenate([hist_len, position ^ jnp.array(order, jnp.int32)])
+    order = [0, 1] + evens[1:] + [key | 1 for key in evens[1:]]
+    shards = position ^ jnp.array(order, jnp.int32)
+    head = jnp.concatenate([hist_len, me[None]])
+    place_first = jnp.concatenate([head, shards[:2]])
+    place = jnp.concatenate([head, shards[2:]])
     base = attend(
         place_first,
-        [slot, held[evens[-1]]],
+        [slot],
         got,
         [(own, 0, HEADS), (near, 0, HEADS)],
         None,
@@ -400,28 +414,22 @@
         size,
         1,
         F32,
-        BASE_COST,
     )[0]
 
-    def forward(first, heads, behind):
-        lo, hi = first * size, (first + heads) * size
-        parts = [
-            jnp.concatenate([held[key][:, lo:hi], held[key][:, width + lo : width + hi]], axis=1)
-            for key in evens[1:]
-        ]
+    def forward(number, behind):
+        parts = [far[number][key] for key in evens[1:]]
         if behind is not None:
             parts, _ = lax.optimization_barrier((parts, behind))
         return [swap(part, "user", 1, count) for part in parts]
 
-    spans = [(sum(GROUPS[:number]), heads) for number, heads in enumerate(GROUPS)]
-    cuts = [forward(*spans[0], None)]
+    cuts = [forward(0, None)]
     returned = []
     after = []
     done = base
     for number, (first, heads) in enumerate(spans):
         if number + 1 < len(spans):
-            cuts.append(forward(*spans[number + 1], (cuts[number], done)))
-        segments = [(held[key], first, HEADS + first) for key in evens[1:]]
+            cuts.append(forward(number + 1, (cuts[number], done)))
+        segments = [(far[number][key], 0, heads) for key in evens[1:]]
         segments += [(cut, 0, heads) for cut in cuts[number]]
         attn = attend(place, after, got, segments, base, first, heads, size, columns, BF16)
         done = attn[0]

time: 123 us -> 121 us (0.984)
  waiting for transfers between devices: 26.6 us -> 23.7 us
    all_to_all x0 -> x1, starting transfers between devices: none -> 3.8 us  [per_device(): lax.all_to_all(send.reshape(columns, capacity, -1), 'cand', split_axis=0,...]
    ppermute x33 -> x28, waiting for transfers between devices: 26.6 us -> 23.7 us  [swap(): return lax.ppermute(array, axis, [(i, i ^ bits) for i in range(count)])]
    ppermute x33 -> x28, starting transfers between devices: 34.6 us -> 31.8 us  [swap(): return lax.ppermute(array, axis, [(i, i ^ bits) for i in range(count)])]
    pallas_call x4, Pallas kernels: 27.3 us -> 25.1 us  [attend(): pl.pallas_call(functools.partial(attend_kernel, size, len(after), count,...]
    pallas_call x1 -> x2, Pallas kernels: 5.2 us -> 6.56 us  [the longest x1 4.87 us: project_gate(): pl.pallas_call(gate_kernel, grid=(first,), in_specs=[pl.BlockSpec((rows,...]
    unnamed x61 -> x52, local copies, waits for them, and re-layouts: 3.49 us -> 3.76 us
  transfers between devices with their start and end apart: 33 -> 29, of which waited for: 6 -> 6; matrix products, arithmetic and copies ran while one was open for 7% -> 5% of each run, Pallas kernels for 36% -> 36%
where the time goes in v4:
time: 121 us; the launch traced here: 120 us
  Pallas kernels  49.2 us (41%)
  starting transfers between devices  35.6 us (29%)
  waiting for transfers between devices  23.7 us (20%)
  local copies, waits for them, and re-layouts  6.13 us (5%)
  other arithmetic  4.1 us (3%)
    ppermute x28, starting transfers between devices, swap(): return lax.ppermute(array, axis, [(i, i ^ bits) for i in range(count)])  31.8 us
    pallas_call x4, Pallas kernels, attend(): pl.pallas_call(functools.partial(attend_kernel, size, len(after), count,...  25.1 us
    ppermute x28, waiting for transfers between devices, swap(): return lax.ppermute(array, axis, [(i, i ^ bits) for i in range(count)])  23.7 us
    pallas_call x1, Pallas kernels, project_queries(): pl.pallas_call(functools.partial(query_kernel, columns, capacity), grid=(...  7.45 us
    pallas_call x1, Pallas kernels, finish(): pl.pallas_call(functools.partial(finish_kernel, len(parts)), in_specs=[vm...  6.39 us
    pallas_call x1, Pallas kernels, project_gate(): pl.pallas_call(gate_kernel, grid=(first,), in_specs=[pl.BlockSpec((rows,...  4.87 us
    all_to_all x1, starting transfers between devices, per_device(): lax.all_to_all(send.reshape(columns, capacity, -1), 'cand', split_axis=0,...  3.8 us
    unnamed x52, local copies, waits for them, and re-layouts  3.76 us
  transfers between devices with their start and end apart: 29, of which 6 were waited for; matrix products, arithmetic and copies ran while one was open for 5% of the time, Pallas kernels for 36%

profile of v4, /device:TPU:0, one launch (start us, length us, event | category | flops | bytes accessed | tf_op | source)
XLA Modules:
  0.0 119.8 jit_solution(16177048288867016307)
XLA Ops:
  0.0 3.0 %collective-permute-start = (bf16[256,2048]{1,0:T(8,128)(2,1)}, bf16[256,2048]{1,0:T(8,128)(2,1)S(1)}, u32[]{:S(2)}, u32[]{:S(2)}) collective-permute-start(bf16[256,2048]{1,0:T(8,128)(2,1)} %bitcast.16), channel_id=1, source_target_pairs={{0,8},{8,0},{16,24},{24,16},{1,9},{9,1},{17,25},{25,17},{2,10},{10... | collective-permute-start | bytes 3145736 | tf_op jit(solution)/shard_map/ppermute | solution.py:360
  3.0 1.0 fusion
  4.0 0.7 pad_maximum_fusion.2
  4.7 2.6 %collective-permute-start.3 = (bf16[256,512]{1,0:T(8,128)(2,1)}, bf16[256,512]{1,0:T(8,128)(2,1)}, u32[]{:S(2)}, u32[]{:S(2)}) collective-permute-start(bf16[256,512]{1,0:T(8,128)(2,1)} %pad_maximum_fusion.2), channel_id=1, source_target_pairs={{0,16},{8,24},{16,0},{24,8},{1,17},{9,25},{17,1},{25,9},{2,18},{10... | collective-permute-start | bytes 786440 | tf_op jit(solution)/shard_map/ppermute | solution.py:360
  7.3 1.3 %fusion.1 = (bf16[256,384]{1,0:T(8,128)(2,1)S(1)}, bf16[256,384]{1,0:T(8,128)(2,1)S(1)}, bf16[256,384]{1,0:T(8,128)(2,1)S(1)}, bf16[256,384]{1,0:T(8,128)(2,1)S(1)}) fusion(bf16[256,2048]{1,0:T(8,128)(2,1)} %bitcast.18), kind=kLoop, calls=%fused_computation.9 | loop fusion | bytes 1572864 | tf_op jit(solution)/shard_map/slice | solution.py:383
  8.6 0.8 pad_maximum_fusion
  9.4 0.3 collective-permute-start.1
  9.7 0.8 pad_maximum_fusion.1
  10.5 2.6 %collective-permute-start.2 = (bf16[256,768]{1,0:T(8,128)(2,1)}, bf16[256,768]{1,0:T(8,128)(2,1)}, u32[]{:S(2)}, u32[]{:S(2)}) collective-permute-start(bf16[256,768]{1,0:T(8,128)(2,1)} %pad_maximum_fusion.1), channel_id=1, source_target_pairs={{0,16},{8,24},{16,0},{24,8},{1,17},{9,25},{17,1},{25,9},{2,18},{10... | collective-permute-start | bytes 1179656 | tf_op jit(solution)/shard_map/ppermute | solution.py:360
  13.1 7.5 %project_queries.1 = bf16[1024,1152]{1,0:T(8,128)(2,1)} custom-call(s32[1,512]{1,0:T(1,128)} %bitcast.22, s32[1,512]{1,0:T(1,128)} %bitcast.24, bf16[512,1024]{1,0:T(8,128)(2,1)} %x_hbm.1, bf16[1024,2048]{1,0:T(8,128)(2,1)} %w_ref.3), custom_call_target="tpu_custom_call" | custom-call | flops 2147483648 | bytes 5242880 | tf_op jit(solution)/shard_map/project_queries/pallas_call | solution.py:83
  20.6 3.8 %all-to-all-start = ((bf16[8,128,1152]{2,1,0:T(8,128)(2,1)}), bf16[8,128,1152]{2,1,0:T(8,128)(2,1)S(1)}, u32[]{:S(2)}, u32[]{:S(2)}) async-start(bf16[8,128,1152]{2,1,0:T(8,128)(2,1)} %bitcast.21), calls=%async_computation | async-start | bytes 4718592 | tf_op jit(solution)/shard_map/all_to_all | solution.py:394
  25.0 0.1 fusion.2
  25.1 0.6 pad_add_fusion.2.place_ref
  25.7 4.9 %project_gate.1.refs_0_.gate_hbm = bf16[512,1024]{1,0:T(8,128)(2,1)} custom-call(bf16[512,1024]{1,0:T(8,128)(2,1)} %x_hbm.1, bf16[1024,2048]{1,0:T(8,128)(2,1)} %w_ref.3), custom_call_target="tpu_custom_call" | custom-call | flops 1073741824 | bytes 4194304 | tf_op jit(solution)/shard_map/project_gate/pallas_call | solution.py:114
  30.6 0.6 broadcast_xor_fusion.owner_ref
  31.2 9.8 %collective-permute-done.1.refs_2_.refs_3_ = bf16[256,768]{1,0:T(8,128)(2,1)} collective-permute-done((bf16[256,768]{1,0:T(8,128)(2,1)}, bf16[256,768]{1,0:T(8,128)(2,1)}, u32[]{:S(2)}, u32[]{:S(2)}) %collective-permute-start.1) | collective-permute-done | bytes 393248 | tf_op jit(solution)/shard_map/ppermute | solution.py:360
  41.0 3.5 %collective-permute-start.4 = (bf16[256,768]{1,0:T(8,128)(2,1)}, bf16[256,768]{1,0:T(8,128)(2,1)}, u32[]{:S(2)}, u32[]{:S(2)}) collective-permute-start(bf16[256,768]{1,0:T(8,128)(2,1)} %collective-permute-done.1.refs_2_.refs_3_), channel_id=1, source_target_pairs={{0,8},{8,0},{16,24},{24,16},{1,9},{9,1},{17,25},{25,17},{2,10},{10... | collective-permute-start | bytes 1179656 | tf_op jit(solution)/shard_map/ppermute | solution.py:360
  44.5 8.6 %collective-permute-done.2.refs_3_.refs_4_ = bf16[256,768]{1,0:T(8,128)(2,1)} collective-permute-done((bf16[256,768]{1,0:T(8,128)(2,1)}, bf16[256,768]{1,0:T(8,128)(2,1)}, u32[]{:S(2)}, u32[]{:S(2)}) %collective-permute-start.2) | collective-permute-done | bytes 393248 | tf_op jit(solution)/shard_map/ppermute | solution.py:360
  53.2 0.0 collective-permute-done.refs_1_.refs_5_.refs_6_
  53.2 1.0 copy-done.1
  54.2 1.7 %slot_column.1.refs_0_.slot_ref.slot_hbm = s32[512,128]{1,0:T(8,128)} custom-call(s32[1,512]{1,0:T(1,128)} %broadcast_xor_fusion.owner_ref, bf16[512,1024]{1,0:T(8,128)(2,1)} %project_gate.1.refs_0_.gate_hbm, bf16[256,2048]{1,0:T(8,128)(2,1)} %copy-done.1, bf16[256,768]{1,0:T(8,128)(2,1)} %collective-permute-done.1.refs_2_.refs_3_, ...), custom_call_target="tpu_custom_call" | custom-call | flops 20000000000 | bytes 262144 | tf_op jit(solution)/shard_map/slot_column/pallas_call | solution.py:139
  55.9 0.0 all-to-all-done
  55.9 1.4 %copy-done = bf16[8,128,1152]{2,1,0:T(8,128)(2,1)} copy-done((bf16[8,128,1152]{2,1,0:T(8,128)(2,1)}, bf16[8,128,1152]{2,1,0:T(8,128)(2,1)S(1)}, u32[]{:S(2)}) %copy-start) | copy-done | bytes 2359320
  57.3 10.2 %attend.4.refs_6_.refs_7_.refs_8_ = f32[1024,1024]{1,0:T(8,128)} custom-call(s32[4]{0:T(128)} %pad_add_fusion.2.place_ref, s32[512,128]{1,0:T(8,128)} %slot_column.1.refs_0_.slot_ref.slot_hbm, bf16[1024,1152]{1,0:T(8,128)(2,1)} %bitcast.8, bf16[1024,1152]{1,0:T(8,128)(2,1)} %bitcast.9, bf16[256,2048]{1,0:T(8,128)(2,1)} %bitcast.19, ...), custom_call_target="tpu_custom_call" | custom-call | flops 2147483648 | bytes 6291456 | tf_op jit(solution)/shard_map/attend/pallas_call | solution.py:226
  67.5 0.0 collective-permute-done.4.refs_4_.refs_5_
  67.5 0.1 collective-permute-start.12
  67.5 0.6 pad_add_fusion.place_ref
  68.2 5.4 %attend.5 = (bf16[128,384]{1,0:T(8,128)(2,1)}, bf16[128,384]{1,0:T(8,128)(2,1)}, bf16[128,384]{1,0:T(8,128)(2,1)}, bf16[128,384]{1,0:T(8,128)(2,1)}, bf16[128,38...) custom-call(s32[4]{0:T(128)} %pad_add_fusion.place_ref, ...), custom_call_target="tpu_custom_call" | custom-call | flops 805306368 | bytes 2359296 | tf_op jit(solution)/shard_map/attend/pallas_call | solution.py:226
  73.6 0.1 collective-permute-start.5
  73.7 1.6 %collective-permute-start.6 = (bf16[128,384]{1,0:T(8,128)(2,1)}, bf16[128,384]{1,0:T(8,128)(2,1)S(1)}, u32[]{:S(2)}, u32[]{:S(2)}) collective-permute-start(bf16[128,384]{1,0:T(8,128)(2,1)} %get-tuple-element.33), channel_id=1, source_target_pairs={{0,2},{1,3},{2,0},{3,1},{4,6},{5,7},{6,4},{7,5},{8,10},{9,11},{10,... | collective-permute-start | bytes 294920 | tf_op jit(solution)/shard_map/ppermute | solution.py:360
  75.2 0.3 collective-permute-start.7
  75.5 1.5 %collective-permute-done.12.refs_5_.refs_6_ = bf16[256,768]{1,0:T(8,128)(2,1)S(1)} collective-permute-done((bf16[256,768]{1,0:T(8,128)(2,1)}, bf16[256,768]{1,0:T(8,128)(2,1)S(1)}, u32[]{:S(2)}, u32[]{:S(2)}) %collective-permute-start.12) | collective-permute-done | bytes 393248 | tf_op jit(solution)/shard_map/ppermute | solution.py:360
  77.1 0.5 collective-permute-start.20
  77.6 1.5 %collective-permute-start.8 = (bf16[128,384]{1,0:T(8,128)(2,1)}, bf16[128,384]{1,0:T(8,128)(2,1)S(1)}, u32[]{:S(2)}, u32[]{:S(2)}) collective-permute-start(bf16[128,384]{1,0:T(8,128)(2,1)} %get-tuple-element.35), channel_id=1, source_target_pairs={{0,4},{1,5},{2,6},{3,7},{4,0},{5,1},{6,2},{7,3},{8,12},{9,13},{10,... | collective-permute-start | bytes 294920 | tf_op jit(solution)/shard_map/ppermute | solution.py:360
  79.1 0.0 collective-permute-done.5.refs_1_
  79.1 0.0 collective-permute-start.9
  79.1 0.5 collective-permute-done.6.refs_2_
  79.5 2.5 %collective-permute-start.10 = (bf16[128,384]{1,0:T(8,128)(2,1)}, bf16[128,384]{1,0:T(8,128)(2,1)S(1)}, u32[]{:S(2)}, u32[]{:S(2)}) collective-permute-start(bf16[128,384]{1,0:T(8,128)(2,1)} %get-tuple-element.37), channel_id=1, source_target_pairs={{0,6},{1,7},{2,4},{3,5},{4,2},{5,3},{6,0},{7,1},{8,14},{9,15},{10,... | collective-permute-start | bytes 294920 | tf_op jit(solution)/shard_map/ppermute | solution.py:360
  82.0 1.4 %collective-permute-start.11 = (bf16[128,384]{1,0:T(8,128)(2,1)}, bf16[128,384]{1,0:T(8,128)(2,1)S(1)}, u32[]{:S(2)}, u32[]{:S(2)}) collective-permute-start(bf16[128,384]{1,0:T(8,128)(2,1)} %get-tuple-element.38), channel_id=1, source_target_pairs={{0,7},{1,6},{2,5},{3,4},{4,3},{5,2},{6,1},{7,0},{8,15},{9,14},{10,... | collective-permute-start | bytes 294920 | tf_op jit(solution)/shard_map/ppermute | solution.py:360
  83.4 5.4 %attend.6 = (bf16[128,384]{1,0:T(8,128)(2,1)}, bf16[128,384]{1,0:T(8,128)(2,1)}, bf16[128,384]{1,0:T(8,128)(2,1)}, bf16[128,384]{1,0:T(8,128)(2,1)}, bf16[128,38...) custom-call(s32[4]{0:T(128)} %pad_add_fusion.place_ref, ...), custom_call_target="tpu_custom_call" | custom-call | flops 805306368 | bytes 2359296 | tf_op jit(solution)/shard_map/attend/pallas_call | solution.py:226
  88.8 0.0 collective-permute-done.8.refs_4_
  88.8 0.1 collective-permute-start.13
  88.9 1.2 collective-permute-start.14
  90.1 0.0 collective-permute-done.10.refs_6_
  90.1 0.7 collective-permute-start.15
  90.8 0.8 collective-permute-start.16
  91.6 0.9 collective-permute-start.17
  92.5 2.3 %collective-permute-done.14.refs_10_ = bf16[128,384]{1,0:T(8,128)(2,1)S(1)} collective-permute-done((bf16[128,384]{1,0:T(8,128)(2,1)}, bf16[128,384]{1,0:T(8,128)(2,1)S(1)}, u32[]{:S(2)}, u32[]{:S(2)}) %collective-permute-start.14) | collective-permute-done | bytes 98336 | tf_op jit(solution)/shard_map/ppermute | solution.py:360
  94.8 1.6 %collective-permute-start.18 = (bf16[128,384]{1,0:T(8,128)(2,1)}, bf16[128,384]{1,0:T(8,128)(2,1)S(1)}, u32[]{:S(2)}, u32[]{:S(2)}) collective-permute-start(bf16[128,384]{1,0:T(8,128)(2,1)} %get-tuple-element.46), channel_id=1, source_target_pairs={{0,6},{1,7},{2,4},{3,5},{4,2},{5,3},{6,0},{7,1},{8,14},{9,15},{10,... | collective-permute-start | bytes 294920 | tf_op jit(solution)/shard_map/ppermute | solution.py:360
  96.4 0.0 collective-permute-start.19
  96.4 0.7 copy-done.3
  97.1 4.1 %attend.7 = (bf16[128,256]{1,0:T(8,128)(2,1)}, bf16[128,256]{1,0:T(8,128)(2,1)}, bf16[128,256]{1,0:T(8,128)(2,1)}, bf16[128,256]{1,0:T(8,128)(2,1)}, bf16[128,25...) custom-call(s32[4]{0:T(128)} %pad_add_fusion.place_ref, ...), custom_call_target="tpu_custom_call" | custom-call | flops 536870912 | bytes 1572864 | tf_op jit(solution)/shard_map/attend/pallas_call | solution.py:226
  101.2 0.0 copy-start.14
  101.2 0.9 collective-permute-start.21
  102.1 1.1 collective-permute-start.22
  103.2 0.3 collective-permute-start.23
  103.5 0.8 collective-permute-start.24
  104.3 1.3 %collective-permute-start.25 = (bf16[128,256]{1,0:T(8,128)(2,1)}, bf16[128,256]{1,0:T(8,128)(2,1)S(1)}, u32[]{:S(2)}, u32[]{:S(2)}) collective-permute-start(bf16[128,256]{1,0:T(8,128)(2,1)} %get-tuple-element.54), channel_id=1, source_target_pairs={{0,5},{1,4},{2,7},{3,6},{4,1},{5,0},{6,3},{7,2},{8,13},{9,12},{10,... | collective-permute-start | bytes 196616 | tf_op jit(solution)/shard_map/ppermute | solution.py:360
  105.6 1.6 %collective-permute-start.26 = (bf16[128,256]{1,0:T(8,128)(2,1)}, bf16[128,256]{1,0:T(8,128)(2,1)S(1)}, u32[]{:S(2)}, u32[]{:S(2)}) collective-permute-start(bf16[128,256]{1,0:T(8,128)(2,1)} %get-tuple-element.55), channel_id=1, source_target_pairs={{0,6},{1,7},{2,4},{3,5},{4,2},{5,3},{6,0},{7,1},{8,14},{9,15},{10,... | collective-permute-start | bytes 196616 | tf_op jit(solution)/shard_map/ppermute | solution.py:360
  107.2 0.8 collective-permute-start.27
  108.0 3.7 %collect.1.early_hbm = bf16[512,768]{1,0:T(8,128)(2,1)} custom-call(s32[512,128]{1,0:T(8,128)} %slot_column.1.refs_0_.slot_ref.slot_hbm, bf16[128,384]{1,0:T(8,128)(2,1)} %get-tuple-element.31.refs_0_, bf16[128,384]{1,0:T(8,128)(2,1)} %copy-done.6, bf16[128,384]{1,0:T(8,128)(2,1)} %copy-done.7, bf16[128,384]{1,0:T(8,128)(2,1)} %copy-done.8, ...), custom_call_target="tpu_custom_call" | custom-call | flops 805306368 | bytes 2359296 | tf_op jit(solution)/shard_map/collect/pallas_call | solution.py:273
  111.8 0.9 collective-permute-done.27.refs_7_
  112.7 0.6 copy-done.25
  113.3 6.4 %finish.1 = bf16[512,1024]{1,0:T(8,128)(2,1)} custom-call(f32[1,1024]{1,0:T(1,128)} %bitcast.23, s32[512,128]{1,0:T(8,128)} %slot_column.1.refs_0_.slot_ref.slot_hbm, bf16[512,768]{1,0:T(8,128)(2,1)} %collect.1.early_hbm, bf16[512,1024]{1,0:T(8,128)(2,1)} %project_gate.1.refs_0_.gate_hbm, bf16[512,1024]{1,0:T(8,128)(2,1)} %x_hbm.1, ...), custom_call_target="tpu_custom_call" | custom-call | flops 2147483648 | bytes 7340032 | tf_op jit(solution)/shard_map/finish/pallas_call | solution.py:335
  (65 shorter events, 0.1 us)
Async XLA Ops:
  0.0 53.2 %collective-permute-start = (bf16[256,2048]{1,0:T(8,128)(2,1)}, bf16[256,2048]{1,0:T(8,128)(2,1)S(1)}, u32[]{:S(2)}, u32[]{:S(2)}) collective-permute-start(bf16[256,2048]{1,0:T(8,128)(2,1)} %bitcast.16), channel_id=1, source_target_pairs={{0,8},{8,0},{16,24},{24,16},{1,9},{9,1},{17,25},{25,17},{2,10},{10... | collective-permute-start | bytes 3145736 | tf_op jit(solution)/shard_map/ppermute | solution.py:360
  4.7 39.8 %collective-permute-start.3 = (bf16[256,512]{1,0:T(8,128)(2,1)}, bf16[256,512]{1,0:T(8,128)(2,1)}, u32[]{:S(2)}, u32[]{:S(2)}) collective-permute-start(bf16[256,512]{1,0:T(8,128)(2,1)} %pad_maximum_fusion.2), channel_id=1, source_target_pairs={{0,16},{8,24},{16,0},{24,8},{1,17},{9,25},{17,1},{25,9},{2,18},{10... | collective-permute-start | bytes 786440 | tf_op jit(solution)/shard_map/ppermute | solution.py:360
  9.4 31.6 %collective-permute-start.1 = (bf16[256,768]{1,0:T(8,128)(2,1)}, bf16[256,768]{1,0:T(8,128)(2,1)}, u32[]{:S(2)}, u32[]{:S(2)}) collective-permute-start(bf16[256,768]{1,0:T(8,128)(2,1)} %pad_maximum_fusion), channel_id=1, source_target_pairs={{0,16},{8,24},{16,0},{24,8},{1,17},{9,25},{17,1},{25,9},{2,18},{10... | collective-permute-start | bytes 1179656 | tf_op jit(solution)/shard_map/ppermute | solution.py:360
  10.5 42.7 %collective-permute-start.2 = (bf16[256,768]{1,0:T(8,128)(2,1)}, bf16[256,768]{1,0:T(8,128)(2,1)}, u32[]{:S(2)}, u32[]{:S(2)}) collective-permute-start(bf16[256,768]{1,0:T(8,128)(2,1)} %pad_maximum_fusion.1), channel_id=1, source_target_pairs={{0,16},{8,24},{16,0},{24,8},{1,17},{9,25},{17,1},{25,9},{2,18},{10... | collective-permute-start | bytes 1179656 | tf_op jit(solution)/shard_map/ppermute | solution.py:360
  20.6 35.3 %all-to-all-start = ((bf16[8,128,1152]{2,1,0:T(8,128)(2,1)}), bf16[8,128,1152]{2,1,0:T(8,128)(2,1)S(1)}, u32[]{:S(2)}, u32[]{:S(2)}) async-start(bf16[8,128,1152]{2,1,0:T(8,128)(2,1)} %bitcast.21), calls=%async_computation | async-start | bytes 4718592 | tf_op jit(solution)/shard_map/all_to_all | solution.py:394
  25.7 4.9 %copy-start.5 = (s32[512,1]{0,1:T(1,128)S(1)}, s32[512,1]{0,1:T(1,128)}, u32[]{:S(2)}) copy-start(s32[512,1]{0,1:T(1,128)} %param.10) | copy-start | bytes 6148
  41.0 26.5 %collective-permute-start.4 = (bf16[256,768]{1,0:T(8,128)(2,1)}, bf16[256,768]{1,0:T(8,128)(2,1)}, u32[]{:S(2)}, u32[]{:S(2)}) collective-permute-start(bf16[256,768]{1,0:T(8,128)(2,1)} %collective-permute-done.1.refs_2_.refs_3_), channel_id=1, source_target_pairs={{0,8},{8,0},{16,24},{24,16},{1,9},{9,1},{17,25},{25,17},{2,10},{10... | collective-permute-start | bytes 1179656 | tf_op jit(solution)/shard_map/ppermute | solution.py:360
  53.2 1.0 copy-start.1
  55.9 1.4 %copy-start = (bf16[8,128,1152]{2,1,0:T(8,128)(2,1)}, bf16[8,128,1152]{2,1,0:T(8,128)(2,1)S(1)}, u32[]{:S(2)}) copy-start(bf16[8,128,1152]{2,1,0:T(8,128)(2,1)S(1)} %all-to-all-done) | copy-start | bytes 7077892
  67.5 9.6 %collective-permute-start.12 = (bf16[256,768]{1,0:T(8,128)(2,1)}, bf16[256,768]{1,0:T(8,128)(2,1)S(1)}, u32[]{:S(2)}, u32[]{:S(2)}) collective-permute-start(bf16[256,768]{1,0:T(8,128)(2,1)} %collective-permute-done.2.refs_3_.refs_4_), channel_id=1, source_target_pairs={{0,8},{8,0},{16,24},{24,16},{1,9},{9,1},{17,25},{25,17},{2,10},{10... | collective-permute-start | bytes 1179656 | tf_op jit(solution)/shard_map/ppermute | solution.py:360
  73.6 5.5 %collective-permute-start.5 = (bf16[128,384]{1,0:T(8,128)(2,1)}, bf16[128,384]{1,0:T(8,128)(2,1)S(1)}, u32[]{:S(2)}, u32[]{:S(2)}) collective-permute-start(bf16[128,384]{1,0:T(8,128)(2,1)} %get-tuple-element.32), channel_id=1, source_target_pairs={{0,1},{1,0},{2,3},{3,2},{4,5},{5,4},{6,7},{7,6},{8,9},{9,8},{10,11... | collective-permute-start | bytes 294920 | tf_op jit(solution)/shard_map/ppermute | solution.py:360
  73.7 5.9 %collective-permute-start.6 = (bf16[128,384]{1,0:T(8,128)(2,1)}, bf16[128,384]{1,0:T(8,128)(2,1)S(1)}, u32[]{:S(2)}, u32[]{:S(2)}) collective-permute-start(bf16[128,384]{1,0:T(8,128)(2,1)} %get-tuple-element.33), channel_id=1, source_target_pairs={{0,2},{1,3},{2,0},{3,1},{4,6},{5,7},{6,4},{7,5},{8,10},{9,11},{10,... | collective-permute-start | bytes 294920 | tf_op jit(solution)/shard_map/ppermute | solution.py:360
  75.2 6.8 %collective-permute-start.7 = (bf16[128,384]{1,0:T(8,128)(2,1)}, bf16[128,384]{1,0:T(8,128)(2,1)S(1)}, u32[]{:S(2)}, u32[]{:S(2)}) collective-permute-start(bf16[128,384]{1,0:T(8,128)(2,1)} %get-tuple-element.34), channel_id=1, source_target_pairs={{0,3},{1,2},{2,1},{3,0},{4,7},{5,6},{6,5},{7,4},{8,11},{9,10},{10,... | collective-permute-start | bytes 294920 | tf_op jit(solution)/shard_map/ppermute | solution.py:360
  77.1 6.3 %copy-start.2 = (bf16[256,768]{1,0:T(8,128)(2,1)}, bf16[256,768]{1,0:T(8,128)(2,1)S(1)}, u32[]{:S(2)}) copy-start(bf16[256,768]{1,0:T(8,128)(2,1)S(1)} %collective-permute-done.12.refs_5_.refs_6_) | copy-start | bytes 1179652
  77.1 19.3 %collective-permute-start.20 = (bf16[256,512]{1,0:T(8,128)(2,1)}, bf16[256,512]{1,0:T(8,128)(2,1)S(1)}, u32[]{:S(2)}, u32[]{:S(2)}) collective-permute-start(bf16[256,512]{1,0:T(8,128)(2,1)} %collective-permute-done.3.refs_4_.refs_5_), channel_id=1, source_target_pairs={{0,8},{8,0},{16,24},{24,16},{1,9},{9,1},{17,25},{25,17},{2,10},{10... | collective-permute-start | bytes 786440 | tf_op jit(solution)/shard_map/ppermute | solution.py:360
  77.6 11.3 %collective-permute-start.8 = (bf16[128,384]{1,0:T(8,128)(2,1)}, bf16[128,384]{1,0:T(8,128)(2,1)S(1)}, u32[]{:S(2)}, u32[]{:S(2)}) collective-permute-start(bf16[128,384]{1,0:T(8,128)(2,1)} %get-tuple-element.35), channel_id=1, source_target_pairs={{0,4},{1,5},{2,6},{3,7},{4,0},{5,1},{6,2},{7,3},{8,12},{9,13},{10,... | collective-permute-start | bytes 294920 | tf_op jit(solution)/shard_map/ppermute | solution.py:360
  79.1 9.7 %copy-start.6 = (bf16[128,384]{1,0:T(8,128)(2,1)}, bf16[128,384]{1,0:T(8,128)(2,1)S(1)}, u32[]{:S(2)}) copy-start(bf16[128,384]{1,0:T(8,128)(2,1)S(1)} %collective-permute-done.5.refs_1_) | copy-start | bytes 294916
  79.1 9.8 %collective-permute-start.9 = (bf16[128,384]{1,0:T(8,128)(2,1)}, bf16[128,384]{1,0:T(8,128)(2,1)S(1)}, u32[]{:S(2)}, u32[]{:S(2)}) collective-permute-start(bf16[128,384]{1,0:T(8,128)(2,1)} %get-tuple-element.36), channel_id=1, source_target_pairs={{0,5},{1,4},{2,7},{3,6},{4,1},{5,0},{6,3},{7,2},{8,13},{9,12},{10,... | collective-permute-start | bytes 294920 | tf_op jit(solution)/shard_map/ppermute | solution.py:360
  79.5 9.2 %copy-start.7 = (bf16[128,384]{1,0:T(8,128)(2,1)}, bf16[128,384]{1,0:T(8,128)(2,1)S(1)}, u32[]{:S(2)}) copy-start(bf16[128,384]{1,0:T(8,128)(2,1)S(1)} %collective-permute-done.6.refs_2_) | copy-start | bytes 294916
  79.5 10.5 %collective-permute-start.10 = (bf16[128,384]{1,0:T(8,128)(2,1)}, bf16[128,384]{1,0:T(8,128)(2,1)S(1)}, u32[]{:S(2)}, u32[]{:S(2)}) collective-permute-start(bf16[128,384]{1,0:T(8,128)(2,1)} %get-tuple-element.37), channel_id=1, source_target_pairs={{0,6},{1,7},{2,4},{3,5},{4,2},{5,3},{6,0},{7,1},{8,14},{9,15},{10,... | collective-permute-start | bytes 294920 | tf_op jit(solution)/shard_map/ppermute | solution.py:360
  82.0 6.8 %copy-start.8 = (bf16[128,384]{1,0:T(8,128)(2,1)}, bf16[128,384]{1,0:T(8,128)(2,1)S(1)}, u32[]{:S(2)}) copy-start(bf16[128,384]{1,0:T(8,128)(2,1)S(1)} %collective-permute-done.7.refs_3_) | copy-start | bytes 294916
  82.0 8.8 %collective-permute-start.11 = (bf16[128,384]{1,0:T(8,128)(2,1)}, bf16[128,384]{1,0:T(8,128)(2,1)S(1)}, u32[]{:S(2)}, u32[]{:S(2)}) collective-permute-start(bf16[128,384]{1,0:T(8,128)(2,1)} %get-tuple-element.38), channel_id=1, source_target_pairs={{0,7},{1,6},{2,5},{3,4},{4,3},{5,2},{6,1},{7,0},{8,15},{9,14},{10,... | collective-permute-start | bytes 294920 | tf_op jit(solution)/shard_map/ppermute | solution.py:360
  88.8 19.1 %copy-start.9 = (bf16[128,384]{1,0:T(8,128)(2,1)}, bf16[128,384]{1,0:T(8,128)(2,1)S(1)}, u32[]{:S(2)}) copy-start(bf16[128,384]{1,0:T(8,128)(2,1)S(1)} %collective-permute-done.8.refs_4_) | copy-start | bytes 294916
  88.8 2.7 %collective-permute-start.13 = (bf16[128,384]{1,0:T(8,128)(2,1)}, bf16[128,384]{1,0:T(8,128)(2,1)S(1)}, u32[]{:S(2)}, u32[]{:S(2)}) collective-permute-start(bf16[128,384]{1,0:T(8,128)(2,1)} %get-tuple-element.41), channel_id=1, source_target_pairs={{0,1},{1,0},{2,3},{3,2},{4,5},{5,4},{6,7},{7,6},{8,9},{9,8},{10,11... | collective-permute-start | bytes 294920 | tf_op jit(solution)/shard_map/ppermute | solution.py:360
  88.9 19.0 %copy-start.10 = (bf16[128,384]{1,0:T(8,128)(2,1)}, bf16[128,384]{1,0:T(8,128)(2,1)S(1)}, u32[]{:S(2)}) copy-start(bf16[128,384]{1,0:T(8,128)(2,1)S(1)} %collective-permute-done.9.refs_5_) | copy-start | bytes 294916
  88.9 5.9 %collective-permute-start.14 = (bf16[128,384]{1,0:T(8,128)(2,1)}, bf16[128,384]{1,0:T(8,128)(2,1)S(1)}, u32[]{:S(2)}, u32[]{:S(2)}) collective-permute-start(bf16[128,384]{1,0:T(8,128)(2,1)} %get-tuple-element.42), channel_id=1, source_target_pairs={{0,2},{1,3},{2,0},{3,1},{4,6},{5,7},{6,4},{7,5},{8,10},{9,11},{10,... | collective-permute-start | bytes 294920 | tf_op jit(solution)/shard_map/ppermute | solution.py:360
  90.1 17.8 %copy-start.11 = (bf16[128,384]{1,0:T(8,128)(2,1)}, bf16[128,384]{1,0:T(8,128)(2,1)S(1)}, u32[]{:S(2)}) copy-start(bf16[128,384]{1,0:T(8,128)(2,1)S(1)} %collective-permute-done.10.refs_6_) | copy-start | bytes 294916
  90.1 11.1 %collective-permute-start.15 = (bf16[128,384]{1,0:T(8,128)(2,1)}, bf16[128,384]{1,0:T(8,128)(2,1)S(1)}, u32[]{:S(2)}, u32[]{:S(2)}) collective-permute-start(bf16[128,384]{1,0:T(8,128)(2,1)} %get-tuple-element.43), channel_id=1, source_target_pairs={{0,3},{1,2},{2,1},{3,0},{4,7},{5,6},{6,5},{7,4},{8,11},{9,10},{10,... | collective-permute-start | bytes 294920 | tf_op jit(solution)/shard_map/ppermute | solution.py:360
  90.8 5.6 %copy-start.4 = (bf16[128,384]{1,0:T(8,128)(2,1)}, bf16[128,384]{1,0:T(8,128)(2,1)S(1)}, u32[]{:S(2)}) copy-start(bf16[128,384]{1,0:T(8,128)(2,1)S(1)} %collective-permute-done.11.refs_7_.refs_1_) | copy-start | bytes 294916
  90.8 11.3 %collective-permute-start.16 = (bf16[128,384]{1,0:T(8,128)(2,1)}, bf16[128,384]{1,0:T(8,128)(2,1)S(1)}, u32[]{:S(2)}, u32[]{:S(2)}) collective-permute-start(bf16[128,384]{1,0:T(8,128)(2,1)} %get-tuple-element.44), channel_id=1, source_target_pairs={{0,4},{1,5},{2,6},{3,7},{4,0},{5,1},{6,2},{7,3},{8,12},{9,13},{10,... | collective-permute-start | bytes 294920 | tf_op jit(solution)/shard_map/ppermute | solution.py:360
  91.6 16.4 %copy-start.12 = (bf16[128,384]{1,0:T(8,128)(2,1)}, bf16[128,384]{1,0:T(8,128)(2,1)S(1)}, u32[]{:S(2)}) copy-start(bf16[128,384]{1,0:T(8,128)(2,1)S(1)} %collective-permute-done.13.refs_9_) | copy-start | bytes 294916
  91.6 11.6 %collective-permute-start.17 = (bf16[128,384]{1,0:T(8,128)(2,1)}, bf16[128,384]{1,0:T(8,128)(2,1)S(1)}, u32[]{:S(2)}, u32[]{:S(2)}) collective-permute-start(bf16[128,384]{1,0:T(8,128)(2,1)} %get-tuple-element.45), channel_id=1, source_target_pairs={{0,5},{1,4},{2,7},{3,6},{4,1},{5,0},{6,3},{7,2},{8,13},{9,12},{10,... | collective-permute-start | bytes 294920 | tf_op jit(solution)/shard_map/ppermute | solution.py:360
  94.8 13.1 %copy-start.13 = (bf16[128,384]{1,0:T(8,128)(2,1)}, bf16[128,384]{1,0:T(8,128)(2,1)S(1)}, u32[]{:S(2)}) copy-start(bf16[128,384]{1,0:T(8,128)(2,1)S(1)} %collective-permute-done.14.refs_10_) | copy-start | bytes 294916
  94.8 8.7 %collective-permute-start.18 = (bf16[128,384]{1,0:T(8,128)(2,1)}, bf16[128,384]{1,0:T(8,128)(2,1)S(1)}, u32[]{:S(2)}, u32[]{:S(2)}) collective-permute-start(bf16[128,384]{1,0:T(8,128)(2,1)} %get-tuple-element.46), channel_id=1, source_target_pairs={{0,6},{1,7},{2,4},{3,5},{4,2},{5,3},{6,0},{7,1},{8,14},{9,15},{10,... | collective-permute-start | bytes 294920 | tf_op jit(solution)/shard_map/ppermute | solution.py:360
  96.4 0.7 copy-start.3
  96.4 7.9 %collective-permute-start.19 = (bf16[128,384]{1,0:T(8,128)(2,1)}, bf16[128,384]{1,0:T(8,128)(2,1)S(1)}, u32[]{:S(2)}, u32[]{:S(2)}) collective-permute-start(bf16[128,384]{1,0:T(8,128)(2,1)} %get-tuple-element.47), channel_id=1, source_target_pairs={{0,7},{1,6},{2,5},{3,4},{4,3},{5,2},{6,1},{7,0},{8,15},{9,14},{10,... | collective-permute-start | bytes 294920 | tf_op jit(solution)/shard_map/ppermute | solution.py:360
  101.2 6.8 %copy-start.14 = (bf16[128,384]{1,0:T(8,128)(2,1)}, bf16[128,384]{1,0:T(8,128)(2,1)S(1)}, u32[]{:S(2)}) copy-start(bf16[128,384]{1,0:T(8,128)(2,1)S(1)} %collective-permute-done.15.refs_11_) | copy-start | bytes 294916
  101.2 4.4 %collective-permute-start.21 = (bf16[128,256]{1,0:T(8,128)(2,1)}, bf16[128,256]{1,0:T(8,128)(2,1)S(1)}, u32[]{:S(2)}, u32[]{:S(2)}) collective-permute-start(bf16[128,256]{1,0:T(8,128)(2,1)} %get-tuple-element.50), channel_id=1, source_target_pairs={{0,1},{1,0},{2,3},{3,2},{4,5},{5,4},{6,7},{7,6},{8,9},{9,8},{10,11... | collective-permute-start | bytes 196616 | tf_op jit(solution)/shard_map/ppermute | solution.py:360
  102.1 5.9 %copy-start.15 = (bf16[128,384]{1,0:T(8,128)(2,1)}, bf16[128,384]{1,0:T(8,128)(2,1)S(1)}, u32[]{:S(2)}) copy-start(bf16[128,384]{1,0:T(8,128)(2,1)S(1)} %collective-permute-done.16.refs_12_) | copy-start | bytes 294916
  102.1 5.1 %collective-permute-start.22 = (bf16[128,256]{1,0:T(8,128)(2,1)}, bf16[128,256]{1,0:T(8,128)(2,1)S(1)}, u32[]{:S(2)}, u32[]{:S(2)}) collective-permute-start(bf16[128,256]{1,0:T(8,128)(2,1)} %get-tuple-element.51), channel_id=1, source_target_pairs={{0,2},{1,3},{2,0},{3,1},{4,6},{5,7},{6,4},{7,5},{8,10},{9,11},{10,... | collective-permute-start | bytes 196616 | tf_op jit(solution)/shard_map/ppermute | solution.py:360
  103.2 4.8 %copy-start.16 = (bf16[128,384]{1,0:T(8,128)(2,1)}, bf16[128,384]{1,0:T(8,128)(2,1)S(1)}, u32[]{:S(2)}) copy-start(bf16[128,384]{1,0:T(8,128)(2,1)S(1)} %collective-permute-done.17.refs_13_) | copy-start | bytes 294916
  103.2 8.5 %collective-permute-start.23 = (bf16[128,256]{1,0:T(8,128)(2,1)}, bf16[128,256]{1,0:T(8,128)(2,1)S(1)}, u32[]{:S(2)}, u32[]{:S(2)}) collective-permute-start(bf16[128,256]{1,0:T(8,128)(2,1)} %get-tuple-element.52), channel_id=1, source_target_pairs={{0,3},{1,2},{2,1},{3,0},{4,7},{5,6},{6,5},{7,4},{8,11},{9,10},{10,... | collective-permute-start | bytes 196616 | tf_op jit(solution)/shard_map/ppermute | solution.py:360
  103.5 4.5 %copy-start.17 = (bf16[128,384]{1,0:T(8,128)(2,1)}, bf16[128,384]{1,0:T(8,128)(2,1)S(1)}, u32[]{:S(2)}) copy-start(bf16[128,384]{1,0:T(8,128)(2,1)S(1)} %collective-permute-done.18.refs_14_) | copy-start | bytes 294916
  103.5 8.2 %collective-permute-start.24 = (bf16[128,256]{1,0:T(8,128)(2,1)}, bf16[128,256]{1,0:T(8,128)(2,1)S(1)}, u32[]{:S(2)}, u32[]{:S(2)}) collective-permute-start(bf16[128,256]{1,0:T(8,128)(2,1)} %get-tuple-element.53), channel_id=1, source_target_pairs={{0,4},{1,5},{2,6},{3,7},{4,0},{5,1},{6,2},{7,3},{8,12},{9,13},{10,... | collective-permute-start | bytes 196616 | tf_op jit(solution)/shard_map/ppermute | solution.py:360
  104.3 3.7 %copy-start.18 = (bf16[128,384]{1,0:T(8,128)(2,1)}, bf16[128,384]{1,0:T(8,128)(2,1)S(1)}, u32[]{:S(2)}) copy-start(bf16[128,384]{1,0:T(8,128)(2,1)S(1)} %collective-permute-done.19.refs_15_) | copy-start | bytes 294916
  104.3 7.5 %collective-permute-start.25 = (bf16[128,256]{1,0:T(8,128)(2,1)}, bf16[128,256]{1,0:T(8,128)(2,1)S(1)}, u32[]{:S(2)}, u32[]{:S(2)}) collective-permute-start(bf16[128,256]{1,0:T(8,128)(2,1)} %get-tuple-element.54), channel_id=1, source_target_pairs={{0,5},{1,4},{2,7},{3,6},{4,1},{5,0},{6,3},{7,2},{8,13},{9,12},{10,... | collective-permute-start | bytes 196616 | tf_op jit(solution)/shard_map/ppermute | solution.py:360
  105.6 7.1 %copy-start.19 = (bf16[128,256]{1,0:T(8,128)(2,1)}, bf16[128,256]{1,0:T(8,128)(2,1)S(1)}, u32[]{:S(2)}) copy-start(bf16[128,256]{1,0:T(8,128)(2,1)S(1)} %collective-permute-done.21.refs_1_) | copy-start | bytes 196612
  105.6 6.2 %collective-permute-start.26 = (bf16[128,256]{1,0:T(8,128)(2,1)}, bf16[128,256]{1,0:T(8,128)(2,1)S(1)}, u32[]{:S(2)}, u32[]{:S(2)}) collective-permute-start(bf16[128,256]{1,0:T(8,128)(2,1)} %get-tuple-element.55), channel_id=1, source_target_pairs={{0,6},{1,7},{2,4},{3,5},{4,2},{5,3},{6,0},{7,1},{8,14},{9,15},{10,... | collective-permute-start | bytes 196616 | tf_op jit(solution)/shard_map/ppermute | solution.py:360
  107.1 5.5 %copy-start.20 = (bf16[128,256]{1,0:T(8,128)(2,1)}, bf16[128,256]{1,0:T(8,128)(2,1)S(1)}, u32[]{:S(2)}) copy-start(bf16[128,256]{1,0:T(8,128)(2,1)S(1)} %collective-permute-done.22.refs_2_) | copy-start | bytes 196612
  107.2 5.5 %collective-permute-start.27 = (bf16[128,256]{1,0:T(8,128)(2,1)}, bf16[128,256]{1,0:T(8,128)(2,1)S(1)}, u32[]{:S(2)}, u32[]{:S(2)}) collective-permute-start(bf16[128,256]{1,0:T(8,128)(2,1)} %get-tuple-element.56), channel_id=1, source_target_pairs={{0,7},{1,6},{2,5},{3,4},{4,3},{5,2},{6,1},{7,0},{8,15},{9,14},{10,... | collective-permute-start | bytes 196616 | tf_op jit(solution)/shard_map/ppermute | solution.py:360
  111.7 0.9 copy-start.21
  111.7 0.9 copy-start.22
  111.8 0.9 copy-start.23
  111.8 0.9 copy-start.24
  112.6 0.6 copy-start.25

commit v5 on v4

v5 whole, which is shorter than its diff:
```python
import functools
import math

import jax
import jax.numpy as jnp
from jax import lax
from jax.experimental import pallas as pl
from jax.experimental.pallas import tpu as pltpu
from jax.sharding import PartitionSpec as P

HEADS = 8
BLK = 128
GROUPS = (4, 4)
norm_eps = 1e-06
F32 = jnp.float32
BF16 = jnp.bfloat16
MIB = 1024 * 1024
WAIT_COST = 20.0
KERNEL_MIB = 24


def params(mib):
    return pltpu.CompilerParams(vmem_limit_bytes=mib * MIB)


def cost(flops, nbytes, transcendentals=0):
    return pl.CostEstimate(
        flops=int(flops), bytes_accessed=int(nbytes), transcendentals=int(transcendentals)
    )


def silu(v):
    half = 0.5 * v
    return half * jnp.tanh(half) + half


def earlier_mask(rows):
    first = lax.broadcasted_iota(jnp.int32, (rows, rows), 0)
    second = lax.broadcasted_iota(jnp.int32, (rows, rows), 1)
    return (first < second).astype(BF16)


def slot_row(owner_row, columns, capacity):
    rows = owner_row.shape[1]
    users = lax.broadcasted_iota(jnp.int32, (columns, rows), 0)
    mine = users == owner_row
    before = jnp.dot(mine.astype(BF16), earlier_mask(rows), preferred_element_type=F32)
    rank = jnp.sum(jnp.where(mine, before, 0.0), axis=0, keepdims=True)
    return owner_row.astype(F32) * capacity + rank


def whole(count=1):
    return [pl.BlockSpec(memory_space=pltpu.VMEM)] * count


def unread(arrays):
    return [pl.BlockSpec(memory_space=pl.ANY)] * len(arrays)


def query_kernel(columns, capacity, owner_ref, visible_ref, x_ref, w_ref, send_ref):
    rows, width = x_ref.shape
    slots = columns * capacity
    slot = slot_row(owner_ref[...], columns, capacity).astype(jnp.int32)
    index = lax.broadcasted_iota(jnp.int32, (slots, rows), 0)
    place = (index == slot).astype(BF16)
    tile = min(256, width)
    for start in range(0, width, tile):
        span = slice(start, start + tile)
        hidden = jnp.dot(x_ref[...], w_ref[:, span], preferred_element_type=F32)
        moved = jnp.dot(place, silu(hidden).astype(BF16), preferred_element_type=F32)
        send_ref[:, span] = moved.astype(BF16)
    seen = jnp.broadcast_to(visible_ref[...].astype(F32), (BLK, rows)).T.astype(BF16)
    send_ref[:, width:] = jnp.dot(place, seen, preferred_element_type=F32).astype(BF16)


def project_queries(owner_row, visible_row, cand_x, w_in, columns, capacity):
    rows, width = cand_x.shape
    slots = columns * capacity
    return pl.pallas_call(
        functools.partial(query_kernel, columns, capacity),
        in_specs=whole(4),
        out_specs=whole()[0],
        out_shape=jax.ShapeDtypeStruct((slots, width + BLK), BF16),
        compiler_params=params(KERNEL_MIB),
        cost_estimate=cost(
            2 * rows * width * width + 2 * slots * rows * width,
            2 * (rows * width + width * width + slots * width),
            rows * width,
        ),
        name="project_queries",
    )(owner_row, visible_row, cand_x, w_in)


def gate_kernel(x_ref, w_ref, gate_ref):
    width = x_ref.shape[1]
    tile = min(256, width)
    for start in range(0, width, tile):
        columns = w_ref[:, width + start : width + start + tile]
        hidden = jnp.dot(x_ref[...], columns, preferred_element_type=F32)
        gate_ref[:, start : start + tile] = silu(hidden).astype(BF16)


def project_gate(cand_x, w_in):
    rows, width = cand_x.shape
    return pl.pallas_call(
        gate_kernel,
        in_specs=whole(2),
        out_specs=whole()[0],
        out_shape=jax.ShapeDtypeStruct((rows, width), BF16),
        compiler_params=params(KERNEL_MIB),
        cost_estimate=cost(
            2 * rows * width * width, 2 * (2 * rows * width + width * width), rows * width
        ),
        name="project_gate",
    )(cand_x, w_in)


def slots_kernel(columns, capacity, owner_ref, *refs):
    slot = slot_row(owner_ref[...], columns, capacity)
    refs[-1][...] = jnp.broadcast_to(slot, (BLK, slot.shape[1])).T.astype(jnp.int32)


def slot_column(owner_row, columns, capacity, after):
    rows = owner_row.shape[1]
    return pl.pallas_call(
        functools.partial(slots_kernel, columns, capacity),
        in_specs=whole() + unread(after),
        out_specs=whole()[0],
        out_shape=jax.ShapeDtypeStruct((rows, BLK), jnp.int32),
        compiler_params=params(KERNEL_MIB),
        cost_estimate=cost(WAIT_COST * 1e9, 4 * rows * BLK),
        name="slot_column",
    )(owner_row, *after)


def attend_kernel(size, heads, first, starts, behind, has_base, outs, place_ref, *refs):
    refs = refs[behind:]
    rows_ref, refs = refs[0], refs[1:]
    parts, refs = refs[: len(starts)], refs[len(starts) :]
    base_ref = refs[0] if has_base else None
    out_refs, shown = refs[int(has_base) : int(has_base) + outs], refs[int(has_base) + outs]
    result = out_refs[0] if outs == 1 else refs[-1]
    slots = rows_ref.shape[0]
    keys = parts[0].shape[0]
    blocks = keys // BLK
    seen = rows_ref[:, HEADS * size :].astype(F32)
    for number in range(len(parts)):
        for block in range(blocks):
            start = (place_ref[2 + number] * blocks + block).astype(F32)
            shown[number * blocks + block] = jnp.where(start < seen, 0.5 / math.sqrt(size), 0.0)
    row = lax.broadcasted_iota(jnp.int32, (keys, size), 0)
    tile = min(512, slots)

    def columns(head):
        return pl.ds(pl.multiple_of(head * size, size), size)

    def one_head(head, carry):
        values = []
        for number, part in enumerate(parts):
            inside = row + place_ref[2 + number] * keys < place_ref[0]
            value = part[:, columns(starts[number][1] + head)].astype(F32)
            values.append(jnp.where(inside, value, 0.0).astype(BF16))
        values = jnp.concatenate(values, axis=0)
        for start in range(0, slots, tile):
            span = slice(start, start + tile)
            queries = rows_ref[span, columns(first + head)]
            weights = []
            for number, part in enumerate(parts):
                scores = lax.dot_general(
                    queries,
                    part[:, columns(starts[number][0] + head)],
                    (((1,), (1,)), ((), ())),
                    preferred_element_type=F32,
                )
                for block in range(blocks):
                    half = scores[:, block * BLK : (block + 1) * BLK]
                    half = half * shown[number * blocks + block, span, :]
                    weights.append((half * jnp.tanh(half) + half).astype(BF16))
            total = jnp.dot(
                jnp.concatenate(weights, axis=1), values, preferred_element_type=F32
            )
            if has_base:
                total = total + base_ref[span, columns(first + head)]
            result[span, columns(head)] = total.astype(result.dtype)
        return carry

    lax.fori_loop(0, heads, one_head, 0)
    if outs > 1:
        capacity = slots // outs
        for number, ref in enumerate(out_refs):
            start = pl.multiple_of((place_ref[1] ^ number) * capacity, capacity)
            ref[...] = result[pl.ds(start, capacity), :]


def attend(place, after, rows, segments, base, first, heads, size, outs, dtype):
    slots = rows.shape[0]
    keys = segments[0][0].shape[0]
    count = len(segments)
    starts = [(key, value) for _, key, value in segments]
    extra = [] if base is None else [base]
    scratch = [pltpu.VMEM((count * (keys // BLK), slots, BLK), F32)]
    if outs > 1:
        scratch.append(pltpu.VMEM((slots, heads * size), BF16))
    return pl.pallas_call(
        functools.partial(
            attend_kernel, size, heads, first, starts, len(after), base is not None, outs
        ),
        in_specs=[pl.BlockSpec(memory_space=pltpu.SMEM)]
        + unread(after)
        + whole(1 + count + len(extra)),
        out_specs=whole(outs),
        out_shape=[jax.ShapeDtypeStruct((slots // outs, heads * size), dtype)] * outs,
        scratch_shapes=scratch,
        compiler_params=params(KERNEL_MIB),
        cost_estimate=cost(
            4 * slots * keys * count * heads * size,
            2 * (2 * slots + count * keys * 2) * heads * size,
            slots * keys * count * heads,
        ),
        name="attend",
    )(place, *after, rows, *[piece for piece, _, _ in segments], *extra)


def placement(slot, slots):
    lane = lax.broadcasted_iota(jnp.int32, (1, BLK), 1)
    return jnp.concatenate(
        [(lane + start == slot).astype(BF16) for start in range(0, slots, BLK)], axis=1
    )


def collect_kernel(groups, slot_ref, *refs):
    parts, out_ref = refs[:-1], refs[-1]
    each = len(parts) // groups
    place = placement(slot_ref[...], each * parts[0].shape[0])
    first = 0
    for group in range(groups):
        rows = jnp.concatenate(
            [part[...] for part in parts[group * each : (group + 1) * each]], axis=0
        )
        last = first + rows.shape[1]
        out_ref[:, first:last] = jnp.dot(place, rows, preferred_element_type=F32).astype(BF16)
        first = last


def collect(slot, groups):
    rows = slot.shape[0]
    parts = [part for group in groups for part in group]
    width = sum(group[0].shape[1] for group in groups)
    slots = len(groups[0]) * groups[0][0].shape[0]
    vmem = pl.BlockSpec(memory_space=pltpu.VMEM)
    return pl.pallas_call(
        functools.partial(collect_kernel, len(groups)),
        in_specs=[vmem] * (1 + len(parts)),
        out_specs=vmem,
        out_shape=jax.ShapeDtypeStruct((rows, width), BF16),
        compiler_params=params(KERNEL_MIB),
        cost_estimate=cost(2 * rows * slots * width, 2 * (rows + slots) * width),
        name="collect",
    )(slot, *parts)


def finish_kernel(slot_ref, gain_ref, early_ref, gate_ref, x_ref, w_ref, *refs):
    parts, (out_hbm, out_ref, sems) = refs[:-3], refs[-3:]
    rows = x_ref.shape[0]
    returned = jnp.concatenate([part[...] for part in parts], axis=0)
    place = placement(slot_ref[...], returned.shape[0])
    late = jnp.dot(place, returned, preferred_element_type=F32)
    tile = rows // 2
    stores = []
    for half in range(2):
        span = slice(half * tile, (half + 1) * tile)
        attn = jnp.concatenate([early_ref[span, :].astype(F32), late[span, :]], axis=1)
        centered = attn - jnp.mean(attn, axis=1, keepdims=True)
        variance = jnp.mean(centered * centered, axis=1, keepdims=True)
        normed = (centered * lax.rsqrt(variance + norm_eps) * gain_ref[...]).astype(BF16)
        mixed = (normed.astype(F32) * gate_ref[span, :].astype(F32)).astype(BF16)
        projected = jnp.dot(mixed, w_ref[...], preferred_element_type=F32)
        out_ref[span, :] = (x_ref[span, :].astype(F32) + projected).astype(BF16)
        store = pltpu.make_async_copy(out_ref.at[span, :], out_hbm.at[span, :], sems.at[half])
        store.start()
        stores.append(store)
    for store in stores:
        store.wait()


def finish(slot, early, gate, cand_x, ln_gain, w_out, parts):
    rows, width = cand_x.shape
    slots = len(parts) * parts[0].shape[0]
    return pl.pallas_call(
        finish_kernel,
        in_specs=whole(6 + len(parts)),
        out_specs=pl.BlockSpec(memory_space=pl.ANY),
        out_shape=jax.ShapeDtypeStruct((rows, width), BF16),
        scratch_shapes=[pltpu.VMEM((rows, width), BF16), pltpu.SemaphoreType.DMA((2,))],
        compiler_params=params(KERNEL_MIB),
        cost_estimate=cost(
            2 * rows * width * (width + slots), 2 * (3 * rows * width + width * width + slots * width)
        ),
        name="finish",
    )(slot, ln_gain.reshape(1, width), early, gate, cand_x, w_out, *parts)


def swap(array, axis, bits, count):
    return lax.ppermute(array, axis, [(i, i ^ bits) for i in range(count)])


def exchange(blocks):
    count = len(blocks)
    return [block if d == 0 else swap(block, "cand", d, count) for d, block in enumerate(blocks)]


def per_device(cand_x, cand_user, visible, hist_len, kv_cache, w_in, w_out, ln_gain):
    rows, width = cand_x.shape
    columns = lax.axis_size("cand")
    count = lax.axis_size("user")
    size = width // HEADS
    capacity = 2 * rows // columns
    own = kv_cache[0]
    me = lax.axis_index("cand").astype(jnp.int32)
    owner_row = cand_user.reshape(1, rows)
    visible_row = visible.reshape(1, rows)

    spans = [(sum(GROUPS[:number]), heads) for number, heads in enumerate(GROUPS)]
    far = []
    for first, heads in spans:
        lo, hi = first * size, (first + heads) * size
        held = {0: jnp.concatenate([own[:, lo:hi], own[:, width + lo : width + hi]], axis=1)}
        bit = count // 2
        while bit > 1:
            for key in sorted(held):
                held[key | bit] = swap(held[key], "user", bit, count)
            bit //= 2
        far.append(held)
    evens = sorted(far[0])
    near = swap(own, "user", 1, count)

    send = project_queries(owner_row, visible_row, cand_x, w_in, columns, capacity)
    got = lax.all_to_all(
        send.reshape(columns, capacity, -1), "cand", split_axis=0, concat_axis=0, tiled=True
    ).reshape(columns * capacity, -1)
    gate = project_gate(cand_x, w_in)
    arrived = [near] + [held[evens[-1]] for held in far]
    slot = slot_column(owner_row ^ me, columns, capacity, [gate] + arrived)
    position = lax.axis_index("user").astype(jnp.int32)
    order = [0, 1] + evens[1:] + [key | 1 for key in evens[1:]]
    shards = position ^ jnp.array(order, jnp.int32)
    head = jnp.concatenate([hist_len, me[None]])
    place_first = jnp.concatenate([head, shards[:2]])
    place = jnp.concatenate([head, shards[2:]])
    base = attend(
        place_first,
        [slot],
        got,
        [(own, 0, HEADS), (near, 0, HEADS)],
        None,
        0,
        HEADS,
        size,
        1,
        F32,
    )[0]

    def forward(number, behind):
        parts = [far[number][key] for key in evens[1:]]
        if behind is not None:
            parts, _ = lax.optimization_barrier((parts, behind))
        return [swap(part, "user", 1, count) for part in parts]

    cuts = [forward(0, None)]
    returned = []
    after = []
    done = base
    for number, (first, heads) in enumerate(spans):
        if number + 1 < len(spans):
            cuts.append(forward(number + 1, (cuts[number], done)))
        segments = [(far[number][key], 0, heads) for key in evens[1:]]
        segments += [(cut, 0, heads) for cut in cuts[number]]
        attn = attend(place, after, got, segments, base, first, heads, size, columns, BF16)
        done = attn[0]
        after = [done] + [group[-1] for group in returned[-1:]]
        returned.append(exchange(attn))
    early = collect(slot, returned[:-1])
    return finish(slot, early, gate, cand_x, ln_gain, w_out, returned[-1])


def solution(mesh):
    in_specs = (
        P(("user", "cand"), None),
        P(("user", "cand"), None),
        P(("user", "cand")),
        P("cand"),
        P("cand", "user", None),
        P(),
        P(),
        P(),
    )
    out_specs = P(("user", "cand"), None)
    return jax.shard_map(
        per_device, mesh=mesh, in_specs=in_specs, out_specs=out_specs, check_vma=False
    )
```

time: 121 us -> 107 us (0.88)
  Pallas kernels: 49.2 us -> 26.5 us
  waiting for transfers between devices: 23.7 us -> 40.3 us
  starting transfers between devices: 35.6 us -> 28.3 us
  local copies, waits for them, and re-layouts: 6.13 us -> 8.82 us
  other arithmetic: 4.1 us -> 1.9 us
    pallas_call x7 -> x6, Pallas kernels: 43.8 us -> 25.5 us  [the longest x3 17.7 us: attend(): pl.pallas_call(functools.partial(attend_kernel, size, heads, first, start...]
    ppermute x28 -> x19, waiting for transfers between devices: 23.7 us -> 40.3 us  [swap(): return lax.ppermute(array, axis, [(i, i ^ bits) for i in range(count)])]
    ppermute x28 -> x19, starting transfers between devices: 31.8 us -> 24.5 us  [swap(): return lax.ppermute(array, axis, [(i, i ^ bits) for i in range(count)])]
    unnamed x52 -> x32, local copies, waits for them, and re-layouts: 3.76 us -> 7.49 us
    pallas_call x1, Pallas kernels: 3.71 us -> 0.71 us  [collect(): pl.pallas_call(functools.partial(collect_kernel, len(groups)), in_specs=[...]
    pallas_call x1, Pallas kernels: 1.69 us -> 0.32 us  [slot_column(): pl.pallas_call(functools.partial(slots_kernel, columns, capacity), in_spe...]
  transfers between devices with their start and end apart: 29 -> 20, of which waited for: 6 -> 7; matrix products, arithmetic and copies ran while one was open for 5% -> 3% of each run, Pallas kernels for 36% -> 22%
where the time goes in v5:
time: 107 us
  waiting for transfers between devices  40.3 us (38%)
  starting transfers between devices  28.3 us (26%)
  Pallas kernels  26.5 us (25%)
  local copies, waits for them, and re-layouts  8.82 us (8%)
  other arithmetic  1.9 us (2%)
    ppermute x19, waiting for transfers between devices, swap(): return lax.ppermute(array, axis, [(i, i ^ bits) for i in range(count)])  40.3 us
    ppermute x19, starting transfers between devices, swap(): return lax.ppermute(array, axis, [(i, i ^ bits) for i in range(count)])  24.5 us
    pallas_call x3, Pallas kernels, attend(): pl.pallas_call(functools.partial(attend_kernel, size, heads, first, start...  17.7 us
    unnamed x32, local copies, waits for them, and re-layouts  7.49 us
    all_to_all x1, starting transfers between devices, per_device(): lax.all_to_all(send.reshape(columns, capacity, -1), 'cand', split_axis=0,...  3.86 us
    pallas_call x1, Pallas kernels, project_queries(): pl.pallas_call(functools.partial(query_kernel, columns, capacity), in_spe...  3.25 us
    pallas_call x1, Pallas kernels, finish(): pl.pallas_call(finish_kernel, in_specs=whole(6 + len(parts)), out_specs=p...  3.15 us
  transfers between devices with their start and end apart: 20, of which 7 were waited for; matrix products, arithmetic and copies ran while one was open for 3% of the time, Pallas kernels for 22%

profile of v5, /device:TPU:0, one launch (start us, length us, event | category | flops | bytes accessed | tf_op | source)
XLA Modules:
  0.0 106.8 jit_solution(6670712740944902907)
XLA Ops:
  0.0 3.1 %collective-permute-start = (bf16[256,2048]{1,0:T(8,128)(2,1)}, bf16[256,2048]{1,0:T(8,128)(2,1)}, u32[]{:S(2)}, u32[]{:S(2)}) collective-permute-start(bf16[256,2048]{1,0:T(8,128)(2,1)} %bitcast.11), channel_id=1, source_target_pairs={{0,8},{8,0},{16,24},{24,16},{1,9},{9,1},{17,25},{25,17},{2,10},{10... | collective-permute-start | bytes 3145736 | tf_op jit(solution)/shard_map/ppermute | solution.py:304
  3.1 1.3 %fusion = (bf16[256,512]{1,0:T(8,128)(2,1)S(1)}, bf16[256,512]{1,0:T(8,128)(2,1)S(1)}, bf16[256,512]{1,0:T(8,128)(2,1)S(1)}, bf16[256,512]{1,0:T(8,128)(2,1)S(1)}) fusion(bf16[256,2048]{1,0:T(8,128)(2,1)} %bitcast.12), kind=kLoop, calls=%fused_computation.7 | loop fusion | bytes 2097152 | tf_op jit(solution)/shard_map/slice | solution.py:327
  4.4 0.9 pad_maximum_fusion
  5.2 2.6 %collective-permute-start.1 = (bf16[256,1024]{1,0:T(8,128)(2,1)}, bf16[256,1024]{1,0:T(8,128)(2,1)}, u32[]{:S(2)}, u32[]{:S(2)}) collective-permute-start(bf16[256,1024]{1,0:T(8,128)(2,1)} %pad_maximum_fusion), channel_id=1, source_target_pairs={{0,16},{8,24},{16,0},{24,8},{1,17},{9,25},{17,1},{25,9},{2,18},{10... | collective-permute-start | bytes 1572872 | tf_op jit(solution)/shard_map/ppermute | solution.py:304
  7.8 0.9 pad_maximum_fusion.1
  8.7 0.3 collective-permute-start.2
  9.0 1.2 %copy-done.4 = bf16[512,1024]{1,0:T(8,128)(2,1)S(1)} copy-done((bf16[512,1024]{1,0:T(8,128)(2,1)S(1)}, bf16[512,1024]{1,0:T(8,128)(2,1)}, u32[]{:S(2)}) %copy-start.4) | copy-done | bytes 1048600
  10.3 3.2 %project_queries.1 = bf16[1024,1152]{1,0:T(8,128)(2,1)S(1)} custom-call(s32[1,512]{1,0:T(1,128)S(1)} %bitcast.15, s32[1,512]{1,0:T(1,128)S(1)} %bitcast.17, bf16[512,1024]{1,0:T(8,128)(2,1)S(1)} %copy-done.4, bf16[1024,2048]{1,0:T(8,128)(2,1)S(1)} %copy-done.1), custom_call_target="tpu_custom_call" | custom-call | flops 2147483648 | bytes 5242880 | tf_op jit(solution)/shard_map/project_queries/pallas_call | solution.py:79
  13.5 1.4 %copy-done.3 = bf16[1024,1152]{1,0:T(8,128)(2,1)} copy-done((bf16[1024,1152]{1,0:T(8,128)(2,1)}, bf16[1024,1152]{1,0:T(8,128)(2,1)S(1)}, u32[]{:S(2)}) %copy-start.3) | copy-done | bytes 2359320
  14.9 3.9 %all-to-all-start = ((bf16[8,128,1152]{2,1,0:T(8,128)(2,1)}), bf16[8,128,1152]{2,1,0:T(8,128)(2,1)S(1)}, u32[]{:S(2)}, u32[]{:S(2)}) async-start(bf16[8,128,1152]{2,1,0:T(8,128)(2,1)} %bitcast.14), calls=%async_computation | async-start | bytes 4718592 | tf_op jit(solution)/shard_map/all_to_all | solution.py:338
  19.5 0.0 copy-start.2
  19.5 2.2 %copy-done.2 = bf16[1024,2048]{1,0:T(8,128)(2,1)S(1)} copy-done((bf16[1024,2048]{1,0:T(8,128)(2,1)S(1)}, bf16[1024,2048]{1,0:T(8,128)(2,1)}, u32[]{:S(2)}) %copy-start.2) | copy-done | bytes 4194328
  21.7 1.4 %project_gate.1.refs_0_.gate_ref = bf16[512,1024]{1,0:T(8,128)(2,1)S(1)} custom-call(bf16[512,1024]{1,0:T(8,128)(2,1)S(1)} %copy-done.5, bf16[1024,2048]{1,0:T(8,128)(2,1)S(1)} %copy-done.2), custom_call_target="tpu_custom_call" | custom-call | flops 1073741824 | bytes 4194304 | tf_op jit(solution)/shard_map/project_gate/pallas_call | solution.py:105
  23.1 0.1 fusion.1
  23.1 0.1 pad_add_fusion.2.place_ref
  23.2 15.0 %collective-permute-done.1.refs_2_.refs_1_ = bf16[256,1024]{1,0:T(8,128)(2,1)} collective-permute-done((bf16[256,1024]{1,0:T(8,128)(2,1)}, bf16[256,1024]{1,0:T(8,128)(2,1)}, u32[]{:S(2)}, u32[]{:S(2)}) %collective-permute-start.1) | collective-permute-done | bytes 524320 | tf_op jit(solution)/shard_map/ppermute | solution.py:304
  38.3 3.5 %collective-permute-start.3 = (bf16[256,1024]{1,0:T(8,128)(2,1)}, bf16[256,1024]{1,0:T(8,128)(2,1)}, u32[]{:S(2)}, u32[]{:S(2)}) collective-permute-start(bf16[256,1024]{1,0:T(8,128)(2,1)} %collective-permute-done.1.refs_2_.refs_1_), channel_id=1, source_target_pairs={{0,8},{8,0},{16,24},{24,16},{1,9},{9,1},{17,25},{25,17},{2,10},{10... | collective-permute-start | bytes 1572872 | tf_op jit(solution)/shard_map/ppermute | solution.py:304
  41.8 11.9 %collective-permute-done.2.refs_3_.refs_2_ = bf16[256,1024]{1,0:T(8,128)(2,1)} collective-permute-done((bf16[256,1024]{1,0:T(8,128)(2,1)}, bf16[256,1024]{1,0:T(8,128)(2,1)}, u32[]{:S(2)}, u32[]{:S(2)}) %collective-permute-start.2) | collective-permute-done | bytes 524320 | tf_op jit(solution)/shard_map/ppermute | solution.py:304
  53.7 0.0 collective-permute-done.refs_1_.refs_3_
  53.7 0.3 slot_column.1.refs_0_.slot_ref
  54.0 0.0 copy-start.7
  54.0 1.0 copy-done.7
  55.0 0.7 copy-done.9
  55.7 0.0 all-to-all-done
  55.7 0.9 copy-done.10
  56.7 8.1 %attend.3.refs_3_.refs_4_ = f32[1024,1024]{1,0:T(8,128)S(1)} custom-call(s32[4]{0:T(128)S(1)} %pad_add_fusion.2.place_ref, s32[512,128]{1,0:T(8,128)S(1)} %copy-done.10, bf16[1024,1152]{1,0:T(8,128)(2,1)S(1)} %bitcast.8, bf16[256,2048]{1,0:T(8,128)(2,1)S(1)} %bitcast.13, bf16[256,2048]{1,0:T(8,128)(2,1)} %collective-permute-done.refs_1_.refs_3_), custom_call_target="tpu_custom_call" | custom-call | flops 2147483648 | bytes 6291456 | tf_op jit(solution)/shard_map/attend/pallas_call | solution.py:204
  64.7 0.0 collective-permute-done.3.refs_2_
  64.7 0.1 collective-permute-start.11
  64.8 0.1 pad_add_fusion.place_ref
  64.9 4.8 %attend.4 = (bf16[128,512]{1,0:T(8,128)(2,1)S(1)}, bf16[128,512]{1,0:T(8,128)(2,1)S(1)}, bf16[128,512]{1,0:T(8,128)(2,1)S(1)}, bf16[128,512]{1,0:T(8,128)(2,1)S(...) custom-call(s32[4]{0:T(128)S(1)} %pad_add_fusion.place_ref, ...), custom_call_target="tpu_custom_call" | custom-call | flops 1073741824 | bytes 3145728 | tf_op jit(solution)/shard_map/attend/pallas_call | solution.py:204
  69.7 0.1 collective-permute-start.4
  69.8 1.6 %collective-permute-start.5 = (bf16[128,512]{1,0:T(8,128)(2,1)S(1)}, bf16[128,512]{1,0:T(8,128)(2,1)S(1)}, u32[]{:S(2)}, u32[]{:S(2)}) collective-permute-start(bf16[128,512]{1,0:T(8,128)(2,1)S(1)} %get-tuple-element.24), channel_id=1, source_target_pairs={{0,2},{1,3},{2,0},{3,1},{4,6},{5,7},{6,4},{7,5},{8,10},{9,11},{10,... | collective-permute-start | bytes 393224 | tf_op jit(solution)/shard_map/ppermute | solution.py:304
  71.3 0.3 collective-permute-start.6
  71.6 1.5 %collective-permute-start.7 = (bf16[128,512]{1,0:T(8,128)(2,1)S(1)}, bf16[128,512]{1,0:T(8,128)(2,1)S(1)}, u32[]{:S(2)}, u32[]{:S(2)}) collective-permute-start(bf16[128,512]{1,0:T(8,128)(2,1)S(1)} %get-tuple-element.26), channel_id=1, source_target_pairs={{0,4},{1,5},{2,6},{3,7},{4,0},{5,1},{6,2},{7,3},{8,12},{9,13},{10,... | collective-permute-start | bytes 393224 | tf_op jit(solution)/shard_map/ppermute | solution.py:304
  73.2 4.0 %collective-permute-done.11.refs_3_ = bf16[256,1024]{1,0:T(8,128)(2,1)S(1)} collective-permute-done((bf16[256,1024]{1,0:T(8,128)(2,1)}, bf16[256,1024]{1,0:T(8,128)(2,1)S(1)}, u32[]{:S(2)}, u32[]{:S(2)}) %collective-permute-start.11) | collective-permute-done | bytes 524320 | tf_op jit(solution)/shard_map/ppermute | solution.py:304
  77.1 0.0 collective-permute-start.8
  77.2 0.0 copy-start.13
  77.2 0.0 copy-start.14
  77.2 4.8 %attend.5 = (bf16[128,512]{1,0:T(8,128)(2,1)S(1)}, bf16[128,512]{1,0:T(8,128)(2,1)S(1)}, bf16[128,512]{1,0:T(8,128)(2,1)S(1)}, bf16[128,512]{1,0:T(8,128)(2,1)S(...) custom-call(s32[4]{0:T(128)S(1)} %pad_add_fusion.place_ref, ...), custom_call_target="tpu_custom_call" | custom-call | flops 1073741824 | bytes 3145728 | tf_op jit(solution)/shard_map/attend/pallas_call | solution.py:204
  82.0 0.0 collective-permute-done.4.refs_1_
  82.0 2.5 %collective-permute-start.9 = (bf16[128,512]{1,0:T(8,128)(2,1)S(1)}, bf16[128,512]{1,0:T(8,128)(2,1)S(1)}, u32[]{:S(2)}, u32[]{:S(2)}) collective-permute-start(bf16[128,512]{1,0:T(8,128)(2,1)S(1)} %get-tuple-element.28), channel_id=1, source_target_pairs={{0,6},{1,7},{2,4},{3,5},{4,2},{5,3},{6,0},{7,1},{8,14},{9,15},{10,... | collective-permute-start | bytes 393224 | tf_op jit(solution)/shard_map/ppermute | solution.py:304
  84.5 0.0 collective-permute-done.5.refs_2_
  84.5 1.4 %collective-permute-start.10 = (bf16[128,512]{1,0:T(8,128)(2,1)S(1)}, bf16[128,512]{1,0:T(8,128)(2,1)S(1)}, u32[]{:S(2)}, u32[]{:S(2)}) collective-permute-start(bf16[128,512]{1,0:T(8,128)(2,1)S(1)} %get-tuple-element.29), channel_id=1, source_target_pairs={{0,7},{1,6},{2,5},{3,4},{4,3},{5,2},{6,1},{7,0},{8,15},{9,14},{10,... | collective-permute-start | bytes 393224 | tf_op jit(solution)/shard_map/ppermute | solution.py:304
  86.0 0.0 collective-permute-done.6.refs_3_
  86.0 0.0 collective-permute-start.12
  86.0 0.0 collective-permute-done.7.refs_4_
  86.0 1.6 %collective-permute-start.13 = (bf16[128,512]{1,0:T(8,128)(2,1)S(1)}, bf16[128,512]{1,0:T(8,128)(2,1)S(1)}, u32[]{:S(2)}, u32[]{:S(2)}) collective-permute-start(bf16[128,512]{1,0:T(8,128)(2,1)S(1)} %get-tuple-element.33), channel_id=1, source_target_pairs={{0,2},{1,3},{2,0},{3,1},{4,6},{5,7},{6,4},{7,5},{8,10},{9,11},{10,... | collective-permute-start | bytes 393224 | tf_op jit(solution)/shard_map/ppermute | solution.py:304
  87.5 0.0 collective-permute-done.8.refs_5_
  87.5 0.3 collective-permute-start.14
  87.8 0.9 collective-permute-done.9.refs_6_
  88.7 2.0 %collective-permute-start.15 = (bf16[128,512]{1,0:T(8,128)(2,1)S(1)}, bf16[128,512]{1,0:T(8,128)(2,1)S(1)}, u32[]{:S(2)}, u32[]{:S(2)}) collective-permute-start(bf16[128,512]{1,0:T(8,128)(2,1)S(1)} %get-tuple-element.35), channel_id=1, source_target_pairs={{0,4},{1,5},{2,6},{3,7},{4,0},{5,1},{6,2},{7,3},{8,12},{9,13},{10,... | collective-permute-start | bytes 393224 | tf_op jit(solution)/shard_map/ppermute | solution.py:304
  90.8 1.7 %collective-permute-done.10.refs_7_ = bf16[128,512]{1,0:T(8,128)(2,1)S(1)} collective-permute-done((bf16[128,512]{1,0:T(8,128)(2,1)S(1)}, bf16[128,512]{1,0:T(8,128)(2,1)S(1)}, u32[]{:S(2)}, u32[]{:S(2)}) %collective-permute-start.10) | collective-permute-done | bytes 131104 | tf_op jit(solution)/shard_map/ppermute | solution.py:304
  92.5 0.5 collective-permute-start.16
  93.0 0.0 collective-permute-done.12.refs_1_
  93.0 1.2 %collective-permute-start.17 = (bf16[128,512]{1,0:T(8,128)(2,1)S(1)}, bf16[128,512]{1,0:T(8,128)(2,1)S(1)}, u32[]{:S(2)}, u32[]{:S(2)}) collective-permute-start(bf16[128,512]{1,0:T(8,128)(2,1)S(1)} %get-tuple-element.37), channel_id=1, source_target_pairs={{0,6},{1,7},{2,4},{3,5},{4,2},{5,3},{6,0},{7,1},{8,14},{9,15},{10,... | collective-permute-start | bytes 393224 | tf_op jit(solution)/shard_map/ppermute | solution.py:304
  94.2 0.7 collective-permute-done.13.refs_2_
  94.9 1.8 %collective-permute-start.18 = (bf16[128,512]{1,0:T(8,128)(2,1)S(1)}, bf16[128,512]{1,0:T(8,128)(2,1)S(1)}, u32[]{:S(2)}, u32[]{:S(2)}) collective-permute-start(bf16[128,512]{1,0:T(8,128)(2,1)S(1)} %get-tuple-element.38), channel_id=1, source_target_pairs={{0,7},{1,6},{2,5},{3,4},{4,3},{5,2},{6,1},{7,0},{8,15},{9,14},{10,... | collective-permute-start | bytes 393224 | tf_op jit(solution)/shard_map/ppermute | solution.py:304
  96.8 0.7 collect.1.early_ref
  97.5 0.0 collective-permute-done.14.refs_3_
  97.5 0.0 collective-permute-done.15.refs_4_
  97.5 6.0 %collective-permute-done.16.refs_5_ = bf16[128,512]{1,0:T(8,128)(2,1)S(1)} collective-permute-done((bf16[128,512]{1,0:T(8,128)(2,1)S(1)}, bf16[128,512]{1,0:T(8,128)(2,1)S(1)}, u32[]{:S(2)}, u32[]{:S(2)}) %collective-permute-start.16) | collective-permute-done | bytes 131104 | tf_op jit(solution)/shard_map/ppermute | solution.py:304
  103.6 0.0 collective-permute-done.17.refs_6_
  103.6 0.0 collective-permute-done.18.refs_7_
  103.6 3.2 %finish.1 = bf16[512,1024]{1,0:T(8,128)(2,1)} custom-call(s32[512,128]{1,0:T(8,128)S(1)} %copy-done.11, f32[1,1024]{1,0:T(1,128)S(1)} %bitcast.16, bf16[512,512]{1,0:T(8,128)(2,1)S(1)} %collect.1.early_ref, bf16[512,1024]{1,0:T(8,128)(2,1)S(1)} %copy-done.8, bf16[512,1024]{1,0:T(8,128)(2,1)S(1)} %copy-done.6, bf16[1024,1024]{1,0:T(8,128)(2,1)S(1)} %copy-done.13, ...), custom_call_target="tpu_custom_call" | custom-call | flops 2147483648 | bytes 7340032 | tf_op jit(solution)/shard_map/finish/pallas_call | solution.py:289
  (24 shorter events, 0.1 us)
Async XLA Ops:
  0.0 9.0 %copy-start.1 = (bf16[1024,2048]{1,0:T(8,128)(2,1)S(1)}, bf16[1024,2048]{1,0:T(8,128)(2,1)}, u32[]{:S(2)}) copy-start(bf16[1024,2048]{1,0:T(8,128)(2,1)} %w_ref.4) | copy-start | bytes 12582916
  0.0 9.0 %copy-start.12 = (s32[512,1]{0,1:T(1,128)S(1)}, s32[512,1]{0,1:T(1,128)}, u32[]{:S(2)}) copy-start(s32[512,1]{0,1:T(1,128)} %param.10) | copy-start | bytes 6148
  0.0 9.0 %copy-start.15 = (s32[512]{0:T(512)S(1)}, s32[512]{0:T(512)}, u32[]{:S(2)}) copy-start(s32[512]{0:T(512)} %param.11) | copy-start | bytes 6148
  0.0 53.7 %collective-permute-start = (bf16[256,2048]{1,0:T(8,128)(2,1)}, bf16[256,2048]{1,0:T(8,128)(2,1)}, u32[]{:S(2)}, u32[]{:S(2)}) collective-permute-start(bf16[256,2048]{1,0:T(8,128)(2,1)} %bitcast.11), channel_id=1, source_target_pairs={{0,8},{8,0},{16,24},{24,16},{1,9},{9,1},{17,25},{25,17},{2,10},{10... | collective-permute-start | bytes 3145736 | tf_op jit(solution)/shard_map/ppermute | solution.py:304
  5.2 33.0 %collective-permute-start.1 = (bf16[256,1024]{1,0:T(8,128)(2,1)}, bf16[256,1024]{1,0:T(8,128)(2,1)}, u32[]{:S(2)}, u32[]{:S(2)}) collective-permute-start(bf16[256,1024]{1,0:T(8,128)(2,1)} %pad_maximum_fusion), channel_id=1, source_target_pairs={{0,16},{8,24},{16,0},{24,8},{1,17},{9,25},{17,1},{25,9},{2,18},{10... | collective-permute-start | bytes 1572872 | tf_op jit(solution)/shard_map/ppermute | solution.py:304
  8.7 45.0 %collective-permute-start.2 = (bf16[256,1024]{1,0:T(8,128)(2,1)}, bf16[256,1024]{1,0:T(8,128)(2,1)}, u32[]{:S(2)}, u32[]{:S(2)}) collective-permute-start(bf16[256,1024]{1,0:T(8,128)(2,1)} %pad_maximum_fusion.1), channel_id=1, source_target_pairs={{0,16},{8,24},{16,0},{24,8},{1,17},{9,25},{17,1},{25,9},{2,18},{10... | collective-permute-start | bytes 1572872 | tf_op jit(solution)/shard_map/ppermute | solution.py:304
  9.0 1.2 %copy-start.4 = (bf16[512,1024]{1,0:T(8,128)(2,1)S(1)}, bf16[512,1024]{1,0:T(8,128)(2,1)}, u32[]{:S(2)}) copy-start(bf16[512,1024]{1,0:T(8,128)(2,1)} %x_ref.5) | copy-start | bytes 3145732
  13.5 1.4 %copy-start.3 = (bf16[1024,1152]{1,0:T(8,128)(2,1)}, bf16[1024,1152]{1,0:T(8,128)(2,1)S(1)}, u32[]{:S(2)}) copy-start(bf16[1024,1152]{1,0:T(8,128)(2,1)S(1)} %project_queries.1) | copy-start | bytes 7077892
  14.9 4.5 %copy-start.5 = (bf16[512,1024]{1,0:T(8,128)(2,1)S(1)}, bf16[512,1024]{1,0:T(8,128)(2,1)}, u32[]{:S(2)}) copy-start(bf16[512,1024]{1,0:T(8,128)(2,1)} %x_ref.5) | copy-start | bytes 3145732
  14.9 40.8 %all-to-all-start = ((bf16[8,128,1152]{2,1,0:T(8,128)(2,1)}), bf16[8,128,1152]{2,1,0:T(8,128)(2,1)S(1)}, u32[]{:S(2)}, u32[]{:S(2)}) async-start(bf16[8,128,1152]{2,1,0:T(8,128)(2,1)} %bitcast.14), calls=%async_computation | async-start | bytes 4718592 | tf_op jit(solution)/shard_map/all_to_all | solution.py:338
  19.5 2.2 %copy-start.2 = (bf16[1024,2048]{1,0:T(8,128)(2,1)S(1)}, bf16[1024,2048]{1,0:T(8,128)(2,1)}, u32[]{:S(2)}) copy-start(bf16[1024,2048]{1,0:T(8,128)(2,1)} %w_ref.4) | copy-start | bytes 12582916
  23.2 32.5 %copy-start = (bf16[1,256,2048]{2,1,0:T(8,128)(2,1)S(1)}, bf16[1,256,2048]{2,1,0:T(8,128)(2,1)}, u32[]{:S(2)}) copy-start(bf16[1,256,2048]{2,1,0:T(8,128)(2,1)} %param.13) | copy-start | bytes 3145732
  38.3 26.5 %collective-permute-start.3 = (bf16[256,1024]{1,0:T(8,128)(2,1)}, bf16[256,1024]{1,0:T(8,128)(2,1)}, u32[]{:S(2)}, u32[]{:S(2)}) collective-permute-start(bf16[256,1024]{1,0:T(8,128)(2,1)} %collective-permute-done.1.refs_2_.refs_1_), channel_id=1, source_target_pairs={{0,8},{8,0},{16,24},{24,16},{1,9},{9,1},{17,25},{25,17},{2,10},{10... | collective-permute-start | bytes 1572872 | tf_op jit(solution)/shard_map/ppermute | solution.py:304
  54.0 1.0 copy-start.7
  55.0 0.7 copy-start.9
  55.7 1.0 copy-start.10
  64.7 12.4 %collective-permute-start.11 = (bf16[256,1024]{1,0:T(8,128)(2,1)}, bf16[256,1024]{1,0:T(8,128)(2,1)S(1)}, u32[]{:S(2)}, u32[]{:S(2)}) collective-permute-start(bf16[256,1024]{1,0:T(8,128)(2,1)} %collective-permute-done.2.refs_3_.refs_2_), channel_id=1, source_target_pairs={{0,8},{8,0},{16,24},{24,16},{1,9},{9,1},{17,25},{25,17},{2,10},{10... | collective-permute-start | bytes 1572872 | tf_op jit(solution)/shard_map/ppermute | solution.py:304
  69.7 12.3 %collective-permute-start.4 = (bf16[128,512]{1,0:T(8,128)(2,1)S(1)}, bf16[128,512]{1,0:T(8,128)(2,1)S(1)}, u32[]{:S(2)}, u32[]{:S(2)}) collective-permute-start(bf16[128,512]{1,0:T(8,128)(2,1)S(1)} %get-tuple-element.23), channel_id=1, source_target_pairs={{0,1},{1,0},{2,3},{3,2},{4,5},{5,4},{6,7},{7,6},{8,9},{9,8},{10,11... | collective-permute-start | bytes 393224 | tf_op jit(solution)/shard_map/ppermute | solution.py:304
  69.8 14.8 %collective-permute-start.5 = (bf16[128,512]{1,0:T(8,128)(2,1)S(1)}, bf16[128,512]{1,0:T(8,128)(2,1)S(1)}, u32[]{:S(2)}, u32[]{:S(2)}) collective-permute-start(bf16[128,512]{1,0:T(8,128)(2,1)S(1)} %get-tuple-element.24), channel_id=1, source_target_pairs={{0,2},{1,3},{2,0},{3,1},{4,6},{5,7},{6,4},{7,5},{8,10},{9,11},{10,... | collective-permute-start | bytes 393224 | tf_op jit(solution)/shard_map/ppermute | solution.py:304
  71.3 14.6 %collective-permute-start.6 = (bf16[128,512]{1,0:T(8,128)(2,1)S(1)}, bf16[128,512]{1,0:T(8,128)(2,1)S(1)}, u32[]{:S(2)}, u32[]{:S(2)}) collective-permute-start(bf16[128,512]{1,0:T(8,128)(2,1)S(1)} %get-tuple-element.25), channel_id=1, source_target_pairs={{0,3},{1,2},{2,1},{3,0},{4,7},{5,6},{6,5},{7,4},{8,11},{9,10},{10,... | collective-permute-start | bytes 393224 | tf_op jit(solution)/shard_map/ppermute | solution.py:304
  71.6 14.3 %collective-permute-start.7 = (bf16[128,512]{1,0:T(8,128)(2,1)S(1)}, bf16[128,512]{1,0:T(8,128)(2,1)S(1)}, u32[]{:S(2)}, u32[]{:S(2)}) collective-permute-start(bf16[128,512]{1,0:T(8,128)(2,1)S(1)} %get-tuple-element.26), channel_id=1, source_target_pairs={{0,4},{1,5},{2,6},{3,7},{4,0},{5,1},{6,2},{7,3},{8,12},{9,13},{10,... | collective-permute-start | bytes 393224 | tf_op jit(solution)/shard_map/ppermute | solution.py:304
  77.1 10.4 %collective-permute-start.8 = (bf16[128,512]{1,0:T(8,128)(2,1)S(1)}, bf16[128,512]{1,0:T(8,128)(2,1)S(1)}, u32[]{:S(2)}, u32[]{:S(2)}) collective-permute-start(bf16[128,512]{1,0:T(8,128)(2,1)S(1)} %get-tuple-element.27), channel_id=1, source_target_pairs={{0,5},{1,4},{2,7},{3,6},{4,1},{5,0},{6,3},{7,2},{8,13},{9,12},{10,... | collective-permute-start | bytes 393224 | tf_op jit(solution)/shard_map/ppermute | solution.py:304
  77.2 19.6 %copy-start.11 = (s32[512,128]{1,0:T(8,128)S(1)}, s32[512,128]{1,0:T(8,128)}, u32[]{:S(2)}) copy-start(s32[512,128]{1,0:T(8,128)} %copy-done.9) | copy-start | bytes 786436
  77.2 26.4 %copy-start.6 = (bf16[512,1024]{1,0:T(8,128)(2,1)S(1)}, bf16[512,1024]{1,0:T(8,128)(2,1)}, u32[]{:S(2)}) copy-start(bf16[512,1024]{1,0:T(8,128)(2,1)} %x_ref.5) | copy-start | bytes 3145732
  77.2 26.4 %copy-start.8 = (bf16[512,1024]{1,0:T(8,128)(2,1)S(1)}, bf16[512,1024]{1,0:T(8,128)(2,1)}, u32[]{:S(2)}) copy-start(bf16[512,1024]{1,0:T(8,128)(2,1)} %copy-done.7) | copy-start | bytes 3145732
  77.2 26.4 %copy-start.13 = (bf16[1024,1024]{1,0:T(8,128)(2,1)S(1)}, bf16[1024,1024]{1,0:T(8,128)(2,1)}, u32[]{:S(2)}) copy-start(bf16[1024,1024]{1,0:T(8,128)(2,1)} %w_ref.5) | copy-start | bytes 6291460
  77.2 26.4 %copy-start.14 = (f32[1024]{0:T(1024)S(1)}, f32[1024]{0:T(1024)}, u32[]{:S(2)}) copy-start(f32[1024]{0:T(1024)} %param.16) | copy-start | bytes 12292
  82.0 6.7 %collective-permute-start.9 = (bf16[128,512]{1,0:T(8,128)(2,1)S(1)}, bf16[128,512]{1,0:T(8,128)(2,1)S(1)}, u32[]{:S(2)}, u32[]{:S(2)}) collective-permute-start(bf16[128,512]{1,0:T(8,128)(2,1)S(1)} %get-tuple-element.28), channel_id=1, source_target_pairs={{0,6},{1,7},{2,4},{3,5},{4,2},{5,3},{6,0},{7,1},{8,14},{9,15},{10,... | collective-permute-start | bytes 393224 | tf_op jit(solution)/shard_map/ppermute | solution.py:304
  84.5 8.0 %collective-permute-start.10 = (bf16[128,512]{1,0:T(8,128)(2,1)S(1)}, bf16[128,512]{1,0:T(8,128)(2,1)S(1)}, u32[]{:S(2)}, u32[]{:S(2)}) collective-permute-start(bf16[128,512]{1,0:T(8,128)(2,1)S(1)} %get-tuple-element.29), channel_id=1, source_target_pairs={{0,7},{1,6},{2,5},{3,4},{4,3},{5,2},{6,1},{7,0},{8,15},{9,14},{10,... | collective-permute-start | bytes 393224 | tf_op jit(solution)/shard_map/ppermute | solution.py:304
  86.0 7.1 %collective-permute-start.12 = (bf16[128,512]{1,0:T(8,128)(2,1)S(1)}, bf16[128,512]{1,0:T(8,128)(2,1)S(1)}, u32[]{:S(2)}, u32[]{:S(2)}) collective-permute-start(bf16[128,512]{1,0:T(8,128)(2,1)S(1)} %get-tuple-element.32), channel_id=1, source_target_pairs={{0,1},{1,0},{2,3},{3,2},{4,5},{5,4},{6,7},{7,6},{8,9},{9,8},{10,11... | collective-permute-start | bytes 393224 | tf_op jit(solution)/shard_map/ppermute | solution.py:304
  86.0 9.0 %collective-permute-start.13 = (bf16[128,512]{1,0:T(8,128)(2,1)S(1)}, bf16[128,512]{1,0:T(8,128)(2,1)S(1)}, u32[]{:S(2)}, u32[]{:S(2)}) collective-permute-start(bf16[128,512]{1,0:T(8,128)(2,1)S(1)} %get-tuple-element.33), channel_id=1, source_target_pairs={{0,2},{1,3},{2,0},{3,1},{4,6},{5,7},{6,4},{7,5},{8,10},{9,11},{10,... | collective-permute-start | bytes 393224 | tf_op jit(solution)/shard_map/ppermute | solution.py:304
  87.5 10.0 %collective-permute-start.14 = (bf16[128,512]{1,0:T(8,128)(2,1)S(1)}, bf16[128,512]{1,0:T(8,128)(2,1)S(1)}, u32[]{:S(2)}, u32[]{:S(2)}) collective-permute-start(bf16[128,512]{1,0:T(8,128)(2,1)S(1)} %get-tuple-element.34), channel_id=1, source_target_pairs={{0,3},{1,2},{2,1},{3,0},{4,7},{5,6},{6,5},{7,4},{8,11},{9,10},{10,... | collective-permute-start | bytes 393224 | tf_op jit(solution)/shard_map/ppermute | solution.py:304
  88.7 8.8 %collective-permute-start.15 = (bf16[128,512]{1,0:T(8,128)(2,1)S(1)}, bf16[128,512]{1,0:T(8,128)(2,1)S(1)}, u32[]{:S(2)}, u32[]{:S(2)}) collective-permute-start(bf16[128,512]{1,0:T(8,128)(2,1)S(1)} %get-tuple-element.35), channel_id=1, source_target_pairs={{0,4},{1,5},{2,6},{3,7},{4,0},{5,1},{6,2},{7,3},{8,12},{9,13},{10,... | collective-permute-start | bytes 393224 | tf_op jit(solution)/shard_map/ppermute | solution.py:304
  92.5 11.0 %collective-permute-start.16 = (bf16[128,512]{1,0:T(8,128)(2,1)S(1)}, bf16[128,512]{1,0:T(8,128)(2,1)S(1)}, u32[]{:S(2)}, u32[]{:S(2)}) collective-permute-start(bf16[128,512]{1,0:T(8,128)(2,1)S(1)} %get-tuple-element.36), channel_id=1, source_target_pairs={{0,5},{1,4},{2,7},{3,6},{4,1},{5,0},{6,3},{7,2},{8,13},{9,12},{10,... | collective-permute-start | bytes 393224 | tf_op jit(solution)/shard_map/ppermute | solution.py:304
  93.0 10.5 %collective-permute-start.17 = (bf16[128,512]{1,0:T(8,128)(2,1)S(1)}, bf16[128,512]{1,0:T(8,128)(2,1)S(1)}, u32[]{:S(2)}, u32[]{:S(2)}) collective-permute-start(bf16[128,512]{1,0:T(8,128)(2,1)S(1)} %get-tuple-element.37), channel_id=1, source_target_pairs={{0,6},{1,7},{2,4},{3,5},{4,2},{5,3},{6,0},{7,1},{8,14},{9,15},{10,... | collective-permute-start | bytes 393224 | tf_op jit(solution)/shard_map/ppermute | solution.py:304
  94.9 8.6 %collective-permute-start.18 = (bf16[128,512]{1,0:T(8,128)(2,1)S(1)}, bf16[128,512]{1,0:T(8,128)(2,1)S(1)}, u32[]{:S(2)}, u32[]{:S(2)}) collective-permute-start(bf16[128,512]{1,0:T(8,128)(2,1)S(1)} %get-tuple-element.38), channel_id=1, source_target_pairs={{0,7},{1,6},{2,5},{3,4},{4,3},{5,2},{6,1},{7,0},{8,15},{9,14},{10,... | collective-permute-start | bytes 393224 | tf_op jit(solution)/shard_map/ppermute | solution.py:304

commit v6 on v5

--- a/solution.py
+++ b/solution.py
@@ -17,6 +17,7 @@
 MIB = 1024 * 1024
 WAIT_COST = 20.0
 KERNEL_MIB = 24
+QUERY_MIB = 60
 
 
 def params(mib):
@@ -57,31 +58,85 @@
     return [pl.BlockSpec(memory_space=pl.ANY)] * len(arrays)
 
 
-def query_kernel(columns, capacity, owner_ref, visible_ref, x_ref, w_ref, send_ref):
+def split_kernel(spans, size, kv_ref, *out_refs):
+    width = kv_ref.shape[1] // 2
+    for (first, heads), ref in zip(spans, out_refs):
+        lo, hi = first * size, (first + heads) * size
+        ref[:, : hi - lo] = kv_ref[:, lo:hi]
+        ref[:, hi - lo :] = kv_ref[:, width + lo : width + hi]
+
+
+def split(kv, spans, size):
+    rows = kv.shape[0]
+    return pl.pallas_call(
+        functools.partial(split_kernel, spans, size),
+        in_specs=whole(),
+        out_specs=whole(len(spans)),
+        out_shape=[jax.ShapeDtypeStruct((rows, 2 * heads * size), BF16) for _, heads in spans],
+        compiler_params=params(KERNEL_MIB),
+        cost_estimate=cost(0, 4 * kv.size),
+        name="split",
+    )(kv)
+
+
+def query_kernel(columns, capacity, owner_ref, visible_ref, x_hbm, w_hbm, send_hbm, *scratch):
+    x_ref, w_ref, send_ref, x_sem, w_sems, out_sems = scratch
     rows, width = x_ref.shape
     slots = columns * capacity
+    tile = min(256, width)
+    spans = [slice(start, start + tile) for start in range(0, width, tile)]
+    x_load = pltpu.make_async_copy(x_hbm, x_ref, x_sem)
+    x_load.start()
+    w_loads = []
+    for number, span in enumerate(spans):
+        load = pltpu.make_async_copy(w_hbm.at[:, span], w_ref.at[:, span], w_sems.at[number])
+        load.start()
+        w_loads.append(load)
     slot = slot_row(owner_ref[...], columns, capacity).astype(jnp.int32)
     index = lax.broadcasted_iota(jnp.int32, (slots, rows), 0)
     place = (index == slot).astype(BF16)
-    tile = min(256, width)
-    for start in range(0, width, tile):
-        span = slice(start, start + tile)
+    seen = jnp.broadcast_to(visible_ref[...].astype(F32), (BLK, rows)).T.astype(BF16)
+    send_ref[:, width:] = jnp.dot(place, seen, preferred_element_type=F32).astype(BF16)
+    stores = []
+
+    def store(span):
+        copy = pltpu.make_async_copy(
+            send_ref.at[:, span], send_hbm.at[:, span], out_sems.at[len(stores)]
+        )
+        copy.start()
+        stores.append(copy)
+
+    store(slice(width, width + BLK))
+    x_load.wait()
+    for number, span in enumerate(spans):
+        w_loads[number].wait()
         hidden = jnp.dot(x_ref[...], w_ref[:, span], preferred_element_type=F32)
         moved = jnp.dot(place, silu(hidden).astype(BF16), preferred_element_type=F32)
         send_ref[:, span] = moved.astype(BF16)
-    seen = jnp.broadcast_to(visible_ref[...].astype(F32), (BLK, rows)).T.astype(BF16)
-    send_ref[:, width:] = jnp.dot(place, seen, preferred_element_type=F32).astype(BF16)
+        store(span)
+    for copy in stores:
+        copy.wait()
 
 
 def project_queries(owner_row, visible_row, cand_x, w_in, columns, capacity):
     rows, width = cand_x.shape
     slots = columns * capacity
+    count = width // min(256, width)
+    anywhere = pl.BlockSpec(memory_space=pl.ANY)
     return pl.pallas_call(
         functools.partial(query_kernel, columns, capacity),
-        in_specs=whole(4),
-        out_specs=whole()[0],
+        in_specs=whole(2) + [anywhere, anywhere],
+        out_specs=anywhere,
         out_shape=jax.ShapeDtypeStruct((slots, width + BLK), BF16),
-        compiler_params=params(KERNEL_MIB),
+        scratch_shapes=[
+            pltpu.VMEM((rows, width), BF16),
+            pltpu.VMEM((width, width), BF16),
+            pltpu.VMEM((slots, width + BLK), BF16),
+            pltpu.SemaphoreType.DMA,
+            pltpu.SemaphoreType.DMA((count,)),
+            pltpu.SemaphoreType.DMA((count + 1,)),
+        ],
+        compiler_params=params(QUERY_MIB),
         cost_estimate=cost(
             2 * rows * width * width + 2 * slots * rows * width,
             2 * (rows * width + width * width + slots * width),
@@ -136,7 +191,8 @@
 def attend_kernel(size, heads, first, starts, behind, has_base, outs, place_ref, *refs):
     refs = refs[behind:]
     rows_ref, refs = refs[0], refs[1:]
-    parts, refs = refs[: len(starts)], refs[len(starts) :]
+    count = len(starts)
+    parts, refs = refs[:count], refs[count:]
     base_ref = refs[0] if has_base else None
     out_refs, shown = refs[int(has_base) : int(has_base) + outs], refs[int(has_base) + outs]
     result = out_refs[0] if outs == 1 else refs[-1]
@@ -144,44 +200,44 @@
     keys = parts[0].shape[0]
     blocks = keys // BLK
     seen = rows_ref[:, HEADS * size :].astype(F32)
-    for number in range(len(parts)):
+    for number in range(count):
         for block in range(blocks):
             start = (place_ref[2 + number] * blocks + block).astype(F32)
-            shown[number * blocks + block] = jnp.where(start < seen, 0.5 / math.sqrt(size), 0.0)
+            shown[number * blocks + block] = (start < seen).astype(F32).astype(BF16)
     row = lax.broadcasted_iota(jnp.int32, (keys, size), 0)
     tile = min(512, slots)
 
-    def columns(head):
-        return pl.ds(pl.multiple_of(head * size, size), size)
+    def columns(start):
+        return pl.ds(pl.multiple_of(start, size), size)
 
     def one_head(head, carry):
         values = []
         for number, part in enumerate(parts):
             inside = row + place_ref[2 + number] * keys < place_ref[0]
-            value = part[:, columns(starts[number][1] + head)].astype(F32)
+            value = part[:, columns((starts[number][1] + head) * size)].astype(F32)
             values.append(jnp.where(inside, value, 0.0).astype(BF16))
         values = jnp.concatenate(values, axis=0)
         for start in range(0, slots, tile):
             span = slice(start, start + tile)
-            queries = rows_ref[span, columns(first + head)]
+            queries = rows_ref[span, columns((first + head) * size)]
             weights = []
             for number, part in enumerate(parts):
                 scores = lax.dot_general(
                     queries,
-                    part[:, columns(starts[number][0] + head)],
+                    part[:, columns((starts[number][0] + head) * size)],
                     (((1,), (1,)), ((), ())),
                     preferred_element_type=F32,
                 )
                 for block in range(blocks):
-                    half = scores[:, block * BLK : (block + 1) * BLK]
-                    half = half * shown[number * blocks + block, span, :]
-                    weights.append((half * jnp.tanh(half) + half).astype(BF16))
+                    half = scores[:, block * BLK : (block + 1) * BLK] * (0.5 / math.sqrt(size))
+                    half = half.astype(BF16) * shown[number * blocks + block, span, :]
+                    weights.append(half * jnp.tanh(half) + half)
             total = jnp.dot(
                 jnp.concatenate(weights, axis=1), values, preferred_element_type=F32
             )
             if has_base:
-                total = total + base_ref[span, columns(first + head)]
-            result[span, columns(head)] = total.astype(result.dtype)
+                total = total + base_ref[span, columns((first + head) * size)]
+            result[span, columns(head * size)] = total.astype(result.dtype)
         return carry
 
     lax.fori_loop(0, heads, one_head, 0)
@@ -198,7 +254,7 @@
     count = len(segments)
     starts = [(key, value) for _, key, value in segments]
     extra = [] if base is None else [base]
-    scratch = [pltpu.VMEM((count * (keys // BLK), slots, BLK), F32)]
+    scratch = [pltpu.VMEM((count * (keys // BLK), slots, BLK), BF16)]
     if outs > 1:
         scratch.append(pltpu.VMEM((slots, heads * size), BF16))
     return pl.pallas_call(
@@ -306,7 +362,11 @@
 
 def exchange(blocks):
     count = len(blocks)
-    return [block if d == 0 else swap(block, "cand", d, count) for d, block in enumerate(blocks)]
+    order = sorted(range(1, count), key=lambda d: (d & 1, d >> 1 == (count >> 1) - 1, d))
+    back = {0: blocks[0]}
+    for d in order:
+        back[d] = swap(blocks[d], "cand", d, count)
+    return [back[d] for d in range(count)]
 
 
 def per_device(cand_x, cand_user, visible, hist_len, kv_cache, w_in, w_out, ln_gain):
@@ -315,69 +375,51 @@
     count = lax.axis_size("user")
     size = width // HEADS
     capacity = 2 * rows // columns
-    own = kv_cache[0]
+    slots = columns * capacity
     me = lax.axis_index("cand").astype(jnp.int32)
     owner_row = cand_user.reshape(1, rows)
     visible_row = visible.reshape(1, rows)
-
     spans = [(sum(GROUPS[:number]), heads) for number, heads in enumerate(GROUPS)]
-    far = []
-    for first, heads in spans:
-        lo, hi = first * size, (first + heads) * size
-        held = {0: jnp.concatenate([own[:, lo:hi], own[:, width + lo : width + hi]], axis=1)}
-        bit = count // 2
-        while bit > 1:
-            for key in sorted(held):
-                held[key | bit] = swap(held[key], "user", bit, count)
-            bit //= 2
-        far.append(held)
-    evens = sorted(far[0])
-    near = swap(own, "user", 1, count)
+
+    held = {0: kv_cache[0], 1: swap(kv_cache[0], "user", 1, count)}
+    bit = count // 2
+    while bit > 1:
+        for key in sorted(key for key in held if key != 1):
+            held[key | bit] = swap(held[key], "user", bit, count)
+        bit //= 2
+    ready = sorted(held)
+    late = [key | 1 for key in ready if key > 1]
 
     send = project_queries(owner_row, visible_row, cand_x, w_in, columns, capacity)
     got = lax.all_to_all(
         send.reshape(columns, capacity, -1), "cand", split_axis=0, concat_axis=0, tiled=True
-    ).reshape(columns * capacity, -1)
+    ).reshape(slots, -1)
     gate = project_gate(cand_x, w_in)
-    arrived = [near] + [held[evens[-1]] for held in far]
+    arrived = [held[key] for key in ready if key]
     slot = slot_column(owner_row ^ me, columns, capacity, [gate] + arrived)
     position = lax.axis_index("user").astype(jnp.int32)
-    order = [0, 1] + evens[1:] + [key | 1 for key in evens[1:]]
-    shards = position ^ jnp.array(order, jnp.int32)
+    shards = position ^ jnp.array(ready + late, jnp.int32)
     head = jnp.concatenate([hist_len, me[None]])
-    place_first = jnp.concatenate([head, shards[:2]])
-    place = jnp.concatenate([head, shards[2:]])
-    base = attend(
-        place_first,
-        [slot],
-        got,
-        [(own, 0, HEADS), (near, 0, HEADS)],
-        None,
-        0,
-        HEADS,
-        size,
-        1,
-        F32,
-    )[0]
-
-    def forward(number, behind):
-        parts = [far[number][key] for key in evens[1:]]
-        if behind is not None:
-            parts, _ = lax.optimization_barrier((parts, behind))
-        return [swap(part, "user", 1, count) for part in parts]
-
-    cuts = [forward(0, None)]
+    place_ready = jnp.concatenate([head, shards[: len(ready)]])
+    place_late = jnp.concatenate([head, shards[len(ready) :]])
+
+    segments = [(held[key], 0, HEADS) for key in ready]
+    base = attend(place_ready, [slot], got, segments, None, 0, HEADS, size, 1, F32)[0]
+    passed = [split(held[key ^ 1], spans, size) for key in late]
+    cuts = []
+    for number in range(len(spans)):
+        parts = [pieces[number] for pieces in passed]
+        if number:
+            parts, _ = lax.optimization_barrier((parts, (cuts[-1], base)))
+        cuts.append([swap(part, "user", 1, count) for part in parts])
     returned = []
     after = []
-    done = base
     for number, (first, heads) in enumerate(spans):
-        if number + 1 < len(spans):
-            cuts.append(forward(number + 1, (cuts[number], done)))
-        segments = [(far[number][key], 0, heads) for key in evens[1:]]
-        segments += [(cut, 0, heads) for cut in cuts[number]]
-        attn = attend(place, after, got, segments, base, first, heads, size, columns, BF16)
-        done = attn[0]
-        after = [done] + [group[-1] for group in returned[-1:]]
+        segments = [(cut, 0, heads) for cut in cuts[number]]
+        attn = attend(
+            place_late, after, got, segments, base, first, heads, size, columns, BF16
+        )
+        after = [attn[0]]
         returned.append(exchange(attn))
     early = collect(slot, returned[:-1])
     return finish(slot, early, gate, cand_x, ln_gain, w_out, returned[-1])

time: 107 us -> 108 us (level)
  Pallas kernels: 26.5 us -> 31.5 us
  starting transfers between devices: 28.3 us -> 26.3 us
  other arithmetic: 1.9 us -> 0.79 us
    pallas_call x1, Pallas kernels: 3.25 us -> 8.28 us  [project_queries(): pl.pallas_call(functools.partial(query_kernel, columns, capacity), in_spe...]
    ppermute x19 -> x18, starting transfers between devices: 24.5 us -> 22.6 us  [swap(): return lax.ppermute(array, axis, [(i, i ^ bits) for i in range(count)])]
    concatenate x4 -> x2, other arithmetic: 1.89 us -> 0.78 us  [the longest x1 0.71 us: per_device(): place_late = jnp.concatenate([head, shards[len(ready):]])]
    unnamed x32 -> x28, local copies, waits for them, and re-layouts: 7.49 us -> 7.12 us
    ppermute x19 -> x18, waiting for transfers between devices: 40.3 us -> 40.1 us  [swap(): return lax.ppermute(array, axis, [(i, i ^ bits) for i in range(count)])]
  transfers between devices with their start and end apart: 20 -> 19, of which waited for: 7 -> 6; matrix products, arithmetic and copies ran while one was open for 3% -> 1% of each run, Pallas kernels for 22% -> 26%
where the time goes in v6:
time: 108 us; the launch traced here: 107 us
  waiting for transfers between devices  40.1 us (37%)
  Pallas kernels  31.5 us (29%)
  starting transfers between devices  26.3 us (24%)
  local copies, waits for them, and re-layouts  7.76 us (7%)
    ppermute x18, waiting for transfers between devices, swap(): return lax.ppermute(array, axis, [(i, i ^ bits) for i in range(count)])  40.1 us
    ppermute x18, starting transfers between devices, swap(): return lax.ppermute(array, axis, [(i, i ^ bits) for i in range(count)])  22.6 us
    pallas_call x3, Pallas kernels, attend(): pl.pallas_call(functools.partial(attend_kernel, size, heads, first, start...  16.8 us
    pallas_call x1, Pallas kernels, project_queries(): pl.pallas_call(functools.partial(query_kernel, columns, capacity), in_spe...  8.28 us
    unnamed x28, local copies, waits for them, and re-layouts  7.12 us
    all_to_all x1, starting transfers between devices, per_device(): lax.all_to_all(send.reshape(columns, capacity, -1), 'cand', split_axis=0,...  3.74 us
    pallas_call x1, Pallas kernels, finish(): pl.pallas_call(finish_kernel, in_specs=whole(6 + len(parts)), out_specs=p...  3.1 us
  transfers between devices with their start and end apart: 19, of which 6 were waited for; matrix products, arithmetic and copies ran while one was open for 1% of the time, Pallas kernels for 26%

profile of v6, /device:TPU:0, one launch (start us, length us, event | category | flops | bytes accessed | tf_op | source)
XLA Modules:
  0.0 107.4 jit_solution(3014874485548687577)
XLA Ops:
  0.0 4.0 %collective-permute-start.1 = (bf16[256,2048]{1,0:T(8,128)(2,1)}, bf16[256,2048]{1,0:T(8,128)(2,1)S(1)}, u32[]{:S(2)}, u32[]{:S(2)}) collective-permute-start(bf16[256,2048]{1,0:T(8,128)(2,1)} %bitcast.12), channel_id=1, source_target_pairs={{0,16},{8,24},{16,0},{24,8},{1,17},{9,25},{17,1},{25,9},{2,18},{10... | collective-permute-start | bytes 3145736 | tf_op jit(solution)/shard_map/ppermute | solution.py:360
  4.0 1.6 %collective-permute-start = (bf16[256,2048]{1,0:T(8,128)(2,1)}, bf16[256,2048]{1,0:T(8,128)(2,1)}, u32[]{:S(2)}, u32[]{:S(2)}) collective-permute-start(bf16[256,2048]{1,0:T(8,128)(2,1)} %bitcast.13), channel_id=1, source_target_pairs={{0,8},{8,0},{16,24},{24,16},{1,9},{9,1},{17,25},{25,17},{2,10},{10... | collective-permute-start | bytes 3145736 | tf_op jit(solution)/shard_map/ppermute | solution.py:360
  5.6 8.3 %project_queries.1 = bf16[1024,1152]{1,0:T(8,128)(2,1)} custom-call(s32[1,512]{1,0:T(1,128)} %bitcast.17, s32[1,512]{1,0:T(1,128)} %bitcast.19, bf16[512,1024]{1,0:T(8,128)(2,1)} %x_ref.3, bf16[1024,2048]{1,0:T(8,128)(2,1)} %w_hbm.1), custom_call_target="tpu_custom_call" | custom-call | flops 2147483648 | bytes 5242880 | tf_op jit(solution)/shard_map/project_queries/pallas_call | solution.py:126
  13.9 3.7 %all-to-all-start = ((bf16[8,128,1152]{2,1,0:T(8,128)(2,1)}), bf16[8,128,1152]{2,1,0:T(8,128)(2,1)S(1)}, u32[]{:S(2)}, u32[]{:S(2)}) async-start(bf16[8,128,1152]{2,1,0:T(8,128)(2,1)} %bitcast.16), calls=%async_computation | async-start | bytes 4718592 | tf_op jit(solution)/shard_map/all_to_all | solution.py:394
  18.3 0.0 copy-start
  18.3 2.2 %copy-done = bf16[1024,2048]{1,0:T(8,128)(2,1)S(1)} copy-done((bf16[1024,2048]{1,0:T(8,128)(2,1)S(1)}, bf16[1024,2048]{1,0:T(8,128)(2,1)}, u32[]{:S(2)}) %copy-start) | copy-done | bytes 4194328
  20.5 1.2 %copy-done.1 = bf16[512,1024]{1,0:T(8,128)(2,1)S(1)} copy-done((bf16[512,1024]{1,0:T(8,128)(2,1)S(1)}, bf16[512,1024]{1,0:T(8,128)(2,1)}, u32[]{:S(2)}) %copy-start.1) | copy-done | bytes 1048600
  21.7 1.4 %project_gate.1.refs_0_.gate_ref = bf16[512,1024]{1,0:T(8,128)(2,1)S(1)} custom-call(bf16[512,1024]{1,0:T(8,128)(2,1)S(1)} %copy-done.1, bf16[1024,2048]{1,0:T(8,128)(2,1)S(1)} %copy-done), custom_call_target="tpu_custom_call" | custom-call | flops 1073741824 | bytes 4194304 | tf_op jit(solution)/shard_map/project_gate/pallas_call | solution.py:160
  23.1 0.0 copy-start.3
  23.1 0.1 pad_add_fusion.1.place_ref
  23.2 0.0 copy-done.13
  23.2 26.8 %collective-permute-done.1.refs_2_.kv_ref.refs_4_ = bf16[256,2048]{1,0:T(8,128)(2,1)S(1)} collective-permute-done((bf16[256,2048]{1,0:T(8,128)(2,1)}, bf16[256,2048]{1,0:T(8,128)(2,1)S(1)}, u32[]{:S(2)}, u32[]{:S(2)}) %collective-permute-start.1) | collective-permute-done | bytes 1048608 | tf_op jit(solution)/shard_map/ppermute | solution.py:360
  50.0 0.9 split.1
  50.9 0.8 copy-done.7
  51.7 0.7 collective-permute-start.2
  52.4 0.0 collective-permute-done.refs_1_.refs_3_
  52.4 0.0 copy-done.3
  52.4 0.3 slot_column.1.refs_0_.slot_ref
  52.7 0.0 copy-start.10
  52.7 0.7 copy-done.10
  53.4 0.0 all-to-all-done
  53.4 1.2 %copy-done.6 = bf16[1,256,2048]{2,1,0:T(8,128)(2,1)S(1)} copy-done((bf16[1,256,2048]{2,1,0:T(8,128)(2,1)S(1)}, bf16[1,256,2048]{2,1,0:T(8,128)(2,1)}, u32[]{:S(2)}) %copy-start.6) | copy-done | bytes 1048600
  54.7 0.9 copy-done.11
  55.6 10.4 %attend.3.refs_2_.refs_3_ = f32[1024,1024]{1,0:T(8,128)S(1)} custom-call(s32[5]{0:T(128)S(1)} %pad_add_fusion.1.place_ref, s32[512,128]{1,0:T(8,128)S(1)} %copy-done.11, bf16[1024,1152]{1,0:T(8,128)(2,1)S(1)} %bitcast.9, bf16[256,2048]{1,0:T(8,128)(2,1)S(1)} %bitcast.14, bf16[256,2048]{1,0:T(8,128)(2,1)} %collective-permute-done.refs_1_.refs_3_, ...), custom_call_target="tpu_custom_call" | custom-call | flops 3221225472 | bytes 7340032 | tf_op jit(solution)/shard_map/attend/pallas_call | solution.py:260
  66.0 0.0 collective-permute-done.2.refs_1_
  66.0 0.0 copy-done.8
  66.0 1.4 %collective-permute-start.10 = (bf16[256,1024]{1,0:T(8,128)(2,1)S(1)}, bf16[256,1024]{1,0:T(8,128)(2,1)S(1)}, u32[]{:S(2)}, u32[]{:S(2)}) collective-permute-start(bf16[256,1024]{1,0:T(8,128)(2,1)S(1)} %copy-done.8), channel_id=1, source_target_pairs={{0,8},{8,0},{16,24},{24,16},{1,9},{9,1},{17,25},{25,17},{2,10},{10... | collective-permute-start | bytes 1572872 | tf_op jit(solution)/shard_map/ppermute | solution.py:360
  67.4 0.6 slice.6
  68.1 0.7 pad_add_fusion.place_ref
  68.8 3.5 %attend.4 = (bf16[128,512]{1,0:T(8,128)(2,1)S(1)}, bf16[128,512]{1,0:T(8,128)(2,1)S(1)}, bf16[128,512]{1,0:T(8,128)(2,1)S(1)}, bf16[128,512]{1,0:T(8,128)(2,1)S(...) custom-call(s32[3]{0:T(128)S(1)} %pad_add_fusion.place_ref, ...), custom_call_target="tpu_custom_call" | custom-call | flops 536870912 | bytes 2621440 | tf_op jit(solution)/shard_map/attend/pallas_call | solution.py:260
  72.2 0.1 collective-permute-start.3
  72.3 1.6 %collective-permute-start.4 = (bf16[128,512]{1,0:T(8,128)(2,1)S(1)}, bf16[128,512]{1,0:T(8,128)(2,1)S(1)}, u32[]{:S(2)}, u32[]{:S(2)}) collective-permute-start(bf16[128,512]{1,0:T(8,128)(2,1)S(1)} %get-tuple-element.27), channel_id=1, source_target_pairs={{0,2},{1,3},{2,0},{3,1},{4,6},{5,7},{6,4},{7,5},{8,10},{9,11},{10,... | collective-permute-start | bytes 393224 | tf_op jit(solution)/shard_map/ppermute | solution.py:360
  73.9 0.3 collective-permute-start.5
  74.2 1.6 %collective-permute-start.6 = (bf16[128,512]{1,0:T(8,128)(2,1)S(1)}, bf16[128,512]{1,0:T(8,128)(2,1)S(1)}, u32[]{:S(2)}, u32[]{:S(2)}) collective-permute-start(bf16[128,512]{1,0:T(8,128)(2,1)S(1)} %get-tuple-element.29), channel_id=1, source_target_pairs={{0,4},{1,5},{2,6},{3,7},{4,0},{5,1},{6,2},{7,3},{8,12},{9,13},{10,... | collective-permute-start | bytes 393224 | tf_op jit(solution)/shard_map/ppermute | solution.py:360
  75.8 3.9 %collective-permute-done.10.refs_2_ = bf16[256,1024]{1,0:T(8,128)(2,1)S(1)} collective-permute-done((bf16[256,1024]{1,0:T(8,128)(2,1)S(1)}, bf16[256,1024]{1,0:T(8,128)(2,1)S(1)}, u32[]{:S(2)}, u32[]{:S(2)}) %collective-permute-start.10) | collective-permute-done | bytes 524320 | tf_op jit(solution)/shard_map/ppermute | solution.py:360
  79.7 0.0 collective-permute-start.7
  79.7 0.0 copy-start.5
  79.7 0.0 copy-start.9
  79.7 3.0 %attend.5 = (bf16[128,512]{1,0:T(8,128)(2,1)S(1)}, bf16[128,512]{1,0:T(8,128)(2,1)S(1)}, bf16[128,512]{1,0:T(8,128)(2,1)S(1)}, bf16[128,512]{1,0:T(8,128)(2,1)S(...) custom-call(s32[3]{0:T(128)S(1)} %pad_add_fusion.place_ref, ...), custom_call_target="tpu_custom_call" | custom-call | flops 536870912 | bytes 2621440 | tf_op jit(solution)/shard_map/attend/pallas_call | solution.py:260
  82.7 0.0 collective-permute-done.3.refs_1_
  82.7 2.5 %collective-permute-start.8 = (bf16[128,512]{1,0:T(8,128)(2,1)S(1)}, bf16[128,512]{1,0:T(8,128)(2,1)S(1)}, u32[]{:S(2)}, u32[]{:S(2)}) collective-permute-start(bf16[128,512]{1,0:T(8,128)(2,1)S(1)} %get-tuple-element.31), channel_id=1, source_target_pairs={{0,6},{1,7},{2,4},{3,5},{4,2},{5,3},{6,0},{7,1},{8,14},{9,15},{10,... | collective-permute-start | bytes 393224 | tf_op jit(solution)/shard_map/ppermute | solution.py:360
  85.2 0.0 collective-permute-done.4.refs_2_
  85.2 1.4 %collective-permute-start.9 = (bf16[128,512]{1,0:T(8,128)(2,1)S(1)}, bf16[128,512]{1,0:T(8,128)(2,1)S(1)}, u32[]{:S(2)}, u32[]{:S(2)}) collective-permute-start(bf16[128,512]{1,0:T(8,128)(2,1)S(1)} %get-tuple-element.32), channel_id=1, source_target_pairs={{0,7},{1,6},{2,5},{3,4},{4,3},{5,2},{6,1},{7,0},{8,15},{9,14},{10,... | collective-permute-start | bytes 393224 | tf_op jit(solution)/shard_map/ppermute | solution.py:360
  86.6 0.0 collective-permute-done.5.refs_3_
  86.6 0.0 collective-permute-start.11
  86.6 0.0 collective-permute-done.6.refs_4_
  86.7 1.6 %collective-permute-start.12 = (bf16[128,512]{1,0:T(8,128)(2,1)S(1)}, bf16[128,512]{1,0:T(8,128)(2,1)S(1)}, u32[]{:S(2)}, u32[]{:S(2)}) collective-permute-start(bf16[128,512]{1,0:T(8,128)(2,1)S(1)} %get-tuple-element.37), channel_id=1, source_target_pairs={{0,2},{1,3},{2,0},{3,1},{4,6},{5,7},{6,4},{7,5},{8,10},{9,11},{10,... | collective-permute-start | bytes 393224 | tf_op jit(solution)/shard_map/ppermute | solution.py:360
  88.2 0.0 collective-permute-done.7.refs_5_
  88.2 0.3 collective-permute-start.13
  88.5 0.9 collective-permute-done.8.refs_6_
  89.4 2.0 %collective-permute-start.14 = (bf16[128,512]{1,0:T(8,128)(2,1)S(1)}, bf16[128,512]{1,0:T(8,128)(2,1)S(1)}, u32[]{:S(2)}, u32[]{:S(2)}) collective-permute-start(bf16[128,512]{1,0:T(8,128)(2,1)S(1)} %get-tuple-element.39), channel_id=1, source_target_pairs={{0,4},{1,5},{2,6},{3,7},{4,0},{5,1},{6,2},{7,3},{8,12},{9,13},{10,... | collective-permute-start | bytes 393224 | tf_op jit(solution)/shard_map/ppermute | solution.py:360
  91.5 1.7 %collective-permute-done.9.refs_7_ = bf16[128,512]{1,0:T(8,128)(2,1)S(1)} collective-permute-done((bf16[128,512]{1,0:T(8,128)(2,1)S(1)}, bf16[128,512]{1,0:T(8,128)(2,1)S(1)}, u32[]{:S(2)}, u32[]{:S(2)}) %collective-permute-start.9) | collective-permute-done | bytes 131104 | tf_op jit(solution)/shard_map/ppermute | solution.py:360
  93.2 0.5 collective-permute-start.15
  93.7 0.0 collective-permute-done.11.refs_1_
  93.7 1.2 %collective-permute-start.16 = (bf16[128,512]{1,0:T(8,128)(2,1)S(1)}, bf16[128,512]{1,0:T(8,128)(2,1)S(1)}, u32[]{:S(2)}, u32[]{:S(2)}) collective-permute-start(bf16[128,512]{1,0:T(8,128)(2,1)S(1)} %get-tuple-element.41), channel_id=1, source_target_pairs={{0,6},{1,7},{2,4},{3,5},{4,2},{5,3},{6,0},{7,1},{8,14},{9,15},{10,... | collective-permute-start | bytes 393224 | tf_op jit(solution)/shard_map/ppermute | solution.py:360
  94.9 0.7 collective-permute-done.12.refs_2_
  95.6 1.8 %collective-permute-start.17 = (bf16[128,512]{1,0:T(8,128)(2,1)S(1)}, bf16[128,512]{1,0:T(8,128)(2,1)S(1)}, u32[]{:S(2)}, u32[]{:S(2)}) collective-permute-start(bf16[128,512]{1,0:T(8,128)(2,1)S(1)} %get-tuple-element.42), channel_id=1, source_target_pairs={{0,7},{1,6},{2,5},{3,4},{4,3},{5,2},{6,1},{7,0},{8,15},{9,14},{10,... | collective-permute-start | bytes 393224 | tf_op jit(solution)/shard_map/ppermute | solution.py:360
  97.5 0.7 collect.1.early_ref
  98.2 0.0 collective-permute-done.13.refs_3_
  98.2 0.0 collective-permute-done.14.refs_4_
  98.2 6.0 %collective-permute-done.15.refs_5_ = bf16[128,512]{1,0:T(8,128)(2,1)S(1)} collective-permute-done((bf16[128,512]{1,0:T(8,128)(2,1)S(1)}, bf16[128,512]{1,0:T(8,128)(2,1)S(1)}, u32[]{:S(2)}, u32[]{:S(2)}) %collective-permute-start.15) | collective-permute-done | bytes 131104 | tf_op jit(solution)/shard_map/ppermute | solution.py:360
  104.2 0.0 collective-permute-done.16.refs_6_
  104.2 0.0 collective-permute-done.17.refs_7_
  104.3 3.1 %finish.1 = bf16[512,1024]{1,0:T(8,128)(2,1)} custom-call(s32[512,128]{1,0:T(8,128)S(1)} %copy-done.12, f32[1,1024]{1,0:T(1,128)S(1)} %bitcast.15, bf16[512,512]{1,0:T(8,128)(2,1)S(1)} %collect.1.early_ref, bf16[512,1024]{1,0:T(8,128)(2,1)S(1)} %copy-done.4, bf16[512,1024]{1,0:T(8,128)(2,1)S(1)} %copy-done.2, bf16[1024,1024]{1,0:T(8,128)(2,1)S(1)} %copy-done.5, ...), custom_call_target="tpu_custom_call" | custom-call | flops 2147483648 | bytes 7340032 | tf_op jit(solution)/shard_map/finish/pallas_call | solution.py:345
  (16 shorter events, 0.0 us)
Async XLA Ops:
  0.0 50.0 %collective-permute-start.1 = (bf16[256,2048]{1,0:T(8,128)(2,1)}, bf16[256,2048]{1,0:T(8,128)(2,1)S(1)}, u32[]{:S(2)}, u32[]{:S(2)}) collective-permute-start(bf16[256,2048]{1,0:T(8,128)(2,1)} %bitcast.12), channel_id=1, source_target_pairs={{0,16},{8,24},{16,0},{24,8},{1,17},{9,25},{17,1},{25,9},{2,18},{10... | collective-permute-start | bytes 3145736 | tf_op jit(solution)/shard_map/ppermute | solution.py:360
  4.0 48.4 %collective-permute-start = (bf16[256,2048]{1,0:T(8,128)(2,1)}, bf16[256,2048]{1,0:T(8,128)(2,1)}, u32[]{:S(2)}, u32[]{:S(2)}) collective-permute-start(bf16[256,2048]{1,0:T(8,128)(2,1)} %bitcast.13), channel_id=1, source_target_pairs={{0,8},{8,0},{16,24},{24,16},{1,9},{9,1},{17,25},{25,17},{2,10},{10... | collective-permute-start | bytes 3145736 | tf_op jit(solution)/shard_map/ppermute | solution.py:360
  13.9 39.5 %all-to-all-start = ((bf16[8,128,1152]{2,1,0:T(8,128)(2,1)}), bf16[8,128,1152]{2,1,0:T(8,128)(2,1)S(1)}, u32[]{:S(2)}, u32[]{:S(2)}) async-start(bf16[8,128,1152]{2,1,0:T(8,128)(2,1)} %bitcast.16), calls=%async_computation | async-start | bytes 4718592 | tf_op jit(solution)/shard_map/all_to_all | solution.py:394
  18.3 2.2 %copy-start = (bf16[1024,2048]{1,0:T(8,128)(2,1)S(1)}, bf16[1024,2048]{1,0:T(8,128)(2,1)}, u32[]{:S(2)}) copy-start(bf16[1024,2048]{1,0:T(8,128)(2,1)} %w_hbm.1) | copy-start | bytes 12582916
  20.5 1.2 %copy-start.1 = (bf16[512,1024]{1,0:T(8,128)(2,1)S(1)}, bf16[512,1024]{1,0:T(8,128)(2,1)}, u32[]{:S(2)}) copy-start(bf16[512,1024]{1,0:T(8,128)(2,1)} %x_ref.3) | copy-start | bytes 3145732
  21.7 1.5 %copy-start.13 = (s32[512,1]{0,1:T(1,128)S(1)}, s32[512,1]{0,1:T(1,128)}, u32[]{:S(2)}) copy-start(s32[512,1]{0,1:T(1,128)} %param.10) | copy-start | bytes 6148
  23.1 29.3 %copy-start.3 = (bf16[512,1024]{1,0:T(8,128)(2,1)}, bf16[512,1024]{1,0:T(8,128)(2,1)S(1)}, u32[]{:S(2)}) copy-start(bf16[512,1024]{1,0:T(8,128)(2,1)S(1)} %project_gate.1.refs_0_.gate_ref) | copy-start | bytes 3145732
  50.9 0.8 copy-start.7
  51.7 14.3 %collective-permute-start.2 = (bf16[256,1024]{1,0:T(8,128)(2,1)}, bf16[256,1024]{1,0:T(8,128)(2,1)}, u32[]{:S(2)}, u32[]{:S(2)}) collective-permute-start(bf16[256,1024]{1,0:T(8,128)(2,1)} %get-tuple-element.24), channel_id=1, source_target_pairs={{0,8},{8,0},{16,24},{24,16},{1,9},{9,1},{17,25},{25,17},{2,10},{10... | collective-permute-start | bytes 1572872 | tf_op jit(solution)/shard_map/ppermute | solution.py:360
  52.7 0.7 copy-start.10
  53.4 1.2 %copy-start.6 = (bf16[1,256,2048]{2,1,0:T(8,128)(2,1)S(1)}, bf16[1,256,2048]{2,1,0:T(8,128)(2,1)}, u32[]{:S(2)}) copy-start(bf16[1,256,2048]{2,1,0:T(8,128)(2,1)} %param.13) | copy-start | bytes 3145732
  54.7 0.9 copy-start.11
  55.6 10.4 %copy-start.8 = (bf16[256,1024]{1,0:T(8,128)(2,1)S(1)}, bf16[256,1024]{1,0:T(8,128)(2,1)}, u32[]{:S(2)}) copy-start(bf16[256,1024]{1,0:T(8,128)(2,1)} %copy-done.7) | copy-start | bytes 1572868
  66.0 13.6 %collective-permute-start.10 = (bf16[256,1024]{1,0:T(8,128)(2,1)S(1)}, bf16[256,1024]{1,0:T(8,128)(2,1)S(1)}, u32[]{:S(2)}, u32[]{:S(2)}) collective-permute-start(bf16[256,1024]{1,0:T(8,128)(2,1)S(1)} %copy-done.8), channel_id=1, source_target_pairs={{0,8},{8,0},{16,24},{24,16},{1,9},{9,1},{17,25},{25,17},{2,10},{10... | collective-permute-start | bytes 1572872 | tf_op jit(solution)/shard_map/ppermute | solution.py:360
  72.2 10.4 %collective-permute-start.3 = (bf16[128,512]{1,0:T(8,128)(2,1)S(1)}, bf16[128,512]{1,0:T(8,128)(2,1)S(1)}, u32[]{:S(2)}, u32[]{:S(2)}) collective-permute-start(bf16[128,512]{1,0:T(8,128)(2,1)S(1)} %get-tuple-element.26), channel_id=1, source_target_pairs={{0,1},{1,0},{2,3},{3,2},{4,5},{5,4},{6,7},{7,6},{8,9},{9,8},{10,11... | collective-permute-start | bytes 393224 | tf_op jit(solution)/shard_map/ppermute | solution.py:360
  72.3 12.9 %collective-permute-start.4 = (bf16[128,512]{1,0:T(8,128)(2,1)S(1)}, bf16[128,512]{1,0:T(8,128)(2,1)S(1)}, u32[]{:S(2)}, u32[]{:S(2)}) collective-permute-start(bf16[128,512]{1,0:T(8,128)(2,1)S(1)} %get-tuple-element.27), channel_id=1, source_target_pairs={{0,2},{1,3},{2,0},{3,1},{4,6},{5,7},{6,4},{7,5},{8,10},{9,11},{10,... | collective-permute-start | bytes 393224 | tf_op jit(solution)/shard_map/ppermute | solution.py:360
  73.9 12.7 %collective-permute-start.5 = (bf16[128,512]{1,0:T(8,128)(2,1)S(1)}, bf16[128,512]{1,0:T(8,128)(2,1)S(1)}, u32[]{:S(2)}, u32[]{:S(2)}) collective-permute-start(bf16[128,512]{1,0:T(8,128)(2,1)S(1)} %get-tuple-element.28), channel_id=1, source_target_pairs={{0,3},{1,2},{2,1},{3,0},{4,7},{5,6},{6,5},{7,4},{8,11},{9,10},{10,... | collective-permute-start | bytes 393224 | tf_op jit(solution)/shard_map/ppermute | solution.py:360
  74.2 12.5 %collective-permute-start.6 = (bf16[128,512]{1,0:T(8,128)(2,1)S(1)}, bf16[128,512]{1,0:T(8,128)(2,1)S(1)}, u32[]{:S(2)}, u32[]{:S(2)}) collective-permute-start(bf16[128,512]{1,0:T(8,128)(2,1)S(1)} %get-tuple-element.29), channel_id=1, source_target_pairs={{0,4},{1,5},{2,6},{3,7},{4,0},{5,1},{6,2},{7,3},{8,12},{9,13},{10,... | collective-permute-start | bytes 393224 | tf_op jit(solution)/shard_map/ppermute | solution.py:360
  79.7 8.5 %collective-permute-start.7 = (bf16[128,512]{1,0:T(8,128)(2,1)S(1)}, bf16[128,512]{1,0:T(8,128)(2,1)S(1)}, u32[]{:S(2)}, u32[]{:S(2)}) collective-permute-start(bf16[128,512]{1,0:T(8,128)(2,1)S(1)} %get-tuple-element.30), channel_id=1, source_target_pairs={{0,5},{1,4},{2,7},{3,6},{4,1},{5,0},{6,3},{7,2},{8,13},{9,12},{10,... | collective-permute-start | bytes 393224 | tf_op jit(solution)/shard_map/ppermute | solution.py:360
  79.7 17.8 %copy-start.12 = (s32[512,128]{1,0:T(8,128)S(1)}, s32[512,128]{1,0:T(8,128)}, u32[]{:S(2)}) copy-start(s32[512,128]{1,0:T(8,128)} %copy-done.10) | copy-start | bytes 786436
  79.7 24.6 %copy-start.2 = (bf16[512,1024]{1,0:T(8,128)(2,1)S(1)}, bf16[512,1024]{1,0:T(8,128)(2,1)}, u32[]{:S(2)}) copy-start(bf16[512,1024]{1,0:T(8,128)(2,1)} %x_ref.3) | copy-start | bytes 3145732
  79.7 24.6 %copy-start.4 = (bf16[512,1024]{1,0:T(8,128)(2,1)S(1)}, bf16[512,1024]{1,0:T(8,128)(2,1)}, u32[]{:S(2)}) copy-start(bf16[512,1024]{1,0:T(8,128)(2,1)} %copy-done.3) | copy-start | bytes 3145732
  79.7 24.6 %copy-start.5 = (bf16[1024,1024]{1,0:T(8,128)(2,1)S(1)}, bf16[1024,1024]{1,0:T(8,128)(2,1)}, u32[]{:S(2)}) copy-start(bf16[1024,1024]{1,0:T(8,128)(2,1)} %w_ref.3) | copy-start | bytes 6291460
  79.7 24.6 %copy-start.9 = (f32[1024]{0:T(1024)S(1)}, f32[1024]{0:T(1024)}, u32[]{:S(2)}) copy-start(f32[1024]{0:T(1024)} %param.16) | copy-start | bytes 12292
  82.7 6.7 %collective-permute-start.8 = (bf16[128,512]{1,0:T(8,128)(2,1)S(1)}, bf16[128,512]{1,0:T(8,128)(2,1)S(1)}, u32[]{:S(2)}, u32[]{:S(2)}) collective-permute-start(bf16[128,512]{1,0:T(8,128)(2,1)S(1)} %get-tuple-element.31), channel_id=1, source_target_pairs={{0,6},{1,7},{2,4},{3,5},{4,2},{5,3},{6,0},{7,1},{8,14},{9,15},{10,... | collective-permute-start | bytes 393224 | tf_op jit(solution)/shard_map/ppermute | solution.py:360
  85.2 8.0 %collective-permute-start.9 = (bf16[128,512]{1,0:T(8,128)(2,1)S(1)}, bf16[128,512]{1,0:T(8,128)(2,1)S(1)}, u32[]{:S(2)}, u32[]{:S(2)}) collective-permute-start(bf16[128,512]{1,0:T(8,128)(2,1)S(1)} %get-tuple-element.32), channel_id=1, source_target_pairs={{0,7},{1,6},{2,5},{3,4},{4,3},{5,2},{6,1},{7,0},{8,15},{9,14},{10,... | collective-permute-start | bytes 393224 | tf_op jit(solution)/shard_map/ppermute | solution.py:360
  86.6 7.1 %collective-permute-start.11 = (bf16[128,512]{1,0:T(8,128)(2,1)S(1)}, bf16[128,512]{1,0:T(8,128)(2,1)S(1)}, u32[]{:S(2)}, u32[]{:S(2)}) collective-permute-start(bf16[128,512]{1,0:T(8,128)(2,1)S(1)} %get-tuple-element.36), channel_id=1, source_target_pairs={{0,1},{1,0},{2,3},{3,2},{4,5},{5,4},{6,7},{7,6},{8,9},{9,8},{10,11... | collective-permute-start | bytes 393224 | tf_op jit(solution)/shard_map/ppermute | solution.py:360
  86.7 9.0 %collective-permute-start.12 = (bf16[128,512]{1,0:T(8,128)(2,1)S(1)}, bf16[128,512]{1,0:T(8,128)(2,1)S(1)}, u32[]{:S(2)}, u32[]{:S(2)}) collective-permute-start(bf16[128,512]{1,0:T(8,128)(2,1)S(1)} %get-tuple-element.37), channel_id=1, source_target_pairs={{0,2},{1,3},{2,0},{3,1},{4,6},{5,7},{6,4},{7,5},{8,10},{9,11},{10,... | collective-permute-start | bytes 393224 | tf_op jit(solution)/shard_map/ppermute | solution.py:360
  88.2 10.0 %collective-permute-start.13 = (bf16[128,512]{1,0:T(8,128)(2,1)S(1)}, bf16[128,512]{1,0:T(8,128)(2,1)S(1)}, u32[]{:S(2)}, u32[]{:S(2)}) collective-permute-start(bf16[128,512]{1,0:T(8,128)(2,1)S(1)} %get-tuple-element.38), channel_id=1, source_target_pairs={{0,3},{1,2},{2,1},{3,0},{4,7},{5,6},{6,5},{7,4},{8,11},{9,10},{10,... | collective-permute-start | bytes 393224 | tf_op jit(solution)/shard_map/ppermute | solution.py:360
  89.4 8.8 %collective-permute-start.14 = (bf16[128,512]{1,0:T(8,128)(2,1)S(1)}, bf16[128,512]{1,0:T(8,128)(2,1)S(1)}, u32[]{:S(2)}, u32[]{:S(2)}) collective-permute-start(bf16[128,512]{1,0:T(8,128)(2,1)S(1)} %get-tuple-element.39), channel_id=1, source_target_pairs={{0,4},{1,5},{2,6},{3,7},{4,0},{5,1},{6,2},{7,3},{8,12},{9,13},{10,... | collective-permute-start | bytes 393224 | tf_op jit(solution)/shard_map/ppermute | solution.py:360
  93.2 11.0 %collective-permute-start.15 = (bf16[128,512]{1,0:T(8,128)(2,1)S(1)}, bf16[128,512]{1,0:T(8,128)(2,1)S(1)}, u32[]{:S(2)}, u32[]{:S(2)}) collective-permute-start(bf16[128,512]{1,0:T(8,128)(2,1)S(1)} %get-tuple-element.40), channel_id=1, source_target_pairs={{0,5},{1,4},{2,7},{3,6},{4,1},{5,0},{6,3},{7,2},{8,13},{9,12},{10,... | collective-permute-start | bytes 393224 | tf_op jit(solution)/shard_map/ppermute | solution.py:360
  93.7 10.5 %collective-permute-start.16 = (bf16[128,512]{1,0:T(8,128)(2,1)S(1)}, bf16[128,512]{1,0:T(8,128)(2,1)S(1)}, u32[]{:S(2)}, u32[]{:S(2)}) collective-permute-start(bf16[128,512]{1,0:T(8,128)(2,1)S(1)} %get-tuple-element.41), channel_id=1, source_target_pairs={{0,6},{1,7},{2,4},{3,5},{4,2},{5,3},{6,0},{7,1},{8,14},{9,15},{10,... | collective-permute-start | bytes 393224 | tf_op jit(solution)/shard_map/ppermute | solution.py:360
  95.6 8.6 %collective-permute-start.17 = (bf16[128,512]{1,0:T(8,128)(2,1)S(1)}, bf16[128,512]{1,0:T(8,128)(2,1)S(1)}, u32[]{:S(2)}, u32[]{:S(2)}) collective-permute-start(bf16[128,512]{1,0:T(8,128)(2,1)S(1)} %get-tuple-element.42), channel_id=1, source_target_pairs={{0,7},{1,6},{2,5},{3,4},{4,3},{5,2},{6,1},{7,0},{8,15},{9,14},{10,... | collective-permute-start | bytes 393224 | tf_op jit(solution)/shard_map/ppermute | solution.py:360

commit v7 on v6

--- a/solution.py
+++ b/solution.py
@@ -15,7 +15,9 @@
 F32 = jnp.float32
 BF16 = jnp.bfloat16
 MIB = 1024 * 1024
-WAIT_COST = 20.0
+WAIT_COST = 30.0
+LATE_SHARE = 20.0
+COLLECT_COST = 20.0
 KERNEL_MIB = 24
 QUERY_MIB = 60
 
@@ -188,16 +190,21 @@
     )(owner_row, *after)
 
 
-def attend_kernel(size, heads, first, starts, behind, has_base, outs, place_ref, *refs):
+def attend_kernel(size, heads, first, starts, behind, has_base, capacity, place_ref, *refs):
     refs = refs[behind:]
     rows_ref, refs = refs[0], refs[1:]
     count = len(starts)
-    parts, refs = refs[:count], refs[count:]
+    parts = []
+    for _, _, pieces in starts:
+        parts.append(refs[:pieces])
+        refs = refs[pieces:]
     base_ref = refs[0] if has_base else None
+    outs = 3 if capacity else 1
     out_refs, shown = refs[int(has_base) : int(has_base) + outs], refs[int(has_base) + outs]
     result = out_refs[0] if outs == 1 else refs[-1]
     slots = rows_ref.shape[0]
-    keys = parts[0].shape[0]
+    columns_of = slots // capacity if capacity else 1
+    keys = sum(piece.shape[0] for piece in parts[0])
     blocks = keys // BLK
     seen = rows_ref[:, HEADS * size :].astype(F32)
     for number in range(count):
@@ -210,11 +217,14 @@
     def columns(start):
         return pl.ds(pl.multiple_of(start, size), size)
 
+    def read(part, start):
+        return jnp.concatenate([piece[:, columns(start)] for piece in part], axis=0)
+
     def one_head(head, carry):
         values = []
         for number, part in enumerate(parts):
             inside = row + place_ref[2 + number] * keys < place_ref[0]
-            value = part[:, columns((starts[number][1] + head) * size)].astype(F32)
+            value = read(part, (starts[number][1] + head) * size).astype(F32)
             values.append(jnp.where(inside, value, 0.0).astype(BF16))
         values = jnp.concatenate(values, axis=0)
         for start in range(0, slots, tile):
@@ -224,7 +234,7 @@
             for number, part in enumerate(parts):
                 scores = lax.dot_general(
                     queries,
-                    part[:, columns((starts[number][0] + head) * size)],
+                    read(part, (starts[number][0] + head) * size),
                     (((1,), (1,)), ((), ())),
                     preferred_element_type=F32,
                 )
@@ -236,45 +246,50 @@
                 jnp.concatenate(weights, axis=1), values, preferred_element_type=F32
             )
             if has_base:
-                total = total + base_ref[span, columns((first + head) * size)]
+                total = total + base_ref[span, columns(head * size)]
             result[span, columns(head * size)] = total.astype(result.dtype)
         return carry
 
     lax.fori_loop(0, heads, one_head, 0)
     if outs > 1:
-        capacity = slots // outs
-        for number, ref in enumerate(out_refs):
-            start = pl.multiple_of((place_ref[1] ^ number) * capacity, capacity)
-            ref[...] = result[pl.ds(start, capacity), :]
-
-
-def attend(place, after, rows, segments, base, first, heads, size, outs, dtype):
+        numbers = list(range(0, columns_of, 2)) + list(range(1, columns_of, 2))
+        for ref in out_refs:
+            for start in range(0, ref.shape[0], capacity):
+                block = place_ref[1] ^ numbers.pop(0)
+                source = pl.ds(pl.multiple_of(block * capacity, capacity), capacity)
+                ref[start : start + capacity, :] = result[source, :]
+
+
+def attend(place, after, rows, segments, base, first, heads, size, capacity, dtype, share):
     slots = rows.shape[0]
-    keys = segments[0][0].shape[0]
+    keys = sum(piece.shape[0] for piece in segments[0][0])
     count = len(segments)
-    starts = [(key, value) for _, key, value in segments]
+    starts = [(key, value, len(pieces)) for pieces, key, value in segments]
+    pieces = [piece for pieces, _, _ in segments for piece in pieces]
+    heights = [slots // 2, slots // 4, slots // 4] if capacity else [slots]
+    outs = len(heights)
     extra = [] if base is None else [base]
     scratch = [pltpu.VMEM((count * (keys // BLK), slots, BLK), BF16)]
     if outs > 1:
         scratch.append(pltpu.VMEM((slots, heads * size), BF16))
     return pl.pallas_call(
         functools.partial(
-            attend_kernel, size, heads, first, starts, len(after), base is not None, outs
+            attend_kernel, size, heads, first, starts, len(after), base is not None, capacity
         ),
         in_specs=[pl.BlockSpec(memory_space=pltpu.SMEM)]
         + unread(after)
-        + whole(1 + count + len(extra)),
+        + whole(1 + len(pieces) + len(extra)),
         out_specs=whole(outs),
-        out_shape=[jax.ShapeDtypeStruct((slots // outs, heads * size), dtype)] * outs,
+        out_shape=[jax.ShapeDtypeStruct((height, heads * size), dtype) for height in heights],
         scratch_shapes=scratch,
         compiler_params=params(KERNEL_MIB),
         cost_estimate=cost(
-            4 * slots * keys * count * heads * size,
+            share * 4 * slots * keys * count * heads * size,
             2 * (2 * slots + count * keys * 2) * heads * size,
             slots * keys * count * heads,
         ),
         name="attend",
-    )(place, *after, rows, *[piece for piece, _, _ in segments], *extra)
+    )(place, *after, rows, *pieces, *extra)
 
 
 def placement(slot, slots):
@@ -284,48 +299,41 @@
     )
 
 
-def collect_kernel(groups, slot_ref, *refs):
-    parts, out_ref = refs[:-1], refs[-1]
-    each = len(parts) // groups
-    place = placement(slot_ref[...], each * parts[0].shape[0])
-    first = 0
-    for group in range(groups):
-        rows = jnp.concatenate(
-            [part[...] for part in parts[group * each : (group + 1) * each]], axis=0
-        )
-        last = first + rows.shape[1]
-        out_ref[:, first:last] = jnp.dot(place, rows, preferred_element_type=F32).astype(BF16)
-        first = last
-
-
-def collect(slot, groups):
-    rows = slot.shape[0]
-    parts = [part for group in groups for part in group]
-    width = sum(group[0].shape[1] for group in groups)
-    slots = len(groups[0]) * groups[0][0].shape[0]
-    vmem = pl.BlockSpec(memory_space=pltpu.VMEM)
-    return pl.pallas_call(
-        functools.partial(collect_kernel, len(groups)),
-        in_specs=[vmem] * (1 + len(parts)),
-        out_specs=vmem,
+def in_slots(parts, capacity):
+    return jnp.concatenate(
+        [part[:capacity, :] for part in parts[:2]] + [part[...] for part in parts[2:]], axis=0
+    )
+
+
+def collect_kernel(capacity, slots, slot_ref, *refs):
+    rows = in_slots(refs[:-1], capacity)
+    place = placement(slot_ref[...], slots)
+    refs[-1][...] = jnp.dot(place, rows, preferred_element_type=F32).astype(BF16)
+
+
+def collect(slot, parts, capacity, slots):
+    rows, width = slot.shape[0], parts[0].shape[1]
+    return pl.pallas_call(
+        functools.partial(collect_kernel, capacity, slots),
+        in_specs=whole(1 + len(parts)),
+        out_specs=whole()[0],
         out_shape=jax.ShapeDtypeStruct((rows, width), BF16),
         compiler_params=params(KERNEL_MIB),
-        cost_estimate=cost(2 * rows * slots * width, 2 * (rows + slots) * width),
+        cost_estimate=cost(COLLECT_COST * 1e9, 2 * (rows + slots) * width),
         name="collect",
     )(slot, *parts)
 
 
-def finish_kernel(slot_ref, gain_ref, early_ref, gate_ref, x_ref, w_ref, *refs):
-    parts, (out_hbm, out_ref, sems) = refs[:-3], refs[-3:]
+def finish_kernel(groups, capacity, slots, slot_ref, gain_ref, gate_ref, x_ref, w_ref, *refs):
+    early, parts, (out_hbm, out_ref, sems) = refs[:groups], refs[groups:-3], refs[-3:]
     rows = x_ref.shape[0]
-    returned = jnp.concatenate([part[...] for part in parts], axis=0)
-    place = placement(slot_ref[...], returned.shape[0])
-    late = jnp.dot(place, returned, preferred_element_type=F32)
+    place = placement(slot_ref[...], slots)
+    late = jnp.dot(place, in_slots(parts, capacity), preferred_element_type=F32)
     tile = rows // 2
     stores = []
     for half in range(2):
         span = slice(half * tile, (half + 1) * tile)
-        attn = jnp.concatenate([early_ref[span, :].astype(F32), late[span, :]], axis=1)
+        attn = jnp.concatenate([part[span, :].astype(F32) for part in early] + [late[span, :]], axis=1)
         centered = attn - jnp.mean(attn, axis=1, keepdims=True)
         variance = jnp.mean(centered * centered, axis=1, keepdims=True)
         normed = (centered * lax.rsqrt(variance + norm_eps) * gain_ref[...]).astype(BF16)
@@ -339,12 +347,11 @@
         store.wait()
 
 
-def finish(slot, early, gate, cand_x, ln_gain, w_out, parts):
+def finish(slot, early, gate, cand_x, ln_gain, w_out, parts, capacity, slots):
     rows, width = cand_x.shape
-    slots = len(parts) * parts[0].shape[0]
-    return pl.pallas_call(
-        finish_kernel,
-        in_specs=whole(6 + len(parts)),
+    return pl.pallas_call(
+        functools.partial(finish_kernel, len(early), capacity, slots),
+        in_specs=whole(5 + len(early) + len(parts)),
         out_specs=pl.BlockSpec(memory_space=pl.ANY),
         out_shape=jax.ShapeDtypeStruct((rows, width), BF16),
         scratch_shapes=[pltpu.VMEM((rows, width), BF16), pltpu.SemaphoreType.DMA((2,))],
@@ -353,20 +360,40 @@
             2 * rows * width * (width + slots), 2 * (3 * rows * width + width * width + slots * width)
         ),
         name="finish",
-    )(slot, ln_gain.reshape(1, width), early, gate, cand_x, w_out, *parts)
+    )(slot, ln_gain.reshape(1, width), gate, cand_x, w_out, *early, *parts)
 
 
 def swap(array, axis, bits, count):
     return lax.ppermute(array, axis, [(i, i ^ bits) for i in range(count)])
 
 
-def exchange(blocks):
-    count = len(blocks)
-    order = sorted(range(1, count), key=lambda d: (d & 1, d >> 1 == (count >> 1) - 1, d))
-    back = {0: blocks[0]}
-    for d in order:
-        back[d] = swap(blocks[d], "cand", d, count)
-    return [back[d] for d in range(count)]
+def forward(piece, number, count):
+    if number == 0:
+        return [swap(piece, "user", 1, count)]
+    half = piece.shape[0] // 2
+    upper = swap(piece[:half], "user", 1, count)
+    lower, _ = lax.optimization_barrier((piece[half:], upper))
+    return [upper, swap(lower, "user", 1, count)]
+
+
+def exchange_cores(even, odds, capacity, count, behind):
+    others = [swap(odd, "cand", 1, count) for odd in odds]
+    if behind is not None:
+        (even, others), _ = lax.optimization_barrier(((even, others), behind))
+    pairs = []
+    for d in range(1, count // 2):
+        first, second = d * capacity, (d * capacity) % odds[0].shape[0]
+        other = others[first // odds[0].shape[0]]
+        pairs.append(
+            jnp.concatenate(
+                [even[first : first + capacity], other[second : second + capacity]], axis=0
+            )
+        )
+    return [even, others[0]], pairs
+
+
+def exchange_chips(pairs, count):
+    return [swap(pair, "cand", 2 * d, count) for d, pair in enumerate(pairs, 1)]
 
 
 def per_device(cand_x, cand_user, visible, hist_len, kv_cache, w_in, w_out, ln_gain):
@@ -381,48 +408,51 @@
     visible_row = visible.reshape(1, rows)
     spans = [(sum(GROUPS[:number]), heads) for number, heads in enumerate(GROUPS)]
 
-    held = {0: kv_cache[0], 1: swap(kv_cache[0], "user", 1, count)}
-    bit = count // 2
-    while bit > 1:
-        for key in sorted(key for key in held if key != 1):
-            held[key | bit] = swap(held[key], "user", bit, count)
-        bit //= 2
-    ready = sorted(held)
-    late = [key | 1 for key in ready if key > 1]
+    near = swap(kv_cache[0], "user", 1, count)
+    far = []
+    for own in split(kv_cache[0], spans, size):
+        held = {0: own}
+        bit = count // 2
+        while bit > 1:
+            for key in sorted(held):
+                held[key | bit] = swap(held[key], "user", bit, count)
+            bit //= 2
+        far.append(held)
+    evens = sorted(far[0])
+    late = [key | 1 for key in evens[1:]]
 
     send = project_queries(owner_row, visible_row, cand_x, w_in, columns, capacity)
     got = lax.all_to_all(
         send.reshape(columns, capacity, -1), "cand", split_axis=0, concat_axis=0, tiled=True
     ).reshape(slots, -1)
     gate = project_gate(cand_x, w_in)
-    arrived = [held[key] for key in ready if key]
+    arrived = [near] + [far[0][key] for key in evens[1:]]
     slot = slot_column(owner_row ^ me, columns, capacity, [gate] + arrived)
     position = lax.axis_index("user").astype(jnp.int32)
-    shards = position ^ jnp.array(ready + late, jnp.int32)
+    shards = position ^ jnp.array(evens + [1] + late, jnp.int32)
     head = jnp.concatenate([hist_len, me[None]])
-    place_ready = jnp.concatenate([head, shards[: len(ready)]])
-    place_late = jnp.concatenate([head, shards[len(ready) :]])
-
-    segments = [(held[key], 0, HEADS) for key in ready]
-    base = attend(place_ready, [slot], got, segments, None, 0, HEADS, size, 1, F32)[0]
-    passed = [split(held[key ^ 1], spans, size) for key in late]
-    cuts = []
-    for number in range(len(spans)):
-        parts = [pieces[number] for pieces in passed]
-        if number:
-            parts, _ = lax.optimization_barrier((parts, (cuts[-1], base)))
-        cuts.append([swap(part, "user", 1, count) for part in parts])
-    returned = []
-    after = []
+    place_ready = jnp.concatenate([head, shards[: len(evens) + 1]])
+    place_late = jnp.concatenate([head, shards[len(evens) + 1 :]])
+
+    early = []
+    after = [slot]
     for number, (first, heads) in enumerate(spans):
-        segments = [(cut, 0, heads) for cut in cuts[number]]
+        held = far[number]
+        cuts = [(forward(held[key], number, count), 0, heads) for key in evens[1:]]
+        segments = [([held[key]], 0, heads) for key in evens]
+        segments.append(([near], first, HEADS + first))
+        base = attend(
+            place_ready, after, got, segments, None, first, heads, size, None, F32, 0.0
+        )[0]
         attn = attend(
-            place_late, after, got, segments, base, first, heads, size, columns, BF16
+            place_late, [], got, cuts, base, first, heads, size, capacity, BF16, LATE_SHARE * (number > 0)
         )
-        after = [attn[0]]
-        returned.append(exchange(attn))
-    early = collect(slot, returned[:-1])
-    return finish(slot, early, gate, cand_x, ln_gain, w_out, returned[-1])
+        here, pairs = exchange_cores(attn[0], attn[1:], capacity, columns, early[-1] if early else None)
+        after = [slot, attn[0]] + pairs
+        returned = here + exchange_chips(pairs, columns)
+        if number + 1 < len(spans):
+            early.append(collect(slot, returned, capacity, slots))
+    return finish(slot, early, gate, cand_x, ln_gain, w_out, returned, capacity, slots)
 
 
 def solution(mesh):

time: 108 us -> 119 us (1.10)
  waiting for transfers between devices: 40.1 us -> 53.5 us
  starting transfers between devices: 26.3 us -> 20.4 us
  Pallas kernels: 31.5 us -> 33.2 us
    ppermute x18 -> x16, waiting for transfers between devices: 40.1 us -> 53.5 us  [swap(): return lax.ppermute(array, axis, [(i, i ^ bits) for i in range(count)])]
    ppermute x18 -> x16, starting transfers between devices: 22.6 us -> 16.6 us  [swap(): return lax.ppermute(array, axis, [(i, i ^ bits) for i in range(count)])]
    slice x1 -> x8, local copies, waits for them, and re-layouts: 0.65 us -> 2.56 us  [the longest x1 1.87 us: forward(): lower, _ = lax.optimization_barrier((piece[half:], upper))]
    pallas_call x3 -> x4, Pallas kernels: 16.8 us -> 18.5 us  [attend(): pl.pallas_call(functools.partial(attend_kernel, size, heads, first, start...]
    unnamed x28 -> x32, local copies, waits for them, and re-layouts: 7.12 us -> 6.37 us
  transfers between devices with their start and end apart: 19 -> 17, of which waited for: 6 -> 6; matrix products, arithmetic and copies ran while one was open for 1% -> 3% of each run, Pallas kernels for 26% -> 26%
where the time goes in v7:
time: 119 us; the launch traced here: 118 us
  waiting for transfers between devices  53.5 us (45%)
  Pallas kernels  33.2 us (28%)
  starting transfers between devices  20.4 us (17%)
  local copies, waits for them, and re-layouts  8.94 us (8%)
    ppermute x16, waiting for transfers between devices, swap(): return lax.ppermute(array, axis, [(i, i ^ bits) for i in range(count)])  53.5 us
    pallas_call x4, Pallas kernels, attend(): pl.pallas_call(functools.partial(attend_kernel, size, heads, first, start...  18.5 us
    ppermute x16, starting transfers between devices, swap(): return lax.ppermute(array, axis, [(i, i ^ bits) for i in range(count)])  16.6 us
    pallas_call x1, Pallas kernels, project_queries(): pl.pallas_call(functools.partial(query_kernel, columns, capacity), in_spe...  8.32 us
    unnamed x32, local copies, waits for them, and re-layouts  6.37 us
    all_to_all x1, starting transfers between devices, per_device(): lax.all_to_all(send.reshape(columns, capacity, -1), 'cand', split_axis=0,...  3.81 us
    pallas_call x1, Pallas kernels, finish(): pl.pallas_call(functools.partial(finish_kernel, len(early), capacity, slo...  3.09 us
  transfers between devices with their start and end apart: 17, of which 6 were waited for; matrix products, arithmetic and copies ran while one was open for 3% of the time, Pallas kernels for 26%

profile of v7, /device:TPU:0, one launch (start us, length us, event | category | flops | bytes accessed | tf_op | source)
XLA Modules:
  0.0 118.1 jit_solution(14659664424060735680)
XLA Ops:
  0.0 3.0 %collective-permute-start = (bf16[256,2048]{1,0:T(8,128)(2,1)}, bf16[256,2048]{1,0:T(8,128)(2,1)S(1)}, u32[]{:S(2)}, u32[]{:S(2)}) collective-permute-start(bf16[256,2048]{1,0:T(8,128)(2,1)} %bitcast.13), channel_id=1, source_target_pairs={{0,8},{8,0},{16,24},{24,16},{1,9},{9,1},{17,25},{25,17},{2,10},{10... | collective-permute-start | bytes 3145736 | tf_op jit(solution)/shard_map/ppermute | solution.py:367
  3.0 1.3 %copy-done.4 = bf16[1,256,2048]{2,1,0:T(8,128)(2,1)S(1)} copy-done((bf16[1,256,2048]{2,1,0:T(8,128)(2,1)S(1)}, bf16[1,256,2048]{2,1,0:T(8,128)(2,1)}, u32[]{:S(2)}) %copy-start.4) | copy-done | bytes 1048600
  4.3 0.9 split.1
  5.2 2.6 %collective-permute-start.1 = (bf16[256,1024]{1,0:T(8,128)(2,1)}, bf16[256,1024]{1,0:T(8,128)(2,1)}, u32[]{:S(2)}, u32[]{:S(2)}) collective-permute-start(bf16[256,1024]{1,0:T(8,128)(2,1)} %get-tuple-element.17.refs_2_), channel_id=1, source_target_pairs={{0,16},{8,24},{16,0},{24,8},{1,17},{9,25},{17,1},{25,9},{2,18},{10... | collective-permute-start | bytes 1572872 | tf_op jit(solution)/shard_map/ppermute | solution.py:367
  7.7 8.3 %project_queries.1 = bf16[1024,1152]{1,0:T(8,128)(2,1)} custom-call(s32[1,512]{1,0:T(1,128)} %bitcast.17, s32[1,512]{1,0:T(1,128)} %bitcast.19, bf16[512,1024]{1,0:T(8,128)(2,1)} %x_ref.3, bf16[1024,2048]{1,0:T(8,128)(2,1)} %w_hbm.1), custom_call_target="tpu_custom_call" | custom-call | flops 2147483648 | bytes 5242880 | tf_op jit(solution)/shard_map/project_queries/pallas_call | solution.py:128
  16.1 0.0 copy-done.9
  16.1 0.0 copy-start.15
  16.1 3.8 %all-to-all-start = ((bf16[8,128,1152]{2,1,0:T(8,128)(2,1)}), bf16[8,128,1152]{2,1,0:T(8,128)(2,1)S(1)}, u32[]{:S(2)}, u32[]{:S(2)}) async-start(bf16[8,128,1152]{2,1,0:T(8,128)(2,1)} %bitcast.16), calls=%async_computation | async-start | bytes 4718592 | tf_op jit(solution)/shard_map/all_to_all | solution.py:425
  19.9 0.4 collective-permute-start.8
  21.0 0.0 copy-done.15
  21.0 0.6 slice.48
  21.6 0.1 pad_add_fusion.1.place_ref
  21.7 0.7 pad_add_fusion.place_ref
  22.4 2.2 %copy-done = bf16[1024,2048]{1,0:T(8,128)(2,1)S(1)} copy-done((bf16[1024,2048]{1,0:T(8,128)(2,1)S(1)}, bf16[1024,2048]{1,0:T(8,128)(2,1)}, u32[]{:S(2)}) %copy-start) | copy-done | bytes 4194328
  24.6 1.2 %copy-done.5 = bf16[512,1024]{1,0:T(8,128)(2,1)S(1)} copy-done((bf16[512,1024]{1,0:T(8,128)(2,1)S(1)}, bf16[512,1024]{1,0:T(8,128)(2,1)}, u32[]{:S(2)}) %copy-start.5) | copy-done | bytes 1048600
  25.8 1.4 %project_gate.1.refs_0_.gate_ref = bf16[512,1024]{1,0:T(8,128)(2,1)S(1)} custom-call(bf16[512,1024]{1,0:T(8,128)(2,1)S(1)} %copy-done.5, bf16[1024,2048]{1,0:T(8,128)(2,1)S(1)} %copy-done), custom_call_target="tpu_custom_call" | custom-call | flops 1073741824 | bytes 4194304 | tf_op jit(solution)/shard_map/project_gate/pallas_call | solution.py:162
  27.2 0.0 copy-done.14
  27.2 0.0 copy-start.7
  27.2 30.7 %collective-permute-done.8.refs_7_ = bf16[256,1024]{1,0:T(8,128)(2,1)} collective-permute-done((bf16[256,1024]{1,0:T(8,128)(2,1)}, bf16[256,1024]{1,0:T(8,128)(2,1)}, u32[]{:S(2)}, u32[]{:S(2)}) %collective-permute-start.8) | collective-permute-done | bytes 524320 | tf_op jit(solution)/shard_map/ppermute | solution.py:367
  57.9 1.9 %fusion.1 = (bf16[128,1024]{1,0:T(8,128)(2,1)}, bf16[128,1024]{1,0:T(8,128)(2,1)}) fusion(bf16[256,1024]{1,0:T(8,128)(2,1)} %collective-permute-done.8.refs_7_), kind=kLoop, calls=%fused_computation.11 | loop fusion | bytes 1048576 | tf_op jit(solution)/shard_map/slice | solution.py:375
  59.8 0.0 collective-permute-start.9
  59.8 0.0 collective-permute-done.1.refs_2_.refs_3_
  59.8 2.0 %collective-permute-start.2 = (bf16[256,1024]{1,0:T(8,128)(2,1)}, bf16[256,1024]{1,0:T(8,128)(2,1)}, u32[]{:S(2)}, u32[]{:S(2)}) collective-permute-start(bf16[256,1024]{1,0:T(8,128)(2,1)} %collective-permute-done.1.refs_2_.refs_3_), channel_id=1, source_target_pairs={{0,8},{8,0},{16,24},{24,16},{1,9},{9,1},{17,25},{25,17},{2,10},{10... | collective-permute-start | bytes 1572872 | tf_op jit(solution)/shard_map/ppermute | solution.py:367
  61.8 0.0 collective-permute-done.refs_1_.refs_4_.refs_8_
  61.8 0.3 slot_column.1.refs_0_.slot_ref
  62.1 0.0 copy-start.1
  62.1 0.7 copy-done.1
  62.8 0.0 all-to-all-done
  62.8 0.9 copy-done.2
  63.8 5.9 %attend.4.refs_2_ = f32[1024,512]{1,0:T(8,128)S(1)} custom-call(s32[5]{0:T(128)S(1)} %pad_add_fusion.1.place_ref, s32[512,128]{1,0:T(8,128)S(1)} %copy-done.2, bf16[1024,1152]{1,0:T(8,128)(2,1)S(1)} %bitcast.9, bf16[256,1024]{1,0:T(8,128)(2,1)} %get-tuple-element.17.refs_2_, bf16[256,1024]{1,0:T(8,128)(2,1)} %collective-permute-done.1.refs_2_.refs_3_, ...), custom_call_target="tpu_custom_call" | custom-call | bytes 3670016 | tf_op jit(solution)/shard_map/attend/pallas_call | solution.py:275
  69.7 9.4 %collective-permute-done.2.refs_1_ = bf16[256,1024]{1,0:T(8,128)(2,1)} collective-permute-done((bf16[256,1024]{1,0:T(8,128)(2,1)}, bf16[256,1024]{1,0:T(8,128)(2,1)}, u32[]{:S(2)}, u32[]{:S(2)}) %collective-permute-start.2) | collective-permute-done | bytes 524320 | tf_op jit(solution)/shard_map/ppermute | solution.py:367
  79.1 3.5 %attend.5 = (bf16[512,512]{1,0:T(8,128)(2,1)S(1)}, bf16[256,512]{1,0:T(8,128)(2,1)S(1)}, bf16[256,512]{1,0:T(8,128)(2,1)S(1)}) custom-call(s32[3]{0:T(128)S(1)} %pad_add_fusion.place_ref, bf16[1024,1152]{1,0:T(8,128)(2,1)S(1)} %bitcast.10, bf16[256,1024]{1,0:T(8,128)(2,1)} %collective-permute-done.2.refs_1_, f32[1024,512]{1,0:T(8,128)S(1)} %attend.4.refs_2_), custom_call_target="tpu_custom_call" | custom-call | bytes 2621440 | tf_op jit(solution)/shard_map/attend/pallas_call | solution.py:275
  82.6 0.1 collective-permute-start.5
  82.6 0.0 collective-permute-done.9.refs_1_
  82.6 0.0 copy-done.13
  82.7 0.3 collective-permute-start.10
  83.0 0.2 collective-permute-start.3
  83.2 0.9 collective-permute-done.5
  84.2 2.4 %collective-permute-start.7 = (bf16[256,512]{1,0:T(8,128)(2,1)S(1)}, bf16[256,512]{1,0:T(8,128)(2,1)S(1)}, u32[]{:S(2)}, u32[]{:S(2)}) collective-permute-start(bf16[256,512]{1,0:T(8,128)(2,1)S(1)} %pad_maximum_fusion.2.refs_4_), channel_id=1, source_target_pairs={{0,6},{1,7},{2,4},{3,5},{4,2},{5,3},{6,0},{7,1},{8,14},{9,15},{10,... | collective-permute-start | bytes 786440 | tf_op jit(solution)/shard_map/ppermute | solution.py:367
  86.6 0.6 collective-permute-start.6
  87.3 0.0 collective-permute-done.3.refs_1_
  87.3 0.6 collective-permute-start.4
  88.0 5.7 %attend.6.refs_3_ = f32[1024,512]{1,0:T(8,128)S(1)} custom-call(s32[5]{0:T(128)S(1)} %pad_add_fusion.1.place_ref, s32[512,128]{1,0:T(8,128)S(1)} %copy-done.2, bf16[512,512]{1,0:T(8,128)(2,1)S(1)} %get-tuple-element.18.refs_0_.refs_1_, bf16[256,512]{1,0:T(8,128)(2,1)S(1)} %pad_maximum_fusion.refs_2_, bf16[256,512]{1,0:T(8,128)(2,1)S(1)} %pad_maximum_fusion.1.refs_3_, ...), custom_call_target="tpu_custom_call" | custom-call | bytes 3670016 | tf_op jit(solution)/shard_map/attend/pallas_call | solution.py:275
  93.7 0.0 collective-permute-done.10.refs_2_
  93.7 3.4 %attend.7 = (bf16[512,512]{1,0:T(8,128)(2,1)S(1)}, bf16[256,512]{1,0:T(8,128)(2,1)S(1)}, bf16[256,512]{1,0:T(8,128)(2,1)S(1)}) custom-call(s32[3]{0:T(128)S(1)} %pad_add_fusion.place_ref, bf16[1024,1152]{1,0:T(8,128)(2,1)S(1)} %bitcast.12, bf16[128,1024]{1,0:T(8,128)(2,1)} %collective-permute-done.9.refs_1_, ...), custom_call_target="tpu_custom_call" | custom-call | flops 10737418240 | bytes 2621440 | tf_op jit(solution)/shard_map/attend/pallas_call | solution.py:275
  97.2 0.1 collective-permute-start.11
  97.2 0.5 collective-permute-start.12
  97.7 0.0 collective-permute-done.7.refs_4_
  97.7 1.4 %collective-permute-done.6.refs_3_ = bf16[256,512]{1,0:T(8,128)(2,1)S(1)} collective-permute-done((bf16[256,512]{1,0:T(8,128)(2,1)S(1)}, bf16[256,512]{1,0:T(8,128)(2,1)S(1)}, u32[]{:S(2)}, u32[]{:S(2)}) %collective-permute-start.6) | collective-permute-done | bytes 262176 | tf_op jit(solution)/shard_map/ppermute | solution.py:367
  99.1 0.0 collective-permute-done.4.refs_2_
  99.2 0.7 collect.1.refs_0_
  99.9 0.0 copy-start.6
  99.9 0.0 copy-start.8
  99.9 0.0 copy-start.12
  99.9 0.0 collective-permute-done.11.refs_2_
  99.9 0.0 collective-permute-done.12
  100.0 1.9 %collective-permute-start.15 = (bf16[256,512]{1,0:T(8,128)(2,1)S(1)}, bf16[256,512]{1,0:T(8,128)(2,1)S(1)}, u32[]{:S(2)}, u32[]{:S(2)}) collective-permute-start(bf16[256,512]{1,0:T(8,128)(2,1)S(1)} %pad_maximum_fusion.5), channel_id=1, source_target_pairs={{0,6},{1,7},{2,4},{3,5},{4,2},{5,3},{6,0},{7,1},{8,14},{9,15},{10,... | collective-permute-start | bytes 786440 | tf_op jit(solution)/shard_map/ppermute | solution.py:367
  101.9 1.2 collective-permute-start.14
  103.1 0.6 collective-permute-start.13
  103.8 6.4 %collective-permute-done.15.refs_5_ = bf16[256,512]{1,0:T(8,128)(2,1)S(1)} collective-permute-done((bf16[256,512]{1,0:T(8,128)(2,1)S(1)}, bf16[256,512]{1,0:T(8,128)(2,1)S(1)}, u32[]{:S(2)}, u32[]{:S(2)}) %collective-permute-start.15) | collective-permute-done | bytes 262176 | tf_op jit(solution)/shard_map/ppermute | solution.py:367
  110.2 4.6 %collective-permute-done.14.refs_4_ = bf16[256,512]{1,0:T(8,128)(2,1)S(1)} collective-permute-done((bf16[256,512]{1,0:T(8,128)(2,1)S(1)}, bf16[256,512]{1,0:T(8,128)(2,1)S(1)}, u32[]{:S(2)}, u32[]{:S(2)}) %collective-permute-start.14) | collective-permute-done | bytes 262176 | tf_op jit(solution)/shard_map/ppermute | solution.py:367
  114.8 0.0 collective-permute-done.13.refs_3_
  114.8 0.0 copy-done.11
  114.9 3.1 %finish.1 = bf16[512,1024]{1,0:T(8,128)(2,1)} custom-call(s32[512,128]{1,0:T(8,128)S(1)} %copy-done.3, f32[1,1024]{1,0:T(1,128)S(1)} %bitcast.15, bf16[512,1024]{1,0:T(8,128)(2,1)S(1)} %copy-done.8, bf16[512,1024]{1,0:T(8,128)(2,1)S(1)} %copy-done.6, bf16[1024,1024]{1,0:T(8,128)(2,1)S(1)} %copy-done.11, bf16[512,512]{1,0:T(8,128)(2,1)S(1)} %collect.1.refs_0_, ...), custom_call_target="tpu_custom_call" | custom-call | flops 2147483648 | bytes 7340032 | tf_op jit(solution)/shard_map/finish/pallas_call | solution.py:352
  (30 shorter events, 0.3 us)
Async XLA Ops:
  0.0 61.8 %collective-permute-start = (bf16[256,2048]{1,0:T(8,128)(2,1)}, bf16[256,2048]{1,0:T(8,128)(2,1)S(1)}, u32[]{:S(2)}, u32[]{:S(2)}) collective-permute-start(bf16[256,2048]{1,0:T(8,128)(2,1)} %bitcast.13), channel_id=1, source_target_pairs={{0,8},{8,0},{16,24},{24,16},{1,9},{9,1},{17,25},{25,17},{2,10},{10... | collective-permute-start | bytes 3145736 | tf_op jit(solution)/shard_map/ppermute | solution.py:367
  3.0 1.3 %copy-start.4 = (bf16[1,256,2048]{2,1,0:T(8,128)(2,1)S(1)}, bf16[1,256,2048]{2,1,0:T(8,128)(2,1)}, u32[]{:S(2)}) copy-start(bf16[1,256,2048]{2,1,0:T(8,128)(2,1)} %param.13) | copy-start | bytes 3145732
  5.1 10.9 %copy-start.9 = (bf16[256,1024]{1,0:T(8,128)(2,1)}, bf16[256,1024]{1,0:T(8,128)(2,1)S(1)}, u32[]{:S(2)}) copy-start(bf16[256,1024]{1,0:T(8,128)(2,1)S(1)} %get-tuple-element.21.refs_6_) | copy-start | bytes 1572868
  5.2 54.6 %collective-permute-start.1 = (bf16[256,1024]{1,0:T(8,128)(2,1)}, bf16[256,1024]{1,0:T(8,128)(2,1)}, u32[]{:S(2)}, u32[]{:S(2)}) collective-permute-start(bf16[256,1024]{1,0:T(8,128)(2,1)} %get-tuple-element.17.refs_2_), channel_id=1, source_target_pairs={{0,16},{8,24},{16,0},{24,8},{1,17},{9,25},{17,1},{25,9},{2,18},{10... | collective-permute-start | bytes 1572872 | tf_op jit(solution)/shard_map/ppermute | solution.py:367
  16.1 4.9 %copy-start.15 = (s32[4]{0:T(128)S(1)}, s32[4]{0:T(128)}, u32[]{:S(2)}) copy-start(s32[4]{0:T(128)} %constant.10.clone) | copy-start | bytes 52
  16.1 46.7 %all-to-all-start = ((bf16[8,128,1152]{2,1,0:T(8,128)(2,1)}), bf16[8,128,1152]{2,1,0:T(8,128)(2,1)S(1)}, u32[]{:S(2)}, u32[]{:S(2)}) async-start(bf16[8,128,1152]{2,1,0:T(8,128)(2,1)} %bitcast.16), calls=%async_computation | async-start | bytes 4718592 | tf_op jit(solution)/shard_map/all_to_all | solution.py:425
  19.9 38.0 %collective-permute-start.8 = (bf16[256,1024]{1,0:T(8,128)(2,1)}, bf16[256,1024]{1,0:T(8,128)(2,1)}, u32[]{:S(2)}, u32[]{:S(2)}) collective-permute-start(bf16[256,1024]{1,0:T(8,128)(2,1)} %copy-done.9), channel_id=1, source_target_pairs={{0,16},{8,24},{16,0},{24,8},{1,17},{9,25},{17,1},{25,9},{2,18},{10... | collective-permute-start | bytes 1572872 | tf_op jit(solution)/shard_map/ppermute | solution.py:367
  22.4 2.2 %copy-start = (bf16[1024,2048]{1,0:T(8,128)(2,1)S(1)}, bf16[1024,2048]{1,0:T(8,128)(2,1)}, u32[]{:S(2)}) copy-start(bf16[1024,2048]{1,0:T(8,128)(2,1)} %w_hbm.1) | copy-start | bytes 12582916
  24.6 1.2 %copy-start.5 = (bf16[512,1024]{1,0:T(8,128)(2,1)S(1)}, bf16[512,1024]{1,0:T(8,128)(2,1)}, u32[]{:S(2)}) copy-start(bf16[512,1024]{1,0:T(8,128)(2,1)} %x_ref.3) | copy-start | bytes 3145732
  25.8 1.4 %copy-start.14 = (s32[512,1]{0,1:T(1,128)S(1)}, s32[512,1]{0,1:T(1,128)}, u32[]{:S(2)}) copy-start(s32[512,1]{0,1:T(1,128)} %param.10) | copy-start | bytes 6148
  27.2 34.6 %copy-start.7 = (bf16[512,1024]{1,0:T(8,128)(2,1)}, bf16[512,1024]{1,0:T(8,128)(2,1)S(1)}, u32[]{:S(2)}) copy-start(bf16[512,1024]{1,0:T(8,128)(2,1)S(1)} %project_gate.1.refs_0_.gate_ref) | copy-start | bytes 3145732
  59.8 22.9 %collective-permute-start.9 = (bf16[128,1024]{1,0:T(8,128)(2,1)}, bf16[128,1024]{1,0:T(8,128)(2,1)}, u32[]{:S(2)}, u32[]{:S(2)}) collective-permute-start(bf16[128,1024]{1,0:T(8,128)(2,1)} %get-tuple-element.33), channel_id=1, source_target_pairs={{0,8},{8,0},{16,24},{24,16},{1,9},{9,1},{17,25},{25,17},{2,10},{10... | collective-permute-start | bytes 786440 | tf_op jit(solution)/shard_map/ppermute | solution.py:367
  59.8 19.3 %collective-permute-start.2 = (bf16[256,1024]{1,0:T(8,128)(2,1)}, bf16[256,1024]{1,0:T(8,128)(2,1)}, u32[]{:S(2)}, u32[]{:S(2)}) collective-permute-start(bf16[256,1024]{1,0:T(8,128)(2,1)} %collective-permute-done.1.refs_2_.refs_3_), channel_id=1, source_target_pairs={{0,8},{8,0},{16,24},{24,16},{1,9},{9,1},{17,25},{25,17},{2,10},{10... | collective-permute-start | bytes 1572872 | tf_op jit(solution)/shard_map/ppermute | solution.py:367
  62.1 0.7 copy-start.1
  62.8 1.0 copy-start.2
  69.7 13.0 %copy-start.13 = (bf16[128,1024]{1,0:T(8,128)(2,1)S(1)}, bf16[128,1024]{1,0:T(8,128)(2,1)}, u32[]{:S(2)}) copy-start(bf16[128,1024]{1,0:T(8,128)(2,1)} %get-tuple-element.22) | copy-start | bytes 786436
  82.5 5.4 %copy-start.10 = (bf16[256,1024]{1,0:T(8,128)(2,1)S(1)}, bf16[256,1024]{1,0:T(8,128)(2,1)}, u32[]{:S(2)}) copy-start(bf16[256,1024]{1,0:T(8,128)(2,1)} %copy-done.9) | copy-start | bytes 1572868
  82.6 1.6 %collective-permute-start.5 = (bf16[256,512]{1,0:T(8,128)(2,1)S(1)}, bf16[256,512]{1,0:T(8,128)(2,1)S(1)}, u32[]{:S(2)}, u32[]{:S(2)}) collective-permute-start(bf16[256,512]{1,0:T(8,128)(2,1)S(1)} %get-tuple-element.20), channel_id=1, source_target_pairs={{0,1},{1,0},{2,3},{3,2},{4,5},{5,4},{6,7},{7,6},{8,9},{9,8},{10,11... | collective-permute-start | bytes 786440 | tf_op jit(solution)/shard_map/ppermute | solution.py:367
  82.7 11.1 %collective-permute-start.10 = (bf16[128,1024]{1,0:T(8,128)(2,1)S(1)}, bf16[128,1024]{1,0:T(8,128)(2,1)S(1)}, u32[]{:S(2)}, u32[]{:S(2)}) collective-permute-start(bf16[128,1024]{1,0:T(8,128)(2,1)S(1)} %copy-done.13), channel_id=1, source_target_pairs={{0,8},{8,0},{16,24},{24,16},{1,9},{9,1},{17,25},{25,17},{2,10},{10... | collective-permute-start | bytes 786440 | tf_op jit(solution)/shard_map/ppermute | solution.py:367
  83.0 4.3 %collective-permute-start.3 = (bf16[256,512]{1,0:T(8,128)(2,1)S(1)}, bf16[256,512]{1,0:T(8,128)(2,1)S(1)}, u32[]{:S(2)}, u32[]{:S(2)}) collective-permute-start(bf16[256,512]{1,0:T(8,128)(2,1)S(1)} %get-tuple-element.19), channel_id=1, source_target_pairs={{0,1},{1,0},{2,3},{3,2},{4,5},{5,4},{6,7},{7,6},{8,9},{9,8},{10,11... | collective-permute-start | bytes 786440 | tf_op jit(solution)/shard_map/ppermute | solution.py:367
  84.2 13.5 %collective-permute-start.7 = (bf16[256,512]{1,0:T(8,128)(2,1)S(1)}, bf16[256,512]{1,0:T(8,128)(2,1)S(1)}, u32[]{:S(2)}, u32[]{:S(2)}) collective-permute-start(bf16[256,512]{1,0:T(8,128)(2,1)S(1)} %pad_maximum_fusion.2.refs_4_), channel_id=1, source_target_pairs={{0,6},{1,7},{2,4},{3,5},{4,2},{5,3},{6,0},{7,1},{8,14},{9,15},{10,... | collective-permute-start | bytes 786440 | tf_op jit(solution)/shard_map/ppermute | solution.py:367
  86.6 12.5 %collective-permute-start.6 = (bf16[256,512]{1,0:T(8,128)(2,1)S(1)}, bf16[256,512]{1,0:T(8,128)(2,1)S(1)}, u32[]{:S(2)}, u32[]{:S(2)}) collective-permute-start(bf16[256,512]{1,0:T(8,128)(2,1)S(1)} %pad_maximum_fusion.1.refs_3_), channel_id=1, source_target_pairs={{0,4},{1,5},{2,6},{3,7},{4,0},{5,1},{6,2},{7,3},{8,12},{9,13},{10,... | collective-permute-start | bytes 786440 | tf_op jit(solution)/shard_map/ppermute | solution.py:367
  87.3 11.9 %collective-permute-start.4 = (bf16[256,512]{1,0:T(8,128)(2,1)S(1)}, bf16[256,512]{1,0:T(8,128)(2,1)S(1)}, u32[]{:S(2)}, u32[]{:S(2)}) collective-permute-start(bf16[256,512]{1,0:T(8,128)(2,1)S(1)} %pad_maximum_fusion.refs_2_), channel_id=1, source_target_pairs={{0,2},{1,3},{2,0},{3,1},{4,6},{5,7},{6,4},{7,5},{8,10},{9,11},{10,... | collective-permute-start | bytes 786440 | tf_op jit(solution)/shard_map/ppermute | solution.py:367
  93.7 5.5 %copy-start.3 = (s32[512,128]{1,0:T(8,128)S(1)}, s32[512,128]{1,0:T(8,128)}, u32[]{:S(2)}) copy-start(s32[512,128]{1,0:T(8,128)} %copy-done.1) | copy-start | bytes 786436
  97.2 2.8 %collective-permute-start.11 = (bf16[256,512]{1,0:T(8,128)(2,1)S(1)}, bf16[256,512]{1,0:T(8,128)(2,1)S(1)}, u32[]{:S(2)}, u32[]{:S(2)}) collective-permute-start(bf16[256,512]{1,0:T(8,128)(2,1)S(1)} %get-tuple-element.24), channel_id=1, source_target_pairs={{0,1},{1,0},{2,3},{3,2},{4,5},{5,4},{6,7},{7,6},{8,9},{9,8},{10,11... | collective-permute-start | bytes 786440 | tf_op jit(solution)/shard_map/ppermute | solution.py:367
  97.2 2.7 %collective-permute-start.12 = (bf16[256,512]{1,0:T(8,128)(2,1)S(1)}, bf16[256,512]{1,0:T(8,128)(2,1)S(1)}, u32[]{:S(2)}, u32[]{:S(2)}) collective-permute-start(bf16[256,512]{1,0:T(8,128)(2,1)S(1)} %get-tuple-element.25), channel_id=1, source_target_pairs={{0,1},{1,0},{2,3},{3,2},{4,5},{5,4},{6,7},{7,6},{8,9},{9,8},{10,11... | collective-permute-start | bytes 786440 | tf_op jit(solution)/shard_map/ppermute | solution.py:367
  99.2 15.7 %copy-start.11 = (bf16[1024,1024]{1,0:T(8,128)(2,1)S(1)}, bf16[1024,1024]{1,0:T(8,128)(2,1)}, u32[]{:S(2)}) copy-start(bf16[1024,1024]{1,0:T(8,128)(2,1)} %w_ref.3) | copy-start | bytes 6291460
  99.9 15.0 %copy-start.6 = (bf16[512,1024]{1,0:T(8,128)(2,1)S(1)}, bf16[512,1024]{1,0:T(8,128)(2,1)}, u32[]{:S(2)}) copy-start(bf16[512,1024]{1,0:T(8,128)(2,1)} %x_ref.3) | copy-start | bytes 3145732
  99.9 15.0 %copy-start.8 = (bf16[512,1024]{1,0:T(8,128)(2,1)S(1)}, bf16[512,1024]{1,0:T(8,128)(2,1)}, u32[]{:S(2)}) copy-start(bf16[512,1024]{1,0:T(8,128)(2,1)} %copy-done.7) | copy-start | bytes 3145732
  99.9 15.0 %copy-start.12 = (f32[1024]{0:T(1024)S(1)}, f32[1024]{0:T(1024)}, u32[]{:S(2)}) copy-start(f32[1024]{0:T(1024)} %param.16) | copy-start | bytes 12292
  100.0 10.2 %collective-permute-start.15 = (bf16[256,512]{1,0:T(8,128)(2,1)S(1)}, bf16[256,512]{1,0:T(8,128)(2,1)S(1)}, u32[]{:S(2)}, u32[]{:S(2)}) collective-permute-start(bf16[256,512]{1,0:T(8,128)(2,1)S(1)} %pad_maximum_fusion.5), channel_id=1, source_target_pairs={{0,6},{1,7},{2,4},{3,5},{4,2},{5,3},{6,0},{7,1},{8,14},{9,15},{10,... | collective-permute-start | bytes 786440 | tf_op jit(solution)/shard_map/ppermute | solution.py:367
  101.9 12.9 %collective-permute-start.14 = (bf16[256,512]{1,0:T(8,128)(2,1)S(1)}, bf16[256,512]{1,0:T(8,128)(2,1)S(1)}, u32[]{:S(2)}, u32[]{:S(2)}) collective-permute-start(bf16[256,512]{1,0:T(8,128)(2,1)S(1)} %pad_maximum_fusion.4), channel_id=1, source_target_pairs={{0,4},{1,5},{2,6},{3,7},{4,0},{5,1},{6,2},{7,3},{8,12},{9,13},{10,... | collective-permute-start | bytes 786440 | tf_op jit(solution)/shard_map/ppermute | solution.py:367
  103.1 11.7 %collective-permute-start.13 = (bf16[256,512]{1,0:T(8,128)(2,1)S(1)}, bf16[256,512]{1,0:T(8,128)(2,1)S(1)}, u32[]{:S(2)}, u32[]{:S(2)}) collective-permute-start(bf16[256,512]{1,0:T(8,128)(2,1)S(1)} %pad_maximum_fusion.3), channel_id=1, source_target_pairs={{0,2},{1,3},{2,0},{3,1},{4,6},{5,7},{6,4},{7,5},{8,10},{9,11},{10,... | collective-permute-start | bytes 786440 | tf_op jit(solution)/shard_map/ppermute | solution.py:367

commit v8 on v7

--- a/solution.py
+++ b/solution.py
@@ -15,11 +15,12 @@
 F32 = jnp.float32
 BF16 = jnp.bfloat16
 MIB = 1024 * 1024
-WAIT_COST = 30.0
+TOKEN = jax.ShapeDtypeStruct((8, BLK), jnp.int32)
+WAIT_COST = 20.0
 LATE_SHARE = 20.0
 COLLECT_COST = 20.0
+SPLIT_COST = 6.0
 KERNEL_MIB = 24
-QUERY_MIB = 60
 
 
 def params(mib):
@@ -60,58 +61,57 @@
     return [pl.BlockSpec(memory_space=pl.ANY)] * len(arrays)
 
 
-def split_kernel(spans, size, kv_ref, *out_refs):
-    width = kv_ref.shape[1] // 2
+def split_kernel(spans, size, kv_hbm, *refs):
+    out_refs, sems = refs[:-1], refs[-1]
+    width = kv_hbm.shape[1] // 2
+    copies = []
     for (first, heads), ref in zip(spans, out_refs):
-        lo, hi = first * size, (first + heads) * size
-        ref[:, : hi - lo] = kv_ref[:, lo:hi]
-        ref[:, hi - lo :] = kv_ref[:, width + lo : width + hi]
+        wide = heads * size
+        for half in range(2):
+            source = kv_hbm.at[:, half * width + first * size : half * width + first * size + wide]
+            target = ref.at[:, half * wide : (half + 1) * wide]
+            copies.append(pltpu.make_async_copy(source, target, sems.at[len(copies)]))
+    for copy in copies:
+        copy.start()
+    for copy in copies:
+        copy.wait()
 
 
 def split(kv, spans, size):
     rows = kv.shape[0]
     return pl.pallas_call(
         functools.partial(split_kernel, spans, size),
-        in_specs=whole(),
+        in_specs=[pl.BlockSpec(memory_space=pl.ANY)],
         out_specs=whole(len(spans)),
         out_shape=[jax.ShapeDtypeStruct((rows, 2 * heads * size), BF16) for _, heads in spans],
-        compiler_params=params(KERNEL_MIB),
-        cost_estimate=cost(0, 4 * kv.size),
+        scratch_shapes=[pltpu.SemaphoreType.DMA((2 * len(spans),))],
+        compiler_params=params(KERNEL_MIB),
+        cost_estimate=cost(SPLIT_COST * 1e9, 4 * kv.size),
         name="split",
     )(kv)
 
 
-def query_kernel(columns, capacity, owner_ref, visible_ref, x_hbm, w_hbm, send_hbm, *scratch):
-    x_ref, w_ref, send_ref, x_sem, w_sems, out_sems = scratch
+def query_kernel(columns, capacity, owner_ref, visible_ref, x_ref, w_ref, send_hbm, send_ref, sems):
     rows, width = x_ref.shape
     slots = columns * capacity
-    tile = min(256, width)
-    spans = [slice(start, start + tile) for start in range(0, width, tile)]
-    x_load = pltpu.make_async_copy(x_hbm, x_ref, x_sem)
-    x_load.start()
-    w_loads = []
-    for number, span in enumerate(spans):
-        load = pltpu.make_async_copy(w_hbm.at[:, span], w_ref.at[:, span], w_sems.at[number])
-        load.start()
-        w_loads.append(load)
     slot = slot_row(owner_ref[...], columns, capacity).astype(jnp.int32)
     index = lax.broadcasted_iota(jnp.int32, (slots, rows), 0)
     place = (index == slot).astype(BF16)
-    seen = jnp.broadcast_to(visible_ref[...].astype(F32), (BLK, rows)).T.astype(BF16)
-    send_ref[:, width:] = jnp.dot(place, seen, preferred_element_type=F32).astype(BF16)
     stores = []
 
     def store(span):
         copy = pltpu.make_async_copy(
-            send_ref.at[:, span], send_hbm.at[:, span], out_sems.at[len(stores)]
+            send_ref.at[:, span], send_hbm.at[:, span], sems.at[len(stores)]
         )
         copy.start()
         stores.append(copy)
 
+    seen = jnp.broadcast_to(visible_ref[...].astype(F32), (BLK, rows)).T.astype(BF16)
+    send_ref[:, width:] = jnp.dot(place, seen, preferred_element_type=F32).astype(BF16)
     store(slice(width, width + BLK))
-    x_load.wait()
-    for number, span in enumerate(spans):
-        w_loads[number].wait()
+    tile = min(256, width)
+    for start in range(0, width, tile):
+        span = slice(start, start + tile)
         hidden = jnp.dot(x_ref[...], w_ref[:, span], preferred_element_type=F32)
         moved = jnp.dot(place, silu(hidden).astype(BF16), preferred_element_type=F32)
         send_ref[:, span] = moved.astype(BF16)
@@ -123,22 +123,16 @@
 def project_queries(owner_row, visible_row, cand_x, w_in, columns, capacity):
     rows, width = cand_x.shape
     slots = columns * capacity
-    count = width // min(256, width)
-    anywhere = pl.BlockSpec(memory_space=pl.ANY)
     return pl.pallas_call(
         functools.partial(query_kernel, columns, capacity),
-        in_specs=whole(2) + [anywhere, anywhere],
-        out_specs=anywhere,
+        in_specs=whole(4),
+        out_specs=pl.BlockSpec(memory_space=pltpu.HBM),
         out_shape=jax.ShapeDtypeStruct((slots, width + BLK), BF16),
         scratch_shapes=[
-            pltpu.VMEM((rows, width), BF16),
-            pltpu.VMEM((width, width), BF16),
             pltpu.VMEM((slots, width + BLK), BF16),
-            pltpu.SemaphoreType.DMA,
-            pltpu.SemaphoreType.DMA((count,)),
-            pltpu.SemaphoreType.DMA((count + 1,)),
+            pltpu.SemaphoreType.DMA((width // min(256, width) + 1,)),
         ],
-        compiler_params=params(QUERY_MIB),
+        compiler_params=params(KERNEL_MIB),
         cost_estimate=cost(
             2 * rows * width * width + 2 * slots * rows * width,
             2 * (rows * width + width * width + slots * width),
@@ -148,7 +142,8 @@
     )(owner_row, visible_row, cand_x, w_in)
 
 
-def gate_kernel(x_ref, w_ref, gate_ref):
+def gate_kernel(x_ref, w_ref, gate_ref, token_ref):
+    token_ref[...] = jnp.zeros_like(token_ref)
     width = x_ref.shape[1]
     tile = min(256, width)
     for start in range(0, width, tile):
@@ -162,8 +157,8 @@
     return pl.pallas_call(
         gate_kernel,
         in_specs=whole(2),
-        out_specs=whole()[0],
-        out_shape=jax.ShapeDtypeStruct((rows, width), BF16),
+        out_specs=whole(2),
+        out_shape=[jax.ShapeDtypeStruct((rows, width), BF16), TOKEN],
         compiler_params=params(KERNEL_MIB),
         cost_estimate=cost(
             2 * rows * width * width, 2 * (2 * rows * width + width * width), rows * width
@@ -173,8 +168,9 @@
 
 
 def slots_kernel(columns, capacity, owner_ref, *refs):
+    refs[-1][...] = jnp.zeros_like(refs[-1])
     slot = slot_row(owner_ref[...], columns, capacity)
-    refs[-1][...] = jnp.broadcast_to(slot, (BLK, slot.shape[1])).T.astype(jnp.int32)
+    refs[-2][...] = jnp.broadcast_to(slot, (BLK, slot.shape[1])).T.astype(jnp.int32)
 
 
 def slot_column(owner_row, columns, capacity, after):
@@ -182,8 +178,8 @@
     return pl.pallas_call(
         functools.partial(slots_kernel, columns, capacity),
         in_specs=whole() + unread(after),
-        out_specs=whole()[0],
-        out_shape=jax.ShapeDtypeStruct((rows, BLK), jnp.int32),
+        out_specs=whole(2),
+        out_shape=[jax.ShapeDtypeStruct((rows, BLK), jnp.int32), TOKEN],
         compiler_params=params(KERNEL_MIB),
         cost_estimate=cost(WAIT_COST * 1e9, 4 * rows * BLK),
         name="slot_column",
@@ -215,12 +211,12 @@
     tile = min(512, slots)
 
     def columns(start):
-        return pl.ds(pl.multiple_of(start, size), size)
+        return slice(start, start + size)
 
     def read(part, start):
         return jnp.concatenate([piece[:, columns(start)] for piece in part], axis=0)
 
-    def one_head(head, carry):
+    def one_head(head):
         values = []
         for number, part in enumerate(parts):
             inside = row + place_ref[2 + number] * keys < place_ref[0]
@@ -248,9 +244,9 @@
             if has_base:
                 total = total + base_ref[span, columns(head * size)]
             result[span, columns(head * size)] = total.astype(result.dtype)
-        return carry
-
-    lax.fori_loop(0, heads, one_head, 0)
+
+    for head in range(heads):
+        one_head(head)
     if outs > 1:
         numbers = list(range(0, columns_of, 2)) + list(range(1, columns_of, 2))
         for ref in out_refs:
@@ -367,15 +363,6 @@
     return lax.ppermute(array, axis, [(i, i ^ bits) for i in range(count)])
 
 
-def forward(piece, number, count):
-    if number == 0:
-        return [swap(piece, "user", 1, count)]
-    half = piece.shape[0] // 2
-    upper = swap(piece[:half], "user", 1, count)
-    lower, _ = lax.optimization_barrier((piece[half:], upper))
-    return [upper, swap(lower, "user", 1, count)]
-
-
 def exchange_cores(even, odds, capacity, count, behind):
     others = [swap(odd, "cand", 1, count) for odd in odds]
     if behind is not None:
@@ -425,30 +412,49 @@
     got = lax.all_to_all(
         send.reshape(columns, capacity, -1), "cand", split_axis=0, concat_axis=0, tiled=True
     ).reshape(slots, -1)
-    gate = project_gate(cand_x, w_in)
-    arrived = [near] + [far[0][key] for key in evens[1:]]
-    slot = slot_column(owner_row ^ me, columns, capacity, [gate] + arrived)
+    gate, gated = project_gate(cand_x, w_in)
+    arrived = [near] + [held[key] for held in far for key in evens[1:]]
+    slot, started = slot_column(owner_row ^ me, columns, capacity, [gated] + arrived)
     position = lax.axis_index("user").astype(jnp.int32)
     shards = position ^ jnp.array(evens + [1] + late, jnp.int32)
     head = jnp.concatenate([hist_len, me[None]])
     place_ready = jnp.concatenate([head, shards[: len(evens) + 1]])
     place_late = jnp.concatenate([head, shards[len(evens) + 1 :]])
 
-    early = []
-    after = [slot]
+    bases = []
+    cuts = []
     for number, (first, heads) in enumerate(spans):
         held = far[number]
-        cuts = [(forward(held[key], number, count), 0, heads) for key in evens[1:]]
         segments = [([held[key]], 0, heads) for key in evens]
         segments.append(([near], first, HEADS + first))
         base = attend(
-            place_ready, after, got, segments, None, first, heads, size, None, F32, 0.0
+            place_ready, [started] + bases, got, segments, None, first, heads, size, None, F32, 0.0
         )[0]
+        passed = [held[key] for key in evens[1:]]
+        if number:
+            passed, _ = lax.optimization_barrier((passed, bases[-1]))
+        cuts.append([([swap(part, "user", 1, count)], 0, heads) for part in passed])
+        bases.append(base)
+    early = []
+    after = []
+    for number, (first, heads) in enumerate(spans):
         attn = attend(
-            place_late, [], got, cuts, base, first, heads, size, capacity, BF16, LATE_SHARE * (number > 0)
+            place_late,
+            after,
+            got,
+            cuts[number],
+            bases[number],
+            first,
+            heads,
+            size,
+            capacity,
+            BF16,
+            LATE_SHARE * (number > 0),
         )
-        here, pairs = exchange_cores(attn[0], attn[1:], capacity, columns, early[-1] if early else None)
-        after = [slot, attn[0]] + pairs
+        here, pairs = exchange_cores(
+            attn[0], attn[1:], capacity, columns, early[-1] if early else None
+        )
+        after = [attn[0]] + pairs
         returned = here + exchange_chips(pairs, columns)
         if number + 1 < len(spans):
             early.append(collect(slot, returned, capacity, slots))

time: 119 us -> 103 us (0.87)
  waiting for transfers between devices: 53.5 us -> 41.6 us
  Pallas kernels: 33.2 us -> 26.9 us
  starting transfers between devices: 20.4 us -> 23.8 us
    ppermute x16 -> x15, waiting for transfers between devices: 53.5 us -> 41.6 us  [swap(): return lax.ppermute(array, axis, [(i, i ^ bits) for i in range(count)])]
    pallas_call x4, Pallas kernels: 18.5 us -> 14.2 us  [attend(): pl.pallas_call(functools.partial(attend_kernel, size, heads, first, start...]
    ppermute x16 -> x15, starting transfers between devices: 16.6 us -> 19.9 us  [swap(): return lax.ppermute(array, axis, [(i, i ^ bits) for i in range(count)])]
    pallas_call x1, Pallas kernels: 8.32 us -> 6.1 us  [project_queries(): pl.pallas_call(functools.partial(query_kernel, columns, capacity), in_spe...]
    slice x1 -> x0, local copies, waits for them, and re-layouts: 1.87 us -> none  [forward(): lower, _ = lax.optimization_barrier((piece[half:], upper))]
    unnamed x32, local copies, waits for them, and re-layouts: 6.37 us -> 7.79 us
  transfers between devices with their start and end apart: 17 -> 16, of which waited for: 6 -> 7; matrix products, arithmetic and copies ran while one was open for 3% -> 1% of each run, Pallas kernels for 26% -> 21%
where the time goes in v8:
time: 103 us
  waiting for transfers between devices  41.6 us (40%)
  Pallas kernels  26.9 us (26%)
  starting transfers between devices  23.8 us (23%)
  local copies, waits for them, and re-layouts  8.52 us (8%)
  between operations  1.15 us (1%)
    ppermute x15, waiting for transfers between devices, swap(): return lax.ppermute(array, axis, [(i, i ^ bits) for i in range(count)])  41.6 us
    ppermute x15, starting transfers between devices, swap(): return lax.ppermute(array, axis, [(i, i ^ bits) for i in range(count)])  19.9 us
    pallas_call x4, Pallas kernels, attend(): pl.pallas_call(functools.partial(attend_kernel, size, heads, first, start...  14.2 us
    unnamed x32, local copies, waits for them, and re-layouts  7.79 us
    pallas_call x1, Pallas kernels, project_queries(): pl.pallas_call(functools.partial(query_kernel, columns, capacity), in_spe...  6.1 us
    all_to_all x1, starting transfers between devices, per_device(): lax.all_to_all(send.reshape(columns, capacity, -1), 'cand', split_axis=0,...  3.93 us
    pallas_call x1, Pallas kernels, finish(): pl.pallas_call(functools.partial(finish_kernel, len(early), capacity, slo...  3.09 us
  transfers between devices with their start and end apart: 16, of which 7 were waited for; matrix products, arithmetic and copies ran while one was open for 1% of the time, Pallas kernels for 21%

profile of v8, /device:TPU:0, one launch (start us, length us, event | category | flops | bytes accessed | tf_op | source)
XLA Modules:
  0.0 102.9 jit_solution(7777124919016961425)
XLA Ops:
  0.0 3.1 %collective-permute-start = (bf16[256,2048]{1,0:T(8,128)(2,1)}, bf16[256,2048]{1,0:T(8,128)(2,1)S(1)}, u32[]{:S(2)}, u32[]{:S(2)}) collective-permute-start(bf16[256,2048]{1,0:T(8,128)(2,1)} %bitcast.15), channel_id=1, source_target_pairs={{0,8},{8,0},{16,24},{24,16},{1,9},{9,1},{17,25},{25,17},{2,10},{10... | collective-permute-start | bytes 3145736 | tf_op jit(solution)/shard_map/ppermute | solution.py:363
  3.1 1.3 %copy-done.8 = bf16[1,256,2048]{2,1,0:T(8,128)(2,1)S(1)} copy-done((bf16[1,256,2048]{2,1,0:T(8,128)(2,1)S(1)}, bf16[1,256,2048]{2,1,0:T(8,128)(2,1)}, u32[]{:S(2)}) %copy-start.8) | copy-done | bytes 1048600
  4.4 1.1 %split.1 = (bf16[256,1024]{1,0:T(8,128)(2,1)}, bf16[256,1024]{1,0:T(8,128)(2,1)}) custom-call(bf16[256,2048]{1,0:T(8,128)(2,1)S(1)} %bitcast.16), custom_call_target="tpu_custom_call" | custom-call | flops 6000000000 | bytes 2097152 | tf_op jit(solution)/shard_map/split/pallas_call | solution.py:82
  5.5 2.7 %collective-permute-start.1 = (bf16[256,1024]{1,0:T(8,128)(2,1)}, bf16[256,1024]{1,0:T(8,128)(2,1)}, u32[]{:S(2)}, u32[]{:S(2)}) collective-permute-start(bf16[256,1024]{1,0:T(8,128)(2,1)} %get-tuple-element.22.refs_2_), channel_id=1, source_target_pairs={{0,16},{8,24},{16,0},{24,8},{1,17},{9,25},{17,1},{25,9},{2,18},{10... | collective-permute-start | bytes 1572872 | tf_op jit(solution)/shard_map/ppermute | solution.py:363
  8.1 0.3 collective-permute-start.2
  8.4 0.0 copy-done
  8.5 0.0 copy-done.3
  8.5 0.0 copy-done.6
  8.5 0.0 copy-done.12
  8.5 6.1 %project_queries.1 = bf16[1024,1152]{1,0:T(8,128)(2,1)S(1)} custom-call(s32[1,512]{1,0:T(1,128)S(1)} %bitcast.14, s32[1,512]{1,0:T(1,128)S(1)} %bitcast.18, bf16[512,1024]{1,0:T(8,128)(2,1)S(1)} %copy-done.3, bf16[1024,2048]{1,0:T(8,128)(2,1)S(1)} %copy-done), custom_call_target="tpu_custom_call" | custom-call | flops 2147483648 | bytes 5242880 | tf_op jit(solution)/shard_map/project_queries/pallas_call | solution.py:126
  14.6 0.0 copy-start.2
  14.6 1.4 %copy-done.2 = bf16[1024,1152]{1,0:T(8,128)(2,1)} copy-done((bf16[1024,1152]{1,0:T(8,128)(2,1)}, bf16[1024,1152]{1,0:T(8,128)(2,1)S(1)}, u32[]{:S(2)}) %copy-start.2) | copy-done | bytes 2359320
  16.0 3.9 %all-to-all-start = ((bf16[8,128,1152]{2,1,0:T(8,128)(2,1)}), bf16[8,128,1152]{2,1,0:T(8,128)(2,1)S(1)}, u32[]{:S(2)}, u32[]{:S(2)}) async-start(bf16[8,128,1152]{2,1,0:T(8,128)(2,1)} %bitcast.13), calls=%async_computation | async-start | bytes 4718592 | tf_op jit(solution)/shard_map/all_to_all | solution.py:412
  20.6 0.0 copy-done.15
  20.6 0.6 slice.42
  21.2 2.2 %copy-done.1 = bf16[1024,2048]{1,0:T(8,128)(2,1)S(1)} copy-done((bf16[1024,2048]{1,0:T(8,128)(2,1)S(1)}, bf16[1024,2048]{1,0:T(8,128)(2,1)}, u32[]{:S(2)}) %copy-start.1) | copy-done | bytes 4194328
  23.4 1.2 %copy-done.4 = bf16[512,1024]{1,0:T(8,128)(2,1)S(1)} copy-done((bf16[512,1024]{1,0:T(8,128)(2,1)S(1)}, bf16[512,1024]{1,0:T(8,128)(2,1)}, u32[]{:S(2)}) %copy-start.4) | copy-done | bytes 1048600
  24.6 1.4 %project_gate.1 = (bf16[512,1024]{1,0:T(8,128)(2,1)S(1)}, s32[8,128]{1,0:T(8,128)S(1)}) custom-call(bf16[512,1024]{1,0:T(8,128)(2,1)S(1)} %copy-done.4, bf16[1024,2048]{1,0:T(8,128)(2,1)S(1)} %copy-done.1), custom_call_target="tpu_custom_call" | custom-call | flops 1073741824 | bytes 4194304 | tf_op jit(solution)/shard_map/project_gate/pallas_call | solution.py:157
  26.0 0.0 copy-start.9
  26.0 1.0 copy-done.9
  27.0 0.7 pad_add_fusion.place_ref
  27.7 0.1 pad_add_fusion.1.place_ref
  27.8 10.5 %collective-permute-done.1.refs_2_.refs_3_ = bf16[256,1024]{1,0:T(8,128)(2,1)} collective-permute-done((bf16[256,1024]{1,0:T(8,128)(2,1)}, bf16[256,1024]{1,0:T(8,128)(2,1)}, u32[]{:S(2)}, u32[]{:S(2)}) %collective-permute-start.1) | collective-permute-done | bytes 524320 | tf_op jit(solution)/shard_map/ppermute | solution.py:363
  38.3 3.6 %collective-permute-start.3 = (bf16[256,1024]{1,0:T(8,128)(2,1)}, bf16[256,1024]{1,0:T(8,128)(2,1)}, u32[]{:S(2)}, u32[]{:S(2)}) collective-permute-start(bf16[256,1024]{1,0:T(8,128)(2,1)} %collective-permute-done.1.refs_2_.refs_3_), channel_id=1, source_target_pairs={{0,8},{8,0},{16,24},{24,16},{1,9},{9,1},{17,25},{25,17},{2,10},{10... | collective-permute-start | bytes 1572872 | tf_op jit(solution)/shard_map/ppermute | solution.py:363
  41.8 12.3 %collective-permute-done.2.refs_3_.refs_4_ = bf16[256,1024]{1,0:T(8,128)(2,1)} collective-permute-done((bf16[256,1024]{1,0:T(8,128)(2,1)}, bf16[256,1024]{1,0:T(8,128)(2,1)}, u32[]{:S(2)}, u32[]{:S(2)}) %collective-permute-start.2) | collective-permute-done | bytes 524320 | tf_op jit(solution)/shard_map/ppermute | solution.py:363
  54.1 0.0 collective-permute-done.refs_1_.refs_4_.refs_5_
  54.1 0.3 slot_column.1
  54.4 0.0 copy-start.13
  54.5 0.7 copy-done.13
  55.2 0.0 all-to-all-done
  55.2 4.8 %attend.4.refs_2_.refs_1_ = f32[1024,512]{1,0:T(8,128)S(1)} custom-call(s32[5]{0:T(128)S(1)} %pad_add_fusion.1.place_ref, s32[8,128]{1,0:T(8,128)S(1)} %get-tuple-element.26.refs_0_, bf16[1024,1152]{1,0:T(8,128)(2,1)S(1)} %bitcast.9, bf16[256,1024]{1,0:T(8,128)(2,1)} %get-tuple-element.22.refs_2_, bf16[256,1024]{1,0:T(8,128)(2,1)} %collective-permute-done.1.refs_2_.refs_3_, ...), custom_call_target="tpu_custom_call" | custom-call | bytes 3670016 | tf_op jit(solution)/shard_map/attend/pallas_call | solution.py:271
  59.9 0.4 collective-permute-done.3.refs_1_
  60.3 2.5 %attend.5 = (bf16[512,512]{1,0:T(8,128)(2,1)S(1)}, bf16[256,512]{1,0:T(8,128)(2,1)S(1)}, bf16[256,512]{1,0:T(8,128)(2,1)S(1)}) custom-call(s32[3]{0:T(128)S(1)} %pad_add_fusion.place_ref, bf16[1024,1152]{1,0:T(8,128)(2,1)S(1)} %bitcast.10, bf16[256,1024]{1,0:T(8,128)(2,1)} %collective-permute-done.3.refs_1_, f32[1024,512]{1,0:T(8,128)S(1)} %attend.4.refs_2_.refs_1_), custom_call_target="tpu_custom_call" | custom-call | bytes 2621440 | tf_op jit(solution)/shard_map/attend/pallas_call | solution.py:271
  62.8 0.1 collective-permute-start.4
  62.9 0.5 collective-permute-start.6
  63.4 1.8 %collective-permute-start.9 = (bf16[256,1024]{1,0:T(8,128)(2,1)}, bf16[256,1024]{1,0:T(8,128)(2,1)S(1)}, u32[]{:S(2)}, u32[]{:S(2)}) collective-permute-start(bf16[256,1024]{1,0:T(8,128)(2,1)} %collective-permute-done.2.refs_3_.refs_4_), channel_id=1, source_target_pairs={{0,8},{8,0},{16,24},{24,16},{1,9},{9,1},{17,25},{25,17},{2,10},{10... | collective-permute-start | bytes 1572872 | tf_op jit(solution)/shard_map/ppermute | solution.py:363
  65.1 4.8 %attend.6.refs_6_ = f32[1024,512]{1,0:T(8,128)S(1)} custom-call(s32[5]{0:T(128)S(1)} %pad_add_fusion.1.place_ref, s32[8,128]{1,0:T(8,128)S(1)} %get-tuple-element.26.refs_0_, f32[1024,512]{1,0:T(8,128)S(1)} %attend.4.refs_2_.refs_1_, bf16[1024,1152]{1,0:T(8,128)(2,1)S(1)} %bitcast.11, bf16[256,1024]{1,0:T(8,128)(2,1)} %get-tuple-element.23.refs_3_, ...), custom_call_target="tpu_custom_call" | custom-call | bytes 3670016 | tf_op jit(solution)/shard_map/attend/pallas_call | solution.py:271
  69.9 0.0 collective-permute-done.4.refs_1_
  70.0 1.6 %collective-permute-start.5 = (bf16[256,512]{1,0:T(8,128)(2,1)S(1)}, bf16[256,512]{1,0:T(8,128)(2,1)S(1)}, u32[]{:S(2)}, u32[]{:S(2)}) collective-permute-start(bf16[256,512]{1,0:T(8,128)(2,1)S(1)} %pad_maximum_fusion.refs_1_), channel_id=1, source_target_pairs={{0,2},{1,3},{2,0},{3,1},{4,6},{5,7},{6,4},{7,5},{8,10},{9,11},{10,... | collective-permute-start | bytes 786440 | tf_op jit(solution)/shard_map/ppermute | solution.py:363
  71.6 0.0 collective-permute-done.6
  71.6 1.6 %collective-permute-start.7 = (bf16[256,512]{1,0:T(8,128)(2,1)S(1)}, bf16[256,512]{1,0:T(8,128)(2,1)S(1)}, u32[]{:S(2)}, u32[]{:S(2)}) collective-permute-start(bf16[256,512]{1,0:T(8,128)(2,1)S(1)} %pad_maximum_fusion.1.refs_2_), channel_id=1, source_target_pairs={{0,4},{1,5},{2,6},{3,7},{4,0},{5,1},{6,2},{7,3},{8,12},{9,13},{10,... | collective-permute-start | bytes 786440 | tf_op jit(solution)/shard_map/ppermute | solution.py:363
  73.2 0.0 copy-start.14
  73.2 0.5 collective-permute-start.8
  73.8 3.7 %collective-permute-done.9.refs_5_ = bf16[256,1024]{1,0:T(8,128)(2,1)S(1)} collective-permute-done((bf16[256,1024]{1,0:T(8,128)(2,1)}, bf16[256,1024]{1,0:T(8,128)(2,1)S(1)}, u32[]{:S(2)}, u32[]{:S(2)}) %collective-permute-start.9) | collective-permute-done | bytes 524320 | tf_op jit(solution)/shard_map/ppermute | solution.py:363
  77.5 2.2 %attend.7 = (bf16[512,512]{1,0:T(8,128)(2,1)S(1)}, bf16[256,512]{1,0:T(8,128)(2,1)S(1)}, bf16[256,512]{1,0:T(8,128)(2,1)S(1)}) custom-call(s32[3]{0:T(128)S(1)} %pad_add_fusion.place_ref, bf16[512,512]{1,0:T(8,128)(2,1)S(1)} %get-tuple-element.27.refs_0_, bf16[256,512]{1,0:T(8,128)(2,1)S(1)} %pad_maximum_fusion.refs_1_, ...), custom_call_target="tpu_custom_call" | custom-call | flops 10737418240 | bytes 2621440 | tf_op jit(solution)/shard_map/attend/pallas_call | solution.py:271
  79.7 0.1 collective-permute-start.10
  79.8 0.5 collective-permute-start.11
  80.3 0.0 collective-permute-done.5.refs_2_
  80.3 4.7 %collective-permute-done.7.refs_3_ = bf16[256,512]{1,0:T(8,128)(2,1)S(1)} collective-permute-done((bf16[256,512]{1,0:T(8,128)(2,1)S(1)}, bf16[256,512]{1,0:T(8,128)(2,1)S(1)}, u32[]{:S(2)}, u32[]{:S(2)}) %collective-permute-start.7) | collective-permute-done | bytes 262176 | tf_op jit(solution)/shard_map/ppermute | solution.py:363
  85.0 0.0 collective-permute-done.8.refs_4_
  85.0 0.0 copy-done.14
  85.0 0.7 collect.1.refs_0_
  85.8 0.0 copy-start.5
  85.8 0.0 copy-start.7
  85.8 0.0 copy-start.11
  85.8 0.0 collective-permute-done.10.refs_2_
  85.8 0.0 collective-permute-done.11
  85.9 1.2 %collective-permute-start.12 = (bf16[256,512]{1,0:T(8,128)(2,1)S(1)}, bf16[256,512]{1,0:T(8,128)(2,1)S(1)}, u32[]{:S(2)}, u32[]{:S(2)}) collective-permute-start(bf16[256,512]{1,0:T(8,128)(2,1)S(1)} %pad_maximum_fusion.3), channel_id=1, source_target_pairs={{0,2},{1,3},{2,0},{3,1},{4,6},{5,7},{6,4},{7,5},{8,10},{9,11},{10,... | collective-permute-start | bytes 786440 | tf_op jit(solution)/shard_map/ppermute | solution.py:363
  87.1 1.0 collective-permute-start.13
  88.1 1.5 %collective-permute-start.14 = (bf16[256,512]{1,0:T(8,128)(2,1)S(1)}, bf16[256,512]{1,0:T(8,128)(2,1)S(1)}, u32[]{:S(2)}, u32[]{:S(2)}) collective-permute-start(bf16[256,512]{1,0:T(8,128)(2,1)S(1)} %pad_maximum_fusion.5), channel_id=1, source_target_pairs={{0,6},{1,7},{2,4},{3,5},{4,2},{5,3},{6,0},{7,1},{8,14},{9,15},{10,... | collective-permute-start | bytes 786440 | tf_op jit(solution)/shard_map/ppermute | solution.py:363
  89.6 5.6 %collective-permute-done.12.refs_3_ = bf16[256,512]{1,0:T(8,128)(2,1)S(1)} collective-permute-done((bf16[256,512]{1,0:T(8,128)(2,1)S(1)}, bf16[256,512]{1,0:T(8,128)(2,1)S(1)}, u32[]{:S(2)}, u32[]{:S(2)}) %collective-permute-start.12) | collective-permute-done | bytes 262176 | tf_op jit(solution)/shard_map/ppermute | solution.py:363
  95.2 4.4 %collective-permute-done.13.refs_4_ = bf16[256,512]{1,0:T(8,128)(2,1)S(1)} collective-permute-done((bf16[256,512]{1,0:T(8,128)(2,1)S(1)}, bf16[256,512]{1,0:T(8,128)(2,1)S(1)}, u32[]{:S(2)}, u32[]{:S(2)}) %collective-permute-start.13) | collective-permute-done | bytes 262176 | tf_op jit(solution)/shard_map/ppermute | solution.py:363
  99.6 0.0 collective-permute-done.14.refs_5_
  99.7 3.1 %finish.1 = bf16[512,1024]{1,0:T(8,128)(2,1)} custom-call(s32[512,128]{1,0:T(8,128)S(1)} %copy-done.14, f32[1,1024]{1,0:T(1,128)S(1)} %bitcast.17, bf16[512,1024]{1,0:T(8,128)(2,1)S(1)} %copy-done.10, bf16[512,1024]{1,0:T(8,128)(2,1)S(1)} %copy-done.5, bf16[1024,1024]{1,0:T(8,128)(2,1)S(1)} %copy-done.7, bf16[512,512]{1,0:T(8,128)(2,1)S(1)} %collect.1.refs_0_, ...), custom_call_target="tpu_custom_call" | custom-call | flops 2147483648 | bytes 7340032 | tf_op jit(solution)/shard_map/finish/pallas_call | solution.py:348
  (27 shorter events, 0.3 us)
Async XLA Ops:
  0.0 8.4 %copy-start = (bf16[1024,2048]{1,0:T(8,128)(2,1)S(1)}, bf16[1024,2048]{1,0:T(8,128)(2,1)}, u32[]{:S(2)}) copy-start(bf16[1024,2048]{1,0:T(8,128)(2,1)} %w_ref.4) | copy-start | bytes 12582916
  0.0 8.5 %copy-start.3 = (bf16[512,1024]{1,0:T(8,128)(2,1)S(1)}, bf16[512,1024]{1,0:T(8,128)(2,1)}, u32[]{:S(2)}) copy-start(bf16[512,1024]{1,0:T(8,128)(2,1)} %x_ref.5) | copy-start | bytes 3145732
  0.0 8.5 %copy-start.6 = (s32[512,1]{0,1:T(1,128)S(1)}, s32[512,1]{0,1:T(1,128)}, u32[]{:S(2)}) copy-start(s32[512,1]{0,1:T(1,128)} %param.10) | copy-start | bytes 6148
  0.0 54.1 %collective-permute-start = (bf16[256,2048]{1,0:T(8,128)(2,1)}, bf16[256,2048]{1,0:T(8,128)(2,1)S(1)}, u32[]{:S(2)}, u32[]{:S(2)}) collective-permute-start(bf16[256,2048]{1,0:T(8,128)(2,1)} %bitcast.15), channel_id=1, source_target_pairs={{0,8},{8,0},{16,24},{24,16},{1,9},{9,1},{17,25},{25,17},{2,10},{10... | collective-permute-start | bytes 3145736 | tf_op jit(solution)/shard_map/ppermute | solution.py:363
  3.1 1.3 %copy-start.8 = (bf16[1,256,2048]{2,1,0:T(8,128)(2,1)S(1)}, bf16[1,256,2048]{2,1,0:T(8,128)(2,1)}, u32[]{:S(2)}) copy-start(bf16[1,256,2048]{2,1,0:T(8,128)(2,1)} %param.13) | copy-start | bytes 3145732
  4.4 4.1 %copy-start.12 = (s32[512]{0:T(512)S(1)}, s32[512]{0:T(512)}, u32[]{:S(2)}) copy-start(s32[512]{0:T(512)} %param.11) | copy-start | bytes 6148
  5.5 32.8 %collective-permute-start.1 = (bf16[256,1024]{1,0:T(8,128)(2,1)}, bf16[256,1024]{1,0:T(8,128)(2,1)}, u32[]{:S(2)}, u32[]{:S(2)}) collective-permute-start(bf16[256,1024]{1,0:T(8,128)(2,1)} %get-tuple-element.22.refs_2_), channel_id=1, source_target_pairs={{0,16},{8,24},{16,0},{24,8},{1,17},{9,25},{17,1},{25,9},{2,18},{10... | collective-permute-start | bytes 1572872 | tf_op jit(solution)/shard_map/ppermute | solution.py:363
  8.1 46.0 %collective-permute-start.2 = (bf16[256,1024]{1,0:T(8,128)(2,1)}, bf16[256,1024]{1,0:T(8,128)(2,1)}, u32[]{:S(2)}, u32[]{:S(2)}) collective-permute-start(bf16[256,1024]{1,0:T(8,128)(2,1)} %get-tuple-element.23.refs_3_), channel_id=1, source_target_pairs={{0,16},{8,24},{16,0},{24,8},{1,17},{9,25},{17,1},{25,9},{2,18},{10... | collective-permute-start | bytes 1572872 | tf_op jit(solution)/shard_map/ppermute | solution.py:363
  14.6 1.4 %copy-start.2 = (bf16[1024,1152]{1,0:T(8,128)(2,1)}, bf16[1024,1152]{1,0:T(8,128)(2,1)S(1)}, u32[]{:S(2)}) copy-start(bf16[1024,1152]{1,0:T(8,128)(2,1)S(1)} %project_queries.1) | copy-start | bytes 7077892
  16.0 4.6 %copy-start.15 = (s32[4]{0:T(128)S(1)}, s32[4]{0:T(128)}, u32[]{:S(2)}) copy-start(s32[4]{0:T(128)} %constant.10.clone) | copy-start | bytes 52
  16.0 39.2 %all-to-all-start = ((bf16[8,128,1152]{2,1,0:T(8,128)(2,1)}), bf16[8,128,1152]{2,1,0:T(8,128)(2,1)S(1)}, u32[]{:S(2)}, u32[]{:S(2)}) async-start(bf16[8,128,1152]{2,1,0:T(8,128)(2,1)} %bitcast.13), calls=%async_computation | async-start | bytes 4718592 | tf_op jit(solution)/shard_map/all_to_all | solution.py:412
  21.2 2.2 %copy-start.1 = (bf16[1024,2048]{1,0:T(8,128)(2,1)S(1)}, bf16[1024,2048]{1,0:T(8,128)(2,1)}, u32[]{:S(2)}) copy-start(bf16[1024,2048]{1,0:T(8,128)(2,1)} %w_ref.4) | copy-start | bytes 12582916
  23.4 1.2 %copy-start.4 = (bf16[512,1024]{1,0:T(8,128)(2,1)S(1)}, bf16[512,1024]{1,0:T(8,128)(2,1)}, u32[]{:S(2)}) copy-start(bf16[512,1024]{1,0:T(8,128)(2,1)} %x_ref.5) | copy-start | bytes 3145732
  26.0 1.0 copy-start.9
  38.3 22.0 %collective-permute-start.3 = (bf16[256,1024]{1,0:T(8,128)(2,1)}, bf16[256,1024]{1,0:T(8,128)(2,1)}, u32[]{:S(2)}, u32[]{:S(2)}) collective-permute-start(bf16[256,1024]{1,0:T(8,128)(2,1)} %collective-permute-done.1.refs_2_.refs_3_), channel_id=1, source_target_pairs={{0,8},{8,0},{16,24},{24,16},{1,9},{9,1},{17,25},{25,17},{2,10},{10... | collective-permute-start | bytes 1572872 | tf_op jit(solution)/shard_map/ppermute | solution.py:363
  54.4 0.7 copy-start.13
  62.8 7.2 %collective-permute-start.4 = (bf16[256,512]{1,0:T(8,128)(2,1)S(1)}, bf16[256,512]{1,0:T(8,128)(2,1)S(1)}, u32[]{:S(2)}, u32[]{:S(2)}) collective-permute-start(bf16[256,512]{1,0:T(8,128)(2,1)S(1)} %get-tuple-element.28), channel_id=1, source_target_pairs={{0,1},{1,0},{2,3},{3,2},{4,5},{5,4},{6,7},{7,6},{8,9},{9,8},{10,11... | collective-permute-start | bytes 786440 | tf_op jit(solution)/shard_map/ppermute | solution.py:363
  62.9 8.7 %collective-permute-start.6 = (bf16[256,512]{1,0:T(8,128)(2,1)S(1)}, bf16[256,512]{1,0:T(8,128)(2,1)S(1)}, u32[]{:S(2)}, u32[]{:S(2)}) collective-permute-start(bf16[256,512]{1,0:T(8,128)(2,1)S(1)} %get-tuple-element.29), channel_id=1, source_target_pairs={{0,1},{1,0},{2,3},{3,2},{4,5},{5,4},{6,7},{7,6},{8,9},{9,8},{10,11... | collective-permute-start | bytes 786440 | tf_op jit(solution)/shard_map/ppermute | solution.py:363
  63.4 14.2 %collective-permute-start.9 = (bf16[256,1024]{1,0:T(8,128)(2,1)}, bf16[256,1024]{1,0:T(8,128)(2,1)S(1)}, u32[]{:S(2)}, u32[]{:S(2)}) collective-permute-start(bf16[256,1024]{1,0:T(8,128)(2,1)} %collective-permute-done.2.refs_3_.refs_4_), channel_id=1, source_target_pairs={{0,8},{8,0},{16,24},{24,16},{1,9},{9,1},{17,25},{25,17},{2,10},{10... | collective-permute-start | bytes 1572872 | tf_op jit(solution)/shard_map/ppermute | solution.py:363
  70.0 10.3 %collective-permute-start.5 = (bf16[256,512]{1,0:T(8,128)(2,1)S(1)}, bf16[256,512]{1,0:T(8,128)(2,1)S(1)}, u32[]{:S(2)}, u32[]{:S(2)}) collective-permute-start(bf16[256,512]{1,0:T(8,128)(2,1)S(1)} %pad_maximum_fusion.refs_1_), channel_id=1, source_target_pairs={{0,2},{1,3},{2,0},{3,1},{4,6},{5,7},{6,4},{7,5},{8,10},{9,11},{10,... | collective-permute-start | bytes 786440 | tf_op jit(solution)/shard_map/ppermute | solution.py:363
  71.6 13.4 %collective-permute-start.7 = (bf16[256,512]{1,0:T(8,128)(2,1)S(1)}, bf16[256,512]{1,0:T(8,128)(2,1)S(1)}, u32[]{:S(2)}, u32[]{:S(2)}) collective-permute-start(bf16[256,512]{1,0:T(8,128)(2,1)S(1)} %pad_maximum_fusion.1.refs_2_), channel_id=1, source_target_pairs={{0,4},{1,5},{2,6},{3,7},{4,0},{5,1},{6,2},{7,3},{8,12},{9,13},{10,... | collective-permute-start | bytes 786440 | tf_op jit(solution)/shard_map/ppermute | solution.py:363
  73.2 11.8 %copy-start.14 = (s32[512,128]{1,0:T(8,128)S(1)}, s32[512,128]{1,0:T(8,128)}, u32[]{:S(2)}) copy-start(s32[512,128]{1,0:T(8,128)} %copy-done.13) | copy-start | bytes 786436
  73.2 11.8 %collective-permute-start.8 = (bf16[256,512]{1,0:T(8,128)(2,1)S(1)}, bf16[256,512]{1,0:T(8,128)(2,1)S(1)}, u32[]{:S(2)}, u32[]{:S(2)}) collective-permute-start(bf16[256,512]{1,0:T(8,128)(2,1)S(1)} %pad_maximum_fusion.2.refs_3_), channel_id=1, source_target_pairs={{0,6},{1,7},{2,4},{3,5},{4,2},{5,3},{6,0},{7,1},{8,14},{9,15},{10,... | collective-permute-start | bytes 786440 | tf_op jit(solution)/shard_map/ppermute | solution.py:363
  79.7 6.0 %collective-permute-start.10 = (bf16[256,512]{1,0:T(8,128)(2,1)S(1)}, bf16[256,512]{1,0:T(8,128)(2,1)S(1)}, u32[]{:S(2)}, u32[]{:S(2)}) collective-permute-start(bf16[256,512]{1,0:T(8,128)(2,1)S(1)} %get-tuple-element.32), channel_id=1, source_target_pairs={{0,1},{1,0},{2,3},{3,2},{4,5},{5,4},{6,7},{7,6},{8,9},{9,8},{10,11... | collective-permute-start | bytes 786440 | tf_op jit(solution)/shard_map/ppermute | solution.py:363
  79.8 6.0 %collective-permute-start.11 = (bf16[256,512]{1,0:T(8,128)(2,1)S(1)}, bf16[256,512]{1,0:T(8,128)(2,1)S(1)}, u32[]{:S(2)}, u32[]{:S(2)}) collective-permute-start(bf16[256,512]{1,0:T(8,128)(2,1)S(1)} %get-tuple-element.33), channel_id=1, source_target_pairs={{0,1},{1,0},{2,3},{3,2},{4,5},{5,4},{6,7},{7,6},{8,9},{9,8},{10,11... | collective-permute-start | bytes 786440 | tf_op jit(solution)/shard_map/ppermute | solution.py:363
  85.0 14.6 %copy-start.10 = (bf16[512,1024]{1,0:T(8,128)(2,1)S(1)}, bf16[512,1024]{1,0:T(8,128)(2,1)}, u32[]{:S(2)}) copy-start(bf16[512,1024]{1,0:T(8,128)(2,1)} %copy-done.9) | copy-start | bytes 3145732
  85.8 13.9 %copy-start.5 = (bf16[512,1024]{1,0:T(8,128)(2,1)S(1)}, bf16[512,1024]{1,0:T(8,128)(2,1)}, u32[]{:S(2)}) copy-start(bf16[512,1024]{1,0:T(8,128)(2,1)} %x_ref.5) | copy-start | bytes 3145732
  85.8 13.9 %copy-start.7 = (bf16[1024,1024]{1,0:T(8,128)(2,1)S(1)}, bf16[1024,1024]{1,0:T(8,128)(2,1)}, u32[]{:S(2)}) copy-start(bf16[1024,1024]{1,0:T(8,128)(2,1)} %w_ref.5) | copy-start | bytes 6291460
  85.8 13.9 %copy-start.11 = (f32[1024]{0:T(1024)S(1)}, f32[1024]{0:T(1024)}, u32[]{:S(2)}) copy-start(f32[1024]{0:T(1024)} %param.16) | copy-start | bytes 12292
  85.9 9.3 %collective-permute-start.12 = (bf16[256,512]{1,0:T(8,128)(2,1)S(1)}, bf16[256,512]{1,0:T(8,128)(2,1)S(1)}, u32[]{:S(2)}, u32[]{:S(2)}) collective-permute-start(bf16[256,512]{1,0:T(8,128)(2,1)S(1)} %pad_maximum_fusion.3), channel_id=1, source_target_pairs={{0,2},{1,3},{2,0},{3,1},{4,6},{5,7},{6,4},{7,5},{8,10},{9,11},{10,... | collective-permute-start | bytes 786440 | tf_op jit(solution)/shard_map/ppermute | solution.py:363
  87.1 12.5 %collective-permute-start.13 = (bf16[256,512]{1,0:T(8,128)(2,1)S(1)}, bf16[256,512]{1,0:T(8,128)(2,1)S(1)}, u32[]{:S(2)}, u32[]{:S(2)}) collective-permute-start(bf16[256,512]{1,0:T(8,128)(2,1)S(1)} %pad_maximum_fusion.4), channel_id=1, source_target_pairs={{0,4},{1,5},{2,6},{3,7},{4,0},{5,1},{6,2},{7,3},{8,12},{9,13},{10,... | collective-permute-start | bytes 786440 | tf_op jit(solution)/shard_map/ppermute | solution.py:363
  88.1 11.5 %collective-permute-start.14 = (bf16[256,512]{1,0:T(8,128)(2,1)S(1)}, bf16[256,512]{1,0:T(8,128)(2,1)S(1)}, u32[]{:S(2)}, u32[]{:S(2)}) collective-permute-start(bf16[256,512]{1,0:T(8,128)(2,1)S(1)} %pad_maximum_fusion.5), channel_id=1, source_target_pairs={{0,6},{1,7},{2,4},{3,5},{4,2},{5,3},{6,0},{7,1},{8,14},{9,15},{10,... | collective-permute-start | bytes 786440 | tf_op jit(solution)/shard_map/ppermute | solution.py:363

commit v9 on v8

--- a/solution.py
+++ b/solution.py
@@ -19,7 +19,7 @@
 WAIT_COST = 20.0
 LATE_SHARE = 20.0
 COLLECT_COST = 20.0
-SPLIT_COST = 6.0
+SLOTS_COST = 6.0
 KERNEL_MIB = 24
 
 
@@ -61,77 +61,49 @@
     return [pl.BlockSpec(memory_space=pl.ANY)] * len(arrays)
 
 
-def split_kernel(spans, size, kv_hbm, *refs):
-    out_refs, sems = refs[:-1], refs[-1]
-    width = kv_hbm.shape[1] // 2
-    copies = []
+def split_kernel(spans, size, kv_ref, *out_refs):
+    width = kv_ref.shape[1] // 2
     for (first, heads), ref in zip(spans, out_refs):
-        wide = heads * size
-        for half in range(2):
-            source = kv_hbm.at[:, half * width + first * size : half * width + first * size + wide]
-            target = ref.at[:, half * wide : (half + 1) * wide]
-            copies.append(pltpu.make_async_copy(source, target, sems.at[len(copies)]))
-    for copy in copies:
-        copy.start()
-    for copy in copies:
-        copy.wait()
+        lo, hi = first * size, (first + heads) * size
+        ref[:, : hi - lo] = kv_ref[:, lo:hi]
+        ref[:, hi - lo :] = kv_ref[:, width + lo : width + hi]
 
 
 def split(kv, spans, size):
     rows = kv.shape[0]
     return pl.pallas_call(
         functools.partial(split_kernel, spans, size),
-        in_specs=[pl.BlockSpec(memory_space=pl.ANY)],
+        in_specs=whole(),
         out_specs=whole(len(spans)),
         out_shape=[jax.ShapeDtypeStruct((rows, 2 * heads * size), BF16) for _, heads in spans],
-        scratch_shapes=[pltpu.SemaphoreType.DMA((2 * len(spans),))],
-        compiler_params=params(KERNEL_MIB),
-        cost_estimate=cost(SPLIT_COST * 1e9, 4 * kv.size),
+        compiler_params=params(KERNEL_MIB),
+        cost_estimate=cost(0, 4 * kv.size),
         name="split",
     )(kv)
 
 
-def query_kernel(columns, capacity, owner_ref, visible_ref, x_ref, w_ref, send_hbm, send_ref, sems):
+def query_kernel(slot_ref, visible_ref, x_ref, w_ref, send_ref):
     rows, width = x_ref.shape
-    slots = columns * capacity
-    slot = slot_row(owner_ref[...], columns, capacity).astype(jnp.int32)
+    slots = send_ref.shape[0]
     index = lax.broadcasted_iota(jnp.int32, (slots, rows), 0)
-    place = (index == slot).astype(BF16)
-    stores = []
-
-    def store(span):
-        copy = pltpu.make_async_copy(
-            send_ref.at[:, span], send_hbm.at[:, span], sems.at[len(stores)]
-        )
-        copy.start()
-        stores.append(copy)
-
+    place = (index == slot_ref[:1, :]).astype(BF16)
     seen = jnp.broadcast_to(visible_ref[...].astype(F32), (BLK, rows)).T.astype(BF16)
     send_ref[:, width:] = jnp.dot(place, seen, preferred_element_type=F32).astype(BF16)
-    store(slice(width, width + BLK))
     tile = min(256, width)
     for start in range(0, width, tile):
         span = slice(start, start + tile)
         hidden = jnp.dot(x_ref[...], w_ref[:, span], preferred_element_type=F32)
         moved = jnp.dot(place, silu(hidden).astype(BF16), preferred_element_type=F32)
         send_ref[:, span] = moved.astype(BF16)
-        store(span)
-    for copy in stores:
-        copy.wait()
-
-
-def project_queries(owner_row, visible_row, cand_x, w_in, columns, capacity):
+
+
+def project_queries(slot, visible_row, cand_x, w_in, slots):
     rows, width = cand_x.shape
-    slots = columns * capacity
-    return pl.pallas_call(
-        functools.partial(query_kernel, columns, capacity),
+    return pl.pallas_call(
+        query_kernel,
         in_specs=whole(4),
-        out_specs=pl.BlockSpec(memory_space=pltpu.HBM),
+        out_specs=whole()[0],
         out_shape=jax.ShapeDtypeStruct((slots, width + BLK), BF16),
-        scratch_shapes=[
-            pltpu.VMEM((slots, width + BLK), BF16),
-            pltpu.SemaphoreType.DMA((width // min(256, width) + 1,)),
-        ],
         compiler_params=params(KERNEL_MIB),
         cost_estimate=cost(
             2 * rows * width * width + 2 * slots * rows * width,
@@ -139,7 +111,7 @@
             rows * width,
         ),
         name="project_queries",
-    )(owner_row, visible_row, cand_x, w_in)
+    )(slot, visible_row, cand_x, w_in)
 
 
 def gate_kernel(x_ref, w_ref, gate_ref, token_ref):
@@ -167,16 +139,34 @@
     )(cand_x, w_in)
 
 
-def slots_kernel(columns, capacity, owner_ref, *refs):
-    refs[-1][...] = jnp.zeros_like(refs[-1])
-    slot = slot_row(owner_ref[...], columns, capacity)
-    refs[-2][...] = jnp.broadcast_to(slot, (BLK, slot.shape[1])).T.astype(jnp.int32)
+def slots_kernel(columns, capacity, owner_ref, row_ref):
+    row = slot_row(owner_ref[...], columns, capacity)
+    row_ref[...] = jnp.broadcast_to(row, row_ref.shape).astype(jnp.int32)
+
+
+def find_slots(owner_row, columns, capacity):
+    return pl.pallas_call(
+        functools.partial(slots_kernel, columns, capacity),
+        in_specs=whole(),
+        out_specs=whole()[0],
+        out_shape=jax.ShapeDtypeStruct((8, owner_row.shape[1]), jnp.int32),
+        compiler_params=params(KERNEL_MIB),
+        cost_estimate=cost(SLOTS_COST * 1e9, 0),
+        name="find_slots",
+    )(owner_row)
+
+
+def column_kernel(columns, capacity, owner_ref, *refs):
+    column_ref, token_ref = refs[-2:]
+    token_ref[...] = jnp.zeros_like(token_ref)
+    row = slot_row(owner_ref[...], columns, capacity)
+    column_ref[...] = jnp.broadcast_to(row, (BLK, row.shape[1])).T.astype(jnp.int32)
 
 
 def slot_column(owner_row, columns, capacity, after):
     rows = owner_row.shape[1]
     return pl.pallas_call(
-        functools.partial(slots_kernel, columns, capacity),
+        functools.partial(column_kernel, columns, capacity),
         in_specs=whole() + unread(after),
         out_specs=whole(2),
         out_shape=[jax.ShapeDtypeStruct((rows, BLK), jnp.int32), TOKEN],
@@ -395,48 +385,47 @@
     visible_row = visible.reshape(1, rows)
     spans = [(sum(GROUPS[:number]), heads) for number, heads in enumerate(GROUPS)]
 
-    near = swap(kv_cache[0], "user", 1, count)
-    far = []
-    for own in split(kv_cache[0], spans, size):
-        held = {0: own}
-        bit = count // 2
-        while bit > 1:
-            for key in sorted(held):
-                held[key | bit] = swap(held[key], "user", bit, count)
-            bit //= 2
-        far.append(held)
-    evens = sorted(far[0])
-    late = [key | 1 for key in evens[1:]]
-
-    send = project_queries(owner_row, visible_row, cand_x, w_in, columns, capacity)
+    row = find_slots(owner_row, columns, capacity)
+    own, _ = lax.optimization_barrier((kv_cache[0], row))
+    held = {0: own}
+    bit = count // 2
+    while bit > 1:
+        for key in sorted(held):
+            held[key | bit] = swap(held[key], "user", bit, count)
+        bit //= 2
+    held[1] = swap(own, "user", 1, count)
+    ready = sorted(held)
+    late = [key | 1 for key in ready if key > 1]
+
+    send = project_queries(row, visible_row, cand_x, w_in, slots)
     got = lax.all_to_all(
         send.reshape(columns, capacity, -1), "cand", split_axis=0, concat_axis=0, tiled=True
     ).reshape(slots, -1)
     gate, gated = project_gate(cand_x, w_in)
-    arrived = [near] + [held[key] for held in far for key in evens[1:]]
-    slot, started = slot_column(owner_row ^ me, columns, capacity, [gated] + arrived)
+    arrived = [gated] + [held[key] for key in ready if key]
+    slot, started = slot_column(owner_row ^ me, columns, capacity, arrived)
     position = lax.axis_index("user").astype(jnp.int32)
-    shards = position ^ jnp.array(evens + [1] + late, jnp.int32)
+    shards = position ^ jnp.array(ready + late, jnp.int32)
     head = jnp.concatenate([hist_len, me[None]])
-    place_ready = jnp.concatenate([head, shards[: len(evens) + 1]])
-    place_late = jnp.concatenate([head, shards[len(evens) + 1 :]])
-
+    place_ready = jnp.concatenate([head, shards[: len(ready)]])
+    place_late = jnp.concatenate([head, shards[len(ready) :]])
+
+    passed = [split(held[key ^ 1], spans, size) for key in late]
     bases = []
+    for number, (first, heads) in enumerate(spans):
+        segments = [([held[key]], first, HEADS + first) for key in ready]
+        bases += attend(
+            place_ready, [started] + bases, got, segments, None, first, heads, size, None, F32, 0.0
+        )
     cuts = []
     for number, (first, heads) in enumerate(spans):
-        held = far[number]
-        segments = [([held[key]], 0, heads) for key in evens]
-        segments.append(([near], first, HEADS + first))
-        base = attend(
-            place_ready, [started] + bases, got, segments, None, first, heads, size, None, F32, 0.0
-        )[0]
-        passed = [held[key] for key in evens[1:]]
+        parts = [pieces[number] for pieces in passed]
         if number:
-            passed, _ = lax.optimization_barrier((passed, bases[-1]))
-        cuts.append([([swap(part, "user", 1, count)], 0, heads) for part in passed])
-        bases.append(base)
+            parts, _ = lax.optimization_barrier((parts, bases))
+        cuts.append([([swap(part, "user", 1, count)], 0, heads) for part in parts])
     early = []
-    after = []
+    after = bases
+    behind = None
     for number, (first, heads) in enumerate(spans):
         attn = attend(
             place_late,
@@ -451,14 +440,14 @@
             BF16,
             LATE_SHARE * (number > 0),
         )
-        here, pairs = exchange_cores(
-            attn[0], attn[1:], capacity, columns, early[-1] if early else None
-        )
+        here, pairs = exchange_cores(attn[0], attn[1:], capacity, columns, behind)
         after = [attn[0]] + pairs
-        returned = here + exchange_chips(pairs, columns)
+        away = exchange_chips(pairs, columns)
+        behind = away
         if number + 1 < len(spans):
-            early.append(collect(slot, returned, capacity, slots))
-    return finish(slot, early, gate, cand_x, ln_gain, w_out, returned, capacity, slots)
+            early.append(collect(slot, here + away, capacity, slots))
+            behind = early[-1]
+    return finish(slot, early, gate, cand_x, ln_gain, w_out, here + away, capacity, slots)
 
 
 def solution(mesh):

time: 103 us -> 106 us (1.029)
  waiting for transfers between devices: 41.6 us -> 50.8 us
  starting transfers between devices: 23.8 us -> 19.9 us
  Pallas kernels: 26.9 us -> 24.8 us
    ppermute x15 -> x14, waiting for transfers between devices: 41.6 us -> 50.8 us  [swap(): return lax.ppermute(array, axis, [(i, i ^ bits) for i in range(count)])]
    ppermute x15 -> x14, starting transfers between devices: 19.9 us -> 16.1 us  [swap(): return lax.ppermute(array, axis, [(i, i ^ bits) for i in range(count)])]
    pallas_call x3 -> x4, Pallas kernels: 7.52 us -> 4.69 us  [the longest x1 3.29 us: project_queries(): pl.pallas_call(query_kernel, in_specs=whole(4), out_specs=whole()[0], out...]
    unnamed x32 -> x34, local copies, waits for them, and re-layouts: 7.79 us -> 7.04 us
  transfers between devices with their start and end apart: 16 -> 15, of which waited for: 7 -> 7; matrix products, arithmetic and copies ran while one was open for 1% -> 2% of each run, Pallas kernels for 21% -> 18%
where the time goes in v9:
time: 106 us; the launch traced here: 105 us
  waiting for transfers between devices  50.8 us (48%)
  Pallas kernels  24.8 us (23%)
  starting transfers between devices  19.9 us (19%)
  local copies, waits for them, and re-layouts  7.8 us (7%)
  between operations  1.14 us (1%)
    ppermute x14, waiting for transfers between devices, swap(): return lax.ppermute(array, axis, [(i, i ^ bits) for i in range(count)])  50.8 us
    ppermute x14, starting transfers between devices, swap(): return lax.ppermute(array, axis, [(i, i ^ bits) for i in range(count)])  16.1 us
    pallas_call x4, Pallas kernels, attend(): pl.pallas_call(functools.partial(attend_kernel, size, heads, first, start...  14.9 us
    unnamed x34, local copies, waits for them, and re-layouts  7.04 us
    all_to_all x1, starting transfers between devices, per_device(): lax.all_to_all(send.reshape(columns, capacity, -1), 'cand', split_axis=0,...  3.8 us
    pallas_call x1, Pallas kernels, project_queries(): pl.pallas_call(query_kernel, in_specs=whole(4), out_specs=whole()[0], out...  3.29 us
    pallas_call x1, Pallas kernels, finish(): pl.pallas_call(functools.partial(finish_kernel, len(early), capacity, slo...  3.1 us
  transfers between devices with their start and end apart: 15, of which 7 were waited for; matrix products, arithmetic and copies ran while one was open for 2% of the time, Pallas kernels for 18%

profile of v9, /device:TPU:0, one launch (start us, length us, event | category | flops | bytes accessed | tf_op | source)
XLA Modules:
  0.0 105.4 jit_solution(11014370474214914855)
XLA Ops:
  0.0 0.7 copy-done.6
  0.7 0.2 find_slots.1.slot_ref
  0.9 4.1 %collective-permute-start.1 = (bf16[256,2048]{1,0:T(8,128)(2,1)}, bf16[256,2048]{1,0:T(8,128)(2,1)S(1)}, u32[]{:S(2)}, u32[]{:S(2)}) collective-permute-start(bf16[256,2048]{1,0:T(8,128)(2,1)} %bitcast.1.refs_2_.refs_3_), channel_id=1, source_target_pairs={{0,16},{8,24},{16,0},{24,8},{1,17},{9,25},{17,1},{25,9},{2,18},{10... | collective-permute-start | bytes 3145736 | tf_op jit(solution)/shard_map/ppermute | solution.py:353
  5.0 1.6 %collective-permute-start = (bf16[256,2048]{1,0:T(8,128)(2,1)}, bf16[256,2048]{1,0:T(8,128)(2,1)}, u32[]{:S(2)}, u32[]{:S(2)}) collective-permute-start(bf16[256,2048]{1,0:T(8,128)(2,1)} %bitcast.1.refs_2_.refs_3_), channel_id=1, source_target_pairs={{0,8},{8,0},{16,24},{24,16},{1,9},{9,1},{17,25},{25,17},{2,10},{10... | collective-permute-start | bytes 3145736 | tf_op jit(solution)/shard_map/ppermute | solution.py:353
  6.6 0.0 copy-done
  6.6 0.0 copy-done.3
  6.6 0.0 copy-done.14
  6.6 3.3 %project_queries.1 = bf16[1024,1152]{1,0:T(8,128)(2,1)S(1)} custom-call(s32[8,512]{1,0:T(8,128)S(1)} %find_slots.1.slot_ref, s32[1,512]{1,0:T(1,128)S(1)} %bitcast.16, bf16[512,1024]{1,0:T(8,128)(2,1)S(1)} %copy-done.3, bf16[1024,2048]{1,0:T(8,128)(2,1)S(1)} %copy-done), custom_call_target="tpu_custom_call" | custom-call | flops 2147483648 | bytes 5242880 | tf_op jit(solution)/shard_map/project_queries/pallas_call | solution.py:102
  9.9 0.0 copy-start.2
  9.9 1.4 %copy-done.2 = bf16[1024,1152]{1,0:T(8,128)(2,1)} copy-done((bf16[1024,1152]{1,0:T(8,128)(2,1)}, bf16[1024,1152]{1,0:T(8,128)(2,1)S(1)}, u32[]{:S(2)}) %copy-start.2) | copy-done | bytes 2359320
  11.3 3.8 %all-to-all-start = ((bf16[8,128,1152]{2,1,0:T(8,128)(2,1)}), bf16[8,128,1152]{2,1,0:T(8,128)(2,1)S(1)}, u32[]{:S(2)}, u32[]{:S(2)}) async-start(bf16[8,128,1152]{2,1,0:T(8,128)(2,1)} %bitcast.13), calls=%async_computation | async-start | bytes 4718592 | tf_op jit(solution)/shard_map/all_to_all | solution.py:401
  15.8 0.6 slice.42
  16.4 2.2 %copy-done.1 = bf16[1024,2048]{1,0:T(8,128)(2,1)S(1)} copy-done((bf16[1024,2048]{1,0:T(8,128)(2,1)S(1)}, bf16[1024,2048]{1,0:T(8,128)(2,1)}, u32[]{:S(2)}) %copy-start.1) | copy-done | bytes 4194328
  18.6 1.2 %copy-done.4 = bf16[512,1024]{1,0:T(8,128)(2,1)S(1)} copy-done((bf16[512,1024]{1,0:T(8,128)(2,1)S(1)}, bf16[512,1024]{1,0:T(8,128)(2,1)}, u32[]{:S(2)}) %copy-start.4) | copy-done | bytes 1048600
  19.8 1.4 %project_gate.1 = (bf16[512,1024]{1,0:T(8,128)(2,1)S(1)}, s32[8,128]{1,0:T(8,128)S(1)}) custom-call(bf16[512,1024]{1,0:T(8,128)(2,1)S(1)} %copy-done.4, bf16[1024,2048]{1,0:T(8,128)(2,1)S(1)} %copy-done.1), custom_call_target="tpu_custom_call" | custom-call | flops 1073741824 | bytes 4194304 | tf_op jit(solution)/shard_map/project_gate/pallas_call | solution.py:129
  21.2 0.0 copy-start.9
  21.2 0.1 pad_add_fusion.1.place_ref
  21.3 0.8 pad_add_fusion.place_ref
  22.1 0.0 copy-done.7
  22.1 28.9 %collective-permute-done.1.refs_2_.refs_4_.refs_5_.kv_ref = bf16[256,2048]{1,0:T(8,128)(2,1)S(1)} collective-permute-done((bf16[256,2048]{1,0:T(8,128)(2,1)}, bf16[256,2048]{1,0:T(8,128)(2,1)S(1)}, u32[]{:S(2)}, u32[]{:S(2)}) %collective-permute-start.1) | collective-permute-done | bytes 1048608 | tf_op jit(solution)/shard_map/ppermute | solution.py:353
  50.9 0.9 split.1
  51.8 0.8 copy-done.11
  52.6 0.7 collective-permute-start.2
  53.3 0.0 collective-permute-done.refs_1_.refs_3_.refs_4_
  53.3 0.0 copy-done.9
  53.3 0.3 slot_column.1
  53.7 0.0 copy-start.15
  53.7 0.7 copy-done.15
  54.4 0.0 all-to-all-done
  54.4 5.1 %attend.4.refs_1_.refs_0_.refs_4_ = f32[1024,512]{1,0:T(8,128)S(1)} custom-call(s32[5]{0:T(128)S(1)} %pad_add_fusion.1.place_ref, s32[8,128]{1,0:T(8,128)S(1)} %get-tuple-element.26.refs_0_, bf16[1024,1152]{1,0:T(8,128)(2,1)S(1)} %bitcast.9, bf16[256,2048]{1,0:T(8,128)(2,1)} %bitcast.1.refs_2_.refs_3_, ...), custom_call_target="tpu_custom_call" | custom-call | bytes 3670016 | tf_op jit(solution)/shard_map/attend/pallas_call | solution.py:261
  59.5 5.1 %attend.5.refs_1_.refs_6_ = f32[1024,512]{1,0:T(8,128)S(1)} custom-call(s32[5]{0:T(128)S(1)} %pad_add_fusion.1.place_ref, s32[8,128]{1,0:T(8,128)S(1)} %get-tuple-element.26.refs_0_, f32[1024,512]{1,0:T(8,128)S(1)} %attend.4.refs_1_.refs_0_.refs_4_, bf16[1024,1152]{1,0:T(8,128)(2,1)S(1)} %bitcast.10, bf16[256,2048]{1,0:T(8,128)(2,1)} %bitcast.1.refs_2_.refs_3_, ...), custom_call_target="tpu_custom_call" | custom-call | bytes 3670016 | tf_op jit(solution)/shard_map/attend/pallas_call | solution.py:261
  64.6 0.0 copy-start.12
  64.6 1.4 %collective-permute-done.2.refs_3_ = bf16[256,1024]{1,0:T(8,128)(2,1)} collective-permute-done((bf16[256,1024]{1,0:T(8,128)(2,1)}, bf16[256,1024]{1,0:T(8,128)(2,1)}, u32[]{:S(2)}, u32[]{:S(2)}) %collective-permute-start.2) | collective-permute-done | bytes 524320 | tf_op jit(solution)/shard_map/ppermute | solution.py:353
  66.0 2.5 %attend.6 = (bf16[512,512]{1,0:T(8,128)(2,1)S(1)}, bf16[256,512]{1,0:T(8,128)(2,1)S(1)}, bf16[256,512]{1,0:T(8,128)(2,1)S(1)}) custom-call(s32[3]{0:T(128)S(1)} %pad_add_fusion.place_ref, f32[1024,512]{1,0:T(8,128)S(1)} %attend.4.refs_1_.refs_0_.refs_4_, f32[1024,512]{1,0:T(8,128)S(1)} %attend.5.refs_1_.refs_6_, bf16[1024,1152]{1,0:T(8,128)(2,1)S(1)} %bitcast.11, ...), custom_call_target="tpu_custom_call" | custom-call | bytes 2621440 | tf_op jit(solution)/shard_map/attend/pallas_call | solution.py:261
  68.5 0.1 collective-permute-start.5
  68.6 0.0 copy-done.12
  68.6 1.6 %collective-permute-start.8 = (bf16[256,1024]{1,0:T(8,128)(2,1)S(1)}, bf16[256,1024]{1,0:T(8,128)(2,1)S(1)}, u32[]{:S(2)}, u32[]{:S(2)}) collective-permute-start(bf16[256,1024]{1,0:T(8,128)(2,1)S(1)} %copy-done.12), channel_id=1, source_target_pairs={{0,8},{8,0},{16,24},{24,16},{1,9},{9,1},{17,25},{25,17},{2,10},{10... | collective-permute-start | bytes 1572872 | tf_op jit(solution)/shard_map/ppermute | solution.py:353
  70.1 0.2 collective-permute-start.3
  70.3 0.0 collective-permute-done.5
  70.4 2.5 %collective-permute-start.7 = (bf16[256,512]{1,0:T(8,128)(2,1)S(1)}, bf16[256,512]{1,0:T(8,128)(2,1)S(1)}, u32[]{:S(2)}, u32[]{:S(2)}) collective-permute-start(bf16[256,512]{1,0:T(8,128)(2,1)S(1)} %pad_maximum_fusion.2.refs_3_), channel_id=1, source_target_pairs={{0,6},{1,7},{2,4},{3,5},{4,2},{5,3},{6,0},{7,1},{8,14},{9,15},{10,... | collective-permute-start | bytes 786440 | tf_op jit(solution)/shard_map/ppermute | solution.py:353
  72.9 0.6 collective-permute-start.6
  73.5 0.0 collective-permute-done.3.refs_1_
  73.6 0.6 collective-permute-start.4
  74.2 8.7 %collective-permute-done.8.refs_5_ = bf16[256,1024]{1,0:T(8,128)(2,1)S(1)} collective-permute-done((bf16[256,1024]{1,0:T(8,128)(2,1)S(1)}, bf16[256,1024]{1,0:T(8,128)(2,1)S(1)}, u32[]{:S(2)}, u32[]{:S(2)}) %collective-permute-start.8) | collective-permute-done | bytes 524320 | tf_op jit(solution)/shard_map/ppermute | solution.py:353
  82.9 2.2 %attend.7 = (bf16[512,512]{1,0:T(8,128)(2,1)S(1)}, bf16[256,512]{1,0:T(8,128)(2,1)S(1)}, bf16[256,512]{1,0:T(8,128)(2,1)S(1)}) custom-call(s32[3]{0:T(128)S(1)} %pad_add_fusion.place_ref, bf16[512,512]{1,0:T(8,128)(2,1)S(1)} %get-tuple-element.28.refs_0_, bf16[256,512]{1,0:T(8,128)(2,1)S(1)} %pad_maximum_fusion.refs_1_, ...), custom_call_target="tpu_custom_call" | custom-call | flops 10737418240 | bytes 2621440 | tf_op jit(solution)/shard_map/attend/pallas_call | solution.py:261
  85.1 0.1 collective-permute-start.10
  85.2 0.5 collective-permute-start.9
  85.7 0.0 collective-permute-done.7.refs_4_
  85.7 0.0 collective-permute-done.6.refs_3_
  85.7 0.0 collective-permute-done.4.refs_2_
  85.7 0.0 copy-start.10
  85.7 0.7 collect.1.refs_0_
  86.4 0.0 copy-start.5
  86.4 0.0 copy-start.8
  86.5 0.0 copy-start.13
  86.5 0.2 collective-permute-done.10
  86.7 0.4 collective-permute-done.9.refs_2_
  87.2 2.3 %collective-permute-start.13 = (bf16[256,512]{1,0:T(8,128)(2,1)S(1)}, bf16[256,512]{1,0:T(8,128)(2,1)S(1)}, u32[]{:S(2)}, u32[]{:S(2)}) collective-permute-start(bf16[256,512]{1,0:T(8,128)(2,1)S(1)} %pad_maximum_fusion.5), channel_id=1, source_target_pairs={{0,6},{1,7},{2,4},{3,5},{4,2},{5,3},{6,0},{7,1},{8,14},{9,15},{10,... | collective-permute-start | bytes 786440 | tf_op jit(solution)/shard_map/ppermute | solution.py:353
  89.5 0.6 collective-permute-start.12
  90.1 0.8 collective-permute-start.11
  90.9 6.4 %collective-permute-done.13.refs_5_ = bf16[256,512]{1,0:T(8,128)(2,1)S(1)} collective-permute-done((bf16[256,512]{1,0:T(8,128)(2,1)S(1)}, bf16[256,512]{1,0:T(8,128)(2,1)S(1)}, u32[]{:S(2)}, u32[]{:S(2)}) %collective-permute-start.13) | collective-permute-done | bytes 262176 | tf_op jit(solution)/shard_map/ppermute | solution.py:353
  97.3 4.8 %collective-permute-done.12.refs_4_ = bf16[256,512]{1,0:T(8,128)(2,1)S(1)} collective-permute-done((bf16[256,512]{1,0:T(8,128)(2,1)S(1)}, bf16[256,512]{1,0:T(8,128)(2,1)S(1)}, u32[]{:S(2)}, u32[]{:S(2)}) %collective-permute-start.12) | collective-permute-done | bytes 262176 | tf_op jit(solution)/shard_map/ppermute | solution.py:353
  102.1 0.0 collective-permute-done.11.refs_3_
  102.1 3.1 %finish.1 = bf16[512,1024]{1,0:T(8,128)(2,1)} custom-call(s32[512,128]{1,0:T(8,128)S(1)} %copy-done.16, f32[1,1024]{1,0:T(1,128)S(1)} %bitcast.15, bf16[512,1024]{1,0:T(8,128)(2,1)S(1)} %copy-done.10, bf16[512,1024]{1,0:T(8,128)(2,1)S(1)} %copy-done.5, bf16[1024,1024]{1,0:T(8,128)(2,1)S(1)} %copy-done.8, bf16[512,512]{1,0:T(8,128)(2,1)S(1)} %collect.1.refs_0_, ...), custom_call_target="tpu_custom_call" | custom-call | flops 2147483648 | bytes 7340032 | tf_op jit(solution)/shard_map/finish/pallas_call | solution.py:338
  (28 shorter events, 0.3 us)
Async XLA Ops:
  0.0 0.7 copy-start.6
  0.7 5.9 %copy-start = (bf16[1024,2048]{1,0:T(8,128)(2,1)S(1)}, bf16[1024,2048]{1,0:T(8,128)(2,1)}, u32[]{:S(2)}) copy-start(bf16[1024,2048]{1,0:T(8,128)(2,1)} %w_ref.4) | copy-start | bytes 12582916
  0.7 5.9 %copy-start.3 = (bf16[512,1024]{1,0:T(8,128)(2,1)S(1)}, bf16[512,1024]{1,0:T(8,128)(2,1)}, u32[]{:S(2)}) copy-start(bf16[512,1024]{1,0:T(8,128)(2,1)} %x_ref.5) | copy-start | bytes 3145732
  0.7 5.9 %copy-start.14 = (s32[512]{0:T(512)S(1)}, s32[512]{0:T(512)}, u32[]{:S(2)}) copy-start(s32[512]{0:T(512)} %param.11) | copy-start | bytes 6148
  0.9 50.1 %collective-permute-start.1 = (bf16[256,2048]{1,0:T(8,128)(2,1)}, bf16[256,2048]{1,0:T(8,128)(2,1)S(1)}, u32[]{:S(2)}, u32[]{:S(2)}) collective-permute-start(bf16[256,2048]{1,0:T(8,128)(2,1)} %bitcast.1.refs_2_.refs_3_), channel_id=1, source_target_pairs={{0,16},{8,24},{16,0},{24,8},{1,17},{9,25},{17,1},{25,9},{2,18},{10... | collective-permute-start | bytes 3145736 | tf_op jit(solution)/shard_map/ppermute | solution.py:353
  5.0 48.3 %collective-permute-start = (bf16[256,2048]{1,0:T(8,128)(2,1)}, bf16[256,2048]{1,0:T(8,128)(2,1)}, u32[]{:S(2)}, u32[]{:S(2)}) collective-permute-start(bf16[256,2048]{1,0:T(8,128)(2,1)} %bitcast.1.refs_2_.refs_3_), channel_id=1, source_target_pairs={{0,8},{8,0},{16,24},{24,16},{1,9},{9,1},{17,25},{25,17},{2,10},{10... | collective-permute-start | bytes 3145736 | tf_op jit(solution)/shard_map/ppermute | solution.py:353
  9.9 1.4 %copy-start.2 = (bf16[1024,1152]{1,0:T(8,128)(2,1)}, bf16[1024,1152]{1,0:T(8,128)(2,1)S(1)}, u32[]{:S(2)}) copy-start(bf16[1024,1152]{1,0:T(8,128)(2,1)S(1)} %project_queries.1) | copy-start | bytes 7077892
  11.3 43.1 %all-to-all-start = ((bf16[8,128,1152]{2,1,0:T(8,128)(2,1)}), bf16[8,128,1152]{2,1,0:T(8,128)(2,1)S(1)}, u32[]{:S(2)}, u32[]{:S(2)}) async-start(bf16[8,128,1152]{2,1,0:T(8,128)(2,1)} %bitcast.13), calls=%async_computation | async-start | bytes 4718592 | tf_op jit(solution)/shard_map/all_to_all | solution.py:401
  16.4 2.2 %copy-start.1 = (bf16[1024,2048]{1,0:T(8,128)(2,1)S(1)}, bf16[1024,2048]{1,0:T(8,128)(2,1)}, u32[]{:S(2)}) copy-start(bf16[1024,2048]{1,0:T(8,128)(2,1)} %w_ref.4) | copy-start | bytes 12582916
  18.6 1.2 %copy-start.4 = (bf16[512,1024]{1,0:T(8,128)(2,1)S(1)}, bf16[512,1024]{1,0:T(8,128)(2,1)}, u32[]{:S(2)}) copy-start(bf16[512,1024]{1,0:T(8,128)(2,1)} %x_ref.5) | copy-start | bytes 3145732
  19.8 2.3 %copy-start.7 = (s32[512,1]{0,1:T(1,128)S(1)}, s32[512,1]{0,1:T(1,128)}, u32[]{:S(2)}) copy-start(s32[512,1]{0,1:T(1,128)} %param.10) | copy-start | bytes 6148
  21.2 32.1 %copy-start.9 = (bf16[512,1024]{1,0:T(8,128)(2,1)}, bf16[512,1024]{1,0:T(8,128)(2,1)S(1)}, u32[]{:S(2)}) copy-start(bf16[512,1024]{1,0:T(8,128)(2,1)S(1)} %get-tuple-element.25.gate_ref) | copy-start | bytes 3145732
  51.8 0.8 copy-start.11
  52.6 13.4 %collective-permute-start.2 = (bf16[256,1024]{1,0:T(8,128)(2,1)}, bf16[256,1024]{1,0:T(8,128)(2,1)}, u32[]{:S(2)}, u32[]{:S(2)}) collective-permute-start(bf16[256,1024]{1,0:T(8,128)(2,1)} %get-tuple-element.27), channel_id=1, source_target_pairs={{0,8},{8,0},{16,24},{24,16},{1,9},{9,1},{17,25},{25,17},{2,10},{10... | collective-permute-start | bytes 1572872 | tf_op jit(solution)/shard_map/ppermute | solution.py:353
  53.7 0.7 copy-start.15
  64.6 4.0 %copy-start.12 = (bf16[256,1024]{1,0:T(8,128)(2,1)S(1)}, bf16[256,1024]{1,0:T(8,128)(2,1)}, u32[]{:S(2)}) copy-start(bf16[256,1024]{1,0:T(8,128)(2,1)} %copy-done.11) | copy-start | bytes 1572868
  68.5 1.9 %collective-permute-start.5 = (bf16[256,512]{1,0:T(8,128)(2,1)S(1)}, bf16[256,512]{1,0:T(8,128)(2,1)S(1)}, u32[]{:S(2)}, u32[]{:S(2)}) collective-permute-start(bf16[256,512]{1,0:T(8,128)(2,1)S(1)} %get-tuple-element.30), channel_id=1, source_target_pairs={{0,1},{1,0},{2,3},{3,2},{4,5},{5,4},{6,7},{7,6},{8,9},{9,8},{10,11... | collective-permute-start | bytes 786440 | tf_op jit(solution)/shard_map/ppermute | solution.py:353
  68.6 14.3 %collective-permute-start.8 = (bf16[256,1024]{1,0:T(8,128)(2,1)S(1)}, bf16[256,1024]{1,0:T(8,128)(2,1)S(1)}, u32[]{:S(2)}, u32[]{:S(2)}) collective-permute-start(bf16[256,1024]{1,0:T(8,128)(2,1)S(1)} %copy-done.12), channel_id=1, source_target_pairs={{0,8},{8,0},{16,24},{24,16},{1,9},{9,1},{17,25},{25,17},{2,10},{10... | collective-permute-start | bytes 1572872 | tf_op jit(solution)/shard_map/ppermute | solution.py:353
  70.1 3.4 %collective-permute-start.3 = (bf16[256,512]{1,0:T(8,128)(2,1)S(1)}, bf16[256,512]{1,0:T(8,128)(2,1)S(1)}, u32[]{:S(2)}, u32[]{:S(2)}) collective-permute-start(bf16[256,512]{1,0:T(8,128)(2,1)S(1)} %get-tuple-element.29), channel_id=1, source_target_pairs={{0,1},{1,0},{2,3},{3,2},{4,5},{5,4},{6,7},{7,6},{8,9},{9,8},{10,11... | collective-permute-start | bytes 786440 | tf_op jit(solution)/shard_map/ppermute | solution.py:353
  70.4 15.3 %collective-permute-start.7 = (bf16[256,512]{1,0:T(8,128)(2,1)S(1)}, bf16[256,512]{1,0:T(8,128)(2,1)S(1)}, u32[]{:S(2)}, u32[]{:S(2)}) collective-permute-start(bf16[256,512]{1,0:T(8,128)(2,1)S(1)} %pad_maximum_fusion.2.refs_3_), channel_id=1, source_target_pairs={{0,6},{1,7},{2,4},{3,5},{4,2},{5,3},{6,0},{7,1},{8,14},{9,15},{10,... | collective-permute-start | bytes 786440 | tf_op jit(solution)/shard_map/ppermute | solution.py:353
  72.9 12.8 %collective-permute-start.6 = (bf16[256,512]{1,0:T(8,128)(2,1)S(1)}, bf16[256,512]{1,0:T(8,128)(2,1)S(1)}, u32[]{:S(2)}, u32[]{:S(2)}) collective-permute-start(bf16[256,512]{1,0:T(8,128)(2,1)S(1)} %pad_maximum_fusion.1.refs_2_), channel_id=1, source_target_pairs={{0,4},{1,5},{2,6},{3,7},{4,0},{5,1},{6,2},{7,3},{8,12},{9,13},{10,... | collective-permute-start | bytes 786440 | tf_op jit(solution)/shard_map/ppermute | solution.py:353
  73.5 12.1 %copy-start.16 = (s32[512,128]{1,0:T(8,128)S(1)}, s32[512,128]{1,0:T(8,128)}, u32[]{:S(2)}) copy-start(s32[512,128]{1,0:T(8,128)} %copy-done.15) | copy-start | bytes 786436
  73.6 12.1 %collective-permute-start.4 = (bf16[256,512]{1,0:T(8,128)(2,1)S(1)}, bf16[256,512]{1,0:T(8,128)(2,1)S(1)}, u32[]{:S(2)}, u32[]{:S(2)}) collective-permute-start(bf16[256,512]{1,0:T(8,128)(2,1)S(1)} %pad_maximum_fusion.refs_1_), channel_id=1, source_target_pairs={{0,2},{1,3},{2,0},{3,1},{4,6},{5,7},{6,4},{7,5},{8,10},{9,11},{10,... | collective-permute-start | bytes 786440 | tf_op jit(solution)/shard_map/ppermute | solution.py:353
  85.1 1.6 %collective-permute-start.10 = (bf16[256,512]{1,0:T(8,128)(2,1)S(1)}, bf16[256,512]{1,0:T(8,128)(2,1)S(1)}, u32[]{:S(2)}, u32[]{:S(2)}) collective-permute-start(bf16[256,512]{1,0:T(8,128)(2,1)S(1)} %get-tuple-element.35), channel_id=1, source_target_pairs={{0,1},{1,0},{2,3},{3,2},{4,5},{5,4},{6,7},{7,6},{8,9},{9,8},{10,11... | collective-permute-start | bytes 786440 | tf_op jit(solution)/shard_map/ppermute | solution.py:353
  85.2 1.9 %collective-permute-start.9 = (bf16[256,512]{1,0:T(8,128)(2,1)S(1)}, bf16[256,512]{1,0:T(8,128)(2,1)S(1)}, u32[]{:S(2)}, u32[]{:S(2)}) collective-permute-start(bf16[256,512]{1,0:T(8,128)(2,1)S(1)} %get-tuple-element.34), channel_id=1, source_target_pairs={{0,1},{1,0},{2,3},{3,2},{4,5},{5,4},{6,7},{7,6},{8,9},{9,8},{10,11... | collective-permute-start | bytes 786440 | tf_op jit(solution)/shard_map/ppermute | solution.py:353
  85.7 16.4 %copy-start.10 = (bf16[512,1024]{1,0:T(8,128)(2,1)S(1)}, bf16[512,1024]{1,0:T(8,128)(2,1)}, u32[]{:S(2)}) copy-start(bf16[512,1024]{1,0:T(8,128)(2,1)} %copy-done.9) | copy-start | bytes 3145732
  86.4 15.7 %copy-start.5 = (bf16[512,1024]{1,0:T(8,128)(2,1)S(1)}, bf16[512,1024]{1,0:T(8,128)(2,1)}, u32[]{:S(2)}) copy-start(bf16[512,1024]{1,0:T(8,128)(2,1)} %x_ref.5) | copy-start | bytes 3145732
  86.4 15.7 %copy-start.8 = (bf16[1024,1024]{1,0:T(8,128)(2,1)S(1)}, bf16[1024,1024]{1,0:T(8,128)(2,1)}, u32[]{:S(2)}) copy-start(bf16[1024,1024]{1,0:T(8,128)(2,1)} %w_ref.5) | copy-start | bytes 6291460
  86.5 15.7 %copy-start.13 = (f32[1024]{0:T(1024)S(1)}, f32[1024]{0:T(1024)}, u32[]{:S(2)}) copy-start(f32[1024]{0:T(1024)} %param.16) | copy-start | bytes 12292
  87.2 10.2 %collective-permute-start.13 = (bf16[256,512]{1,0:T(8,128)(2,1)S(1)}, bf16[256,512]{1,0:T(8,128)(2,1)S(1)}, u32[]{:S(2)}, u32[]{:S(2)}) collective-permute-start(bf16[256,512]{1,0:T(8,128)(2,1)S(1)} %pad_maximum_fusion.5), channel_id=1, source_target_pairs={{0,6},{1,7},{2,4},{3,5},{4,2},{5,3},{6,0},{7,1},{8,14},{9,15},{10,... | collective-permute-start | bytes 786440 | tf_op jit(solution)/shard_map/ppermute | solution.py:353
  89.5 12.6 %collective-permute-start.12 = (bf16[256,512]{1,0:T(8,128)(2,1)S(1)}, bf16[256,512]{1,0:T(8,128)(2,1)S(1)}, u32[]{:S(2)}, u32[]{:S(2)}) collective-permute-start(bf16[256,512]{1,0:T(8,128)(2,1)S(1)} %pad_maximum_fusion.4), channel_id=1, source_target_pairs={{0,4},{1,5},{2,6},{3,7},{4,0},{5,1},{6,2},{7,3},{8,12},{9,13},{10,... | collective-permute-start | bytes 786440 | tf_op jit(solution)/shard_map/ppermute | solution.py:353
  90.1 12.0 %collective-permute-start.11 = (bf16[256,512]{1,0:T(8,128)(2,1)S(1)}, bf16[256,512]{1,0:T(8,128)(2,1)S(1)}, u32[]{:S(2)}, u32[]{:S(2)}) collective-permute-start(bf16[256,512]{1,0:T(8,128)(2,1)S(1)} %pad_maximum_fusion.3), channel_id=1, source_target_pairs={{0,2},{1,3},{2,0},{3,1},{4,6},{5,7},{6,4},{7,5},{8,10},{9,11},{10,... | collective-permute-start | bytes 786440 | tf_op jit(solution)/shard_map/ppermute | solution.py:353

commit v10 on v9

--- a/solution.py
+++ b/solution.py
@@ -61,27 +61,6 @@
     return [pl.BlockSpec(memory_space=pl.ANY)] * len(arrays)
 
 
-def split_kernel(spans, size, kv_ref, *out_refs):
-    width = kv_ref.shape[1] // 2
-    for (first, heads), ref in zip(spans, out_refs):
-        lo, hi = first * size, (first + heads) * size
-        ref[:, : hi - lo] = kv_ref[:, lo:hi]
-        ref[:, hi - lo :] = kv_ref[:, width + lo : width + hi]
-
-
-def split(kv, spans, size):
-    rows = kv.shape[0]
-    return pl.pallas_call(
-        functools.partial(split_kernel, spans, size),
-        in_specs=whole(),
-        out_specs=whole(len(spans)),
-        out_shape=[jax.ShapeDtypeStruct((rows, 2 * heads * size), BF16) for _, heads in spans],
-        compiler_params=params(KERNEL_MIB),
-        cost_estimate=cost(0, 4 * kv.size),
-        name="split",
-    )(kv)
-
-
 def query_kernel(slot_ref, visible_ref, x_ref, w_ref, send_ref):
     rows, width = x_ref.shape
     slots = send_ref.shape[0]
@@ -139,21 +118,53 @@
     )(cand_x, w_in)
 
 
-def slots_kernel(columns, capacity, owner_ref, row_ref):
+def prepare_kernel(columns, capacity, spans, size, owner_ref, kv_hbm, row_ref, *refs):
+    part_refs, sems = refs[:-1], refs[-1]
+    width = kv_hbm.shape[1] // 2
+    copies = []
+    for (first, heads), ref in zip(spans, part_refs):
+        wide = heads * size
+        for start in (0, width):
+            source = kv_hbm.at[:, start + first * size : start + first * size + wide]
+            target = ref.at[:, wide * (start > 0) : wide * (start > 0) + wide]
+            copies.append(pltpu.make_async_copy(source, target, sems.at[len(copies)]))
+    for copy in copies:
+        copy.start()
     row = slot_row(owner_ref[...], columns, capacity)
     row_ref[...] = jnp.broadcast_to(row, row_ref.shape).astype(jnp.int32)
-
-
-def find_slots(owner_row, columns, capacity):
-    return pl.pallas_call(
-        functools.partial(slots_kernel, columns, capacity),
-        in_specs=whole(),
+    for copy in copies:
+        copy.wait()
+
+
+def prepare(owner_row, kv, spans, size, columns, capacity):
+    rows = kv.shape[0]
+    return pl.pallas_call(
+        functools.partial(prepare_kernel, columns, capacity, spans, size),
+        in_specs=whole() + [pl.BlockSpec(memory_space=pl.ANY)],
+        out_specs=whole(1 + len(spans)),
+        out_shape=[jax.ShapeDtypeStruct((8, owner_row.shape[1]), jnp.int32)]
+        + [jax.ShapeDtypeStruct((rows, 2 * heads * size), BF16) for _, heads in spans],
+        scratch_shapes=[pltpu.SemaphoreType.DMA((2 * len(spans),))],
+        compiler_params=params(KERNEL_MIB),
+        cost_estimate=cost(SLOTS_COST * 1e9, 0),
+        name="prepare",
+    )(owner_row, kv)
+
+
+def wait_kernel(*refs):
+    refs[-1][...] = jnp.zeros_like(refs[-1])
+
+
+def wait_for(arrays):
+    return pl.pallas_call(
+        wait_kernel,
+        in_specs=unread(arrays),
         out_specs=whole()[0],
-        out_shape=jax.ShapeDtypeStruct((8, owner_row.shape[1]), jnp.int32),
-        compiler_params=params(KERNEL_MIB),
-        cost_estimate=cost(SLOTS_COST * 1e9, 0),
-        name="find_slots",
-    )(owner_row)
+        out_shape=TOKEN,
+        compiler_params=params(KERNEL_MIB),
+        cost_estimate=cost(WAIT_COST * 1e9, 0),
+        name="wait_for",
+    )(*arrays)
 
 
 def column_kernel(columns, capacity, owner_ref, *refs):
@@ -385,54 +396,55 @@
     visible_row = visible.reshape(1, rows)
     spans = [(sum(GROUPS[:number]), heads) for number, heads in enumerate(GROUPS)]
 
-    row = find_slots(owner_row, columns, capacity)
-    own, _ = lax.optimization_barrier((kv_cache[0], row))
-    held = {0: own}
-    bit = count // 2
-    while bit > 1:
-        for key in sorted(held):
-            held[key | bit] = swap(held[key], "user", bit, count)
-        bit //= 2
-    held[1] = swap(own, "user", 1, count)
-    ready = sorted(held)
-    late = [key | 1 for key in ready if key > 1]
+    row, *parts = prepare(owner_row, kv_cache[0], spans, size, columns, capacity)
+    near = None
+    far = []
+    for part in parts:
+        if far:
+            part, _ = lax.optimization_barrier((part, far[-1]))
+        held = {0: part}
+        bit = count // 2
+        while bit > 1:
+            for key in sorted(held):
+                held[key | bit] = swap(held[key], "user", bit, count)
+            bit //= 2
+        if near is None:
+            own, _ = lax.optimization_barrier((kv_cache[0], row))
+            near = swap(own, "user", 1, count)
+        far.append(held)
+    evens = sorted(far[0])
+    late = [key | 1 for key in evens[1:]]
 
     send = project_queries(row, visible_row, cand_x, w_in, slots)
     got = lax.all_to_all(
         send.reshape(columns, capacity, -1), "cand", split_axis=0, concat_axis=0, tiled=True
     ).reshape(slots, -1)
     gate, gated = project_gate(cand_x, w_in)
-    arrived = [gated] + [held[key] for key in ready if key]
+    arrived = [gated, near] + [far[0][key] for key in evens[1:]]
     slot, started = slot_column(owner_row ^ me, columns, capacity, arrived)
     position = lax.axis_index("user").astype(jnp.int32)
-    shards = position ^ jnp.array(ready + late, jnp.int32)
+    shards = position ^ jnp.array(evens + [1] + late, jnp.int32)
     head = jnp.concatenate([hist_len, me[None]])
-    place_ready = jnp.concatenate([head, shards[: len(ready)]])
-    place_late = jnp.concatenate([head, shards[len(ready) :]])
-
-    passed = [split(held[key ^ 1], spans, size) for key in late]
-    bases = []
-    for number, (first, heads) in enumerate(spans):
-        segments = [([held[key]], first, HEADS + first) for key in ready]
-        bases += attend(
-            place_ready, [started] + bases, got, segments, None, first, heads, size, None, F32, 0.0
-        )
-    cuts = []
-    for number, (first, heads) in enumerate(spans):
-        parts = [pieces[number] for pieces in passed]
-        if number:
-            parts, _ = lax.optimization_barrier((parts, bases))
-        cuts.append([([swap(part, "user", 1, count)], 0, heads) for part in parts])
+    place_ready = jnp.concatenate([head, shards[: len(evens) + 1]])
+    place_late = jnp.concatenate([head, shards[len(evens) + 1 :]])
+
     early = []
-    after = bases
+    after = [started]
     behind = None
     for number, (first, heads) in enumerate(spans):
+        held = far[number]
+        cuts = [([swap(held[key], "user", 1, count)], 0, heads) for key in evens[1:]]
+        segments = [([held[key]], 0, heads) for key in evens]
+        segments.append(([near], first, HEADS + first))
+        base = attend(
+            place_ready, after, got, segments, None, first, heads, size, None, F32, 0.0
+        )[0]
         attn = attend(
             place_late,
-            after,
+            [],
             got,
-            cuts[number],
-            bases[number],
+            cuts,
+            base,
             first,
             heads,
             size,
@@ -441,10 +453,10 @@
             LATE_SHARE * (number > 0),
         )
         here, pairs = exchange_cores(attn[0], attn[1:], capacity, columns, behind)
-        after = [attn[0]] + pairs
         away = exchange_chips(pairs, columns)
-        behind = away
         if number + 1 < len(spans):
+            token = wait_for([attn[0]] + [far[number + 1][key] for key in evens[1:]])
+            after = [token] + pairs
             early.append(collect(slot, here + away, capacity, slots))
             behind = early[-1]
     return finish(slot, early, gate, cand_x, ln_gain, w_out, here + away, capacity, slots)

time: 106 us -> 104 us (0.981)
  waiting for transfers between devices: 50.8 us -> 44.5 us
  starting transfers between devices: 19.9 us -> 23.7 us
    ppermute x14 -> x15, waiting for transfers between devices: 50.8 us -> 44.5 us  [swap(): return lax.ppermute(array, axis, [(i, i ^ bits) for i in range(count)])]
    ppermute x14 -> x15, starting transfers between devices: 16.1 us -> 19.7 us  [swap(): return lax.ppermute(array, axis, [(i, i ^ bits) for i in range(count)])]
    pallas_call x2, Pallas kernels: 1.07 us -> 2.18 us  [the longest x1 2.17 us: prepare(): pl.pallas_call(functools.partial(prepare_kernel, columns, capacity, spans...]
    unnamed x34 -> x36, local copies, waits for them, and re-layouts: 7.04 us -> 7.22 us
  transfers between devices with their start and end apart: 15 -> 16, of which waited for: 7 -> 7; matrix products, arithmetic and copies ran while one was open for 2% -> 2% of each run, Pallas kernels for 18% -> 20%
where the time goes in v10:
time: 104 us
  waiting for transfers between devices  44.5 us (43%)
  Pallas kernels  25.6 us (25%)
  starting transfers between devices  23.7 us (23%)
  local copies, waits for them, and re-layouts  7.98 us (8%)
  between operations  1.15 us (1%)
    ppermute x15, waiting for transfers between devices, swap(): return lax.ppermute(array, axis, [(i, i ^ bits) for i in range(count)])  44.5 us
    ppermute x15, starting transfers between devices, swap(): return lax.ppermute(array, axis, [(i, i ^ bits) for i in range(count)])  19.7 us
    pallas_call x4, Pallas kernels, attend(): pl.pallas_call(functools.partial(attend_kernel, size, heads, first, start...  14.6 us
    unnamed x36, local copies, waits for them, and re-layouts  7.22 us
    all_to_all x1, starting transfers between devices, per_device(): lax.all_to_all(send.reshape(columns, capacity, -1), 'cand', split_axis=0,...  3.93 us
    pallas_call x1, Pallas kernels, project_queries(): pl.pallas_call(query_kernel, in_specs=whole(4), out_specs=whole()[0], out...  3.29 us
    pallas_call x1, Pallas kernels, finish(): pl.pallas_call(functools.partial(finish_kernel, len(early), capacity, slo...  3.09 us
    pallas_call x1, Pallas kernels, prepare(): pl.pallas_call(functools.partial(prepare_kernel, columns, capacity, spans...  2.17 us
  transfers between devices with their start and end apart: 16, of which 7 were waited for; matrix products, arithmetic and copies ran while one was open for 2% of the time, Pallas kernels for 20%

profile of v10, /device:TPU:0, one launch (start us, length us, event | category | flops | bytes accessed | tf_op | source)
XLA Modules:
  0.0 103.8 jit_solution(6006650578726355287)
XLA Ops:
  0.0 0.7 copy-done.8
  0.7 2.2 %prepare.1 = (s32[8,512]{1,0:T(8,128)S(1)}, bf16[256,1024]{1,0:T(8,128)(2,1)}, bf16[256,1024]{1,0:T(8,128)(2,1)S(1)}) custom-call(s32[1,512]{1,0:T(1,128)S(1)} %bitcast.14, bf16[256,2048]{1,0:T(8,128)(2,1)} %bitcast.1.kv_hbm), custom_call_target="tpu_custom_call" | custom-call | flops 6000000000 | tf_op jit(solution)/shard_map/prepare/pallas_call | solution.py:141
  2.9 0.0 copy-start.6
  2.9 4.1 %collective-permute-start.1 = (bf16[256,1024]{1,0:T(8,128)(2,1)}, bf16[256,1024]{1,0:T(8,128)(2,1)}, u32[]{:S(2)}, u32[]{:S(2)}) collective-permute-start(bf16[256,1024]{1,0:T(8,128)(2,1)} %get-tuple-element.26.refs_2_), channel_id=1, source_target_pairs={{0,16},{8,24},{16,0},{24,8},{1,17},{9,25},{17,1},{25,9},{2,18},{10... | collective-permute-start | bytes 1572872 | tf_op jit(solution)/shard_map/ppermute | solution.py:364
  7.0 1.6 %collective-permute-start = (bf16[256,2048]{1,0:T(8,128)(2,1)}, bf16[256,2048]{1,0:T(8,128)(2,1)S(1)}, u32[]{:S(2)}, u32[]{:S(2)}) collective-permute-start(bf16[256,2048]{1,0:T(8,128)(2,1)} %bitcast.1.kv_hbm), channel_id=1, source_target_pairs={{0,8},{8,0},{16,24},{24,16},{1,9},{9,1},{17,25},{25,17},{2,10},{10... | collective-permute-start | bytes 3145736 | tf_op jit(solution)/shard_map/ppermute | solution.py:364
  8.6 0.0 copy-done.14
  8.6 3.3 %project_queries.1 = bf16[1024,1152]{1,0:T(8,128)(2,1)S(1)} custom-call(s32[8,512]{1,0:T(8,128)S(1)} %get-tuple-element.24.slot_ref, s32[1,512]{1,0:T(1,128)S(1)} %bitcast.16, bf16[512,1024]{1,0:T(8,128)(2,1)S(1)} %copy-done.3, bf16[1024,2048]{1,0:T(8,128)(2,1)S(1)} %copy-done), custom_call_target="tpu_custom_call" | custom-call | flops 2147483648 | bytes 5242880 | tf_op jit(solution)/shard_map/project_queries/pallas_call | solution.py:81
  11.9 0.0 copy-done.6
  11.9 0.0 copy-start.2
  11.9 1.4 %copy-done.2 = bf16[1024,1152]{1,0:T(8,128)(2,1)} copy-done((bf16[1024,1152]{1,0:T(8,128)(2,1)}, bf16[1024,1152]{1,0:T(8,128)(2,1)S(1)}, u32[]{:S(2)}) %copy-start.2) | copy-done | bytes 2359320
  13.3 3.9 %all-to-all-start = ((bf16[8,128,1152]{2,1,0:T(8,128)(2,1)}), bf16[8,128,1152]{2,1,0:T(8,128)(2,1)S(1)}, u32[]{:S(2)}, u32[]{:S(2)}) async-start(bf16[8,128,1152]{2,1,0:T(8,128)(2,1)} %bitcast.13), calls=%async_computation | async-start | bytes 4718592 | tf_op jit(solution)/shard_map/all_to_all | solution.py:419
  17.3 0.7 slice.42
  18.6 12.0 %collective-permute-done.1.refs_2_.refs_3_ = bf16[256,1024]{1,0:T(8,128)(2,1)} collective-permute-done((bf16[256,1024]{1,0:T(8,128)(2,1)}, bf16[256,1024]{1,0:T(8,128)(2,1)}, u32[]{:S(2)}, u32[]{:S(2)}) %collective-permute-start.1) | collective-permute-done | bytes 524320 | tf_op jit(solution)/shard_map/ppermute | solution.py:364
  30.6 0.0 collective-permute-start.8
  30.6 2.2 %copy-done.1 = bf16[1024,2048]{1,0:T(8,128)(2,1)S(1)} copy-done((bf16[1024,2048]{1,0:T(8,128)(2,1)S(1)}, bf16[1024,2048]{1,0:T(8,128)(2,1)}, u32[]{:S(2)}) %copy-start.1) | copy-done | bytes 4194328
  32.8 1.2 %copy-done.4 = bf16[512,1024]{1,0:T(8,128)(2,1)S(1)} copy-done((bf16[512,1024]{1,0:T(8,128)(2,1)S(1)}, bf16[512,1024]{1,0:T(8,128)(2,1)}, u32[]{:S(2)}) %copy-start.4) | copy-done | bytes 1048600
  34.0 1.4 %project_gate.1 = (bf16[512,1024]{1,0:T(8,128)(2,1)S(1)}, s32[8,128]{1,0:T(8,128)S(1)}) custom-call(bf16[512,1024]{1,0:T(8,128)(2,1)S(1)} %copy-done.4, bf16[1024,2048]{1,0:T(8,128)(2,1)S(1)} %copy-done.1), custom_call_target="tpu_custom_call" | custom-call | flops 1073741824 | bytes 4194304 | tf_op jit(solution)/shard_map/project_gate/pallas_call | solution.py:108
  35.4 0.0 copy-start.11
  35.4 1.0 copy-done.11
  36.3 0.7 pad_add_fusion.place_ref
  37.1 0.1 pad_add_fusion.1.place_ref
  37.1 0.0 copy-done.9
  37.1 4.1 %collective-permute-start.2 = (bf16[256,1024]{1,0:T(8,128)(2,1)}, bf16[256,1024]{1,0:T(8,128)(2,1)}, u32[]{:S(2)}, u32[]{:S(2)}) collective-permute-start(bf16[256,1024]{1,0:T(8,128)(2,1)} %collective-permute-done.1.refs_2_.refs_3_), channel_id=1, source_target_pairs={{0,8},{8,0},{16,24},{24,16},{1,9},{9,1},{17,25},{25,17},{2,10},{10... | collective-permute-start | bytes 1572872 | tf_op jit(solution)/shard_map/ppermute | solution.py:364
  41.3 14.9 %collective-permute-done.8.refs_1_.refs_6_ = bf16[256,1024]{1,0:T(8,128)(2,1)} collective-permute-done((bf16[256,1024]{1,0:T(8,128)(2,1)}, bf16[256,1024]{1,0:T(8,128)(2,1)}, u32[]{:S(2)}, u32[]{:S(2)}) %collective-permute-start.8) | collective-permute-done | bytes 524320 | tf_op jit(solution)/shard_map/ppermute | solution.py:364
  56.2 1.4 %collective-permute-start.9 = (bf16[256,1024]{1,0:T(8,128)(2,1)}, bf16[256,1024]{1,0:T(8,128)(2,1)}, u32[]{:S(2)}, u32[]{:S(2)}) collective-permute-start(bf16[256,1024]{1,0:T(8,128)(2,1)} %collective-permute-done.8.refs_1_.refs_6_), channel_id=1, source_target_pairs={{0,8},{8,0},{16,24},{24,16},{1,9},{9,1},{17,25},{25,17},{2,10},{10... | collective-permute-start | bytes 1572872 | tf_op jit(solution)/shard_map/ppermute | solution.py:364
  57.6 0.0 collective-permute-done.refs_1_.refs_4_.refs_7_
  57.6 0.3 slot_column.1
  58.0 0.7 copy-done.15
  58.6 0.0 all-to-all-done
  58.6 4.8 %attend.4.refs_2_ = f32[1024,512]{1,0:T(8,128)S(1)} custom-call(s32[5]{0:T(128)S(1)} %pad_add_fusion.1.place_ref, s32[8,128]{1,0:T(8,128)S(1)} %get-tuple-element.29.refs_0_, bf16[1024,1152]{1,0:T(8,128)(2,1)S(1)} %bitcast.9, bf16[256,1024]{1,0:T(8,128)(2,1)} %get-tuple-element.26.refs_2_, bf16[256,1024]{1,0:T(8,128)(2,1)} %collective-permute-done.1.refs_2_.refs_3_, ...), custom_call_target="tpu_custom_call" | custom-call | bytes 3670016 | tf_op jit(solution)/shard_map/attend/pallas_call | solution.py:272
  63.4 2.5 %collective-permute-done.2.refs_1_ = bf16[256,1024]{1,0:T(8,128)(2,1)} collective-permute-done((bf16[256,1024]{1,0:T(8,128)(2,1)}, bf16[256,1024]{1,0:T(8,128)(2,1)}, u32[]{:S(2)}, u32[]{:S(2)}) %collective-permute-start.2) | collective-permute-done | bytes 524320 | tf_op jit(solution)/shard_map/ppermute | solution.py:364
  65.9 2.5 %attend.5 = (bf16[512,512]{1,0:T(8,128)(2,1)S(1)}, bf16[256,512]{1,0:T(8,128)(2,1)S(1)}, bf16[256,512]{1,0:T(8,128)(2,1)S(1)}) custom-call(s32[3]{0:T(128)S(1)} %pad_add_fusion.place_ref, bf16[1024,1152]{1,0:T(8,128)(2,1)S(1)} %bitcast.10, bf16[256,1024]{1,0:T(8,128)(2,1)} %collective-permute-done.2.refs_1_, f32[1024,512]{1,0:T(8,128)S(1)} %attend.4.refs_2_), custom_call_target="tpu_custom_call" | custom-call | bytes 2621440 | tf_op jit(solution)/shard_map/attend/pallas_call | solution.py:272
  68.4 0.1 collective-permute-start.3
  68.5 0.5 collective-permute-start.5
  69.0 1.0 collective-permute-done.3.refs_1_
  70.1 1.6 %collective-permute-start.4 = (bf16[256,512]{1,0:T(8,128)(2,1)S(1)}, bf16[256,512]{1,0:T(8,128)(2,1)S(1)}, u32[]{:S(2)}, u32[]{:S(2)}) collective-permute-start(bf16[256,512]{1,0:T(8,128)(2,1)S(1)} %pad_maximum_fusion.refs_1_), channel_id=1, source_target_pairs={{0,2},{1,3},{2,0},{3,1},{4,6},{5,7},{6,4},{7,5},{8,10},{9,11},{10,... | collective-permute-start | bytes 786440 | tf_op jit(solution)/shard_map/ppermute | solution.py:364
  71.7 0.0 collective-permute-done.5
  71.7 1.6 %collective-permute-start.6 = (bf16[256,512]{1,0:T(8,128)(2,1)S(1)}, bf16[256,512]{1,0:T(8,128)(2,1)S(1)}, u32[]{:S(2)}, u32[]{:S(2)}) collective-permute-start(bf16[256,512]{1,0:T(8,128)(2,1)S(1)} %pad_maximum_fusion.1.refs_2_), channel_id=1, source_target_pairs={{0,4},{1,5},{2,6},{3,7},{4,0},{5,1},{6,2},{7,3},{8,12},{9,13},{10,... | collective-permute-start | bytes 786440 | tf_op jit(solution)/shard_map/ppermute | solution.py:364
  73.3 0.5 collective-permute-start.7
  73.8 4.6 %attend.6.refs_2_ = f32[1024,512]{1,0:T(8,128)S(1)} custom-call(s32[5]{0:T(128)S(1)} %pad_add_fusion.1.place_ref, s32[8,128]{1,0:T(8,128)S(1)} %wait_for.1.refs_0_, bf16[256,512]{1,0:T(8,128)(2,1)S(1)} %pad_maximum_fusion.refs_1_, bf16[256,512]{1,0:T(8,128)(2,1)S(1)} %pad_maximum_fusion.1.refs_2_, bf16[256,512]{1,0:T(8,128)(2,1)S(1)} %pad_maximum_fusion.2.refs_3_, ...), custom_call_target="tpu_custom_call" | custom-call | bytes 3670016 | tf_op jit(solution)/shard_map/attend/pallas_call | solution.py:272
  78.4 0.0 copy-start.16
  78.5 0.0 collective-permute-done.9.refs_1_
  78.5 2.8 %attend.7 = (bf16[512,512]{1,0:T(8,128)(2,1)S(1)}, bf16[256,512]{1,0:T(8,128)(2,1)S(1)}, bf16[256,512]{1,0:T(8,128)(2,1)S(1)}) custom-call(s32[3]{0:T(128)S(1)} %pad_add_fusion.place_ref, bf16[1024,1152]{1,0:T(8,128)(2,1)S(1)} %bitcast.12, bf16[256,1024]{1,0:T(8,128)(2,1)} %collective-permute-done.9.refs_1_, f32[1024,512]{1,0:T(8,128)S(1)} %attend.6.refs_2_), custom_call_target="tpu_custom_call" | custom-call | flops 10737418240 | bytes 2621440 | tf_op jit(solution)/shard_map/attend/pallas_call | solution.py:272
  81.2 0.1 collective-permute-start.10
  81.3 0.5 collective-permute-start.11
  81.8 0.0 collective-permute-done.4.refs_2_
  81.8 3.7 %collective-permute-done.6.refs_3_ = bf16[256,512]{1,0:T(8,128)(2,1)S(1)} collective-permute-done((bf16[256,512]{1,0:T(8,128)(2,1)S(1)}, bf16[256,512]{1,0:T(8,128)(2,1)S(1)}, u32[]{:S(2)}, u32[]{:S(2)}) %collective-permute-start.6) | collective-permute-done | bytes 262176 | tf_op jit(solution)/shard_map/ppermute | solution.py:364
  85.5 0.0 collective-permute-done.7.refs_4_
  85.5 0.7 collect.1.refs_0_
  86.2 0.0 copy-start.5
  86.2 0.0 copy-start.10
  86.2 0.0 copy-start.13
  86.2 0.0 collective-permute-done.10.refs_2_
  86.2 0.0 collective-permute-done.11
  86.3 1.2 %collective-permute-start.12 = (bf16[256,512]{1,0:T(8,128)(2,1)S(1)}, bf16[256,512]{1,0:T(8,128)(2,1)S(1)}, u32[]{:S(2)}, u32[]{:S(2)}) collective-permute-start(bf16[256,512]{1,0:T(8,128)(2,1)S(1)} %pad_maximum_fusion.3), channel_id=1, source_target_pairs={{0,2},{1,3},{2,0},{3,1},{4,6},{5,7},{6,4},{7,5},{8,10},{9,11},{10,... | collective-permute-start | bytes 786440 | tf_op jit(solution)/shard_map/ppermute | solution.py:364
  87.6 1.0 collective-permute-start.13
  88.6 1.5 %collective-permute-start.14 = (bf16[256,512]{1,0:T(8,128)(2,1)S(1)}, bf16[256,512]{1,0:T(8,128)(2,1)S(1)}, u32[]{:S(2)}, u32[]{:S(2)}) collective-permute-start(bf16[256,512]{1,0:T(8,128)(2,1)S(1)} %pad_maximum_fusion.5), channel_id=1, source_target_pairs={{0,6},{1,7},{2,4},{3,5},{4,2},{5,3},{6,0},{7,1},{8,14},{9,15},{10,... | collective-permute-start | bytes 786440 | tf_op jit(solution)/shard_map/ppermute | solution.py:364
  90.1 5.6 %collective-permute-done.12.refs_3_ = bf16[256,512]{1,0:T(8,128)(2,1)S(1)} collective-permute-done((bf16[256,512]{1,0:T(8,128)(2,1)S(1)}, bf16[256,512]{1,0:T(8,128)(2,1)S(1)}, u32[]{:S(2)}, u32[]{:S(2)}) %collective-permute-start.12) | collective-permute-done | bytes 262176 | tf_op jit(solution)/shard_map/ppermute | solution.py:364
  95.7 4.8 %collective-permute-done.13.refs_4_ = bf16[256,512]{1,0:T(8,128)(2,1)S(1)} collective-permute-done((bf16[256,512]{1,0:T(8,128)(2,1)S(1)}, bf16[256,512]{1,0:T(8,128)(2,1)S(1)}, u32[]{:S(2)}, u32[]{:S(2)}) %collective-permute-start.13) | collective-permute-done | bytes 262176 | tf_op jit(solution)/shard_map/ppermute | solution.py:364
  100.5 0.0 collective-permute-done.14.refs_5_
  100.5 0.0 copy-done.5
  100.5 0.0 copy-done.10
  100.5 0.0 copy-done.13
  100.5 3.1 %finish.1 = bf16[512,1024]{1,0:T(8,128)(2,1)} custom-call(s32[512,128]{1,0:T(8,128)S(1)} %copy-done.16, f32[1,1024]{1,0:T(1,128)S(1)} %bitcast.15, bf16[512,1024]{1,0:T(8,128)(2,1)S(1)} %copy-done.12, bf16[512,1024]{1,0:T(8,128)(2,1)S(1)} %copy-done.5, bf16[1024,1024]{1,0:T(8,128)(2,1)S(1)} %copy-done.10, bf16[512,512]{1,0:T(8,128)(2,1)S(1)} %collect.1.refs_0_, ...), custom_call_target="tpu_custom_call" | custom-call | flops 2147483648 | bytes 7340032 | tf_op jit(solution)/shard_map/finish/pallas_call | solution.py:349
  (32 shorter events, 0.3 us)
Async XLA Ops:
  0.0 0.7 copy-start.8
  0.7 7.9 %copy-start = (bf16[1024,2048]{1,0:T(8,128)(2,1)S(1)}, bf16[1024,2048]{1,0:T(8,128)(2,1)}, u32[]{:S(2)}) copy-start(bf16[1024,2048]{1,0:T(8,128)(2,1)} %w_ref.4) | copy-start | bytes 12582916
  0.7 7.9 %copy-start.3 = (bf16[512,1024]{1,0:T(8,128)(2,1)S(1)}, bf16[512,1024]{1,0:T(8,128)(2,1)}, u32[]{:S(2)}) copy-start(bf16[512,1024]{1,0:T(8,128)(2,1)} %x_ref.5) | copy-start | bytes 3145732
  0.7 7.9 %copy-start.14 = (s32[512]{0:T(512)S(1)}, s32[512]{0:T(512)}, u32[]{:S(2)}) copy-start(s32[512]{0:T(512)} %param.11) | copy-start | bytes 6148
  2.9 9.0 %copy-start.6 = (bf16[256,1024]{1,0:T(8,128)(2,1)}, bf16[256,1024]{1,0:T(8,128)(2,1)S(1)}, u32[]{:S(2)}) copy-start(bf16[256,1024]{1,0:T(8,128)(2,1)S(1)} %get-tuple-element.34.refs_5_) | copy-start | bytes 1572868
  2.9 27.7 %collective-permute-start.1 = (bf16[256,1024]{1,0:T(8,128)(2,1)}, bf16[256,1024]{1,0:T(8,128)(2,1)}, u32[]{:S(2)}, u32[]{:S(2)}) collective-permute-start(bf16[256,1024]{1,0:T(8,128)(2,1)} %get-tuple-element.26.refs_2_), channel_id=1, source_target_pairs={{0,16},{8,24},{16,0},{24,8},{1,17},{9,25},{17,1},{25,9},{2,18},{10... | collective-permute-start | bytes 1572872 | tf_op jit(solution)/shard_map/ppermute | solution.py:364
  7.0 50.6 %collective-permute-start = (bf16[256,2048]{1,0:T(8,128)(2,1)}, bf16[256,2048]{1,0:T(8,128)(2,1)S(1)}, u32[]{:S(2)}, u32[]{:S(2)}) collective-permute-start(bf16[256,2048]{1,0:T(8,128)(2,1)} %bitcast.1.kv_hbm), channel_id=1, source_target_pairs={{0,8},{8,0},{16,24},{24,16},{1,9},{9,1},{17,25},{25,17},{2,10},{10... | collective-permute-start | bytes 3145736 | tf_op jit(solution)/shard_map/ppermute | solution.py:364
  11.9 1.4 %copy-start.2 = (bf16[1024,1152]{1,0:T(8,128)(2,1)}, bf16[1024,1152]{1,0:T(8,128)(2,1)S(1)}, u32[]{:S(2)}) copy-start(bf16[1024,1152]{1,0:T(8,128)(2,1)S(1)} %project_queries.1) | copy-start | bytes 7077892
  13.3 3.9 %copy-start.17 = (s32[4]{0:T(128)S(1)}, s32[4]{0:T(128)}, u32[]{:S(2)}) copy-start(s32[4]{0:T(128)} %constant.10.clone) | copy-start | bytes 52
  13.3 45.3 %all-to-all-start = ((bf16[8,128,1152]{2,1,0:T(8,128)(2,1)}), bf16[8,128,1152]{2,1,0:T(8,128)(2,1)S(1)}, u32[]{:S(2)}, u32[]{:S(2)}) async-start(bf16[8,128,1152]{2,1,0:T(8,128)(2,1)} %bitcast.13), calls=%async_computation | async-start | bytes 4718592 | tf_op jit(solution)/shard_map/all_to_all | solution.py:419
  30.6 25.7 %collective-permute-start.8 = (bf16[256,1024]{1,0:T(8,128)(2,1)}, bf16[256,1024]{1,0:T(8,128)(2,1)}, u32[]{:S(2)}, u32[]{:S(2)}) collective-permute-start(bf16[256,1024]{1,0:T(8,128)(2,1)} %copy-done.6), channel_id=1, source_target_pairs={{0,16},{8,24},{16,0},{24,8},{1,17},{9,25},{17,1},{25,9},{2,18},{10... | collective-permute-start | bytes 1572872 | tf_op jit(solution)/shard_map/ppermute | solution.py:364
  30.6 2.2 %copy-start.1 = (bf16[1024,2048]{1,0:T(8,128)(2,1)S(1)}, bf16[1024,2048]{1,0:T(8,128)(2,1)}, u32[]{:S(2)}) copy-start(bf16[1024,2048]{1,0:T(8,128)(2,1)} %w_ref.4) | copy-start | bytes 12582916
  32.8 1.2 %copy-start.4 = (bf16[512,1024]{1,0:T(8,128)(2,1)S(1)}, bf16[512,1024]{1,0:T(8,128)(2,1)}, u32[]{:S(2)}) copy-start(bf16[512,1024]{1,0:T(8,128)(2,1)} %x_ref.5) | copy-start | bytes 3145732
  34.0 3.2 %copy-start.9 = (s32[512,1]{0,1:T(1,128)S(1)}, s32[512,1]{0,1:T(1,128)}, u32[]{:S(2)}) copy-start(s32[512,1]{0,1:T(1,128)} %param.10) | copy-start | bytes 6148
  35.4 1.0 copy-start.11
  37.1 28.8 %collective-permute-start.2 = (bf16[256,1024]{1,0:T(8,128)(2,1)}, bf16[256,1024]{1,0:T(8,128)(2,1)}, u32[]{:S(2)}, u32[]{:S(2)}) collective-permute-start(bf16[256,1024]{1,0:T(8,128)(2,1)} %collective-permute-done.1.refs_2_.refs_3_), channel_id=1, source_target_pairs={{0,8},{8,0},{16,24},{24,16},{1,9},{9,1},{17,25},{25,17},{2,10},{10... | collective-permute-start | bytes 1572872 | tf_op jit(solution)/shard_map/ppermute | solution.py:364
  56.2 22.2 %collective-permute-start.9 = (bf16[256,1024]{1,0:T(8,128)(2,1)}, bf16[256,1024]{1,0:T(8,128)(2,1)}, u32[]{:S(2)}, u32[]{:S(2)}) collective-permute-start(bf16[256,1024]{1,0:T(8,128)(2,1)} %collective-permute-done.8.refs_1_.refs_6_), channel_id=1, source_target_pairs={{0,8},{8,0},{16,24},{24,16},{1,9},{9,1},{17,25},{25,17},{2,10},{10... | collective-permute-start | bytes 1572872 | tf_op jit(solution)/shard_map/ppermute | solution.py:364
  57.9 0.7 copy-start.15
  68.4 1.6 %collective-permute-start.3 = (bf16[256,512]{1,0:T(8,128)(2,1)S(1)}, bf16[256,512]{1,0:T(8,128)(2,1)S(1)}, u32[]{:S(2)}, u32[]{:S(2)}) collective-permute-start(bf16[256,512]{1,0:T(8,128)(2,1)S(1)} %get-tuple-element.31), channel_id=1, source_target_pairs={{0,1},{1,0},{2,3},{3,2},{4,5},{5,4},{6,7},{7,6},{8,9},{9,8},{10,11... | collective-permute-start | bytes 786440 | tf_op jit(solution)/shard_map/ppermute | solution.py:364
  68.5 3.2 %collective-permute-start.5 = (bf16[256,512]{1,0:T(8,128)(2,1)S(1)}, bf16[256,512]{1,0:T(8,128)(2,1)S(1)}, u32[]{:S(2)}, u32[]{:S(2)}) collective-permute-start(bf16[256,512]{1,0:T(8,128)(2,1)S(1)} %get-tuple-element.32), channel_id=1, source_target_pairs={{0,1},{1,0},{2,3},{3,2},{4,5},{5,4},{6,7},{7,6},{8,9},{9,8},{10,11... | collective-permute-start | bytes 786440 | tf_op jit(solution)/shard_map/ppermute | solution.py:364
  69.0 4.8 %copy-start.7 = (bf16[256,1024]{1,0:T(8,128)(2,1)S(1)}, bf16[256,1024]{1,0:T(8,128)(2,1)}, u32[]{:S(2)}) copy-start(bf16[256,1024]{1,0:T(8,128)(2,1)} %copy-done.6) | copy-start | bytes 1572868
  70.1 11.7 %collective-permute-start.4 = (bf16[256,512]{1,0:T(8,128)(2,1)S(1)}, bf16[256,512]{1,0:T(8,128)(2,1)S(1)}, u32[]{:S(2)}, u32[]{:S(2)}) collective-permute-start(bf16[256,512]{1,0:T(8,128)(2,1)S(1)} %pad_maximum_fusion.refs_1_), channel_id=1, source_target_pairs={{0,2},{1,3},{2,0},{3,1},{4,6},{5,7},{6,4},{7,5},{8,10},{9,11},{10,... | collective-permute-start | bytes 786440 | tf_op jit(solution)/shard_map/ppermute | solution.py:364
  71.7 13.8 %collective-permute-start.6 = (bf16[256,512]{1,0:T(8,128)(2,1)S(1)}, bf16[256,512]{1,0:T(8,128)(2,1)S(1)}, u32[]{:S(2)}, u32[]{:S(2)}) collective-permute-start(bf16[256,512]{1,0:T(8,128)(2,1)S(1)} %pad_maximum_fusion.1.refs_2_), channel_id=1, source_target_pairs={{0,4},{1,5},{2,6},{3,7},{4,0},{5,1},{6,2},{7,3},{8,12},{9,13},{10,... | collective-permute-start | bytes 786440 | tf_op jit(solution)/shard_map/ppermute | solution.py:364
  73.3 12.1 %collective-permute-start.7 = (bf16[256,512]{1,0:T(8,128)(2,1)S(1)}, bf16[256,512]{1,0:T(8,128)(2,1)S(1)}, u32[]{:S(2)}, u32[]{:S(2)}) collective-permute-start(bf16[256,512]{1,0:T(8,128)(2,1)S(1)} %pad_maximum_fusion.2.refs_3_), channel_id=1, source_target_pairs={{0,6},{1,7},{2,4},{3,5},{4,2},{5,3},{6,0},{7,1},{8,14},{9,15},{10,... | collective-permute-start | bytes 786440 | tf_op jit(solution)/shard_map/ppermute | solution.py:364
  78.4 7.0 %copy-start.16 = (s32[512,128]{1,0:T(8,128)S(1)}, s32[512,128]{1,0:T(8,128)}, u32[]{:S(2)}) copy-start(s32[512,128]{1,0:T(8,128)} %copy-done.15) | copy-start | bytes 786436
  81.2 5.0 %collective-permute-start.10 = (bf16[256,512]{1,0:T(8,128)(2,1)S(1)}, bf16[256,512]{1,0:T(8,128)(2,1)S(1)}, u32[]{:S(2)}, u32[]{:S(2)}) collective-permute-start(bf16[256,512]{1,0:T(8,128)(2,1)S(1)} %get-tuple-element.36), channel_id=1, source_target_pairs={{0,1},{1,0},{2,3},{3,2},{4,5},{5,4},{6,7},{7,6},{8,9},{9,8},{10,11... | collective-permute-start | bytes 786440 | tf_op jit(solution)/shard_map/ppermute | solution.py:364
  81.3 5.0 %collective-permute-start.11 = (bf16[256,512]{1,0:T(8,128)(2,1)S(1)}, bf16[256,512]{1,0:T(8,128)(2,1)S(1)}, u32[]{:S(2)}, u32[]{:S(2)}) collective-permute-start(bf16[256,512]{1,0:T(8,128)(2,1)S(1)} %get-tuple-element.37), channel_id=1, source_target_pairs={{0,1},{1,0},{2,3},{3,2},{4,5},{5,4},{6,7},{7,6},{8,9},{9,8},{10,11... | collective-permute-start | bytes 786440 | tf_op jit(solution)/shard_map/ppermute | solution.py:364
  85.5 15.0 %copy-start.12 = (bf16[512,1024]{1,0:T(8,128)(2,1)S(1)}, bf16[512,1024]{1,0:T(8,128)(2,1)}, u32[]{:S(2)}) copy-start(bf16[512,1024]{1,0:T(8,128)(2,1)} %copy-done.11) | copy-start | bytes 3145732
  86.2 14.3 %copy-start.5 = (bf16[512,1024]{1,0:T(8,128)(2,1)S(1)}, bf16[512,1024]{1,0:T(8,128)(2,1)}, u32[]{:S(2)}) copy-start(bf16[512,1024]{1,0:T(8,128)(2,1)} %x_ref.5) | copy-start | bytes 3145732
  86.2 14.3 %copy-start.10 = (bf16[1024,1024]{1,0:T(8,128)(2,1)S(1)}, bf16[1024,1024]{1,0:T(8,128)(2,1)}, u32[]{:S(2)}) copy-start(bf16[1024,1024]{1,0:T(8,128)(2,1)} %w_ref.5) | copy-start | bytes 6291460
  86.2 14.3 %copy-start.13 = (f32[1024]{0:T(1024)S(1)}, f32[1024]{0:T(1024)}, u32[]{:S(2)}) copy-start(f32[1024]{0:T(1024)} %param.16) | copy-start | bytes 12292
  86.3 9.3 %collective-permute-start.12 = (bf16[256,512]{1,0:T(8,128)(2,1)S(1)}, bf16[256,512]{1,0:T(8,128)(2,1)S(1)}, u32[]{:S(2)}, u32[]{:S(2)}) collective-permute-start(bf16[256,512]{1,0:T(8,128)(2,1)S(1)} %pad_maximum_fusion.3), channel_id=1, source_target_pairs={{0,2},{1,3},{2,0},{3,1},{4,6},{5,7},{6,4},{7,5},{8,10},{9,11},{10,... | collective-permute-start | bytes 786440 | tf_op jit(solution)/shard_map/ppermute | solution.py:364
  87.6 12.9 %collective-permute-start.13 = (bf16[256,512]{1,0:T(8,128)(2,1)S(1)}, bf16[256,512]{1,0:T(8,128)(2,1)S(1)}, u32[]{:S(2)}, u32[]{:S(2)}) collective-permute-start(bf16[256,512]{1,0:T(8,128)(2,1)S(1)} %pad_maximum_fusion.4), channel_id=1, source_target_pairs={{0,4},{1,5},{2,6},{3,7},{4,0},{5,1},{6,2},{7,3},{8,12},{9,13},{10,... | collective-permute-start | bytes 786440 | tf_op jit(solution)/shard_map/ppermute | solution.py:364
  88.6 11.9 %collective-permute-start.14 = (bf16[256,512]{1,0:T(8,128)(2,1)S(1)}, bf16[256,512]{1,0:T(8,128)(2,1)S(1)}, u32[]{:S(2)}, u32[]{:S(2)}) collective-permute-start(bf16[256,512]{1,0:T(8,128)(2,1)S(1)} %pad_maximum_fusion.5), channel_id=1, source_target_pairs={{0,6},{1,7},{2,4},{3,5},{4,2},{5,3},{6,0},{7,1},{8,14},{9,15},{10,... | collective-permute-start | bytes 786440 | tf_op jit(solution)/shard_map/ppermute | solution.py:364

commit v11 on v10

--- a/solution.py
+++ b/solution.py
@@ -16,7 +16,7 @@
 BF16 = jnp.bfloat16
 MIB = 1024 * 1024
 TOKEN = jax.ShapeDtypeStruct((8, BLK), jnp.int32)
-WAIT_COST = 20.0
+WAIT_COST = 12.0
 LATE_SHARE = 20.0
 COLLECT_COST = 20.0
 SLOTS_COST = 6.0
@@ -187,18 +187,20 @@
     )(owner_row, *after)
 
 
-def attend_kernel(size, heads, first, starts, behind, has_base, capacity, place_ref, *refs):
+def attend_kernel(size, heads, first, starts, behind, has_base, capacity, length_ref, *refs):
     refs = refs[behind:]
     rows_ref, refs = refs[0], refs[1:]
     count = len(starts)
     parts = []
-    for _, _, pieces in starts:
+    for _, _, _, pieces in starts:
         parts.append(refs[:pieces])
         refs = refs[pieces:]
     base_ref = refs[0] if has_base else None
     outs = 3 if capacity else 1
     out_refs, shown = refs[int(has_base) : int(has_base) + outs], refs[int(has_base) + outs]
     result = out_refs[0] if outs == 1 else refs[-1]
+    me = lax.axis_index("cand")
+    places = [lax.axis_index("user") ^ start[0] for start in starts]
     slots = rows_ref.shape[0]
     columns_of = slots // capacity if capacity else 1
     keys = sum(piece.shape[0] for piece in parts[0])
@@ -206,7 +208,7 @@
     seen = rows_ref[:, HEADS * size :].astype(F32)
     for number in range(count):
         for block in range(blocks):
-            start = (place_ref[2 + number] * blocks + block).astype(F32)
+            start = (places[number] * blocks + block).astype(F32)
             shown[number * blocks + block] = (start < seen).astype(F32).astype(BF16)
     row = lax.broadcasted_iota(jnp.int32, (keys, size), 0)
     tile = min(512, slots)
@@ -220,8 +222,8 @@
     def one_head(head):
         values = []
         for number, part in enumerate(parts):
-            inside = row + place_ref[2 + number] * keys < place_ref[0]
-            value = read(part, (starts[number][1] + head) * size).astype(F32)
+            inside = row + places[number] * keys < length_ref[0]
+            value = read(part, (starts[number][2] + head) * size).astype(F32)
             values.append(jnp.where(inside, value, 0.0).astype(BF16))
         values = jnp.concatenate(values, axis=0)
         for start in range(0, slots, tile):
@@ -231,7 +233,7 @@
             for number, part in enumerate(parts):
                 scores = lax.dot_general(
                     queries,
-                    read(part, (starts[number][0] + head) * size),
+                    read(part, (starts[number][1] + head) * size),
                     (((1,), (1,)), ((), ())),
                     preferred_element_type=F32,
                 )
@@ -252,17 +254,17 @@
         numbers = list(range(0, columns_of, 2)) + list(range(1, columns_of, 2))
         for ref in out_refs:
             for start in range(0, ref.shape[0], capacity):
-                block = place_ref[1] ^ numbers.pop(0)
+                block = me ^ numbers.pop(0)
                 source = pl.ds(pl.multiple_of(block * capacity, capacity), capacity)
                 ref[start : start + capacity, :] = result[source, :]
 
 
-def attend(place, after, rows, segments, base, first, heads, size, capacity, dtype, share):
+def attend(length, after, rows, segments, base, first, heads, size, capacity, dtype, share):
     slots = rows.shape[0]
-    keys = sum(piece.shape[0] for piece in segments[0][0])
+    keys = sum(piece.shape[0] for piece in segments[0][1])
     count = len(segments)
-    starts = [(key, value, len(pieces)) for pieces, key, value in segments]
-    pieces = [piece for pieces, _, _ in segments for piece in pieces]
+    starts = [(place, key, value, len(pieces)) for place, pieces, key, value in segments]
+    pieces = [piece for _, pieces, _, _ in segments for piece in pieces]
     heights = [slots // 2, slots // 4, slots // 4] if capacity else [slots]
     outs = len(heights)
     extra = [] if base is None else [base]
@@ -286,7 +288,7 @@
             slots * keys * count * heads,
         ),
         name="attend",
-    )(place, *after, rows, *pieces, *extra)
+    )(length, *after, rows, *pieces, *extra)
 
 
 def placement(slot, slots):
@@ -396,12 +398,14 @@
     visible_row = visible.reshape(1, rows)
     spans = [(sum(GROUPS[:number]), heads) for number, heads in enumerate(GROUPS)]
 
+    gate, gated = project_gate(cand_x, w_in)
     row, *parts = prepare(owner_row, kv_cache[0], spans, size, columns, capacity)
+    send = project_queries(row, visible_row, cand_x, w_in, slots)
     near = None
     far = []
     for part in parts:
         if far:
-            part, _ = lax.optimization_barrier((part, far[-1]))
+            part, _ = lax.optimization_barrier((part, (far[-1], gated, send)))
         held = {0: part}
         bit = count // 2
         while bit > 1:
@@ -413,34 +417,25 @@
             near = swap(own, "user", 1, count)
         far.append(held)
     evens = sorted(far[0])
-    late = [key | 1 for key in evens[1:]]
-
-    send = project_queries(row, visible_row, cand_x, w_in, slots)
+
     got = lax.all_to_all(
         send.reshape(columns, capacity, -1), "cand", split_axis=0, concat_axis=0, tiled=True
     ).reshape(slots, -1)
-    gate, gated = project_gate(cand_x, w_in)
     arrived = [gated, near] + [far[0][key] for key in evens[1:]]
     slot, started = slot_column(owner_row ^ me, columns, capacity, arrived)
-    position = lax.axis_index("user").astype(jnp.int32)
-    shards = position ^ jnp.array(evens + [1] + late, jnp.int32)
-    head = jnp.concatenate([hist_len, me[None]])
-    place_ready = jnp.concatenate([head, shards[: len(evens) + 1]])
-    place_late = jnp.concatenate([head, shards[len(evens) + 1 :]])
-
     early = []
     after = [started]
     behind = None
     for number, (first, heads) in enumerate(spans):
         held = far[number]
-        cuts = [([swap(held[key], "user", 1, count)], 0, heads) for key in evens[1:]]
-        segments = [([held[key]], 0, heads) for key in evens]
-        segments.append(([near], first, HEADS + first))
+        cuts = [(key | 1, [swap(held[key], "user", 1, count)], 0, heads) for key in evens[1:]]
+        segments = [(key, [held[key]], 0, heads) for key in evens]
+        segments.append((1, [near], first, HEADS + first))
         base = attend(
-            place_ready, after, got, segments, None, first, heads, size, None, F32, 0.0
+            hist_len, after, got, segments, None, first, heads, size, None, F32, 0.0
         )[0]
         attn = attend(
-            place_late,
+            hist_len,
             [],
             got,
             cuts,

time: 104 us -> 104 us (level)
  waiting for transfers between devices: 44.5 us -> 46 us
    ppermute x15, waiting for transfers between devices: 44.5 us -> 46 us  [swap(): return lax.ppermute(array, axis, [(i, i ^ bits) for i in range(count)])]
    unnamed x36 -> x30, local copies, waits for them, and re-layouts: 7.22 us -> 7.2 us
  transfers between devices with their start and end apart: 16 -> 16, of which waited for: 7 -> 7; matrix products, arithmetic and copies ran while one was open for 2% -> 0% of each run, Pallas kernels for 20% -> 20%
where the time goes in v11:
time: 104 us
  waiting for transfers between devices  46 us (44%)
  Pallas kernels  25.9 us (25%)
  starting transfers between devices  23.5 us (23%)
  local copies, waits for them, and re-layouts  7.32 us (7%)
  between operations  1.14 us (1%)
    ppermute x15, waiting for transfers between devices, swap(): return lax.ppermute(array, axis, [(i, i ^ bits) for i in range(count)])  46 us
    ppermute x15, starting transfers between devices, swap(): return lax.ppermute(array, axis, [(i, i ^ bits) for i in range(count)])  19.7 us
    pallas_call x4, Pallas kernels, attend(): pl.pallas_call(functools.partial(attend_kernel, size, heads, first, start...  14.7 us
    unnamed x30, local copies, waits for them, and re-layouts  7.2 us
    all_to_all x1, starting transfers between devices, per_device(): lax.all_to_all(send.reshape(columns, capacity, -1), 'cand', split_axis=0,...  3.8 us
    pallas_call x1, Pallas kernels, project_queries(): pl.pallas_call(query_kernel, in_specs=whole(4), out_specs=whole()[0], out...  3.29 us
    pallas_call x1, Pallas kernels, finish(): pl.pallas_call(functools.partial(finish_kernel, len(early), capacity, slo...  3.1 us
    pallas_call x1, Pallas kernels, prepare(): pl.pallas_call(functools.partial(prepare_kernel, columns, capacity, spans...  2.36 us
  transfers between devices with their start and end apart: 16, of which 7 were waited for; matrix products, arithmetic and copies ran while one was open for 0% of the time, Pallas kernels for 20%

profile of v11, /device:TPU:0, one launch (start us, length us, event | category | flops | bytes accessed | tf_op | source)
XLA Modules:
  0.0 104.0 jit_solution(3808055961193506475)
XLA Ops:
  0.0 0.7 copy-done.6
  0.7 2.4 %prepare.1 = (s32[8,512]{1,0:T(8,128)S(1)}, bf16[256,1024]{1,0:T(8,128)(2,1)}, bf16[256,1024]{1,0:T(8,128)(2,1)}) custom-call(s32[1,512]{1,0:T(1,128)S(1)} %bitcast.12, bf16[256,2048]{1,0:T(8,128)(2,1)} %bitcast.1.kv_hbm), custom_call_target="tpu_custom_call" | custom-call | flops 6000000000 | tf_op jit(solution)/shard_map/prepare/pallas_call | solution.py:141
  3.1 4.1 %collective-permute-start.1 = (bf16[256,1024]{1,0:T(8,128)(2,1)}, bf16[256,1024]{1,0:T(8,128)(2,1)}, u32[]{:S(2)}, u32[]{:S(2)}) collective-permute-start(bf16[256,1024]{1,0:T(8,128)(2,1)} %get-tuple-element.26.refs_2_), channel_id=1, source_target_pairs={{0,16},{8,24},{16,0},{24,8},{1,17},{9,25},{17,1},{25,9},{2,18},{10... | collective-permute-start | bytes 1572872 | tf_op jit(solution)/shard_map/ppermute | solution.py:366
  7.2 1.6 %collective-permute-start = (bf16[256,2048]{1,0:T(8,128)(2,1)}, bf16[256,2048]{1,0:T(8,128)(2,1)S(1)}, u32[]{:S(2)}, u32[]{:S(2)}) collective-permute-start(bf16[256,2048]{1,0:T(8,128)(2,1)} %bitcast.1.kv_hbm), channel_id=1, source_target_pairs={{0,8},{8,0},{16,24},{24,16},{1,9},{9,1},{17,25},{25,17},{2,10},{10... | collective-permute-start | bytes 3145736 | tf_op jit(solution)/shard_map/ppermute | solution.py:366
  8.7 0.0 copy-done
  8.7 0.0 copy-done.3
  8.7 0.0 copy-done.12
  8.7 3.3 %project_queries.1 = bf16[1024,1152]{1,0:T(8,128)(2,1)S(1)} custom-call(s32[8,512]{1,0:T(8,128)S(1)} %get-tuple-element.24.slot_ref, s32[1,512]{1,0:T(1,128)S(1)} %bitcast.14, bf16[512,1024]{1,0:T(8,128)(2,1)S(1)} %copy-done.3, bf16[1024,2048]{1,0:T(8,128)(2,1)S(1)} %copy-done), custom_call_target="tpu_custom_call" | custom-call | flops 2147483648 | bytes 5242880 | tf_op jit(solution)/shard_map/project_queries/pallas_call | solution.py:81
  12.0 0.0 copy-start.2
  12.1 1.4 %copy-done.2 = bf16[1024,1152]{1,0:T(8,128)(2,1)} copy-done((bf16[1024,1152]{1,0:T(8,128)(2,1)}, bf16[1024,1152]{1,0:T(8,128)(2,1)S(1)}, u32[]{:S(2)}) %copy-start.2) | copy-done | bytes 2359320
  13.5 3.8 %all-to-all-start = ((bf16[8,128,1152]{2,1,0:T(8,128)(2,1)}), bf16[8,128,1152]{2,1,0:T(8,128)(2,1)S(1)}, u32[]{:S(2)}, u32[]{:S(2)}) async-start(bf16[8,128,1152]{2,1,0:T(8,128)(2,1)} %bitcast.11), calls=%async_computation | async-start | bytes 4718592 | tf_op jit(solution)/shard_map/all_to_all | solution.py:421
  17.3 0.0 copy-start.1
  17.3 2.2 %copy-done.1 = bf16[1024,2048]{1,0:T(8,128)(2,1)S(1)} copy-done((bf16[1024,2048]{1,0:T(8,128)(2,1)S(1)}, bf16[1024,2048]{1,0:T(8,128)(2,1)}, u32[]{:S(2)}) %copy-start.1) | copy-done | bytes 4194328
  19.5 1.2 %copy-done.4 = bf16[512,1024]{1,0:T(8,128)(2,1)S(1)} copy-done((bf16[512,1024]{1,0:T(8,128)(2,1)S(1)}, bf16[512,1024]{1,0:T(8,128)(2,1)}, u32[]{:S(2)}) %copy-start.4) | copy-done | bytes 1048600
  20.7 1.4 %project_gate.1 = (bf16[512,1024]{1,0:T(8,128)(2,1)S(1)}, s32[8,128]{1,0:T(8,128)S(1)}) custom-call(bf16[512,1024]{1,0:T(8,128)(2,1)S(1)} %copy-done.4, bf16[1024,2048]{1,0:T(8,128)(2,1)S(1)} %copy-done.1), custom_call_target="tpu_custom_call" | custom-call | flops 1073741824 | bytes 4194304 | tf_op jit(solution)/shard_map/project_gate/pallas_call | solution.py:108
  22.1 0.0 copy-start.9
  22.1 1.0 copy-done.9
  23.1 7.7 %collective-permute-done.1.refs_2_.refs_3_ = bf16[256,1024]{1,0:T(8,128)(2,1)} collective-permute-done((bf16[256,1024]{1,0:T(8,128)(2,1)}, bf16[256,1024]{1,0:T(8,128)(2,1)}, u32[]{:S(2)}, u32[]{:S(2)}) %collective-permute-start.1) | collective-permute-done | bytes 524320 | tf_op jit(solution)/shard_map/ppermute | solution.py:366
  30.7 0.0 collective-permute-start.8
  31.4 0.0 copy-done.7
  31.4 4.2 %collective-permute-start.2 = (bf16[256,1024]{1,0:T(8,128)(2,1)}, bf16[256,1024]{1,0:T(8,128)(2,1)}, u32[]{:S(2)}, u32[]{:S(2)}) collective-permute-start(bf16[256,1024]{1,0:T(8,128)(2,1)} %collective-permute-done.1.refs_2_.refs_3_), channel_id=1, source_target_pairs={{0,8},{8,0},{16,24},{24,16},{1,9},{9,1},{17,25},{25,17},{2,10},{10... | collective-permute-start | bytes 1572872 | tf_op jit(solution)/shard_map/ppermute | solution.py:366
  35.6 20.8 %collective-permute-done.8.refs_1_.refs_6_ = bf16[256,1024]{1,0:T(8,128)(2,1)} collective-permute-done((bf16[256,1024]{1,0:T(8,128)(2,1)}, bf16[256,1024]{1,0:T(8,128)(2,1)}, u32[]{:S(2)}, u32[]{:S(2)}) %collective-permute-start.8) | collective-permute-done | bytes 524320 | tf_op jit(solution)/shard_map/ppermute | solution.py:366
  56.4 1.4 %collective-permute-start.9 = (bf16[256,1024]{1,0:T(8,128)(2,1)}, bf16[256,1024]{1,0:T(8,128)(2,1)}, u32[]{:S(2)}, u32[]{:S(2)}) collective-permute-start(bf16[256,1024]{1,0:T(8,128)(2,1)} %collective-permute-done.8.refs_1_.refs_6_), channel_id=1, source_target_pairs={{0,8},{8,0},{16,24},{24,16},{1,9},{9,1},{17,25},{25,17},{2,10},{10... | collective-permute-start | bytes 1572872 | tf_op jit(solution)/shard_map/ppermute | solution.py:366
  57.8 0.0 collective-permute-done.refs_1_.refs_4_.refs_7_
  57.8 0.3 slot_column.1
  58.1 0.0 copy-start.13
  58.1 0.7 copy-done.13
  58.8 0.0 all-to-all-done
  58.8 4.8 %attend.4.refs_2_ = f32[1024,512]{1,0:T(8,128)S(1)} custom-call(s32[1]{0:T(128)S(6)} %copy.9.length_ref, s32[8,128]{1,0:T(8,128)S(1)} %get-tuple-element.29.refs_0_, bf16[1024,1152]{1,0:T(8,128)(2,1)S(1)} %bitcast.7, bf16[256,1024]{1,0:T(8,128)(2,1)} %get-tuple-element.26.refs_2_, bf16[256,1024]{1,0:T(8,128)(2,1)} %collective-permute-done.1.refs_2_.refs_3_, ...), custom_call_target="tpu_custom_call" | custom-call | bytes 3670016 | tf_op jit(solution)/shard_map/attend/pallas_call | solution.py:274
  63.6 2.5 %collective-permute-done.2.refs_1_ = bf16[256,1024]{1,0:T(8,128)(2,1)} collective-permute-done((bf16[256,1024]{1,0:T(8,128)(2,1)}, bf16[256,1024]{1,0:T(8,128)(2,1)}, u32[]{:S(2)}, u32[]{:S(2)}) %collective-permute-start.2) | collective-permute-done | bytes 524320 | tf_op jit(solution)/shard_map/ppermute | solution.py:366
  66.1 2.5 %attend.5 = (bf16[512,512]{1,0:T(8,128)(2,1)S(1)}, bf16[256,512]{1,0:T(8,128)(2,1)S(1)}, bf16[256,512]{1,0:T(8,128)(2,1)S(1)}) custom-call(s32[1]{0:T(128)S(6)} %copy.9.length_ref, bf16[1024,1152]{1,0:T(8,128)(2,1)S(1)} %bitcast.8, bf16[256,1024]{1,0:T(8,128)(2,1)} %collective-permute-done.2.refs_1_, f32[1024,512]{1,0:T(8,128)S(1)} %attend.4.refs_2_), custom_call_target="tpu_custom_call" | custom-call | bytes 2621440 | tf_op jit(solution)/shard_map/attend/pallas_call | solution.py:274
  68.6 0.1 collective-permute-start.3
  68.7 0.5 collective-permute-start.5
  69.2 1.0 collective-permute-done.3.refs_1_
  70.2 1.6 %collective-permute-start.4 = (bf16[256,512]{1,0:T(8,128)(2,1)S(1)}, bf16[256,512]{1,0:T(8,128)(2,1)S(1)}, u32[]{:S(2)}, u32[]{:S(2)}) collective-permute-start(bf16[256,512]{1,0:T(8,128)(2,1)S(1)} %pad_maximum_fusion.refs_1_), channel_id=1, source_target_pairs={{0,2},{1,3},{2,0},{3,1},{4,6},{5,7},{6,4},{7,5},{8,10},{9,11},{10,... | collective-permute-start | bytes 786440 | tf_op jit(solution)/shard_map/ppermute | solution.py:366
  71.8 0.0 collective-permute-done.5
  71.9 1.6 %collective-permute-start.6 = (bf16[256,512]{1,0:T(8,128)(2,1)S(1)}, bf16[256,512]{1,0:T(8,128)(2,1)S(1)}, u32[]{:S(2)}, u32[]{:S(2)}) collective-permute-start(bf16[256,512]{1,0:T(8,128)(2,1)S(1)} %pad_maximum_fusion.1.refs_2_), channel_id=1, source_target_pairs={{0,4},{1,5},{2,6},{3,7},{4,0},{5,1},{6,2},{7,3},{8,12},{9,13},{10,... | collective-permute-start | bytes 786440 | tf_op jit(solution)/shard_map/ppermute | solution.py:366
  73.5 0.5 collective-permute-start.7
  74.0 4.8 %attend.6.refs_2_ = f32[1024,512]{1,0:T(8,128)S(1)} custom-call(s32[1]{0:T(128)S(6)} %copy.9.length_ref, s32[8,128]{1,0:T(8,128)S(1)} %wait_for.1.refs_0_, bf16[256,512]{1,0:T(8,128)(2,1)S(1)} %pad_maximum_fusion.refs_1_, bf16[256,512]{1,0:T(8,128)(2,1)S(1)} %pad_maximum_fusion.1.refs_2_, bf16[256,512]{1,0:T(8,128)(2,1)S(1)} %pad_maximum_fusion.2.refs_3_, ...), custom_call_target="tpu_custom_call" | custom-call | bytes 3670016 | tf_op jit(solution)/shard_map/attend/pallas_call | solution.py:274
  78.8 0.0 copy-start.14
  78.8 0.0 collective-permute-done.9.refs_1_
  78.8 2.7 %attend.7 = (bf16[512,512]{1,0:T(8,128)(2,1)S(1)}, bf16[256,512]{1,0:T(8,128)(2,1)S(1)}, bf16[256,512]{1,0:T(8,128)(2,1)S(1)}) custom-call(s32[1]{0:T(128)S(6)} %copy.9.length_ref, bf16[1024,1152]{1,0:T(8,128)(2,1)S(1)} %bitcast.10, bf16[256,1024]{1,0:T(8,128)(2,1)} %collective-permute-done.9.refs_1_, f32[1024,512]{1,0:T(8,128)S(1)} %attend.6.refs_2_), custom_call_target="tpu_custom_call" | custom-call | flops 10737418240 | bytes 2621440 | tf_op jit(solution)/shard_map/attend/pallas_call | solution.py:274
  81.5 0.1 collective-permute-start.10
  81.6 0.5 collective-permute-start.11
  82.1 0.0 collective-permute-done.4.refs_2_
  82.1 3.5 %collective-permute-done.6.refs_3_ = bf16[256,512]{1,0:T(8,128)(2,1)S(1)} collective-permute-done((bf16[256,512]{1,0:T(8,128)(2,1)S(1)}, bf16[256,512]{1,0:T(8,128)(2,1)S(1)}, u32[]{:S(2)}, u32[]{:S(2)}) %collective-permute-start.6) | collective-permute-done | bytes 262176 | tf_op jit(solution)/shard_map/ppermute | solution.py:366
  85.6 0.0 collective-permute-done.7.refs_4_
  85.6 0.0 copy-done.14
  85.7 0.7 collect.1.refs_0_
  86.4 0.0 copy-start.5
  86.4 0.0 copy-start.8
  86.4 0.0 copy-start.11
  86.4 0.0 collective-permute-done.10.refs_2_
  86.4 0.0 collective-permute-done.11
  86.5 1.2 %collective-permute-start.12 = (bf16[256,512]{1,0:T(8,128)(2,1)S(1)}, bf16[256,512]{1,0:T(8,128)(2,1)S(1)}, u32[]{:S(2)}, u32[]{:S(2)}) collective-permute-start(bf16[256,512]{1,0:T(8,128)(2,1)S(1)} %pad_maximum_fusion.3), channel_id=1, source_target_pairs={{0,2},{1,3},{2,0},{3,1},{4,6},{5,7},{6,4},{7,5},{8,10},{9,11},{10,... | collective-permute-start | bytes 786440 | tf_op jit(solution)/shard_map/ppermute | solution.py:366
  87.7 1.0 collective-permute-start.13
  88.8 1.5 %collective-permute-start.14 = (bf16[256,512]{1,0:T(8,128)(2,1)S(1)}, bf16[256,512]{1,0:T(8,128)(2,1)S(1)}, u32[]{:S(2)}, u32[]{:S(2)}) collective-permute-start(bf16[256,512]{1,0:T(8,128)(2,1)S(1)} %pad_maximum_fusion.5), channel_id=1, source_target_pairs={{0,6},{1,7},{2,4},{3,5},{4,2},{5,3},{6,0},{7,1},{8,14},{9,15},{10,... | collective-permute-start | bytes 786440 | tf_op jit(solution)/shard_map/ppermute | solution.py:366
  90.3 5.6 %collective-permute-done.12.refs_3_ = bf16[256,512]{1,0:T(8,128)(2,1)S(1)} collective-permute-done((bf16[256,512]{1,0:T(8,128)(2,1)S(1)}, bf16[256,512]{1,0:T(8,128)(2,1)S(1)}, u32[]{:S(2)}, u32[]{:S(2)}) %collective-permute-start.12) | collective-permute-done | bytes 262176 | tf_op jit(solution)/shard_map/ppermute | solution.py:366
  95.8 4.8 %collective-permute-done.13.refs_4_ = bf16[256,512]{1,0:T(8,128)(2,1)S(1)} collective-permute-done((bf16[256,512]{1,0:T(8,128)(2,1)S(1)}, bf16[256,512]{1,0:T(8,128)(2,1)S(1)}, u32[]{:S(2)}, u32[]{:S(2)}) %collective-permute-start.13) | collective-permute-done | bytes 262176 | tf_op jit(solution)/shard_map/ppermute | solution.py:366
  100.7 0.0 collective-permute-done.14.refs_5_
  100.7 0.0 copy-done.10
  100.7 0.0 copy-done.5
  100.7 0.0 copy-done.8
  100.7 3.1 %finish.1 = bf16[512,1024]{1,0:T(8,128)(2,1)} custom-call(s32[512,128]{1,0:T(8,128)S(1)} %copy-done.14, f32[1,1024]{1,0:T(1,128)S(1)} %bitcast.13, bf16[512,1024]{1,0:T(8,128)(2,1)S(1)} %copy-done.10, bf16[512,1024]{1,0:T(8,128)(2,1)S(1)} %copy-done.5, bf16[1024,1024]{1,0:T(8,128)(2,1)S(1)} %copy-done.8, bf16[512,512]{1,0:T(8,128)(2,1)S(1)} %collect.1.refs_0_, ...), custom_call_target="tpu_custom_call" | custom-call | flops 2147483648 | bytes 7340032 | tf_op jit(solution)/shard_map/finish/pallas_call | solution.py:351
  (22 shorter events, 0.2 us)
Async XLA Ops:
  0.0 0.7 copy-start.6
  0.7 8.1 %copy-start = (bf16[1024,2048]{1,0:T(8,128)(2,1)S(1)}, bf16[1024,2048]{1,0:T(8,128)(2,1)}, u32[]{:S(2)}) copy-start(bf16[1024,2048]{1,0:T(8,128)(2,1)} %w_ref.4) | copy-start | bytes 12582916
  0.7 8.1 %copy-start.3 = (bf16[512,1024]{1,0:T(8,128)(2,1)S(1)}, bf16[512,1024]{1,0:T(8,128)(2,1)}, u32[]{:S(2)}) copy-start(bf16[512,1024]{1,0:T(8,128)(2,1)} %x_ref.5) | copy-start | bytes 3145732
  0.7 8.1 %copy-start.12 = (s32[512]{0:T(512)S(1)}, s32[512]{0:T(512)}, u32[]{:S(2)}) copy-start(s32[512]{0:T(512)} %param.10) | copy-start | bytes 6148
  3.1 27.7 %collective-permute-start.1 = (bf16[256,1024]{1,0:T(8,128)(2,1)}, bf16[256,1024]{1,0:T(8,128)(2,1)}, u32[]{:S(2)}, u32[]{:S(2)}) collective-permute-start(bf16[256,1024]{1,0:T(8,128)(2,1)} %get-tuple-element.26.refs_2_), channel_id=1, source_target_pairs={{0,16},{8,24},{16,0},{24,8},{1,17},{9,25},{17,1},{25,9},{2,18},{10... | collective-permute-start | bytes 1572872 | tf_op jit(solution)/shard_map/ppermute | solution.py:366
  7.2 50.6 %collective-permute-start = (bf16[256,2048]{1,0:T(8,128)(2,1)}, bf16[256,2048]{1,0:T(8,128)(2,1)S(1)}, u32[]{:S(2)}, u32[]{:S(2)}) collective-permute-start(bf16[256,2048]{1,0:T(8,128)(2,1)} %bitcast.1.kv_hbm), channel_id=1, source_target_pairs={{0,8},{8,0},{16,24},{24,16},{1,9},{9,1},{17,25},{25,17},{2,10},{10... | collective-permute-start | bytes 3145736 | tf_op jit(solution)/shard_map/ppermute | solution.py:366
  12.0 1.4 %copy-start.2 = (bf16[1024,1152]{1,0:T(8,128)(2,1)}, bf16[1024,1152]{1,0:T(8,128)(2,1)S(1)}, u32[]{:S(2)}) copy-start(bf16[1024,1152]{1,0:T(8,128)(2,1)S(1)} %project_queries.1) | copy-start | bytes 7077892
  13.5 45.3 %all-to-all-start = ((bf16[8,128,1152]{2,1,0:T(8,128)(2,1)}), bf16[8,128,1152]{2,1,0:T(8,128)(2,1)S(1)}, u32[]{:S(2)}, u32[]{:S(2)}) async-start(bf16[8,128,1152]{2,1,0:T(8,128)(2,1)} %bitcast.11), calls=%async_computation | async-start | bytes 4718592 | tf_op jit(solution)/shard_map/all_to_all | solution.py:421
  17.3 2.2 %copy-start.1 = (bf16[1024,2048]{1,0:T(8,128)(2,1)S(1)}, bf16[1024,2048]{1,0:T(8,128)(2,1)}, u32[]{:S(2)}) copy-start(bf16[1024,2048]{1,0:T(8,128)(2,1)} %w_ref.4) | copy-start | bytes 12582916
  19.5 1.2 %copy-start.4 = (bf16[512,1024]{1,0:T(8,128)(2,1)S(1)}, bf16[512,1024]{1,0:T(8,128)(2,1)}, u32[]{:S(2)}) copy-start(bf16[512,1024]{1,0:T(8,128)(2,1)} %x_ref.5) | copy-start | bytes 3145732
  20.7 10.7 %copy-start.7 = (s32[512,1]{0,1:T(1,128)S(1)}, s32[512,1]{0,1:T(1,128)}, u32[]{:S(2)}) copy-start(s32[512,1]{0,1:T(1,128)} %param.9) | copy-start | bytes 6148
  22.1 1.0 copy-start.9
  30.7 25.7 %collective-permute-start.8 = (bf16[256,1024]{1,0:T(8,128)(2,1)}, bf16[256,1024]{1,0:T(8,128)(2,1)}, u32[]{:S(2)}, u32[]{:S(2)}) collective-permute-start(bf16[256,1024]{1,0:T(8,128)(2,1)} %get-tuple-element.34.refs_5_), channel_id=1, source_target_pairs={{0,16},{8,24},{16,0},{24,8},{1,17},{9,25},{17,1},{25,9},{2,18},{10... | collective-permute-start | bytes 1572872 | tf_op jit(solution)/shard_map/ppermute | solution.py:366
  31.4 34.7 %collective-permute-start.2 = (bf16[256,1024]{1,0:T(8,128)(2,1)}, bf16[256,1024]{1,0:T(8,128)(2,1)}, u32[]{:S(2)}, u32[]{:S(2)}) collective-permute-start(bf16[256,1024]{1,0:T(8,128)(2,1)} %collective-permute-done.1.refs_2_.refs_3_), channel_id=1, source_target_pairs={{0,8},{8,0},{16,24},{24,16},{1,9},{9,1},{17,25},{25,17},{2,10},{10... | collective-permute-start | bytes 1572872 | tf_op jit(solution)/shard_map/ppermute | solution.py:366
  56.4 22.4 %collective-permute-start.9 = (bf16[256,1024]{1,0:T(8,128)(2,1)}, bf16[256,1024]{1,0:T(8,128)(2,1)}, u32[]{:S(2)}, u32[]{:S(2)}) collective-permute-start(bf16[256,1024]{1,0:T(8,128)(2,1)} %collective-permute-done.8.refs_1_.refs_6_), channel_id=1, source_target_pairs={{0,8},{8,0},{16,24},{24,16},{1,9},{9,1},{17,25},{25,17},{2,10},{10... | collective-permute-start | bytes 1572872 | tf_op jit(solution)/shard_map/ppermute | solution.py:366
  58.1 0.7 copy-start.13
  68.6 1.6 %collective-permute-start.3 = (bf16[256,512]{1,0:T(8,128)(2,1)S(1)}, bf16[256,512]{1,0:T(8,128)(2,1)S(1)}, u32[]{:S(2)}, u32[]{:S(2)}) collective-permute-start(bf16[256,512]{1,0:T(8,128)(2,1)S(1)} %get-tuple-element.31), channel_id=1, source_target_pairs={{0,1},{1,0},{2,3},{3,2},{4,5},{5,4},{6,7},{7,6},{8,9},{9,8},{10,11... | collective-permute-start | bytes 786440 | tf_op jit(solution)/shard_map/ppermute | solution.py:366
  68.7 3.2 %collective-permute-start.5 = (bf16[256,512]{1,0:T(8,128)(2,1)S(1)}, bf16[256,512]{1,0:T(8,128)(2,1)S(1)}, u32[]{:S(2)}, u32[]{:S(2)}) collective-permute-start(bf16[256,512]{1,0:T(8,128)(2,1)S(1)} %get-tuple-element.32), channel_id=1, source_target_pairs={{0,1},{1,0},{2,3},{3,2},{4,5},{5,4},{6,7},{7,6},{8,9},{9,8},{10,11... | collective-permute-start | bytes 786440 | tf_op jit(solution)/shard_map/ppermute | solution.py:366
  70.2 11.9 %collective-permute-start.4 = (bf16[256,512]{1,0:T(8,128)(2,1)S(1)}, bf16[256,512]{1,0:T(8,128)(2,1)S(1)}, u32[]{:S(2)}, u32[]{:S(2)}) collective-permute-start(bf16[256,512]{1,0:T(8,128)(2,1)S(1)} %pad_maximum_fusion.refs_1_), channel_id=1, source_target_pairs={{0,2},{1,3},{2,0},{3,1},{4,6},{5,7},{6,4},{7,5},{8,10},{9,11},{10,... | collective-permute-start | bytes 786440 | tf_op jit(solution)/shard_map/ppermute | solution.py:366
  71.9 13.8 %collective-permute-start.6 = (bf16[256,512]{1,0:T(8,128)(2,1)S(1)}, bf16[256,512]{1,0:T(8,128)(2,1)S(1)}, u32[]{:S(2)}, u32[]{:S(2)}) collective-permute-start(bf16[256,512]{1,0:T(8,128)(2,1)S(1)} %pad_maximum_fusion.1.refs_2_), channel_id=1, source_target_pairs={{0,4},{1,5},{2,6},{3,7},{4,0},{5,1},{6,2},{7,3},{8,12},{9,13},{10,... | collective-permute-start | bytes 786440 | tf_op jit(solution)/shard_map/ppermute | solution.py:366
  73.5 12.1 %collective-permute-start.7 = (bf16[256,512]{1,0:T(8,128)(2,1)S(1)}, bf16[256,512]{1,0:T(8,128)(2,1)S(1)}, u32[]{:S(2)}, u32[]{:S(2)}) collective-permute-start(bf16[256,512]{1,0:T(8,128)(2,1)S(1)} %pad_maximum_fusion.2.refs_3_), channel_id=1, source_target_pairs={{0,6},{1,7},{2,4},{3,5},{4,2},{5,3},{6,0},{7,1},{8,14},{9,15},{10,... | collective-permute-start | bytes 786440 | tf_op jit(solution)/shard_map/ppermute | solution.py:366
  78.8 6.9 %copy-start.14 = (s32[512,128]{1,0:T(8,128)S(1)}, s32[512,128]{1,0:T(8,128)}, u32[]{:S(2)}) copy-start(s32[512,128]{1,0:T(8,128)} %copy-done.13) | copy-start | bytes 786436
  81.5 4.9 %collective-permute-start.10 = (bf16[256,512]{1,0:T(8,128)(2,1)S(1)}, bf16[256,512]{1,0:T(8,128)(2,1)S(1)}, u32[]{:S(2)}, u32[]{:S(2)}) collective-permute-start(bf16[256,512]{1,0:T(8,128)(2,1)S(1)} %get-tuple-element.36), channel_id=1, source_target_pairs={{0,1},{1,0},{2,3},{3,2},{4,5},{5,4},{6,7},{7,6},{8,9},{9,8},{10,11... | collective-permute-start | bytes 786440 | tf_op jit(solution)/shard_map/ppermute | solution.py:366
  81.6 4.8 %collective-permute-start.11 = (bf16[256,512]{1,0:T(8,128)(2,1)S(1)}, bf16[256,512]{1,0:T(8,128)(2,1)S(1)}, u32[]{:S(2)}, u32[]{:S(2)}) collective-permute-start(bf16[256,512]{1,0:T(8,128)(2,1)S(1)} %get-tuple-element.37), channel_id=1, source_target_pairs={{0,1},{1,0},{2,3},{3,2},{4,5},{5,4},{6,7},{7,6},{8,9},{9,8},{10,11... | collective-permute-start | bytes 786440 | tf_op jit(solution)/shard_map/ppermute | solution.py:366
  85.6 15.0 %copy-start.10 = (bf16[512,1024]{1,0:T(8,128)(2,1)S(1)}, bf16[512,1024]{1,0:T(8,128)(2,1)}, u32[]{:S(2)}) copy-start(bf16[512,1024]{1,0:T(8,128)(2,1)} %copy-done.9) | copy-start | bytes 3145732
  86.4 14.3 %copy-start.5 = (bf16[512,1024]{1,0:T(8,128)(2,1)S(1)}, bf16[512,1024]{1,0:T(8,128)(2,1)}, u32[]{:S(2)}) copy-start(bf16[512,1024]{1,0:T(8,128)(2,1)} %x_ref.5) | copy-start | bytes 3145732
  86.4 14.3 %copy-start.8 = (bf16[1024,1024]{1,0:T(8,128)(2,1)S(1)}, bf16[1024,1024]{1,0:T(8,128)(2,1)}, u32[]{:S(2)}) copy-start(bf16[1024,1024]{1,0:T(8,128)(2,1)} %w_ref.5) | copy-start | bytes 6291460
  86.4 14.3 %copy-start.11 = (f32[1024]{0:T(1024)S(1)}, f32[1024]{0:T(1024)}, u32[]{:S(2)}) copy-start(f32[1024]{0:T(1024)} %param.15) | copy-start | bytes 12292
  86.5 9.3 %collective-permute-start.12 = (bf16[256,512]{1,0:T(8,128)(2,1)S(1)}, bf16[256,512]{1,0:T(8,128)(2,1)S(1)}, u32[]{:S(2)}, u32[]{:S(2)}) collective-permute-start(bf16[256,512]{1,0:T(8,128)(2,1)S(1)} %pad_maximum_fusion.3), channel_id=1, source_target_pairs={{0,2},{1,3},{2,0},{3,1},{4,6},{5,7},{6,4},{7,5},{8,10},{9,11},{10,... | collective-permute-start | bytes 786440 | tf_op jit(solution)/shard_map/ppermute | solution.py:366
  87.7 12.9 %collective-permute-start.13 = (bf16[256,512]{1,0:T(8,128)(2,1)S(1)}, bf16[256,512]{1,0:T(8,128)(2,1)S(1)}, u32[]{:S(2)}, u32[]{:S(2)}) collective-permute-start(bf16[256,512]{1,0:T(8,128)(2,1)S(1)} %pad_maximum_fusion.4), channel_id=1, source_target_pairs={{0,4},{1,5},{2,6},{3,7},{4,0},{5,1},{6,2},{7,3},{8,12},{9,13},{10,... | collective-permute-start | bytes 786440 | tf_op jit(solution)/shard_map/ppermute | solution.py:366
  88.8 11.9 %collective-permute-start.14 = (bf16[256,512]{1,0:T(8,128)(2,1)S(1)}, bf16[256,512]{1,0:T(8,128)(2,1)S(1)}, u32[]{:S(2)}, u32[]{:S(2)}) collective-permute-start(bf16[256,512]{1,0:T(8,128)(2,1)S(1)} %pad_maximum_fusion.5), channel_id=1, source_target_pairs={{0,6},{1,7},{2,4},{3,5},{4,2},{5,3},{6,0},{7,1},{8,14},{9,15},{10,... | collective-permute-start | bytes 786440 | tf_op jit(solution)/shard_map/ppermute | solution.py:366

commit v12 on v11

--- a/solution.py
+++ b/solution.py
@@ -11,12 +11,13 @@
 HEADS = 8
 BLK = 128
 GROUPS = (4, 4)
+PIECES = (1, 1)
 norm_eps = 1e-06
 F32 = jnp.float32
 BF16 = jnp.bfloat16
 MIB = 1024 * 1024
 TOKEN = jax.ShapeDtypeStruct((8, BLK), jnp.int32)
-WAIT_COST = 12.0
+WAIT_COST = 20.0
 LATE_SHARE = 20.0
 COLLECT_COST = 20.0
 SLOTS_COST = 6.0
@@ -119,15 +120,18 @@
 
 
 def prepare_kernel(columns, capacity, spans, size, owner_ref, kv_hbm, row_ref, *refs):
-    part_refs, sems = refs[:-1], refs[-1]
-    width = kv_hbm.shape[1] // 2
+    part_refs, sems = list(refs[:-1]), refs[-1]
+    keys, width = kv_hbm.shape[0], kv_hbm.shape[1] // 2
     copies = []
-    for (first, heads), ref in zip(spans, part_refs):
-        wide = heads * size
-        for start in (0, width):
-            source = kv_hbm.at[:, start + first * size : start + first * size + wide]
-            target = ref.at[:, wide * (start > 0) : wide * (start > 0) + wide]
-            copies.append(pltpu.make_async_copy(source, target, sems.at[len(copies)]))
+    for (first, heads), count in zip(spans, PIECES):
+        wide, height = heads * size, keys // count
+        for number in range(count):
+            ref = part_refs.pop(0)
+            for half in range(2):
+                start = half * width + first * size
+                source = kv_hbm.at[number * height : (number + 1) * height, start : start + wide]
+                target = ref.at[:, half * wide : (half + 1) * wide]
+                copies.append(pltpu.make_async_copy(source, target, sems.at[len(copies)]))
     for copy in copies:
         copy.start()
     row = slot_row(owner_ref[...], columns, capacity)
@@ -137,18 +141,21 @@
 
 
 def prepare(owner_row, kv, spans, size, columns, capacity):
-    rows = kv.shape[0]
-    return pl.pallas_call(
+    shapes = []
+    for (_, heads), count in zip(spans, PIECES):
+        shape = (kv.shape[0] // count, 2 * heads * size)
+        shapes += [jax.ShapeDtypeStruct(shape, BF16)] * count
+    row, *parts = pl.pallas_call(
         functools.partial(prepare_kernel, columns, capacity, spans, size),
         in_specs=whole() + [pl.BlockSpec(memory_space=pl.ANY)],
-        out_specs=whole(1 + len(spans)),
-        out_shape=[jax.ShapeDtypeStruct((8, owner_row.shape[1]), jnp.int32)]
-        + [jax.ShapeDtypeStruct((rows, 2 * heads * size), BF16) for _, heads in spans],
-        scratch_shapes=[pltpu.SemaphoreType.DMA((2 * len(spans),))],
+        out_specs=whole(1 + len(shapes)),
+        out_shape=[jax.ShapeDtypeStruct((8, owner_row.shape[1]), jnp.int32)] + shapes,
+        scratch_shapes=[pltpu.SemaphoreType.DMA((2 * len(shapes),))],
         compiler_params=params(KERNEL_MIB),
         cost_estimate=cost(SLOTS_COST * 1e9, 0),
         name="prepare",
     )(owner_row, kv)
+    return row, [[parts.pop(0) for _ in range(count)] for count in PIECES]
 
 
 def wait_kernel(*refs):
@@ -366,6 +373,17 @@
     return lax.ppermute(array, axis, [(i, i ^ bits) for i in range(count)])
 
 
+def tied(arrays, behind):
+    return lax.optimization_barrier((arrays, behind))[0]
+
+
+def neighbours(pieces, count):
+    back = []
+    for piece in pieces:
+        back.append(swap(tied(piece, back[-1]) if back else piece, "user", 1, count))
+    return back
+
+
 def exchange_cores(even, odds, capacity, count, behind):
     others = [swap(odd, "cand", 1, count) for odd in odds]
     if behind is not None:
@@ -399,38 +417,42 @@
     spans = [(sum(GROUPS[:number]), heads) for number, heads in enumerate(GROUPS)]
 
     gate, gated = project_gate(cand_x, w_in)
-    row, *parts = prepare(owner_row, kv_cache[0], spans, size, columns, capacity)
+    row, parts = prepare(owner_row, kv_cache[0], spans, size, columns, capacity)
     send = project_queries(row, visible_row, cand_x, w_in, slots)
-    near = None
     far = []
-    for part in parts:
+    for number, pieces in enumerate(parts):
         if far:
-            part, _ = lax.optimization_barrier((part, (far[-1], gated, send)))
-        held = {0: part}
+            pieces = tied(pieces, (far[-1], gated, send))
+        held = {0: pieces}
         bit = count // 2
         while bit > 1:
             for key in sorted(held):
-                held[key | bit] = swap(held[key], "user", bit, count)
+                held[key | bit] = [swap(piece, "user", bit, count) for piece in held[key]]
             bit //= 2
-        if near is None:
-            own, _ = lax.optimization_barrier((kv_cache[0], row))
-            near = swap(own, "user", 1, count)
         far.append(held)
     evens = sorted(far[0])
+    near = []
+    for number, pieces in enumerate(parts):
+        if number:
+            pieces = tied(pieces, [far[number][key] for key in evens[1:]])
+        near.append(neighbours(pieces, count))
 
     got = lax.all_to_all(
         send.reshape(columns, capacity, -1), "cand", split_axis=0, concat_axis=0, tiled=True
     ).reshape(slots, -1)
-    arrived = [gated, near] + [far[0][key] for key in evens[1:]]
+    arrived = [gated] + near[0]
+    for key in evens[1:]:
+        arrived += far[0][key]
     slot, started = slot_column(owner_row ^ me, columns, capacity, arrived)
     early = []
     after = [started]
     behind = None
     for number, (first, heads) in enumerate(spans):
         held = far[number]
-        cuts = [(key | 1, [swap(held[key], "user", 1, count)], 0, heads) for key in evens[1:]]
-        segments = [(key, [held[key]], 0, heads) for key in evens]
-        segments.append((1, [near], first, HEADS + first))
+        close = (1, near[number], 0, heads)
+        segments = [(key, held[key], 0, heads) for key in evens] + [close] * (number == 0)
+        cuts = [(key | 1, neighbours(held[key], count), 0, heads) for key in evens[1:]]
+        cuts += [close] * (number > 0)
         base = attend(
             hist_len, after, got, segments, None, first, heads, size, None, F32, 0.0
         )[0]
@@ -450,7 +472,9 @@
         here, pairs = exchange_cores(attn[0], attn[1:], capacity, columns, behind)
         away = exchange_chips(pairs, columns)
         if number + 1 < len(spans):
-            token = wait_for([attn[0]] + [far[number + 1][key] for key in evens[1:]])
+            token = wait_for(
+                [attn[0]] + [piece for key in evens[1:] for piece in far[number + 1][key]]
+            )
             after = [token] + pairs
             early.append(collect(slot, here + away, capacity, slots))
             behind = early[-1]

time: 104 us -> 105 us (level)
  waiting for transfers between devices: 46 us -> 47.6 us
    ppermute x15 -> x16, waiting for transfers between devices: 46 us -> 47.6 us  [swap(): return lax.ppermute(array, axis, [(i, i ^ bits) for i in range(count)])]
    pallas_call x1, Pallas kernels: 2.36 us -> 1.3 us  [prepare(): pl.pallas_call(functools.partial(prepare_kernel, columns, capacity, spans...]
    unnamed x30 -> x28, local copies, waits for them, and re-layouts: 7.2 us -> 6.27 us
    ppermute x15 -> x16, starting transfers between devices: 19.7 us -> 20.2 us  [swap(): return lax.ppermute(array, axis, [(i, i ^ bits) for i in range(count)])]
  transfers between devices with their start and end apart: 16 -> 17, of which waited for: 7 -> 8; matrix products, arithmetic and copies ran while one was open for 0% -> 0% of each run, Pallas kernels for 20% -> 20%
where the time goes in v12:
time: 105 us; the launch traced here: 104 us
  waiting for transfers between devices  47.6 us (45%)
  Pallas kernels  25.1 us (24%)
  starting transfers between devices  24 us (23%)
  local copies, waits for them, and re-layouts  6.38 us (6%)
  between operations  1.13 us (1%)
    ppermute x16, waiting for transfers between devices, swap(): return lax.ppermute(array, axis, [(i, i ^ bits) for i in range(count)])  47.6 us
    ppermute x16, starting transfers between devices, swap(): return lax.ppermute(array, axis, [(i, i ^ bits) for i in range(count)])  20.2 us
    pallas_call x4, Pallas kernels, attend(): pl.pallas_call(functools.partial(attend_kernel, size, heads, first, start...  15 us
    unnamed x28, local copies, waits for them, and re-layouts  6.27 us
    all_to_all x1, starting transfers between devices, per_device(): lax.all_to_all(send.reshape(columns, capacity, -1), 'cand', split_axis=0,...  3.8 us
    pallas_call x1, Pallas kernels, project_queries(): pl.pallas_call(query_kernel, in_specs=whole(4), out_specs=whole()[0], out...  3.29 us
    pallas_call x1, Pallas kernels, finish(): pl.pallas_call(functools.partial(finish_kernel, len(early), capacity, slo...  3.09 us
  transfers between devices with their start and end apart: 17, of which 8 were waited for; matrix products, arithmetic and copies ran while one was open for 0% of the time, Pallas kernels for 20%

profile of v12, /device:TPU:0, one launch (start us, length us, event | category | flops | bytes accessed | tf_op | source)
XLA Modules:
  0.0 104.4 jit_solution(8353248954704213206)
XLA Ops:
  0.0 0.7 copy-done.4
  0.7 1.2 %copy-done.7 = bf16[1,256,2048]{2,1,0:T(8,128)(2,1)S(1)} copy-done((bf16[1,256,2048]{2,1,0:T(8,128)(2,1)S(1)}, bf16[1,256,2048]{2,1,0:T(8,128)(2,1)}, u32[]{:S(2)}) %copy-start.7) | copy-done | bytes 1048600
  1.9 1.3 %prepare.1 = (s32[8,512]{1,0:T(8,128)S(1)}, bf16[256,1024]{1,0:T(8,128)(2,1)}, bf16[256,1024]{1,0:T(8,128)(2,1)}) custom-call(s32[1,512]{1,0:T(1,128)S(1)} %bitcast.12, bf16[256,2048]{1,0:T(8,128)(2,1)S(1)} %bitcast.13), custom_call_target="tpu_custom_call" | custom-call | flops 6000000000 | tf_op jit(solution)/shard_map/prepare/pallas_call | solution.py:148
  3.2 4.1 %collective-permute-start.1 = (bf16[256,1024]{1,0:T(8,128)(2,1)}, bf16[256,1024]{1,0:T(8,128)(2,1)}, u32[]{:S(2)}, u32[]{:S(2)}) collective-permute-start(bf16[256,1024]{1,0:T(8,128)(2,1)} %get-tuple-element.24.refs_2_), channel_id=1, source_target_pairs={{0,16},{8,24},{16,0},{24,8},{1,17},{9,25},{17,1},{25,9},{2,18},{10... | collective-permute-start | bytes 1572872 | tf_op jit(solution)/shard_map/ppermute | solution.py:373
  7.3 1.6 %collective-permute-start = (bf16[256,1024]{1,0:T(8,128)(2,1)}, bf16[256,1024]{1,0:T(8,128)(2,1)}, u32[]{:S(2)}, u32[]{:S(2)}) collective-permute-start(bf16[256,1024]{1,0:T(8,128)(2,1)} %get-tuple-element.24.refs_2_), channel_id=1, source_target_pairs={{0,8},{8,0},{16,24},{24,16},{1,9},{9,1},{17,25},{25,17},{2,10},{10... | collective-permute-start | bytes 1572872 | tf_op jit(solution)/shard_map/ppermute | solution.py:373
  8.9 0.0 copy-done
  8.9 0.0 copy-done.3
  8.9 0.0 copy-done.11
  8.9 3.3 %project_queries.1 = bf16[1024,1152]{1,0:T(8,128)(2,1)S(1)} custom-call(s32[8,512]{1,0:T(8,128)S(1)} %get-tuple-element.27.slot_ref, s32[1,512]{1,0:T(1,128)S(1)} %bitcast.15, bf16[512,1024]{1,0:T(8,128)(2,1)S(1)} %copy-done.3, bf16[1024,2048]{1,0:T(8,128)(2,1)S(1)} %copy-done), custom_call_target="tpu_custom_call" | custom-call | flops 2147483648 | bytes 5242880 | tf_op jit(solution)/shard_map/project_queries/pallas_call | solution.py:82
  12.2 0.0 copy-start.2
  12.2 1.4 %copy-done.2 = bf16[1024,1152]{1,0:T(8,128)(2,1)} copy-done((bf16[1024,1152]{1,0:T(8,128)(2,1)}, bf16[1024,1152]{1,0:T(8,128)(2,1)S(1)}, u32[]{:S(2)}) %copy-start.2) | copy-done | bytes 2359320
  13.6 3.8 %all-to-all-start = ((bf16[8,128,1152]{2,1,0:T(8,128)(2,1)}), bf16[8,128,1152]{2,1,0:T(8,128)(2,1)S(1)}, u32[]{:S(2)}, u32[]{:S(2)}) async-start(bf16[8,128,1152]{2,1,0:T(8,128)(2,1)} %bitcast.11), calls=%async_computation | async-start | bytes 4718592 | tf_op jit(solution)/shard_map/all_to_all | solution.py:440
  18.1 0.0 copy-start.1
  18.1 2.2 %copy-done.1 = bf16[1024,2048]{1,0:T(8,128)(2,1)S(1)} copy-done((bf16[1024,2048]{1,0:T(8,128)(2,1)S(1)}, bf16[1024,2048]{1,0:T(8,128)(2,1)}, u32[]{:S(2)}) %copy-start.1) | copy-done | bytes 4194328
  20.3 1.4 %project_gate.1 = (bf16[512,1024]{1,0:T(8,128)(2,1)S(1)}, s32[8,128]{1,0:T(8,128)S(1)}) custom-call(bf16[512,1024]{1,0:T(8,128)(2,1)S(1)} %copy-done.3, bf16[1024,2048]{1,0:T(8,128)(2,1)S(1)} %copy-done.1), custom_call_target="tpu_custom_call" | custom-call | flops 1073741824 | bytes 4194304 | tf_op jit(solution)/shard_map/project_gate/pallas_call | solution.py:109
  21.7 0.0 copy-done.5
  21.7 0.0 copy-start.8
  21.7 9.2 %collective-permute-done.1.refs_2_.refs_3_ = bf16[256,1024]{1,0:T(8,128)(2,1)} collective-permute-done((bf16[256,1024]{1,0:T(8,128)(2,1)}, bf16[256,1024]{1,0:T(8,128)(2,1)}, u32[]{:S(2)}, u32[]{:S(2)}) %collective-permute-start.1) | collective-permute-done | bytes 524320 | tf_op jit(solution)/shard_map/ppermute | solution.py:373
  30.9 0.0 collective-permute-start.8
  30.9 4.0 %collective-permute-start.2 = (bf16[256,1024]{1,0:T(8,128)(2,1)}, bf16[256,1024]{1,0:T(8,128)(2,1)}, u32[]{:S(2)}, u32[]{:S(2)}) collective-permute-start(bf16[256,1024]{1,0:T(8,128)(2,1)} %collective-permute-done.1.refs_2_.refs_3_), channel_id=1, source_target_pairs={{0,8},{8,0},{16,24},{24,16},{1,9},{9,1},{17,25},{25,17},{2,10},{10... | collective-permute-start | bytes 1572872 | tf_op jit(solution)/shard_map/ppermute | solution.py:373
  34.9 0.0 collective-permute-done.refs_1_.refs_4_
  34.9 0.3 slot_column.1
  35.2 0.0 copy-done.8
  35.3 0.7 copy-done.12
  36.0 20.5 %collective-permute-done.8.refs_1_.refs_6_ = bf16[256,1024]{1,0:T(8,128)(2,1)} collective-permute-done((bf16[256,1024]{1,0:T(8,128)(2,1)}, bf16[256,1024]{1,0:T(8,128)(2,1)}, u32[]{:S(2)}, u32[]{:S(2)}) %collective-permute-start.8) | collective-permute-done | bytes 524320 | tf_op jit(solution)/shard_map/ppermute | solution.py:373
  56.5 0.0 collective-permute-start.10
  56.5 2.0 %collective-permute-start.9 = (bf16[256,1024]{1,0:T(8,128)(2,1)}, bf16[256,1024]{1,0:T(8,128)(2,1)}, u32[]{:S(2)}, u32[]{:S(2)}) collective-permute-start(bf16[256,1024]{1,0:T(8,128)(2,1)} %collective-permute-done.8.refs_1_.refs_6_), channel_id=1, source_target_pairs={{0,8},{8,0},{16,24},{24,16},{1,9},{9,1},{17,25},{25,17},{2,10},{10... | collective-permute-start | bytes 1572872 | tf_op jit(solution)/shard_map/ppermute | solution.py:373
  58.5 0.0 all-to-all-done
  58.5 4.9 %attend.4.refs_2_ = f32[1024,512]{1,0:T(8,128)S(1)} custom-call(s32[1]{0:T(128)S(6)} %copy.9.length_ref, s32[8,128]{1,0:T(8,128)S(1)} %get-tuple-element.28.refs_0_, bf16[1024,1152]{1,0:T(8,128)(2,1)S(1)} %bitcast.7, bf16[256,1024]{1,0:T(8,128)(2,1)} %get-tuple-element.24.refs_2_, bf16[256,1024]{1,0:T(8,128)(2,1)} %collective-permute-done.1.refs_2_.refs_3_, ...), custom_call_target="tpu_custom_call" | custom-call | bytes 3670016 | tf_op jit(solution)/shard_map/attend/pallas_call | solution.py:281
  63.5 0.0 collective-permute-done.2.refs_1_
  63.5 2.5 %attend.5 = (bf16[512,512]{1,0:T(8,128)(2,1)S(1)}, bf16[256,512]{1,0:T(8,128)(2,1)S(1)}, bf16[256,512]{1,0:T(8,128)(2,1)S(1)}) custom-call(s32[1]{0:T(128)S(6)} %copy.9.length_ref, bf16[1024,1152]{1,0:T(8,128)(2,1)S(1)} %bitcast.8, bf16[256,1024]{1,0:T(8,128)(2,1)} %collective-permute-done.2.refs_1_, f32[1024,512]{1,0:T(8,128)S(1)} %attend.4.refs_2_), custom_call_target="tpu_custom_call" | custom-call | bytes 2621440 | tf_op jit(solution)/shard_map/attend/pallas_call | solution.py:281
  66.0 0.1 collective-permute-start.3
  66.0 0.5 collective-permute-start.5
  66.6 1.0 collective-permute-done.3.refs_1_
  67.6 1.3 %collective-permute-start.4 = (bf16[256,512]{1,0:T(8,128)(2,1)S(1)}, bf16[256,512]{1,0:T(8,128)(2,1)S(1)}, u32[]{:S(2)}, u32[]{:S(2)}) collective-permute-start(bf16[256,512]{1,0:T(8,128)(2,1)S(1)} %pad_maximum_fusion.refs_1_), channel_id=1, source_target_pairs={{0,2},{1,3},{2,0},{3,1},{4,6},{5,7},{6,4},{7,5},{8,10},{9,11},{10,... | collective-permute-start | bytes 786440 | tf_op jit(solution)/shard_map/ppermute | solution.py:373
  68.9 0.0 collective-permute-done.5
  69.0 1.6 %collective-permute-start.6 = (bf16[256,512]{1,0:T(8,128)(2,1)S(1)}, bf16[256,512]{1,0:T(8,128)(2,1)S(1)}, u32[]{:S(2)}, u32[]{:S(2)}) collective-permute-start(bf16[256,512]{1,0:T(8,128)(2,1)S(1)} %pad_maximum_fusion.1.refs_2_), channel_id=1, source_target_pairs={{0,4},{1,5},{2,6},{3,7},{4,0},{5,1},{6,2},{7,3},{8,12},{9,13},{10,... | collective-permute-start | bytes 786440 | tf_op jit(solution)/shard_map/ppermute | solution.py:373
  70.6 0.8 collective-permute-start.7
  71.4 3.7 %attend.6.refs_3_ = f32[1024,512]{1,0:T(8,128)S(1)} custom-call(s32[1]{0:T(128)S(6)} %copy.9.length_ref, s32[8,128]{1,0:T(8,128)S(1)} %wait_for.1.refs_0_, bf16[256,512]{1,0:T(8,128)(2,1)S(1)} %pad_maximum_fusion.refs_1_, bf16[256,512]{1,0:T(8,128)(2,1)S(1)} %pad_maximum_fusion.1.refs_2_, bf16[256,512]{1,0:T(8,128)(2,1)S(1)} %pad_maximum_fusion.2.refs_3_, ...), custom_call_target="tpu_custom_call" | custom-call | bytes 3145728 | tf_op jit(solution)/shard_map/attend/pallas_call | solution.py:281
  75.0 0.0 copy-start.13
  75.0 0.0 collective-permute-done.10.refs_2_
  75.1 5.1 %collective-permute-done.9.refs_1_ = bf16[256,1024]{1,0:T(8,128)(2,1)} collective-permute-done((bf16[256,1024]{1,0:T(8,128)(2,1)}, bf16[256,1024]{1,0:T(8,128)(2,1)}, u32[]{:S(2)}, u32[]{:S(2)}) %collective-permute-start.9) | collective-permute-done | bytes 524320 | tf_op jit(solution)/shard_map/ppermute | solution.py:373
  80.2 4.0 %attend.7 = (bf16[512,512]{1,0:T(8,128)(2,1)S(1)}, bf16[256,512]{1,0:T(8,128)(2,1)S(1)}, bf16[256,512]{1,0:T(8,128)(2,1)S(1)}) custom-call(s32[1]{0:T(128)S(6)} %copy.9.length_ref, bf16[1024,1152]{1,0:T(8,128)(2,1)S(1)} %bitcast.10, bf16[256,1024]{1,0:T(8,128)(2,1)} %collective-permute-done.9.refs_1_, bf16[256,1024]{1,0:T(8,128)(2,1)} %collective-permute-done.10.refs_2_, ...), custom_call_target="tpu_custom_call" | custom-call | flops 21474836480 | bytes 3145728 | tf_op jit(solution)/shard_map/attend/pallas_call | solution.py:281
  84.2 0.1 collective-permute-start.11
  84.2 0.5 collective-permute-start.12
  84.7 0.0 collective-permute-done.4.refs_2_
  84.7 0.0 collective-permute-done.6.refs_3_
  84.7 0.0 collective-permute-done.7.refs_4_
  84.7 0.0 copy-done.13
  84.8 0.7 collect.1.refs_0_
  85.5 0.0 copy-start.6
  85.5 0.0 copy-start.9
  85.5 0.0 copy-start.10
  85.5 0.3 collective-permute-done.11.refs_2_
  85.8 0.4 collective-permute-done.12
  86.2 1.1 %collective-permute-start.13 = (bf16[256,512]{1,0:T(8,128)(2,1)S(1)}, bf16[256,512]{1,0:T(8,128)(2,1)S(1)}, u32[]{:S(2)}, u32[]{:S(2)}) collective-permute-start(bf16[256,512]{1,0:T(8,128)(2,1)S(1)} %pad_maximum_fusion.3), channel_id=1, source_target_pairs={{0,2},{1,3},{2,0},{3,1},{4,6},{5,7},{6,4},{7,5},{8,10},{9,11},{10,... | collective-permute-start | bytes 786440 | tf_op jit(solution)/shard_map/ppermute | solution.py:373
  87.3 1.6 %collective-permute-start.14 = (bf16[256,512]{1,0:T(8,128)(2,1)S(1)}, bf16[256,512]{1,0:T(8,128)(2,1)S(1)}, u32[]{:S(2)}, u32[]{:S(2)}) collective-permute-start(bf16[256,512]{1,0:T(8,128)(2,1)S(1)} %pad_maximum_fusion.4), channel_id=1, source_target_pairs={{0,4},{1,5},{2,6},{3,7},{4,0},{5,1},{6,2},{7,3},{8,12},{9,13},{10,... | collective-permute-start | bytes 786440 | tf_op jit(solution)/shard_map/ppermute | solution.py:373
  88.9 1.0 collective-permute-start.15
  90.0 5.5 %collective-permute-done.13.refs_3_ = bf16[256,512]{1,0:T(8,128)(2,1)S(1)} collective-permute-done((bf16[256,512]{1,0:T(8,128)(2,1)S(1)}, bf16[256,512]{1,0:T(8,128)(2,1)S(1)}, u32[]{:S(2)}, u32[]{:S(2)}) %collective-permute-start.13) | collective-permute-done | bytes 262176 | tf_op jit(solution)/shard_map/ppermute | solution.py:373
  95.5 5.6 %collective-permute-done.14.refs_4_ = bf16[256,512]{1,0:T(8,128)(2,1)S(1)} collective-permute-done((bf16[256,512]{1,0:T(8,128)(2,1)S(1)}, bf16[256,512]{1,0:T(8,128)(2,1)S(1)}, u32[]{:S(2)}, u32[]{:S(2)}) %collective-permute-start.14) | collective-permute-done | bytes 262176 | tf_op jit(solution)/shard_map/ppermute | solution.py:373
  101.1 0.0 collective-permute-done.15.refs_5_
  101.1 0.0 copy-done.9
  101.1 0.0 copy-done.10
  101.1 3.1 %finish.1 = bf16[512,1024]{1,0:T(8,128)(2,1)} custom-call(s32[512,128]{1,0:T(8,128)S(1)} %copy-done.13, f32[1,1024]{1,0:T(1,128)S(1)} %bitcast.14, bf16[512,1024]{1,0:T(8,128)(2,1)S(1)} %copy-done.9, bf16[512,1024]{1,0:T(8,128)(2,1)S(1)} %copy-done.3, bf16[1024,1024]{1,0:T(8,128)(2,1)S(1)} %copy-done.6, bf16[512,512]{1,0:T(8,128)(2,1)S(1)} %collect.1.refs_0_, ...), custom_call_target="tpu_custom_call" | custom-call | flops 2147483648 | bytes 7340032 | tf_op jit(solution)/shard_map/finish/pallas_call | solution.py:358
  (22 shorter events, 0.2 us)
Async XLA Ops:
  0.0 0.7 copy-start.4
  0.7 1.2 %copy-start.7 = (bf16[1,256,2048]{2,1,0:T(8,128)(2,1)S(1)}, bf16[1,256,2048]{2,1,0:T(8,128)(2,1)}, u32[]{:S(2)}) copy-start(bf16[1,256,2048]{2,1,0:T(8,128)(2,1)} %param.12) | copy-start | bytes 3145732
  1.9 7.0 %copy-start = (bf16[1024,2048]{1,0:T(8,128)(2,1)S(1)}, bf16[1024,2048]{1,0:T(8,128)(2,1)}, u32[]{:S(2)}) copy-start(bf16[1024,2048]{1,0:T(8,128)(2,1)} %w_ref.4) | copy-start | bytes 12582916
  1.9 7.0 %copy-start.3 = (bf16[512,1024]{1,0:T(8,128)(2,1)S(1)}, bf16[512,1024]{1,0:T(8,128)(2,1)}, u32[]{:S(2)}) copy-start(bf16[512,1024]{1,0:T(8,128)(2,1)} %x_ref.5) | copy-start | bytes 3145732
  1.9 7.0 %copy-start.11 = (s32[512]{0:T(512)S(1)}, s32[512]{0:T(512)}, u32[]{:S(2)}) copy-start(s32[512]{0:T(512)} %param.10) | copy-start | bytes 6148
  3.2 27.7 %collective-permute-start.1 = (bf16[256,1024]{1,0:T(8,128)(2,1)}, bf16[256,1024]{1,0:T(8,128)(2,1)}, u32[]{:S(2)}, u32[]{:S(2)}) collective-permute-start(bf16[256,1024]{1,0:T(8,128)(2,1)} %get-tuple-element.24.refs_2_), channel_id=1, source_target_pairs={{0,16},{8,24},{16,0},{24,8},{1,17},{9,25},{17,1},{25,9},{2,18},{10... | collective-permute-start | bytes 1572872 | tf_op jit(solution)/shard_map/ppermute | solution.py:373
  7.3 27.6 %collective-permute-start = (bf16[256,1024]{1,0:T(8,128)(2,1)}, bf16[256,1024]{1,0:T(8,128)(2,1)}, u32[]{:S(2)}, u32[]{:S(2)}) collective-permute-start(bf16[256,1024]{1,0:T(8,128)(2,1)} %get-tuple-element.24.refs_2_), channel_id=1, source_target_pairs={{0,8},{8,0},{16,24},{24,16},{1,9},{9,1},{17,25},{25,17},{2,10},{10... | collective-permute-start | bytes 1572872 | tf_op jit(solution)/shard_map/ppermute | solution.py:373
  12.2 1.4 %copy-start.2 = (bf16[1024,1152]{1,0:T(8,128)(2,1)}, bf16[1024,1152]{1,0:T(8,128)(2,1)S(1)}, u32[]{:S(2)}) copy-start(bf16[1024,1152]{1,0:T(8,128)(2,1)S(1)} %project_queries.1) | copy-start | bytes 7077892
  13.6 44.9 %all-to-all-start = ((bf16[8,128,1152]{2,1,0:T(8,128)(2,1)}), bf16[8,128,1152]{2,1,0:T(8,128)(2,1)S(1)}, u32[]{:S(2)}, u32[]{:S(2)}) async-start(bf16[8,128,1152]{2,1,0:T(8,128)(2,1)} %bitcast.11), calls=%async_computation | async-start | bytes 4718592 | tf_op jit(solution)/shard_map/all_to_all | solution.py:440
  18.1 2.2 %copy-start.1 = (bf16[1024,2048]{1,0:T(8,128)(2,1)S(1)}, bf16[1024,2048]{1,0:T(8,128)(2,1)}, u32[]{:S(2)}) copy-start(bf16[1024,2048]{1,0:T(8,128)(2,1)} %w_ref.4) | copy-start | bytes 12582916
  20.3 1.4 %copy-start.5 = (s32[512,1]{0,1:T(1,128)S(1)}, s32[512,1]{0,1:T(1,128)}, u32[]{:S(2)}) copy-start(s32[512,1]{0,1:T(1,128)} %param.9) | copy-start | bytes 6148
  21.7 13.5 %copy-start.8 = (bf16[512,1024]{1,0:T(8,128)(2,1)}, bf16[512,1024]{1,0:T(8,128)(2,1)S(1)}, u32[]{:S(2)}) copy-start(bf16[512,1024]{1,0:T(8,128)(2,1)S(1)} %get-tuple-element.26.gate_ref) | copy-start | bytes 3145732
  30.9 25.6 %collective-permute-start.8 = (bf16[256,1024]{1,0:T(8,128)(2,1)}, bf16[256,1024]{1,0:T(8,128)(2,1)}, u32[]{:S(2)}, u32[]{:S(2)}) collective-permute-start(bf16[256,1024]{1,0:T(8,128)(2,1)} %get-tuple-element.34.refs_5_), channel_id=1, source_target_pairs={{0,16},{8,24},{16,0},{24,8},{1,17},{9,25},{17,1},{25,9},{2,18},{10... | collective-permute-start | bytes 1572872 | tf_op jit(solution)/shard_map/ppermute | solution.py:373
  30.9 32.6 %collective-permute-start.2 = (bf16[256,1024]{1,0:T(8,128)(2,1)}, bf16[256,1024]{1,0:T(8,128)(2,1)}, u32[]{:S(2)}, u32[]{:S(2)}) collective-permute-start(bf16[256,1024]{1,0:T(8,128)(2,1)} %collective-permute-done.1.refs_2_.refs_3_), channel_id=1, source_target_pairs={{0,8},{8,0},{16,24},{24,16},{1,9},{9,1},{17,25},{25,17},{2,10},{10... | collective-permute-start | bytes 1572872 | tf_op jit(solution)/shard_map/ppermute | solution.py:373
  35.3 0.7 copy-start.12
  56.5 18.5 %collective-permute-start.10 = (bf16[256,1024]{1,0:T(8,128)(2,1)}, bf16[256,1024]{1,0:T(8,128)(2,1)}, u32[]{:S(2)}, u32[]{:S(2)}) collective-permute-start(bf16[256,1024]{1,0:T(8,128)(2,1)} %get-tuple-element.34.refs_5_), channel_id=1, source_target_pairs={{0,8},{8,0},{16,24},{24,16},{1,9},{9,1},{17,25},{25,17},{2,10},{10... | collective-permute-start | bytes 1572872 | tf_op jit(solution)/shard_map/ppermute | solution.py:373
  56.5 23.7 %collective-permute-start.9 = (bf16[256,1024]{1,0:T(8,128)(2,1)}, bf16[256,1024]{1,0:T(8,128)(2,1)}, u32[]{:S(2)}, u32[]{:S(2)}) collective-permute-start(bf16[256,1024]{1,0:T(8,128)(2,1)} %collective-permute-done.8.refs_1_.refs_6_), channel_id=1, source_target_pairs={{0,8},{8,0},{16,24},{24,16},{1,9},{9,1},{17,25},{25,17},{2,10},{10... | collective-permute-start | bytes 1572872 | tf_op jit(solution)/shard_map/ppermute | solution.py:373
  66.0 1.6 %collective-permute-start.3 = (bf16[256,512]{1,0:T(8,128)(2,1)S(1)}, bf16[256,512]{1,0:T(8,128)(2,1)S(1)}, u32[]{:S(2)}, u32[]{:S(2)}) collective-permute-start(bf16[256,512]{1,0:T(8,128)(2,1)S(1)} %get-tuple-element.30), channel_id=1, source_target_pairs={{0,1},{1,0},{2,3},{3,2},{4,5},{5,4},{6,7},{7,6},{8,9},{9,8},{10,11... | collective-permute-start | bytes 786440 | tf_op jit(solution)/shard_map/ppermute | solution.py:373
  66.0 2.9 %collective-permute-start.5 = (bf16[256,512]{1,0:T(8,128)(2,1)S(1)}, bf16[256,512]{1,0:T(8,128)(2,1)S(1)}, u32[]{:S(2)}, u32[]{:S(2)}) collective-permute-start(bf16[256,512]{1,0:T(8,128)(2,1)S(1)} %get-tuple-element.31), channel_id=1, source_target_pairs={{0,1},{1,0},{2,3},{3,2},{4,5},{5,4},{6,7},{7,6},{8,9},{9,8},{10,11... | collective-permute-start | bytes 786440 | tf_op jit(solution)/shard_map/ppermute | solution.py:373
  67.6 17.1 %collective-permute-start.4 = (bf16[256,512]{1,0:T(8,128)(2,1)S(1)}, bf16[256,512]{1,0:T(8,128)(2,1)S(1)}, u32[]{:S(2)}, u32[]{:S(2)}) collective-permute-start(bf16[256,512]{1,0:T(8,128)(2,1)S(1)} %pad_maximum_fusion.refs_1_), channel_id=1, source_target_pairs={{0,2},{1,3},{2,0},{3,1},{4,6},{5,7},{6,4},{7,5},{8,10},{9,11},{10,... | collective-permute-start | bytes 786440 | tf_op jit(solution)/shard_map/ppermute | solution.py:373
  69.0 15.8 %collective-permute-start.6 = (bf16[256,512]{1,0:T(8,128)(2,1)S(1)}, bf16[256,512]{1,0:T(8,128)(2,1)S(1)}, u32[]{:S(2)}, u32[]{:S(2)}) collective-permute-start(bf16[256,512]{1,0:T(8,128)(2,1)S(1)} %pad_maximum_fusion.1.refs_2_), channel_id=1, source_target_pairs={{0,4},{1,5},{2,6},{3,7},{4,0},{5,1},{6,2},{7,3},{8,12},{9,13},{10,... | collective-permute-start | bytes 786440 | tf_op jit(solution)/shard_map/ppermute | solution.py:373
  70.6 14.2 %collective-permute-start.7 = (bf16[256,512]{1,0:T(8,128)(2,1)S(1)}, bf16[256,512]{1,0:T(8,128)(2,1)S(1)}, u32[]{:S(2)}, u32[]{:S(2)}) collective-permute-start(bf16[256,512]{1,0:T(8,128)(2,1)S(1)} %pad_maximum_fusion.2.refs_3_), channel_id=1, source_target_pairs={{0,6},{1,7},{2,4},{3,5},{4,2},{5,3},{6,0},{7,1},{8,14},{9,15},{10,... | collective-permute-start | bytes 786440 | tf_op jit(solution)/shard_map/ppermute | solution.py:373
  75.0 9.7 %copy-start.13 = (s32[512,128]{1,0:T(8,128)S(1)}, s32[512,128]{1,0:T(8,128)}, u32[]{:S(2)}) copy-start(s32[512,128]{1,0:T(8,128)} %copy-done.12) | copy-start | bytes 786436
  84.2 1.6 %collective-permute-start.11 = (bf16[256,512]{1,0:T(8,128)(2,1)S(1)}, bf16[256,512]{1,0:T(8,128)(2,1)S(1)}, u32[]{:S(2)}, u32[]{:S(2)}) collective-permute-start(bf16[256,512]{1,0:T(8,128)(2,1)S(1)} %get-tuple-element.36), channel_id=1, source_target_pairs={{0,1},{1,0},{2,3},{3,2},{4,5},{5,4},{6,7},{7,6},{8,9},{9,8},{10,11... | collective-permute-start | bytes 786440 | tf_op jit(solution)/shard_map/ppermute | solution.py:373
  84.2 1.9 %collective-permute-start.12 = (bf16[256,512]{1,0:T(8,128)(2,1)S(1)}, bf16[256,512]{1,0:T(8,128)(2,1)S(1)}, u32[]{:S(2)}, u32[]{:S(2)}) collective-permute-start(bf16[256,512]{1,0:T(8,128)(2,1)S(1)} %get-tuple-element.37), channel_id=1, source_target_pairs={{0,1},{1,0},{2,3},{3,2},{4,5},{5,4},{6,7},{7,6},{8,9},{9,8},{10,11... | collective-permute-start | bytes 786440 | tf_op jit(solution)/shard_map/ppermute | solution.py:373
  85.5 15.6 %copy-start.6 = (bf16[1024,1024]{1,0:T(8,128)(2,1)S(1)}, bf16[1024,1024]{1,0:T(8,128)(2,1)}, u32[]{:S(2)}) copy-start(bf16[1024,1024]{1,0:T(8,128)(2,1)} %w_ref.5) | copy-start | bytes 6291460
  85.5 15.6 %copy-start.9 = (bf16[512,1024]{1,0:T(8,128)(2,1)S(1)}, bf16[512,1024]{1,0:T(8,128)(2,1)}, u32[]{:S(2)}) copy-start(bf16[512,1024]{1,0:T(8,128)(2,1)} %copy-done.8) | copy-start | bytes 3145732
  85.5 15.6 %copy-start.10 = (f32[1024]{0:T(1024)S(1)}, f32[1024]{0:T(1024)}, u32[]{:S(2)}) copy-start(f32[1024]{0:T(1024)} %param.15) | copy-start | bytes 12292
  86.2 9.2 %collective-permute-start.13 = (bf16[256,512]{1,0:T(8,128)(2,1)S(1)}, bf16[256,512]{1,0:T(8,128)(2,1)S(1)}, u32[]{:S(2)}, u32[]{:S(2)}) collective-permute-start(bf16[256,512]{1,0:T(8,128)(2,1)S(1)} %pad_maximum_fusion.3), channel_id=1, source_target_pairs={{0,2},{1,3},{2,0},{3,1},{4,6},{5,7},{6,4},{7,5},{8,10},{9,11},{10,... | collective-permute-start | bytes 786440 | tf_op jit(solution)/shard_map/ppermute | solution.py:373
  87.3 13.8 %collective-permute-start.14 = (bf16[256,512]{1,0:T(8,128)(2,1)S(1)}, bf16[256,512]{1,0:T(8,128)(2,1)S(1)}, u32[]{:S(2)}, u32[]{:S(2)}) collective-permute-start(bf16[256,512]{1,0:T(8,128)(2,1)S(1)} %pad_maximum_fusion.4), channel_id=1, source_target_pairs={{0,4},{1,5},{2,6},{3,7},{4,0},{5,1},{6,2},{7,3},{8,12},{9,13},{10,... | collective-permute-start | bytes 786440 | tf_op jit(solution)/shard_map/ppermute | solution.py:373
  88.9 12.1 %collective-permute-start.15 = (bf16[256,512]{1,0:T(8,128)(2,1)S(1)}, bf16[256,512]{1,0:T(8,128)(2,1)S(1)}, u32[]{:S(2)}, u32[]{:S(2)}) collective-permute-start(bf16[256,512]{1,0:T(8,128)(2,1)S(1)} %pad_maximum_fusion.5), channel_id=1, source_target_pairs={{0,6},{1,7},{2,4},{3,5},{4,2},{5,3},{6,0},{7,1},{8,14},{9,15},{10,... | collective-permute-start | bytes 786440 | tf_op jit(solution)/shard_map/ppermute | solution.py:373

commit v13 on v11

--- a/solution.py
+++ b/solution.py
@@ -16,7 +16,7 @@
 BF16 = jnp.bfloat16
 MIB = 1024 * 1024
 TOKEN = jax.ShapeDtypeStruct((8, BLK), jnp.int32)
-WAIT_COST = 12.0
+WAIT_COST = 20.0
 LATE_SHARE = 20.0
 COLLECT_COST = 20.0
 SLOTS_COST = 6.0
@@ -405,7 +405,7 @@
     far = []
     for part in parts:
         if far:
-            part, _ = lax.optimization_barrier((part, (far[-1], gated, send)))
+            part, _ = lax.optimization_barrier((part, send))
         held = {0: part}
         bit = count // 2
         while bit > 1:
@@ -421,7 +421,7 @@
     got = lax.all_to_all(
         send.reshape(columns, capacity, -1), "cand", split_axis=0, concat_axis=0, tiled=True
     ).reshape(slots, -1)
-    arrived = [gated, near] + [far[0][key] for key in evens[1:]]
+    arrived = [gated, near] + [held[key] for held in far for key in evens[1:]]
     slot, started = slot_column(owner_row ^ me, columns, capacity, arrived)
     early = []
     after = [started]

time: 104 us -> 103 us (level)
  waiting for transfers between devices: 46 us -> 43.9 us
    ppermute x15, waiting for transfers between devices: 46 us -> 43.9 us  [swap(): return lax.ppermute(array, axis, [(i, i ^ bits) for i in range(count)])]
  transfers between devices with their start and end apart: 16 -> 16, of which waited for: 7 -> 9; matrix products, arithmetic and copies ran while one was open for 0% -> 0% of each run, Pallas kernels for 20% -> 20%
where the time goes in v13:
time: 103 us
  waiting for transfers between devices  43.9 us (43%)
  Pallas kernels  25.9 us (25%)
  starting transfers between devices  24.4 us (24%)
  local copies, waits for them, and re-layouts  7.32 us (7%)
  between operations  1.12 us (1%)
    ppermute x15, waiting for transfers between devices, swap(): return lax.ppermute(array, axis, [(i, i ^ bits) for i in range(count)])  43.9 us
    ppermute x15, starting transfers between devices, swap(): return lax.ppermute(array, axis, [(i, i ^ bits) for i in range(count)])  20.6 us
    pallas_call x4, Pallas kernels, attend(): pl.pallas_call(functools.partial(attend_kernel, size, heads, first, start...  14.7 us
    unnamed x30, local copies, waits for them, and re-layouts  7.2 us
    all_to_all x1, starting transfers between devices, per_device(): lax.all_to_all(send.reshape(columns, capacity, -1), 'cand', split_axis=0,...  3.8 us
    pallas_call x1, Pallas kernels, project_queries(): pl.pallas_call(query_kernel, in_specs=whole(4), out_specs=whole()[0], out...  3.29 us
    pallas_call x1, Pallas kernels, finish(): pl.pallas_call(functools.partial(finish_kernel, len(early), capacity, slo...  3.08 us
    pallas_call x1, Pallas kernels, prepare(): pl.pallas_call(functools.partial(prepare_kernel, columns, capacity, spans...  2.36 us
  transfers between devices with their start and end apart: 16, of which 9 were waited for; matrix products, arithmetic and copies ran while one was open for 0% of the time, Pallas kernels for 20%

profile of v13, /device:TPU:0, one launch (start us, length us, event | category | flops | bytes accessed | tf_op | source)
XLA Modules:
  0.0 102.8 jit_solution(7648604460556080319)
XLA Ops:
  0.0 0.7 copy-done.6
  0.7 2.4 %prepare.1 = (s32[8,512]{1,0:T(8,128)S(1)}, bf16[256,1024]{1,0:T(8,128)(2,1)}, bf16[256,1024]{1,0:T(8,128)(2,1)}) custom-call(s32[1,512]{1,0:T(1,128)S(1)} %bitcast.12, bf16[256,2048]{1,0:T(8,128)(2,1)} %bitcast.1.kv_hbm), custom_call_target="tpu_custom_call" | custom-call | flops 6000000000 | tf_op jit(solution)/shard_map/prepare/pallas_call | solution.py:141
  3.1 3.1 %collective-permute-start = (bf16[256,2048]{1,0:T(8,128)(2,1)}, bf16[256,2048]{1,0:T(8,128)(2,1)S(1)}, u32[]{:S(2)}, u32[]{:S(2)}) collective-permute-start(bf16[256,2048]{1,0:T(8,128)(2,1)} %bitcast.1.kv_hbm), channel_id=1, source_target_pairs={{0,8},{8,0},{16,24},{24,16},{1,9},{9,1},{17,25},{25,17},{2,10},{10... | collective-permute-start | bytes 3145736 | tf_op jit(solution)/shard_map/ppermute | solution.py:366
  6.1 2.6 %collective-permute-start.1 = (bf16[256,1024]{1,0:T(8,128)(2,1)}, bf16[256,1024]{1,0:T(8,128)(2,1)}, u32[]{:S(2)}, u32[]{:S(2)}) collective-permute-start(bf16[256,1024]{1,0:T(8,128)(2,1)} %get-tuple-element.26.refs_2_), channel_id=1, source_target_pairs={{0,16},{8,24},{16,0},{24,8},{1,17},{9,25},{17,1},{25,9},{2,18},{10... | collective-permute-start | bytes 1572872 | tf_op jit(solution)/shard_map/ppermute | solution.py:366
  8.7 0.0 copy-done
  8.7 0.0 copy-done.3
  8.7 0.0 copy-done.12
  8.7 3.3 %project_queries.1 = bf16[1024,1152]{1,0:T(8,128)(2,1)S(1)} custom-call(s32[8,512]{1,0:T(8,128)S(1)} %get-tuple-element.24.slot_ref, s32[1,512]{1,0:T(1,128)S(1)} %bitcast.14, bf16[512,1024]{1,0:T(8,128)(2,1)S(1)} %copy-done.3, bf16[1024,2048]{1,0:T(8,128)(2,1)S(1)} %copy-done), custom_call_target="tpu_custom_call" | custom-call | flops 2147483648 | bytes 5242880 | tf_op jit(solution)/shard_map/project_queries/pallas_call | solution.py:81
  12.0 0.0 copy-start.2
  12.1 1.4 %copy-done.2 = bf16[1024,1152]{1,0:T(8,128)(2,1)} copy-done((bf16[1024,1152]{1,0:T(8,128)(2,1)}, bf16[1024,1152]{1,0:T(8,128)(2,1)S(1)}, u32[]{:S(2)}) %copy-start.2) | copy-done | bytes 2359320
  13.5 0.3 collective-permute-start.2
  13.8 3.8 %all-to-all-start = ((bf16[8,128,1152]{2,1,0:T(8,128)(2,1)}), bf16[8,128,1152]{2,1,0:T(8,128)(2,1)S(1)}, u32[]{:S(2)}, u32[]{:S(2)}) async-start(bf16[8,128,1152]{2,1,0:T(8,128)(2,1)} %bitcast.11), calls=%async_computation | async-start | bytes 4718592 | tf_op jit(solution)/shard_map/all_to_all | solution.py:421
  18.3 0.0 copy-start.1
  18.3 2.2 %copy-done.1 = bf16[1024,2048]{1,0:T(8,128)(2,1)S(1)} copy-done((bf16[1024,2048]{1,0:T(8,128)(2,1)S(1)}, bf16[1024,2048]{1,0:T(8,128)(2,1)}, u32[]{:S(2)}) %copy-start.1) | copy-done | bytes 4194328
  20.5 1.2 %copy-done.4 = bf16[512,1024]{1,0:T(8,128)(2,1)S(1)} copy-done((bf16[512,1024]{1,0:T(8,128)(2,1)S(1)}, bf16[512,1024]{1,0:T(8,128)(2,1)}, u32[]{:S(2)}) %copy-start.4) | copy-done | bytes 1048600
  21.7 1.4 %project_gate.1 = (bf16[512,1024]{1,0:T(8,128)(2,1)S(1)}, s32[8,128]{1,0:T(8,128)S(1)}) custom-call(bf16[512,1024]{1,0:T(8,128)(2,1)S(1)} %copy-done.4, bf16[1024,2048]{1,0:T(8,128)(2,1)S(1)} %copy-done.1), custom_call_target="tpu_custom_call" | custom-call | flops 1073741824 | bytes 4194304 | tf_op jit(solution)/shard_map/project_gate/pallas_call | solution.py:108
  23.1 0.0 copy-start.9
  23.1 1.0 copy-done.9
  24.0 0.0 copy-done.7
  24.1 17.3 %collective-permute-done.1.refs_2_.refs_3_ = bf16[256,1024]{1,0:T(8,128)(2,1)} collective-permute-done((bf16[256,1024]{1,0:T(8,128)(2,1)}, bf16[256,1024]{1,0:T(8,128)(2,1)}, u32[]{:S(2)}, u32[]{:S(2)}) %collective-permute-start.1) | collective-permute-done | bytes 524320 | tf_op jit(solution)/shard_map/ppermute | solution.py:366
  41.3 3.5 %collective-permute-start.3 = (bf16[256,1024]{1,0:T(8,128)(2,1)}, bf16[256,1024]{1,0:T(8,128)(2,1)}, u32[]{:S(2)}, u32[]{:S(2)}) collective-permute-start(bf16[256,1024]{1,0:T(8,128)(2,1)} %collective-permute-done.1.refs_2_.refs_3_), channel_id=1, source_target_pairs={{0,8},{8,0},{16,24},{24,16},{1,9},{9,1},{17,25},{25,17},{2,10},{10... | collective-permute-start | bytes 1572872 | tf_op jit(solution)/shard_map/ppermute | solution.py:366
  44.9 8.7 %collective-permute-done.2.refs_3_.refs_1_.refs_6_ = bf16[256,1024]{1,0:T(8,128)(2,1)} collective-permute-done((bf16[256,1024]{1,0:T(8,128)(2,1)}, bf16[256,1024]{1,0:T(8,128)(2,1)}, u32[]{:S(2)}, u32[]{:S(2)}) %collective-permute-start.2) | collective-permute-done | bytes 524320 | tf_op jit(solution)/shard_map/ppermute | solution.py:366
  53.5 2.5 %collective-permute-start.9 = (bf16[256,1024]{1,0:T(8,128)(2,1)}, bf16[256,1024]{1,0:T(8,128)(2,1)}, u32[]{:S(2)}, u32[]{:S(2)}) collective-permute-start(bf16[256,1024]{1,0:T(8,128)(2,1)} %collective-permute-done.2.refs_3_.refs_1_.refs_6_), channel_id=1, source_target_pairs={{0,8},{8,0},{16,24},{24,16},{1,9},{9,1},{17,25},{25,17},{2,10},{10... | collective-permute-start | bytes 1572872 | tf_op jit(solution)/shard_map/ppermute | solution.py:366
  56.0 0.0 collective-permute-done.refs_1_.refs_4_.refs_7_
  56.0 0.3 slot_column.1
  56.4 0.0 copy-start.13
  56.4 0.7 copy-done.13
  57.1 0.0 all-to-all-done
  57.1 4.8 %attend.4.refs_2_ = f32[1024,512]{1,0:T(8,128)S(1)} custom-call(s32[1]{0:T(128)S(6)} %copy.9.length_ref, s32[8,128]{1,0:T(8,128)S(1)} %get-tuple-element.31.refs_0_, bf16[1024,1152]{1,0:T(8,128)(2,1)S(1)} %bitcast.7, bf16[256,1024]{1,0:T(8,128)(2,1)} %get-tuple-element.26.refs_2_, bf16[256,1024]{1,0:T(8,128)(2,1)} %collective-permute-done.1.refs_2_.refs_3_, ...), custom_call_target="tpu_custom_call" | custom-call | bytes 3670016 | tf_op jit(solution)/shard_map/attend/pallas_call | solution.py:274
  61.8 2.3 %collective-permute-done.3.refs_1_ = bf16[256,1024]{1,0:T(8,128)(2,1)} collective-permute-done((bf16[256,1024]{1,0:T(8,128)(2,1)}, bf16[256,1024]{1,0:T(8,128)(2,1)}, u32[]{:S(2)}, u32[]{:S(2)}) %collective-permute-start.3) | collective-permute-done | bytes 524320 | tf_op jit(solution)/shard_map/ppermute | solution.py:366
  64.2 2.5 %attend.5 = (bf16[512,512]{1,0:T(8,128)(2,1)S(1)}, bf16[256,512]{1,0:T(8,128)(2,1)S(1)}, bf16[256,512]{1,0:T(8,128)(2,1)S(1)}) custom-call(s32[1]{0:T(128)S(6)} %copy.9.length_ref, bf16[1024,1152]{1,0:T(8,128)(2,1)S(1)} %bitcast.8, bf16[256,1024]{1,0:T(8,128)(2,1)} %collective-permute-done.3.refs_1_, f32[1024,512]{1,0:T(8,128)S(1)} %attend.4.refs_2_), custom_call_target="tpu_custom_call" | custom-call | bytes 2621440 | tf_op jit(solution)/shard_map/attend/pallas_call | solution.py:274
  66.6 0.1 collective-permute-start.6
  66.7 0.5 collective-permute-start.4
  67.3 1.0 collective-permute-done.6
  68.3 3.0 %collective-permute-start.8 = (bf16[256,512]{1,0:T(8,128)(2,1)S(1)}, bf16[256,512]{1,0:T(8,128)(2,1)S(1)}, u32[]{:S(2)}, u32[]{:S(2)}) collective-permute-start(bf16[256,512]{1,0:T(8,128)(2,1)S(1)} %pad_maximum_fusion.2.refs_3_), channel_id=1, source_target_pairs={{0,6},{1,7},{2,4},{3,5},{4,2},{5,3},{6,0},{7,1},{8,14},{9,15},{10,... | collective-permute-start | bytes 786440 | tf_op jit(solution)/shard_map/ppermute | solution.py:366
  71.3 0.6 collective-permute-start.7
  71.9 0.0 collective-permute-done.4.refs_1_
  71.9 0.1 collective-permute-start.5
  72.1 4.8 %attend.6.refs_2_ = f32[1024,512]{1,0:T(8,128)S(1)} custom-call(s32[1]{0:T(128)S(6)} %copy.9.length_ref, s32[8,128]{1,0:T(8,128)S(1)} %wait_for.1.refs_0_, bf16[256,512]{1,0:T(8,128)(2,1)S(1)} %pad_maximum_fusion.refs_1_, bf16[256,512]{1,0:T(8,128)(2,1)S(1)} %pad_maximum_fusion.1.refs_2_, bf16[256,512]{1,0:T(8,128)(2,1)S(1)} %pad_maximum_fusion.2.refs_3_, ...), custom_call_target="tpu_custom_call" | custom-call | bytes 3670016 | tf_op jit(solution)/shard_map/attend/pallas_call | solution.py:274
  76.8 0.0 copy-start.14
  76.8 0.0 collective-permute-done.9.refs_1_
  76.8 2.7 %attend.7 = (bf16[512,512]{1,0:T(8,128)(2,1)S(1)}, bf16[256,512]{1,0:T(8,128)(2,1)S(1)}, bf16[256,512]{1,0:T(8,128)(2,1)S(1)}) custom-call(s32[1]{0:T(128)S(6)} %copy.9.length_ref, bf16[1024,1152]{1,0:T(8,128)(2,1)S(1)} %bitcast.10, bf16[256,1024]{1,0:T(8,128)(2,1)} %collective-permute-done.9.refs_1_, f32[1024,512]{1,0:T(8,128)S(1)} %attend.6.refs_2_), custom_call_target="tpu_custom_call" | custom-call | flops 10737418240 | bytes 2621440 | tf_op jit(solution)/shard_map/attend/pallas_call | solution.py:274
  79.6 0.1 collective-permute-start.10
  79.7 0.5 collective-permute-start.11
  80.2 0.0 collective-permute-done.8.refs_4_
  80.2 3.3 %collective-permute-done.7.refs_3_ = bf16[256,512]{1,0:T(8,128)(2,1)S(1)} collective-permute-done((bf16[256,512]{1,0:T(8,128)(2,1)S(1)}, bf16[256,512]{1,0:T(8,128)(2,1)S(1)}, u32[]{:S(2)}, u32[]{:S(2)}) %collective-permute-start.7) | collective-permute-done | bytes 262176 | tf_op jit(solution)/shard_map/ppermute | solution.py:366
  83.5 0.3 collective-permute-done.5.refs_2_
  83.8 0.0 copy-done.14
  83.8 0.7 collect.1.refs_0_
  84.5 0.0 copy-start.5
  84.5 0.0 copy-start.8
  84.5 0.0 copy-start.11
  84.6 0.0 collective-permute-done.10.refs_2_
  84.6 0.0 collective-permute-done.11
  84.7 1.6 %collective-permute-start.14 = (bf16[256,512]{1,0:T(8,128)(2,1)S(1)}, bf16[256,512]{1,0:T(8,128)(2,1)S(1)}, u32[]{:S(2)}, u32[]{:S(2)}) collective-permute-start(bf16[256,512]{1,0:T(8,128)(2,1)S(1)} %pad_maximum_fusion.5), channel_id=1, source_target_pairs={{0,6},{1,7},{2,4},{3,5},{4,2},{5,3},{6,0},{7,1},{8,14},{9,15},{10,... | collective-permute-start | bytes 786440 | tf_op jit(solution)/shard_map/ppermute | solution.py:366
  86.3 1.5 %collective-permute-start.13 = (bf16[256,512]{1,0:T(8,128)(2,1)S(1)}, bf16[256,512]{1,0:T(8,128)(2,1)S(1)}, u32[]{:S(2)}, u32[]{:S(2)}) collective-permute-start(bf16[256,512]{1,0:T(8,128)(2,1)S(1)} %pad_maximum_fusion.4), channel_id=1, source_target_pairs={{0,4},{1,5},{2,6},{3,7},{4,0},{5,1},{6,2},{7,3},{8,12},{9,13},{10,... | collective-permute-start | bytes 786440 | tf_op jit(solution)/shard_map/ppermute | solution.py:366
  87.8 0.6 collective-permute-start.12
  88.4 6.5 %collective-permute-done.14.refs_5_ = bf16[256,512]{1,0:T(8,128)(2,1)S(1)} collective-permute-done((bf16[256,512]{1,0:T(8,128)(2,1)S(1)}, bf16[256,512]{1,0:T(8,128)(2,1)S(1)}, u32[]{:S(2)}, u32[]{:S(2)}) %collective-permute-start.14) | collective-permute-done | bytes 262176 | tf_op jit(solution)/shard_map/ppermute | solution.py:366
  94.9 4.3 %collective-permute-done.13.refs_4_ = bf16[256,512]{1,0:T(8,128)(2,1)S(1)} collective-permute-done((bf16[256,512]{1,0:T(8,128)(2,1)S(1)}, bf16[256,512]{1,0:T(8,128)(2,1)S(1)}, u32[]{:S(2)}, u32[]{:S(2)}) %collective-permute-start.13) | collective-permute-done | bytes 262176 | tf_op jit(solution)/shard_map/ppermute | solution.py:366
  99.2 0.3 collective-permute-done.12.refs_3_
  99.5 0.0 copy-done.10
  99.5 0.0 copy-done.5
  99.5 0.0 copy-done.11
  99.5 3.1 %finish.1 = bf16[512,1024]{1,0:T(8,128)(2,1)} custom-call(s32[512,128]{1,0:T(8,128)S(1)} %copy-done.14, f32[1,1024]{1,0:T(1,128)S(1)} %bitcast.13, bf16[512,1024]{1,0:T(8,128)(2,1)S(1)} %copy-done.10, bf16[512,1024]{1,0:T(8,128)(2,1)S(1)} %copy-done.5, bf16[1024,1024]{1,0:T(8,128)(2,1)S(1)} %copy-done.8, bf16[512,512]{1,0:T(8,128)(2,1)S(1)} %collect.1.refs_0_, ...), custom_call_target="tpu_custom_call" | custom-call | flops 2147483648 | bytes 7340032 | tf_op jit(solution)/shard_map/finish/pallas_call | solution.py:351
  (22 shorter events, 0.2 us)
Async XLA Ops:
  0.0 0.7 copy-start.6
  0.7 8.1 %copy-start = (bf16[1024,2048]{1,0:T(8,128)(2,1)S(1)}, bf16[1024,2048]{1,0:T(8,128)(2,1)}, u32[]{:S(2)}) copy-start(bf16[1024,2048]{1,0:T(8,128)(2,1)} %w_ref.4) | copy-start | bytes 12582916
  0.7 8.1 %copy-start.3 = (bf16[512,1024]{1,0:T(8,128)(2,1)S(1)}, bf16[512,1024]{1,0:T(8,128)(2,1)}, u32[]{:S(2)}) copy-start(bf16[512,1024]{1,0:T(8,128)(2,1)} %x_ref.5) | copy-start | bytes 3145732
  0.7 8.1 %copy-start.12 = (s32[512]{0:T(512)S(1)}, s32[512]{0:T(512)}, u32[]{:S(2)}) copy-start(s32[512]{0:T(512)} %param.10) | copy-start | bytes 6148
  3.1 53.0 %collective-permute-start = (bf16[256,2048]{1,0:T(8,128)(2,1)}, bf16[256,2048]{1,0:T(8,128)(2,1)S(1)}, u32[]{:S(2)}, u32[]{:S(2)}) collective-permute-start(bf16[256,2048]{1,0:T(8,128)(2,1)} %bitcast.1.kv_hbm), channel_id=1, source_target_pairs={{0,8},{8,0},{16,24},{24,16},{1,9},{9,1},{17,25},{25,17},{2,10},{10... | collective-permute-start | bytes 3145736 | tf_op jit(solution)/shard_map/ppermute | solution.py:366
  6.1 35.2 %collective-permute-start.1 = (bf16[256,1024]{1,0:T(8,128)(2,1)}, bf16[256,1024]{1,0:T(8,128)(2,1)}, u32[]{:S(2)}, u32[]{:S(2)}) collective-permute-start(bf16[256,1024]{1,0:T(8,128)(2,1)} %get-tuple-element.26.refs_2_), channel_id=1, source_target_pairs={{0,16},{8,24},{16,0},{24,8},{1,17},{9,25},{17,1},{25,9},{2,18},{10... | collective-permute-start | bytes 1572872 | tf_op jit(solution)/shard_map/ppermute | solution.py:366
  12.0 1.4 %copy-start.2 = (bf16[1024,1152]{1,0:T(8,128)(2,1)}, bf16[1024,1152]{1,0:T(8,128)(2,1)S(1)}, u32[]{:S(2)}) copy-start(bf16[1024,1152]{1,0:T(8,128)(2,1)S(1)} %project_queries.1) | copy-start | bytes 7077892
  13.5 40.0 %collective-permute-start.2 = (bf16[256,1024]{1,0:T(8,128)(2,1)}, bf16[256,1024]{1,0:T(8,128)(2,1)}, u32[]{:S(2)}, u32[]{:S(2)}) collective-permute-start(bf16[256,1024]{1,0:T(8,128)(2,1)} %get-tuple-element.28.refs_5_), channel_id=1, source_target_pairs={{0,16},{8,24},{16,0},{24,8},{1,17},{9,25},{17,1},{25,9},{2,18},{10... | collective-permute-start | bytes 1572872 | tf_op jit(solution)/shard_map/ppermute | solution.py:366
  13.8 43.3 %all-to-all-start = ((bf16[8,128,1152]{2,1,0:T(8,128)(2,1)}), bf16[8,128,1152]{2,1,0:T(8,128)(2,1)S(1)}, u32[]{:S(2)}, u32[]{:S(2)}) async-start(bf16[8,128,1152]{2,1,0:T(8,128)(2,1)} %bitcast.11), calls=%async_computation | async-start | bytes 4718592 | tf_op jit(solution)/shard_map/all_to_all | solution.py:421
  18.3 2.2 %copy-start.1 = (bf16[1024,2048]{1,0:T(8,128)(2,1)S(1)}, bf16[1024,2048]{1,0:T(8,128)(2,1)}, u32[]{:S(2)}) copy-start(bf16[1024,2048]{1,0:T(8,128)(2,1)} %w_ref.4) | copy-start | bytes 12582916
  20.5 1.2 %copy-start.4 = (bf16[512,1024]{1,0:T(8,128)(2,1)S(1)}, bf16[512,1024]{1,0:T(8,128)(2,1)}, u32[]{:S(2)}) copy-start(bf16[512,1024]{1,0:T(8,128)(2,1)} %x_ref.5) | copy-start | bytes 3145732
  21.7 2.4 %copy-start.7 = (s32[512,1]{0,1:T(1,128)S(1)}, s32[512,1]{0,1:T(1,128)}, u32[]{:S(2)}) copy-start(s32[512,1]{0,1:T(1,128)} %param.9) | copy-start | bytes 6148
  23.1 1.0 copy-start.9
  41.3 22.9 %collective-permute-start.3 = (bf16[256,1024]{1,0:T(8,128)(2,1)}, bf16[256,1024]{1,0:T(8,128)(2,1)}, u32[]{:S(2)}, u32[]{:S(2)}) collective-permute-start(bf16[256,1024]{1,0:T(8,128)(2,1)} %collective-permute-done.1.refs_2_.refs_3_), channel_id=1, source_target_pairs={{0,8},{8,0},{16,24},{24,16},{1,9},{9,1},{17,25},{25,17},{2,10},{10... | collective-permute-start | bytes 1572872 | tf_op jit(solution)/shard_map/ppermute | solution.py:366
  53.5 23.3 %collective-permute-start.9 = (bf16[256,1024]{1,0:T(8,128)(2,1)}, bf16[256,1024]{1,0:T(8,128)(2,1)}, u32[]{:S(2)}, u32[]{:S(2)}) collective-permute-start(bf16[256,1024]{1,0:T(8,128)(2,1)} %collective-permute-done.2.refs_3_.refs_1_.refs_6_), channel_id=1, source_target_pairs={{0,8},{8,0},{16,24},{24,16},{1,9},{9,1},{17,25},{25,17},{2,10},{10... | collective-permute-start | bytes 1572872 | tf_op jit(solution)/shard_map/ppermute | solution.py:366
  56.4 0.7 copy-start.13
  66.6 1.6 %collective-permute-start.6 = (bf16[256,512]{1,0:T(8,128)(2,1)S(1)}, bf16[256,512]{1,0:T(8,128)(2,1)S(1)}, u32[]{:S(2)}, u32[]{:S(2)}) collective-permute-start(bf16[256,512]{1,0:T(8,128)(2,1)S(1)} %get-tuple-element.34), channel_id=1, source_target_pairs={{0,1},{1,0},{2,3},{3,2},{4,5},{5,4},{6,7},{7,6},{8,9},{9,8},{10,11... | collective-permute-start | bytes 786440 | tf_op jit(solution)/shard_map/ppermute | solution.py:366
  66.7 5.2 %collective-permute-start.4 = (bf16[256,512]{1,0:T(8,128)(2,1)S(1)}, bf16[256,512]{1,0:T(8,128)(2,1)S(1)}, u32[]{:S(2)}, u32[]{:S(2)}) collective-permute-start(bf16[256,512]{1,0:T(8,128)(2,1)S(1)} %get-tuple-element.33), channel_id=1, source_target_pairs={{0,1},{1,0},{2,3},{3,2},{4,5},{5,4},{6,7},{7,6},{8,9},{9,8},{10,11... | collective-permute-start | bytes 786440 | tf_op jit(solution)/shard_map/ppermute | solution.py:366
  68.3 11.9 %collective-permute-start.8 = (bf16[256,512]{1,0:T(8,128)(2,1)S(1)}, bf16[256,512]{1,0:T(8,128)(2,1)S(1)}, u32[]{:S(2)}, u32[]{:S(2)}) collective-permute-start(bf16[256,512]{1,0:T(8,128)(2,1)S(1)} %pad_maximum_fusion.2.refs_3_), channel_id=1, source_target_pairs={{0,6},{1,7},{2,4},{3,5},{4,2},{5,3},{6,0},{7,1},{8,14},{9,15},{10,... | collective-permute-start | bytes 786440 | tf_op jit(solution)/shard_map/ppermute | solution.py:366
  71.3 12.2 %collective-permute-start.7 = (bf16[256,512]{1,0:T(8,128)(2,1)S(1)}, bf16[256,512]{1,0:T(8,128)(2,1)S(1)}, u32[]{:S(2)}, u32[]{:S(2)}) collective-permute-start(bf16[256,512]{1,0:T(8,128)(2,1)S(1)} %pad_maximum_fusion.1.refs_2_), channel_id=1, source_target_pairs={{0,4},{1,5},{2,6},{3,7},{4,0},{5,1},{6,2},{7,3},{8,12},{9,13},{10,... | collective-permute-start | bytes 786440 | tf_op jit(solution)/shard_map/ppermute | solution.py:366
  71.9 11.9 %collective-permute-start.5 = (bf16[256,512]{1,0:T(8,128)(2,1)S(1)}, bf16[256,512]{1,0:T(8,128)(2,1)S(1)}, u32[]{:S(2)}, u32[]{:S(2)}) collective-permute-start(bf16[256,512]{1,0:T(8,128)(2,1)S(1)} %pad_maximum_fusion.refs_1_), channel_id=1, source_target_pairs={{0,2},{1,3},{2,0},{3,1},{4,6},{5,7},{6,4},{7,5},{8,10},{9,11},{10,... | collective-permute-start | bytes 786440 | tf_op jit(solution)/shard_map/ppermute | solution.py:366
  76.8 7.0 %copy-start.14 = (s32[512,128]{1,0:T(8,128)S(1)}, s32[512,128]{1,0:T(8,128)}, u32[]{:S(2)}) copy-start(s32[512,128]{1,0:T(8,128)} %copy-done.13) | copy-start | bytes 786436
  79.6 5.0 %collective-permute-start.10 = (bf16[256,512]{1,0:T(8,128)(2,1)S(1)}, bf16[256,512]{1,0:T(8,128)(2,1)S(1)}, u32[]{:S(2)}, u32[]{:S(2)}) collective-permute-start(bf16[256,512]{1,0:T(8,128)(2,1)S(1)} %get-tuple-element.36), channel_id=1, source_target_pairs={{0,1},{1,0},{2,3},{3,2},{4,5},{5,4},{6,7},{7,6},{8,9},{9,8},{10,11... | collective-permute-start | bytes 786440 | tf_op jit(solution)/shard_map/ppermute | solution.py:366
  79.7 4.9 %collective-permute-start.11 = (bf16[256,512]{1,0:T(8,128)(2,1)S(1)}, bf16[256,512]{1,0:T(8,128)(2,1)S(1)}, u32[]{:S(2)}, u32[]{:S(2)}) collective-permute-start(bf16[256,512]{1,0:T(8,128)(2,1)S(1)} %get-tuple-element.37), channel_id=1, source_target_pairs={{0,1},{1,0},{2,3},{3,2},{4,5},{5,4},{6,7},{7,6},{8,9},{9,8},{10,11... | collective-permute-start | bytes 786440 | tf_op jit(solution)/shard_map/ppermute | solution.py:366
  83.8 15.7 %copy-start.10 = (bf16[512,1024]{1,0:T(8,128)(2,1)S(1)}, bf16[512,1024]{1,0:T(8,128)(2,1)}, u32[]{:S(2)}) copy-start(bf16[512,1024]{1,0:T(8,128)(2,1)} %copy-done.9) | copy-start | bytes 3145732
  84.5 15.0 %copy-start.5 = (bf16[512,1024]{1,0:T(8,128)(2,1)S(1)}, bf16[512,1024]{1,0:T(8,128)(2,1)}, u32[]{:S(2)}) copy-start(bf16[512,1024]{1,0:T(8,128)(2,1)} %x_ref.5) | copy-start | bytes 3145732
  84.5 15.0 %copy-start.8 = (bf16[1024,1024]{1,0:T(8,128)(2,1)S(1)}, bf16[1024,1024]{1,0:T(8,128)(2,1)}, u32[]{:S(2)}) copy-start(bf16[1024,1024]{1,0:T(8,128)(2,1)} %w_ref.5) | copy-start | bytes 6291460
  84.5 15.0 %copy-start.11 = (f32[1024]{0:T(1024)S(1)}, f32[1024]{0:T(1024)}, u32[]{:S(2)}) copy-start(f32[1024]{0:T(1024)} %param.15) | copy-start | bytes 12292
  84.7 10.2 %collective-permute-start.14 = (bf16[256,512]{1,0:T(8,128)(2,1)S(1)}, bf16[256,512]{1,0:T(8,128)(2,1)S(1)}, u32[]{:S(2)}, u32[]{:S(2)}) collective-permute-start(bf16[256,512]{1,0:T(8,128)(2,1)S(1)} %pad_maximum_fusion.5), channel_id=1, source_target_pairs={{0,6},{1,7},{2,4},{3,5},{4,2},{5,3},{6,0},{7,1},{8,14},{9,15},{10,... | collective-permute-start | bytes 786440 | tf_op jit(solution)/shard_map/ppermute | solution.py:366
  86.3 12.9 %collective-permute-start.13 = (bf16[256,512]{1,0:T(8,128)(2,1)S(1)}, bf16[256,512]{1,0:T(8,128)(2,1)S(1)}, u32[]{:S(2)}, u32[]{:S(2)}) collective-permute-start(bf16[256,512]{1,0:T(8,128)(2,1)S(1)} %pad_maximum_fusion.4), channel_id=1, source_target_pairs={{0,4},{1,5},{2,6},{3,7},{4,0},{5,1},{6,2},{7,3},{8,12},{9,13},{10,... | collective-permute-start | bytes 786440 | tf_op jit(solution)/shard_map/ppermute | solution.py:366
  87.8 11.7 %collective-permute-start.12 = (bf16[256,512]{1,0:T(8,128)(2,1)S(1)}, bf16[256,512]{1,0:T(8,128)(2,1)S(1)}, u32[]{:S(2)}, u32[]{:S(2)}) collective-permute-start(bf16[256,512]{1,0:T(8,128)(2,1)S(1)} %pad_maximum_fusion.3), channel_id=1, source_target_pairs={{0,2},{1,3},{2,0},{3,1},{4,6},{5,7},{6,4},{7,5},{8,10},{9,11},{10,... | collective-permute-start | bytes 786440 | tf_op jit(solution)/shard_map/ppermute | solution.py:366

commit v14 on v12

--- a/solution.py
+++ b/solution.py
@@ -422,7 +422,7 @@
     far = []
     for number, pieces in enumerate(parts):
         if far:
-            pieces = tied(pieces, (far[-1], gated, send))
+            pieces = tied(pieces, send)
         held = {0: pieces}
         bit = count // 2
         while bit > 1:
@@ -431,18 +431,21 @@
             bit //= 2
         far.append(held)
     evens = sorted(far[0])
-    near = []
+    near, passed = [], []
     for number, pieces in enumerate(parts):
+        onward = [far[number][key] for key in evens[1:]]
         if number:
-            pieces = tied(pieces, [far[number][key] for key in evens[1:]])
+            pieces, onward = tied((pieces, onward), (onward, passed[-1]))
+        passed.append([neighbours(held, count) for held in onward])
         near.append(neighbours(pieces, count))
 
     got = lax.all_to_all(
         send.reshape(columns, capacity, -1), "cand", split_axis=0, concat_axis=0, tiled=True
     ).reshape(slots, -1)
     arrived = [gated] + near[0]
-    for key in evens[1:]:
-        arrived += far[0][key]
+    for held in far:
+        for key in evens[1:]:
+            arrived += held[key]
     slot, started = slot_column(owner_row ^ me, columns, capacity, arrived)
     early = []
     after = [started]
@@ -451,7 +454,7 @@
         held = far[number]
         close = (1, near[number], 0, heads)
         segments = [(key, held[key], 0, heads) for key in evens] + [close] * (number == 0)
-        cuts = [(key | 1, neighbours(held[key], count), 0, heads) for key in evens[1:]]
+        cuts = [(key | 1, cut, 0, heads) for key, cut in zip(evens[1:], passed[number])]
         cuts += [close] * (number > 0)
         base = attend(
             hist_len, after, got, segments, None, first, heads, size, None, F32, 0.0

time: 105 us -> 106 us (level)
  starting transfers between devices: 24 us -> 26.2 us
    ppermute x16, starting transfers between devices: 20.2 us -> 22.4 us  [swap(): return lax.ppermute(array, axis, [(i, i ^ bits) for i in range(count)])]
    unnamed x28 -> x32, local copies, waits for them, and re-layouts: 6.27 us -> 7.05 us
  transfers between devices with their start and end apart: 17 -> 17, of which waited for: 8 -> 7; matrix products, arithmetic and copies ran while one was open for 0% -> 0% of each run, Pallas kernels for 20% -> 19%
where the time goes in v14:
time: 106 us
  waiting for transfers between devices  47.3 us (45%)
  starting transfers between devices  26.2 us (25%)
  Pallas kernels  24.1 us (23%)
  local copies, waits for them, and re-layouts  7.16 us (7%)
  between operations  1.14 us (1%)
    ppermute x16, waiting for transfers between devices, swap(): return lax.ppermute(array, axis, [(i, i ^ bits) for i in range(count)])  47.3 us
    ppermute x16, starting transfers between devices, swap(): return lax.ppermute(array, axis, [(i, i ^ bits) for i in range(count)])  22.4 us
    pallas_call x4, Pallas kernels, attend(): pl.pallas_call(functools.partial(attend_kernel, size, heads, first, start...  14 us
    unnamed x32, local copies, waits for them, and re-layouts  7.05 us
    all_to_all x1, starting transfers between devices, per_device(): lax.all_to_all(send.reshape(columns, capacity, -1), 'cand', split_axis=0,...  3.8 us
    pallas_call x1, Pallas kernels, project_queries(): pl.pallas_call(query_kernel, in_specs=whole(4), out_specs=whole()[0], out...  3.29 us
    pallas_call x1, Pallas kernels, finish(): pl.pallas_call(functools.partial(finish_kernel, len(early), capacity, slo...  3.09 us
  transfers between devices with their start and end apart: 17, of which 7 were waited for; matrix products, arithmetic and copies ran while one was open for 0% of the time, Pallas kernels for 19%

profile of v14, /device:TPU:0, one launch (start us, length us, event | category | flops | bytes accessed | tf_op | source)
XLA Modules:
  0.0 106.1 jit_solution(15615514542231391865)
XLA Ops:
  0.0 0.7 copy-done.6
  0.7 1.2 %copy-done.9 = bf16[1,256,2048]{2,1,0:T(8,128)(2,1)S(1)} copy-done((bf16[1,256,2048]{2,1,0:T(8,128)(2,1)S(1)}, bf16[1,256,2048]{2,1,0:T(8,128)(2,1)}, u32[]{:S(2)}) %copy-start.9) | copy-done | bytes 1048600
  1.9 1.3 %prepare.1 = (s32[8,512]{1,0:T(8,128)S(1)}, bf16[256,1024]{1,0:T(8,128)(2,1)}, bf16[256,1024]{1,0:T(8,128)(2,1)}) custom-call(s32[1,512]{1,0:T(1,128)S(1)} %bitcast.12, bf16[256,2048]{1,0:T(8,128)(2,1)S(1)} %bitcast.13), custom_call_target="tpu_custom_call" | custom-call | flops 6000000000 | tf_op jit(solution)/shard_map/prepare/pallas_call | solution.py:148
  3.2 4.1 %collective-permute-start.1 = (bf16[256,1024]{1,0:T(8,128)(2,1)}, bf16[256,1024]{1,0:T(8,128)(2,1)}, u32[]{:S(2)}, u32[]{:S(2)}) collective-permute-start(bf16[256,1024]{1,0:T(8,128)(2,1)} %get-tuple-element.25.refs_2_), channel_id=1, source_target_pairs={{0,16},{8,24},{16,0},{24,8},{1,17},{9,25},{17,1},{25,9},{2,18},{10... | collective-permute-start | bytes 1572872 | tf_op jit(solution)/shard_map/ppermute | solution.py:373
  7.3 1.6 %collective-permute-start = (bf16[256,1024]{1,0:T(8,128)(2,1)}, bf16[256,1024]{1,0:T(8,128)(2,1)}, u32[]{:S(2)}, u32[]{:S(2)}) collective-permute-start(bf16[256,1024]{1,0:T(8,128)(2,1)} %get-tuple-element.25.refs_2_), channel_id=1, source_target_pairs={{0,8},{8,0},{16,24},{24,16},{1,9},{9,1},{17,25},{25,17},{2,10},{10... | collective-permute-start | bytes 1572872 | tf_op jit(solution)/shard_map/ppermute | solution.py:373
  8.9 0.0 copy-done
  8.9 0.0 copy-done.3
  8.9 0.0 copy-done.13
  8.9 3.3 %project_queries.1 = bf16[1024,1152]{1,0:T(8,128)(2,1)S(1)} custom-call(s32[8,512]{1,0:T(8,128)S(1)} %get-tuple-element.27.slot_ref, s32[1,512]{1,0:T(1,128)S(1)} %bitcast.15, bf16[512,1024]{1,0:T(8,128)(2,1)S(1)} %copy-done.3, bf16[1024,2048]{1,0:T(8,128)(2,1)S(1)} %copy-done), custom_call_target="tpu_custom_call" | custom-call | flops 2147483648 | bytes 5242880 | tf_op jit(solution)/shard_map/project_queries/pallas_call | solution.py:82
  12.2 0.0 copy-start.2
  12.2 1.4 %copy-done.2 = bf16[1024,1152]{1,0:T(8,128)(2,1)} copy-done((bf16[1024,1152]{1,0:T(8,128)(2,1)}, bf16[1024,1152]{1,0:T(8,128)(2,1)S(1)}, u32[]{:S(2)}) %copy-start.2) | copy-done | bytes 2359320
  13.6 0.3 collective-permute-start.2
  14.0 3.8 %all-to-all-start = ((bf16[8,128,1152]{2,1,0:T(8,128)(2,1)}), bf16[8,128,1152]{2,1,0:T(8,128)(2,1)S(1)}, u32[]{:S(2)}, u32[]{:S(2)}) async-start(bf16[8,128,1152]{2,1,0:T(8,128)(2,1)} %bitcast.11), calls=%async_computation | async-start | bytes 4718592 | tf_op jit(solution)/shard_map/all_to_all | solution.py:442
  18.4 0.0 copy-start.1
  18.4 2.2 %copy-done.1 = bf16[1024,2048]{1,0:T(8,128)(2,1)S(1)} copy-done((bf16[1024,2048]{1,0:T(8,128)(2,1)S(1)}, bf16[1024,2048]{1,0:T(8,128)(2,1)}, u32[]{:S(2)}) %copy-start.1) | copy-done | bytes 4194328
  20.6 1.4 %project_gate.1 = (bf16[512,1024]{1,0:T(8,128)(2,1)S(1)}, s32[8,128]{1,0:T(8,128)S(1)}) custom-call(bf16[512,1024]{1,0:T(8,128)(2,1)S(1)} %copy-done.3, bf16[1024,2048]{1,0:T(8,128)(2,1)S(1)} %copy-done.1), custom_call_target="tpu_custom_call" | custom-call | flops 1073741824 | bytes 4194304 | tf_op jit(solution)/shard_map/project_gate/pallas_call | solution.py:109
  22.0 0.0 copy-done.7
  22.0 0.0 copy-start.10
  22.0 10.5 %collective-permute-done.1.refs_2_.refs_3_ = bf16[256,1024]{1,0:T(8,128)(2,1)} collective-permute-done((bf16[256,1024]{1,0:T(8,128)(2,1)}, bf16[256,1024]{1,0:T(8,128)(2,1)}, u32[]{:S(2)}, u32[]{:S(2)}) %collective-permute-start.1) | collective-permute-done | bytes 524320 | tf_op jit(solution)/shard_map/ppermute | solution.py:373
  32.5 0.0 collective-permute-start.3
  32.5 0.0 collective-permute-done.refs_1_.refs_4_
  32.5 20.9 %collective-permute-done.2.refs_3_.refs_1_.refs_6_ = bf16[256,1024]{1,0:T(8,128)(2,1)} collective-permute-done((bf16[256,1024]{1,0:T(8,128)(2,1)}, bf16[256,1024]{1,0:T(8,128)(2,1)}, u32[]{:S(2)}, u32[]{:S(2)}) %collective-permute-start.2) | collective-permute-done | bytes 524320 | tf_op jit(solution)/shard_map/ppermute | solution.py:373
  53.4 0.3 slot_column.1
  53.7 0.0 copy-done.10
  53.8 0.0 copy-start.14
  53.8 0.7 copy-done.14
  54.5 0.0 collective-permute-done.3.refs_1_
  54.5 0.8 copy-done.4
  55.3 0.6 collective-permute-start.9
  55.9 1.4 %collective-permute-start.10 = (bf16[256,1024]{1,0:T(8,128)(2,1)}, bf16[256,1024]{1,0:T(8,128)(2,1)}, u32[]{:S(2)}, u32[]{:S(2)}) collective-permute-start(bf16[256,1024]{1,0:T(8,128)(2,1)} %get-tuple-element.36.refs_5_), channel_id=1, source_target_pairs={{0,8},{8,0},{16,24},{24,16},{1,9},{9,1},{17,25},{25,17},{2,10},{10... | collective-permute-start | bytes 1572872 | tf_op jit(solution)/shard_map/ppermute | solution.py:373
  57.3 0.0 all-to-all-done
  57.3 5.0 %attend.4.refs_2_ = f32[1024,512]{1,0:T(8,128)S(1)} custom-call(s32[1]{0:T(128)S(6)} %copy.9.length_ref, s32[8,128]{1,0:T(8,128)S(1)} %get-tuple-element.31.refs_0_, bf16[1024,1152]{1,0:T(8,128)(2,1)S(1)} %bitcast.7, bf16[256,1024]{1,0:T(8,128)(2,1)} %get-tuple-element.25.refs_2_, bf16[256,1024]{1,0:T(8,128)(2,1)} %collective-permute-done.1.refs_2_.refs_3_, ...), custom_call_target="tpu_custom_call" | custom-call | bytes 3670016 | tf_op jit(solution)/shard_map/attend/pallas_call | solution.py:281
  62.3 1.5 %attend.5 = (bf16[512,512]{1,0:T(8,128)(2,1)S(1)}, bf16[256,512]{1,0:T(8,128)(2,1)S(1)}, bf16[256,512]{1,0:T(8,128)(2,1)S(1)}) custom-call(s32[1]{0:T(128)S(6)} %copy.9.length_ref, bf16[1024,1152]{1,0:T(8,128)(2,1)S(1)} %bitcast.8, bf16[256,1024]{1,0:T(8,128)(2,1)S(1)} %copy-done.5, f32[1024,512]{1,0:T(8,128)S(1)} %attend.4.refs_2_), custom_call_target="tpu_custom_call" | custom-call | bytes 2621440 | tf_op jit(solution)/shard_map/attend/pallas_call | solution.py:281
  63.8 0.1 collective-permute-start.4
  63.8 0.5 collective-permute-start.6
  64.4 1.0 collective-permute-done.4.refs_1_
  65.4 7.7 %collective-permute-start.5 = (bf16[256,512]{1,0:T(8,128)(2,1)S(1)}, bf16[256,512]{1,0:T(8,128)(2,1)S(1)}, u32[]{:S(2)}, u32[]{:S(2)}) collective-permute-start(bf16[256,512]{1,0:T(8,128)(2,1)S(1)} %pad_maximum_fusion.refs_1_), channel_id=1, source_target_pairs={{0,2},{1,3},{2,0},{3,1},{4,6},{5,7},{6,4},{7,5},{8,10},{9,11},{10,... | collective-permute-start | bytes 786440 | tf_op jit(solution)/shard_map/ppermute | solution.py:373
  73.1 0.0 collective-permute-done.6
  73.2 1.6 %collective-permute-start.7 = (bf16[256,512]{1,0:T(8,128)(2,1)S(1)}, bf16[256,512]{1,0:T(8,128)(2,1)S(1)}, u32[]{:S(2)}, u32[]{:S(2)}) collective-permute-start(bf16[256,512]{1,0:T(8,128)(2,1)S(1)} %pad_maximum_fusion.1.refs_2_), channel_id=1, source_target_pairs={{0,4},{1,5},{2,6},{3,7},{4,0},{5,1},{6,2},{7,3},{8,12},{9,13},{10,... | collective-permute-start | bytes 786440 | tf_op jit(solution)/shard_map/ppermute | solution.py:373
  74.8 0.3 collective-permute-start.8
  75.0 3.7 %attend.6.refs_3_ = f32[1024,512]{1,0:T(8,128)S(1)} custom-call(s32[1]{0:T(128)S(6)} %copy.9.length_ref, s32[8,128]{1,0:T(8,128)S(1)} %wait_for.1.refs_0_, bf16[256,512]{1,0:T(8,128)(2,1)S(1)} %pad_maximum_fusion.refs_1_, bf16[256,512]{1,0:T(8,128)(2,1)S(1)} %pad_maximum_fusion.1.refs_2_, bf16[256,512]{1,0:T(8,128)(2,1)S(1)} %pad_maximum_fusion.2.refs_3_, ...), custom_call_target="tpu_custom_call" | custom-call | bytes 3145728 | tf_op jit(solution)/shard_map/attend/pallas_call | solution.py:281
  78.7 0.0 collective-permute-done.9.refs_1_
  78.7 1.1 %collective-permute-done.10.refs_2_ = bf16[256,1024]{1,0:T(8,128)(2,1)} collective-permute-done((bf16[256,1024]{1,0:T(8,128)(2,1)}, bf16[256,1024]{1,0:T(8,128)(2,1)}, u32[]{:S(2)}, u32[]{:S(2)}) %collective-permute-start.10) | collective-permute-done | bytes 524320 | tf_op jit(solution)/shard_map/ppermute | solution.py:373
  79.9 4.0 %attend.7 = (bf16[512,512]{1,0:T(8,128)(2,1)S(1)}, bf16[256,512]{1,0:T(8,128)(2,1)S(1)}, bf16[256,512]{1,0:T(8,128)(2,1)S(1)}) custom-call(s32[1]{0:T(128)S(6)} %copy.9.length_ref, bf16[1024,1152]{1,0:T(8,128)(2,1)S(1)} %bitcast.10, bf16[256,1024]{1,0:T(8,128)(2,1)} %collective-permute-done.9.refs_1_, bf16[256,1024]{1,0:T(8,128)(2,1)} %collective-permute-done.10.refs_2_, ...), custom_call_target="tpu_custom_call" | custom-call | flops 21474836480 | bytes 3145728 | tf_op jit(solution)/shard_map/attend/pallas_call | solution.py:281
  83.8 0.1 collective-permute-start.11
  83.9 0.5 collective-permute-start.12
  84.4 0.0 collective-permute-done.5.refs_2_
  84.4 2.5 %collective-permute-done.7.refs_3_ = bf16[256,512]{1,0:T(8,128)(2,1)S(1)} collective-permute-done((bf16[256,512]{1,0:T(8,128)(2,1)S(1)}, bf16[256,512]{1,0:T(8,128)(2,1)S(1)}, u32[]{:S(2)}, u32[]{:S(2)}) %collective-permute-start.7) | collective-permute-done | bytes 262176 | tf_op jit(solution)/shard_map/ppermute | solution.py:373
  86.9 0.0 collective-permute-done.8.refs_4_
  86.9 0.0 copy-done.15
  86.9 0.7 collect.1.refs_0_
  87.6 0.0 copy-start.8
  87.6 0.0 copy-start.11
  87.7 0.0 copy-start.12
  87.7 0.0 collective-permute-done.11.refs_2_
  87.7 0.0 collective-permute-done.12
  87.8 1.2 %collective-permute-start.13 = (bf16[256,512]{1,0:T(8,128)(2,1)S(1)}, bf16[256,512]{1,0:T(8,128)(2,1)S(1)}, u32[]{:S(2)}, u32[]{:S(2)}) collective-permute-start(bf16[256,512]{1,0:T(8,128)(2,1)S(1)} %pad_maximum_fusion.3), channel_id=1, source_target_pairs={{0,2},{1,3},{2,0},{3,1},{4,6},{5,7},{6,4},{7,5},{8,10},{9,11},{10,... | collective-permute-start | bytes 786440 | tf_op jit(solution)/shard_map/ppermute | solution.py:373
  89.1 1.6 %collective-permute-start.14 = (bf16[256,512]{1,0:T(8,128)(2,1)S(1)}, bf16[256,512]{1,0:T(8,128)(2,1)S(1)}, u32[]{:S(2)}, u32[]{:S(2)}) collective-permute-start(bf16[256,512]{1,0:T(8,128)(2,1)S(1)} %pad_maximum_fusion.4), channel_id=1, source_target_pairs={{0,4},{1,5},{2,6},{3,7},{4,0},{5,1},{6,2},{7,3},{8,12},{9,13},{10,... | collective-permute-start | bytes 786440 | tf_op jit(solution)/shard_map/ppermute | solution.py:373
  90.7 0.9 collective-permute-start.15
  91.5 5.6 %collective-permute-done.13.refs_3_ = bf16[256,512]{1,0:T(8,128)(2,1)S(1)} collective-permute-done((bf16[256,512]{1,0:T(8,128)(2,1)S(1)}, bf16[256,512]{1,0:T(8,128)(2,1)S(1)}, u32[]{:S(2)}, u32[]{:S(2)}) %collective-permute-start.13) | collective-permute-done | bytes 262176 | tf_op jit(solution)/shard_map/ppermute | solution.py:373
  97.1 5.7 %collective-permute-done.14.refs_4_ = bf16[256,512]{1,0:T(8,128)(2,1)S(1)} collective-permute-done((bf16[256,512]{1,0:T(8,128)(2,1)S(1)}, bf16[256,512]{1,0:T(8,128)(2,1)S(1)}, u32[]{:S(2)}, u32[]{:S(2)}) %collective-permute-start.14) | collective-permute-done | bytes 262176 | tf_op jit(solution)/shard_map/ppermute | solution.py:373
  102.8 0.0 collective-permute-done.15.refs_5_
  102.8 0.0 copy-done.11
  102.8 3.1 %finish.1 = bf16[512,1024]{1,0:T(8,128)(2,1)} custom-call(s32[512,128]{1,0:T(8,128)S(1)} %copy-done.15, f32[1,1024]{1,0:T(1,128)S(1)} %bitcast.14, bf16[512,1024]{1,0:T(8,128)(2,1)S(1)} %copy-done.11, bf16[512,1024]{1,0:T(8,128)(2,1)S(1)} %copy-done.3, bf16[1024,1024]{1,0:T(8,128)(2,1)S(1)} %copy-done.8, bf16[512,512]{1,0:T(8,128)(2,1)S(1)} %collect.1.refs_0_, ...), custom_call_target="tpu_custom_call" | custom-call | flops 2147483648 | bytes 7340032 | tf_op jit(solution)/shard_map/finish/pallas_call | solution.py:358
  (26 shorter events, 0.3 us)
Async XLA Ops:
  0.0 0.7 copy-start.6
  0.7 1.2 %copy-start.9 = (bf16[1,256,2048]{2,1,0:T(8,128)(2,1)S(1)}, bf16[1,256,2048]{2,1,0:T(8,128)(2,1)}, u32[]{:S(2)}) copy-start(bf16[1,256,2048]{2,1,0:T(8,128)(2,1)} %param.12) | copy-start | bytes 3145732
  1.9 7.0 %copy-start = (bf16[1024,2048]{1,0:T(8,128)(2,1)S(1)}, bf16[1024,2048]{1,0:T(8,128)(2,1)}, u32[]{:S(2)}) copy-start(bf16[1024,2048]{1,0:T(8,128)(2,1)} %w_ref.4) | copy-start | bytes 12582916
  1.9 7.0 %copy-start.3 = (bf16[512,1024]{1,0:T(8,128)(2,1)S(1)}, bf16[512,1024]{1,0:T(8,128)(2,1)}, u32[]{:S(2)}) copy-start(bf16[512,1024]{1,0:T(8,128)(2,1)} %x_ref.5) | copy-start | bytes 3145732
  1.9 7.0 %copy-start.13 = (s32[512]{0:T(512)S(1)}, s32[512]{0:T(512)}, u32[]{:S(2)}) copy-start(s32[512]{0:T(512)} %param.10) | copy-start | bytes 6148
  3.2 29.3 %collective-permute-start.1 = (bf16[256,1024]{1,0:T(8,128)(2,1)}, bf16[256,1024]{1,0:T(8,128)(2,1)}, u32[]{:S(2)}, u32[]{:S(2)}) collective-permute-start(bf16[256,1024]{1,0:T(8,128)(2,1)} %get-tuple-element.25.refs_2_), channel_id=1, source_target_pairs={{0,16},{8,24},{16,0},{24,8},{1,17},{9,25},{17,1},{25,9},{2,18},{10... | collective-permute-start | bytes 1572872 | tf_op jit(solution)/shard_map/ppermute | solution.py:373
  7.3 25.2 %collective-permute-start = (bf16[256,1024]{1,0:T(8,128)(2,1)}, bf16[256,1024]{1,0:T(8,128)(2,1)}, u32[]{:S(2)}, u32[]{:S(2)}) collective-permute-start(bf16[256,1024]{1,0:T(8,128)(2,1)} %get-tuple-element.25.refs_2_), channel_id=1, source_target_pairs={{0,8},{8,0},{16,24},{24,16},{1,9},{9,1},{17,25},{25,17},{2,10},{10... | collective-permute-start | bytes 1572872 | tf_op jit(solution)/shard_map/ppermute | solution.py:373
  12.2 1.4 %copy-start.2 = (bf16[1024,1152]{1,0:T(8,128)(2,1)}, bf16[1024,1152]{1,0:T(8,128)(2,1)S(1)}, u32[]{:S(2)}) copy-start(bf16[1024,1152]{1,0:T(8,128)(2,1)S(1)} %project_queries.1) | copy-start | bytes 7077892
  13.6 39.8 %collective-permute-start.2 = (bf16[256,1024]{1,0:T(8,128)(2,1)}, bf16[256,1024]{1,0:T(8,128)(2,1)}, u32[]{:S(2)}, u32[]{:S(2)}) collective-permute-start(bf16[256,1024]{1,0:T(8,128)(2,1)} %get-tuple-element.36.refs_5_), channel_id=1, source_target_pairs={{0,16},{8,24},{16,0},{24,8},{1,17},{9,25},{17,1},{25,9},{2,18},{10... | collective-permute-start | bytes 1572872 | tf_op jit(solution)/shard_map/ppermute | solution.py:373
  14.0 43.3 %all-to-all-start = ((bf16[8,128,1152]{2,1,0:T(8,128)(2,1)}), bf16[8,128,1152]{2,1,0:T(8,128)(2,1)S(1)}, u32[]{:S(2)}, u32[]{:S(2)}) async-start(bf16[8,128,1152]{2,1,0:T(8,128)(2,1)} %bitcast.11), calls=%async_computation | async-start | bytes 4718592 | tf_op jit(solution)/shard_map/all_to_all | solution.py:442
  18.4 2.2 %copy-start.1 = (bf16[1024,2048]{1,0:T(8,128)(2,1)S(1)}, bf16[1024,2048]{1,0:T(8,128)(2,1)}, u32[]{:S(2)}) copy-start(bf16[1024,2048]{1,0:T(8,128)(2,1)} %w_ref.4) | copy-start | bytes 12582916
  20.6 1.4 %copy-start.7 = (s32[512,1]{0,1:T(1,128)S(1)}, s32[512,1]{0,1:T(1,128)}, u32[]{:S(2)}) copy-start(s32[512,1]{0,1:T(1,128)} %param.9) | copy-start | bytes 6148
  22.0 31.7 %copy-start.10 = (bf16[512,1024]{1,0:T(8,128)(2,1)}, bf16[512,1024]{1,0:T(8,128)(2,1)S(1)}, u32[]{:S(2)}) copy-start(bf16[512,1024]{1,0:T(8,128)(2,1)S(1)} %get-tuple-element.30.gate_ref) | copy-start | bytes 3145732
  32.5 21.9 %collective-permute-start.3 = (bf16[256,1024]{1,0:T(8,128)(2,1)}, bf16[256,1024]{1,0:T(8,128)(2,1)S(1)}, u32[]{:S(2)}, u32[]{:S(2)}) collective-permute-start(bf16[256,1024]{1,0:T(8,128)(2,1)} %collective-permute-done.1.refs_2_.refs_3_), channel_id=1, source_target_pairs={{0,8},{8,0},{16,24},{24,16},{1,9},{9,1},{17,25},{25,17},{2,10},{10... | collective-permute-start | bytes 1572872 | tf_op jit(solution)/shard_map/ppermute | solution.py:373
  53.8 0.7 copy-start.14
  54.5 0.8 copy-start.4
  55.3 23.4 %collective-permute-start.9 = (bf16[256,1024]{1,0:T(8,128)(2,1)}, bf16[256,1024]{1,0:T(8,128)(2,1)}, u32[]{:S(2)}, u32[]{:S(2)}) collective-permute-start(bf16[256,1024]{1,0:T(8,128)(2,1)} %collective-permute-done.2.refs_3_.refs_1_.refs_6_), channel_id=1, source_target_pairs={{0,8},{8,0},{16,24},{24,16},{1,9},{9,1},{17,25},{25,17},{2,10},{10... | collective-permute-start | bytes 1572872 | tf_op jit(solution)/shard_map/ppermute | solution.py:373
  55.9 24.0 %collective-permute-start.10 = (bf16[256,1024]{1,0:T(8,128)(2,1)}, bf16[256,1024]{1,0:T(8,128)(2,1)}, u32[]{:S(2)}, u32[]{:S(2)}) collective-permute-start(bf16[256,1024]{1,0:T(8,128)(2,1)} %get-tuple-element.36.refs_5_), channel_id=1, source_target_pairs={{0,8},{8,0},{16,24},{24,16},{1,9},{9,1},{17,25},{25,17},{2,10},{10... | collective-permute-start | bytes 1572872 | tf_op jit(solution)/shard_map/ppermute | solution.py:373
  57.3 5.0 %copy-start.5 = (bf16[256,1024]{1,0:T(8,128)(2,1)S(1)}, bf16[256,1024]{1,0:T(8,128)(2,1)}, u32[]{:S(2)}) copy-start(bf16[256,1024]{1,0:T(8,128)(2,1)} %copy-done.4) | copy-start | bytes 1572868
  63.8 1.6 %collective-permute-start.4 = (bf16[256,512]{1,0:T(8,128)(2,1)S(1)}, bf16[256,512]{1,0:T(8,128)(2,1)S(1)}, u32[]{:S(2)}, u32[]{:S(2)}) collective-permute-start(bf16[256,512]{1,0:T(8,128)(2,1)S(1)} %get-tuple-element.33), channel_id=1, source_target_pairs={{0,1},{1,0},{2,3},{3,2},{4,5},{5,4},{6,7},{7,6},{8,9},{9,8},{10,11... | collective-permute-start | bytes 786440 | tf_op jit(solution)/shard_map/ppermute | solution.py:373
  63.8 9.3 %collective-permute-start.6 = (bf16[256,512]{1,0:T(8,128)(2,1)S(1)}, bf16[256,512]{1,0:T(8,128)(2,1)S(1)}, u32[]{:S(2)}, u32[]{:S(2)}) collective-permute-start(bf16[256,512]{1,0:T(8,128)(2,1)S(1)} %get-tuple-element.34), channel_id=1, source_target_pairs={{0,1},{1,0},{2,3},{3,2},{4,5},{5,4},{6,7},{7,6},{8,9},{9,8},{10,11... | collective-permute-start | bytes 786440 | tf_op jit(solution)/shard_map/ppermute | solution.py:373
  65.4 19.0 %collective-permute-start.5 = (bf16[256,512]{1,0:T(8,128)(2,1)S(1)}, bf16[256,512]{1,0:T(8,128)(2,1)S(1)}, u32[]{:S(2)}, u32[]{:S(2)}) collective-permute-start(bf16[256,512]{1,0:T(8,128)(2,1)S(1)} %pad_maximum_fusion.refs_1_), channel_id=1, source_target_pairs={{0,2},{1,3},{2,0},{3,1},{4,6},{5,7},{6,4},{7,5},{8,10},{9,11},{10,... | collective-permute-start | bytes 786440 | tf_op jit(solution)/shard_map/ppermute | solution.py:373
  73.2 13.8 %collective-permute-start.7 = (bf16[256,512]{1,0:T(8,128)(2,1)S(1)}, bf16[256,512]{1,0:T(8,128)(2,1)S(1)}, u32[]{:S(2)}, u32[]{:S(2)}) collective-permute-start(bf16[256,512]{1,0:T(8,128)(2,1)S(1)} %pad_maximum_fusion.1.refs_2_), channel_id=1, source_target_pairs={{0,4},{1,5},{2,6},{3,7},{4,0},{5,1},{6,2},{7,3},{8,12},{9,13},{10,... | collective-permute-start | bytes 786440 | tf_op jit(solution)/shard_map/ppermute | solution.py:373
  74.8 12.1 %collective-permute-start.8 = (bf16[256,512]{1,0:T(8,128)(2,1)S(1)}, bf16[256,512]{1,0:T(8,128)(2,1)S(1)}, u32[]{:S(2)}, u32[]{:S(2)}) collective-permute-start(bf16[256,512]{1,0:T(8,128)(2,1)S(1)} %pad_maximum_fusion.2.refs_3_), channel_id=1, source_target_pairs={{0,6},{1,7},{2,4},{3,5},{4,2},{5,3},{6,0},{7,1},{8,14},{9,15},{10,... | collective-permute-start | bytes 786440 | tf_op jit(solution)/shard_map/ppermute | solution.py:373
  78.7 8.2 %copy-start.15 = (s32[512,128]{1,0:T(8,128)S(1)}, s32[512,128]{1,0:T(8,128)}, u32[]{:S(2)}) copy-start(s32[512,128]{1,0:T(8,128)} %copy-done.14) | copy-start | bytes 786436
  83.8 3.8 %collective-permute-start.11 = (bf16[256,512]{1,0:T(8,128)(2,1)S(1)}, bf16[256,512]{1,0:T(8,128)(2,1)S(1)}, u32[]{:S(2)}, u32[]{:S(2)}) collective-permute-start(bf16[256,512]{1,0:T(8,128)(2,1)S(1)} %get-tuple-element.38), channel_id=1, source_target_pairs={{0,1},{1,0},{2,3},{3,2},{4,5},{5,4},{6,7},{7,6},{8,9},{9,8},{10,11... | collective-permute-start | bytes 786440 | tf_op jit(solution)/shard_map/ppermute | solution.py:373
  83.9 3.8 %collective-permute-start.12 = (bf16[256,512]{1,0:T(8,128)(2,1)S(1)}, bf16[256,512]{1,0:T(8,128)(2,1)S(1)}, u32[]{:S(2)}, u32[]{:S(2)}) collective-permute-start(bf16[256,512]{1,0:T(8,128)(2,1)S(1)} %get-tuple-element.39), channel_id=1, source_target_pairs={{0,1},{1,0},{2,3},{3,2},{4,5},{5,4},{6,7},{7,6},{8,9},{9,8},{10,11... | collective-permute-start | bytes 786440 | tf_op jit(solution)/shard_map/ppermute | solution.py:373
  87.6 15.2 %copy-start.8 = (bf16[1024,1024]{1,0:T(8,128)(2,1)S(1)}, bf16[1024,1024]{1,0:T(8,128)(2,1)}, u32[]{:S(2)}) copy-start(bf16[1024,1024]{1,0:T(8,128)(2,1)} %w_ref.5) | copy-start | bytes 6291460
  87.6 15.2 %copy-start.11 = (bf16[512,1024]{1,0:T(8,128)(2,1)S(1)}, bf16[512,1024]{1,0:T(8,128)(2,1)}, u32[]{:S(2)}) copy-start(bf16[512,1024]{1,0:T(8,128)(2,1)} %copy-done.10) | copy-start | bytes 3145732
  87.7 15.2 %copy-start.12 = (f32[1024]{0:T(1024)S(1)}, f32[1024]{0:T(1024)}, u32[]{:S(2)}) copy-start(f32[1024]{0:T(1024)} %param.15) | copy-start | bytes 12292
  87.8 9.3 %collective-permute-start.13 = (bf16[256,512]{1,0:T(8,128)(2,1)S(1)}, bf16[256,512]{1,0:T(8,128)(2,1)S(1)}, u32[]{:S(2)}, u32[]{:S(2)}) collective-permute-start(bf16[256,512]{1,0:T(8,128)(2,1)S(1)} %pad_maximum_fusion.3), channel_id=1, source_target_pairs={{0,2},{1,3},{2,0},{3,1},{4,6},{5,7},{6,4},{7,5},{8,10},{9,11},{10,... | collective-permute-start | bytes 786440 | tf_op jit(solution)/shard_map/ppermute | solution.py:373
  89.1 13.8 %collective-permute-start.14 = (bf16[256,512]{1,0:T(8,128)(2,1)S(1)}, bf16[256,512]{1,0:T(8,128)(2,1)S(1)}, u32[]{:S(2)}, u32[]{:S(2)}) collective-permute-start(bf16[256,512]{1,0:T(8,128)(2,1)S(1)} %pad_maximum_fusion.4), channel_id=1, source_target_pairs={{0,4},{1,5},{2,6},{3,7},{4,0},{5,1},{6,2},{7,3},{8,12},{9,13},{10,... | collective-permute-start | bytes 786440 | tf_op jit(solution)/shard_map/ppermute | solution.py:373
  90.7 12.1 %collective-permute-start.15 = (bf16[256,512]{1,0:T(8,128)(2,1)S(1)}, bf16[256,512]{1,0:T(8,128)(2,1)S(1)}, u32[]{:S(2)}, u32[]{:S(2)}) collective-permute-start(bf16[256,512]{1,0:T(8,128)(2,1)S(1)} %pad_maximum_fusion.5), channel_id=1, source_target_pairs={{0,6},{1,7},{2,4},{3,5},{4,2},{5,3},{6,0},{7,1},{8,14},{9,15},{10,... | collective-permute-start | bytes 786440 | tf_op jit(solution)/shard_map/ppermute | solution.py:373

commit v15 on v13

--- a/solution.py
+++ b/solution.py
@@ -10,7 +10,7 @@
 
 HEADS = 8
 BLK = 128
-GROUPS = (4, 4)
+GROUPS = (3, 3, 2)
 norm_eps = 1e-06
 F32 = jnp.float32
 BF16 = jnp.bfloat16
@@ -424,16 +424,22 @@
     arrived = [gated, near] + [held[key] for held in far for key in evens[1:]]
     slot, started = slot_column(owner_row ^ me, columns, capacity, arrived)
     early = []
+    bases = []
     after = [started]
     behind = None
     for number, (first, heads) in enumerate(spans):
         held = far[number]
-        cuts = [(key | 1, [swap(held[key], "user", 1, count)], 0, heads) for key in evens[1:]]
+        passed = [held[key] for key in evens[1:]]
+        if number > 1:
+            passed, _ = lax.optimization_barrier((passed, bases[0]))
+        passed = [[swap(part, "user", 1, count)] for part in passed]
+        cuts = [(key | 1, cut, 0, heads) for key, cut in zip(evens[1:], passed)]
         segments = [(key, [held[key]], 0, heads) for key in evens]
         segments.append((1, [near], first, HEADS + first))
         base = attend(
             hist_len, after, got, segments, None, first, heads, size, None, F32, 0.0
         )[0]
+        bases.append(base)
         attn = attend(
             hist_len,
             [],

time: 103 us -> 104 us (level)
  waiting for transfers between devices: 43.9 us -> 31 us
  starting transfers between devices: 24.4 us -> 35 us
  Pallas kernels: 25.9 us -> 28.2 us
    ppermute x15 -> x22, waiting for transfers between devices: 43.9 us -> 31 us  [swap(): return lax.ppermute(array, axis, [(i, i ^ bits) for i in range(count)])]
    ppermute x15 -> x22, starting transfers between devices: 20.6 us -> 31.2 us  [swap(): return lax.ppermute(array, axis, [(i, i ^ bits) for i in range(count)])]
    pallas_call x4 -> x6, Pallas kernels: 14.7 us -> 16 us  [attend(): pl.pallas_call(functools.partial(attend_kernel, size, heads, first, start...]
    unnamed x30 -> x34, local copies, waits for them, and re-layouts: 7.2 us -> 7.91 us
  transfers between devices with their start and end apart: 16 -> 23, of which waited for: 9 -> 10; matrix products, arithmetic and copies ran while one was open for 0% -> 0% of each run, Pallas kernels for 20% -> 22%
where the time goes in v15:
time: 104 us
  starting transfers between devices  35 us (34%)
  waiting for transfers between devices  31 us (30%)
  Pallas kernels  28.2 us (27%)
  local copies, waits for them, and re-layouts  8.07 us (8%)
  between operations  1.26 us (1%)
    ppermute x22, starting transfers between devices, swap(): return lax.ppermute(array, axis, [(i, i ^ bits) for i in range(count)])  31.2 us
    ppermute x22, waiting for transfers between devices, swap(): return lax.ppermute(array, axis, [(i, i ^ bits) for i in range(count)])  31 us
    pallas_call x6, Pallas kernels, attend(): pl.pallas_call(functools.partial(attend_kernel, size, heads, first, start...  16 us
    unnamed x34, local copies, waits for them, and re-layouts  7.91 us
    all_to_all x1, starting transfers between devices, per_device(): lax.all_to_all(send.reshape(columns, capacity, -1), 'cand', split_axis=0,...  3.8 us
    pallas_call x1, Pallas kernels, finish(): pl.pallas_call(functools.partial(finish_kernel, len(early), capacity, slo...  3.48 us
    pallas_call x1, Pallas kernels, project_queries(): pl.pallas_call(query_kernel, in_specs=whole(4), out_specs=whole()[0], out...  3.29 us
    pallas_call x1, Pallas kernels, prepare(): pl.pallas_call(functools.partial(prepare_kernel, columns, capacity, spans...  2.37 us
  transfers between devices with their start and end apart: 23, of which 10 were waited for; matrix products, arithmetic and copies ran while one was open for 0% of the time, Pallas kernels for 22%

profile of v15, /device:TPU:0, one launch (start us, length us, event | category | flops | bytes accessed | tf_op | source)
XLA Modules:
  0.0 103.7 jit_solution(4627166402145211241)
XLA Ops:
  0.0 0.7 copy-done.8
  0.7 2.4 %prepare.1 = (s32[8,512]{1,0:T(8,128)S(1)}, bf16[256,768]{1,0:T(8,128)(2,1)}, bf16[256,768]{1,0:T(8,128)(2,1)}, bf16[256,512]{1,0:T(8,128)(2,1)S(1)}) custom-call(s32[1,512]{1,0:T(1,128)S(1)} %bitcast.14, bf16[256,2048]{1,0:T(8,128)(2,1)} %bitcast.1.kv_hbm), custom_call_target="tpu_custom_call" | custom-call | flops 6000000000 | tf_op jit(solution)/shard_map/prepare/pallas_call | solution.py:141
  3.1 0.7 copy-done.6
  3.8 3.0 %collective-permute-start = (bf16[256,2048]{1,0:T(8,128)(2,1)}, bf16[256,2048]{1,0:T(8,128)(2,1)S(1)}, u32[]{:S(2)}, u32[]{:S(2)}) collective-permute-start(bf16[256,2048]{1,0:T(8,128)(2,1)} %bitcast.1.kv_hbm), channel_id=1, source_target_pairs={{0,8},{8,0},{16,24},{24,16},{1,9},{9,1},{17,25},{25,17},{2,10},{10... | collective-permute-start | bytes 3145736 | tf_op jit(solution)/shard_map/ppermute | solution.py:366
  6.8 2.6 %collective-permute-start.1 = (bf16[256,768]{1,0:T(8,128)(2,1)}, bf16[256,768]{1,0:T(8,128)(2,1)}, u32[]{:S(2)}, u32[]{:S(2)}) collective-permute-start(bf16[256,768]{1,0:T(8,128)(2,1)} %get-tuple-element.35.refs_2_), channel_id=1, source_target_pairs={{0,16},{8,24},{16,0},{24,8},{1,17},{9,25},{17,1},{25,9},{2,18},{10... | collective-permute-start | bytes 1179656 | tf_op jit(solution)/shard_map/ppermute | solution.py:366
  9.4 3.3 %project_queries.1 = bf16[1024,1152]{1,0:T(8,128)(2,1)S(1)} custom-call(s32[8,512]{1,0:T(8,128)S(1)} %get-tuple-element.33.slot_ref, s32[1,512]{1,0:T(1,128)S(1)} %bitcast.16, bf16[512,1024]{1,0:T(8,128)(2,1)S(1)} %copy-done.3, bf16[1024,2048]{1,0:T(8,128)(2,1)S(1)} %copy-done), custom_call_target="tpu_custom_call" | custom-call | flops 2147483648 | bytes 5242880 | tf_op jit(solution)/shard_map/project_queries/pallas_call | solution.py:81
  12.7 1.4 %copy-done.2 = bf16[1024,1152]{1,0:T(8,128)(2,1)} copy-done((bf16[1024,1152]{1,0:T(8,128)(2,1)}, bf16[1024,1152]{1,0:T(8,128)(2,1)S(1)}, u32[]{:S(2)}) %copy-start.2) | copy-done | bytes 2359320
  14.1 0.3 collective-permute-start.2
  14.4 3.8 %all-to-all-start = ((bf16[8,128,1152]{2,1,0:T(8,128)(2,1)}), bf16[8,128,1152]{2,1,0:T(8,128)(2,1)S(1)}, u32[]{:S(2)}, u32[]{:S(2)}) async-start(bf16[8,128,1152]{2,1,0:T(8,128)(2,1)} %bitcast.13), calls=%async_computation | async-start | bytes 4718592 | tf_op jit(solution)/shard_map/all_to_all | solution.py:421
  18.2 2.7 %collective-permute-start.3 = (bf16[256,512]{1,0:T(8,128)(2,1)}, bf16[256,512]{1,0:T(8,128)(2,1)}, u32[]{:S(2)}, u32[]{:S(2)}) collective-permute-start(bf16[256,512]{1,0:T(8,128)(2,1)} %copy-done.6), channel_id=1, source_target_pairs={{0,16},{8,24},{16,0},{24,8},{1,17},{9,25},{17,1},{25,9},{2,18},{10... | collective-permute-start | bytes 786440 | tf_op jit(solution)/shard_map/ppermute | solution.py:366
  20.9 2.2 %copy-done.1 = bf16[1024,2048]{1,0:T(8,128)(2,1)S(1)} copy-done((bf16[1024,2048]{1,0:T(8,128)(2,1)S(1)}, bf16[1024,2048]{1,0:T(8,128)(2,1)}, u32[]{:S(2)}) %copy-start.1) | copy-done | bytes 4194328
  23.1 1.2 %copy-done.4 = bf16[512,1024]{1,0:T(8,128)(2,1)S(1)} copy-done((bf16[512,1024]{1,0:T(8,128)(2,1)S(1)}, bf16[512,1024]{1,0:T(8,128)(2,1)}, u32[]{:S(2)}) %copy-start.4) | copy-done | bytes 1048600
  24.3 1.4 %project_gate.1 = (bf16[512,1024]{1,0:T(8,128)(2,1)S(1)}, s32[8,128]{1,0:T(8,128)S(1)}) custom-call(bf16[512,1024]{1,0:T(8,128)(2,1)S(1)} %copy-done.4, bf16[1024,2048]{1,0:T(8,128)(2,1)S(1)} %copy-done.1), custom_call_target="tpu_custom_call" | custom-call | flops 1073741824 | bytes 4194304 | tf_op jit(solution)/shard_map/project_gate/pallas_call | solution.py:108
  25.7 0.0 copy-start.11
  25.7 1.0 copy-done.11
  27.4 11.8 %collective-permute-done.1.refs_2_.refs_3_ = bf16[256,768]{1,0:T(8,128)(2,1)} collective-permute-done((bf16[256,768]{1,0:T(8,128)(2,1)}, bf16[256,768]{1,0:T(8,128)(2,1)}, u32[]{:S(2)}, u32[]{:S(2)}) %collective-permute-start.1) | collective-permute-done | bytes 393248 | tf_op jit(solution)/shard_map/ppermute | solution.py:366
  39.2 3.5 %collective-permute-start.4 = (bf16[256,768]{1,0:T(8,128)(2,1)}, bf16[256,768]{1,0:T(8,128)(2,1)}, u32[]{:S(2)}, u32[]{:S(2)}) collective-permute-start(bf16[256,768]{1,0:T(8,128)(2,1)} %collective-permute-done.1.refs_2_.refs_3_), channel_id=1, source_target_pairs={{0,8},{8,0},{16,24},{24,16},{1,9},{9,1},{17,25},{25,17},{2,10},{10... | collective-permute-start | bytes 1179656 | tf_op jit(solution)/shard_map/ppermute | solution.py:366
  42.7 4.9 %collective-permute-done.2.refs_3_.refs_1_.refs_6_ = bf16[256,768]{1,0:T(8,128)(2,1)} collective-permute-done((bf16[256,768]{1,0:T(8,128)(2,1)}, bf16[256,768]{1,0:T(8,128)(2,1)}, u32[]{:S(2)}, u32[]{:S(2)}) %collective-permute-start.2) | collective-permute-done | bytes 393248 | tf_op jit(solution)/shard_map/ppermute | solution.py:366
  47.6 3.5 %collective-permute-start.10 = (bf16[256,768]{1,0:T(8,128)(2,1)}, bf16[256,768]{1,0:T(8,128)(2,1)}, u32[]{:S(2)}, u32[]{:S(2)}) collective-permute-start(bf16[256,768]{1,0:T(8,128)(2,1)} %collective-permute-done.2.refs_3_.refs_1_.refs_6_), channel_id=1, source_target_pairs={{0,8},{8,0},{16,24},{24,16},{1,9},{9,1},{17,25},{25,17},{2,10},{10... | collective-permute-start | bytes 1179656 | tf_op jit(solution)/shard_map/ppermute | solution.py:366
  51.1 3.0 %collective-permute-done.3.refs_4_.refs_1_.refs_6_ = bf16[256,512]{1,0:T(8,128)(2,1)} collective-permute-done((bf16[256,512]{1,0:T(8,128)(2,1)}, bf16[256,512]{1,0:T(8,128)(2,1)}, u32[]{:S(2)}, u32[]{:S(2)}) %collective-permute-start.3) | collective-permute-done | bytes 262176 | tf_op jit(solution)/shard_map/ppermute | solution.py:366
  54.2 0.0 collective-permute-done.refs_1_.refs_4_.refs_7_
  54.2 0.3 slot_column.1
  54.5 0.7 copy-done.15
  55.2 3.8 %attend.6.refs_2_ = f32[1024,384]{1,0:T(8,128)S(1)} custom-call(s32[1]{0:T(128)S(6)} %copy.9.length_ref, s32[8,128]{1,0:T(8,128)S(1)} %get-tuple-element.42.refs_0_, bf16[1024,1152]{1,0:T(8,128)(2,1)S(1)} %bitcast.7, bf16[256,768]{1,0:T(8,128)(2,1)} %get-tuple-element.35.refs_2_, bf16[256,768]{1,0:T(8,128)(2,1)} %collective-permute-done.1.refs_2_.refs_3_, ...), custom_call_target="tpu_custom_call" | custom-call | bytes 2752512 | tf_op jit(solution)/shard_map/attend/pallas_call | solution.py:274
  59.1 2.6 %collective-permute-start.16 = (bf16[256,512]{1,0:T(8,128)(2,1)}, bf16[256,512]{1,0:T(8,128)(2,1)S(1)}, u32[]{:S(2)}, u32[]{:S(2)}) collective-permute-start(bf16[256,512]{1,0:T(8,128)(2,1)} %collective-permute-done.3.refs_4_.refs_1_.refs_6_), channel_id=1, source_target_pairs={{0,8},{8,0},{16,24},{24,16},{1,9},{9,1},{17,25},{25,17},{2,10},{10... | collective-permute-start | bytes 786440 | tf_op jit(solution)/shard_map/ppermute | solution.py:366
  61.7 0.3 collective-permute-done.4.refs_1_
  62.0 2.2 %attend.7 = (bf16[512,384]{1,0:T(8,128)(2,1)S(1)}, bf16[256,384]{1,0:T(8,128)(2,1)S(1)}, bf16[256,384]{1,0:T(8,128)(2,1)S(1)}) custom-call(s32[1]{0:T(128)S(6)} %copy.9.length_ref, bf16[1024,1152]{1,0:T(8,128)(2,1)S(1)} %bitcast.8, bf16[256,768]{1,0:T(8,128)(2,1)} %collective-permute-done.4.refs_1_, f32[1024,384]{1,0:T(8,128)S(1)} %attend.6.refs_2_), custom_call_target="tpu_custom_call" | custom-call | bytes 1966080 | tf_op jit(solution)/shard_map/attend/pallas_call | solution.py:274
  64.2 0.1 collective-permute-start.5
  64.2 0.5 collective-permute-start.7
  64.8 0.9 collective-permute-done.5.refs_1_
  65.7 2.0 %collective-permute-start.6 = (bf16[256,384]{1,0:T(8,128)(2,1)S(1)}, bf16[256,384]{1,0:T(8,128)(2,1)S(1)}, u32[]{:S(2)}, u32[]{:S(2)}) collective-permute-start(bf16[256,384]{1,0:T(8,128)(2,1)S(1)} %pad_maximum_fusion.refs_1_), channel_id=1, source_target_pairs={{0,2},{1,3},{2,0},{3,1},{4,6},{5,7},{6,4},{7,5},{8,10},{9,11},{10,... | collective-permute-start | bytes 589832 | tf_op jit(solution)/shard_map/ppermute | solution.py:366
  67.8 0.0 collective-permute-done.7
  67.8 1.6 %collective-permute-start.8 = (bf16[256,384]{1,0:T(8,128)(2,1)S(1)}, bf16[256,384]{1,0:T(8,128)(2,1)S(1)}, u32[]{:S(2)}, u32[]{:S(2)}) collective-permute-start(bf16[256,384]{1,0:T(8,128)(2,1)S(1)} %pad_maximum_fusion.1.refs_2_), channel_id=1, source_target_pairs={{0,4},{1,5},{2,6},{3,7},{4,0},{5,1},{6,2},{7,3},{8,12},{9,13},{10,... | collective-permute-start | bytes 589832 | tf_op jit(solution)/shard_map/ppermute | solution.py:366
  69.4 0.2 collective-permute-start.9
  69.6 3.8 %attend.8.refs_2_ = f32[1024,384]{1,0:T(8,128)S(1)} custom-call(s32[1]{0:T(128)S(6)} %copy.9.length_ref, s32[8,128]{1,0:T(8,128)S(1)} %wait_for.2.refs_0_, bf16[256,384]{1,0:T(8,128)(2,1)S(1)} %pad_maximum_fusion.refs_1_, bf16[256,384]{1,0:T(8,128)(2,1)S(1)} %pad_maximum_fusion.1.refs_2_, bf16[256,384]{1,0:T(8,128)(2,1)S(1)} %pad_maximum_fusion.2.refs_3_, ...), custom_call_target="tpu_custom_call" | custom-call | bytes 2752512 | tf_op jit(solution)/shard_map/attend/pallas_call | solution.py:274
  73.5 0.0 collective-permute-done.10.refs_1_
  73.5 2.2 %attend.9 = (bf16[512,384]{1,0:T(8,128)(2,1)S(1)}, bf16[256,384]{1,0:T(8,128)(2,1)S(1)}, bf16[256,384]{1,0:T(8,128)(2,1)S(1)}) custom-call(s32[1]{0:T(128)S(6)} %copy.9.length_ref, bf16[1024,1152]{1,0:T(8,128)(2,1)S(1)} %bitcast.10, bf16[256,768]{1,0:T(8,128)(2,1)} %collective-permute-done.10.refs_1_, f32[1024,384]{1,0:T(8,128)S(1)} %attend.8.refs_2_), custom_call_target="tpu_custom_call" | custom-call | flops 8053063680 | bytes 1966080 | tf_op jit(solution)/shard_map/attend/pallas_call | solution.py:274
  75.6 0.1 collective-permute-start.11
  75.7 0.5 collective-permute-start.12
  76.2 2.5 %collective-permute-done.8.refs_3_ = bf16[256,384]{1,0:T(8,128)(2,1)S(1)} collective-permute-done((bf16[256,384]{1,0:T(8,128)(2,1)S(1)}, bf16[256,384]{1,0:T(8,128)(2,1)S(1)}, u32[]{:S(2)}, u32[]{:S(2)}) %collective-permute-start.8) | collective-permute-done | bytes 196640 | tf_op jit(solution)/shard_map/ppermute | solution.py:366
  78.8 0.7 collect.2.refs_0_
  79.5 0.0 collective-permute-done.11.refs_1_
  79.5 0.0 collective-permute-done.12
  79.6 1.2 %collective-permute-start.13 = (bf16[256,384]{1,0:T(8,128)(2,1)S(1)}, bf16[256,384]{1,0:T(8,128)(2,1)S(1)}, u32[]{:S(2)}, u32[]{:S(2)}) collective-permute-start(bf16[256,384]{1,0:T(8,128)(2,1)S(1)} %pad_maximum_fusion.3.refs_1_), channel_id=1, source_target_pairs={{0,2},{1,3},{2,0},{3,1},{4,6},{5,7},{6,4},{7,5},{8,10},{9,11},{10,... | collective-permute-start | bytes 589832 | tf_op jit(solution)/shard_map/ppermute | solution.py:366
  80.8 1.0 collective-permute-start.14
  81.9 1.5 %collective-permute-start.15 = (bf16[256,384]{1,0:T(8,128)(2,1)S(1)}, bf16[256,384]{1,0:T(8,128)(2,1)S(1)}, u32[]{:S(2)}, u32[]{:S(2)}) collective-permute-start(bf16[256,384]{1,0:T(8,128)(2,1)S(1)} %pad_maximum_fusion.5.refs_3_), channel_id=1, source_target_pairs={{0,6},{1,7},{2,4},{3,5},{4,2},{5,3},{6,0},{7,1},{8,14},{9,15},{10,... | collective-permute-start | bytes 589832 | tf_op jit(solution)/shard_map/ppermute | solution.py:366
  83.4 3.1 %attend.10.refs_2_ = f32[1024,256]{1,0:T(8,128)S(1)} custom-call(s32[1]{0:T(128)S(6)} %copy.9.length_ref, s32[8,128]{1,0:T(8,128)S(1)} %wait_for.3.refs_0_, bf16[256,384]{1,0:T(8,128)(2,1)S(1)} %pad_maximum_fusion.3.refs_1_, bf16[256,384]{1,0:T(8,128)(2,1)S(1)} %pad_maximum_fusion.4.refs_2_, bf16[256,384]{1,0:T(8,128)(2,1)S(1)} %pad_maximum_fusion.5.refs_3_, ...), custom_call_target="tpu_custom_call" | custom-call | bytes 1835008 | tf_op jit(solution)/shard_map/attend/pallas_call | solution.py:274
  86.5 0.9 attend.11
  87.4 0.1 collective-permute-start.17
  87.4 0.0 copy-start.5
  87.5 0.0 copy-start.10
  87.5 0.0 copy-start.12
  87.5 0.0 copy-start.13
  87.5 0.5 collective-permute-start.18
  88.0 2.9 %collective-permute-done.14.refs_3_ = bf16[256,384]{1,0:T(8,128)(2,1)S(1)} collective-permute-done((bf16[256,384]{1,0:T(8,128)(2,1)S(1)}, bf16[256,384]{1,0:T(8,128)(2,1)S(1)}, u32[]{:S(2)}, u32[]{:S(2)}) %collective-permute-start.14) | collective-permute-done | bytes 196640 | tf_op jit(solution)/shard_map/ppermute | solution.py:366
  90.9 0.7 collect.3.refs_1_
  91.7 0.0 collective-permute-done.18
  91.8 1.0 %collective-permute-start.19 = (bf16[256,256]{1,0:T(8,128)(2,1)S(1)}, bf16[256,256]{1,0:T(8,128)(2,1)S(1)}, u32[]{:S(2)}, u32[]{:S(2)}) collective-permute-start(bf16[256,256]{1,0:T(8,128)(2,1)S(1)} %pad_maximum_fusion.6), channel_id=1, source_target_pairs={{0,2},{1,3},{2,0},{3,1},{4,6},{5,7},{6,4},{7,5},{8,10},{9,11},{10,... | collective-permute-start | bytes 393224 | tf_op jit(solution)/shard_map/ppermute | solution.py:366
  92.8 1.2 %collective-permute-start.20 = (bf16[256,256]{1,0:T(8,128)(2,1)S(1)}, bf16[256,256]{1,0:T(8,128)(2,1)S(1)}, u32[]{:S(2)}, u32[]{:S(2)}) collective-permute-start(bf16[256,256]{1,0:T(8,128)(2,1)S(1)} %pad_maximum_fusion.7), channel_id=1, source_target_pairs={{0,4},{1,5},{2,6},{3,7},{4,0},{5,1},{6,2},{7,3},{8,12},{9,13},{10,... | collective-permute-start | bytes 393224 | tf_op jit(solution)/shard_map/ppermute | solution.py:366
  94.1 1.4 %collective-permute-start.21 = (bf16[256,256]{1,0:T(8,128)(2,1)S(1)}, bf16[256,256]{1,0:T(8,128)(2,1)S(1)}, u32[]{:S(2)}, u32[]{:S(2)}) collective-permute-start(bf16[256,256]{1,0:T(8,128)(2,1)S(1)} %pad_maximum_fusion.8), channel_id=1, source_target_pairs={{0,6},{1,7},{2,4},{3,5},{4,2},{5,3},{6,0},{7,1},{8,14},{9,15},{10,... | collective-permute-start | bytes 393224 | tf_op jit(solution)/shard_map/ppermute | solution.py:366
  95.5 2.6 %collective-permute-done.19.refs_4_ = bf16[256,256]{1,0:T(8,128)(2,1)S(1)} collective-permute-done((bf16[256,256]{1,0:T(8,128)(2,1)S(1)}, bf16[256,256]{1,0:T(8,128)(2,1)S(1)}, u32[]{:S(2)}, u32[]{:S(2)}) %collective-permute-start.19) | collective-permute-done | bytes 131104 | tf_op jit(solution)/shard_map/ppermute | solution.py:366
  98.1 0.8 collective-permute-done.20.refs_5_
  98.9 1.1 %collective-permute-done.21.refs_6_ = bf16[256,256]{1,0:T(8,128)(2,1)S(1)} collective-permute-done((bf16[256,256]{1,0:T(8,128)(2,1)S(1)}, bf16[256,256]{1,0:T(8,128)(2,1)S(1)}, u32[]{:S(2)}, u32[]{:S(2)}) %collective-permute-start.21) | collective-permute-done | bytes 131104 | tf_op jit(solution)/shard_map/ppermute | solution.py:366
  100.0 3.5 %finish.1 = bf16[512,1024]{1,0:T(8,128)(2,1)} custom-call(s32[512,128]{1,0:T(8,128)S(1)} %copy-done.16, f32[1,1024]{1,0:T(1,128)S(1)} %bitcast.15, bf16[512,1024]{1,0:T(8,128)(2,1)S(1)} %copy-done.12, bf16[512,1024]{1,0:T(8,128)(2,1)S(1)} %copy-done.5, bf16[1024,1024]{1,0:T(8,128)(2,1)S(1)} %copy-done.10, bf16[512,384]{1,0:T(8,128)(2,1)S(1)} %collect.2.refs_0_, ...), custom_call_target="tpu_custom_call" | custom-call | flops 2147483648 | bytes 7340032 | tf_op jit(solution)/shard_map/finish/pallas_call | solution.py:351
  (50 shorter events, 0.4 us)
Async XLA Ops:
  0.0 0.7 copy-start.8
  0.7 8.7 %copy-start = (bf16[1024,2048]{1,0:T(8,128)(2,1)S(1)}, bf16[1024,2048]{1,0:T(8,128)(2,1)}, u32[]{:S(2)}) copy-start(bf16[1024,2048]{1,0:T(8,128)(2,1)} %w_ref.4) | copy-start | bytes 12582916
  0.7 8.7 %copy-start.3 = (bf16[512,1024]{1,0:T(8,128)(2,1)S(1)}, bf16[512,1024]{1,0:T(8,128)(2,1)}, u32[]{:S(2)}) copy-start(bf16[512,1024]{1,0:T(8,128)(2,1)} %x_ref.5) | copy-start | bytes 3145732
  0.7 8.7 %copy-start.14 = (s32[512]{0:T(512)S(1)}, s32[512]{0:T(512)}, u32[]{:S(2)}) copy-start(s32[512]{0:T(512)} %param.10) | copy-start | bytes 6148
  3.1 0.7 copy-start.6
  3.8 50.4 %collective-permute-start = (bf16[256,2048]{1,0:T(8,128)(2,1)}, bf16[256,2048]{1,0:T(8,128)(2,1)S(1)}, u32[]{:S(2)}, u32[]{:S(2)}) collective-permute-start(bf16[256,2048]{1,0:T(8,128)(2,1)} %bitcast.1.kv_hbm), channel_id=1, source_target_pairs={{0,8},{8,0},{16,24},{24,16},{1,9},{9,1},{17,25},{25,17},{2,10},{10... | collective-permute-start | bytes 3145736 | tf_op jit(solution)/shard_map/ppermute | solution.py:366
  6.8 32.4 %collective-permute-start.1 = (bf16[256,768]{1,0:T(8,128)(2,1)}, bf16[256,768]{1,0:T(8,128)(2,1)}, u32[]{:S(2)}, u32[]{:S(2)}) collective-permute-start(bf16[256,768]{1,0:T(8,128)(2,1)} %get-tuple-element.35.refs_2_), channel_id=1, source_target_pairs={{0,16},{8,24},{16,0},{24,8},{1,17},{9,25},{17,1},{25,9},{2,18},{10... | collective-permute-start | bytes 1179656 | tf_op jit(solution)/shard_map/ppermute | solution.py:366
  12.7 1.4 %copy-start.2 = (bf16[1024,1152]{1,0:T(8,128)(2,1)}, bf16[1024,1152]{1,0:T(8,128)(2,1)S(1)}, u32[]{:S(2)}) copy-start(bf16[1024,1152]{1,0:T(8,128)(2,1)S(1)} %project_queries.1) | copy-start | bytes 7077892
  14.1 33.5 %collective-permute-start.2 = (bf16[256,768]{1,0:T(8,128)(2,1)}, bf16[256,768]{1,0:T(8,128)(2,1)}, u32[]{:S(2)}, u32[]{:S(2)}) collective-permute-start(bf16[256,768]{1,0:T(8,128)(2,1)} %get-tuple-element.37.refs_5_), channel_id=1, source_target_pairs={{0,16},{8,24},{16,0},{24,8},{1,17},{9,25},{17,1},{25,9},{2,18},{10... | collective-permute-start | bytes 1179656 | tf_op jit(solution)/shard_map/ppermute | solution.py:366
  14.4 40.8 %all-to-all-start = ((bf16[8,128,1152]{2,1,0:T(8,128)(2,1)}), bf16[8,128,1152]{2,1,0:T(8,128)(2,1)S(1)}, u32[]{:S(2)}, u32[]{:S(2)}) async-start(bf16[8,128,1152]{2,1,0:T(8,128)(2,1)} %bitcast.13), calls=%async_computation | async-start | bytes 4718592 | tf_op jit(solution)/shard_map/all_to_all | solution.py:421
  18.2 35.9 %collective-permute-start.3 = (bf16[256,512]{1,0:T(8,128)(2,1)}, bf16[256,512]{1,0:T(8,128)(2,1)}, u32[]{:S(2)}, u32[]{:S(2)}) collective-permute-start(bf16[256,512]{1,0:T(8,128)(2,1)} %copy-done.6), channel_id=1, source_target_pairs={{0,16},{8,24},{16,0},{24,8},{1,17},{9,25},{17,1},{25,9},{2,18},{10... | collective-permute-start | bytes 786440 | tf_op jit(solution)/shard_map/ppermute | solution.py:366
  20.9 2.2 %copy-start.1 = (bf16[1024,2048]{1,0:T(8,128)(2,1)S(1)}, bf16[1024,2048]{1,0:T(8,128)(2,1)}, u32[]{:S(2)}) copy-start(bf16[1024,2048]{1,0:T(8,128)(2,1)} %w_ref.4) | copy-start | bytes 12582916
  23.1 1.2 %copy-start.4 = (bf16[512,1024]{1,0:T(8,128)(2,1)S(1)}, bf16[512,1024]{1,0:T(8,128)(2,1)}, u32[]{:S(2)}) copy-start(bf16[512,1024]{1,0:T(8,128)(2,1)} %x_ref.5) | copy-start | bytes 3145732
  24.3 3.0 %copy-start.9 = (s32[512,1]{0,1:T(1,128)S(1)}, s32[512,1]{0,1:T(1,128)}, u32[]{:S(2)}) copy-start(s32[512,1]{0,1:T(1,128)} %param.9) | copy-start | bytes 6148
  25.7 1.0 copy-start.11
  39.2 22.8 %collective-permute-start.4 = (bf16[256,768]{1,0:T(8,128)(2,1)}, bf16[256,768]{1,0:T(8,128)(2,1)}, u32[]{:S(2)}, u32[]{:S(2)}) collective-permute-start(bf16[256,768]{1,0:T(8,128)(2,1)} %collective-permute-done.1.refs_2_.refs_3_), channel_id=1, source_target_pairs={{0,8},{8,0},{16,24},{24,16},{1,9},{9,1},{17,25},{25,17},{2,10},{10... | collective-permute-start | bytes 1179656 | tf_op jit(solution)/shard_map/ppermute | solution.py:366
  47.6 25.9 %collective-permute-start.10 = (bf16[256,768]{1,0:T(8,128)(2,1)}, bf16[256,768]{1,0:T(8,128)(2,1)}, u32[]{:S(2)}, u32[]{:S(2)}) collective-permute-start(bf16[256,768]{1,0:T(8,128)(2,1)} %collective-permute-done.2.refs_3_.refs_1_.refs_6_), channel_id=1, source_target_pairs={{0,8},{8,0},{16,24},{24,16},{1,9},{9,1},{17,25},{25,17},{2,10},{10... | collective-permute-start | bytes 1179656 | tf_op jit(solution)/shard_map/ppermute | solution.py:366
  54.5 0.7 copy-start.15
  59.1 27.4 %collective-permute-start.16 = (bf16[256,512]{1,0:T(8,128)(2,1)}, bf16[256,512]{1,0:T(8,128)(2,1)S(1)}, u32[]{:S(2)}, u32[]{:S(2)}) collective-permute-start(bf16[256,512]{1,0:T(8,128)(2,1)} %collective-permute-done.3.refs_4_.refs_1_.refs_6_), channel_id=1, source_target_pairs={{0,8},{8,0},{16,24},{24,16},{1,9},{9,1},{17,25},{25,17},{2,10},{10... | collective-permute-start | bytes 786440 | tf_op jit(solution)/shard_map/ppermute | solution.py:366
  64.2 1.5 %collective-permute-start.5 = (bf16[256,384]{1,0:T(8,128)(2,1)S(1)}, bf16[256,384]{1,0:T(8,128)(2,1)S(1)}, u32[]{:S(2)}, u32[]{:S(2)}) collective-permute-start(bf16[256,384]{1,0:T(8,128)(2,1)S(1)} %get-tuple-element.44), channel_id=1, source_target_pairs={{0,1},{1,0},{2,3},{3,2},{4,5},{5,4},{6,7},{7,6},{8,9},{9,8},{10,11... | collective-permute-start | bytes 589832 | tf_op jit(solution)/shard_map/ppermute | solution.py:366
  64.2 3.5 %collective-permute-start.7 = (bf16[256,384]{1,0:T(8,128)(2,1)S(1)}, bf16[256,384]{1,0:T(8,128)(2,1)S(1)}, u32[]{:S(2)}, u32[]{:S(2)}) collective-permute-start(bf16[256,384]{1,0:T(8,128)(2,1)S(1)} %get-tuple-element.45), channel_id=1, source_target_pairs={{0,1},{1,0},{2,3},{3,2},{4,5},{5,4},{6,7},{7,6},{8,9},{9,8},{10,11... | collective-permute-start | bytes 589832 | tf_op jit(solution)/shard_map/ppermute | solution.py:366
  65.7 10.0 %collective-permute-start.6 = (bf16[256,384]{1,0:T(8,128)(2,1)S(1)}, bf16[256,384]{1,0:T(8,128)(2,1)S(1)}, u32[]{:S(2)}, u32[]{:S(2)}) collective-permute-start(bf16[256,384]{1,0:T(8,128)(2,1)S(1)} %pad_maximum_fusion.refs_1_), channel_id=1, source_target_pairs={{0,2},{1,3},{2,0},{3,1},{4,6},{5,7},{6,4},{7,5},{8,10},{9,11},{10,... | collective-permute-start | bytes 589832 | tf_op jit(solution)/shard_map/ppermute | solution.py:366
  67.8 10.9 %collective-permute-start.8 = (bf16[256,384]{1,0:T(8,128)(2,1)S(1)}, bf16[256,384]{1,0:T(8,128)(2,1)S(1)}, u32[]{:S(2)}, u32[]{:S(2)}) collective-permute-start(bf16[256,384]{1,0:T(8,128)(2,1)S(1)} %pad_maximum_fusion.1.refs_2_), channel_id=1, source_target_pairs={{0,4},{1,5},{2,6},{3,7},{4,0},{5,1},{6,2},{7,3},{8,12},{9,13},{10,... | collective-permute-start | bytes 589832 | tf_op jit(solution)/shard_map/ppermute | solution.py:366
  69.4 9.3 %collective-permute-start.9 = (bf16[256,384]{1,0:T(8,128)(2,1)S(1)}, bf16[256,384]{1,0:T(8,128)(2,1)S(1)}, u32[]{:S(2)}, u32[]{:S(2)}) collective-permute-start(bf16[256,384]{1,0:T(8,128)(2,1)S(1)} %pad_maximum_fusion.2.refs_3_), channel_id=1, source_target_pairs={{0,6},{1,7},{2,4},{3,5},{4,2},{5,3},{6,0},{7,1},{8,14},{9,15},{10,... | collective-permute-start | bytes 589832 | tf_op jit(solution)/shard_map/ppermute | solution.py:366
  75.6 3.9 %collective-permute-start.11 = (bf16[256,384]{1,0:T(8,128)(2,1)S(1)}, bf16[256,384]{1,0:T(8,128)(2,1)S(1)}, u32[]{:S(2)}, u32[]{:S(2)}) collective-permute-start(bf16[256,384]{1,0:T(8,128)(2,1)S(1)} %get-tuple-element.47), channel_id=1, source_target_pairs={{0,1},{1,0},{2,3},{3,2},{4,5},{5,4},{6,7},{7,6},{8,9},{9,8},{10,11... | collective-permute-start | bytes 589832 | tf_op jit(solution)/shard_map/ppermute | solution.py:366
  75.7 3.1 %copy-start.16 = (s32[512,128]{1,0:T(8,128)S(1)}, s32[512,128]{1,0:T(8,128)}, u32[]{:S(2)}) copy-start(s32[512,128]{1,0:T(8,128)} %copy-done.15) | copy-start | bytes 786436
  75.7 3.8 %collective-permute-start.12 = (bf16[256,384]{1,0:T(8,128)(2,1)S(1)}, bf16[256,384]{1,0:T(8,128)(2,1)S(1)}, u32[]{:S(2)}, u32[]{:S(2)}) collective-permute-start(bf16[256,384]{1,0:T(8,128)(2,1)S(1)} %get-tuple-element.48), channel_id=1, source_target_pairs={{0,1},{1,0},{2,3},{3,2},{4,5},{5,4},{6,7},{7,6},{8,9},{9,8},{10,11... | collective-permute-start | bytes 589832 | tf_op jit(solution)/shard_map/ppermute | solution.py:366
  79.5 3.9 %copy-start.7 = (bf16[256,512]{1,0:T(8,128)(2,1)S(1)}, bf16[256,512]{1,0:T(8,128)(2,1)}, u32[]{:S(2)}) copy-start(bf16[256,512]{1,0:T(8,128)(2,1)} %copy-done.6) | copy-start | bytes 786436
  79.6 8.4 %collective-permute-start.13 = (bf16[256,384]{1,0:T(8,128)(2,1)S(1)}, bf16[256,384]{1,0:T(8,128)(2,1)S(1)}, u32[]{:S(2)}, u32[]{:S(2)}) collective-permute-start(bf16[256,384]{1,0:T(8,128)(2,1)S(1)} %pad_maximum_fusion.3.refs_1_), channel_id=1, source_target_pairs={{0,2},{1,3},{2,0},{3,1},{4,6},{5,7},{6,4},{7,5},{8,10},{9,11},{10,... | collective-permute-start | bytes 589832 | tf_op jit(solution)/shard_map/ppermute | solution.py:366
  80.8 10.1 %collective-permute-start.14 = (bf16[256,384]{1,0:T(8,128)(2,1)S(1)}, bf16[256,384]{1,0:T(8,128)(2,1)S(1)}, u32[]{:S(2)}, u32[]{:S(2)}) collective-permute-start(bf16[256,384]{1,0:T(8,128)(2,1)S(1)} %pad_maximum_fusion.4.refs_2_), channel_id=1, source_target_pairs={{0,4},{1,5},{2,6},{3,7},{4,0},{5,1},{6,2},{7,3},{8,12},{9,13},{10,... | collective-permute-start | bytes 589832 | tf_op jit(solution)/shard_map/ppermute | solution.py:366
  81.9 9.1 %collective-permute-start.15 = (bf16[256,384]{1,0:T(8,128)(2,1)S(1)}, bf16[256,384]{1,0:T(8,128)(2,1)S(1)}, u32[]{:S(2)}, u32[]{:S(2)}) collective-permute-start(bf16[256,384]{1,0:T(8,128)(2,1)S(1)} %pad_maximum_fusion.5.refs_3_), channel_id=1, source_target_pairs={{0,6},{1,7},{2,4},{3,5},{4,2},{5,3},{6,0},{7,1},{8,14},{9,15},{10,... | collective-permute-start | bytes 589832 | tf_op jit(solution)/shard_map/ppermute | solution.py:366
  87.4 4.3 %collective-permute-start.17 = (bf16[256,256]{1,0:T(8,128)(2,1)S(1)}, bf16[256,256]{1,0:T(8,128)(2,1)S(1)}, u32[]{:S(2)}, u32[]{:S(2)}) collective-permute-start(bf16[256,256]{1,0:T(8,128)(2,1)S(1)} %get-tuple-element.54), channel_id=1, source_target_pairs={{0,1},{1,0},{2,3},{3,2},{4,5},{5,4},{6,7},{7,6},{8,9},{9,8},{10,11... | collective-permute-start | bytes 393224 | tf_op jit(solution)/shard_map/ppermute | solution.py:366
  87.4 12.6 %copy-start.5 = (bf16[512,1024]{1,0:T(8,128)(2,1)S(1)}, bf16[512,1024]{1,0:T(8,128)(2,1)}, u32[]{:S(2)}) copy-start(bf16[512,1024]{1,0:T(8,128)(2,1)} %x_ref.5) | copy-start | bytes 3145732
  87.5 12.6 %copy-start.10 = (bf16[1024,1024]{1,0:T(8,128)(2,1)S(1)}, bf16[1024,1024]{1,0:T(8,128)(2,1)}, u32[]{:S(2)}) copy-start(bf16[1024,1024]{1,0:T(8,128)(2,1)} %w_ref.5) | copy-start | bytes 6291460
  87.5 12.5 %copy-start.12 = (bf16[512,1024]{1,0:T(8,128)(2,1)S(1)}, bf16[512,1024]{1,0:T(8,128)(2,1)}, u32[]{:S(2)}) copy-start(bf16[512,1024]{1,0:T(8,128)(2,1)} %copy-done.11) | copy-start | bytes 3145732
  87.5 12.5 %copy-start.13 = (f32[1024]{0:T(1024)S(1)}, f32[1024]{0:T(1024)}, u32[]{:S(2)}) copy-start(f32[1024]{0:T(1024)} %param.15) | copy-start | bytes 12292
  87.5 4.2 %collective-permute-start.18 = (bf16[256,256]{1,0:T(8,128)(2,1)S(1)}, bf16[256,256]{1,0:T(8,128)(2,1)S(1)}, u32[]{:S(2)}, u32[]{:S(2)}) collective-permute-start(bf16[256,256]{1,0:T(8,128)(2,1)S(1)} %get-tuple-element.55), channel_id=1, source_target_pairs={{0,1},{1,0},{2,3},{3,2},{4,5},{5,4},{6,7},{7,6},{8,9},{9,8},{10,11... | collective-permute-start | bytes 393224 | tf_op jit(solution)/shard_map/ppermute | solution.py:366
  91.8 6.3 %collective-permute-start.19 = (bf16[256,256]{1,0:T(8,128)(2,1)S(1)}, bf16[256,256]{1,0:T(8,128)(2,1)S(1)}, u32[]{:S(2)}, u32[]{:S(2)}) collective-permute-start(bf16[256,256]{1,0:T(8,128)(2,1)S(1)} %pad_maximum_fusion.6), channel_id=1, source_target_pairs={{0,2},{1,3},{2,0},{3,1},{4,6},{5,7},{6,4},{7,5},{8,10},{9,11},{10,... | collective-permute-start | bytes 393224 | tf_op jit(solution)/shard_map/ppermute | solution.py:366
  92.8 6.1 %collective-permute-start.20 = (bf16[256,256]{1,0:T(8,128)(2,1)S(1)}, bf16[256,256]{1,0:T(8,128)(2,1)S(1)}, u32[]{:S(2)}, u32[]{:S(2)}) collective-permute-start(bf16[256,256]{1,0:T(8,128)(2,1)S(1)} %pad_maximum_fusion.7), channel_id=1, source_target_pairs={{0,4},{1,5},{2,6},{3,7},{4,0},{5,1},{6,2},{7,3},{8,12},{9,13},{10,... | collective-permute-start | bytes 393224 | tf_op jit(solution)/shard_map/ppermute | solution.py:366
  94.1 5.9 %collective-permute-start.21 = (bf16[256,256]{1,0:T(8,128)(2,1)S(1)}, bf16[256,256]{1,0:T(8,128)(2,1)S(1)}, u32[]{:S(2)}, u32[]{:S(2)}) collective-permute-start(bf16[256,256]{1,0:T(8,128)(2,1)S(1)} %pad_maximum_fusion.8), channel_id=1, source_target_pairs={{0,6},{1,7},{2,4},{3,5},{4,2},{5,3},{6,0},{7,1},{8,14},{9,15},{10,... | collective-permute-start | bytes 393224 | tf_op jit(solution)/shard_map/ppermute | solution.py:366

commit v16 on v13

--- a/solution.py
+++ b/solution.py
@@ -401,7 +401,7 @@
     gate, gated = project_gate(cand_x, w_in)
     row, *parts = prepare(owner_row, kv_cache[0], spans, size, columns, capacity)
     send = project_queries(row, visible_row, cand_x, w_in, slots)
-    near = None
+    near = []
     far = []
     for part in parts:
         if far:
@@ -412,16 +412,14 @@
             for key in sorted(held):
                 held[key | bit] = swap(held[key], "user", bit, count)
             bit //= 2
-        if near is None:
-            own, _ = lax.optimization_barrier((kv_cache[0], row))
-            near = swap(own, "user", 1, count)
+        near.append(swap(part, "user", 1, count))
         far.append(held)
     evens = sorted(far[0])
 
     got = lax.all_to_all(
         send.reshape(columns, capacity, -1), "cand", split_axis=0, concat_axis=0, tiled=True
     ).reshape(slots, -1)
-    arrived = [gated, near] + [held[key] for held in far for key in evens[1:]]
+    arrived = [gated] + near + [held[key] for held in far for key in evens[1:]]
     slot, started = slot_column(owner_row ^ me, columns, capacity, arrived)
     early = []
     after = [started]
@@ -430,7 +428,7 @@
         held = far[number]
         cuts = [(key | 1, [swap(held[key], "user", 1, count)], 0, heads) for key in evens[1:]]
         segments = [(key, [held[key]], 0, heads) for key in evens]
-        segments.append((1, [near], first, HEADS + first))
+        segments.append((1, [near[number]], 0, heads))
         base = attend(
             hist_len, after, got, segments, None, first, heads, size, None, F32, 0.0
         )[0]

time: 103 us -> 111 us (1.078)
  waiting for transfers between devices: 43.9 us -> 56.4 us
  starting transfers between devices: 24.4 us -> 20.6 us
    ppermute x15 -> x16, waiting for transfers between devices: 43.9 us -> 56.4 us  [swap(): return lax.ppermute(array, axis, [(i, i ^ bits) for i in range(count)])]
    ppermute x15 -> x16, starting transfers between devices: 20.6 us -> 16.8 us  [swap(): return lax.ppermute(array, axis, [(i, i ^ bits) for i in range(count)])]
    unnamed x30 -> x28, local copies, waits for them, and re-layouts: 7.2 us -> 7.23 us
  transfers between devices with their start and end apart: 16 -> 17, of which waited for: 9 -> 10; matrix products, arithmetic and copies ran while one was open for 0% -> 0% of each run, Pallas kernels for 20% -> 19%
where the time goes in v16:
time: 111 us
  waiting for transfers between devices  56.4 us (51%)
  Pallas kernels  24.9 us (22%)
  starting transfers between devices  20.6 us (19%)
  local copies, waits for them, and re-layouts  7.34 us (7%)
  between operations  1.33 us (1%)
    ppermute x16, waiting for transfers between devices, swap(): return lax.ppermute(array, axis, [(i, i ^ bits) for i in range(count)])  56.4 us
    ppermute x16, starting transfers between devices, swap(): return lax.ppermute(array, axis, [(i, i ^ bits) for i in range(count)])  16.8 us
    pallas_call x4, Pallas kernels, attend(): pl.pallas_call(functools.partial(attend_kernel, size, heads, first, start...  14.8 us
    unnamed x28, local copies, waits for them, and re-layouts  7.23 us
    all_to_all x1, starting transfers between devices, per_device(): lax.all_to_all(send.reshape(columns, capacity, -1), 'cand', split_axis=0,...  3.8 us
    pallas_call x1, Pallas kernels, project_queries(): pl.pallas_call(query_kernel, in_specs=whole(4), out_specs=whole()[0], out...  3.29 us
    pallas_call x1, Pallas kernels, finish(): pl.pallas_call(functools.partial(finish_kernel, len(early), capacity, slo...  3.1 us
  transfers between devices with their start and end apart: 17, of which 10 were waited for; matrix products, arithmetic and copies ran while one was open for 0% of the time, Pallas kernels for 19%

profile of v16, /device:TPU:0, one launch (start us, length us, event | category | flops | bytes accessed | tf_op | source)
XLA Modules:
  0.0 110.7 jit_solution(8218178811570032913)
XLA Ops:
  0.0 0.7 copy-done.4
  0.7 1.2 %copy-done.7 = bf16[1,256,2048]{2,1,0:T(8,128)(2,1)S(1)} copy-done((bf16[1,256,2048]{2,1,0:T(8,128)(2,1)S(1)}, bf16[1,256,2048]{2,1,0:T(8,128)(2,1)}, u32[]{:S(2)}) %copy-start.7) | copy-done | bytes 1048600
  1.9 1.3 %prepare.1 = (s32[8,512]{1,0:T(8,128)S(1)}, bf16[256,1024]{1,0:T(8,128)(2,1)}, bf16[256,1024]{1,0:T(8,128)(2,1)}) custom-call(s32[1,512]{1,0:T(1,128)S(1)} %bitcast.12, bf16[256,2048]{1,0:T(8,128)(2,1)S(1)} %bitcast.13), custom_call_target="tpu_custom_call" | custom-call | flops 6000000000 | tf_op jit(solution)/shard_map/prepare/pallas_call | solution.py:141
  3.2 4.1 %collective-permute-start.2 = (bf16[256,1024]{1,0:T(8,128)(2,1)}, bf16[256,1024]{1,0:T(8,128)(2,1)}, u32[]{:S(2)}, u32[]{:S(2)}) collective-permute-start(bf16[256,1024]{1,0:T(8,128)(2,1)} %get-tuple-element.23.refs_2_), channel_id=1, source_target_pairs={{0,16},{8,24},{16,0},{24,8},{1,17},{9,25},{17,1},{25,9},{2,18},{10... | collective-permute-start | bytes 1572872 | tf_op jit(solution)/shard_map/ppermute | solution.py:366
  7.3 0.0 copy-done
  7.3 0.0 copy-done.3
  7.3 0.0 copy-done.11
  7.3 3.3 %project_queries.1 = bf16[1024,1152]{1,0:T(8,128)(2,1)S(1)} custom-call(s32[8,512]{1,0:T(8,128)S(1)} %get-tuple-element.25.slot_ref, s32[1,512]{1,0:T(1,128)S(1)} %bitcast.15, bf16[512,1024]{1,0:T(8,128)(2,1)S(1)} %copy-done.3, bf16[1024,2048]{1,0:T(8,128)(2,1)S(1)} %copy-done), custom_call_target="tpu_custom_call" | custom-call | flops 2147483648 | bytes 5242880 | tf_op jit(solution)/shard_map/project_queries/pallas_call | solution.py:81
  10.6 0.0 copy-start.2
  10.6 1.4 %copy-done.2 = bf16[1024,1152]{1,0:T(8,128)(2,1)} copy-done((bf16[1024,1152]{1,0:T(8,128)(2,1)}, bf16[1024,1152]{1,0:T(8,128)(2,1)S(1)}, u32[]{:S(2)}) %copy-start.2) | copy-done | bytes 2359320
  12.1 1.5 %collective-permute-start.3 = (bf16[256,1024]{1,0:T(8,128)(2,1)}, bf16[256,1024]{1,0:T(8,128)(2,1)}, u32[]{:S(2)}, u32[]{:S(2)}) collective-permute-start(bf16[256,1024]{1,0:T(8,128)(2,1)} %get-tuple-element.26.refs_5_), channel_id=1, source_target_pairs={{0,16},{8,24},{16,0},{24,8},{1,17},{9,25},{17,1},{25,9},{2,18},{10... | collective-permute-start | bytes 1572872 | tf_op jit(solution)/shard_map/ppermute | solution.py:366
  13.5 1.6 %collective-permute-start.1 = (bf16[256,1024]{1,0:T(8,128)(2,1)}, bf16[256,1024]{1,0:T(8,128)(2,1)}, u32[]{:S(2)}, u32[]{:S(2)}) collective-permute-start(bf16[256,1024]{1,0:T(8,128)(2,1)} %get-tuple-element.26.refs_5_), channel_id=1, source_target_pairs={{0,8},{8,0},{16,24},{24,16},{1,9},{9,1},{17,25},{25,17},{2,10},{10... | collective-permute-start | bytes 1572872 | tf_op jit(solution)/shard_map/ppermute | solution.py:366
  15.1 0.4 collective-permute-start
  15.6 3.8 %all-to-all-start = ((bf16[8,128,1152]{2,1,0:T(8,128)(2,1)}), bf16[8,128,1152]{2,1,0:T(8,128)(2,1)S(1)}, u32[]{:S(2)}, u32[]{:S(2)}) async-start(bf16[8,128,1152]{2,1,0:T(8,128)(2,1)} %bitcast.11), calls=%async_computation | async-start | bytes 4718592 | tf_op jit(solution)/shard_map/all_to_all | solution.py:419
  20.0 0.0 copy-start.1
  20.0 2.2 %copy-done.1 = bf16[1024,2048]{1,0:T(8,128)(2,1)S(1)} copy-done((bf16[1024,2048]{1,0:T(8,128)(2,1)S(1)}, bf16[1024,2048]{1,0:T(8,128)(2,1)}, u32[]{:S(2)}) %copy-start.1) | copy-done | bytes 4194328
  22.2 1.4 %project_gate.1 = (bf16[512,1024]{1,0:T(8,128)(2,1)S(1)}, s32[8,128]{1,0:T(8,128)S(1)}) custom-call(bf16[512,1024]{1,0:T(8,128)(2,1)S(1)} %copy-done.3, bf16[1024,2048]{1,0:T(8,128)(2,1)S(1)} %copy-done.1), custom_call_target="tpu_custom_call" | custom-call | flops 1073741824 | bytes 4194304 | tf_op jit(solution)/shard_map/project_gate/pallas_call | solution.py:108
  23.6 0.0 copy-start.8
  23.6 1.0 copy-done.8
  24.6 0.0 copy-done.5
  24.6 18.4 %collective-permute-done.2.refs_3_ = bf16[256,1024]{1,0:T(8,128)(2,1)} collective-permute-done((bf16[256,1024]{1,0:T(8,128)(2,1)}, bf16[256,1024]{1,0:T(8,128)(2,1)}, u32[]{:S(2)}, u32[]{:S(2)}) %collective-permute-start.2) | collective-permute-done | bytes 524320 | tf_op jit(solution)/shard_map/ppermute | solution.py:366
  43.0 0.0 collective-permute-start.4
  43.0 10.4 %collective-permute-done.3.refs_4_.refs_1_.refs_6_ = bf16[256,1024]{1,0:T(8,128)(2,1)} collective-permute-done((bf16[256,1024]{1,0:T(8,128)(2,1)}, bf16[256,1024]{1,0:T(8,128)(2,1)}, u32[]{:S(2)}, u32[]{:S(2)}) %collective-permute-start.3) | collective-permute-done | bytes 524320 | tf_op jit(solution)/shard_map/ppermute | solution.py:366
  53.4 0.7 collective-permute-start.10
  54.0 0.0 collective-permute-done.1.refs_2_.refs_7_
  54.0 7.2 %collective-permute-done.refs_1_.refs_4_ = bf16[256,1024]{1,0:T(8,128)(2,1)} collective-permute-done((bf16[256,1024]{1,0:T(8,128)(2,1)}, bf16[256,1024]{1,0:T(8,128)(2,1)}, u32[]{:S(2)}, u32[]{:S(2)}) %collective-permute-start) | collective-permute-done | bytes 524320 | tf_op jit(solution)/shard_map/ppermute | solution.py:366
  61.2 0.3 slot_column.1
  61.6 0.0 copy-start.12
  61.6 0.7 copy-done.12
  62.3 0.0 all-to-all-done
  62.3 4.9 %attend.4.refs_2_ = f32[1024,512]{1,0:T(8,128)S(1)} custom-call(s32[1]{0:T(128)S(6)} %copy.9.length_ref, s32[8,128]{1,0:T(8,128)S(1)} %get-tuple-element.29.refs_0_, bf16[1024,1152]{1,0:T(8,128)(2,1)S(1)} %bitcast.7, bf16[256,1024]{1,0:T(8,128)(2,1)} %get-tuple-element.23.refs_2_, bf16[256,1024]{1,0:T(8,128)(2,1)} %collective-permute-done.2.refs_3_, ...), custom_call_target="tpu_custom_call" | custom-call | bytes 3670016 | tf_op jit(solution)/shard_map/attend/pallas_call | solution.py:274
  67.2 5.3 %collective-permute-done.4.refs_1_ = bf16[256,1024]{1,0:T(8,128)(2,1)} collective-permute-done((bf16[256,1024]{1,0:T(8,128)(2,1)}, bf16[256,1024]{1,0:T(8,128)(2,1)}, u32[]{:S(2)}, u32[]{:S(2)}) %collective-permute-start.4) | collective-permute-done | bytes 524320 | tf_op jit(solution)/shard_map/ppermute | solution.py:366
  72.5 2.5 %attend.5 = (bf16[512,512]{1,0:T(8,128)(2,1)S(1)}, bf16[256,512]{1,0:T(8,128)(2,1)S(1)}, bf16[256,512]{1,0:T(8,128)(2,1)S(1)}) custom-call(s32[1]{0:T(128)S(6)} %copy.9.length_ref, bf16[1024,1152]{1,0:T(8,128)(2,1)S(1)} %bitcast.8, bf16[256,1024]{1,0:T(8,128)(2,1)} %collective-permute-done.4.refs_1_, f32[1024,512]{1,0:T(8,128)S(1)} %attend.4.refs_2_), custom_call_target="tpu_custom_call" | custom-call | bytes 2621440 | tf_op jit(solution)/shard_map/attend/pallas_call | solution.py:274
  75.0 0.1 collective-permute-start.7
  75.0 0.5 collective-permute-start.5
  75.6 1.0 collective-permute-done.7
  76.6 2.6 %collective-permute-start.9 = (bf16[256,512]{1,0:T(8,128)(2,1)S(1)}, bf16[256,512]{1,0:T(8,128)(2,1)S(1)}, u32[]{:S(2)}, u32[]{:S(2)}) collective-permute-start(bf16[256,512]{1,0:T(8,128)(2,1)S(1)} %pad_maximum_fusion.2.refs_3_), channel_id=1, source_target_pairs={{0,6},{1,7},{2,4},{3,5},{4,2},{5,3},{6,0},{7,1},{8,14},{9,15},{10,... | collective-permute-start | bytes 786440 | tf_op jit(solution)/shard_map/ppermute | solution.py:366
  79.2 0.6 collective-permute-start.8
  79.8 0.0 collective-permute-done.5.refs_1_
  79.8 0.6 collective-permute-start.6
  80.4 4.9 %attend.6.refs_2_ = f32[1024,512]{1,0:T(8,128)S(1)} custom-call(s32[1]{0:T(128)S(6)} %copy.9.length_ref, s32[8,128]{1,0:T(8,128)S(1)} %wait_for.1.refs_0_, bf16[256,512]{1,0:T(8,128)(2,1)S(1)} %pad_maximum_fusion.refs_1_, bf16[256,512]{1,0:T(8,128)(2,1)S(1)} %pad_maximum_fusion.1.refs_2_, bf16[256,512]{1,0:T(8,128)(2,1)S(1)} %pad_maximum_fusion.2.refs_3_, ...), custom_call_target="tpu_custom_call" | custom-call | bytes 3670016 | tf_op jit(solution)/shard_map/attend/pallas_call | solution.py:274
  85.3 0.0 copy-start.13
  85.3 0.0 collective-permute-done.10.refs_1_
  85.3 2.5 %attend.7 = (bf16[512,512]{1,0:T(8,128)(2,1)S(1)}, bf16[256,512]{1,0:T(8,128)(2,1)S(1)}, bf16[256,512]{1,0:T(8,128)(2,1)S(1)}) custom-call(s32[1]{0:T(128)S(6)} %copy.9.length_ref, bf16[1024,1152]{1,0:T(8,128)(2,1)S(1)} %bitcast.10, bf16[256,1024]{1,0:T(8,128)(2,1)} %collective-permute-done.10.refs_1_, f32[1024,512]{1,0:T(8,128)S(1)} %attend.6.refs_2_), custom_call_target="tpu_custom_call" | custom-call | flops 10737418240 | bytes 2621440 | tf_op jit(solution)/shard_map/attend/pallas_call | solution.py:274
  88.1 0.1 collective-permute-start.11
  88.1 0.5 collective-permute-start.12
  88.6 0.0 collective-permute-done.9.refs_4_
  88.6 2.9 %collective-permute-done.8.refs_3_ = bf16[256,512]{1,0:T(8,128)(2,1)S(1)} collective-permute-done((bf16[256,512]{1,0:T(8,128)(2,1)S(1)}, bf16[256,512]{1,0:T(8,128)(2,1)S(1)}, u32[]{:S(2)}, u32[]{:S(2)}) %collective-permute-start.8) | collective-permute-done | bytes 262176 | tf_op jit(solution)/shard_map/ppermute | solution.py:366
  91.6 0.1 collective-permute-done.6.refs_2_
  91.7 0.7 collect.1.refs_0_
  92.4 0.0 copy-start.6
  92.4 0.0 copy-start.9
  92.4 0.0 copy-start.10
  92.5 0.0 collective-permute-done.11.refs_2_
  92.5 0.0 collective-permute-done.12
  92.6 1.8 %collective-permute-start.15 = (bf16[256,512]{1,0:T(8,128)(2,1)S(1)}, bf16[256,512]{1,0:T(8,128)(2,1)S(1)}, u32[]{:S(2)}, u32[]{:S(2)}) collective-permute-start(bf16[256,512]{1,0:T(8,128)(2,1)S(1)} %pad_maximum_fusion.5), channel_id=1, source_target_pairs={{0,6},{1,7},{2,4},{3,5},{4,2},{5,3},{6,0},{7,1},{8,14},{9,15},{10,... | collective-permute-start | bytes 786440 | tf_op jit(solution)/shard_map/ppermute | solution.py:366
  94.3 1.3 %collective-permute-start.14 = (bf16[256,512]{1,0:T(8,128)(2,1)S(1)}, bf16[256,512]{1,0:T(8,128)(2,1)S(1)}, u32[]{:S(2)}, u32[]{:S(2)}) collective-permute-start(bf16[256,512]{1,0:T(8,128)(2,1)S(1)} %pad_maximum_fusion.4), channel_id=1, source_target_pairs={{0,4},{1,5},{2,6},{3,7},{4,0},{5,1},{6,2},{7,3},{8,12},{9,13},{10,... | collective-permute-start | bytes 786440 | tf_op jit(solution)/shard_map/ppermute | solution.py:366
  95.7 0.6 collective-permute-start.13
  96.3 6.5 %collective-permute-done.15.refs_5_ = bf16[256,512]{1,0:T(8,128)(2,1)S(1)} collective-permute-done((bf16[256,512]{1,0:T(8,128)(2,1)S(1)}, bf16[256,512]{1,0:T(8,128)(2,1)S(1)}, u32[]{:S(2)}, u32[]{:S(2)}) %collective-permute-start.15) | collective-permute-done | bytes 262176 | tf_op jit(solution)/shard_map/ppermute | solution.py:366
  102.8 4.5 %collective-permute-done.14.refs_4_ = bf16[256,512]{1,0:T(8,128)(2,1)S(1)} collective-permute-done((bf16[256,512]{1,0:T(8,128)(2,1)S(1)}, bf16[256,512]{1,0:T(8,128)(2,1)S(1)}, u32[]{:S(2)}, u32[]{:S(2)}) %collective-permute-start.14) | collective-permute-done | bytes 262176 | tf_op jit(solution)/shard_map/ppermute | solution.py:366
  107.2 0.1 collective-permute-done.13.refs_3_
  107.4 0.0 copy-done.6
  107.4 0.0 copy-done.10
  107.4 3.1 %finish.1 = bf16[512,1024]{1,0:T(8,128)(2,1)} custom-call(s32[512,128]{1,0:T(8,128)S(1)} %copy-done.13, f32[1,1024]{1,0:T(1,128)S(1)} %bitcast.14, bf16[512,1024]{1,0:T(8,128)(2,1)S(1)} %copy-done.9, bf16[512,1024]{1,0:T(8,128)(2,1)S(1)} %copy-done.3, bf16[1024,1024]{1,0:T(8,128)(2,1)S(1)} %copy-done.6, bf16[512,512]{1,0:T(8,128)(2,1)S(1)} %collect.1.refs_0_, ...), custom_call_target="tpu_custom_call" | custom-call | flops 2147483648 | bytes 7340032 | tf_op jit(solution)/shard_map/finish/pallas_call | solution.py:351
  (22 shorter events, 0.2 us)
Async XLA Ops:
  0.0 0.7 copy-start.4
  0.7 1.2 %copy-start.7 = (bf16[1,256,2048]{2,1,0:T(8,128)(2,1)S(1)}, bf16[1,256,2048]{2,1,0:T(8,128)(2,1)}, u32[]{:S(2)}) copy-start(bf16[1,256,2048]{2,1,0:T(8,128)(2,1)} %param.12) | copy-start | bytes 3145732
  1.9 5.4 %copy-start = (bf16[1024,2048]{1,0:T(8,128)(2,1)S(1)}, bf16[1024,2048]{1,0:T(8,128)(2,1)}, u32[]{:S(2)}) copy-start(bf16[1024,2048]{1,0:T(8,128)(2,1)} %w_ref.4) | copy-start | bytes 12582916
  1.9 5.4 %copy-start.3 = (bf16[512,1024]{1,0:T(8,128)(2,1)S(1)}, bf16[512,1024]{1,0:T(8,128)(2,1)}, u32[]{:S(2)}) copy-start(bf16[512,1024]{1,0:T(8,128)(2,1)} %x_ref.5) | copy-start | bytes 3145732
  1.9 5.4 %copy-start.11 = (s32[512]{0:T(512)S(1)}, s32[512]{0:T(512)}, u32[]{:S(2)}) copy-start(s32[512]{0:T(512)} %param.10) | copy-start | bytes 6148
  3.2 39.7 %collective-permute-start.2 = (bf16[256,1024]{1,0:T(8,128)(2,1)}, bf16[256,1024]{1,0:T(8,128)(2,1)}, u32[]{:S(2)}, u32[]{:S(2)}) collective-permute-start(bf16[256,1024]{1,0:T(8,128)(2,1)} %get-tuple-element.23.refs_2_), channel_id=1, source_target_pairs={{0,16},{8,24},{16,0},{24,8},{1,17},{9,25},{17,1},{25,9},{2,18},{10... | collective-permute-start | bytes 1572872 | tf_op jit(solution)/shard_map/ppermute | solution.py:366
  10.6 1.4 %copy-start.2 = (bf16[1024,1152]{1,0:T(8,128)(2,1)}, bf16[1024,1152]{1,0:T(8,128)(2,1)S(1)}, u32[]{:S(2)}) copy-start(bf16[1024,1152]{1,0:T(8,128)(2,1)S(1)} %project_queries.1) | copy-start | bytes 7077892
  12.1 41.3 %collective-permute-start.3 = (bf16[256,1024]{1,0:T(8,128)(2,1)}, bf16[256,1024]{1,0:T(8,128)(2,1)}, u32[]{:S(2)}, u32[]{:S(2)}) collective-permute-start(bf16[256,1024]{1,0:T(8,128)(2,1)} %get-tuple-element.26.refs_5_), channel_id=1, source_target_pairs={{0,16},{8,24},{16,0},{24,8},{1,17},{9,25},{17,1},{25,9},{2,18},{10... | collective-permute-start | bytes 1572872 | tf_op jit(solution)/shard_map/ppermute | solution.py:366
  13.5 40.5 %collective-permute-start.1 = (bf16[256,1024]{1,0:T(8,128)(2,1)}, bf16[256,1024]{1,0:T(8,128)(2,1)}, u32[]{:S(2)}, u32[]{:S(2)}) collective-permute-start(bf16[256,1024]{1,0:T(8,128)(2,1)} %get-tuple-element.26.refs_5_), channel_id=1, source_target_pairs={{0,8},{8,0},{16,24},{24,16},{1,9},{9,1},{17,25},{25,17},{2,10},{10... | collective-permute-start | bytes 1572872 | tf_op jit(solution)/shard_map/ppermute | solution.py:366
  15.1 46.1 %collective-permute-start = (bf16[256,1024]{1,0:T(8,128)(2,1)}, bf16[256,1024]{1,0:T(8,128)(2,1)}, u32[]{:S(2)}, u32[]{:S(2)}) collective-permute-start(bf16[256,1024]{1,0:T(8,128)(2,1)} %get-tuple-element.23.refs_2_), channel_id=1, source_target_pairs={{0,8},{8,0},{16,24},{24,16},{1,9},{9,1},{17,25},{25,17},{2,10},{10... | collective-permute-start | bytes 1572872 | tf_op jit(solution)/shard_map/ppermute | solution.py:366
  15.6 46.7 %all-to-all-start = ((bf16[8,128,1152]{2,1,0:T(8,128)(2,1)}), bf16[8,128,1152]{2,1,0:T(8,128)(2,1)S(1)}, u32[]{:S(2)}, u32[]{:S(2)}) async-start(bf16[8,128,1152]{2,1,0:T(8,128)(2,1)} %bitcast.11), calls=%async_computation | async-start | bytes 4718592 | tf_op jit(solution)/shard_map/all_to_all | solution.py:419
  20.0 2.2 %copy-start.1 = (bf16[1024,2048]{1,0:T(8,128)(2,1)S(1)}, bf16[1024,2048]{1,0:T(8,128)(2,1)}, u32[]{:S(2)}) copy-start(bf16[1024,2048]{1,0:T(8,128)(2,1)} %w_ref.4) | copy-start | bytes 12582916
  22.2 2.4 %copy-start.5 = (s32[512,1]{0,1:T(1,128)S(1)}, s32[512,1]{0,1:T(1,128)}, u32[]{:S(2)}) copy-start(s32[512,1]{0,1:T(1,128)} %param.9) | copy-start | bytes 6148
  23.6 1.0 copy-start.8
  43.0 29.5 %collective-permute-start.4 = (bf16[256,1024]{1,0:T(8,128)(2,1)}, bf16[256,1024]{1,0:T(8,128)(2,1)}, u32[]{:S(2)}, u32[]{:S(2)}) collective-permute-start(bf16[256,1024]{1,0:T(8,128)(2,1)} %collective-permute-done.2.refs_3_), channel_id=1, source_target_pairs={{0,8},{8,0},{16,24},{24,16},{1,9},{9,1},{17,25},{25,17},{2,10},{10... | collective-permute-start | bytes 1572872 | tf_op jit(solution)/shard_map/ppermute | solution.py:366
  53.4 31.9 %collective-permute-start.10 = (bf16[256,1024]{1,0:T(8,128)(2,1)}, bf16[256,1024]{1,0:T(8,128)(2,1)}, u32[]{:S(2)}, u32[]{:S(2)}) collective-permute-start(bf16[256,1024]{1,0:T(8,128)(2,1)} %collective-permute-done.3.refs_4_.refs_1_.refs_6_), channel_id=1, source_target_pairs={{0,8},{8,0},{16,24},{24,16},{1,9},{9,1},{17,25},{25,17},{2,10},{10... | collective-permute-start | bytes 1572872 | tf_op jit(solution)/shard_map/ppermute | solution.py:366
  61.6 0.7 copy-start.12
  75.0 1.6 %collective-permute-start.7 = (bf16[256,512]{1,0:T(8,128)(2,1)S(1)}, bf16[256,512]{1,0:T(8,128)(2,1)S(1)}, u32[]{:S(2)}, u32[]{:S(2)}) collective-permute-start(bf16[256,512]{1,0:T(8,128)(2,1)S(1)} %get-tuple-element.32), channel_id=1, source_target_pairs={{0,1},{1,0},{2,3},{3,2},{4,5},{5,4},{6,7},{7,6},{8,9},{9,8},{10,11... | collective-permute-start | bytes 786440 | tf_op jit(solution)/shard_map/ppermute | solution.py:366
  75.0 4.7 %collective-permute-start.5 = (bf16[256,512]{1,0:T(8,128)(2,1)S(1)}, bf16[256,512]{1,0:T(8,128)(2,1)S(1)}, u32[]{:S(2)}, u32[]{:S(2)}) collective-permute-start(bf16[256,512]{1,0:T(8,128)(2,1)S(1)} %get-tuple-element.31), channel_id=1, source_target_pairs={{0,1},{1,0},{2,3},{3,2},{4,5},{5,4},{6,7},{7,6},{8,9},{9,8},{10,11... | collective-permute-start | bytes 786440 | tf_op jit(solution)/shard_map/ppermute | solution.py:366
  76.6 12.0 %collective-permute-start.9 = (bf16[256,512]{1,0:T(8,128)(2,1)S(1)}, bf16[256,512]{1,0:T(8,128)(2,1)S(1)}, u32[]{:S(2)}, u32[]{:S(2)}) collective-permute-start(bf16[256,512]{1,0:T(8,128)(2,1)S(1)} %pad_maximum_fusion.2.refs_3_), channel_id=1, source_target_pairs={{0,6},{1,7},{2,4},{3,5},{4,2},{5,3},{6,0},{7,1},{8,14},{9,15},{10,... | collective-permute-start | bytes 786440 | tf_op jit(solution)/shard_map/ppermute | solution.py:366
  79.2 12.3 %collective-permute-start.8 = (bf16[256,512]{1,0:T(8,128)(2,1)S(1)}, bf16[256,512]{1,0:T(8,128)(2,1)S(1)}, u32[]{:S(2)}, u32[]{:S(2)}) collective-permute-start(bf16[256,512]{1,0:T(8,128)(2,1)S(1)} %pad_maximum_fusion.1.refs_2_), channel_id=1, source_target_pairs={{0,4},{1,5},{2,6},{3,7},{4,0},{5,1},{6,2},{7,3},{8,12},{9,13},{10,... | collective-permute-start | bytes 786440 | tf_op jit(solution)/shard_map/ppermute | solution.py:366
  79.8 11.9 %collective-permute-start.6 = (bf16[256,512]{1,0:T(8,128)(2,1)S(1)}, bf16[256,512]{1,0:T(8,128)(2,1)S(1)}, u32[]{:S(2)}, u32[]{:S(2)}) collective-permute-start(bf16[256,512]{1,0:T(8,128)(2,1)S(1)} %pad_maximum_fusion.refs_1_), channel_id=1, source_target_pairs={{0,2},{1,3},{2,0},{3,1},{4,6},{5,7},{6,4},{7,5},{8,10},{9,11},{10,... | collective-permute-start | bytes 786440 | tf_op jit(solution)/shard_map/ppermute | solution.py:366
  85.3 6.4 %copy-start.13 = (s32[512,128]{1,0:T(8,128)S(1)}, s32[512,128]{1,0:T(8,128)}, u32[]{:S(2)}) copy-start(s32[512,128]{1,0:T(8,128)} %copy-done.12) | copy-start | bytes 786436
  88.1 4.4 %collective-permute-start.11 = (bf16[256,512]{1,0:T(8,128)(2,1)S(1)}, bf16[256,512]{1,0:T(8,128)(2,1)S(1)}, u32[]{:S(2)}, u32[]{:S(2)}) collective-permute-start(bf16[256,512]{1,0:T(8,128)(2,1)S(1)} %get-tuple-element.34), channel_id=1, source_target_pairs={{0,1},{1,0},{2,3},{3,2},{4,5},{5,4},{6,7},{7,6},{8,9},{9,8},{10,11... | collective-permute-start | bytes 786440 | tf_op jit(solution)/shard_map/ppermute | solution.py:366
  88.1 4.3 %collective-permute-start.12 = (bf16[256,512]{1,0:T(8,128)(2,1)S(1)}, bf16[256,512]{1,0:T(8,128)(2,1)S(1)}, u32[]{:S(2)}, u32[]{:S(2)}) collective-permute-start(bf16[256,512]{1,0:T(8,128)(2,1)S(1)} %get-tuple-element.35), channel_id=1, source_target_pairs={{0,1},{1,0},{2,3},{3,2},{4,5},{5,4},{6,7},{7,6},{8,9},{9,8},{10,11... | collective-permute-start | bytes 786440 | tf_op jit(solution)/shard_map/ppermute | solution.py:366
  92.4 15.0 %copy-start.6 = (bf16[1024,1024]{1,0:T(8,128)(2,1)S(1)}, bf16[1024,1024]{1,0:T(8,128)(2,1)}, u32[]{:S(2)}) copy-start(bf16[1024,1024]{1,0:T(8,128)(2,1)} %w_ref.5) | copy-start | bytes 6291460
  92.4 15.0 %copy-start.9 = (bf16[512,1024]{1,0:T(8,128)(2,1)S(1)}, bf16[512,1024]{1,0:T(8,128)(2,1)}, u32[]{:S(2)}) copy-start(bf16[512,1024]{1,0:T(8,128)(2,1)} %copy-done.8) | copy-start | bytes 3145732
  92.4 14.9 %copy-start.10 = (f32[1024]{0:T(1024)S(1)}, f32[1024]{0:T(1024)}, u32[]{:S(2)}) copy-start(f32[1024]{0:T(1024)} %param.15) | copy-start | bytes 12292
  92.6 10.2 %collective-permute-start.15 = (bf16[256,512]{1,0:T(8,128)(2,1)S(1)}, bf16[256,512]{1,0:T(8,128)(2,1)S(1)}, u32[]{:S(2)}, u32[]{:S(2)}) collective-permute-start(bf16[256,512]{1,0:T(8,128)(2,1)S(1)} %pad_maximum_fusion.5), channel_id=1, source_target_pairs={{0,6},{1,7},{2,4},{3,5},{4,2},{5,3},{6,0},{7,1},{8,14},{9,15},{10,... | collective-permute-start | bytes 786440 | tf_op jit(solution)/shard_map/ppermute | solution.py:366
  94.3 12.9 %collective-permute-start.14 = (bf16[256,512]{1,0:T(8,128)(2,1)S(1)}, bf16[256,512]{1,0:T(8,128)(2,1)S(1)}, u32[]{:S(2)}, u32[]{:S(2)}) collective-permute-start(bf16[256,512]{1,0:T(8,128)(2,1)S(1)} %pad_maximum_fusion.4), channel_id=1, source_target_pairs={{0,4},{1,5},{2,6},{3,7},{4,0},{5,1},{6,2},{7,3},{8,12},{9,13},{10,... | collective-permute-start | bytes 786440 | tf_op jit(solution)/shard_map/ppermute | solution.py:366
  95.7 11.7 %collective-permute-start.13 = (bf16[256,512]{1,0:T(8,128)(2,1)S(1)}, bf16[256,512]{1,0:T(8,128)(2,1)S(1)}, u32[]{:S(2)}, u32[]{:S(2)}) collective-permute-start(bf16[256,512]{1,0:T(8,128)(2,1)S(1)} %pad_maximum_fusion.3), channel_id=1, source_target_pairs={{0,2},{1,3},{2,0},{3,1},{4,6},{5,7},{6,4},{7,5},{8,10},{9,11},{10,... | collective-permute-start | bytes 786440 | tf_op jit(solution)/shard_map/ppermute | solution.py:366

commit v17 on v13

--- a/solution.py
+++ b/solution.py
@@ -18,7 +18,6 @@
 TOKEN = jax.ShapeDtypeStruct((8, BLK), jnp.int32)
 WAIT_COST = 20.0
 LATE_SHARE = 20.0
-COLLECT_COST = 20.0
 SLOTS_COST = 6.0
 KERNEL_MIB = 24
 
@@ -305,22 +304,22 @@
 
 
 def collect_kernel(capacity, slots, slot_ref, *refs):
-    rows = in_slots(refs[:-1], capacity)
+    rows = in_slots(refs[:-2], capacity)
     place = placement(slot_ref[...], slots)
     refs[-1][...] = jnp.dot(place, rows, preferred_element_type=F32).astype(BF16)
 
 
-def collect(slot, parts, capacity, slots):
+def collect(slot, parts, after, capacity, slots):
     rows, width = slot.shape[0], parts[0].shape[1]
     return pl.pallas_call(
         functools.partial(collect_kernel, capacity, slots),
-        in_specs=whole(1 + len(parts)),
+        in_specs=whole(1 + len(parts)) + unread([after]),
         out_specs=whole()[0],
         out_shape=jax.ShapeDtypeStruct((rows, width), BF16),
         compiler_params=params(KERNEL_MIB),
-        cost_estimate=cost(COLLECT_COST * 1e9, 2 * (rows + slots) * width),
+        cost_estimate=cost(2 * rows * slots * width, 2 * (rows + slots) * width),
         name="collect",
-    )(slot, *parts)
+    )(slot, *parts, after)
 
 
 def finish_kernel(groups, capacity, slots, slot_ref, gain_ref, gate_ref, x_ref, w_ref, *refs):
@@ -452,8 +451,8 @@
         if number + 1 < len(spans):
             token = wait_for([attn[0]] + [far[number + 1][key] for key in evens[1:]])
             after = [token] + pairs
-            early.append(collect(slot, here + away, capacity, slots))
-            behind = early[-1]
+            behind = wait_for(away)
+            early.append(collect(slot, here + away, behind, capacity, slots))
     return finish(slot, early, gate, cand_x, ln_gain, w_out, here + away, capacity, slots)
 
 

time: 103 us -> 103 us (level)
  no operation moved by 1% of the time
where the time goes in v17:
time: 103 us; the launch traced here: 102 us
  waiting for transfers between devices  43.3 us (42%)
  Pallas kernels  25.9 us (25%)
  starting transfers between devices  24.4 us (24%)
  local copies, waits for them, and re-layouts  7.32 us (7%)
  between operations  1.1 us (1%)
    ppermute x15, waiting for transfers between devices, swap(): return lax.ppermute(array, axis, [(i, i ^ bits) for i in range(count)])  43.3 us
    ppermute x15, starting transfers between devices, swap(): return lax.ppermute(array, axis, [(i, i ^ bits) for i in range(count)])  20.6 us
    pallas_call x4, Pallas kernels, attend(): pl.pallas_call(functools.partial(attend_kernel, size, heads, first, start...  14.7 us
    unnamed x30, local copies, waits for them, and re-layouts  7.21 us
    all_to_all x1, starting transfers between devices, per_device(): lax.all_to_all(send.reshape(columns, capacity, -1), 'cand', split_axis=0,...  3.8 us
    pallas_call x1, Pallas kernels, project_queries(): pl.pallas_call(query_kernel, in_specs=whole(4), out_specs=whole()[0], out...  3.29 us
    pallas_call x1, Pallas kernels, finish(): pl.pallas_call(functools.partial(finish_kernel, len(early), capacity, slo...  3.1 us
    pallas_call x1, Pallas kernels, prepare(): pl.pallas_call(functools.partial(prepare_kernel, columns, capacity, spans...  2.36 us
  transfers between devices with their start and end apart: 16, of which 9 were waited for; matrix products, arithmetic and copies ran while one was open for 0% of the time, Pallas kernels for 20%

profile of v17, /device:TPU:0, one launch (start us, length us, event | category | flops | bytes accessed | tf_op | source)
XLA Modules:
  0.0 102.1 jit_solution(9903710809868425636)
XLA Ops:
  0.0 0.7 copy-done.8
  0.7 2.4 %prepare.1 = (s32[8,512]{1,0:T(8,128)S(1)}, bf16[256,1024]{1,0:T(8,128)(2,1)}, bf16[256,1024]{1,0:T(8,128)(2,1)}) custom-call(s32[1,512]{1,0:T(1,128)S(1)} %bitcast.12, bf16[256,2048]{1,0:T(8,128)(2,1)} %bitcast.1.kv_hbm), custom_call_target="tpu_custom_call" | custom-call | flops 6000000000 | tf_op jit(solution)/shard_map/prepare/pallas_call | solution.py:140
  3.1 3.1 %collective-permute-start = (bf16[256,2048]{1,0:T(8,128)(2,1)}, bf16[256,2048]{1,0:T(8,128)(2,1)S(1)}, u32[]{:S(2)}, u32[]{:S(2)}) collective-permute-start(bf16[256,2048]{1,0:T(8,128)(2,1)} %bitcast.1.kv_hbm), channel_id=1, source_target_pairs={{0,8},{8,0},{16,24},{24,16},{1,9},{9,1},{17,25},{25,17},{2,10},{10... | collective-permute-start | bytes 3145736 | tf_op jit(solution)/shard_map/ppermute | solution.py:365
  6.1 2.6 %collective-permute-start.1 = (bf16[256,1024]{1,0:T(8,128)(2,1)}, bf16[256,1024]{1,0:T(8,128)(2,1)}, u32[]{:S(2)}, u32[]{:S(2)}) collective-permute-start(bf16[256,1024]{1,0:T(8,128)(2,1)} %get-tuple-element.26.refs_2_), channel_id=1, source_target_pairs={{0,16},{8,24},{16,0},{24,8},{1,17},{9,25},{17,1},{25,9},{2,18},{10... | collective-permute-start | bytes 1572872 | tf_op jit(solution)/shard_map/ppermute | solution.py:365
  8.7 0.0 copy-done
  8.7 0.0 copy-done.3
  8.7 0.0 copy-done.14
  8.7 3.3 %project_queries.1 = bf16[1024,1152]{1,0:T(8,128)(2,1)S(1)} custom-call(s32[8,512]{1,0:T(8,128)S(1)} %get-tuple-element.24.slot_ref, s32[1,512]{1,0:T(1,128)S(1)} %bitcast.14, bf16[512,1024]{1,0:T(8,128)(2,1)S(1)} %copy-done.3, bf16[1024,2048]{1,0:T(8,128)(2,1)S(1)} %copy-done), custom_call_target="tpu_custom_call" | custom-call | flops 2147483648 | bytes 5242880 | tf_op jit(solution)/shard_map/project_queries/pallas_call | solution.py:80
  12.0 0.0 copy-start.2
  12.1 1.4 %copy-done.2 = bf16[1024,1152]{1,0:T(8,128)(2,1)} copy-done((bf16[1024,1152]{1,0:T(8,128)(2,1)}, bf16[1024,1152]{1,0:T(8,128)(2,1)S(1)}, u32[]{:S(2)}) %copy-start.2) | copy-done | bytes 2359320
  13.5 0.3 collective-permute-start.2
  13.8 3.8 %all-to-all-start = ((bf16[8,128,1152]{2,1,0:T(8,128)(2,1)}), bf16[8,128,1152]{2,1,0:T(8,128)(2,1)S(1)}, u32[]{:S(2)}, u32[]{:S(2)}) async-start(bf16[8,128,1152]{2,1,0:T(8,128)(2,1)} %bitcast.11), calls=%async_computation | async-start | bytes 4718592 | tf_op jit(solution)/shard_map/all_to_all | solution.py:420
  18.3 0.0 copy-start.1
  18.3 2.2 %copy-done.1 = bf16[1024,2048]{1,0:T(8,128)(2,1)S(1)} copy-done((bf16[1024,2048]{1,0:T(8,128)(2,1)S(1)}, bf16[1024,2048]{1,0:T(8,128)(2,1)}, u32[]{:S(2)}) %copy-start.1) | copy-done | bytes 4194328
  20.5 1.2 %copy-done.4 = bf16[512,1024]{1,0:T(8,128)(2,1)S(1)} copy-done((bf16[512,1024]{1,0:T(8,128)(2,1)S(1)}, bf16[512,1024]{1,0:T(8,128)(2,1)}, u32[]{:S(2)}) %copy-start.4) | copy-done | bytes 1048600
  21.7 1.4 %project_gate.1 = (bf16[512,1024]{1,0:T(8,128)(2,1)S(1)}, s32[8,128]{1,0:T(8,128)S(1)}) custom-call(bf16[512,1024]{1,0:T(8,128)(2,1)S(1)} %copy-done.4, bf16[1024,2048]{1,0:T(8,128)(2,1)S(1)} %copy-done.1), custom_call_target="tpu_custom_call" | custom-call | flops 1073741824 | bytes 4194304 | tf_op jit(solution)/shard_map/project_gate/pallas_call | solution.py:107
  23.1 0.0 copy-start.11
  23.1 1.0 copy-done.11
  24.0 0.0 copy-done.9
  24.1 17.3 %collective-permute-done.1.refs_2_.refs_3_ = bf16[256,1024]{1,0:T(8,128)(2,1)} collective-permute-done((bf16[256,1024]{1,0:T(8,128)(2,1)}, bf16[256,1024]{1,0:T(8,128)(2,1)}, u32[]{:S(2)}, u32[]{:S(2)}) %collective-permute-start.1) | collective-permute-done | bytes 524320 | tf_op jit(solution)/shard_map/ppermute | solution.py:365
  41.3 3.5 %collective-permute-start.3 = (bf16[256,1024]{1,0:T(8,128)(2,1)}, bf16[256,1024]{1,0:T(8,128)(2,1)}, u32[]{:S(2)}, u32[]{:S(2)}) collective-permute-start(bf16[256,1024]{1,0:T(8,128)(2,1)} %collective-permute-done.1.refs_2_.refs_3_), channel_id=1, source_target_pairs={{0,8},{8,0},{16,24},{24,16},{1,9},{9,1},{17,25},{25,17},{2,10},{10... | collective-permute-start | bytes 1572872 | tf_op jit(solution)/shard_map/ppermute | solution.py:365
  44.9 8.7 %collective-permute-done.2.refs_3_.refs_1_.refs_6_ = bf16[256,1024]{1,0:T(8,128)(2,1)} collective-permute-done((bf16[256,1024]{1,0:T(8,128)(2,1)}, bf16[256,1024]{1,0:T(8,128)(2,1)}, u32[]{:S(2)}, u32[]{:S(2)}) %collective-permute-start.2) | collective-permute-done | bytes 524320 | tf_op jit(solution)/shard_map/ppermute | solution.py:365
  53.5 2.5 %collective-permute-start.9 = (bf16[256,1024]{1,0:T(8,128)(2,1)}, bf16[256,1024]{1,0:T(8,128)(2,1)}, u32[]{:S(2)}, u32[]{:S(2)}) collective-permute-start(bf16[256,1024]{1,0:T(8,128)(2,1)} %collective-permute-done.2.refs_3_.refs_1_.refs_6_), channel_id=1, source_target_pairs={{0,8},{8,0},{16,24},{24,16},{1,9},{9,1},{17,25},{25,17},{2,10},{10... | collective-permute-start | bytes 1572872 | tf_op jit(solution)/shard_map/ppermute | solution.py:365
  56.0 0.0 collective-permute-done.refs_1_.refs_4_.refs_7_
  56.0 0.3 slot_column.1
  56.4 0.0 copy-start.6
  56.4 0.7 copy-done.6
  57.1 0.0 all-to-all-done
  57.1 4.8 %attend.4.refs_2_ = f32[1024,512]{1,0:T(8,128)S(1)} custom-call(s32[1]{0:T(128)S(6)} %copy.9.length_ref, s32[8,128]{1,0:T(8,128)S(1)} %get-tuple-element.31.refs_0_, bf16[1024,1152]{1,0:T(8,128)(2,1)S(1)} %bitcast.7, bf16[256,1024]{1,0:T(8,128)(2,1)} %get-tuple-element.26.refs_2_, bf16[256,1024]{1,0:T(8,128)(2,1)} %collective-permute-done.1.refs_2_.refs_3_, ...), custom_call_target="tpu_custom_call" | custom-call | bytes 3670016 | tf_op jit(solution)/shard_map/attend/pallas_call | solution.py:273
  61.8 2.3 %collective-permute-done.3.refs_1_ = bf16[256,1024]{1,0:T(8,128)(2,1)} collective-permute-done((bf16[256,1024]{1,0:T(8,128)(2,1)}, bf16[256,1024]{1,0:T(8,128)(2,1)}, u32[]{:S(2)}, u32[]{:S(2)}) %collective-permute-start.3) | collective-permute-done | bytes 524320 | tf_op jit(solution)/shard_map/ppermute | solution.py:365
  64.2 2.5 %attend.5 = (bf16[512,512]{1,0:T(8,128)(2,1)S(1)}, bf16[256,512]{1,0:T(8,128)(2,1)S(1)}, bf16[256,512]{1,0:T(8,128)(2,1)S(1)}) custom-call(s32[1]{0:T(128)S(6)} %copy.9.length_ref, bf16[1024,1152]{1,0:T(8,128)(2,1)S(1)} %bitcast.8, bf16[256,1024]{1,0:T(8,128)(2,1)} %collective-permute-done.3.refs_1_, f32[1024,512]{1,0:T(8,128)S(1)} %attend.4.refs_2_), custom_call_target="tpu_custom_call" | custom-call | bytes 2621440 | tf_op jit(solution)/shard_map/attend/pallas_call | solution.py:273
  66.6 0.1 collective-permute-start.6
  66.7 0.5 collective-permute-start.4
  67.3 1.0 collective-permute-done.6
  68.3 3.0 %collective-permute-start.8 = (bf16[256,512]{1,0:T(8,128)(2,1)S(1)}, bf16[256,512]{1,0:T(8,128)(2,1)S(1)}, u32[]{:S(2)}, u32[]{:S(2)}) collective-permute-start(bf16[256,512]{1,0:T(8,128)(2,1)S(1)} %pad_maximum_fusion.2.refs_3_), channel_id=1, source_target_pairs={{0,6},{1,7},{2,4},{3,5},{4,2},{5,3},{6,0},{7,1},{8,14},{9,15},{10,... | collective-permute-start | bytes 786440 | tf_op jit(solution)/shard_map/ppermute | solution.py:365
  71.3 0.6 collective-permute-start.7
  71.9 0.0 collective-permute-done.4.refs_1_
  71.9 0.1 collective-permute-start.5
  72.1 4.8 %attend.6.refs_2_ = f32[1024,512]{1,0:T(8,128)S(1)} custom-call(s32[1]{0:T(128)S(6)} %copy.9.length_ref, s32[8,128]{1,0:T(8,128)S(1)} %wait_for.3.refs_0_, bf16[256,512]{1,0:T(8,128)(2,1)S(1)} %pad_maximum_fusion.refs_1_, bf16[256,512]{1,0:T(8,128)(2,1)S(1)} %pad_maximum_fusion.1.refs_2_, bf16[256,512]{1,0:T(8,128)(2,1)S(1)} %pad_maximum_fusion.2.refs_3_, ...), custom_call_target="tpu_custom_call" | custom-call | bytes 3670016 | tf_op jit(solution)/shard_map/attend/pallas_call | solution.py:273
  76.8 0.0 collective-permute-done.9.refs_1_
  76.8 2.7 %attend.7 = (bf16[512,512]{1,0:T(8,128)(2,1)S(1)}, bf16[256,512]{1,0:T(8,128)(2,1)S(1)}, bf16[256,512]{1,0:T(8,128)(2,1)S(1)}) custom-call(s32[1]{0:T(128)S(6)} %copy.9.length_ref, bf16[1024,1152]{1,0:T(8,128)(2,1)S(1)} %bitcast.10, bf16[256,1024]{1,0:T(8,128)(2,1)} %collective-permute-done.9.refs_1_, f32[1024,512]{1,0:T(8,128)S(1)} %attend.6.refs_2_), custom_call_target="tpu_custom_call" | custom-call | flops 10737418240 | bytes 2621440 | tf_op jit(solution)/shard_map/attend/pallas_call | solution.py:273
  79.5 0.1 collective-permute-start.10
  79.6 0.5 collective-permute-start.11
  80.1 0.0 collective-permute-done.8.refs_2_.refs_4_
  80.1 3.4 %collective-permute-done.7.refs_1_.refs_3_ = bf16[256,512]{1,0:T(8,128)(2,1)S(1)} collective-permute-done((bf16[256,512]{1,0:T(8,128)(2,1)S(1)}, bf16[256,512]{1,0:T(8,128)(2,1)S(1)}, u32[]{:S(2)}, u32[]{:S(2)}) %collective-permute-start.7) | collective-permute-done | bytes 262176 | tf_op jit(solution)/shard_map/ppermute | solution.py:365
  83.5 0.3 collective-permute-done.5.refs_0_.refs_2_
  83.8 0.0 collective-permute-done.10.refs_2_
  83.8 0.0 collective-permute-done.11
  83.9 0.0 copy-start.5
  83.9 0.0 copy-start.10
  83.9 0.0 copy-start.12
  83.9 0.0 copy-start.13
  84.0 1.6 %collective-permute-start.14 = (bf16[256,512]{1,0:T(8,128)(2,1)S(1)}, bf16[256,512]{1,0:T(8,128)(2,1)S(1)}, u32[]{:S(2)}, u32[]{:S(2)}) collective-permute-start(bf16[256,512]{1,0:T(8,128)(2,1)S(1)} %pad_maximum_fusion.5), channel_id=1, source_target_pairs={{0,6},{1,7},{2,4},{3,5},{4,2},{5,3},{6,0},{7,1},{8,14},{9,15},{10,... | collective-permute-start | bytes 786440 | tf_op jit(solution)/shard_map/ppermute | solution.py:365
  85.6 1.5 %collective-permute-start.13 = (bf16[256,512]{1,0:T(8,128)(2,1)S(1)}, bf16[256,512]{1,0:T(8,128)(2,1)S(1)}, u32[]{:S(2)}, u32[]{:S(2)}) collective-permute-start(bf16[256,512]{1,0:T(8,128)(2,1)S(1)} %pad_maximum_fusion.4), channel_id=1, source_target_pairs={{0,4},{1,5},{2,6},{3,7},{4,0},{5,1},{6,2},{7,3},{8,12},{9,13},{10,... | collective-permute-start | bytes 786440 | tf_op jit(solution)/shard_map/ppermute | solution.py:365
  87.1 0.6 collective-permute-start.12
  87.7 0.0 copy-done.7
  87.7 0.7 collect.1.refs_0_
  88.4 5.8 %collective-permute-done.14.refs_5_ = bf16[256,512]{1,0:T(8,128)(2,1)S(1)} collective-permute-done((bf16[256,512]{1,0:T(8,128)(2,1)S(1)}, bf16[256,512]{1,0:T(8,128)(2,1)S(1)}, u32[]{:S(2)}, u32[]{:S(2)}) %collective-permute-start.14) | collective-permute-done | bytes 262176 | tf_op jit(solution)/shard_map/ppermute | solution.py:365
  94.2 4.3 %collective-permute-done.13.refs_4_ = bf16[256,512]{1,0:T(8,128)(2,1)S(1)} collective-permute-done((bf16[256,512]{1,0:T(8,128)(2,1)S(1)}, bf16[256,512]{1,0:T(8,128)(2,1)S(1)}, u32[]{:S(2)}, u32[]{:S(2)}) %collective-permute-start.13) | collective-permute-done | bytes 262176 | tf_op jit(solution)/shard_map/ppermute | solution.py:365
  98.5 0.3 collective-permute-done.12.refs_3_
  98.8 0.0 copy-done.5
  98.8 0.0 copy-done.10
  98.8 0.0 copy-done.12
  98.8 3.1 %finish.1 = bf16[512,1024]{1,0:T(8,128)(2,1)} custom-call(s32[512,128]{1,0:T(8,128)S(1)} %copy-done.7, f32[1,1024]{1,0:T(1,128)S(1)} %bitcast.13, bf16[512,1024]{1,0:T(8,128)(2,1)S(1)} %copy-done.12, bf16[512,1024]{1,0:T(8,128)(2,1)S(1)} %copy-done.5, bf16[1024,1024]{1,0:T(8,128)(2,1)S(1)} %copy-done.10, bf16[512,512]{1,0:T(8,128)(2,1)S(1)} %collect.1.refs_0_, ...), custom_call_target="tpu_custom_call" | custom-call | flops 2147483648 | bytes 7340032 | tf_op jit(solution)/shard_map/finish/pallas_call | solution.py:350
  (23 shorter events, 0.2 us)
Async XLA Ops:
  0.0 0.7 copy-start.8
  0.7 8.1 %copy-start = (bf16[1024,2048]{1,0:T(8,128)(2,1)S(1)}, bf16[1024,2048]{1,0:T(8,128)(2,1)}, u32[]{:S(2)}) copy-start(bf16[1024,2048]{1,0:T(8,128)(2,1)} %w_ref.4) | copy-start | bytes 12582916
  0.7 8.1 %copy-start.3 = (bf16[512,1024]{1,0:T(8,128)(2,1)S(1)}, bf16[512,1024]{1,0:T(8,128)(2,1)}, u32[]{:S(2)}) copy-start(bf16[512,1024]{1,0:T(8,128)(2,1)} %x_ref.5) | copy-start | bytes 3145732
  0.7 8.1 %copy-start.14 = (s32[512]{0:T(512)S(1)}, s32[512]{0:T(512)}, u32[]{:S(2)}) copy-start(s32[512]{0:T(512)} %param.10) | copy-start | bytes 6148
  3.1 53.0 %collective-permute-start = (bf16[256,2048]{1,0:T(8,128)(2,1)}, bf16[256,2048]{1,0:T(8,128)(2,1)S(1)}, u32[]{:S(2)}, u32[]{:S(2)}) collective-permute-start(bf16[256,2048]{1,0:T(8,128)(2,1)} %bitcast.1.kv_hbm), channel_id=1, source_target_pairs={{0,8},{8,0},{16,24},{24,16},{1,9},{9,1},{17,25},{25,17},{2,10},{10... | collective-permute-start | bytes 3145736 | tf_op jit(solution)/shard_map/ppermute | solution.py:365
  6.1 35.2 %collective-permute-start.1 = (bf16[256,1024]{1,0:T(8,128)(2,1)}, bf16[256,1024]{1,0:T(8,128)(2,1)}, u32[]{:S(2)}, u32[]{:S(2)}) collective-permute-start(bf16[256,1024]{1,0:T(8,128)(2,1)} %get-tuple-element.26.refs_2_), channel_id=1, source_target_pairs={{0,16},{8,24},{16,0},{24,8},{1,17},{9,25},{17,1},{25,9},{2,18},{10... | collective-permute-start | bytes 1572872 | tf_op jit(solution)/shard_map/ppermute | solution.py:365
  12.0 1.4 %copy-start.2 = (bf16[1024,1152]{1,0:T(8,128)(2,1)}, bf16[1024,1152]{1,0:T(8,128)(2,1)S(1)}, u32[]{:S(2)}) copy-start(bf16[1024,1152]{1,0:T(8,128)(2,1)S(1)} %project_queries.1) | copy-start | bytes 7077892
  13.5 40.0 %collective-permute-start.2 = (bf16[256,1024]{1,0:T(8,128)(2,1)}, bf16[256,1024]{1,0:T(8,128)(2,1)}, u32[]{:S(2)}, u32[]{:S(2)}) collective-permute-start(bf16[256,1024]{1,0:T(8,128)(2,1)} %get-tuple-element.28.refs_5_), channel_id=1, source_target_pairs={{0,16},{8,24},{16,0},{24,8},{1,17},{9,25},{17,1},{25,9},{2,18},{10... | collective-permute-start | bytes 1572872 | tf_op jit(solution)/shard_map/ppermute | solution.py:365
  13.8 43.3 %all-to-all-start = ((bf16[8,128,1152]{2,1,0:T(8,128)(2,1)}), bf16[8,128,1152]{2,1,0:T(8,128)(2,1)S(1)}, u32[]{:S(2)}, u32[]{:S(2)}) async-start(bf16[8,128,1152]{2,1,0:T(8,128)(2,1)} %bitcast.11), calls=%async_computation | async-start | bytes 4718592 | tf_op jit(solution)/shard_map/all_to_all | solution.py:420
  18.3 2.2 %copy-start.1 = (bf16[1024,2048]{1,0:T(8,128)(2,1)S(1)}, bf16[1024,2048]{1,0:T(8,128)(2,1)}, u32[]{:S(2)}) copy-start(bf16[1024,2048]{1,0:T(8,128)(2,1)} %w_ref.4) | copy-start | bytes 12582916
  20.5 1.2 %copy-start.4 = (bf16[512,1024]{1,0:T(8,128)(2,1)S(1)}, bf16[512,1024]{1,0:T(8,128)(2,1)}, u32[]{:S(2)}) copy-start(bf16[512,1024]{1,0:T(8,128)(2,1)} %x_ref.5) | copy-start | bytes 3145732
  21.7 2.4 %copy-start.9 = (s32[512,1]{0,1:T(1,128)S(1)}, s32[512,1]{0,1:T(1,128)}, u32[]{:S(2)}) copy-start(s32[512,1]{0,1:T(1,128)} %param.9) | copy-start | bytes 6148
  23.1 1.0 copy-start.11
  41.3 22.9 %collective-permute-start.3 = (bf16[256,1024]{1,0:T(8,128)(2,1)}, bf16[256,1024]{1,0:T(8,128)(2,1)}, u32[]{:S(2)}, u32[]{:S(2)}) collective-permute-start(bf16[256,1024]{1,0:T(8,128)(2,1)} %collective-permute-done.1.refs_2_.refs_3_), channel_id=1, source_target_pairs={{0,8},{8,0},{16,24},{24,16},{1,9},{9,1},{17,25},{25,17},{2,10},{10... | collective-permute-start | bytes 1572872 | tf_op jit(solution)/shard_map/ppermute | solution.py:365
  53.5 23.3 %collective-permute-start.9 = (bf16[256,1024]{1,0:T(8,128)(2,1)}, bf16[256,1024]{1,0:T(8,128)(2,1)}, u32[]{:S(2)}, u32[]{:S(2)}) collective-permute-start(bf16[256,1024]{1,0:T(8,128)(2,1)} %collective-permute-done.2.refs_3_.refs_1_.refs_6_), channel_id=1, source_target_pairs={{0,8},{8,0},{16,24},{24,16},{1,9},{9,1},{17,25},{25,17},{2,10},{10... | collective-permute-start | bytes 1572872 | tf_op jit(solution)/shard_map/ppermute | solution.py:365
  56.4 0.7 copy-start.6
  66.6 1.6 %collective-permute-start.6 = (bf16[256,512]{1,0:T(8,128)(2,1)S(1)}, bf16[256,512]{1,0:T(8,128)(2,1)S(1)}, u32[]{:S(2)}, u32[]{:S(2)}) collective-permute-start(bf16[256,512]{1,0:T(8,128)(2,1)S(1)} %get-tuple-element.34), channel_id=1, source_target_pairs={{0,1},{1,0},{2,3},{3,2},{4,5},{5,4},{6,7},{7,6},{8,9},{9,8},{10,11... | collective-permute-start | bytes 786440 | tf_op jit(solution)/shard_map/ppermute | solution.py:365
  66.7 5.2 %collective-permute-start.4 = (bf16[256,512]{1,0:T(8,128)(2,1)S(1)}, bf16[256,512]{1,0:T(8,128)(2,1)S(1)}, u32[]{:S(2)}, u32[]{:S(2)}) collective-permute-start(bf16[256,512]{1,0:T(8,128)(2,1)S(1)} %get-tuple-element.33), channel_id=1, source_target_pairs={{0,1},{1,0},{2,3},{3,2},{4,5},{5,4},{6,7},{7,6},{8,9},{9,8},{10,11... | collective-permute-start | bytes 786440 | tf_op jit(solution)/shard_map/ppermute | solution.py:365
  68.3 11.8 %collective-permute-start.8 = (bf16[256,512]{1,0:T(8,128)(2,1)S(1)}, bf16[256,512]{1,0:T(8,128)(2,1)S(1)}, u32[]{:S(2)}, u32[]{:S(2)}) collective-permute-start(bf16[256,512]{1,0:T(8,128)(2,1)S(1)} %pad_maximum_fusion.2.refs_3_), channel_id=1, source_target_pairs={{0,6},{1,7},{2,4},{3,5},{4,2},{5,3},{6,0},{7,1},{8,14},{9,15},{10,... | collective-permute-start | bytes 786440 | tf_op jit(solution)/shard_map/ppermute | solution.py:365
  71.3 12.2 %collective-permute-start.7 = (bf16[256,512]{1,0:T(8,128)(2,1)S(1)}, bf16[256,512]{1,0:T(8,128)(2,1)S(1)}, u32[]{:S(2)}, u32[]{:S(2)}) collective-permute-start(bf16[256,512]{1,0:T(8,128)(2,1)S(1)} %pad_maximum_fusion.1.refs_2_), channel_id=1, source_target_pairs={{0,4},{1,5},{2,6},{3,7},{4,0},{5,1},{6,2},{7,3},{8,12},{9,13},{10,... | collective-permute-start | bytes 786440 | tf_op jit(solution)/shard_map/ppermute | solution.py:365
  71.9 11.9 %collective-permute-start.5 = (bf16[256,512]{1,0:T(8,128)(2,1)S(1)}, bf16[256,512]{1,0:T(8,128)(2,1)S(1)}, u32[]{:S(2)}, u32[]{:S(2)}) collective-permute-start(bf16[256,512]{1,0:T(8,128)(2,1)S(1)} %pad_maximum_fusion.refs_1_), channel_id=1, source_target_pairs={{0,2},{1,3},{2,0},{3,1},{4,6},{5,7},{6,4},{7,5},{8,10},{9,11},{10,... | collective-permute-start | bytes 786440 | tf_op jit(solution)/shard_map/ppermute | solution.py:365
  79.5 4.3 %collective-permute-start.10 = (bf16[256,512]{1,0:T(8,128)(2,1)S(1)}, bf16[256,512]{1,0:T(8,128)(2,1)S(1)}, u32[]{:S(2)}, u32[]{:S(2)}) collective-permute-start(bf16[256,512]{1,0:T(8,128)(2,1)S(1)} %get-tuple-element.36), channel_id=1, source_target_pairs={{0,1},{1,0},{2,3},{3,2},{4,5},{5,4},{6,7},{7,6},{8,9},{9,8},{10,11... | collective-permute-start | bytes 786440 | tf_op jit(solution)/shard_map/ppermute | solution.py:365
  79.6 4.2 %collective-permute-start.11 = (bf16[256,512]{1,0:T(8,128)(2,1)S(1)}, bf16[256,512]{1,0:T(8,128)(2,1)S(1)}, u32[]{:S(2)}, u32[]{:S(2)}) collective-permute-start(bf16[256,512]{1,0:T(8,128)(2,1)S(1)} %get-tuple-element.37), channel_id=1, source_target_pairs={{0,1},{1,0},{2,3},{3,2},{4,5},{5,4},{6,7},{7,6},{8,9},{9,8},{10,11... | collective-permute-start | bytes 786440 | tf_op jit(solution)/shard_map/ppermute | solution.py:365
  83.8 3.9 %copy-start.7 = (s32[512,128]{1,0:T(8,128)S(1)}, s32[512,128]{1,0:T(8,128)}, u32[]{:S(2)}) copy-start(s32[512,128]{1,0:T(8,128)} %copy-done.6) | copy-start | bytes 786436
  83.9 14.9 %copy-start.5 = (bf16[512,1024]{1,0:T(8,128)(2,1)S(1)}, bf16[512,1024]{1,0:T(8,128)(2,1)}, u32[]{:S(2)}) copy-start(bf16[512,1024]{1,0:T(8,128)(2,1)} %x_ref.5) | copy-start | bytes 3145732
  83.9 14.9 %copy-start.10 = (bf16[1024,1024]{1,0:T(8,128)(2,1)S(1)}, bf16[1024,1024]{1,0:T(8,128)(2,1)}, u32[]{:S(2)}) copy-start(bf16[1024,1024]{1,0:T(8,128)(2,1)} %w_ref.5) | copy-start | bytes 6291460
  83.9 14.9 %copy-start.12 = (bf16[512,1024]{1,0:T(8,128)(2,1)S(1)}, bf16[512,1024]{1,0:T(8,128)(2,1)}, u32[]{:S(2)}) copy-start(bf16[512,1024]{1,0:T(8,128)(2,1)} %copy-done.11) | copy-start | bytes 3145732
  83.9 14.9 %copy-start.13 = (f32[1024]{0:T(1024)S(1)}, f32[1024]{0:T(1024)}, u32[]{:S(2)}) copy-start(f32[1024]{0:T(1024)} %param.15) | copy-start | bytes 12292
  84.0 10.2 %collective-permute-start.14 = (bf16[256,512]{1,0:T(8,128)(2,1)S(1)}, bf16[256,512]{1,0:T(8,128)(2,1)S(1)}, u32[]{:S(2)}, u32[]{:S(2)}) collective-permute-start(bf16[256,512]{1,0:T(8,128)(2,1)S(1)} %pad_maximum_fusion.5), channel_id=1, source_target_pairs={{0,6},{1,7},{2,4},{3,5},{4,2},{5,3},{6,0},{7,1},{8,14},{9,15},{10,... | collective-permute-start | bytes 786440 | tf_op jit(solution)/shard_map/ppermute | solution.py:365
  85.6 12.9 %collective-permute-start.13 = (bf16[256,512]{1,0:T(8,128)(2,1)S(1)}, bf16[256,512]{1,0:T(8,128)(2,1)S(1)}, u32[]{:S(2)}, u32[]{:S(2)}) collective-permute-start(bf16[256,512]{1,0:T(8,128)(2,1)S(1)} %pad_maximum_fusion.4), channel_id=1, source_target_pairs={{0,4},{1,5},{2,6},{3,7},{4,0},{5,1},{6,2},{7,3},{8,12},{9,13},{10,... | collective-permute-start | bytes 786440 | tf_op jit(solution)/shard_map/ppermute | solution.py:365
  87.1 11.7 %collective-permute-start.12 = (bf16[256,512]{1,0:T(8,128)(2,1)S(1)}, bf16[256,512]{1,0:T(8,128)(2,1)S(1)}, u32[]{:S(2)}, u32[]{:S(2)}) collective-permute-start(bf16[256,512]{1,0:T(8,128)(2,1)S(1)} %pad_maximum_fusion.3), channel_id=1, source_target_pairs={{0,2},{1,3},{2,0},{3,1},{4,6},{5,7},{6,4},{7,5},{8,10},{9,11},{10,... | collective-permute-start | bytes 786440 | tf_op jit(solution)/shard_map/ppermute | solution.py:365

commit v18 on v17

--- a/solution.py
+++ b/solution.py
@@ -427,7 +427,13 @@
     behind = None
     for number, (first, heads) in enumerate(spans):
         held = far[number]
-        cuts = [(key | 1, [swap(held[key], "user", 1, count)], 0, heads) for key in evens[1:]]
+        passed = [held[key] for key in evens[1:]]
+        if number:
+            passed, _ = lax.optimization_barrier((passed, attn[0]))
+        cuts = [
+            (key | 1, [swap(part, "user", 1, count)], 0, heads)
+            for key, part in zip(evens[1:], passed)
+        ]
         segments = [(key, [held[key]], 0, heads) for key in evens]
         segments.append((1, [near], first, HEADS + first))
         base = attend(

time: 103 us -> 103 us (level); the launches traced: 102 us -> 103 us
  waiting for transfers between devices: 43.3 us -> 46.1 us
  Pallas kernels: 25.9 us -> 24.6 us
    ppermute x15, waiting for transfers between devices: 43.3 us -> 46.1 us  [swap(): return lax.ppermute(array, axis, [(i, i ^ bits) for i in range(count)])]
    pallas_call x4, Pallas kernels: 14.7 us -> 13.4 us  [attend(): pl.pallas_call(functools.partial(attend_kernel, size, heads, first, start...]
  transfers between devices with their start and end apart: 16 -> 16, of which waited for: 9 -> 9; matrix products, arithmetic and copies ran while one was open for 0% -> 0% of each run, Pallas kernels for 20% -> 16%
where the time goes in v18:
time: 103 us
  waiting for transfers between devices  46.1 us (45%)
  Pallas kernels  24.6 us (24%)
  starting transfers between devices  23.9 us (23%)
  local copies, waits for them, and re-layouts  7.33 us (7%)
  between operations  1.11 us (1%)
    ppermute x15, waiting for transfers between devices, swap(): return lax.ppermute(array, axis, [(i, i ^ bits) for i in range(count)])  46.1 us
    ppermute x15, starting transfers between devices, swap(): return lax.ppermute(array, axis, [(i, i ^ bits) for i in range(count)])  20.1 us
    pallas_call x4, Pallas kernels, attend(): pl.pallas_call(functools.partial(attend_kernel, size, heads, first, start...  13.4 us
    unnamed x30, local copies, waits for them, and re-layouts  7.22 us
    all_to_all x1, starting transfers between devices, per_device(): lax.all_to_all(send.reshape(columns, capacity, -1), 'cand', split_axis=0,...  3.8 us
    pallas_call x1, Pallas kernels, project_queries(): pl.pallas_call(query_kernel, in_specs=whole(4), out_specs=whole()[0], out...  3.29 us
    pallas_call x1, Pallas kernels, finish(): pl.pallas_call(functools.partial(finish_kernel, len(early), capacity, slo...  3.1 us
    pallas_call x1, Pallas kernels, prepare(): pl.pallas_call(functools.partial(prepare_kernel, columns, capacity, spans...  2.36 us
  transfers between devices with their start and end apart: 16, of which 9 were waited for; matrix products, arithmetic and copies ran while one was open for 0% of the time, Pallas kernels for 16%

profile of v18, /device:TPU:0, one launch (start us, length us, event | category | flops | bytes accessed | tf_op | source)
XLA Modules:
  0.0 103.1 jit_solution(17062982013562780510)
XLA Ops:
  0.0 0.7 copy-done.8
  0.7 2.4 %prepare.1 = (s32[8,512]{1,0:T(8,128)S(1)}, bf16[256,1024]{1,0:T(8,128)(2,1)}, bf16[256,1024]{1,0:T(8,128)(2,1)}) custom-call(s32[1,512]{1,0:T(1,128)S(1)} %bitcast.12, bf16[256,2048]{1,0:T(8,128)(2,1)} %bitcast.1.kv_hbm), custom_call_target="tpu_custom_call" | custom-call | flops 6000000000 | tf_op jit(solution)/shard_map/prepare/pallas_call | solution.py:140
  3.1 3.1 %collective-permute-start = (bf16[256,2048]{1,0:T(8,128)(2,1)}, bf16[256,2048]{1,0:T(8,128)(2,1)S(1)}, u32[]{:S(2)}, u32[]{:S(2)}) collective-permute-start(bf16[256,2048]{1,0:T(8,128)(2,1)} %bitcast.1.kv_hbm), channel_id=1, source_target_pairs={{0,8},{8,0},{16,24},{24,16},{1,9},{9,1},{17,25},{25,17},{2,10},{10... | collective-permute-start | bytes 3145736 | tf_op jit(solution)/shard_map/ppermute | solution.py:365
  6.1 2.6 %collective-permute-start.1 = (bf16[256,1024]{1,0:T(8,128)(2,1)}, bf16[256,1024]{1,0:T(8,128)(2,1)}, u32[]{:S(2)}, u32[]{:S(2)}) collective-permute-start(bf16[256,1024]{1,0:T(8,128)(2,1)} %get-tuple-element.27.refs_2_), channel_id=1, source_target_pairs={{0,16},{8,24},{16,0},{24,8},{1,17},{9,25},{17,1},{25,9},{2,18},{10... | collective-permute-start | bytes 1572872 | tf_op jit(solution)/shard_map/ppermute | solution.py:365
  8.7 0.0 copy-done
  8.7 0.0 copy-done.3
  8.7 0.0 copy-done.14
  8.7 3.3 %project_queries.1 = bf16[1024,1152]{1,0:T(8,128)(2,1)S(1)} custom-call(s32[8,512]{1,0:T(8,128)S(1)} %get-tuple-element.25.slot_ref, s32[1,512]{1,0:T(1,128)S(1)} %bitcast.14, bf16[512,1024]{1,0:T(8,128)(2,1)S(1)} %copy-done.3, bf16[1024,2048]{1,0:T(8,128)(2,1)S(1)} %copy-done), custom_call_target="tpu_custom_call" | custom-call | flops 2147483648 | bytes 5242880 | tf_op jit(solution)/shard_map/project_queries/pallas_call | solution.py:80
  12.0 0.0 copy-start.2
  12.1 1.4 %copy-done.2 = bf16[1024,1152]{1,0:T(8,128)(2,1)} copy-done((bf16[1024,1152]{1,0:T(8,128)(2,1)}, bf16[1024,1152]{1,0:T(8,128)(2,1)S(1)}, u32[]{:S(2)}) %copy-start.2) | copy-done | bytes 2359320
  13.5 0.3 collective-permute-start.2
  13.8 3.8 %all-to-all-start = ((bf16[8,128,1152]{2,1,0:T(8,128)(2,1)}), bf16[8,128,1152]{2,1,0:T(8,128)(2,1)S(1)}, u32[]{:S(2)}, u32[]{:S(2)}) async-start(bf16[8,128,1152]{2,1,0:T(8,128)(2,1)} %bitcast.11), calls=%async_computation | async-start | bytes 4718592 | tf_op jit(solution)/shard_map/all_to_all | solution.py:420
  18.3 0.0 copy-start.1
  18.3 2.2 %copy-done.1 = bf16[1024,2048]{1,0:T(8,128)(2,1)S(1)} copy-done((bf16[1024,2048]{1,0:T(8,128)(2,1)S(1)}, bf16[1024,2048]{1,0:T(8,128)(2,1)}, u32[]{:S(2)}) %copy-start.1) | copy-done | bytes 4194328
  20.5 1.2 %copy-done.4 = bf16[512,1024]{1,0:T(8,128)(2,1)S(1)} copy-done((bf16[512,1024]{1,0:T(8,128)(2,1)S(1)}, bf16[512,1024]{1,0:T(8,128)(2,1)}, u32[]{:S(2)}) %copy-start.4) | copy-done | bytes 1048600
  21.7 1.4 %project_gate.1 = (bf16[512,1024]{1,0:T(8,128)(2,1)S(1)}, s32[8,128]{1,0:T(8,128)S(1)}) custom-call(bf16[512,1024]{1,0:T(8,128)(2,1)S(1)} %copy-done.4, bf16[1024,2048]{1,0:T(8,128)(2,1)S(1)} %copy-done.1), custom_call_target="tpu_custom_call" | custom-call | flops 1073741824 | bytes 4194304 | tf_op jit(solution)/shard_map/project_gate/pallas_call | solution.py:107
  23.1 0.0 copy-start.11
  23.1 1.0 copy-done.11
  24.0 0.0 copy-done.9
  24.1 17.3 %collective-permute-done.1.refs_2_.refs_3_ = bf16[256,1024]{1,0:T(8,128)(2,1)} collective-permute-done((bf16[256,1024]{1,0:T(8,128)(2,1)}, bf16[256,1024]{1,0:T(8,128)(2,1)}, u32[]{:S(2)}, u32[]{:S(2)}) %collective-permute-start.1) | collective-permute-done | bytes 524320 | tf_op jit(solution)/shard_map/ppermute | solution.py:365
  41.3 3.5 %collective-permute-start.3 = (bf16[256,1024]{1,0:T(8,128)(2,1)}, bf16[256,1024]{1,0:T(8,128)(2,1)}, u32[]{:S(2)}, u32[]{:S(2)}) collective-permute-start(bf16[256,1024]{1,0:T(8,128)(2,1)} %collective-permute-done.1.refs_2_.refs_3_), channel_id=1, source_target_pairs={{0,8},{8,0},{16,24},{24,16},{1,9},{9,1},{17,25},{25,17},{2,10},{10... | collective-permute-start | bytes 1572872 | tf_op jit(solution)/shard_map/ppermute | solution.py:365
  44.9 8.7 %collective-permute-done.2.refs_3_.refs_1_.refs_6_ = bf16[256,1024]{1,0:T(8,128)(2,1)} collective-permute-done((bf16[256,1024]{1,0:T(8,128)(2,1)}, bf16[256,1024]{1,0:T(8,128)(2,1)}, u32[]{:S(2)}, u32[]{:S(2)}) %collective-permute-start.2) | collective-permute-done | bytes 524320 | tf_op jit(solution)/shard_map/ppermute | solution.py:365
  53.5 0.0 collective-permute-done.refs_1_.refs_4_.refs_7_
  53.5 0.3 slot_column.1
  53.8 0.0 copy-start.6
  53.9 0.7 copy-done.6
  54.6 0.0 all-to-all-done
  54.6 4.8 %attend.4.refs_2_ = f32[1024,512]{1,0:T(8,128)S(1)} custom-call(s32[1]{0:T(128)S(6)} %copy.9.length_ref, s32[8,128]{1,0:T(8,128)S(1)} %get-tuple-element.32.refs_0_, bf16[1024,1152]{1,0:T(8,128)(2,1)S(1)} %bitcast.7, bf16[256,1024]{1,0:T(8,128)(2,1)} %get-tuple-element.27.refs_2_, bf16[256,1024]{1,0:T(8,128)(2,1)} %collective-permute-done.1.refs_2_.refs_3_, ...), custom_call_target="tpu_custom_call" | custom-call | bytes 3670016 | tf_op jit(solution)/shard_map/attend/pallas_call | solution.py:273
  59.3 4.0 %collective-permute-done.3.refs_1_ = bf16[256,1024]{1,0:T(8,128)(2,1)} collective-permute-done((bf16[256,1024]{1,0:T(8,128)(2,1)}, bf16[256,1024]{1,0:T(8,128)(2,1)}, u32[]{:S(2)}, u32[]{:S(2)}) %collective-permute-start.3) | collective-permute-done | bytes 524320 | tf_op jit(solution)/shard_map/ppermute | solution.py:365
  63.3 2.5 %attend.5 = (bf16[512,512]{1,0:T(8,128)(2,1)S(1)}, bf16[256,512]{1,0:T(8,128)(2,1)S(1)}, bf16[256,512]{1,0:T(8,128)(2,1)S(1)}) custom-call(s32[1]{0:T(128)S(6)} %copy.9.length_ref, bf16[1024,1152]{1,0:T(8,128)(2,1)S(1)} %bitcast.8, bf16[256,1024]{1,0:T(8,128)(2,1)} %collective-permute-done.3.refs_1_, f32[1024,512]{1,0:T(8,128)S(1)} %attend.4.refs_2_), custom_call_target="tpu_custom_call" | custom-call | bytes 2621440 | tf_op jit(solution)/shard_map/attend/pallas_call | solution.py:273
  65.8 0.1 collective-permute-start.4
  65.9 0.5 collective-permute-start.6
  66.4 1.8 %collective-permute-start.9 = (bf16[256,1024]{1,0:T(8,128)(2,1)}, bf16[256,1024]{1,0:T(8,128)(2,1)S(1)}, u32[]{:S(2)}, u32[]{:S(2)}) collective-permute-start(bf16[256,1024]{1,0:T(8,128)(2,1)} %collective-permute-done.2.refs_3_.refs_1_.refs_6_), channel_id=1, source_target_pairs={{0,8},{8,0},{16,24},{24,16},{1,9},{9,1},{17,25},{25,17},{2,10},{10... | collective-permute-start | bytes 1572872 | tf_op jit(solution)/shard_map/ppermute | solution.py:365
  68.2 0.0 collective-permute-done.4.refs_1_
  68.3 1.6 %collective-permute-start.5 = (bf16[256,512]{1,0:T(8,128)(2,1)S(1)}, bf16[256,512]{1,0:T(8,128)(2,1)S(1)}, u32[]{:S(2)}, u32[]{:S(2)}) collective-permute-start(bf16[256,512]{1,0:T(8,128)(2,1)S(1)} %pad_maximum_fusion.refs_1_), channel_id=1, source_target_pairs={{0,2},{1,3},{2,0},{3,1},{4,6},{5,7},{6,4},{7,5},{8,10},{9,11},{10,... | collective-permute-start | bytes 786440 | tf_op jit(solution)/shard_map/ppermute | solution.py:365
  69.8 0.0 collective-permute-done.6
  69.9 1.6 %collective-permute-start.7 = (bf16[256,512]{1,0:T(8,128)(2,1)S(1)}, bf16[256,512]{1,0:T(8,128)(2,1)S(1)}, u32[]{:S(2)}, u32[]{:S(2)}) collective-permute-start(bf16[256,512]{1,0:T(8,128)(2,1)S(1)} %pad_maximum_fusion.1.refs_2_), channel_id=1, source_target_pairs={{0,4},{1,5},{2,6},{3,7},{4,0},{5,1},{6,2},{7,3},{8,12},{9,13},{10,... | collective-permute-start | bytes 786440 | tf_op jit(solution)/shard_map/ppermute | solution.py:365
  71.5 0.5 collective-permute-start.8
  72.0 4.8 %attend.6.refs_2_ = f32[1024,512]{1,0:T(8,128)S(1)} custom-call(s32[1]{0:T(128)S(6)} %copy.9.length_ref, s32[8,128]{1,0:T(8,128)S(1)} %wait_for.3.refs_0_, bf16[256,512]{1,0:T(8,128)(2,1)S(1)} %pad_maximum_fusion.refs_1_, bf16[256,512]{1,0:T(8,128)(2,1)S(1)} %pad_maximum_fusion.1.refs_2_, bf16[256,512]{1,0:T(8,128)(2,1)S(1)} %pad_maximum_fusion.2.refs_3_, ...), custom_call_target="tpu_custom_call" | custom-call | bytes 3670016 | tf_op jit(solution)/shard_map/attend/pallas_call | solution.py:273
  76.8 3.8 %collective-permute-done.9.refs_1_ = bf16[256,1024]{1,0:T(8,128)(2,1)S(1)} collective-permute-done((bf16[256,1024]{1,0:T(8,128)(2,1)}, bf16[256,1024]{1,0:T(8,128)(2,1)S(1)}, u32[]{:S(2)}, u32[]{:S(2)}) %collective-permute-start.9) | collective-permute-done | bytes 524320 | tf_op jit(solution)/shard_map/ppermute | solution.py:365
  80.6 1.4 %attend.7 = (bf16[512,512]{1,0:T(8,128)(2,1)S(1)}, bf16[256,512]{1,0:T(8,128)(2,1)S(1)}, bf16[256,512]{1,0:T(8,128)(2,1)S(1)}) custom-call(s32[1]{0:T(128)S(6)} %copy.9.length_ref, bf16[1024,1152]{1,0:T(8,128)(2,1)S(1)} %bitcast.10, bf16[256,1024]{1,0:T(8,128)(2,1)S(1)} %collective-permute-done.9.refs_1_, f32[1024,512]{1,0:T(8,128)S(1)} %attend.6.refs_2_), custom_call_target="tpu_custom_call" | custom-call | flops 10737418240 | bytes 2621440 | tf_op jit(solution)/shard_map/attend/pallas_call | solution.py:273
  82.0 0.3 collective-permute-start.10
  82.3 0.5 collective-permute-start.11
  82.8 0.0 collective-permute-done.5.refs_0_.refs_2_
  82.8 0.5 collective-permute-done.7.refs_1_.refs_3_
  83.3 0.0 collective-permute-done.8.refs_2_.refs_4_
  83.3 0.5 collective-permute-done.10.refs_2_
  83.8 0.4 collective-permute-done.11
  84.2 0.0 copy-start.5
  84.3 0.0 copy-start.10
  84.3 0.0 copy-start.12
  84.3 0.0 copy-start.13
  84.4 1.7 %collective-permute-start.12 = (bf16[256,512]{1,0:T(8,128)(2,1)S(1)}, bf16[256,512]{1,0:T(8,128)(2,1)S(1)}, u32[]{:S(2)}, u32[]{:S(2)}) collective-permute-start(bf16[256,512]{1,0:T(8,128)(2,1)S(1)} %pad_maximum_fusion.3), channel_id=1, source_target_pairs={{0,2},{1,3},{2,0},{3,1},{4,6},{5,7},{6,4},{7,5},{8,10},{9,11},{10,... | collective-permute-start | bytes 786440 | tf_op jit(solution)/shard_map/ppermute | solution.py:365
  86.1 1.6 %collective-permute-start.13 = (bf16[256,512]{1,0:T(8,128)(2,1)S(1)}, bf16[256,512]{1,0:T(8,128)(2,1)S(1)}, u32[]{:S(2)}, u32[]{:S(2)}) collective-permute-start(bf16[256,512]{1,0:T(8,128)(2,1)S(1)} %pad_maximum_fusion.4), channel_id=1, source_target_pairs={{0,4},{1,5},{2,6},{3,7},{4,0},{5,1},{6,2},{7,3},{8,12},{9,13},{10,... | collective-permute-start | bytes 786440 | tf_op jit(solution)/shard_map/ppermute | solution.py:365
  87.7 0.4 collective-permute-start.14
  88.1 0.0 copy-done.7
  88.1 0.7 collect.1.refs_0_
  88.8 4.8 %collective-permute-done.12.refs_3_ = bf16[256,512]{1,0:T(8,128)(2,1)S(1)} collective-permute-done((bf16[256,512]{1,0:T(8,128)(2,1)S(1)}, bf16[256,512]{1,0:T(8,128)(2,1)S(1)}, u32[]{:S(2)}, u32[]{:S(2)}) %collective-permute-start.12) | collective-permute-done | bytes 262176 | tf_op jit(solution)/shard_map/ppermute | solution.py:365
  93.6 6.2 %collective-permute-done.13.refs_4_ = bf16[256,512]{1,0:T(8,128)(2,1)S(1)} collective-permute-done((bf16[256,512]{1,0:T(8,128)(2,1)S(1)}, bf16[256,512]{1,0:T(8,128)(2,1)S(1)}, u32[]{:S(2)}, u32[]{:S(2)}) %collective-permute-start.13) | collective-permute-done | bytes 262176 | tf_op jit(solution)/shard_map/ppermute | solution.py:365
  99.8 0.0 collective-permute-done.14.refs_5_
  99.8 0.0 copy-done.5
  99.8 0.0 copy-done.12
  99.8 0.0 copy-done.13
  99.8 3.1 %finish.1 = bf16[512,1024]{1,0:T(8,128)(2,1)} custom-call(s32[512,128]{1,0:T(8,128)S(1)} %copy-done.7, f32[1,1024]{1,0:T(1,128)S(1)} %bitcast.13, bf16[512,1024]{1,0:T(8,128)(2,1)S(1)} %copy-done.12, bf16[512,1024]{1,0:T(8,128)(2,1)S(1)} %copy-done.5, bf16[1024,1024]{1,0:T(8,128)(2,1)S(1)} %copy-done.10, bf16[512,512]{1,0:T(8,128)(2,1)S(1)} %collect.1.refs_0_, ...), custom_call_target="tpu_custom_call" | custom-call | flops 2147483648 | bytes 7340032 | tf_op jit(solution)/shard_map/finish/pallas_call | solution.py:350
  (23 shorter events, 0.2 us)
Async XLA Ops:
  0.0 0.7 copy-start.8
  0.7 8.1 %copy-start = (bf16[1024,2048]{1,0:T(8,128)(2,1)S(1)}, bf16[1024,2048]{1,0:T(8,128)(2,1)}, u32[]{:S(2)}) copy-start(bf16[1024,2048]{1,0:T(8,128)(2,1)} %w_ref.4) | copy-start | bytes 12582916
  0.7 8.1 %copy-start.3 = (bf16[512,1024]{1,0:T(8,128)(2,1)S(1)}, bf16[512,1024]{1,0:T(8,128)(2,1)}, u32[]{:S(2)}) copy-start(bf16[512,1024]{1,0:T(8,128)(2,1)} %x_ref.5) | copy-start | bytes 3145732
  0.7 8.1 %copy-start.14 = (s32[512]{0:T(512)S(1)}, s32[512]{0:T(512)}, u32[]{:S(2)}) copy-start(s32[512]{0:T(512)} %param.10) | copy-start | bytes 6148
  3.1 50.5 %collective-permute-start = (bf16[256,2048]{1,0:T(8,128)(2,1)}, bf16[256,2048]{1,0:T(8,128)(2,1)S(1)}, u32[]{:S(2)}, u32[]{:S(2)}) collective-permute-start(bf16[256,2048]{1,0:T(8,128)(2,1)} %bitcast.1.kv_hbm), channel_id=1, source_target_pairs={{0,8},{8,0},{16,24},{24,16},{1,9},{9,1},{17,25},{25,17},{2,10},{10... | collective-permute-start | bytes 3145736 | tf_op jit(solution)/shard_map/ppermute | solution.py:365
  6.1 35.2 %collective-permute-start.1 = (bf16[256,1024]{1,0:T(8,128)(2,1)}, bf16[256,1024]{1,0:T(8,128)(2,1)}, u32[]{:S(2)}, u32[]{:S(2)}) collective-permute-start(bf16[256,1024]{1,0:T(8,128)(2,1)} %get-tuple-element.27.refs_2_), channel_id=1, source_target_pairs={{0,16},{8,24},{16,0},{24,8},{1,17},{9,25},{17,1},{25,9},{2,18},{10... | collective-permute-start | bytes 1572872 | tf_op jit(solution)/shard_map/ppermute | solution.py:365
  12.0 1.4 %copy-start.2 = (bf16[1024,1152]{1,0:T(8,128)(2,1)}, bf16[1024,1152]{1,0:T(8,128)(2,1)S(1)}, u32[]{:S(2)}) copy-start(bf16[1024,1152]{1,0:T(8,128)(2,1)S(1)} %project_queries.1) | copy-start | bytes 7077892
  13.5 40.0 %collective-permute-start.2 = (bf16[256,1024]{1,0:T(8,128)(2,1)}, bf16[256,1024]{1,0:T(8,128)(2,1)}, u32[]{:S(2)}, u32[]{:S(2)}) collective-permute-start(bf16[256,1024]{1,0:T(8,128)(2,1)} %get-tuple-element.29.refs_5_), channel_id=1, source_target_pairs={{0,16},{8,24},{16,0},{24,8},{1,17},{9,25},{17,1},{25,9},{2,18},{10... | collective-permute-start | bytes 1572872 | tf_op jit(solution)/shard_map/ppermute | solution.py:365
  13.8 40.8 %all-to-all-start = ((bf16[8,128,1152]{2,1,0:T(8,128)(2,1)}), bf16[8,128,1152]{2,1,0:T(8,128)(2,1)S(1)}, u32[]{:S(2)}, u32[]{:S(2)}) async-start(bf16[8,128,1152]{2,1,0:T(8,128)(2,1)} %bitcast.11), calls=%async_computation | async-start | bytes 4718592 | tf_op jit(solution)/shard_map/all_to_all | solution.py:420
  18.3 2.2 %copy-start.1 = (bf16[1024,2048]{1,0:T(8,128)(2,1)S(1)}, bf16[1024,2048]{1,0:T(8,128)(2,1)}, u32[]{:S(2)}) copy-start(bf16[1024,2048]{1,0:T(8,128)(2,1)} %w_ref.4) | copy-start | bytes 12582916
  20.5 1.2 %copy-start.4 = (bf16[512,1024]{1,0:T(8,128)(2,1)S(1)}, bf16[512,1024]{1,0:T(8,128)(2,1)}, u32[]{:S(2)}) copy-start(bf16[512,1024]{1,0:T(8,128)(2,1)} %x_ref.5) | copy-start | bytes 3145732
  21.7 2.4 %copy-start.9 = (s32[512,1]{0,1:T(1,128)S(1)}, s32[512,1]{0,1:T(1,128)}, u32[]{:S(2)}) copy-start(s32[512,1]{0,1:T(1,128)} %param.9) | copy-start | bytes 6148
  23.1 1.0 copy-start.11
  41.3 22.0 %collective-permute-start.3 = (bf16[256,1024]{1,0:T(8,128)(2,1)}, bf16[256,1024]{1,0:T(8,128)(2,1)}, u32[]{:S(2)}, u32[]{:S(2)}) collective-permute-start(bf16[256,1024]{1,0:T(8,128)(2,1)} %collective-permute-done.1.refs_2_.refs_3_), channel_id=1, source_target_pairs={{0,8},{8,0},{16,24},{24,16},{1,9},{9,1},{17,25},{25,17},{2,10},{10... | collective-permute-start | bytes 1572872 | tf_op jit(solution)/shard_map/ppermute | solution.py:365
  53.8 0.7 copy-start.6
  65.8 2.4 %collective-permute-start.4 = (bf16[256,512]{1,0:T(8,128)(2,1)S(1)}, bf16[256,512]{1,0:T(8,128)(2,1)S(1)}, u32[]{:S(2)}, u32[]{:S(2)}) collective-permute-start(bf16[256,512]{1,0:T(8,128)(2,1)S(1)} %get-tuple-element.34), channel_id=1, source_target_pairs={{0,1},{1,0},{2,3},{3,2},{4,5},{5,4},{6,7},{7,6},{8,9},{9,8},{10,11... | collective-permute-start | bytes 786440 | tf_op jit(solution)/shard_map/ppermute | solution.py:365
  65.9 3.9 %collective-permute-start.6 = (bf16[256,512]{1,0:T(8,128)(2,1)S(1)}, bf16[256,512]{1,0:T(8,128)(2,1)S(1)}, u32[]{:S(2)}, u32[]{:S(2)}) collective-permute-start(bf16[256,512]{1,0:T(8,128)(2,1)S(1)} %get-tuple-element.35), channel_id=1, source_target_pairs={{0,1},{1,0},{2,3},{3,2},{4,5},{5,4},{6,7},{7,6},{8,9},{9,8},{10,11... | collective-permute-start | bytes 786440 | tf_op jit(solution)/shard_map/ppermute | solution.py:365
  66.4 14.2 %collective-permute-start.9 = (bf16[256,1024]{1,0:T(8,128)(2,1)}, bf16[256,1024]{1,0:T(8,128)(2,1)S(1)}, u32[]{:S(2)}, u32[]{:S(2)}) collective-permute-start(bf16[256,1024]{1,0:T(8,128)(2,1)} %collective-permute-done.2.refs_3_.refs_1_.refs_6_), channel_id=1, source_target_pairs={{0,8},{8,0},{16,24},{24,16},{1,9},{9,1},{17,25},{25,17},{2,10},{10... | collective-permute-start | bytes 1572872 | tf_op jit(solution)/shard_map/ppermute | solution.py:365
  68.3 14.5 %collective-permute-start.5 = (bf16[256,512]{1,0:T(8,128)(2,1)S(1)}, bf16[256,512]{1,0:T(8,128)(2,1)S(1)}, u32[]{:S(2)}, u32[]{:S(2)}) collective-permute-start(bf16[256,512]{1,0:T(8,128)(2,1)S(1)} %pad_maximum_fusion.refs_1_), channel_id=1, source_target_pairs={{0,2},{1,3},{2,0},{3,1},{4,6},{5,7},{6,4},{7,5},{8,10},{9,11},{10,... | collective-permute-start | bytes 786440 | tf_op jit(solution)/shard_map/ppermute | solution.py:365
  69.9 13.4 %collective-permute-start.7 = (bf16[256,512]{1,0:T(8,128)(2,1)S(1)}, bf16[256,512]{1,0:T(8,128)(2,1)S(1)}, u32[]{:S(2)}, u32[]{:S(2)}) collective-permute-start(bf16[256,512]{1,0:T(8,128)(2,1)S(1)} %pad_maximum_fusion.1.refs_2_), channel_id=1, source_target_pairs={{0,4},{1,5},{2,6},{3,7},{4,0},{5,1},{6,2},{7,3},{8,12},{9,13},{10,... | collective-permute-start | bytes 786440 | tf_op jit(solution)/shard_map/ppermute | solution.py:365
  71.5 11.8 %collective-permute-start.8 = (bf16[256,512]{1,0:T(8,128)(2,1)S(1)}, bf16[256,512]{1,0:T(8,128)(2,1)S(1)}, u32[]{:S(2)}, u32[]{:S(2)}) collective-permute-start(bf16[256,512]{1,0:T(8,128)(2,1)S(1)} %pad_maximum_fusion.2.refs_3_), channel_id=1, source_target_pairs={{0,6},{1,7},{2,4},{3,5},{4,2},{5,3},{6,0},{7,1},{8,14},{9,15},{10,... | collective-permute-start | bytes 786440 | tf_op jit(solution)/shard_map/ppermute | solution.py:365
  82.0 1.8 %collective-permute-start.10 = (bf16[256,512]{1,0:T(8,128)(2,1)S(1)}, bf16[256,512]{1,0:T(8,128)(2,1)S(1)}, u32[]{:S(2)}, u32[]{:S(2)}) collective-permute-start(bf16[256,512]{1,0:T(8,128)(2,1)S(1)} %get-tuple-element.38), channel_id=1, source_target_pairs={{0,1},{1,0},{2,3},{3,2},{4,5},{5,4},{6,7},{7,6},{8,9},{9,8},{10,11... | collective-permute-start | bytes 786440 | tf_op jit(solution)/shard_map/ppermute | solution.py:365
  82.3 1.9 %collective-permute-start.11 = (bf16[256,512]{1,0:T(8,128)(2,1)S(1)}, bf16[256,512]{1,0:T(8,128)(2,1)S(1)}, u32[]{:S(2)}, u32[]{:S(2)}) collective-permute-start(bf16[256,512]{1,0:T(8,128)(2,1)S(1)} %get-tuple-element.39), channel_id=1, source_target_pairs={{0,1},{1,0},{2,3},{3,2},{4,5},{5,4},{6,7},{7,6},{8,9},{9,8},{10,11... | collective-permute-start | bytes 786440 | tf_op jit(solution)/shard_map/ppermute | solution.py:365
  83.3 4.8 %copy-start.7 = (s32[512,128]{1,0:T(8,128)S(1)}, s32[512,128]{1,0:T(8,128)}, u32[]{:S(2)}) copy-start(s32[512,128]{1,0:T(8,128)} %copy-done.6) | copy-start | bytes 786436
  84.2 15.6 %copy-start.5 = (bf16[512,1024]{1,0:T(8,128)(2,1)S(1)}, bf16[512,1024]{1,0:T(8,128)(2,1)}, u32[]{:S(2)}) copy-start(bf16[512,1024]{1,0:T(8,128)(2,1)} %x_ref.5) | copy-start | bytes 3145732
  84.3 15.6 %copy-start.10 = (bf16[1024,1024]{1,0:T(8,128)(2,1)S(1)}, bf16[1024,1024]{1,0:T(8,128)(2,1)}, u32[]{:S(2)}) copy-start(bf16[1024,1024]{1,0:T(8,128)(2,1)} %w_ref.5) | copy-start | bytes 6291460
  84.3 15.6 %copy-start.12 = (bf16[512,1024]{1,0:T(8,128)(2,1)S(1)}, bf16[512,1024]{1,0:T(8,128)(2,1)}, u32[]{:S(2)}) copy-start(bf16[512,1024]{1,0:T(8,128)(2,1)} %copy-done.11) | copy-start | bytes 3145732
  84.3 15.6 %copy-start.13 = (f32[1024]{0:T(1024)S(1)}, f32[1024]{0:T(1024)}, u32[]{:S(2)}) copy-start(f32[1024]{0:T(1024)} %param.15) | copy-start | bytes 12292
  84.4 9.2 %collective-permute-start.12 = (bf16[256,512]{1,0:T(8,128)(2,1)S(1)}, bf16[256,512]{1,0:T(8,128)(2,1)S(1)}, u32[]{:S(2)}, u32[]{:S(2)}) collective-permute-start(bf16[256,512]{1,0:T(8,128)(2,1)S(1)} %pad_maximum_fusion.3), channel_id=1, source_target_pairs={{0,2},{1,3},{2,0},{3,1},{4,6},{5,7},{6,4},{7,5},{8,10},{9,11},{10,... | collective-permute-start | bytes 786440 | tf_op jit(solution)/shard_map/ppermute | solution.py:365
  86.1 13.8 %collective-permute-start.13 = (bf16[256,512]{1,0:T(8,128)(2,1)S(1)}, bf16[256,512]{1,0:T(8,128)(2,1)S(1)}, u32[]{:S(2)}, u32[]{:S(2)}) collective-permute-start(bf16[256,512]{1,0:T(8,128)(2,1)S(1)} %pad_maximum_fusion.4), channel_id=1, source_target_pairs={{0,4},{1,5},{2,6},{3,7},{4,0},{5,1},{6,2},{7,3},{8,12},{9,13},{10,... | collective-permute-start | bytes 786440 | tf_op jit(solution)/shard_map/ppermute | solution.py:365
  87.7 12.1 %collective-permute-start.14 = (bf16[256,512]{1,0:T(8,128)(2,1)S(1)}, bf16[256,512]{1,0:T(8,128)(2,1)S(1)}, u32[]{:S(2)}, u32[]{:S(2)}) collective-permute-start(bf16[256,512]{1,0:T(8,128)(2,1)S(1)} %pad_maximum_fusion.5), channel_id=1, source_target_pairs={{0,6},{1,7},{2,4},{3,5},{4,2},{5,3},{6,0},{7,1},{8,14},{9,15},{10,... | collective-permute-start | bytes 786440 | tf_op jit(solution)/shard_map/ppermute | solution.py:365
